TPU v7x, 32 devices: a whole 2x2x4 slice. The times are simulated.
32 devices in a mesh: groups: 2 (over y), wide: 4 (over z), narrow: 4 (over x, core).
Axes of the slice: x: 2, y: 2, z: 4, core: 2. Of those that a mesh axis runs over, the one named last changes fastest.
Arguments:
- inputs: bfloat16 [48, 8192], P(('groups', 'wide'), 'narrow'), parts along dimension 0, may hold values from -6 to 6
- cotangent: bfloat16 [48, 8192], P(('groups', 'wide'), 'narrow'), parts along dimension 0, may hold values from -3 to 3
- gate_weight: bfloat16 [8192, 24576], P('narrow', 'wide'), may hold values from -0.0625 to 0.0625
- up_weight: bfloat16 [8192, 24576], P('narrow', 'wide'), may hold values from -0.0625 to 0.0625
- down_weight: bfloat16 [24576, 8192], P('wide', 'narrow'), may hold values from -0.0390625 to 0.0390625
- ia3_scale: float32 [24576], P('wide'), may hold values from 0.3 to 3
- seq_ids: int32 [48], P('groups'), parts along dimension 0, may hold values from 0 to 3, as said below
Outputs:
- example_grads: float32 [8, 24576], P('groups', ('wide', 'narrow')), parts along dimension 0
- grad_norms: float32 [8], P('groups'), parts along dimension 0
- input_grad: bfloat16 [48, 8192], P(('groups', 'wide'), 'narrow'), parts along dimension 0
There are 2 independent parts, one for each index of `groups`. A program takes and returns all parts, laid end to end along the dimension named above; an argument that names none is the same for every part. Nothing has to cross between parts.
Inputs may be any that keep to these rules, and one draw needn't show every extreme that they name: `seq_ids`: ids never fall along the tokens; every one of the 4 sequences has at least one token, and one sequence, drawn at random, has exactly 12.
All inputs are finite; a program needn't handle non-finite values.
Results may differ from a plain program's by a relative error of at most 0.0051.
Values may be sent and summed in bfloat16 or wider, within the bound.
No kernel may reach another device: no remote copies, remote signals or barrier semaphores. Data moves between devices by JAX's collectives and lax.ppermute only.
A program may use at most 192 MiB of HBM per device.

v0:
```python
import jax
import jax.numpy as jnp
from jax import lax
from jax.sharding import PartitionSpec as P

SEQS = 4


def contract_rows(left, right):
    return lax.dot_general(
        left, right, (((1,), (1,)), ((), ())), preferred_element_type=jnp.float32
    )


def local_grads(gate_pre, up_pre, mid_grad, scale_part):
    sigmoid_gate = jax.nn.sigmoid(gate_pre)
    activation = gate_pre * sigmoid_gate
    hidden = activation * up_pre
    scaled = scale_part[None, :] * mid_grad
    d_up = (scaled * activation).astype(jnp.bfloat16)
    d_gate = (scaled * up_pre * sigmoid_gate * (1.0 + gate_pre * (1.0 - sigmoid_gate))).astype(
        jnp.bfloat16
    )
    return (hidden * mid_grad, d_gate, d_up)


def local(inputs, cotangent, gate_weight, up_weight, down_weight, ia3_scale, seq_ids):
    panel_inputs = lax.all_gather(inputs, "wide", axis=0, tiled=True)
    panel_cotangent = lax.all_gather(cotangent, "wide", axis=0, tiled=True)
    gate_part = jnp.dot(panel_inputs, gate_weight, preferred_element_type=jnp.float32)
    up_part = jnp.dot(panel_inputs, up_weight, preferred_element_type=jnp.float32)
    mid_part = contract_rows(panel_cotangent, down_weight)
    quarter = gate_weight.shape[1] // lax.axis_size("narrow")
    position = lax.axis_index("narrow")
    onehot_full = (seq_ids[None, :] == jnp.arange(SEQS, dtype=jnp.int32)[:, None]).astype(
        jnp.float32
    )
    gate_pre, up_pre, mid_grad = (
        lax.psum_scatter(gate_part, "narrow", scatter_dimension=1, tiled=True),
        lax.psum_scatter(up_part, "narrow", scatter_dimension=1, tiled=True),
        lax.psum_scatter(mid_part, "narrow", scatter_dimension=1, tiled=True),
    )
    scale_part = lax.dynamic_slice_in_dim(ia3_scale, position * quarter, quarter, 0)
    product, d_gate, d_up = local_grads(gate_pre, up_pre, mid_grad, scale_part)
    example_grads = jnp.dot(onehot_full, product, precision=lax.Precision.HIGHEST)
    whole_gate, whole_up = (
        lax.all_gather(d_gate, "narrow", axis=1, tiled=True),
        lax.all_gather(d_up, "narrow", axis=1, tiled=True),
    )
    squares = lax.psum(jnp.sum(example_grads * example_grads, axis=1), ("wide", "narrow"))
    grad_norms = jnp.sqrt(squares)
    input_grad = lax.psum_scatter(
        contract_rows(whole_gate, gate_weight) + contract_rows(whole_up, up_weight),
        "wide",
        scatter_dimension=0,
        tiled=True,
    ).astype(jnp.bfloat16)
    return (example_grads, grad_norms, input_grad)


def solution(mesh):
    return jax.shard_map(
        local,
        mesh=mesh,
        in_specs=(
            P(("groups", "wide"), "narrow"),
            P(("groups", "wide"), "narrow"),
            P("narrow", "wide"),
            P("narrow", "wide"),
            P("wide", "narrow"),
            P("wide"),
            P("groups"),
        ),
        out_specs=(P("groups", ("wide", "narrow")), P("groups"), P(("groups", "wide"), "narrow")),
        check_vma=False,
    )
```

profile of v0, /device:TPU:0, one launch (start us, length us, event | category | flops | bytes accessed | tf_op | source)
XLA Modules:
  0.0 199.5 jit_solution(17374402428923369356)
XLA Ops:
  7.2 0.0 copy-start.3
  7.2 0.0 reduce-scatter.10.cloned.1.call-start
  7.2 15.3 %all-gather.1 = bf16[4,6,2048]{2,1,0:T(8,128)(2,1)S(1)} all-gather(bf16[1,6,2048]{2,1,0:T(8,128)(2,1)} %bitcast.15), channel_id=1, replica_groups=mesh['groups'=2,'wide'=4,'narrow'=4] {'wide'}, dimensions={0}, use_global_device_ids=true | all-gather | bytes 122880 | tf_op jit(solution)/shard_map/all_gather | solution.py:29
  22.5 12.4 %fusion.10 = f32[24,6144]{1,0:T(8,128)} fusion(bf16[24,2048]{1,0:T(8,128)(2,1)S(1)} %reshape.11, bf16[6144,2048]{1,0:T(8,128)(2,1)} %param.11), kind=kOutput, calls=%fused_computation.15 | convolution fusion | flops 603979776 | bytes 25853952 | tf_op jit(solution)/shard_map/dot_general | solution.py:10
  34.9 0.0 reduce-scatter.10.cloned.1.call-update
  34.9 0.0 reduce-scatter.8.cloned.1.call-start
  35.0 0.0 copy-done.3
  35.0 13.5 %all-gather = bf16[4,6,2048]{2,1,0:T(8,128)(2,1)S(1)} all-gather(bf16[1,6,2048]{2,1,0:T(8,128)(2,1)S(1)} %bitcast.16), channel_id=1, replica_groups=mesh['groups'=2,'wide'=4,'narrow'=4] {'wide'}, dimensions={0}, use_global_device_ids=true | all-gather | bytes 122880 | tf_op jit(solution)/shard_map/all_gather | solution.py:28
  48.5 0.0 copy-start.4
  48.5 10.9 %fusion.9 = f32[24,6144]{1,0:T(8,128)} fusion(bf16[24,2048]{1,0:T(8,128)(2,1)S(1)} %reshape.9, bf16[2048,6144]{1,0:T(8,128)(2,1)} %param.10), kind=kOutput, calls=%fused_computation.14 | convolution fusion | flops 603979776 | bytes 25853952 | tf_op jit(solution)/shard_map/dot_general | solution.py:31
  59.4 0.0 reduce-scatter.8.cloned.1.call-update
  59.4 0.0 reduce-scatter.6.cloned.1.call-start
  59.5 10.9 %fusion.8 = f32[24,6144]{1,0:T(8,128)} fusion(bf16[24,2048]{1,0:T(8,128)(2,1)S(1)} %reshape.9, bf16[2048,6144]{1,0:T(8,128)(2,1)} %param.9), kind=kOutput, calls=%fused_computation.13 | convolution fusion | flops 603979776 | bytes 25853952 | tf_op jit(solution)/shard_map/dot_general | solution.py:30
  70.4 0.0 reduce-scatter.6.cloned.1.call-update
  70.4 0.8 dynamic_slice.3
  71.2 0.0 copy-done.4
  71.2 0.6 dynamic-slice.4
  72.4 0.0 reduce-scatter.10.cloned.1.call-done
  72.4 10.6 %reduce-scatter.8.cloned.1.call-done = f32[24,1536]{1,0:T(8,128)} async-done(((f32[24,6144]{1,0:T(8,128)}), f32[24,1536]{1,0:T(8,128)}) %reduce-scatter.8.cloned.1.call-update) | async-done | bytes 147472 | tf_op jit(solution)/shard_map/reduce_scatter | solution.py:40
  83.1 24.6 %reduce-scatter.6.cloned.1.call-done = f32[24,1536]{1,0:T(8,128)} async-done(((f32[24,6144]{1,0:T(8,128)}), f32[24,1536]{1,0:T(8,128)}) %reduce-scatter.6.cloned.1.call-update) | async-done | bytes 147472 | tf_op jit(solution)/shard_map/reduce_scatter | solution.py:39
  107.7 1.1 multiply_convert_fusion
  108.8 5.9 %all_gather.14 = bf16[24,6144]{1,0:T(8,128)(2,1)S(1)} all-gather(bf16[24,1536]{1,0:T(8,128)(2,1)S(1)} %get-tuple-element.4), channel_id=1, replica_groups=mesh['groups'=2,'wide'=4,'narrow'=4] {'narrow'}, dimensions={1}, use_global_device_ids=true | all-gather | bytes 368640 | tf_op jit(solution)/shard_map/all_gather | solution.py:47
  114.7 11.5 %fusion.11 = f32[24,2048]{1,0:T(8,128)S(1)} fusion(bf16[24,6144]{1,0:T(8,128)(2,1)S(1)} %all_gather.14, bf16[2048,6144]{1,0:T(8,128)(2,1)} %param.9), kind=kOutput, calls=%fused_computation.16 | convolution fusion | flops 603979776 | bytes 25657344 | tf_op jit(solution)/shard_map/dot_general | solution.py:10
  126.2 0.0 copy-start
  126.2 0.0 copy-start.1
  126.2 0.0 copy-start.2
  126.2 0.0 copy-start.5
  126.2 6.4 %all_gather.15 = bf16[24,6144]{1,0:T(8,128)(2,1)S(1)} all-gather(bf16[24,1536]{1,0:T(8,128)(2,1)S(1)} %get-tuple-element.3), channel_id=1, replica_groups=mesh['groups'=2,'wide'=4,'narrow'=4] {'narrow'}, dimensions={1}, use_global_device_ids=true | all-gather | bytes 368640 | tf_op jit(solution)/shard_map/all_gather | solution.py:48
  132.6 11.5 %convolution_add_fusion = f32[24,2048]{1,0:T(8,128)S(1)} fusion(f32[24,2048]{1,0:T(8,128)S(1)} %fusion.11, bf16[24,6144]{1,0:T(8,128)(2,1)S(1)} %all_gather.15, bf16[2048,6144]{1,0:T(8,128)(2,1)} %param.10), kind=kOutput, calls=%fused_computation | convolution fusion | flops 604028928 | bytes 25853952 | tf_op jit(solution)/shard_map/dot_general | solution.py:10
  144.1 15.1 %fusion = f32[8,2048]{1,0:T(8,128)S(1)} fusion(f32[24,2048]{1,0:T(8,128)S(1)} %convolution_add_fusion), kind=kCustom, calls=%all-reduce-scatter | all-reduce-scatter fusion | flops 65537 | bytes 262656
  159.3 2.0 collective-permute-start
  161.2 0.0 copy-done
  161.2 0.0 copy-done.1
  161.3 0.0 copy-done.2
  161.3 0.0 copy-done.5
  161.3 0.9 multiply_reduce_fusion
  162.2 29.5 %psum.7 = f32[4]{0:T(128)S(1)} all-reduce(f32[4]{0:T(128)S(1)} %get-tuple-element.5), channel_id=1, replica_groups=mesh['groups'=2,'wide'=4,'narrow'=4] {'wide','narrow'}, use_global_device_ids=true, to_apply=%region_4.0 | all-reduce | flops 4 | bytes 32 | tf_op jit(solution)/shard_map/psum | solution.py:50
  191.7 0.5 sqrt.3
  192.2 0.0 collective-permute-done
  192.2 0.1 concatenate
  192.4 0.6 dynamic-slice_convert_fusion
  (3 shorter events, 0.1 us)
Async XLA Ops:
  7.2 27.8 %copy-start.3 = (bf16[6,2048]{1,0:T(8,128)(2,1)S(1)}, bf16[6,2048]{1,0:T(8,128)(2,1)}, u32[]{:S(2)}) copy-start(bf16[6,2048]{1,0:T(8,128)(2,1)} %param.7) | copy-start | bytes 73732
  7.2 65.3 %reduce-scatter.10.cloned.1.call-start = ((), (), s32[]{:S(2)}) async-start(), calls=%async_computation.5 | async-start | bytes 737280 | tf_op jit(solution)/shard_map/reduce_scatter | solution.py:41
  34.9 48.2 %reduce-scatter.8.cloned.1.call-start = ((), (), s32[]{:S(2)}) async-start(), calls=%async_computation.4 | async-start | bytes 737280 | tf_op jit(solution)/shard_map/reduce_scatter | solution.py:40
  48.5 22.6 %copy-start.4 = (u32[32]{0:T(128)S(1)}, u32[32]{0:T(128)}, u32[]{:S(2)}) copy-start(u32[32]{0:T(128)} %constant.18) | copy-start | bytes 388
  59.4 48.2 %reduce-scatter.6.cloned.1.call-start = ((), (), s32[]{:S(2)}) async-start(), calls=%async_computation.3 | async-start | bytes 737280 | tf_op jit(solution)/shard_map/reduce_scatter | solution.py:39
  126.2 35.1 %copy-start = (f32[24,1536]{1,0:T(8,128)S(1)}, f32[24,1536]{1,0:T(8,128)}, u32[]{:S(2)}) copy-start(f32[24,1536]{1,0:T(8,128)} %reduce-scatter.10.cloned.1.call-done) | copy-start | bytes 442372
  126.2 35.0 %copy-start.1 = (f32[24,1536]{1,0:T(8,128)S(1)}, f32[24,1536]{1,0:T(8,128)}, u32[]{:S(2)}) copy-start(f32[24,1536]{1,0:T(8,128)} %reduce-scatter.8.cloned.1.call-done) | copy-start | bytes 442372
  126.2 35.0 %copy-start.2 = (f32[24,1536]{1,0:T(8,128)S(1)}, f32[24,1536]{1,0:T(8,128)}, u32[]{:S(2)}) copy-start(f32[24,1536]{1,0:T(8,128)} %reduce-scatter.6.cloned.1.call-done) | copy-start | bytes 442372
  126.2 35.0 %copy-start.5 = (s32[24]{0:T(128)S(1)}, s32[24]{0:T(128)}, u32[]{:S(2)}) copy-start(s32[24]{0:T(128)} %param.13) | copy-start | bytes 292
  159.3 33.0 %collective-permute-start = (bf16[6,2048]{1,0:T(8,128)(2,1)S(1)}, bf16[6,2048]{1,0:T(8,128)(2,1)S(1)}, u32[]{:S(2)}, u32[]{:S(2)}) collective-permute-start(bf16[6,2048]{1,0:T(8,128)(2,1)S(1)} %slice), channel_id=1, source_target_pairs={{0,4},{4,8},{8,12},{1,5},{5,9},{9,13},{2,6},{6,10},{10,14},{3,7},{... | collective-permute-start | bytes 73736
Sparse Core Ops, SparseCore 0:
  35.0 23.3 reduce-scatter.9
  61.0 22.0 reduce-scatter.7
  85.6 22.0 reduce-scatter.5
where the time goes:
time: 200 us
  blocking collectives  85.6 us (43%)
  matrix products  58.1 us (29%)
  waiting for transfers between devices  35.3 us (18%)
  between operations  14.5 us (7%)
  local copies, waits for them, and re-layouts  2.78 us (1%)
  starting transfers between devices  2.1 us (1%)
    dot_general x3, matrix products, contract_rows(): lax.dot_general(left, right, (((1,), (1,)), ((), ())), preferred_element_...  35.4 us
    psum x1, blocking collectives, local(): lax.psum(jnp.sum(example_grads * example_grads, axis=1), ('wide', 'narrow'))  29.5 us
    reduce_scatter x1, waiting for transfers between devices, local(): lax.psum_scatter(gate_part, 'narrow', scatter_dimension=1, tiled=True)  24.6 us
    all_gather x1, blocking collectives, local(): panel_cotangent = lax.all_gather(cotangent, 'wide', axis=0, tiled=True)  15.3 us
    unnamed x1, blocking collectives  15.1 us
    all_gather x1, blocking collectives, local(): panel_inputs = lax.all_gather(inputs, 'wide', axis=0, tiled=True)  13.5 us
    dot_general x1, matrix products, local(): jnp.dot(panel_inputs, gate_weight, preferred_element_type=jnp.float32)  10.9 us
    dot_general x1, matrix products, local(): jnp.dot(panel_inputs, up_weight, preferred_element_type=jnp.float32)  10.9 us
  transfers between devices with their start and end apart: 4, of which 2 were waited for; matrix products, arithmetic and copies ran while one was open for 12% of the time, Pallas kernels for 0%

commit v1 on v0

--- a/solution.py
+++ b/solution.py
@@ -1,9 +1,14 @@
+import functools
+
 import jax
 import jax.numpy as jnp
 from jax import lax
+from jax.experimental import pallas as pl
+from jax.experimental.pallas import tpu as pltpu
 from jax.sharding import PartitionSpec as P
 
 SEQS = 4
+KERNEL_VMEM = 12 << 20
 
 
 def contract_rows(left, right):
@@ -16,7 +21,7 @@
     sigmoid_gate = jax.nn.sigmoid(gate_pre)
     activation = gate_pre * sigmoid_gate
     hidden = activation * up_pre
-    scaled = scale_part[None, :] * mid_grad
+    scaled = scale_part * mid_grad
     d_up = (scaled * activation).astype(jnp.bfloat16)
     d_gate = (scaled * up_pre * sigmoid_gate * (1.0 + gate_pre * (1.0 - sigmoid_gate))).astype(
         jnp.bfloat16
@@ -24,7 +29,7 @@
     return (hidden * mid_grad, d_gate, d_up)
 
 
-def local(inputs, cotangent, gate_weight, up_weight, down_weight, ia3_scale, seq_ids):
+def whole_block(inputs, cotangent, gate_weight, up_weight, down_weight, ia3_scale, seq_ids):
     panel_inputs = lax.all_gather(inputs, "wide", axis=0, tiled=True)
     panel_cotangent = lax.all_gather(cotangent, "wide", axis=0, tiled=True)
     gate_part = jnp.dot(panel_inputs, gate_weight, preferred_element_type=jnp.float32)
@@ -41,7 +46,7 @@
         lax.psum_scatter(mid_part, "narrow", scatter_dimension=1, tiled=True),
     )
     scale_part = lax.dynamic_slice_in_dim(ia3_scale, position * quarter, quarter, 0)
-    product, d_gate, d_up = local_grads(gate_pre, up_pre, mid_grad, scale_part)
+    product, d_gate, d_up = local_grads(gate_pre, up_pre, mid_grad, scale_part[None, :])
     example_grads = jnp.dot(onehot_full, product, precision=lax.Precision.HIGHEST)
     whole_gate, whole_up = (
         lax.all_gather(d_gate, "narrow", axis=1, tiled=True),
@@ -56,6 +61,257 @@
         tiled=True,
     ).astype(jnp.bfloat16)
     return (example_grads, grad_norms, input_grad)
+
+
+def exchange(array, axes, size, step):
+    return lax.ppermute(array, axes, [(i, i ^ step) for i in range(size)])
+
+
+def in_vmem(shape, dtype):
+    return pltpu.VMEM(shape, dtype)
+
+
+def held(array):
+    return pltpu.with_memory_space_constraint(array, pltpu.VMEM)
+
+
+def specs(count, space=pltpu.VMEM):
+    return [pl.BlockSpec(memory_space=space)] * count
+
+
+def load_kernel(strips, groups, gate, up, down, gate_held, up_held, down_held, sem):
+    narrow, group = lax.axis_index("narrow"), lax.axis_index("groups")
+    width = gate_held.shape[2]
+    copies = []
+    for s in range(strips):
+        start = pl.multiple_of(((narrow ^ s) * groups + group) * width, width)
+        copies.append(pltpu.make_async_copy(down.at[pl.ds(start, width), :], down_held.at[s], sem.at[0, s]))
+        copies.append(pltpu.make_async_copy(gate.at[:, pl.ds(start, width)], gate_held.at[s], sem.at[1, s]))
+        copies.append(pltpu.make_async_copy(up.at[:, pl.ds(start, width)], up_held.at[s], sem.at[2, s]))
+    for copy in copies:
+        copy.start()
+    for copy in copies:
+        copy.wait()
+
+
+def forward_kernel(strips, peers, *refs):
+    inputs, cotangent = refs[:2]
+    arrived = refs[2 : 1 + peers]
+    gate, up, down = refs[1 + peers : 4 + peers]
+    own, sends = refs[4 + peers], refs[5 + peers : 4 + peers + strips]
+    rows, cots = refs[4 + peers + strips :]
+    share = inputs.shape[0]
+    rows[0:share, :] = inputs[...].astype(jnp.float32)
+    cots[0:share, :] = cotangent[...].astype(jnp.float32)
+    for s in range(1, peers):
+        both = arrived[s - 1][...].astype(jnp.float32)
+        rows[s * share : (s + 1) * share, :] = both[:share]
+        cots[s * share : (s + 1) * share, :] = both[share:]
+    tokens, cotans = rows[...].astype(jnp.bfloat16), cots[...].astype(jnp.bfloat16)
+    for s in range(strips):
+        gate_part = jnp.dot(tokens, gate[s], preferred_element_type=jnp.float32)
+        up_part = jnp.dot(tokens, up[s], preferred_element_type=jnp.float32)
+        mid_part = contract_rows(cotans, down[s])
+        target = own if s == 0 else sends[s - 1]
+        for i, part in enumerate((gate_part, up_part, mid_part)):
+            target[i] = part.astype(target.dtype)
+
+
+def middle_kernel(strips, groups, wide, *refs):
+    own, arrived = refs[0], refs[1:strips]
+    scale, ids, other_ids = refs[strips : strips + 3]
+    message, grads, other_grads, stage = refs[strips + 3 :]
+    _, tokens, width = own.shape
+    narrow, group, position = lax.axis_index("narrow"), lax.axis_index("groups"), lax.axis_index("wide")
+    share = tokens // (groups * wide)
+    sums = [own[i] + sum(ref[i].astype(jnp.float32) for ref in arrived) for i in range(3)]
+    start = pl.multiple_of((narrow * groups + group) * width, width)
+    product, d_gate, d_up = local_grads(*sums, scale[:, pl.ds(start, width)])
+    message[0:tokens, :] = d_gate
+    message[tokens : 2 * tokens, :] = d_up
+    row = lax.broadcasted_iota(jnp.int32, (8, 128), 0)
+    keys = []
+    for base in range(0, tokens, 8):
+        key = jnp.zeros((8, 128), jnp.int32)
+        for r in range(8):
+            block, j = divmod(base + r, share)
+            source = ids if block < wide else other_ids
+            key = jnp.where(row == r, source[(position ^ (block % wide)) * share + j], key)
+        keys.append(jnp.concatenate([key] * (width // 128), axis=1))
+    key = jnp.concatenate(keys, axis=0)
+    half = tokens // groups
+    for side, target in enumerate((grads, other_grads)):
+        part, seq = product[side * half : (side + 1) * half], key[side * half : (side + 1) * half]
+        for e in range(SEQS):
+            total = jnp.sum(jnp.where(seq == e, part, 0.0), axis=0, keepdims=True)
+            target[e : e + 1, :] = total
+            stage[side * SEQS + e : side * SEQS + e + 1, :] = total * total
+    squares = jnp.broadcast_to(jnp.sum(stage[...], axis=1, keepdims=True), stage.shape)
+    high = squares.astype(jnp.bfloat16).astype(jnp.float32)
+    message[2 * tokens :, :] = jnp.concatenate([high, squares - high], axis=0).astype(jnp.bfloat16)
+
+
+def backward_kernel(strips, peers, *refs):
+    messages, (gate, up) = refs[:strips], refs[strips : strips + 2]
+    own, sends = refs[strips + 2], refs[strips + 3 : strips + 2 + peers]
+    total, stage = refs[strips + 2 + peers :]
+    tokens, features = total.shape
+    tile = 512
+    for start in range(0, features, tile):
+        part = None
+        for s in range(strips):
+            for i, weight in enumerate((gate, up)):
+                term = contract_rows(
+                    messages[s][i * tokens : (i + 1) * tokens, :], weight[s, start : start + tile, :]
+                )
+                part = term if part is None else part + term
+        total[:, start : start + tile] = part
+    squares = sum(message[2 * tokens :, 0:128].astype(jnp.float32) for message in messages)
+    squares = squares[0:8] + squares[8:16]
+    high = squares.astype(jnp.bfloat16).astype(jnp.float32)
+    low = squares - high
+    share = tokens // peers
+    stage[...] = jnp.zeros_like(stage)
+    for k in range(8):
+        stage[6:7, k * 128 : (k + 1) * 128] = high[k : k + 1]
+        stage[7:8, k * 128 : (k + 1) * 128] = low[k : k + 1]
+    for s in range(peers):
+        stage[0:share, :] = total[s * share : (s + 1) * share, :]
+        target = own if s == 0 else sends[s - 1]
+        target[...] = stage[...].astype(target.dtype)
+
+
+def last_kernel(peers, wide, *refs):
+    blocks = refs[:peers]
+    grads, other = refs[peers : peers + 2]
+    input_grad, example_grads, norms = refs[peers + 2 :]
+    share, width = input_grad.shape[0], grads.shape[1]
+    group = lax.axis_index("groups")
+    total = jnp.zeros(blocks[0].shape, jnp.float32)
+    squares = jnp.zeros((1, SEQS * 128), jnp.float32)
+    for s, block in enumerate(blocks):
+        values = block[...].astype(jnp.float32)
+        total = total + values
+        first = SEQS * 128 * (s // wide)
+        squares = squares + values[6:7, first : first + SEQS * 128] + values[7:8, first : first + SEQS * 128]
+    input_grad[...] = total[0:share].astype(jnp.bfloat16)
+    roots = jnp.sqrt(squares)
+    for e in range(SEQS):
+        norms[e] = jnp.max(roots[:, e * 128 : (e + 1) * 128])
+    example_grads[:, pl.ds(pl.multiple_of(group * width, width), width)] = grads[...]
+    example_grads[:, pl.ds(pl.multiple_of((1 - group) * width, width), width)] = other[...]
+
+
+def shared(inputs, cotangent, gate_weight, up_weight, down_weight, ia3_scale, seq_ids):
+    groups, wide, strips = lax.axis_size("groups"), lax.axis_size("wide"), lax.axis_size("narrow")
+    peers = groups * wide
+    share, features = inputs.shape
+    hidden = gate_weight.shape[1]
+    width = hidden // (strips * groups)
+    tokens = share * peers
+    f32, bf16 = jnp.float32, jnp.bfloat16
+    params = pltpu.CompilerParams(vmem_limit_bytes=KERNEL_VMEM)
+
+    both = jnp.concatenate([inputs, cotangent], axis=0)
+    arrived = [exchange(both, ("groups", "wide"), peers, s) for s in range(1, peers)]
+    other_ids = exchange(seq_ids, "groups", groups, 1)
+
+    weight_bytes = 3 * strips * features * width * 2
+    gate, up, down = pl.pallas_call(
+        functools.partial(load_kernel, strips, groups),
+        out_shape=[
+            in_vmem((strips, features, width), bf16),
+            in_vmem((strips, features, width), bf16),
+            in_vmem((strips, width, features), bf16),
+        ],
+        in_specs=specs(3, pl.ANY),
+        out_specs=specs(3),
+        scratch_shapes=[pltpu.SemaphoreType.DMA((3, strips))],
+        compiler_params=params,
+        cost_estimate=pl.CostEstimate(flops=0, bytes_accessed=2 * weight_bytes, transcendentals=0),
+        name="load_weights",
+    )(gate_weight, up_weight, down_weight)
+
+    partials = pl.pallas_call(
+        functools.partial(forward_kernel, strips, peers),
+        out_shape=[in_vmem((3, tokens, width), f32)] + [in_vmem((3, tokens, width), bf16)] * (strips - 1),
+        in_specs=specs(4 + peers),
+        out_specs=specs(strips),
+        scratch_shapes=[pltpu.VMEM((tokens, features), f32)] * 2,
+        compiler_params=params,
+        cost_estimate=pl.CostEstimate(
+            flops=2 * tokens * weight_bytes // 2, bytes_accessed=weight_bytes, transcendentals=0
+        ),
+        name="forward",
+    )(inputs, cotangent, *arrived, held(gate), held(up), held(down))
+    terms = [exchange(partials[s], "narrow", strips, s) for s in range(1, strips)]
+
+    message, grads, other_grads = pl.pallas_call(
+        functools.partial(middle_kernel, strips, groups, wide),
+        out_shape=[
+            in_vmem((2 * tokens + 16, width), bf16),
+            in_vmem((SEQS, width), f32),
+            in_vmem((SEQS, width), f32),
+        ],
+        in_specs=specs(strips + 1) + specs(2, pltpu.SMEM),
+        out_specs=specs(3),
+        scratch_shapes=[pltpu.VMEM((groups * SEQS, width), f32)],
+        compiler_params=params,
+        name="middle",
+    )(partials[0], *terms, ia3_scale[None, :], seq_ids, other_ids)
+    messages = [message] + [exchange(message, "narrow", strips, s) for s in range(1, strips)]
+    other_part = exchange(other_grads, "groups", groups, 1)
+
+    blocks = pl.pallas_call(
+        functools.partial(backward_kernel, strips, peers),
+        out_shape=[in_vmem((8, features), f32)] + [in_vmem((8, features), bf16)] * (peers - 1),
+        in_specs=specs(strips + 2),
+        out_specs=specs(peers),
+        scratch_shapes=[pltpu.VMEM((tokens, features), f32), pltpu.VMEM((8, features), f32)],
+        compiler_params=params,
+        cost_estimate=pl.CostEstimate(
+            flops=2 * tokens * weight_bytes // 3, bytes_accessed=weight_bytes * 2 // 3, transcendentals=0
+        ),
+        name="backward",
+    )(*messages, held(gate), held(up))
+    blocks = [blocks[0]] + [exchange(blocks[s], ("groups", "wide"), peers, s) for s in range(1, peers)]
+
+    input_grad, example_grads, norms = pl.pallas_call(
+        functools.partial(last_kernel, peers, wide),
+        out_shape=[
+            jax.ShapeDtypeStruct((share, features), bf16),
+            jax.ShapeDtypeStruct((SEQS, groups * width), f32),
+            jax.ShapeDtypeStruct((SEQS,), f32),
+        ],
+        in_specs=specs(peers + 2),
+        out_specs=specs(2) + specs(1, pltpu.SMEM),
+        compiler_params=params,
+        name="last",
+    )(*blocks, grads, other_part)
+    return (example_grads, norms, input_grad)
+
+
+def power_of_two(number):
+    return number & (number - 1) == 0
+
+
+def local(inputs, cotangent, gate_weight, up_weight, down_weight, ia3_scale, seq_ids):
+    groups, wide, narrow = lax.axis_size("groups"), lax.axis_size("wide"), lax.axis_size("narrow")
+    share, (features, hidden) = inputs.shape[0], gate_weight.shape
+    fits = (
+        groups == 2
+        and power_of_two(wide)
+        and power_of_two(narrow)
+        and hidden % (narrow * groups * 256) == 0
+        and features % 512 == 0
+        and features >= 2 * SEQS * 128
+        and share <= 6
+        and (share * wide) % 8 == 0
+        and (share * wide * groups) % 16 == 0
+        and 3 * features * hidden // groups * 2 <= 40 << 20
+    )
+    plan = shared if fits else whole_block
+    return plan(inputs, cotangent, gate_weight, up_weight, down_weight, ia3_scale, seq_ids)
 
 
 def solution(mesh):

time: 200 us -> 93.7 us (0.47)
  blocking collectives: 85.6 us -> 0 us
  matrix products: 58.1 us -> 0 us
  Pallas kernels: 0 us -> 29.7 us
  starting transfers between devices: 2.1 us -> 30.3 us
  between operations: 14.5 us -> 0.78 us
  waiting for transfers between devices: 35.3 us -> 22.8 us
  local copies, waits for them, and re-layouts: 2.78 us -> 9.11 us
    dot_general x6 -> x0, matrix products: 58.1 us -> none  [the longest x3 35.4 us: contract_rows(): lax.dot_general(left, right, (((1,), (1,)), ((), ())), preferred_element_...]
    all_gather x4 -> x0, blocking collectives: 41 us -> none  [the longest x1 15.3 us: local(): panel_cotangent = lax.all_gather(cotangent, 'wide', axis=0, tiled=True)]
    reduce_scatter x3 -> x0, waiting for transfers between devices: 35.2 us -> none  [the longest x1 24.6 us: local(): lax.psum_scatter(gate_part, 'narrow', scatter_dimension=1, tiled=True)]
    ppermute x0 -> x22, starting transfers between devices: none -> 30.3 us  [exchange(): return lax.ppermute(array, axes, [(i, i ^ step) for i in range(size)])]
    pallas_call x0 -> x5, Pallas kernels: none -> 29.7 us  [the longest x1 12.4 us: shared(): pl.pallas_call(functools.partial(load_kernel, strips, groups), out_shape=...]
    psum x1 -> x0, blocking collectives: 29.5 us -> none  [local(): lax.psum(jnp.sum(example_grads * example_grads, axis=1), ('wide', 'narrow'))]
    ppermute x0 -> x22, waiting for transfers between devices: none -> 22.8 us  [exchange(): return lax.ppermute(array, axes, [(i, i ^ step) for i in range(size)])]
    unnamed x1 -> x0, blocking collectives: 15.1 us -> none
  transfers between devices with their start and end apart: 4 -> 22, of which waited for: 2 -> 7; matrix products, arithmetic and copies ran while one was open for 12% -> 0% of each run, Pallas kernels for 0% -> 13%
where the time goes in v1:
time: 93.7 us; the launch traced here: 93.5 us
  starting transfers between devices  30.3 us (32%)
  Pallas kernels  29.7 us (32%)
  waiting for transfers between devices  22.8 us (24%)
  local copies, waits for them, and re-layouts  9.11 us (10%)
    ppermute x22, starting transfers between devices, exchange(): return lax.ppermute(array, axes, [(i, i ^ step) for i in range(size)])  30.3 us
    ppermute x22, waiting for transfers between devices, exchange(): return lax.ppermute(array, axes, [(i, i ^ step) for i in range(size)])  22.8 us
    pallas_call x1, Pallas kernels, shared(): pl.pallas_call(functools.partial(load_kernel, strips, groups), out_shape=...  12.4 us
    unnamed x12, local copies, waits for them, and re-layouts  9.11 us
    pallas_call x1, Pallas kernels, shared(): pl.pallas_call(functools.partial(forward_kernel, strips, peers), out_shap...  8.11 us
    pallas_call x1, Pallas kernels, shared(): pl.pallas_call(functools.partial(backward_kernel, strips, peers), out_sha...  7.51 us
  transfers between devices with their start and end apart: 22, of which 7 were waited for; matrix products, arithmetic and copies ran while one was open for 0% of the time, Pallas kernels for 13%

profile of v1, /device:TPU:0, one launch (start us, length us, event | category | flops | bytes accessed | tf_op | source)
XLA Modules:
  0.0 93.5 jit_solution(6644337252281967560)
XLA Ops:
  0.6 0.8 pad_maximum_fusion
  1.4 0.0 copy-start.2
  1.4 0.0 copy-start.3
  1.5 3.1 %collective-permute-start = (bf16[12,2048]{1,0:T(8,128)(2,1)S(1)}, bf16[12,2048]{1,0:T(8,128)(2,1)S(1)}, u32[]{:S(2)}, u32[]{:S(2)}) collective-permute-start(bf16[12,2048]{1,0:T(8,128)(2,1)S(1)} %pad_maximum_fusion), channel_id=1, source_target_pairs={{0,4},{4,0},{8,12},{12,8},{16,20},{20,16},{24,28},{28,24},{1,5},{5... | collective-permute-start | bytes 147464 | tf_op jit(solution)/shard_map/ppermute | solution.py:67
  4.5 2.6 %collective-permute-start.1 = (bf16[12,2048]{1,0:T(8,128)(2,1)S(1)}, bf16[12,2048]{1,0:T(8,128)(2,1)S(1)}, u32[]{:S(2)}, u32[]{:S(2)}) collective-permute-start(bf16[12,2048]{1,0:T(8,128)(2,1)S(1)} %pad_maximum_fusion), channel_id=1, source_target_pairs={{0,8},{4,12},{8,0},{12,4},{16,24},{20,28},{24,16},{28,20},{1,9},{5... | collective-permute-start | bytes 147464 | tf_op jit(solution)/shard_map/ppermute | solution.py:67
  7.1 0.0 collective-permute-start.2
  7.1 1.7 %collective-permute-start.3 = (bf16[12,2048]{1,0:T(8,128)(2,1)S(1)}, bf16[12,2048]{1,0:T(8,128)(2,1)S(1)}, u32[]{:S(2)}, u32[]{:S(2)}) collective-permute-start(bf16[12,2048]{1,0:T(8,128)(2,1)S(1)} %pad_maximum_fusion), channel_id=1, source_target_pairs={{0,16},{4,20},{8,24},{12,28},{16,0},{20,4},{24,8},{28,12},{1,17},{... | collective-permute-start | bytes 147464 | tf_op jit(solution)/shard_map/ppermute | solution.py:67
  8.9 0.6 collective-permute-start.4
  9.5 0.0 collective-permute-done.refs_2_
  9.5 4.4 %collective-permute-start.5 = (bf16[12,2048]{1,0:T(8,128)(2,1)S(1)}, bf16[12,2048]{1,0:T(8,128)(2,1)S(1)}, u32[]{:S(2)}, u32[]{:S(2)}) collective-permute-start(bf16[12,2048]{1,0:T(8,128)(2,1)S(1)} %pad_maximum_fusion), channel_id=1, source_target_pairs={{0,24},{4,28},{8,16},{12,20},{16,8},{20,12},{24,0},{28,4},{1,25},{... | collective-permute-start | bytes 147464 | tf_op jit(solution)/shard_map/ppermute | solution.py:67
  13.9 0.0 collective-permute-done.1.refs_3_
  14.0 2.4 %collective-permute-start.6 = (bf16[12,2048]{1,0:T(8,128)(2,1)S(1)}, bf16[12,2048]{1,0:T(8,128)(2,1)S(1)}, u32[]{:S(2)}, u32[]{:S(2)}) collective-permute-start(bf16[12,2048]{1,0:T(8,128)(2,1)S(1)} %pad_maximum_fusion), channel_id=1, source_target_pairs={{0,28},{4,24},{8,20},{12,16},{16,12},{20,8},{24,4},{28,0},{1,29},{... | collective-permute-start | bytes 147464 | tf_op jit(solution)/shard_map/ppermute | solution.py:67
  16.3 12.4 %load_weights.1 = (bf16[4,2048,768]{2,1,0:T(8,128)(2,1)S(1)}, bf16[4,2048,768]{2,1,0:T(8,128)(2,1)S(1)}, bf16[4,768,2048]{2,1,0:T(8,128)(2,1)S(1)}) custom-call(bf16[2048,6144]{1,0:T(8,128)(2,1)} %gate.1, bf16[2048,6144]{1,0:T(8,128)(2,1)} %up.1, bf16[6144,2048]{1,0:T(8,128)(2,1)} %down.1), custom_call_target="tpu_custom_call" | custom-call | bytes 75497472 | tf_op jit(solution)/shard_map/load_weights/pallas_call | solution.py:220
  28.7 0.0 copy-start.5
  28.7 0.0 copy-start.4
  28.8 0.0 collective-permute-done.3.refs_5_
  28.8 0.0 collective-permute-done.6.refs_8_
  28.8 8.1 %forward.1 = (f32[3,48,768]{2,1,0:T(8,128)S(1)}, bf16[3,48,768]{2,1,0:T(8,128)(2,1)S(1)}, bf16[3,48,768]{2,1,0:T(8,128)(2,1)S(1)}, bf16[3,48,768]{2,1,0:T(8,128)(2,1)S(1)}) custom-call(bf16[6,2048]{1,0:T(8,128)(2,1)S(1)} %copy-done.2, bf16[6,2048]{1,0:T(8,128)(2,1)S(1)} %copy-done.3, bf16[12,2048]{1,0:T(8,128)(2,1)S(1)} %collective-permute-done.refs_2_, ...), custom_call_target="tpu_custom_call" | custom-call | flops 1811939328 | bytes 37748736 | tf_op jit(solution)/shard_map/forward/pallas_call | solution.py:235
  37.0 4.5 %copy-done = bf16[4,2048,768]{2,1,0:T(8,128)(2,1)} copy-done((bf16[4,2048,768]{2,1,0:T(8,128)(2,1)}, bf16[4,2048,768]{2,1,0:T(8,128)(2,1)S(1)}, u32[]{:S(2)}) %copy-start) | copy-done | bytes 12582936
  41.5 0.0 collective-permute-start.7
  41.5 1.5 %collective-permute-start.8 = (bf16[3,48,768]{2,1,0:T(8,128)(2,1)S(1)}, bf16[3,48,768]{2,1,0:T(8,128)(2,1)S(1)}, u32[]{:S(2)}, u32[]{:S(2)}) collective-permute-start(bf16[3,48,768]{2,1,0:T(8,128)(2,1)S(1)} %get-tuple-element.29), channel_id=1, source_target_pairs={{0,2},{1,3},{2,0},{3,1},{4,6},{5,7},{6,4},{7,5},{8,10},{9,11},{10,... | collective-permute-start | bytes 663560 | tf_op jit(solution)/shard_map/ppermute | solution.py:67
  43.0 0.4 collective-permute-start.9
  43.3 0.1 collective-permute-start.10
  43.4 3.5 %collective-permute-done.10.refs_6_ = s32[24]{0:T(128)S(1)} collective-permute-done((s32[24]{0:T(128)S(1)}, s32[24]{0:T(128)S(1)}, u32[]{:S(2)}, u32[]{:S(2)}) %collective-permute-start.10) | collective-permute-done | bytes 128 | tf_op jit(solution)/shard_map/ppermute | solution.py:67
  46.9 0.0 collective-permute-done.7.refs_1_
  46.9 2.8 %collective-permute-done.8.refs_2_ = bf16[3,48,768]{2,1,0:T(8,128)(2,1)S(1)} collective-permute-done((bf16[3,48,768]{2,1,0:T(8,128)(2,1)S(1)}, bf16[3,48,768]{2,1,0:T(8,128)(2,1)S(1)}, u32[]{:S(2)}, u32[]{:S(2)}) %collective-permute-start.8) | collective-permute-done | bytes 221216 | tf_op jit(solution)/shard_map/ppermute | solution.py:67
  49.7 4.0 %collective-permute-done.9.refs_3_ = bf16[3,48,768]{2,1,0:T(8,128)(2,1)S(1)} collective-permute-done((bf16[3,48,768]{2,1,0:T(8,128)(2,1)S(1)}, bf16[3,48,768]{2,1,0:T(8,128)(2,1)S(1)}, u32[]{:S(2)}, u32[]{:S(2)}) %collective-permute-start.9) | collective-permute-done | bytes 221216 | tf_op jit(solution)/shard_map/ppermute | solution.py:67
  53.7 1.0 %middle.1 = (bf16[112,768]{1,0:T(8,128)(2,1)S(1)}, f32[4,768]{1,0:T(4,128)S(1)}, f32[4,768]{1,0:T(4,128)S(1)}) custom-call(f32[3,48,768]{2,1,0:T(8,128)S(1)} %get-tuple-element.27.refs_0_, bf16[3,48,768]{2,1,0:T(8,128)(2,1)S(1)} %collective-permute-done.7.refs_1_, bf16[3,48,768]{2,1,0:T(8,128)(2,1)S(1)} %collective-permute-done.8.refs_2_, ...), custom_call_target="tpu_custom_call" | custom-call | tf_op jit(solution)/shard_map/middle/pallas_call | solution.py:249
  54.6 0.2 collective-permute-start.11
  54.8 1.5 %collective-permute-start.12 = (bf16[112,768]{1,0:T(8,128)(2,1)S(1)}, bf16[112,768]{1,0:T(8,128)(2,1)S(1)}, u32[]{:S(2)}, u32[]{:S(2)}) collective-permute-start(bf16[112,768]{1,0:T(8,128)(2,1)S(1)} %get-tuple-element.31.refs_0_), channel_id=1, source_target_pairs={{0,2},{1,3},{2,0},{3,1},{4,6},{5,7},{6,4},{7,5},{8,10},{9,11},{10,... | collective-permute-start | bytes 516104 | tf_op jit(solution)/shard_map/ppermute | solution.py:67
  56.3 0.2 collective-permute-start.13
  56.5 0.0 collective-permute-done.11.refs_1_
  56.5 5.5 %collective-permute-done.12.refs_2_ = bf16[112,768]{1,0:T(8,128)(2,1)S(1)} collective-permute-done((bf16[112,768]{1,0:T(8,128)(2,1)S(1)}, bf16[112,768]{1,0:T(8,128)(2,1)S(1)}, u32[]{:S(2)}, u32[]{:S(2)}) %collective-permute-start.12) | collective-permute-done | bytes 172064 | tf_op jit(solution)/shard_map/ppermute | solution.py:67
  62.0 2.4 %collective-permute-done.13.refs_3_ = bf16[112,768]{1,0:T(8,128)(2,1)S(1)} collective-permute-done((bf16[112,768]{1,0:T(8,128)(2,1)S(1)}, bf16[112,768]{1,0:T(8,128)(2,1)S(1)}, u32[]{:S(2)}, u32[]{:S(2)}) %collective-permute-start.13) | collective-permute-done | bytes 172064 | tf_op jit(solution)/shard_map/ppermute | solution.py:67
  64.5 4.6 %copy-done.1 = bf16[4,2048,768]{2,1,0:T(8,128)(2,1)S(1)} copy-done((bf16[4,2048,768]{2,1,0:T(8,128)(2,1)S(1)}, bf16[4,2048,768]{2,1,0:T(8,128)(2,1)}, u32[]{:S(2)}) %copy-start.1) | copy-done | bytes 12582936
  69.0 7.5 %backward.1 = (f32[8,2048]{1,0:T(8,128)S(1)}, bf16[8,2048]{1,0:T(8,128)(2,1)S(1)}, bf16[8,2048]{1,0:T(8,128)(2,1)S(1)}, bf16[8,2048]{1,0:T(8,128)(2,1)S(1)}, bf1...) custom-call(bf16[112,768]{1,0:T(8,128)(2,1)S(1)} %get-tuple-element., ...), custom_call_target="tpu_custom_call" | custom-call | flops 1207959552 | bytes 25165824 | tf_op jit(solution)/shard_map/backward/pallas_call | solution.py:265
  76.6 0.1 collective-permute-start.14
  76.6 1.9 %collective-permute-start.15 = (bf16[8,2048]{1,0:T(8,128)(2,1)S(1)}, bf16[8,2048]{1,0:T(8,128)(2,1)S(1)}, u32[]{:S(2)}, u32[]{:S(2)}) collective-permute-start(bf16[8,2048]{1,0:T(8,128)(2,1)S(1)} %get-tuple-element.34), channel_id=1, source_target_pairs={{0,8},{4,12},{8,0},{12,4},{16,24},{20,28},{24,16},{28,20},{1,9},{5... | collective-permute-start | bytes 98312 | tf_op jit(solution)/shard_map/ppermute | solution.py:67
  78.6 1.3 %collective-permute-start.21 = (f32[4,768]{1,0:T(4,128)S(1)}, f32[4,768]{1,0:T(4,128)S(1)}, u32[]{:S(2)}, u32[]{:S(2)}) collective-permute-start(f32[4,768]{1,0:T(4,128)S(1)} %get-tuple-element.41), channel_id=1, source_target_pairs={{0,16},{16,0},{1,17},{17,1},{2,18},{18,2},{3,19},{19,3},{4,20},{20... | collective-permute-start | bytes 36872 | tf_op jit(solution)/shard_map/ppermute | solution.py:67
  79.9 1.2 %collective-permute-start.16 = (bf16[8,2048]{1,0:T(8,128)(2,1)S(1)}, bf16[8,2048]{1,0:T(8,128)(2,1)S(1)}, u32[]{:S(2)}, u32[]{:S(2)}) collective-permute-start(bf16[8,2048]{1,0:T(8,128)(2,1)S(1)} %get-tuple-element.35), channel_id=1, source_target_pairs={{0,12},{4,8},{8,4},{12,0},{16,28},{20,24},{24,20},{28,16},{1,13},{... | collective-permute-start | bytes 98312 | tf_op jit(solution)/shard_map/ppermute | solution.py:67
  81.1 2.0 %collective-permute-start.17 = (bf16[8,2048]{1,0:T(8,128)(2,1)S(1)}, bf16[8,2048]{1,0:T(8,128)(2,1)S(1)}, u32[]{:S(2)}, u32[]{:S(2)}) collective-permute-start(bf16[8,2048]{1,0:T(8,128)(2,1)S(1)} %get-tuple-element.36), channel_id=1, source_target_pairs={{0,16},{4,20},{8,24},{12,28},{16,0},{20,4},{24,8},{28,12},{1,17},{... | collective-permute-start | bytes 98312 | tf_op jit(solution)/shard_map/ppermute | solution.py:67
  83.0 0.0 collective-permute-start.18
  83.1 3.1 %collective-permute-start.19 = (bf16[8,2048]{1,0:T(8,128)(2,1)S(1)}, bf16[8,2048]{1,0:T(8,128)(2,1)S(1)}, u32[]{:S(2)}, u32[]{:S(2)}) collective-permute-start(bf16[8,2048]{1,0:T(8,128)(2,1)S(1)} %get-tuple-element.38), channel_id=1, source_target_pairs={{0,24},{4,28},{8,16},{12,20},{16,8},{20,12},{24,0},{28,4},{1,25},{... | collective-permute-start | bytes 98312 | tf_op jit(solution)/shard_map/ppermute | solution.py:67
  86.2 0.0 collective-permute-done.15.refs_2_
  86.2 2.1 %collective-permute-start.20 = (bf16[8,2048]{1,0:T(8,128)(2,1)S(1)}, bf16[8,2048]{1,0:T(8,128)(2,1)S(1)}, u32[]{:S(2)}, u32[]{:S(2)}) collective-permute-start(bf16[8,2048]{1,0:T(8,128)(2,1)S(1)} %get-tuple-element.39), channel_id=1, source_target_pairs={{0,28},{4,24},{8,20},{12,16},{16,12},{20,8},{24,4},{28,0},{1,29},{... | collective-permute-start | bytes 98312 | tf_op jit(solution)/shard_map/ppermute | solution.py:67
  88.3 0.5 collective-permute-done.19.refs_6_
  88.8 4.0 %collective-permute-done.20.refs_7_ = bf16[8,2048]{1,0:T(8,128)(2,1)S(1)} collective-permute-done((bf16[8,2048]{1,0:T(8,128)(2,1)S(1)}, bf16[8,2048]{1,0:T(8,128)(2,1)S(1)}, u32[]{:S(2)}, u32[]{:S(2)}) %collective-permute-start.20) | collective-permute-done | bytes 32800 | tf_op jit(solution)/shard_map/ppermute | solution.py:67
  92.8 0.7 last.1
  (14 shorter events, 0.0 us)
Async XLA Ops:
  1.4 27.4 %copy-start.2 = (bf16[6,2048]{1,0:T(8,128)(2,1)S(1)}, bf16[6,2048]{1,0:T(8,128)(2,1)}, u32[]{:S(2)}) copy-start(bf16[6,2048]{1,0:T(8,128)(2,1)} %refs_0_.1) | copy-start | bytes 73732
  1.4 27.4 %copy-start.3 = (bf16[6,2048]{1,0:T(8,128)(2,1)S(1)}, bf16[6,2048]{1,0:T(8,128)(2,1)}, u32[]{:S(2)}) copy-start(bf16[6,2048]{1,0:T(8,128)(2,1)} %refs_1_.1) | copy-start | bytes 73732
  1.5 8.0 %collective-permute-start = (bf16[12,2048]{1,0:T(8,128)(2,1)S(1)}, bf16[12,2048]{1,0:T(8,128)(2,1)S(1)}, u32[]{:S(2)}, u32[]{:S(2)}) collective-permute-start(bf16[12,2048]{1,0:T(8,128)(2,1)S(1)} %pad_maximum_fusion), channel_id=1, source_target_pairs={{0,4},{4,0},{8,12},{12,8},{16,20},{20,16},{24,28},{28,24},{1,5},{5... | collective-permute-start | bytes 147464 | tf_op jit(solution)/shard_map/ppermute | solution.py:67
  4.5 9.4 %collective-permute-start.1 = (bf16[12,2048]{1,0:T(8,128)(2,1)S(1)}, bf16[12,2048]{1,0:T(8,128)(2,1)S(1)}, u32[]{:S(2)}, u32[]{:S(2)}) collective-permute-start(bf16[12,2048]{1,0:T(8,128)(2,1)S(1)} %pad_maximum_fusion), channel_id=1, source_target_pairs={{0,8},{4,12},{8,0},{12,4},{16,24},{20,28},{24,16},{28,20},{1,9},{5... | collective-permute-start | bytes 147464 | tf_op jit(solution)/shard_map/ppermute | solution.py:67
  7.1 21.6 %collective-permute-start.2 = (bf16[12,2048]{1,0:T(8,128)(2,1)S(1)}, bf16[12,2048]{1,0:T(8,128)(2,1)S(1)}, u32[]{:S(2)}, u32[]{:S(2)}) collective-permute-start(bf16[12,2048]{1,0:T(8,128)(2,1)S(1)} %pad_maximum_fusion), channel_id=1, source_target_pairs={{0,12},{4,8},{8,4},{12,0},{16,28},{20,24},{24,20},{28,16},{1,13},{... | collective-permute-start | bytes 147464 | tf_op jit(solution)/shard_map/ppermute | solution.py:67
  7.1 21.6 %collective-permute-start.3 = (bf16[12,2048]{1,0:T(8,128)(2,1)S(1)}, bf16[12,2048]{1,0:T(8,128)(2,1)S(1)}, u32[]{:S(2)}, u32[]{:S(2)}) collective-permute-start(bf16[12,2048]{1,0:T(8,128)(2,1)S(1)} %pad_maximum_fusion), channel_id=1, source_target_pairs={{0,16},{4,20},{8,24},{12,28},{16,0},{20,4},{24,8},{28,12},{1,17},{... | collective-permute-start | bytes 147464 | tf_op jit(solution)/shard_map/ppermute | solution.py:67
  8.9 19.9 %collective-permute-start.4 = (bf16[12,2048]{1,0:T(8,128)(2,1)S(1)}, bf16[12,2048]{1,0:T(8,128)(2,1)S(1)}, u32[]{:S(2)}, u32[]{:S(2)}) collective-permute-start(bf16[12,2048]{1,0:T(8,128)(2,1)S(1)} %pad_maximum_fusion), channel_id=1, source_target_pairs={{0,20},{4,16},{8,28},{12,24},{16,4},{20,0},{24,12},{28,8},{1,21},{... | collective-permute-start | bytes 147464 | tf_op jit(solution)/shard_map/ppermute | solution.py:67
  9.5 19.3 %collective-permute-start.5 = (bf16[12,2048]{1,0:T(8,128)(2,1)S(1)}, bf16[12,2048]{1,0:T(8,128)(2,1)S(1)}, u32[]{:S(2)}, u32[]{:S(2)}) collective-permute-start(bf16[12,2048]{1,0:T(8,128)(2,1)S(1)} %pad_maximum_fusion), channel_id=1, source_target_pairs={{0,24},{4,28},{8,16},{12,20},{16,8},{20,12},{24,0},{28,4},{1,25},{... | collective-permute-start | bytes 147464 | tf_op jit(solution)/shard_map/ppermute | solution.py:67
  14.0 14.9 %collective-permute-start.6 = (bf16[12,2048]{1,0:T(8,128)(2,1)S(1)}, bf16[12,2048]{1,0:T(8,128)(2,1)S(1)}, u32[]{:S(2)}, u32[]{:S(2)}) collective-permute-start(bf16[12,2048]{1,0:T(8,128)(2,1)S(1)} %pad_maximum_fusion), channel_id=1, source_target_pairs={{0,28},{4,24},{8,20},{12,16},{16,12},{20,8},{24,4},{28,0},{1,29},{... | collective-permute-start | bytes 147464 | tf_op jit(solution)/shard_map/ppermute | solution.py:67
  28.7 14.6 %copy-start.5 = (s32[24]{0:T(128)S(1)}, s32[24]{0:T(128)}, u32[]{:S(2)}) copy-start(s32[24]{0:T(128)} %refs_5_.1) | copy-start | bytes 292
  28.7 24.9 %copy-start.4 = (f32[6144]{0:T(1024)S(1)}, f32[6144]{0:T(1024)}, u32[]{:S(2)}) copy-start(f32[6144]{0:T(1024)} %param.12) | copy-start | bytes 73732
  36.9 4.5 %copy-start = (bf16[4,2048,768]{2,1,0:T(8,128)(2,1)}, bf16[4,2048,768]{2,1,0:T(8,128)(2,1)S(1)}, u32[]{:S(2)}) copy-start(bf16[4,2048,768]{2,1,0:T(8,128)(2,1)S(1)} %get-tuple-element.25.refs_10_.refs_5_) | copy-start | bytes 37748740
  41.5 5.4 %collective-permute-start.7 = (bf16[3,48,768]{2,1,0:T(8,128)(2,1)S(1)}, bf16[3,48,768]{2,1,0:T(8,128)(2,1)S(1)}, u32[]{:S(2)}, u32[]{:S(2)}) collective-permute-start(bf16[3,48,768]{2,1,0:T(8,128)(2,1)S(1)} %get-tuple-element.28), channel_id=1, source_target_pairs={{0,1},{1,0},{2,3},{3,2},{4,5},{5,4},{6,7},{7,6},{8,9},{9,8},{10,11... | collective-permute-start | bytes 663560 | tf_op jit(solution)/shard_map/ppermute | solution.py:67
  41.5 8.2 %collective-permute-start.8 = (bf16[3,48,768]{2,1,0:T(8,128)(2,1)S(1)}, bf16[3,48,768]{2,1,0:T(8,128)(2,1)S(1)}, u32[]{:S(2)}, u32[]{:S(2)}) collective-permute-start(bf16[3,48,768]{2,1,0:T(8,128)(2,1)S(1)} %get-tuple-element.29), channel_id=1, source_target_pairs={{0,2},{1,3},{2,0},{3,1},{4,6},{5,7},{6,4},{7,5},{8,10},{9,11},{10,... | collective-permute-start | bytes 663560 | tf_op jit(solution)/shard_map/ppermute | solution.py:67
  43.0 10.7 %collective-permute-start.9 = (bf16[3,48,768]{2,1,0:T(8,128)(2,1)S(1)}, bf16[3,48,768]{2,1,0:T(8,128)(2,1)S(1)}, u32[]{:S(2)}, u32[]{:S(2)}) collective-permute-start(bf16[3,48,768]{2,1,0:T(8,128)(2,1)S(1)} %get-tuple-element.30), channel_id=1, source_target_pairs={{0,3},{1,2},{2,1},{3,0},{4,7},{5,6},{6,5},{7,4},{8,11},{9,10},{10,... | collective-permute-start | bytes 663560 | tf_op jit(solution)/shard_map/ppermute | solution.py:67
  43.3 3.5 %collective-permute-start.10 = (s32[24]{0:T(128)S(1)}, s32[24]{0:T(128)S(1)}, u32[]{:S(2)}, u32[]{:S(2)}) collective-permute-start(s32[24]{0:T(128)S(1)} %copy-done.5), channel_id=1, source_target_pairs={{0,16},{16,0},{1,17},{17,1},{2,18},{18,2},{3,19},{19,3},{4,20},{20... | collective-permute-start | bytes 296 | tf_op jit(solution)/shard_map/ppermute | solution.py:67
  54.6 1.9 %collective-permute-start.11 = (bf16[112,768]{1,0:T(8,128)(2,1)S(1)}, bf16[112,768]{1,0:T(8,128)(2,1)S(1)}, u32[]{:S(2)}, u32[]{:S(2)}) collective-permute-start(bf16[112,768]{1,0:T(8,128)(2,1)S(1)} %get-tuple-element.31.refs_0_), channel_id=1, source_target_pairs={{0,1},{1,0},{2,3},{3,2},{4,5},{5,4},{6,7},{7,6},{8,9},{9,8},{10,11... | collective-permute-start | bytes 516104 | tf_op jit(solution)/shard_map/ppermute | solution.py:67
  54.8 7.2 %collective-permute-start.12 = (bf16[112,768]{1,0:T(8,128)(2,1)S(1)}, bf16[112,768]{1,0:T(8,128)(2,1)S(1)}, u32[]{:S(2)}, u32[]{:S(2)}) collective-permute-start(bf16[112,768]{1,0:T(8,128)(2,1)S(1)} %get-tuple-element.31.refs_0_), channel_id=1, source_target_pairs={{0,2},{1,3},{2,0},{3,1},{4,6},{5,7},{6,4},{7,5},{8,10},{9,11},{10,... | collective-permute-start | bytes 516104 | tf_op jit(solution)/shard_map/ppermute | solution.py:67
  56.3 8.1 %collective-permute-start.13 = (bf16[112,768]{1,0:T(8,128)(2,1)S(1)}, bf16[112,768]{1,0:T(8,128)(2,1)S(1)}, u32[]{:S(2)}, u32[]{:S(2)}) collective-permute-start(bf16[112,768]{1,0:T(8,128)(2,1)S(1)} %get-tuple-element.31.refs_0_), channel_id=1, source_target_pairs={{0,3},{1,2},{2,1},{3,0},{4,7},{5,6},{6,5},{7,4},{8,11},{9,10},{10,... | collective-permute-start | bytes 516104 | tf_op jit(solution)/shard_map/ppermute | solution.py:67
  64.5 4.6 %copy-start.1 = (bf16[4,2048,768]{2,1,0:T(8,128)(2,1)S(1)}, bf16[4,2048,768]{2,1,0:T(8,128)(2,1)}, u32[]{:S(2)}) copy-start(bf16[4,2048,768]{2,1,0:T(8,128)(2,1)} %copy-done) | copy-start | bytes 37748740
  76.6 6.5 %collective-permute-start.14 = (bf16[8,2048]{1,0:T(8,128)(2,1)S(1)}, bf16[8,2048]{1,0:T(8,128)(2,1)S(1)}, u32[]{:S(2)}, u32[]{:S(2)}) collective-permute-start(bf16[8,2048]{1,0:T(8,128)(2,1)S(1)} %get-tuple-element.33), channel_id=1, source_target_pairs={{0,4},{4,0},{8,12},{12,8},{16,20},{20,16},{24,28},{28,24},{1,5},{5... | collective-permute-start | bytes 98312 | tf_op jit(solution)/shard_map/ppermute | solution.py:67
  76.6 9.5 %collective-permute-start.15 = (bf16[8,2048]{1,0:T(8,128)(2,1)S(1)}, bf16[8,2048]{1,0:T(8,128)(2,1)S(1)}, u32[]{:S(2)}, u32[]{:S(2)}) collective-permute-start(bf16[8,2048]{1,0:T(8,128)(2,1)S(1)} %get-tuple-element.34), channel_id=1, source_target_pairs={{0,8},{4,12},{8,0},{12,4},{16,24},{20,28},{24,16},{28,20},{1,9},{5... | collective-permute-start | bytes 98312 | tf_op jit(solution)/shard_map/ppermute | solution.py:67
  78.6 4.5 %collective-permute-start.21 = (f32[4,768]{1,0:T(4,128)S(1)}, f32[4,768]{1,0:T(4,128)S(1)}, u32[]{:S(2)}, u32[]{:S(2)}) collective-permute-start(f32[4,768]{1,0:T(4,128)S(1)} %get-tuple-element.41), channel_id=1, source_target_pairs={{0,16},{16,0},{1,17},{17,1},{2,18},{18,2},{3,19},{19,3},{4,20},{20... | collective-permute-start | bytes 36872 | tf_op jit(solution)/shard_map/ppermute | solution.py:67
  79.9 8.4 %collective-permute-start.16 = (bf16[8,2048]{1,0:T(8,128)(2,1)S(1)}, bf16[8,2048]{1,0:T(8,128)(2,1)S(1)}, u32[]{:S(2)}, u32[]{:S(2)}) collective-permute-start(bf16[8,2048]{1,0:T(8,128)(2,1)S(1)} %get-tuple-element.35), channel_id=1, source_target_pairs={{0,12},{4,8},{8,4},{12,0},{16,28},{20,24},{24,20},{28,16},{1,13},{... | collective-permute-start | bytes 98312 | tf_op jit(solution)/shard_map/ppermute | solution.py:67
  81.1 7.2 %collective-permute-start.17 = (bf16[8,2048]{1,0:T(8,128)(2,1)S(1)}, bf16[8,2048]{1,0:T(8,128)(2,1)S(1)}, u32[]{:S(2)}, u32[]{:S(2)}) collective-permute-start(bf16[8,2048]{1,0:T(8,128)(2,1)S(1)} %get-tuple-element.36), channel_id=1, source_target_pairs={{0,16},{4,20},{8,24},{12,28},{16,0},{20,4},{24,8},{28,12},{1,17},{... | collective-permute-start | bytes 98312 | tf_op jit(solution)/shard_map/ppermute | solution.py:67
  83.0 5.2 %collective-permute-start.18 = (bf16[8,2048]{1,0:T(8,128)(2,1)S(1)}, bf16[8,2048]{1,0:T(8,128)(2,1)S(1)}, u32[]{:S(2)}, u32[]{:S(2)}) collective-permute-start(bf16[8,2048]{1,0:T(8,128)(2,1)S(1)} %get-tuple-element.37), channel_id=1, source_target_pairs={{0,20},{4,16},{8,28},{12,24},{16,4},{20,0},{24,12},{28,8},{1,21},{... | collective-permute-start | bytes 98312 | tf_op jit(solution)/shard_map/ppermute | solution.py:67
  83.1 5.8 %collective-permute-start.19 = (bf16[8,2048]{1,0:T(8,128)(2,1)S(1)}, bf16[8,2048]{1,0:T(8,128)(2,1)S(1)}, u32[]{:S(2)}, u32[]{:S(2)}) collective-permute-start(bf16[8,2048]{1,0:T(8,128)(2,1)S(1)} %get-tuple-element.38), channel_id=1, source_target_pairs={{0,24},{4,28},{8,16},{12,20},{16,8},{20,12},{24,0},{28,4},{1,25},{... | collective-permute-start | bytes 98312 | tf_op jit(solution)/shard_map/ppermute | solution.py:67
  86.2 6.6 %collective-permute-start.20 = (bf16[8,2048]{1,0:T(8,128)(2,1)S(1)}, bf16[8,2048]{1,0:T(8,128)(2,1)S(1)}, u32[]{:S(2)}, u32[]{:S(2)}) collective-permute-start(bf16[8,2048]{1,0:T(8,128)(2,1)S(1)} %get-tuple-element.39), channel_id=1, source_target_pairs={{0,28},{4,24},{8,20},{12,16},{16,12},{20,8},{24,4},{28,0},{1,29},{... | collective-permute-start | bytes 98312 | tf_op jit(solution)/shard_map/ppermute | solution.py:67

commit v2 on v1

--- a/solution.py
+++ b/solution.py
@@ -94,112 +94,116 @@
         copy.wait()
 
 
-def forward_kernel(strips, peers, *refs):
-    inputs, cotangent = refs[:2]
-    arrived = refs[2 : 1 + peers]
-    gate, up, down = refs[1 + peers : 4 + peers]
-    own, sends = refs[4 + peers], refs[5 + peers : 4 + peers + strips]
-    rows, cots = refs[4 + peers + strips :]
-    share = inputs.shape[0]
-    rows[0:share, :] = inputs[...].astype(jnp.float32)
-    cots[0:share, :] = cotangent[...].astype(jnp.float32)
-    for s in range(1, peers):
-        both = arrived[s - 1][...].astype(jnp.float32)
-        rows[s * share : (s + 1) * share, :] = both[:share]
-        cots[s * share : (s + 1) * share, :] = both[share:]
+def forward_kernel(strips, peers, arrived, gate, up, down, own, sends, rows, cots):
+    narrow = lax.axis_index("narrow")
+    share = arrived.shape[1] // 2
+    for p in range(peers):
+        both = arrived[p].astype(jnp.float32)
+        rows[p * share : (p + 1) * share, :] = both[:share]
+        cots[p * share : (p + 1) * share, :] = both[share:]
     tokens, cotans = rows[...].astype(jnp.bfloat16), cots[...].astype(jnp.bfloat16)
     for s in range(strips):
         gate_part = jnp.dot(tokens, gate[s], preferred_element_type=jnp.float32)
         up_part = jnp.dot(tokens, up[s], preferred_element_type=jnp.float32)
         mid_part = contract_rows(cotans, down[s])
-        target = own if s == 0 else sends[s - 1]
         for i, part in enumerate((gate_part, up_part, mid_part)):
-            target[i] = part.astype(target.dtype)
-
-
-def middle_kernel(strips, groups, wide, *refs):
-    own, arrived = refs[0], refs[1:strips]
-    scale, ids, other_ids = refs[strips : strips + 3]
-    message, grads, other_grads, stage = refs[strips + 3 :]
+            if s == 0:
+                own[i] = part
+            sends[narrow ^ s, i] = part.astype(sends.dtype)
+
+
+def middle_kernel(strips, groups, wide, own, arrived, scale, ids, other_ids, gate, up, message, grads, other_grads, stage):
+    del gate, up
     _, tokens, width = own.shape
-    narrow, group, position = lax.axis_index("narrow"), lax.axis_index("groups"), lax.axis_index("wide")
-    share = tokens // (groups * wide)
-    sums = [own[i] + sum(ref[i].astype(jnp.float32) for ref in arrived) for i in range(3)]
+    narrow, group = lax.axis_index("narrow"), lax.axis_index("groups")
+    sums = []
+    for i in range(3):
+        total = own[i]
+        for s in range(1, strips):
+            total = total + arrived[narrow ^ s, i].astype(jnp.float32)
+        sums.append(total)
     start = pl.multiple_of((narrow * groups + group) * width, width)
     product, d_gate, d_up = local_grads(*sums, scale[:, pl.ds(start, width)])
-    message[0:tokens, :] = d_gate
-    message[tokens : 2 * tokens, :] = d_up
     row = lax.broadcasted_iota(jnp.int32, (8, 128), 0)
+    half = tokens // groups
     keys = []
     for base in range(0, tokens, 8):
         key = jnp.zeros((8, 128), jnp.int32)
+        side, offset = divmod(base, half)
         for r in range(8):
-            block, j = divmod(base + r, share)
-            source = ids if block < wide else other_ids
-            key = jnp.where(row == r, source[(position ^ (block % wide)) * share + j], key)
+            value = jnp.where(group == side, ids[offset + r], other_ids[offset + r])
+            key = jnp.where(row == r, value, key)
         keys.append(jnp.concatenate([key] * (width // 128), axis=1))
     key = jnp.concatenate(keys, axis=0)
-    half = tokens // groups
-    for side, target in enumerate((grads, other_grads)):
+    for side in range(groups):
         part, seq = product[side * half : (side + 1) * half], key[side * half : (side + 1) * half]
         for e in range(SEQS):
             total = jnp.sum(jnp.where(seq == e, part, 0.0), axis=0, keepdims=True)
-            target[e : e + 1, :] = total
-            stage[side * SEQS + e : side * SEQS + e + 1, :] = total * total
-    squares = jnp.broadcast_to(jnp.sum(stage[...], axis=1, keepdims=True), stage.shape)
+            stage[side * SEQS + e : side * SEQS + e + 1, :] = total
+    every = stage[...]
+    first, second = every[:SEQS], every[SEQS:]
+    grads[...] = jnp.where(group == 0, first, second)
+    other_grads[...] = jnp.where(group == 0, second, first)
+    squares = jnp.broadcast_to(jnp.sum(every * every, axis=1, keepdims=True), every.shape)
     high = squares.astype(jnp.bfloat16).astype(jnp.float32)
-    message[2 * tokens :, :] = jnp.concatenate([high, squares - high], axis=0).astype(jnp.bfloat16)
-
-
-def backward_kernel(strips, peers, *refs):
-    messages, (gate, up) = refs[:strips], refs[strips : strips + 2]
-    own, sends = refs[strips + 2], refs[strips + 3 : strips + 2 + peers]
-    total, stage = refs[strips + 2 + peers :]
+    tail = jnp.concatenate([high, squares - high], axis=0).astype(jnp.bfloat16)
+    for s in range(strips):
+        message[s, 0:tokens, :] = d_gate
+        message[s, tokens : 2 * tokens, :] = d_up
+        message[s, 2 * tokens :, :] = tail
+
+
+def backward_kernel(strips, groups, wide, messages, gate, up, own, sends, total, stage):
     tokens, features = total.shape
+    peers = groups * wide
+    narrow = lax.axis_index("narrow")
+    peer = lax.axis_index("groups") * wide + lax.axis_index("wide")
     tile = 512
     for start in range(0, features, tile):
         part = None
         for s in range(strips):
             for i, weight in enumerate((gate, up)):
                 term = contract_rows(
-                    messages[s][i * tokens : (i + 1) * tokens, :], weight[s, start : start + tile, :]
+                    messages[narrow ^ s, i * tokens : (i + 1) * tokens, :], weight[s, start : start + tile, :]
                 )
                 part = term if part is None else part + term
         total[:, start : start + tile] = part
-    squares = sum(message[2 * tokens :, 0:128].astype(jnp.float32) for message in messages)
+    squares = sum(messages[s, 2 * tokens :, 0:128].astype(jnp.float32) for s in range(strips))
     squares = squares[0:8] + squares[8:16]
     high = squares.astype(jnp.bfloat16).astype(jnp.float32)
     low = squares - high
     share = tokens // peers
-    stage[...] = jnp.zeros_like(stage)
-    for k in range(8):
-        stage[6:7, k * 128 : (k + 1) * 128] = high[k : k + 1]
-        stage[7:8, k * 128 : (k + 1) * 128] = low[k : k + 1]
-    for s in range(peers):
-        stage[0:share, :] = total[s * share : (s + 1) * share, :]
-        target = own if s == 0 else sends[s - 1]
-        target[...] = stage[...].astype(target.dtype)
-
-
-def last_kernel(peers, wide, *refs):
-    blocks = refs[:peers]
-    grads, other = refs[peers : peers + 2]
-    input_grad, example_grads, norms = refs[peers + 2 :]
+    for p in range(peers):
+        stage[p, 0:share, :] = total[p * share : (p + 1) * share, :]
+        stage[p, 6:8, :] = jnp.zeros((2, features), jnp.float32)
+        for k in range(8):
+            stage[p, 6:7, k * 128 : (k + 1) * 128] = high[k : k + 1]
+            stage[p, 7:8, k * 128 : (k + 1) * 128] = low[k : k + 1]
+        sends[p] = stage[p].astype(jnp.bfloat16)
+    own[...] = stage[peer]
+
+
+def last_kernel(groups, wide, own, blocks, grads, other, input_grad, example_grads, norms):
+    peers = groups * wide
     share, width = input_grad.shape[0], grads.shape[1]
     group = lax.axis_index("groups")
-    total = jnp.zeros(blocks[0].shape, jnp.float32)
-    squares = jnp.zeros((1, SEQS * 128), jnp.float32)
-    for s, block in enumerate(blocks):
-        values = block[...].astype(jnp.float32)
-        total = total + values
-        first = SEQS * 128 * (s // wide)
-        squares = squares + values[6:7, first : first + SEQS * 128] + values[7:8, first : first + SEQS * 128]
+    peer = group * wide + lax.axis_index("wide")
+    total = own[...]
+    for s in range(1, peers):
+        total = total + blocks[peer ^ s].astype(jnp.float32)
     input_grad[...] = total[0:share].astype(jnp.bfloat16)
+    lanes = SEQS * 128
+    squares = total[6:7] + total[7:8]
+    squares = jnp.where(group == 0, squares[:, 0:lanes], squares[:, lanes : 2 * lanes])
     roots = jnp.sqrt(squares)
     for e in range(SEQS):
         norms[e] = jnp.max(roots[:, e * 128 : (e + 1) * 128])
     example_grads[:, pl.ds(pl.multiple_of(group * width, width), width)] = grads[...]
     example_grads[:, pl.ds(pl.multiple_of((1 - group) * width, width), width)] = other[...]
+
+
+def swap_blocks(array, axes):
+    return lax.all_to_all(array, axes, 0, 0, tiled=True)
 
 
 def shared(inputs, cotangent, gate_weight, up_weight, down_weight, ia3_scale, seq_ids):
@@ -213,7 +217,7 @@
     params = pltpu.CompilerParams(vmem_limit_bytes=KERNEL_VMEM)
 
     both = jnp.concatenate([inputs, cotangent], axis=0)
-    arrived = [exchange(both, ("groups", "wide"), peers, s) for s in range(1, peers)]
+    arrived = swap_blocks(jnp.broadcast_to(both[None], (peers,) + both.shape), ("groups", "wide"))
     other_ids = exchange(seq_ids, "groups", groups, 1)
 
     weight_bytes = 3 * strips * features * width * 2
@@ -232,62 +236,62 @@
         name="load_weights",
     )(gate_weight, up_weight, down_weight)
 
-    partials = pl.pallas_call(
+    own_part, parts = pl.pallas_call(
         functools.partial(forward_kernel, strips, peers),
-        out_shape=[in_vmem((3, tokens, width), f32)] + [in_vmem((3, tokens, width), bf16)] * (strips - 1),
-        in_specs=specs(4 + peers),
-        out_specs=specs(strips),
+        out_shape=[in_vmem((3, tokens, width), f32), in_vmem((strips, 3, tokens, width), bf16)],
+        in_specs=specs(4),
+        out_specs=specs(2),
         scratch_shapes=[pltpu.VMEM((tokens, features), f32)] * 2,
         compiler_params=params,
         cost_estimate=pl.CostEstimate(
             flops=2 * tokens * weight_bytes // 2, bytes_accessed=weight_bytes, transcendentals=0
         ),
         name="forward",
-    )(inputs, cotangent, *arrived, held(gate), held(up), held(down))
-    terms = [exchange(partials[s], "narrow", strips, s) for s in range(1, strips)]
+    )(arrived, held(gate), held(up), held(down))
+    terms = swap_blocks(parts, "narrow")
 
     message, grads, other_grads = pl.pallas_call(
         functools.partial(middle_kernel, strips, groups, wide),
         out_shape=[
-            in_vmem((2 * tokens + 16, width), bf16),
+            in_vmem((strips, 2 * tokens + 16, width), bf16),
             in_vmem((SEQS, width), f32),
             in_vmem((SEQS, width), f32),
         ],
-        in_specs=specs(strips + 1) + specs(2, pltpu.SMEM),
+        in_specs=specs(3) + specs(2, pltpu.SMEM) + specs(2),
         out_specs=specs(3),
         scratch_shapes=[pltpu.VMEM((groups * SEQS, width), f32)],
         compiler_params=params,
         name="middle",
-    )(partials[0], *terms, ia3_scale[None, :], seq_ids, other_ids)
-    messages = [message] + [exchange(message, "narrow", strips, s) for s in range(1, strips)]
+    )(own_part, terms, ia3_scale[None, :], seq_ids, other_ids, held(gate), held(up))
+    messages = swap_blocks(message, "narrow")
     other_part = exchange(other_grads, "groups", groups, 1)
 
-    blocks = pl.pallas_call(
-        functools.partial(backward_kernel, strips, peers),
-        out_shape=[in_vmem((8, features), f32)] + [in_vmem((8, features), bf16)] * (peers - 1),
-        in_specs=specs(strips + 2),
-        out_specs=specs(peers),
-        scratch_shapes=[pltpu.VMEM((tokens, features), f32), pltpu.VMEM((8, features), f32)],
+    own_block, blocks = pl.pallas_call(
+        functools.partial(backward_kernel, strips, groups, wide),
+        out_shape=[in_vmem((8, features), f32), in_vmem((peers, 8, features), bf16)],
+        in_specs=specs(3),
+        out_specs=specs(2),
+        scratch_shapes=[pltpu.VMEM((tokens, features), f32), pltpu.VMEM((peers, 8, features), f32)],
         compiler_params=params,
         cost_estimate=pl.CostEstimate(
             flops=2 * tokens * weight_bytes // 3, bytes_accessed=weight_bytes * 2 // 3, transcendentals=0
         ),
         name="backward",
-    )(*messages, held(gate), held(up))
-    blocks = [blocks[0]] + [exchange(blocks[s], ("groups", "wide"), peers, s) for s in range(1, peers)]
+    )(messages, held(gate), held(up))
+    blocks = swap_blocks(blocks, ("groups", "wide"))
 
     input_grad, example_grads, norms = pl.pallas_call(
-        functools.partial(last_kernel, peers, wide),
+        functools.partial(last_kernel, groups, wide),
         out_shape=[
             jax.ShapeDtypeStruct((share, features), bf16),
             jax.ShapeDtypeStruct((SEQS, groups * width), f32),
             jax.ShapeDtypeStruct((SEQS,), f32),
         ],
-        in_specs=specs(peers + 2),
+        in_specs=specs(4),
         out_specs=specs(2) + specs(1, pltpu.SMEM),
         compiler_params=params,
         name="last",
-    )(*blocks, grads, other_part)
+    )(own_block, blocks, grads, other_part)
     return (example_grads, norms, input_grad)
 
 

time: 93.7 us -> 123 us (1.31)
  local copies, waits for them, and re-layouts: 9.11 us -> 37.4 us
  blocking collectives: 0 us -> 13 us
  starting transfers between devices: 30.3 us -> 20.7 us
  waiting for transfers between devices: 22.8 us -> 18.5 us
  Pallas kernels: 29.7 us -> 31 us
    unnamed x12 -> x20, local copies, waits for them, and re-layouts: 9.11 us -> 36.5 us
    ppermute x22 -> x2, starting transfers between devices: 30.3 us -> 4.03 us  [exchange(): return lax.ppermute(array, axes, [(i, i ^ step) for i in range(size)])]
    ppermute x22 -> x2, waiting for transfers between devices: 22.8 us -> 4.12 us  [exchange(): return lax.ppermute(array, axes, [(i, i ^ step) for i in range(size)])]
    all_to_all x0 -> x3, starting transfers between devices: none -> 16.7 us  [swap_blocks(): return lax.all_to_all(array, axes, 0, 0, tiled=True)]
    all_to_all x0 -> x3, waiting for transfers between devices: none -> 14.4 us  [swap_blocks(): return lax.all_to_all(array, axes, 0, 0, tiled=True)]
    all_to_all x0 -> x1, blocking collectives: none -> 13 us  [swap_blocks(): return lax.all_to_all(array, axes, 0, 0, tiled=True)]
  transfers between devices with their start and end apart: 22 -> 5, of which waited for: 7 -> 4; matrix products, arithmetic and copies ran while one was open for 0% -> 0% of each run, Pallas kernels for 13% -> 10%
where the time goes in v2:
time: 123 us; the launch traced here: 122 us
  local copies, waits for them, and re-layouts  37.4 us (30%)
  Pallas kernels  31 us (25%)
  starting transfers between devices  20.7 us (17%)
  waiting for transfers between devices  18.5 us (15%)
  blocking collectives  13 us (11%)
    unnamed x20, local copies, waits for them, and re-layouts  36.5 us
    all_to_all x3, starting transfers between devices, swap_blocks(): return lax.all_to_all(array, axes, 0, 0, tiled=True)  16.7 us
    all_to_all x3, waiting for transfers between devices, swap_blocks(): return lax.all_to_all(array, axes, 0, 0, tiled=True)  14.4 us
    all_to_all x1, blocking collectives, swap_blocks(): return lax.all_to_all(array, axes, 0, 0, tiled=True)  13 us
    pallas_call x1, Pallas kernels, shared(): pl.pallas_call(functools.partial(load_kernel, strips, groups), out_shape=...  12.1 us
    pallas_call x1, Pallas kernels, shared(): pl.pallas_call(functools.partial(forward_kernel, strips, peers), out_shap...  9.06 us
    pallas_call x1, Pallas kernels, shared(): pl.pallas_call(functools.partial(backward_kernel, strips, groups, wide),...  8.21 us
    ppermute x2, waiting for transfers between devices, exchange(): return lax.ppermute(array, axes, [(i, i ^ step) for i in range(size)])  4.12 us
  transfers between devices with their start and end apart: 5, of which 4 were waited for; matrix products, arithmetic and copies ran while one was open for 0% of the time, Pallas kernels for 10%

profile of v2, /device:TPU:0, one launch (start us, length us, event | category | flops | bytes accessed | tf_op | source)
XLA Modules:
  0.0 122.1 jit_solution(18420510363839333983)
XLA Ops:
  0.6 0.8 pad_maximum_fusion
  1.4 0.8 broadcast_in_dim.4
  2.3 7.3 %all-to-all-start = ((bf16[8,12,2048]{2,1,0:T(8,128)(2,1)}), bf16[8,12,2048]{2,1,0:T(8,128)(2,1)S(1)}, u32[]{:S(2)}, u32[]{:S(2)}) async-start(bf16[8,12,2048]{2,1,0:T(8,128)(2,1)} %broadcast_in_dim.4), calls=%async_computation | async-start | bytes 1048576 | tf_op jit(solution)/shard_map/all_to_all | solution.py:206
  9.6 0.0 copy-start.8
  9.6 12.1 %load_weights.1 = (bf16[4,2048,768]{2,1,0:T(8,128)(2,1)S(1)}, bf16[4,2048,768]{2,1,0:T(8,128)(2,1)S(1)}, bf16[4,768,2048]{2,1,0:T(8,128)(2,1)S(1)}) custom-call(bf16[2048,6144]{1,0:T(8,128)(2,1)} %gate.1, bf16[2048,6144]{1,0:T(8,128)(2,1)} %up.1, bf16[6144,2048]{1,0:T(8,128)(2,1)} %down.1), custom_call_target="tpu_custom_call" | custom-call | bytes 75497472 | tf_op jit(solution)/shard_map/load_weights/pallas_call | solution.py:224
  21.7 0.0 copy-start
  21.7 4.5 %copy-done = bf16[4,2048,768]{2,1,0:T(8,128)(2,1)} copy-done((bf16[4,2048,768]{2,1,0:T(8,128)(2,1)}, bf16[4,2048,768]{2,1,0:T(8,128)(2,1)S(1)}, u32[]{:S(2)}) %copy-start) | copy-done | bytes 12582936
  26.2 0.0 copy-start.3
  26.2 4.5 %copy-done.3 = bf16[4,2048,768]{2,1,0:T(8,128)(2,1)} copy-done((bf16[4,2048,768]{2,1,0:T(8,128)(2,1)}, bf16[4,2048,768]{2,1,0:T(8,128)(2,1)S(1)}, u32[]{:S(2)}) %copy-start.3) | copy-done | bytes 12582936
  30.7 0.0 copy-start.6
  30.7 4.6 %copy-done.6 = bf16[4,768,2048]{2,1,0:T(8,128)(2,1)} copy-done((bf16[4,768,2048]{2,1,0:T(8,128)(2,1)}, bf16[4,768,2048]{2,1,0:T(8,128)(2,1)S(1)}, u32[]{:S(2)}) %copy-start.6) | copy-done | bytes 12582936
  35.3 0.0 copy-start.9
  35.3 0.0 all-to-all-done.arrived
  35.3 0.0 copy-start.1
  35.3 4.6 %copy-done.1 = bf16[4,2048,768]{2,1,0:T(8,128)(2,1)S(1)} copy-done((bf16[4,2048,768]{2,1,0:T(8,128)(2,1)S(1)}, bf16[4,2048,768]{2,1,0:T(8,128)(2,1)}, u32[]{:S(2)}) %copy-start.1) | copy-done | bytes 12582936
  39.9 0.0 copy-start.4
  39.9 4.6 %copy-done.4 = bf16[4,2048,768]{2,1,0:T(8,128)(2,1)S(1)} copy-done((bf16[4,2048,768]{2,1,0:T(8,128)(2,1)S(1)}, bf16[4,2048,768]{2,1,0:T(8,128)(2,1)}, u32[]{:S(2)}) %copy-start.4) | copy-done | bytes 12582936
  44.5 0.0 copy-start.7
  44.5 4.6 %copy-done.7 = bf16[4,768,2048]{2,1,0:T(8,128)(2,1)S(1)} copy-done((bf16[4,768,2048]{2,1,0:T(8,128)(2,1)S(1)}, bf16[4,768,2048]{2,1,0:T(8,128)(2,1)}, u32[]{:S(2)}) %copy-start.7) | copy-done | bytes 12582936
  49.1 9.1 %forward.1 = (f32[3,48,768]{2,1,0:T(8,128)S(1)}, bf16[4,3,48,768]{3,2,1,0:T(8,128)(2,1)}) custom-call(bf16[8,12,2048]{2,1,0:T(8,128)(2,1)S(1)} %all-to-all-done.arrived, bf16[4,2048,768]{2,1,0:T(8,128)(2,1)S(1)} %copy-done.1, bf16[4,2048,768]{2,1,0:T(8,128)(2,1)S(1)} %copy-done.4, bf16[4,768,2048]{2,1,0:T(8,128)(2,1)S(1)} %copy-done.7), custom_call_target="tpu_custom_call" | custom-call | flops 1811939328 | bytes 37748736 | tf_op jit(solution)/shard_map/forward/pallas_call | solution.py:239
  58.1 3.5 %all-to-all-start.1 = ((bf16[4,3,48,768]{3,2,1,0:T(8,128)(2,1)}), bf16[4,3,48,768]{3,2,1,0:T(8,128)(2,1)S(1)}, u32[]{:S(2)}, u32[]{:S(2)}) async-start(bf16[4,3,48,768]{3,2,1,0:T(8,128)(2,1)} %get-tuple-element.20), calls=%async_computation.1 | async-start | bytes 1769472 | tf_op jit(solution)/shard_map/all_to_all | solution.py:206
  61.6 0.0 copy-done.9
  61.7 2.0 %collective-permute-start = (s32[24]{0:T(128)S(1)}, s32[24]{0:T(128)S(1)}, u32[]{:S(2)}, u32[]{:S(2)}) collective-permute-start(s32[24]{0:T(128)S(1)} %copy-done.9), channel_id=1, source_target_pairs={{0,16},{16,0},{1,17},{17,1},{2,18},{18,2},{3,19},{19,3},{4,20},{20... | collective-permute-start | bytes 296 | tf_op jit(solution)/shard_map/ppermute | solution.py:67
  63.7 1.6 %collective-permute-done.other_ids = s32[24]{0:T(128)S(1)} collective-permute-done((s32[24]{0:T(128)S(1)}, s32[24]{0:T(128)S(1)}, u32[]{:S(2)}, u32[]{:S(2)}) %collective-permute-start) | collective-permute-done | bytes 128 | tf_op jit(solution)/shard_map/ppermute | solution.py:67
  65.3 9.1 %all-to-all-done.1.arrived = bf16[4,3,48,768]{3,2,1,0:T(8,128)(2,1)S(1)} async-done(((bf16[4,3,48,768]{3,2,1,0:T(8,128)(2,1)}), bf16[4,3,48,768]{3,2,1,0:T(8,128)(2,1)S(1)}, u32[]{:S(2)}, u32[]{:S(2)}) %all-to-all-start.1) | async-done | bytes 884768 | tf_op jit(solution)/shard_map/all_to_all | solution.py:206
  74.3 0.0 copy-done.8
  74.3 0.0 copy-start.2
  74.3 4.6 %copy-done.2 = bf16[4,2048,768]{2,1,0:T(8,128)(2,1)S(1)} copy-done((bf16[4,2048,768]{2,1,0:T(8,128)(2,1)S(1)}, bf16[4,2048,768]{2,1,0:T(8,128)(2,1)}, u32[]{:S(2)}) %copy-start.2) | copy-done | bytes 12582936
  78.9 0.0 copy-start.5
  78.9 4.6 %copy-done.5 = bf16[4,2048,768]{2,1,0:T(8,128)(2,1)S(1)} copy-done((bf16[4,2048,768]{2,1,0:T(8,128)(2,1)S(1)}, bf16[4,2048,768]{2,1,0:T(8,128)(2,1)}, u32[]{:S(2)}) %copy-start.5) | copy-done | bytes 12582936
  83.5 1.0 middle.1
  84.4 13.0 %all_to_all.20.messages = bf16[4,112,768]{2,1,0:T(8,128)(2,1)S(1)} all-to-all(bf16[4,112,768]{2,1,0:T(8,128)(2,1)S(1)} %get-tuple-element.21), channel_id=1, replica_groups=mesh['groups'=2,'wide'=4,'narrow'=4] {'narrow'}, dimensions={0} | all-to-all | bytes 1376256 | tf_op jit(solution)/shard_map/all_to_all | solution.py:206
  97.4 8.2 %backward.1 = (f32[8,2048]{1,0:T(8,128)S(1)}, bf16[8,8,2048]{2,1,0:T(8,128)(2,1)}) custom-call(bf16[4,112,768]{2,1,0:T(8,128)(2,1)S(1)} %all_to_all.20.messages, bf16[4,2048,768]{2,1,0:T(8,128)(2,1)S(1)} %copy-done.2, bf16[4,2048,768]{2,1,0:T(8,128)(2,1)S(1)} %copy-done.5), custom_call_target="tpu_custom_call" | custom-call | flops 1207959552 | bytes 25165824 | tf_op jit(solution)/shard_map/backward/pallas_call | solution.py:269
  105.6 5.9 %all-to-all-start.3 = ((bf16[8,8,2048]{2,1,0:T(8,128)(2,1)}), bf16[8,8,2048]{2,1,0:T(8,128)(2,1)S(1)}, u32[]{:S(2)}, u32[]{:S(2)}) async-start(bf16[8,8,2048]{2,1,0:T(8,128)(2,1)} %get-tuple-element.23), calls=%async_computation.3 | async-start | bytes 524288 | tf_op jit(solution)/shard_map/all_to_all | solution.py:206
  111.5 2.0 %collective-permute-start.1 = (f32[4,768]{1,0:T(4,128)S(1)}, f32[4,768]{1,0:T(4,128)S(1)}, u32[]{:S(2)}, u32[]{:S(2)}) collective-permute-start(f32[4,768]{1,0:T(4,128)S(1)} %get-tuple-element.25), channel_id=1, source_target_pairs={{0,16},{16,0},{1,17},{17,1},{2,18},{18,2},{3,19},{19,3},{4,20},{20... | collective-permute-start | bytes 36872 | tf_op jit(solution)/shard_map/ppermute | solution.py:67
  113.6 2.5 %collective-permute-done.1.other = f32[4,768]{1,0:T(4,128)S(1)} collective-permute-done((f32[4,768]{1,0:T(4,128)S(1)}, f32[4,768]{1,0:T(4,128)S(1)}, u32[]{:S(2)}, u32[]{:S(2)}) %collective-permute-start.1) | collective-permute-done | bytes 12320 | tf_op jit(solution)/shard_map/ppermute | solution.py:67
  116.1 5.3 %all-to-all-done.3.blocks = bf16[8,8,2048]{2,1,0:T(8,128)(2,1)S(1)} async-done(((bf16[8,8,2048]{2,1,0:T(8,128)(2,1)}), bf16[8,8,2048]{2,1,0:T(8,128)(2,1)S(1)}, u32[]{:S(2)}, u32[]{:S(2)}) %all-to-all-start.3) | async-done | bytes 262176 | tf_op jit(solution)/shard_map/all_to_all | solution.py:206
  121.4 0.7 last.1
Async XLA Ops:
  2.3 33.1 %all-to-all-start = ((bf16[8,12,2048]{2,1,0:T(8,128)(2,1)}), bf16[8,12,2048]{2,1,0:T(8,128)(2,1)S(1)}, u32[]{:S(2)}, u32[]{:S(2)}) async-start(bf16[8,12,2048]{2,1,0:T(8,128)(2,1)} %broadcast_in_dim.4), calls=%async_computation | async-start | bytes 1048576 | tf_op jit(solution)/shard_map/all_to_all | solution.py:206
  9.6 64.8 %copy-start.8 = (f32[6144]{0:T(1024)S(1)}, f32[6144]{0:T(1024)}, u32[]{:S(2)}) copy-start(f32[6144]{0:T(1024)} %param.12) | copy-start | bytes 73732
  21.7 4.5 %copy-start = (bf16[4,2048,768]{2,1,0:T(8,128)(2,1)}, bf16[4,2048,768]{2,1,0:T(8,128)(2,1)S(1)}, u32[]{:S(2)}) copy-start(bf16[4,2048,768]{2,1,0:T(8,128)(2,1)S(1)} %get-tuple-element.16.gate) | copy-start | bytes 37748740
  26.2 4.5 %copy-start.3 = (bf16[4,2048,768]{2,1,0:T(8,128)(2,1)}, bf16[4,2048,768]{2,1,0:T(8,128)(2,1)S(1)}, u32[]{:S(2)}) copy-start(bf16[4,2048,768]{2,1,0:T(8,128)(2,1)S(1)} %get-tuple-element.17.up) | copy-start | bytes 37748740
  30.7 4.6 %copy-start.6 = (bf16[4,768,2048]{2,1,0:T(8,128)(2,1)}, bf16[4,768,2048]{2,1,0:T(8,128)(2,1)S(1)}, u32[]{:S(2)}) copy-start(bf16[4,768,2048]{2,1,0:T(8,128)(2,1)S(1)} %get-tuple-element.18.down) | copy-start | bytes 37748740
  35.3 26.3 %copy-start.9 = (s32[24]{0:T(128)S(1)}, s32[24]{0:T(128)}, u32[]{:S(2)}) copy-start(s32[24]{0:T(128)} %ids.1) | copy-start | bytes 292
  35.3 4.6 %copy-start.1 = (bf16[4,2048,768]{2,1,0:T(8,128)(2,1)S(1)}, bf16[4,2048,768]{2,1,0:T(8,128)(2,1)}, u32[]{:S(2)}) copy-start(bf16[4,2048,768]{2,1,0:T(8,128)(2,1)} %copy-done) | copy-start | bytes 37748740
  39.9 4.6 %copy-start.4 = (bf16[4,2048,768]{2,1,0:T(8,128)(2,1)S(1)}, bf16[4,2048,768]{2,1,0:T(8,128)(2,1)}, u32[]{:S(2)}) copy-start(bf16[4,2048,768]{2,1,0:T(8,128)(2,1)} %copy-done.3) | copy-start | bytes 37748740
  44.5 4.6 %copy-start.7 = (bf16[4,768,2048]{2,1,0:T(8,128)(2,1)S(1)}, bf16[4,768,2048]{2,1,0:T(8,128)(2,1)}, u32[]{:S(2)}) copy-start(bf16[4,768,2048]{2,1,0:T(8,128)(2,1)} %copy-done.6) | copy-start | bytes 37748740
  58.1 16.2 %all-to-all-start.1 = ((bf16[4,3,48,768]{3,2,1,0:T(8,128)(2,1)}), bf16[4,3,48,768]{3,2,1,0:T(8,128)(2,1)S(1)}, u32[]{:S(2)}, u32[]{:S(2)}) async-start(bf16[4,3,48,768]{3,2,1,0:T(8,128)(2,1)} %get-tuple-element.20), calls=%async_computation.1 | async-start | bytes 1769472 | tf_op jit(solution)/shard_map/all_to_all | solution.py:206
  61.7 3.6 %collective-permute-start = (s32[24]{0:T(128)S(1)}, s32[24]{0:T(128)S(1)}, u32[]{:S(2)}, u32[]{:S(2)}) collective-permute-start(s32[24]{0:T(128)S(1)} %copy-done.9), channel_id=1, source_target_pairs={{0,16},{16,0},{1,17},{17,1},{2,18},{18,2},{3,19},{19,3},{4,20},{20... | collective-permute-start | bytes 296 | tf_op jit(solution)/shard_map/ppermute | solution.py:67
  74.3 4.6 %copy-start.2 = (bf16[4,2048,768]{2,1,0:T(8,128)(2,1)S(1)}, bf16[4,2048,768]{2,1,0:T(8,128)(2,1)}, u32[]{:S(2)}) copy-start(bf16[4,2048,768]{2,1,0:T(8,128)(2,1)} %copy-done) | copy-start | bytes 37748740
  78.9 4.6 %copy-start.5 = (bf16[4,2048,768]{2,1,0:T(8,128)(2,1)S(1)}, bf16[4,2048,768]{2,1,0:T(8,128)(2,1)}, u32[]{:S(2)}) copy-start(bf16[4,2048,768]{2,1,0:T(8,128)(2,1)} %copy-done.3) | copy-start | bytes 37748740
  105.6 15.8 %all-to-all-start.3 = ((bf16[8,8,2048]{2,1,0:T(8,128)(2,1)}), bf16[8,8,2048]{2,1,0:T(8,128)(2,1)S(1)}, u32[]{:S(2)}, u32[]{:S(2)}) async-start(bf16[8,8,2048]{2,1,0:T(8,128)(2,1)} %get-tuple-element.23), calls=%async_computation.3 | async-start | bytes 524288 | tf_op jit(solution)/shard_map/all_to_all | solution.py:206
  111.5 4.5 %collective-permute-start.1 = (f32[4,768]{1,0:T(4,128)S(1)}, f32[4,768]{1,0:T(4,128)S(1)}, u32[]{:S(2)}, u32[]{:S(2)}) collective-permute-start(f32[4,768]{1,0:T(4,128)S(1)} %get-tuple-element.25), channel_id=1, source_target_pairs={{0,16},{16,0},{1,17},{17,1},{2,18},{18,2},{3,19},{19,3},{4,20},{20... | collective-permute-start | bytes 36872 | tf_op jit(solution)/shard_map/ppermute | solution.py:67

commit v3 on v0

--- a/solution.py
+++ b/solution.py
@@ -1,9 +1,14 @@
+import functools
+
 import jax
 import jax.numpy as jnp
 from jax import lax
+from jax.experimental import pallas as pl
+from jax.experimental.pallas import tpu as pltpu
 from jax.sharding import PartitionSpec as P
 
 SEQS = 4
+KERNEL_VMEM = 6 << 20
 
 
 def contract_rows(left, right):
@@ -16,7 +21,7 @@
     sigmoid_gate = jax.nn.sigmoid(gate_pre)
     activation = gate_pre * sigmoid_gate
     hidden = activation * up_pre
-    scaled = scale_part[None, :] * mid_grad
+    scaled = scale_part * mid_grad
     d_up = (scaled * activation).astype(jnp.bfloat16)
     d_gate = (scaled * up_pre * sigmoid_gate * (1.0 + gate_pre * (1.0 - sigmoid_gate))).astype(
         jnp.bfloat16
@@ -24,7 +29,7 @@
     return (hidden * mid_grad, d_gate, d_up)
 
 
-def local(inputs, cotangent, gate_weight, up_weight, down_weight, ia3_scale, seq_ids):
+def whole_block(inputs, cotangent, gate_weight, up_weight, down_weight, ia3_scale, seq_ids):
     panel_inputs = lax.all_gather(inputs, "wide", axis=0, tiled=True)
     panel_cotangent = lax.all_gather(cotangent, "wide", axis=0, tiled=True)
     gate_part = jnp.dot(panel_inputs, gate_weight, preferred_element_type=jnp.float32)
@@ -41,7 +46,7 @@
         lax.psum_scatter(mid_part, "narrow", scatter_dimension=1, tiled=True),
     )
     scale_part = lax.dynamic_slice_in_dim(ia3_scale, position * quarter, quarter, 0)
-    product, d_gate, d_up = local_grads(gate_pre, up_pre, mid_grad, scale_part)
+    product, d_gate, d_up = local_grads(gate_pre, up_pre, mid_grad, scale_part[None, :])
     example_grads = jnp.dot(onehot_full, product, precision=lax.Precision.HIGHEST)
     whole_gate, whole_up = (
         lax.all_gather(d_gate, "narrow", axis=1, tiled=True),
@@ -56,6 +61,409 @@
         tiled=True,
     ).astype(jnp.bfloat16)
     return (example_grads, grad_norms, input_grad)
+
+
+def exchange(array, axis, step):
+    return lax.ppermute(array, axis, [(i, i ^ step) for i in range(lax.axis_size(axis))])
+
+
+def held(array):
+    return pltpu.with_memory_space_constraint(array, pltpu.VMEM)
+
+
+def call(body, name, outs, args, spaces=None, scratch=(), out_spaces=None):
+    spaces, out_spaces = spaces or {}, out_spaces or {}
+    many = isinstance(outs, list)
+    out_specs = [
+        pl.BlockSpec(memory_space=out_spaces.get(i, pltpu.VMEM)) for i in range(len(outs) if many else 1)
+    ]
+    return pl.pallas_call(
+        body,
+        out_shape=outs,
+        in_specs=[pl.BlockSpec(memory_space=spaces.get(i, pltpu.VMEM)) for i in range(len(args))],
+        out_specs=out_specs if many else out_specs[0],
+        scratch_shapes=list(scratch),
+        compiler_params=pltpu.CompilerParams(vmem_limit_bytes=KERNEL_VMEM),
+        cost_estimate=pl.CostEstimate(flops=1000, bytes_accessed=1000, transcendentals=0),
+        name=name,
+    )(*args)
+
+
+def pack_kernel(inputs, cotangent, out, stage):
+    share, features = inputs.shape
+    half = features // 2
+    for i, ref in enumerate((inputs, cotangent)):
+        rows = ref[...].astype(jnp.float32)
+        for j in range(2):
+            stage[(2 * i + j) * share : (2 * i + j + 1) * share, :] = rows[:, j * half : (j + 1) * half]
+    for k in range(out.shape[0]):
+        out[k] = stage[8 * k : 8 * k + 8, :].astype(jnp.bfloat16)
+
+
+def relay_kernel(share, *refs):
+    blocks, ids, out = refs[:-3], refs[-3], refs[-1]
+    slabs = blocks[0].shape[0]
+    position = lax.axis_index("wide")
+    for i, block in enumerate(blocks):
+        out[i * slabs : (i + 1) * slabs] = block[...]
+    row = lax.broadcasted_iota(jnp.int32, (8, 128), 0)
+    keys = []
+    for k in range(len(blocks) * share // 8):
+        key = jnp.zeros((8, 128), jnp.int32)
+        for r in range(8):
+            block, j = divmod(8 * k + r, share)
+            key = jnp.where(row == r, ids[(position ^ block) * share + j], key)
+        keys.append(key.astype(jnp.float32))
+    keys.append(jnp.zeros((8, out.shape[2] - 128 * len(keys)), jnp.float32))
+    out[len(blocks) * slabs] = jnp.concatenate(keys, axis=1).astype(jnp.bfloat16)
+
+
+def load_kernel(strip, groups, *refs):
+    gate, up, down = refs[:3]
+    gate_held, up_held, down_held, sem = refs[-4:]
+    start_load(strip, groups, (gate, up, down), (gate_held, up_held, down_held), sem)()
+
+
+def start_load(strip, groups, sources, targets, sem):
+    width = targets[0].shape[1]
+    owner = lax.axis_index("narrow") ^ strip
+    start = pl.multiple_of((owner * groups + lax.axis_index("groups")) * width, width)
+    gate, up, down = sources
+    copies = [
+        pltpu.make_async_copy(gate.at[:, pl.ds(start, width)], targets[0], sem.at[0]),
+        pltpu.make_async_copy(up.at[:, pl.ds(start, width)], targets[1], sem.at[1]),
+        pltpu.make_async_copy(down.at[pl.ds(start, width), :], targets[2], sem.at[2]),
+    ]
+    for copy in copies:
+        copy.start()
+
+    def wait():
+        for copy in copies:
+            copy.wait()
+
+    return wait
+
+
+def strip_parts(tokens, cotans, weights):
+    gate, up, down = weights
+    tokens, cotans = tokens[...], cotans[...]
+    yield jnp.dot(tokens, gate[...], preferred_element_type=jnp.float32)
+    yield jnp.dot(tokens, up[...], preferred_element_type=jnp.float32)
+    yield contract_rows(cotans, down[...])
+
+
+def first_kernel(share, *refs):
+    relayed, other, gate, up, down = refs[:5]
+    tokens, cotans, part, rows, cots = refs[-5:]
+    slabs, half = 4 * share // 8, rows.shape[1] // 2
+    count = (relayed.shape[0] - 1) // slabs
+    for side, source in enumerate((relayed, other)):
+        for i in range(count):
+            packed = source[i * slabs : (i + 1) * slabs].astype(jnp.float32).reshape(4 * share, half)
+            at = (side * count + i) * share
+            for j, target in enumerate((rows, rows, cots, cots)):
+                span = slice((j % 2) * half, (j % 2 + 1) * half)
+                target[at : at + share, span] = packed[j * share : (j + 1) * share]
+    tokens[...] = rows[...].astype(jnp.bfloat16)
+    cotans[...] = cots[...].astype(jnp.bfloat16)
+    forward_kernel(tokens, cotans, gate, up, down, part)
+
+
+def forward_kernel(tokens, cotans, gate, up, down, out):
+    for i, part in enumerate(strip_parts(tokens, cotans, (gate, up, down))):
+        out[i] = part.astype(out.dtype)
+
+
+def forward_add_kernel(tokens, cotans, gate, up, down, arrived, out):
+    for i, part in enumerate(strip_parts(tokens, cotans, (gate, up, down))):
+        out[i] = (part + arrived[i].astype(jnp.float32)).astype(out.dtype)
+
+
+def forward_load_kernel(strip, groups, tokens, cotans, gate, up, down, next_gate, next_up, next_down, *refs):
+    out, targets, sem = refs[-5], refs[-4:-1], refs[-1]
+    wait = start_load(strip, groups, (next_gate, next_up, next_down), targets, sem)
+    forward_kernel(tokens, cotans, gate, up, down, out)
+    wait()
+
+
+def middle_kernel(groups, *refs):
+    own, arrived, crossed, scale, relayed, other_relayed = refs[:6]
+    message, grads, other_grads, stage = refs[-4:]
+    _, tokens, width = own.shape
+    narrow, group = lax.axis_index("narrow"), lax.axis_index("groups")
+    sums = [own[i] + arrived[i].astype(jnp.float32) + crossed[i].astype(jnp.float32) for i in range(3)]
+    start = pl.multiple_of((narrow * groups + group) * width, width)
+    product, d_gate, d_up = local_grads(*sums, scale[:, pl.ds(start, width)])
+    message[0:tokens, :] = d_gate
+    message[tokens : 2 * tokens, :] = d_up
+    half = tokens // groups
+    for side, (source, target) in enumerate(((relayed, grads), (other_relayed, other_grads))):
+        marks = source[source.shape[0] - 1].astype(jnp.float32)
+        seq = jnp.concatenate(
+            [
+                jnp.concatenate([marks[:, k * 128 : (k + 1) * 128]] * (width // 128), axis=1)
+                for k in range(half // 8)
+            ],
+            axis=0,
+        )
+        part = product[side * half : (side + 1) * half]
+        for e in range(SEQS):
+            total = jnp.sum(jnp.where(seq == float(e), part, 0.0), axis=0, keepdims=True)
+            target[e : e + 1, :] = total
+            stage[side * SEQS + e : side * SEQS + e + 1, :] = total
+    every = stage[...]
+    squares = jnp.broadcast_to(jnp.sum(every * every, axis=1, keepdims=True), every.shape)
+    high = squares.astype(jnp.bfloat16).astype(jnp.float32)
+    message[2 * tokens :, :] = jnp.concatenate([high, squares - high], axis=0).astype(jnp.bfloat16)
+
+
+TILE = 512
+
+
+def backward_part(message, gate, up, start):
+    tokens = (message.shape[0] - 16) // 2
+    gate_term = contract_rows(message[0:tokens, :], gate[start : start + TILE, :])
+    return gate_term + contract_rows(message[tokens : 2 * tokens, :], up[start : start + TILE, :])
+
+
+def backward_first_kernel(message, gate, up, total):
+    for start in range(0, total.shape[1], TILE):
+        total[:, start : start + TILE] = backward_part(message, gate, up, start)
+
+
+def backward_next_kernel(message, gate, up, before, total):
+    for start in range(0, total.shape[1], TILE):
+        total[:, start : start + TILE] = before[:, start : start + TILE] + backward_part(message, gate, up, start)
+
+
+def split_high(values):
+    high = values.astype(jnp.bfloat16).astype(jnp.float32)
+    return high, values - high
+
+
+def backward_last_kernel(message, gate, up, before, *refs):
+    others, other_grads = refs[:3], refs[3]
+    own, own_tail, send = refs[4:7]
+    half, features = own.shape
+    for start in range(0, features, TILE):
+        span = slice(start, start + TILE)
+        total = before[:, span] + backward_part(message, gate, up, start)
+        own[:, span] = total[:half]
+        for k in range(half // 8):
+            send[k, :, span] = total[half + 8 * k : half + 8 * k + 8].astype(jnp.bfloat16)
+    squares = sum(ref[ref.shape[0] - 16 :, 0:128].astype(jnp.float32) for ref in (message,) + others)
+    high, low = split_high(squares[0:8] + squares[8:16])
+    own_tail[...] = jnp.zeros_like(own_tail)
+    width = other_grads.shape[1]
+    for i, rows in enumerate(split_high(other_grads[...])):
+        own_tail[i * SEQS : (i + 1) * SEQS, 0:width] = rows
+    first = features - 8 * 128
+    for k in range(8):
+        span = slice(first + k * 128, first + (k + 1) * 128)
+        own_tail[0:1, span] = high[k : k + 1]
+        own_tail[1:2, span] = low[k : k + 1]
+    send[half // 8] = own_tail[...].astype(jnp.bfloat16)
+
+
+def combine_kernel(share, own, own_tail, arrived, grads, *refs):
+    example_grads, own_block, sends, total = refs[0], refs[1], refs[2:-1], refs[-1]
+    half, features = own.shape
+    width = grads.shape[1]
+    group = lax.axis_index("groups")
+    slabs = half // 8
+    for k in range(slabs):
+        total[8 * k : 8 * k + 8, :] = own[8 * k : 8 * k + 8, :] + arrived[k].astype(jnp.float32)
+    tail = arrived[slabs].astype(jnp.float32)
+    other = tail[0:SEQS, 0:width] + tail[SEQS : 2 * SEQS, 0:width]
+    example_grads[:, pl.ds(pl.multiple_of(group * width, width), width)] = grads[...]
+    example_grads[:, pl.ds(pl.multiple_of((1 - group) * width, width), width)] = other
+    first, lanes = features - 8 * 128, SEQS * 128
+    here = own_tail[0:1, first : first + lanes] + own_tail[1:2, first : first + lanes]
+    there = tail[0:1, first + lanes : first + 2 * lanes] + tail[1:2, first + lanes : first + 2 * lanes]
+    high, low = split_high(here + there)
+    for i, target in enumerate((own_block,) + tuple(sends)):
+        rows = total[i * share : (i + 1) * share, :]
+        if i == 0:
+            target[...] = jnp.zeros_like(target)
+            target[0:share, :] = rows
+            target[6:7, 0:lanes] = high
+            target[7:8, 0:lanes] = low
+        else:
+            total[half : half + share, :] = rows
+            if i == 1:
+                total[half + 6 : half + 8, :] = jnp.zeros((2, features), jnp.float32)
+                total[half + 6 : half + 7, 0:lanes] = high
+                total[half + 7 : half + 8, 0:lanes] = low
+            target[...] = total[half : half + 8, :].astype(jnp.bfloat16)
+
+
+def last_kernel(*refs):
+    own, arrived, (input_grad, norms) = refs[0], refs[1:-2], refs[-2:]
+    total = own[...] + sum(ref[...].astype(jnp.float32) for ref in arrived)
+    input_grad[...] = total[0 : input_grad.shape[0]].astype(jnp.bfloat16)
+    roots = jnp.sqrt(total[6:7, 0 : SEQS * 128] + total[7:8, 0 : SEQS * 128])
+    for e in range(SEQS):
+        norms[e] = jnp.max(roots[:, e * 128 : (e + 1) * 128])
+
+
+def shared(inputs, cotangent, gate_weight, up_weight, down_weight, ia3_scale, seq_ids):
+    groups, wide, strips = lax.axis_size("groups"), lax.axis_size("wide"), lax.axis_size("narrow")
+    share, features = inputs.shape
+    width = gate_weight.shape[1] // (strips * groups)
+    half = share * wide
+    tokens = half * groups
+    f32, bf16 = jnp.float32, jnp.bfloat16
+    slabs = 4 * share // 8
+    weights = tuple(
+        pltpu.with_memory_space_constraint(weight, pltpu.HBM)
+        for weight in (gate_weight, up_weight, down_weight)
+    )
+    weight_shapes = [
+        pltpu.VMEM((features, width), bf16),
+        pltpu.VMEM((features, width), bf16),
+        pltpu.VMEM((width, features), bf16),
+    ]
+    load_sem = [pltpu.SemaphoreType.DMA((3,))]
+
+    def load(strip, after=()):
+        args = weights + tuple(after)
+        return call(
+            functools.partial(load_kernel, strip, groups),
+            f"load_{strip}",
+            weight_shapes,
+            args,
+            {i: pltpu.HBM if i < 3 else pl.ANY for i in range(len(args))},
+            load_sem,
+        )
+
+    def hold(strip):
+        return [held(array) for array in kept[strip]]
+
+    kept = {}
+    packed = call(
+        pack_kernel,
+        "pack",
+        pltpu.VMEM((slabs, 8, features // 2), bf16),
+        [pltpu.with_memory_space_constraint(array, pltpu.HBM) for array in (inputs, cotangent)],
+        scratch=[pltpu.VMEM((4 * share, features // 2), f32)],
+    )
+    blocks = [packed] + [exchange(packed, "wide", s) for s in range(1, wide)]
+    kept[3] = load(3)
+    relayed = call(
+        functools.partial(relay_kernel, share),
+        "relay",
+        pltpu.VMEM((wide * slabs + 1, 8, features // 2), bf16),
+        blocks + [seq_ids] + hold(3)[:1],
+        {wide: pltpu.SMEM},
+    )
+    other_relayed = exchange(relayed, "groups", 1)
+    kept[2] = load(2, [relayed])
+    kept[1] = load(1, [relayed])
+
+    tokens_all, cotans_all, diagonal = call(
+        functools.partial(first_kernel, share),
+        "forward_3",
+        [pltpu.VMEM((tokens, features), bf16)] * 2 + [pltpu.VMEM((3, tokens, width), bf16)],
+        [relayed, other_relayed] + hold(3) + hold(2)[:1] + hold(1)[:1],
+        scratch=[pltpu.VMEM((tokens, features), f32)] * 2,
+    )
+    panel = [tokens_all, cotans_all]
+    diagonal = exchange(diagonal, "narrow", 1)
+    crossing = call(
+        forward_add_kernel,
+        "forward_2",
+        pltpu.VMEM((3, tokens, width), bf16),
+        panel + hold(2) + [diagonal],
+    )
+    crossed = exchange(crossing, "narrow", 2)
+    near, *kept[0] = call(
+        functools.partial(forward_load_kernel, 0, groups),
+        "forward_1",
+        [pltpu.VMEM((3, tokens, width), bf16)] + weight_shapes,
+        panel + hold(1) + list(weights) + [held(crossing)],
+        {5: pltpu.HBM, 6: pltpu.HBM, 7: pltpu.HBM},
+        load_sem,
+    )
+    near = exchange(near, "narrow", 1)
+    own_part = call(
+        forward_kernel, "forward_0", pltpu.VMEM((3, tokens, width), f32), panel + hold(0)
+    )
+
+    resident = [array for s in range(strips) for array in hold(s)[:2]]
+    message, grads, other_grads = call(
+        functools.partial(middle_kernel, groups),
+        "middle",
+        [
+            pltpu.VMEM((2 * tokens + 16, width), bf16),
+            pltpu.VMEM((SEQS, width), f32),
+            pltpu.VMEM((SEQS, width), f32),
+        ],
+        [own_part, near, crossed, ia3_scale[None, :], relayed, other_relayed] + resident,
+        scratch=[pltpu.VMEM((groups * SEQS, width), f32)],
+    )
+
+    total = pltpu.VMEM((tokens, features), f32)
+    message_1 = exchange(message, "narrow", 1)
+    message_2 = exchange(message, "narrow", 2)
+    sums = call(backward_first_kernel, "backward_0", total, [message] + hold(0)[:2])
+    sums = call(backward_next_kernel, "backward_1", total, [message_1] + hold(1)[:2] + [sums])
+    message_2, sums = lax.optimization_barrier((message_2, sums))
+    message_3 = exchange(message_2, "narrow", 1)
+    sums = call(backward_next_kernel, "backward_2", total, [message_2] + hold(2)[:2] + [sums])
+    own, own_tail, send = call(
+        backward_last_kernel,
+        "backward_3",
+        [
+            pltpu.VMEM((half, features), f32),
+            pltpu.VMEM((8, features), f32),
+            pltpu.VMEM((half // 8 + 1, 8, features), bf16),
+        ],
+        [message_3] + hold(3)[:2] + [sums, message, message_1, message_2, other_grads],
+    )
+    arrived = exchange(send, "groups", 1)
+    example_grads, own_block, *sends = call(
+        functools.partial(combine_kernel, share),
+        "combine",
+        [jax.ShapeDtypeStruct((SEQS, groups * width), f32), pltpu.VMEM((8, features), f32)]
+        + [pltpu.VMEM((8, features), bf16)] * (wide - 1),
+        [own, own_tail, arrived, grads],
+        scratch=[pltpu.VMEM((half + 8, features), f32)],
+    )
+    arrived = [exchange(block, "wide", s + 1) for s, block in enumerate(sends)]
+    input_grad, norms = call(
+        last_kernel,
+        "last",
+        [jax.ShapeDtypeStruct((share, features), bf16), jax.ShapeDtypeStruct((SEQS,), f32)],
+        [own_block] + arrived,
+        out_spaces={1: pltpu.SMEM},
+    )
+    return (example_grads, norms, input_grad)
+
+
+def power_of_two(number):
+    return number & (number - 1) == 0
+
+
+def local(inputs, cotangent, gate_weight, up_weight, down_weight, ia3_scale, seq_ids):
+    groups, wide, narrow = lax.axis_size("groups"), lax.axis_size("wide"), lax.axis_size("narrow")
+    share, (features, hidden) = inputs.shape[0], gate_weight.shape
+    width = hidden // (narrow * groups)
+    fits = (
+        groups == 2
+        and narrow == 4
+        and power_of_two(wide)
+        and hidden % (narrow * groups * 256) == 0
+        and features % TILE == 0
+        and features >= 2048
+        and width <= features - 1024
+        and share <= 6
+        and share % 2 == 0
+        and (share * wide) % 8 == 0
+        and share * wide <= 64
+        and 3 * features * hidden // groups * 2 <= 40 << 20
+    )
+    plan = shared if fits else whole_block
+    return plan(inputs, cotangent, gate_weight, up_weight, down_weight, ia3_scale, seq_ids)
 
 
 def solution(mesh):

time: 200 us -> 69.1 us (0.35)
  blocking collectives: 85.6 us -> 0 us
  matrix products: 58.1 us -> 0 us
  Pallas kernels: 0 us -> 34.6 us
  waiting for transfers between devices: 35.3 us -> 18 us
  between operations: 14.5 us -> 0.81 us
  starting transfers between devices: 2.1 us -> 15.6 us
  local copies, waits for them, and re-layouts: 2.78 us -> 0.01 us
    dot_general x6 -> x0, matrix products: 58.1 us -> none  [the longest x3 35.4 us: contract_rows(): lax.dot_general(left, right, (((1,), (1,)), ((), ())), preferred_element_...]
    all_gather x4 -> x0, blocking collectives: 41 us -> none  [the longest x1 15.3 us: local(): panel_cotangent = lax.all_gather(cotangent, 'wide', axis=0, tiled=True)]
    reduce_scatter x3 -> x0, waiting for transfers between devices: 35.2 us -> none  [the longest x1 24.6 us: local(): lax.psum_scatter(gate_part, 'narrow', scatter_dimension=1, tiled=True)]
    pallas_call x0 -> x16, Pallas kernels: none -> 34.6 us  [call(): pl.pallas_call(body, out_shape=outs, in_specs=[pl.BlockSpec(memory_space=...]
    psum x1 -> x0, blocking collectives: 29.5 us -> none  [local(): lax.psum(jnp.sum(example_grads * example_grads, axis=1), ('wide', 'narrow'))]
    ppermute x0 -> x14, waiting for transfers between devices: none -> 18 us  [exchange(): lax.ppermute(array, axis, [(i, i ^ step) for i in range(lax.axis_size(axi...]
    ppermute x0 -> x14, starting transfers between devices: none -> 15.6 us  [exchange(): lax.ppermute(array, axis, [(i, i ^ step) for i in range(lax.axis_size(axi...]
    unnamed x1 -> x0, blocking collectives: 15.1 us -> none
  transfers between devices with their start and end apart: 4 -> 14, of which waited for: 2 -> 7; matrix products, arithmetic and copies ran while one was open for 12% -> 0% of each run, Pallas kernels for 0% -> 28%
where the time goes in v3:
time: 69.1 us; the launch traced here: 69 us
  Pallas kernels  34.6 us (50%)
  waiting for transfers between devices  18 us (26%)
  starting transfers between devices  15.6 us (23%)
  between operations  0.81 us (1%)
    pallas_call x16, Pallas kernels, call(): pl.pallas_call(body, out_shape=outs, in_specs=[pl.BlockSpec(memory_space=...  34.6 us
    ppermute x14, waiting for transfers between devices, exchange(): lax.ppermute(array, axis, [(i, i ^ step) for i in range(lax.axis_size(axi...  18 us
    ppermute x14, starting transfers between devices, exchange(): lax.ppermute(array, axis, [(i, i ^ step) for i in range(lax.axis_size(axi...  15.6 us
  transfers between devices with their start and end apart: 14, of which 7 were waited for; matrix products, arithmetic and copies ran while one was open for 0% of the time, Pallas kernels for 28%

profile of v3, /device:TPU:0, one launch (start us, length us, event | category | flops | bytes accessed | tf_op | source)
XLA Modules:
  0.0 69.0 jit_solution(5988761328801401178)
XLA Ops:
  0.6 0.8 %pack.1.refs_0_ = bf16[3,8,1024]{2,1,0:T(8,128)(2,1)S(1)} custom-call(bf16[6,2048]{1,0:T(8,128)(2,1)} %inputs.1, bf16[6,2048]{1,0:T(8,128)(2,1)} %cotangent.1), custom_call_target="tpu_custom_call" | custom-call | flops 1000 | bytes 1000 | tf_op jit(solution)/shard_map/pack/pallas_call | solution.py:80
  1.4 0.0 copy-start.1
  1.4 3.1 %collective-permute-start = (bf16[3,8,1024]{2,1,0:T(8,128)(2,1)S(1)}, bf16[3,8,1024]{2,1,0:T(8,128)(2,1)S(1)}, u32[]{:S(2)}, u32[]{:S(2)}) collective-permute-start(bf16[3,8,1024]{2,1,0:T(8,128)(2,1)S(1)} %pack.1.refs_0_), channel_id=1, source_target_pairs={{0,4},{4,0},{8,12},{12,8},{1,5},{5,1},{9,13},{13,9},{2,6},{6,2},{1... | collective-permute-start | bytes 147464 | tf_op jit(solution)/shard_map/ppermute | solution.py:67
  4.5 2.6 %collective-permute-start.1 = (bf16[3,8,1024]{2,1,0:T(8,128)(2,1)S(1)}, bf16[3,8,1024]{2,1,0:T(8,128)(2,1)S(1)}, u32[]{:S(2)}, u32[]{:S(2)}) collective-permute-start(bf16[3,8,1024]{2,1,0:T(8,128)(2,1)S(1)} %pack.1.refs_0_), channel_id=1, source_target_pairs={{0,8},{4,12},{8,0},{12,4},{1,9},{5,13},{9,1},{13,5},{2,10},{6,14},... | collective-permute-start | bytes 147464 | tf_op jit(solution)/shard_map/ppermute | solution.py:67
  7.1 0.0 collective-permute-start.2
  7.1 3.8 %load_3.1 = (bf16[2048,768]{1,0:T(8,128)(2,1)S(1)}, bf16[2048,768]{1,0:T(8,128)(2,1)S(1)}, bf16[768,2048]{1,0:T(8,128)(2,1)S(1)}) custom-call(bf16[2048,6144]{1,0:T(8,128)(2,1)} %next_gate.1, bf16[2048,6144]{1,0:T(8,128)(2,1)} %next_up.1, bf16[6144,2048]{1,0:T(8,128)(2,1)} %next_down.1), custom_call_target="tpu_custom_call" | custom-call | flops 1000 | bytes 1000 | tf_op jit(solution)/shard_map/load_3/pallas_call | solution.py:80
  10.9 0.0 collective-permute-done.refs_1_
  11.0 0.0 collective-permute-done.1.refs_2_
  11.0 2.0 %collective-permute-done.2.refs_3_ = bf16[3,8,1024]{2,1,0:T(8,128)(2,1)S(1)} collective-permute-done((bf16[3,8,1024]{2,1,0:T(8,128)(2,1)S(1)}, bf16[3,8,1024]{2,1,0:T(8,128)(2,1)S(1)}, u32[]{:S(2)}, u32[]{:S(2)}) %collective-permute-start.2) | collective-permute-done | bytes 49184 | tf_op jit(solution)/shard_map/ppermute | solution.py:67
  13.0 0.0 copy-done.1
  13.0 0.6 relay.1.refs_3_.refs_0_.refs_4_
  13.6 1.6 %collective-permute-start.3 = (bf16[13,8,1024]{2,1,0:T(8,128)(2,1)S(1)}, bf16[13,8,1024]{2,1,0:T(8,128)(2,1)S(1)}, u32[]{:S(2)}, u32[]{:S(2)}) collective-permute-start(bf16[13,8,1024]{2,1,0:T(8,128)(2,1)S(1)} %relay.1.refs_3_.refs_0_.refs_4_), channel_id=1, source_target_pairs={{0,16},{16,0},{1,17},{17,1},{2,18},{18,2},{3,19},{19,3},{4,20},{20... | collective-permute-start | bytes 638984 | tf_op jit(solution)/shard_map/ppermute | solution.py:67
  15.2 3.8 %load_2.1 = (bf16[2048,768]{1,0:T(8,128)(2,1)S(1)}, bf16[2048,768]{1,0:T(8,128)(2,1)S(1)}, bf16[768,2048]{1,0:T(8,128)(2,1)S(1)}) custom-call(bf16[2048,6144]{1,0:T(8,128)(2,1)} %next_gate.1, bf16[2048,6144]{1,0:T(8,128)(2,1)} %next_up.1, bf16[6144,2048]{1,0:T(8,128)(2,1)} %next_down.1, bf16[13,8,1024]{2,1,0:T(8,128)(2,1)S(1)} %relay.1.refs_3_.refs_0_.refs_4_), custom_call_target="tpu_custom_call" | custom-call | flops 1000 | bytes 1000 | tf_op jit(solution)/shard_map/load_2/pallas_call | solution.py:80
  19.0 3.8 %load_1.1 = (bf16[2048,768]{1,0:T(8,128)(2,1)S(1)}, bf16[2048,768]{1,0:T(8,128)(2,1)S(1)}, bf16[768,2048]{1,0:T(8,128)(2,1)S(1)}) custom-call(bf16[2048,6144]{1,0:T(8,128)(2,1)} %next_gate.1, bf16[2048,6144]{1,0:T(8,128)(2,1)} %next_up.1, bf16[6144,2048]{1,0:T(8,128)(2,1)} %next_down.1, bf16[13,8,1024]{2,1,0:T(8,128)(2,1)S(1)} %relay.1.refs_3_.refs_0_.refs_4_), custom_call_target="tpu_custom_call" | custom-call | flops 1000 | bytes 1000 | tf_op jit(solution)/shard_map/load_1/pallas_call | solution.py:80
  22.8 0.0 collective-permute-done.3.refs_1_.refs_5_
  22.8 2.2 %forward_3.1 = (bf16[48,2048]{1,0:T(8,128)(2,1)S(1)}, bf16[48,2048]{1,0:T(8,128)(2,1)S(1)}, bf16[3,48,768]{2,1,0:T(8,128)(2,1)S(1)}) custom-call(bf16[13,8,1024]{2,1,0:T(8,128)(2,1)S(1)} %relay.1.refs_3_.refs_0_.refs_4_, bf16[13,8,1024]{2,1,0:T(8,128)(2,1)S(1)} %collective-permute-done.3.refs_1_.refs_5_, ...), custom_call_target="tpu_custom_call" | custom-call | flops 1000 | bytes 1000 | tf_op jit(solution)/shard_map/forward_3/pallas_call | solution.py:80
  25.1 0.1 collective-permute-start.4
  25.1 1.5 %collective-permute-done.4.arrived = bf16[3,48,768]{2,1,0:T(8,128)(2,1)S(1)} collective-permute-done((bf16[3,48,768]{2,1,0:T(8,128)(2,1)S(1)}, bf16[3,48,768]{2,1,0:T(8,128)(2,1)S(1)}, u32[]{:S(2)}, u32[]{:S(2)}) %collective-permute-start.4) | collective-permute-done | bytes 221216 | tf_op jit(solution)/shard_map/ppermute | solution.py:67
  26.6 2.1 %forward_2.1.refs_0_ = bf16[3,48,768]{2,1,0:T(8,128)(2,1)S(1)} custom-call(bf16[48,2048]{1,0:T(8,128)(2,1)S(1)} %get-tuple-element.39.tokens, bf16[48,2048]{1,0:T(8,128)(2,1)S(1)} %get-tuple-element.40.cotans, bf16[2048,768]{1,0:T(8,128)(2,1)S(1)} %get-tuple-element.37.refs_5_.gate.refs_10_, bf16[2048,768]{1,0:T(8,128)(2,1)S(1)} %get-tuple-element.43.up.refs_11_, ...), custom_call_target="tpu_custom_call" | custom-call | flops 1000 | bytes 1000 | tf_op jit(solution)/shard_map/forward_2/pallas_call | solution.py:80
  28.8 5.8 %forward_1.1 = (bf16[3,48,768]{2,1,0:T(8,128)(2,1)S(1)}, bf16[2048,768]{1,0:T(8,128)(2,1)S(1)}, bf16[2048,768]{1,0:T(8,128)(2,1)S(1)}, bf16[768,2048]{1,0:T(8,128)(2,1)S(1)}) custom-call(bf16[48,2048]{1,0:T(8,128)(2,1)S(1)} %get-tuple-element.39.tokens, bf16[48,2048]{1,0:T(8,128)(2,1)S(1)} %get-tuple-element.40.cotans, ...), custom_call_target="tpu_custom_call" | custom-call | flops 1000 | bytes 1000 | tf_op jit(solution)/shard_map/forward_1/pallas_call | solution.py:80
  34.6 0.2 collective-permute-start.5
  34.8 1.5 %collective-permute-start.6 = (bf16[3,48,768]{2,1,0:T(8,128)(2,1)S(1)}, bf16[3,48,768]{2,1,0:T(8,128)(2,1)S(1)}, u32[]{:S(2)}, u32[]{:S(2)}) collective-permute-start(bf16[3,48,768]{2,1,0:T(8,128)(2,1)S(1)} %forward_2.1.refs_0_), channel_id=1, source_target_pairs={{0,2},{1,3},{2,0},{3,1},{4,6},{5,7},{6,4},{7,5},{8,10},{9,11},{10,... | collective-permute-start | bytes 663560 | tf_op jit(solution)/shard_map/ppermute | solution.py:67
  36.3 0.0 copy-start
  36.3 2.1 %forward_0.1.refs_0_ = f32[3,48,768]{2,1,0:T(8,128)S(1)} custom-call(bf16[48,2048]{1,0:T(8,128)(2,1)S(1)} %get-tuple-element.39.tokens, bf16[48,2048]{1,0:T(8,128)(2,1)S(1)} %get-tuple-element.40.cotans, bf16[2048,768]{1,0:T(8,128)(2,1)S(1)} %get-tuple-element.46.gate.refs_6_, bf16[2048,768]{1,0:T(8,128)(2,1)S(1)} %get-tuple-element.47.up.refs_7_, ...), custom_call_target="tpu_custom_call" | custom-call | flops 1000 | bytes 1000 | tf_op jit(solution)/shard_map/forward_0/pallas_call | solution.py:80
  38.4 0.0 collective-permute-done.5.refs_1_
  38.4 4.1 %collective-permute-done.6.refs_2_ = bf16[3,48,768]{2,1,0:T(8,128)(2,1)S(1)} collective-permute-done((bf16[3,48,768]{2,1,0:T(8,128)(2,1)S(1)}, bf16[3,48,768]{2,1,0:T(8,128)(2,1)S(1)}, u32[]{:S(2)}, u32[]{:S(2)}) %collective-permute-start.6) | collective-permute-done | bytes 221216 | tf_op jit(solution)/shard_map/ppermute | solution.py:67
  42.5 0.0 copy-done
  42.5 0.4 middle.1
  42.9 0.0 collective-permute-start.8
  42.9 1.6 %collective-permute-start.7 = (bf16[112,768]{1,0:T(8,128)(2,1)S(1)}, bf16[112,768]{1,0:T(8,128)(2,1)S(1)}, u32[]{:S(2)}, u32[]{:S(2)}) collective-permute-start(bf16[112,768]{1,0:T(8,128)(2,1)S(1)} %get-tuple-element.50.message.refs_0_), channel_id=1, source_target_pairs={{0,2},{1,3},{2,0},{3,1},{4,6},{5,7},{6,4},{7,5},{8,10},{9,11},{10,... | collective-permute-start | bytes 516104 | tf_op jit(solution)/shard_map/ppermute | solution.py:67
  44.4 1.9 %backward_0.1.before = f32[48,2048]{1,0:T(8,128)S(1)} custom-call(bf16[112,768]{1,0:T(8,128)(2,1)S(1)} %get-tuple-element.50.message.refs_0_, bf16[2048,768]{1,0:T(8,128)(2,1)S(1)} %get-tuple-element.46.gate.refs_6_, bf16[2048,768]{1,0:T(8,128)(2,1)S(1)} %get-tuple-element.47.up.refs_7_), custom_call_target="tpu_custom_call" | custom-call | flops 1000 | bytes 1000 | tf_op jit(solution)/shard_map/backward_0/pallas_call | solution.py:80
  46.3 0.0 collective-permute-done.8.message.refs_1_
  46.3 1.9 %backward_1.1.before = f32[48,2048]{1,0:T(8,128)S(1)} custom-call(bf16[112,768]{1,0:T(8,128)(2,1)S(1)} %collective-permute-done.8.message.refs_1_, bf16[2048,768]{1,0:T(8,128)(2,1)S(1)} %get-tuple-element.38.refs_6_.gate.refs_8_, bf16[2048,768]{1,0:T(8,128)(2,1)S(1)} %get-tuple-element.41.up.refs_9_, f32[48,2048]{1,0:T(8,128)S(1)} %backward_0.1.before), custom_call_target="tpu_custom_call" | custom-call | flops 1000 | bytes 1000 | tf_op jit(solution)/shard_map/backward_1/pallas_call | solution.py:80
  48.3 1.3 %collective-permute-done.7.message.refs_2_ = bf16[112,768]{1,0:T(8,128)(2,1)S(1)} collective-permute-done((bf16[112,768]{1,0:T(8,128)(2,1)S(1)}, bf16[112,768]{1,0:T(8,128)(2,1)S(1)}, u32[]{:S(2)}, u32[]{:S(2)}) %collective-permute-start.7) | collective-permute-done | bytes 172064 | tf_op jit(solution)/shard_map/ppermute | solution.py:67
  49.6 0.0 collective-permute-start.9
  49.6 1.9 %backward_2.1.before = f32[48,2048]{1,0:T(8,128)S(1)} custom-call(bf16[112,768]{1,0:T(8,128)(2,1)S(1)} %collective-permute-done.7.message.refs_2_, bf16[2048,768]{1,0:T(8,128)(2,1)S(1)} %get-tuple-element.37.refs_5_.gate.refs_10_, bf16[2048,768]{1,0:T(8,128)(2,1)S(1)} %get-tuple-element.43.up.refs_11_, f32[48,2048]{1,0:T(8,128)S(1)} %backward_1.1.before), custom_call_target="tpu_custom_call" | custom-call | flops 1000 | bytes 1000 | tf_op jit(solution)/shard_map/backward_2/pallas_call | solution.py:80
  51.6 0.0 collective-permute-done.9.message
  51.6 2.0 %backward_3.1 = (f32[24,2048]{1,0:T(8,128)S(1)}, f32[8,2048]{1,0:T(8,128)S(1)}, bf16[4,8,2048]{2,1,0:T(8,128)(2,1)S(1)}) custom-call(bf16[112,768]{1,0:T(8,128)(2,1)S(1)} %collective-permute-done.9.message, bf16[2048,768]{1,0:T(8,128)(2,1)S(1)} %get-tuple-element.34.refs_5_.refs_2_.refs_12_.gate, ...), custom_call_target="tpu_custom_call" | custom-call | flops 1000 | bytes 1000 | tf_op jit(solution)/shard_map/backward_3/pallas_call | solution.py:80
  53.6 0.6 collective-permute-start.10
  54.2 5.4 %collective-permute-done.10.arrived = bf16[4,8,2048]{2,1,0:T(8,128)(2,1)S(1)} collective-permute-done((bf16[4,8,2048]{2,1,0:T(8,128)(2,1)S(1)}, bf16[4,8,2048]{2,1,0:T(8,128)(2,1)S(1)}, u32[]{:S(2)}, u32[]{:S(2)}) %collective-permute-start.10) | collective-permute-done | bytes 131104 | tf_op jit(solution)/shard_map/ppermute | solution.py:67
  59.6 0.7 combine.1
  60.2 0.0 collective-permute-start.11
  60.2 2.4 %collective-permute-start.12 = (bf16[8,2048]{1,0:T(8,128)(2,1)S(1)}, bf16[8,2048]{1,0:T(8,128)(2,1)S(1)}, u32[]{:S(2)}, u32[]{:S(2)}) collective-permute-start(bf16[8,2048]{1,0:T(8,128)(2,1)S(1)} %get-tuple-element.61), channel_id=1, source_target_pairs={{0,8},{4,12},{8,0},{12,4},{1,9},{5,13},{9,1},{13,5},{2,10},{6,14},... | collective-permute-start | bytes 98312 | tf_op jit(solution)/shard_map/ppermute | solution.py:67
  62.6 2.0 %collective-permute-start.13 = (bf16[8,2048]{1,0:T(8,128)(2,1)S(1)}, bf16[8,2048]{1,0:T(8,128)(2,1)S(1)}, u32[]{:S(2)}, u32[]{:S(2)}) collective-permute-start(bf16[8,2048]{1,0:T(8,128)(2,1)S(1)} %get-tuple-element.62), channel_id=1, source_target_pairs={{0,12},{4,8},{8,4},{12,0},{1,13},{5,9},{9,5},{13,1},{2,14},{6,10},... | collective-permute-start | bytes 98312 | tf_op jit(solution)/shard_map/ppermute | solution.py:67
  64.6 0.0 collective-permute-done.11.refs_1_
  64.6 0.7 %collective-permute-done.12.refs_2_ = bf16[8,2048]{1,0:T(8,128)(2,1)S(1)} collective-permute-done((bf16[8,2048]{1,0:T(8,128)(2,1)S(1)}, bf16[8,2048]{1,0:T(8,128)(2,1)S(1)}, u32[]{:S(2)}, u32[]{:S(2)}) %collective-permute-start.12) | collective-permute-done | bytes 32800 | tf_op jit(solution)/shard_map/ppermute | solution.py:67
  65.3 3.0 %collective-permute-done.13.refs_3_ = bf16[8,2048]{1,0:T(8,128)(2,1)S(1)} collective-permute-done((bf16[8,2048]{1,0:T(8,128)(2,1)S(1)}, bf16[8,2048]{1,0:T(8,128)(2,1)S(1)}, u32[]{:S(2)}, u32[]{:S(2)}) %collective-permute-start.13) | collective-permute-done | bytes 32800 | tf_op jit(solution)/shard_map/ppermute | solution.py:67
  68.3 0.7 last.1
Async XLA Ops:
  1.4 11.6 %copy-start.1 = (s32[24]{0:T(128)S(1)}, s32[24]{0:T(128)}, u32[]{:S(2)}) copy-start(s32[24]{0:T(128)} %refs_4_.1) | copy-start | bytes 292
  1.4 9.5 %collective-permute-start = (bf16[3,8,1024]{2,1,0:T(8,128)(2,1)S(1)}, bf16[3,8,1024]{2,1,0:T(8,128)(2,1)S(1)}, u32[]{:S(2)}, u32[]{:S(2)}) collective-permute-start(bf16[3,8,1024]{2,1,0:T(8,128)(2,1)S(1)} %pack.1.refs_0_), channel_id=1, source_target_pairs={{0,4},{4,0},{8,12},{12,8},{1,5},{5,1},{9,13},{13,9},{2,6},{6,2},{1... | collective-permute-start | bytes 147464 | tf_op jit(solution)/shard_map/ppermute | solution.py:67
  4.5 6.4 %collective-permute-start.1 = (bf16[3,8,1024]{2,1,0:T(8,128)(2,1)S(1)}, bf16[3,8,1024]{2,1,0:T(8,128)(2,1)S(1)}, u32[]{:S(2)}, u32[]{:S(2)}) collective-permute-start(bf16[3,8,1024]{2,1,0:T(8,128)(2,1)S(1)} %pack.1.refs_0_), channel_id=1, source_target_pairs={{0,8},{4,12},{8,0},{12,4},{1,9},{5,13},{9,1},{13,5},{2,10},{6,14},... | collective-permute-start | bytes 147464 | tf_op jit(solution)/shard_map/ppermute | solution.py:67
  7.1 5.9 %collective-permute-start.2 = (bf16[3,8,1024]{2,1,0:T(8,128)(2,1)S(1)}, bf16[3,8,1024]{2,1,0:T(8,128)(2,1)S(1)}, u32[]{:S(2)}, u32[]{:S(2)}) collective-permute-start(bf16[3,8,1024]{2,1,0:T(8,128)(2,1)S(1)} %pack.1.refs_0_), channel_id=1, source_target_pairs={{0,12},{4,8},{8,4},{12,0},{1,13},{5,9},{9,5},{13,1},{2,14},{6,10},... | collective-permute-start | bytes 147464 | tf_op jit(solution)/shard_map/ppermute | solution.py:67
  13.6 9.2 %collective-permute-start.3 = (bf16[13,8,1024]{2,1,0:T(8,128)(2,1)S(1)}, bf16[13,8,1024]{2,1,0:T(8,128)(2,1)S(1)}, u32[]{:S(2)}, u32[]{:S(2)}) collective-permute-start(bf16[13,8,1024]{2,1,0:T(8,128)(2,1)S(1)} %relay.1.refs_3_.refs_0_.refs_4_), channel_id=1, source_target_pairs={{0,16},{16,0},{1,17},{17,1},{2,18},{18,2},{3,19},{19,3},{4,20},{20... | collective-permute-start | bytes 638984 | tf_op jit(solution)/shard_map/ppermute | solution.py:67
  25.1 1.5 %collective-permute-start.4 = (bf16[3,48,768]{2,1,0:T(8,128)(2,1)S(1)}, bf16[3,48,768]{2,1,0:T(8,128)(2,1)S(1)}, u32[]{:S(2)}, u32[]{:S(2)}) collective-permute-start(bf16[3,48,768]{2,1,0:T(8,128)(2,1)S(1)} %get-tuple-element.45), channel_id=1, source_target_pairs={{0,1},{1,0},{2,3},{3,2},{4,5},{5,4},{6,7},{7,6},{8,9},{9,8},{10,11... | collective-permute-start | bytes 663560 | tf_op jit(solution)/shard_map/ppermute | solution.py:67
  34.6 3.8 %collective-permute-start.5 = (bf16[3,48,768]{2,1,0:T(8,128)(2,1)S(1)}, bf16[3,48,768]{2,1,0:T(8,128)(2,1)S(1)}, u32[]{:S(2)}, u32[]{:S(2)}) collective-permute-start(bf16[3,48,768]{2,1,0:T(8,128)(2,1)S(1)} %get-tuple-element.49), channel_id=1, source_target_pairs={{0,1},{1,0},{2,3},{3,2},{4,5},{5,4},{6,7},{7,6},{8,9},{9,8},{10,11... | collective-permute-start | bytes 663560 | tf_op jit(solution)/shard_map/ppermute | solution.py:67
  34.8 7.7 %collective-permute-start.6 = (bf16[3,48,768]{2,1,0:T(8,128)(2,1)S(1)}, bf16[3,48,768]{2,1,0:T(8,128)(2,1)S(1)}, u32[]{:S(2)}, u32[]{:S(2)}) collective-permute-start(bf16[3,48,768]{2,1,0:T(8,128)(2,1)S(1)} %forward_2.1.refs_0_), channel_id=1, source_target_pairs={{0,2},{1,3},{2,0},{3,1},{4,6},{5,7},{6,4},{7,5},{8,10},{9,11},{10,... | collective-permute-start | bytes 663560 | tf_op jit(solution)/shard_map/ppermute | solution.py:67
  36.3 6.2 %copy-start = (f32[6144]{0:T(1024)S(1)}, f32[6144]{0:T(1024)}, u32[]{:S(2)}) copy-start(f32[6144]{0:T(1024)} %param.12) | copy-start | bytes 73732
  42.9 3.5 %collective-permute-start.8 = (bf16[112,768]{1,0:T(8,128)(2,1)S(1)}, bf16[112,768]{1,0:T(8,128)(2,1)S(1)}, u32[]{:S(2)}, u32[]{:S(2)}) collective-permute-start(bf16[112,768]{1,0:T(8,128)(2,1)S(1)} %get-tuple-element.50.message.refs_0_), channel_id=1, source_target_pairs={{0,1},{1,0},{2,3},{3,2},{4,5},{5,4},{6,7},{7,6},{8,9},{9,8},{10,11... | collective-permute-start | bytes 516104 | tf_op jit(solution)/shard_map/ppermute | solution.py:67
  42.9 6.8 %collective-permute-start.7 = (bf16[112,768]{1,0:T(8,128)(2,1)S(1)}, bf16[112,768]{1,0:T(8,128)(2,1)S(1)}, u32[]{:S(2)}, u32[]{:S(2)}) collective-permute-start(bf16[112,768]{1,0:T(8,128)(2,1)S(1)} %get-tuple-element.50.message.refs_0_), channel_id=1, source_target_pairs={{0,2},{1,3},{2,0},{3,1},{4,6},{5,7},{6,4},{7,5},{8,10},{9,11},{10,... | collective-permute-start | bytes 516104 | tf_op jit(solution)/shard_map/ppermute | solution.py:67
  49.6 2.0 %collective-permute-start.9 = (bf16[112,768]{1,0:T(8,128)(2,1)S(1)}, bf16[112,768]{1,0:T(8,128)(2,1)S(1)}, u32[]{:S(2)}, u32[]{:S(2)}) collective-permute-start(bf16[112,768]{1,0:T(8,128)(2,1)S(1)} %collective-permute-done.7.message.refs_2_), channel_id=1, source_target_pairs={{0,1},{1,0},{2,3},{3,2},{4,5},{5,4},{6,7},{7,6},{8,9},{9,8},{10,11... | collective-permute-start | bytes 516104 | tf_op jit(solution)/shard_map/ppermute | solution.py:67
  53.6 6.0 %collective-permute-start.10 = (bf16[4,8,2048]{2,1,0:T(8,128)(2,1)S(1)}, bf16[4,8,2048]{2,1,0:T(8,128)(2,1)S(1)}, u32[]{:S(2)}, u32[]{:S(2)}) collective-permute-start(bf16[4,8,2048]{2,1,0:T(8,128)(2,1)S(1)} %get-tuple-element.56), channel_id=1, source_target_pairs={{0,16},{16,0},{1,17},{17,1},{2,18},{18,2},{3,19},{19,3},{4,20},{20... | collective-permute-start | bytes 393224 | tf_op jit(solution)/shard_map/ppermute | solution.py:67
  60.2 4.4 %collective-permute-start.11 = (bf16[8,2048]{1,0:T(8,128)(2,1)S(1)}, bf16[8,2048]{1,0:T(8,128)(2,1)S(1)}, u32[]{:S(2)}, u32[]{:S(2)}) collective-permute-start(bf16[8,2048]{1,0:T(8,128)(2,1)S(1)} %get-tuple-element.60), channel_id=1, source_target_pairs={{0,4},{4,0},{8,12},{12,8},{1,5},{5,1},{9,13},{13,9},{2,6},{6,2},{1... | collective-permute-start | bytes 98312 | tf_op jit(solution)/shard_map/ppermute | solution.py:67
  60.2 5.1 %collective-permute-start.12 = (bf16[8,2048]{1,0:T(8,128)(2,1)S(1)}, bf16[8,2048]{1,0:T(8,128)(2,1)S(1)}, u32[]{:S(2)}, u32[]{:S(2)}) collective-permute-start(bf16[8,2048]{1,0:T(8,128)(2,1)S(1)} %get-tuple-element.61), channel_id=1, source_target_pairs={{0,8},{4,12},{8,0},{12,4},{1,9},{5,13},{9,1},{13,5},{2,10},{6,14},... | collective-permute-start | bytes 98312 | tf_op jit(solution)/shard_map/ppermute | solution.py:67
  62.6 5.7 %collective-permute-start.13 = (bf16[8,2048]{1,0:T(8,128)(2,1)S(1)}, bf16[8,2048]{1,0:T(8,128)(2,1)S(1)}, u32[]{:S(2)}, u32[]{:S(2)}) collective-permute-start(bf16[8,2048]{1,0:T(8,128)(2,1)S(1)} %get-tuple-element.62), channel_id=1, source_target_pairs={{0,12},{4,8},{8,4},{12,0},{1,13},{5,9},{9,5},{13,1},{2,14},{6,10},... | collective-permute-start | bytes 98312 | tf_op jit(solution)/shard_map/ppermute | solution.py:67

commit v4 on v3

--- a/solution.py
+++ b/solution.py
@@ -118,42 +118,72 @@
     out[len(blocks) * slabs] = jnp.concatenate(keys, axis=1).astype(jnp.bfloat16)
 
 
-def load_kernel(strip, groups, *refs):
-    gate, up, down = refs[:3]
-    gate_held, up_held, down_held, sem = refs[-4:]
-    start_load(strip, groups, (gate, up, down), (gate_held, up_held, down_held), sem)()
-
-
-def start_load(strip, groups, sources, targets, sem):
-    width = targets[0].shape[1]
-    owner = lax.axis_index("narrow") ^ strip
-    start = pl.multiple_of((owner * groups + lax.axis_index("groups")) * width, width)
-    gate, up, down = sources
-    copies = [
-        pltpu.make_async_copy(gate.at[:, pl.ds(start, width)], targets[0], sem.at[0]),
-        pltpu.make_async_copy(up.at[:, pl.ds(start, width)], targets[1], sem.at[1]),
-        pltpu.make_async_copy(down.at[pl.ds(start, width), :], targets[2], sem.at[2]),
-    ]
+GATE, UP, DOWN = range(3)
+WHOLE_STRIP = (GATE, UP, DOWN)
+
+
+def start_loads(pieces, groups, sources, targets, sem):
+    copies = []
+    for i, (kind, strip) in enumerate(pieces):
+        target = targets[i]
+        width = target.shape[0 if kind == DOWN else 1]
+        owner = lax.axis_index("narrow") ^ strip
+        start = pl.multiple_of((owner * groups + lax.axis_index("groups")) * width, width)
+        source = sources[kind]
+        source = source.at[pl.ds(start, width), :] if kind == DOWN else source.at[:, pl.ds(start, width)]
+        copies.append(pltpu.make_async_copy(source, target, sem.at[i]))
     for copy in copies:
         copy.start()
-
-    def wait():
+    return copies
+
+
+def load_kernel(pieces, groups, *refs):
+    count = len(pieces)
+    for copy in start_loads(pieces, groups, refs[:3], refs[-1 - count : -1], refs[-1]):
+        copy.wait()
+
+
+def loading(body, pieces, groups, outs):
+    count = len(pieces)
+
+    def kernel(*refs):
+        sources, rest = refs[:3], refs[3:]
+        at = len(rest) - outs[1] - 1 - count
+        targets, sem = rest[at : at + count], rest[at + count + outs[1]]
+        copies = start_loads(pieces, groups, sources, targets, sem)
+        body(*rest[:at], *rest[at + count : at + count + outs[1]])
         for copy in copies:
             copy.wait()
 
-    return wait
-
-
-def strip_parts(tokens, cotans, weights):
-    gate, up, down = weights
-    tokens, cotans = tokens[...], cotans[...]
-    yield jnp.dot(tokens, gate[...], preferred_element_type=jnp.float32)
-    yield jnp.dot(tokens, up[...], preferred_element_type=jnp.float32)
-    yield contract_rows(cotans, down[...])
-
-
-def first_kernel(share, *refs):
-    relayed, other, gate, up, down = refs[:5]
+    return kernel
+
+
+def strip_parts(tokens, cotans, gate, up, down, put):
+    tile = 256
+
+    @pl.loop(0, gate.shape[1] // tile)
+    def _(i):
+        span = pl.ds(pl.multiple_of(i * tile, tile), tile)
+        put(GATE, span, jnp.dot(tokens[...], gate[:, span], preferred_element_type=jnp.float32))
+        put(UP, span, jnp.dot(tokens[...], up[:, span], preferred_element_type=jnp.float32))
+        put(DOWN, span, contract_rows(cotans[...], down[span, :]))
+
+
+def forward_kernel(tokens, cotans, gate, up, down, out):
+    def put(kind, span, part):
+        out[kind, :, span] = part
+
+    strip_parts(tokens, cotans, gate, up, down, put)
+
+
+def forward_add_kernel(tokens, cotans, gate, up, down, arrived, out):
+    def put(kind, span, part):
+        out[kind, :, span] = (part + arrived[kind, :, span]).astype(out.dtype)
+
+    strip_parts(tokens, cotans, gate, up, down, put)
+
+
+def first_kernel(share, relayed, other, gate, up, down, *refs):
     tokens, cotans, part, rows, cots = refs[-5:]
     slabs, half = 4 * share // 8, rows.shape[1] // 2
     count = (relayed.shape[0] - 1) // slabs
@@ -169,21 +199,17 @@
     forward_kernel(tokens, cotans, gate, up, down, part)
 
 
-def forward_kernel(tokens, cotans, gate, up, down, out):
-    for i, part in enumerate(strip_parts(tokens, cotans, (gate, up, down))):
-        out[i] = part.astype(out.dtype)
-
-
-def forward_add_kernel(tokens, cotans, gate, up, down, arrived, out):
-    for i, part in enumerate(strip_parts(tokens, cotans, (gate, up, down))):
-        out[i] = (part + arrived[i].astype(jnp.float32)).astype(out.dtype)
-
-
-def forward_load_kernel(strip, groups, tokens, cotans, gate, up, down, next_gate, next_up, next_down, *refs):
-    out, targets, sem = refs[-5], refs[-4:-1], refs[-1]
-    wait = start_load(strip, groups, (next_gate, next_up, next_down), targets, sem)
-    forward_kernel(tokens, cotans, gate, up, down, out)
-    wait()
+def own_strip_kernel(groups, *refs):
+    sources, (tokens, cotans) = refs[:3], refs[3:5]
+    out, (gate, up, down), sem = refs[-5], refs[-4:-1], refs[-1]
+    pieces = [(kind, 0) for kind in WHOLE_STRIP]
+    copies = start_loads(pieces, groups, sources, (gate, up, down), sem)
+    copies[GATE].wait()
+    out[GATE] = jnp.dot(tokens[...], gate[...], preferred_element_type=jnp.float32)
+    copies[UP].wait()
+    out[UP] = jnp.dot(tokens[...], up[...], preferred_element_type=jnp.float32)
+    copies[DOWN].wait()
+    out[DOWN] = contract_rows(cotans[...], down[...])
 
 
 def middle_kernel(groups, *refs):
@@ -191,7 +217,7 @@
     message, grads, other_grads, stage = refs[-4:]
     _, tokens, width = own.shape
     narrow, group = lax.axis_index("narrow"), lax.axis_index("groups")
-    sums = [own[i] + arrived[i].astype(jnp.float32) + crossed[i].astype(jnp.float32) for i in range(3)]
+    sums = [own[i] + arrived[i] + crossed[i].astype(jnp.float32) for i in range(3)]
     start = pl.multiple_of((narrow * groups + group) * width, width)
     product, d_gate, d_up = local_grads(*sums, scale[:, pl.ds(start, width)])
     message[0:tokens, :] = d_gate
@@ -323,23 +349,35 @@
         pltpu.VMEM((features, width), bf16),
         pltpu.VMEM((width, features), bf16),
     ]
-    load_sem = [pltpu.SemaphoreType.DMA((3,))]
-
-    def load(strip, after=()):
+    kept = {}
+
+    def load(name, pieces, after=()):
         args = weights + tuple(after)
-        return call(
-            functools.partial(load_kernel, strip, groups),
-            f"load_{strip}",
-            weight_shapes,
+        arrays = call(
+            functools.partial(load_kernel, pieces, groups),
+            name,
+            [weight_shapes[kind] for kind, _ in pieces],
             args,
             {i: pltpu.HBM if i < 3 else pl.ANY for i in range(len(args))},
-            load_sem,
+            [pltpu.SemaphoreType.DMA((len(pieces),))],
         )
-
-    def hold(strip):
-        return [held(array) for array in kept[strip]]
-
-    kept = {}
+        kept.update(zip(pieces, arrays))
+
+    def call_loading(body, name, pieces, outs, args, scratch=()):
+        made = call(
+            loading(body, pieces, groups, (len(outs), len(outs) + len(scratch))),
+            name,
+            [weight_shapes[kind] for kind, _ in pieces] + outs,
+            list(weights) + args,
+            {i: pltpu.HBM for i in range(3)},
+            list(scratch) + [pltpu.SemaphoreType.DMA((len(pieces),))],
+        )
+        kept.update(zip(pieces, made))
+        return made[len(pieces) :]
+
+    def hold(strip, kinds=WHOLE_STRIP):
+        return [held(kept[kind, strip]) for kind in kinds]
+
     packed = call(
         pack_kernel,
         "pack",
@@ -347,28 +385,31 @@
         [pltpu.with_memory_space_constraint(array, pltpu.HBM) for array in (inputs, cotangent)],
         scratch=[pltpu.VMEM((4 * share, features // 2), f32)],
     )
-    blocks = [packed] + [exchange(packed, "wide", s) for s in range(1, wide)]
-    kept[3] = load(3)
+    arrived = {s: exchange(packed, "wide", s) for s in reversed(range(1, wide))}
+    load("load_a", [(kind, 3) for kind in WHOLE_STRIP])
     relayed = call(
         functools.partial(relay_kernel, share),
         "relay",
         pltpu.VMEM((wide * slabs + 1, 8, features // 2), bf16),
-        blocks + [seq_ids] + hold(3)[:1],
+        [packed] + [arrived[s] for s in range(1, wide)] + [seq_ids] + hold(3, [GATE]),
         {wide: pltpu.SMEM},
     )
     other_relayed = exchange(relayed, "groups", 1)
-    kept[2] = load(2, [relayed])
-    kept[1] = load(1, [relayed])
-
-    tokens_all, cotans_all, diagonal = call(
+    load("load_b", [(kind, 1) for kind in WHOLE_STRIP] + [(GATE, 2)], [relayed])
+
+    part = pltpu.VMEM((3, tokens, width), f32)
+    tokens_all, cotans_all, diagonal = call_loading(
         functools.partial(first_kernel, share),
         "forward_3",
-        [pltpu.VMEM((tokens, features), bf16)] * 2 + [pltpu.VMEM((3, tokens, width), bf16)],
-        [relayed, other_relayed] + hold(3) + hold(2)[:1] + hold(1)[:1],
-        scratch=[pltpu.VMEM((tokens, features), f32)] * 2,
+        [(UP, 2)],
+        [pltpu.VMEM((tokens, features), bf16)] * 2 + [part],
+        [relayed, other_relayed] + hold(3) + hold(1, [GATE]),
+        [pltpu.VMEM((tokens, features), f32)] * 2,
     )
     panel = [tokens_all, cotans_all]
     diagonal = exchange(diagonal, "narrow", 1)
+    (near,) = call_loading(forward_kernel, "forward_1", [(DOWN, 2)], [part], panel + hold(1))
+    near = exchange(near, "narrow", 1)
     crossing = call(
         forward_add_kernel,
         "forward_2",
@@ -376,20 +417,17 @@
         panel + hold(2) + [diagonal],
     )
     crossed = exchange(crossing, "narrow", 2)
-    near, *kept[0] = call(
-        functools.partial(forward_load_kernel, 0, groups),
-        "forward_1",
-        [pltpu.VMEM((3, tokens, width), bf16)] + weight_shapes,
-        panel + hold(1) + list(weights) + [held(crossing)],
-        {5: pltpu.HBM, 6: pltpu.HBM, 7: pltpu.HBM},
-        load_sem,
-    )
-    near = exchange(near, "narrow", 1)
-    own_part = call(
-        forward_kernel, "forward_0", pltpu.VMEM((3, tokens, width), f32), panel + hold(0)
-    )
-
-    resident = [array for s in range(strips) for array in hold(s)[:2]]
+    own_part, *arrays = call(
+        functools.partial(own_strip_kernel, groups),
+        "forward_0",
+        [part] + weight_shapes,
+        list(weights) + panel + [held(crossing)],
+        {i: pltpu.HBM for i in range(3)},
+        [pltpu.SemaphoreType.DMA((3,))],
+    )
+    kept.update({(kind, 0): array for kind, array in enumerate(arrays)})
+
+    resident = [array for s in range(strips) for array in hold(s, [GATE, UP])]
     message, grads, other_grads = call(
         functools.partial(middle_kernel, groups),
         "middle",
@@ -405,11 +443,11 @@
     total = pltpu.VMEM((tokens, features), f32)
     message_1 = exchange(message, "narrow", 1)
     message_2 = exchange(message, "narrow", 2)
-    sums = call(backward_first_kernel, "backward_0", total, [message] + hold(0)[:2])
-    sums = call(backward_next_kernel, "backward_1", total, [message_1] + hold(1)[:2] + [sums])
+    sums = call(backward_first_kernel, "backward_0", total, [message] + hold(0, [GATE, UP]))
+    sums = call(backward_next_kernel, "backward_1", total, [message_1] + hold(1, [GATE, UP]) + [sums])
     message_2, sums = lax.optimization_barrier((message_2, sums))
     message_3 = exchange(message_2, "narrow", 1)
-    sums = call(backward_next_kernel, "backward_2", total, [message_2] + hold(2)[:2] + [sums])
+    sums = call(backward_next_kernel, "backward_2", total, [message_2] + hold(2, [GATE, UP]) + [sums])
     own, own_tail, send = call(
         backward_last_kernel,
         "backward_3",
@@ -418,7 +456,7 @@
             pltpu.VMEM((8, features), f32),
             pltpu.VMEM((half // 8 + 1, 8, features), bf16),
         ],
-        [message_3] + hold(3)[:2] + [sums, message, message_1, message_2, other_grads],
+        [message_3] + hold(3, [GATE, UP]) + [sums, message, message_1, message_2, other_grads],
     )
     arrived = exchange(send, "groups", 1)
     example_grads, own_block, *sends = call(

time: 69.1 us -> 62 us (0.90)
  waiting for transfers between devices: 18 us -> 12.3 us
  Pallas kernels: 34.6 us -> 32.1 us
  starting transfers between devices: 15.6 us -> 16.6 us
    ppermute x14, waiting for transfers between devices: 18 us -> 12.3 us  [exchange(): lax.ppermute(array, axis, [(i, i ^ step) for i in range(lax.axis_size(axi...]
    pallas_call x16 -> x15, Pallas kernels: 34.6 us -> 32.1 us  [call(): pl.pallas_call(body, out_shape=outs, in_specs=[pl.BlockSpec(memory_space=...]
    ppermute x14, starting transfers between devices: 15.6 us -> 16.6 us  [exchange(): lax.ppermute(array, axis, [(i, i ^ step) for i in range(lax.axis_size(axi...]
  transfers between devices with their start and end apart: 14 -> 14, of which waited for: 7 -> 6; matrix products, arithmetic and copies ran while one was open for 0% -> 0% of each run, Pallas kernels for 28% -> 40%
where the time goes in v4:
time: 62 us; the launch traced here: 61.8 us
  Pallas kernels  32.1 us (52%)
  starting transfers between devices  16.6 us (27%)
  waiting for transfers between devices  12.3 us (20%)
  between operations  0.8 us (1%)
    pallas_call x15, Pallas kernels, call(): pl.pallas_call(body, out_shape=outs, in_specs=[pl.BlockSpec(memory_space=...  32.1 us
    ppermute x14, starting transfers between devices, exchange(): lax.ppermute(array, axis, [(i, i ^ step) for i in range(lax.axis_size(axi...  16.6 us
    ppermute x14, waiting for transfers between devices, exchange(): lax.ppermute(array, axis, [(i, i ^ step) for i in range(lax.axis_size(axi...  12.3 us
  transfers between devices with their start and end apart: 14, of which 6 were waited for; matrix products, arithmetic and copies ran while one was open for 0% of the time, Pallas kernels for 40%

profile of v4, /device:TPU:0, one launch (start us, length us, event | category | flops | bytes accessed | tf_op | source)
XLA Modules:
  0.0 61.8 jit_solution(18365666946971715683)
XLA Ops:
  0.6 0.8 %pack.1.refs_0_ = bf16[3,8,1024]{2,1,0:T(8,128)(2,1)S(1)} custom-call(bf16[6,2048]{1,0:T(8,128)(2,1)} %inputs.1, bf16[6,2048]{1,0:T(8,128)(2,1)} %cotangent.1), custom_call_target="tpu_custom_call" | custom-call | flops 1000 | bytes 1000 | tf_op jit(solution)/shard_map/pack/pallas_call | solution.py:80
  1.4 0.0 copy-start.1
  1.4 3.1 %collective-permute-start = (bf16[3,8,1024]{2,1,0:T(8,128)(2,1)S(1)}, bf16[3,8,1024]{2,1,0:T(8,128)(2,1)S(1)}, u32[]{:S(2)}, u32[]{:S(2)}) collective-permute-start(bf16[3,8,1024]{2,1,0:T(8,128)(2,1)S(1)} %pack.1.refs_0_), channel_id=1, source_target_pairs={{0,4},{4,0},{8,12},{12,8},{1,5},{5,1},{9,13},{13,9},{2,6},{6,2},{1... | collective-permute-start | bytes 147464 | tf_op jit(solution)/shard_map/ppermute | solution.py:67
  4.5 2.6 %collective-permute-start.1 = (bf16[3,8,1024]{2,1,0:T(8,128)(2,1)S(1)}, bf16[3,8,1024]{2,1,0:T(8,128)(2,1)S(1)}, u32[]{:S(2)}, u32[]{:S(2)}) collective-permute-start(bf16[3,8,1024]{2,1,0:T(8,128)(2,1)S(1)} %pack.1.refs_0_), channel_id=1, source_target_pairs={{0,8},{4,12},{8,0},{12,4},{1,9},{5,13},{9,1},{13,5},{2,10},{6,14},... | collective-permute-start | bytes 147464 | tf_op jit(solution)/shard_map/ppermute | solution.py:67
  7.1 0.0 collective-permute-start.2
  7.1 3.8 %load_a.1 = (bf16[2048,768]{1,0:T(8,128)(2,1)S(1)}, bf16[2048,768]{1,0:T(8,128)(2,1)S(1)}, bf16[768,2048]{1,0:T(8,128)(2,1)S(1)}) custom-call(bf16[2048,6144]{1,0:T(8,128)(2,1)} %refs_0_.9, bf16[2048,6144]{1,0:T(8,128)(2,1)} %refs_1_.9, bf16[6144,2048]{1,0:T(8,128)(2,1)} %refs_2_.9), custom_call_target="tpu_custom_call" | custom-call | flops 1000 | bytes 1000 | tf_op jit(solution)/shard_map/load_a/pallas_call | solution.py:80
  10.9 0.0 collective-permute-done.refs_1_
  11.0 0.0 collective-permute-done.1.refs_2_
  11.0 2.0 %collective-permute-done.2.refs_3_ = bf16[3,8,1024]{2,1,0:T(8,128)(2,1)S(1)} collective-permute-done((bf16[3,8,1024]{2,1,0:T(8,128)(2,1)S(1)}, bf16[3,8,1024]{2,1,0:T(8,128)(2,1)S(1)}, u32[]{:S(2)}, u32[]{:S(2)}) %collective-permute-start.2) | collective-permute-done | bytes 49184 | tf_op jit(solution)/shard_map/ppermute | solution.py:67
  13.0 0.0 copy-done.1
  13.0 0.6 relay.1.refs_3_.refs_4_
  13.6 1.6 %collective-permute-start.3 = (bf16[13,8,1024]{2,1,0:T(8,128)(2,1)S(1)}, bf16[13,8,1024]{2,1,0:T(8,128)(2,1)S(1)}, u32[]{:S(2)}, u32[]{:S(2)}) collective-permute-start(bf16[13,8,1024]{2,1,0:T(8,128)(2,1)S(1)} %relay.1.refs_3_.refs_4_), channel_id=1, source_target_pairs={{0,16},{16,0},{1,17},{17,1},{2,18},{18,2},{3,19},{19,3},{4,20},{20... | collective-permute-start | bytes 638984 | tf_op jit(solution)/shard_map/ppermute | solution.py:67
  15.2 4.7 %load_b.1 = (bf16[2048,768]{1,0:T(8,128)(2,1)S(1)}, bf16[2048,768]{1,0:T(8,128)(2,1)S(1)}, bf16[768,2048]{1,0:T(8,128)(2,1)S(1)}, bf16[2048,768]{1,0:T(8,128)(2,1)S(1)}) custom-call(bf16[2048,6144]{1,0:T(8,128)(2,1)} %refs_0_.9, bf16[2048,6144]{1,0:T(8,128)(2,1)} %refs_1_.9, bf16[6144,2048]{1,0:T(8,128)(2,1)} %refs_2_.9, ...), custom_call_target="tpu_custom_call" | custom-call | flops 1000 | bytes 1000 | tf_op jit(solution)/shard_map/load_b/pallas_call | solution.py:80
  19.9 0.0 collective-permute-done.3.refs_4_.refs_5_
  19.9 2.5 %forward_3.1 = (bf16[2048,768]{1,0:T(8,128)(2,1)S(1)}, bf16[48,2048]{1,0:T(8,128)(2,1)S(1)}, bf16[48,2048]{1,0:T(8,128)(2,1)S(1)}, f32[3,48,768]{2,1,0:T(8,128)S(1)}) custom-call(bf16[2048,6144]{1,0:T(8,128)(2,1)} %refs_0_.9, bf16[2048,6144]{1,0:T(8,128)(2,1)} %refs_1_.9, bf16[6144,2048]{1,0:T(8,128)(2,1)} %refs_2_.9, ...), custom_call_target="tpu_custom_call" | custom-call | flops 1000 | bytes 1000 | tf_op jit(solution)/shard_map/forward_3/pallas_call | solution.py:80
  22.5 0.1 collective-permute-start.4
  22.5 2.4 %forward_1.1 = (bf16[768,2048]{1,0:T(8,128)(2,1)S(1)}, f32[3,48,768]{2,1,0:T(8,128)S(1)}) custom-call(bf16[2048,6144]{1,0:T(8,128)(2,1)} %refs_0_.9, bf16[2048,6144]{1,0:T(8,128)(2,1)} %refs_1_.9, bf16[6144,2048]{1,0:T(8,128)(2,1)} %refs_2_.9, bf16[48,2048]{1,0:T(8,128)(2,1)S(1)} %get-tuple-element.38.refs_3_.tokens, ...), custom_call_target="tpu_custom_call" | custom-call | flops 1000 | bytes 1000 | tf_op jit(solution)/shard_map/forward_1/pallas_call | solution.py:80
  25.0 0.5 collective-permute-start.5
  25.5 0.0 collective-permute-done.4.arrived
  25.5 2.4 %forward_2.1.refs_5_ = bf16[3,48,768]{2,1,0:T(8,128)(2,1)S(1)} custom-call(bf16[48,2048]{1,0:T(8,128)(2,1)S(1)} %get-tuple-element.38.refs_3_.tokens, bf16[48,2048]{1,0:T(8,128)(2,1)S(1)} %get-tuple-element.39.refs_4_.cotans, bf16[2048,768]{1,0:T(8,128)(2,1)S(1)} %get-tuple-element.40.gate.refs_10_, bf16[2048,768]{1,0:T(8,128)(2,1)S(1)} %get-tuple-element.41.up.refs_11_, ...), custom_call_target="tpu_custom_call" | custom-call | flops 1000 | bytes 1000 | tf_op jit(solution)/shard_map/forward_2/pallas_call | solution.py:80
  27.9 0.0 copy-start
  27.9 1.6 %collective-permute-start.6 = (bf16[3,48,768]{2,1,0:T(8,128)(2,1)S(1)}, bf16[3,48,768]{2,1,0:T(8,128)(2,1)S(1)}, u32[]{:S(2)}, u32[]{:S(2)}) collective-permute-start(bf16[3,48,768]{2,1,0:T(8,128)(2,1)S(1)} %forward_2.1.refs_5_), channel_id=1, source_target_pairs={{0,2},{1,3},{2,0},{3,1},{4,6},{5,7},{6,4},{7,5},{8,10},{9,11},{10,... | collective-permute-start | bytes 663560 | tf_op jit(solution)/shard_map/ppermute | solution.py:67
  29.5 5.4 %forward_0.1 = (f32[3,48,768]{2,1,0:T(8,128)S(1)}, bf16[2048,768]{1,0:T(8,128)(2,1)S(1)}, bf16[2048,768]{1,0:T(8,128)(2,1)S(1)}, bf16[768,2048]{1,0:T(8,128)(2,1)}) custom-call(bf16[2048,6144]{1,0:T(8,128)(2,1)} %refs_0_.9, bf16[2048,6144]{1,0:T(8,128)(2,1)} %refs_1_.9, bf16[6144,2048]{1,0:T(8,128)(2,1)} %refs_2_.9, ...), custom_call_target="tpu_custom_call" | custom-call | flops 1000 | bytes 1000 | tf_op jit(solution)/shard_map/forward_0/pallas_call | solution.py:80
  35.0 0.0 collective-permute-done.5.refs_1_
  35.0 0.4 collective-permute-done.6.refs_2_
  35.4 0.0 copy-done
  35.4 0.4 middle.1
  35.7 0.0 collective-permute-start.8
  35.7 1.6 %collective-permute-start.7 = (bf16[112,768]{1,0:T(8,128)(2,1)S(1)}, bf16[112,768]{1,0:T(8,128)(2,1)S(1)}, u32[]{:S(2)}, u32[]{:S(2)}) collective-permute-start(bf16[112,768]{1,0:T(8,128)(2,1)S(1)} %get-tuple-element.50.message.refs_0_), channel_id=1, source_target_pairs={{0,2},{1,3},{2,0},{3,1},{4,6},{5,7},{6,4},{7,5},{8,10},{9,11},{10,... | collective-permute-start | bytes 516104 | tf_op jit(solution)/shard_map/ppermute | solution.py:67
  37.3 1.9 %backward_0.1.before = f32[48,2048]{1,0:T(8,128)S(1)} custom-call(bf16[112,768]{1,0:T(8,128)(2,1)S(1)} %get-tuple-element.50.message.refs_0_, bf16[2048,768]{1,0:T(8,128)(2,1)S(1)} %get-tuple-element.48.refs_6_.gate, bf16[2048,768]{1,0:T(8,128)(2,1)S(1)} %get-tuple-element.49.refs_7_.up), custom_call_target="tpu_custom_call" | custom-call | flops 1000 | bytes 1000 | tf_op jit(solution)/shard_map/backward_0/pallas_call | solution.py:80
  39.2 0.0 collective-permute-done.8.message.refs_1_
  39.2 1.9 %backward_1.1.before = f32[48,2048]{1,0:T(8,128)S(1)} custom-call(bf16[112,768]{1,0:T(8,128)(2,1)S(1)} %collective-permute-done.8.message.refs_1_, bf16[2048,768]{1,0:T(8,128)(2,1)S(1)} %get-tuple-element.37.refs_8_.refs_5_.gate, bf16[2048,768]{1,0:T(8,128)(2,1)S(1)} %get-tuple-element.42.refs_6_.refs_9_.up, f32[48,2048]{1,0:T(8,128)S(1)} %backward_0.1.before), custom_call_target="tpu_custom_call" | custom-call | flops 1000 | bytes 1000 | tf_op jit(solution)/shard_map/backward_1/pallas_call | solution.py:80
  41.2 1.3 %collective-permute-done.7.message.refs_2_ = bf16[112,768]{1,0:T(8,128)(2,1)S(1)} collective-permute-done((bf16[112,768]{1,0:T(8,128)(2,1)S(1)}, bf16[112,768]{1,0:T(8,128)(2,1)S(1)}, u32[]{:S(2)}, u32[]{:S(2)}) %collective-permute-start.7) | collective-permute-done | bytes 172064 | tf_op jit(solution)/shard_map/ppermute | solution.py:67
  42.5 0.0 collective-permute-start.9
  42.5 1.9 %backward_2.1.before = f32[48,2048]{1,0:T(8,128)S(1)} custom-call(bf16[112,768]{1,0:T(8,128)(2,1)S(1)} %collective-permute-done.7.message.refs_2_, bf16[2048,768]{1,0:T(8,128)(2,1)S(1)} %get-tuple-element.40.gate.refs_10_, bf16[2048,768]{1,0:T(8,128)(2,1)S(1)} %get-tuple-element.41.up.refs_11_, f32[48,2048]{1,0:T(8,128)S(1)} %backward_1.1.before), custom_call_target="tpu_custom_call" | custom-call | flops 1000 | bytes 1000 | tf_op jit(solution)/shard_map/backward_2/pallas_call | solution.py:80
  44.5 0.0 collective-permute-done.9.message
  44.5 2.0 %backward_3.1 = (f32[24,2048]{1,0:T(8,128)S(1)}, f32[8,2048]{1,0:T(8,128)S(1)}, bf16[4,8,2048]{2,1,0:T(8,128)(2,1)S(1)}) custom-call(bf16[112,768]{1,0:T(8,128)(2,1)S(1)} %collective-permute-done.9.message, bf16[2048,768]{1,0:T(8,128)(2,1)S(1)} %get-tuple-element.34.refs_5_.refs_12_.gate, bf16[2048,768]{1,0:T(8,128)(2,1)S(1)} %get-tuple-element.35.refs_6_.refs_13_.up, ...), custom_call_target="tpu_custom_call" | custom-call | flops 1000 | bytes 1000 | tf_op jit(solution)/shard_map/backward_3/pallas_call | solution.py:80
  46.5 1.2 %collective-permute-start.10 = (bf16[4,8,2048]{2,1,0:T(8,128)(2,1)S(1)}, bf16[4,8,2048]{2,1,0:T(8,128)(2,1)S(1)}, u32[]{:S(2)}, u32[]{:S(2)}) collective-permute-start(bf16[4,8,2048]{2,1,0:T(8,128)(2,1)S(1)} %get-tuple-element.56), channel_id=1, source_target_pairs={{0,16},{16,0},{1,17},{17,1},{2,18},{18,2},{3,19},{19,3},{4,20},{20... | collective-permute-start | bytes 393224 | tf_op jit(solution)/shard_map/ppermute | solution.py:67
  47.6 4.8 %collective-permute-done.10.arrived = bf16[4,8,2048]{2,1,0:T(8,128)(2,1)S(1)} collective-permute-done((bf16[4,8,2048]{2,1,0:T(8,128)(2,1)S(1)}, bf16[4,8,2048]{2,1,0:T(8,128)(2,1)S(1)}, u32[]{:S(2)}, u32[]{:S(2)}) %collective-permute-start.10) | collective-permute-done | bytes 131104 | tf_op jit(solution)/shard_map/ppermute | solution.py:67
  52.4 0.7 %combine.1 = (f32[4,1536]{1,0:T(4,128)}, f32[8,2048]{1,0:T(8,128)S(1)}, bf16[8,2048]{1,0:T(8,128)(2,1)S(1)}, bf16[8,2048]{1,0:T(8,128)(2,1)S(1)}, bf16[8,2048]{1,0:T(8,128)(2,1)S(1)}) custom-call(f32[24,2048]{1,0:T(8,128)S(1)} %get-tuple-element.54.own, f32[8,2048]{1,0:T(8,128)S(1)} %get-tuple-element.55.own_tail, ...), custom_call_target="tpu_custom_call" | custom-call | flops 1000 | bytes 1000 | tf_op jit(solution)/shard_map/combine/pallas_call | solution.py:80
  53.1 0.0 collective-permute-start.11
  53.1 2.4 %collective-permute-start.12 = (bf16[8,2048]{1,0:T(8,128)(2,1)S(1)}, bf16[8,2048]{1,0:T(8,128)(2,1)S(1)}, u32[]{:S(2)}, u32[]{:S(2)}) collective-permute-start(bf16[8,2048]{1,0:T(8,128)(2,1)S(1)} %get-tuple-element.61), channel_id=1, source_target_pairs={{0,8},{4,12},{8,0},{12,4},{1,9},{5,13},{9,1},{13,5},{2,10},{6,14},... | collective-permute-start | bytes 98312 | tf_op jit(solution)/shard_map/ppermute | solution.py:67
  55.5 2.0 %collective-permute-start.13 = (bf16[8,2048]{1,0:T(8,128)(2,1)S(1)}, bf16[8,2048]{1,0:T(8,128)(2,1)S(1)}, u32[]{:S(2)}, u32[]{:S(2)}) collective-permute-start(bf16[8,2048]{1,0:T(8,128)(2,1)S(1)} %get-tuple-element.62), channel_id=1, source_target_pairs={{0,12},{4,8},{8,4},{12,0},{1,13},{5,9},{9,5},{13,1},{2,14},{6,10},... | collective-permute-start | bytes 98312 | tf_op jit(solution)/shard_map/ppermute | solution.py:67
  57.5 0.0 collective-permute-done.11.refs_1_
  57.5 0.7 %collective-permute-done.12.refs_2_ = bf16[8,2048]{1,0:T(8,128)(2,1)S(1)} collective-permute-done((bf16[8,2048]{1,0:T(8,128)(2,1)S(1)}, bf16[8,2048]{1,0:T(8,128)(2,1)S(1)}, u32[]{:S(2)}, u32[]{:S(2)}) %collective-permute-start.12) | collective-permute-done | bytes 32800 | tf_op jit(solution)/shard_map/ppermute | solution.py:67
  58.2 3.0 %collective-permute-done.13.refs_3_ = bf16[8,2048]{1,0:T(8,128)(2,1)S(1)} collective-permute-done((bf16[8,2048]{1,0:T(8,128)(2,1)S(1)}, bf16[8,2048]{1,0:T(8,128)(2,1)S(1)}, u32[]{:S(2)}, u32[]{:S(2)}) %collective-permute-start.13) | collective-permute-done | bytes 32800 | tf_op jit(solution)/shard_map/ppermute | solution.py:67
  61.2 0.7 %last.1 = (bf16[6,2048]{1,0:T(8,128)(2,1)}, f32[4]{0:T(128)}) custom-call(f32[8,2048]{1,0:T(8,128)S(1)} %get-tuple-element.59.refs_0_, bf16[8,2048]{1,0:T(8,128)(2,1)S(1)} %collective-permute-done.11.refs_1_, bf16[8,2048]{1,0:T(8,128)(2,1)S(1)} %collective-permute-done.12.refs_2_, bf16[8,2048]{1,0:T(8,128)(2,1)S(1)} %collective-permute-done.13.refs_3_), custom_call_target="tpu_custom_call" | custom-call | flops 1000 | bytes 1000 | tf_op jit(solution)/shard_map/last/pallas_call | solution.py:80
Async XLA Ops:
  1.4 11.6 %copy-start.1 = (s32[24]{0:T(128)S(1)}, s32[24]{0:T(128)}, u32[]{:S(2)}) copy-start(s32[24]{0:T(128)} %refs_4_.1) | copy-start | bytes 292
  1.4 9.5 %collective-permute-start = (bf16[3,8,1024]{2,1,0:T(8,128)(2,1)S(1)}, bf16[3,8,1024]{2,1,0:T(8,128)(2,1)S(1)}, u32[]{:S(2)}, u32[]{:S(2)}) collective-permute-start(bf16[3,8,1024]{2,1,0:T(8,128)(2,1)S(1)} %pack.1.refs_0_), channel_id=1, source_target_pairs={{0,4},{4,0},{8,12},{12,8},{1,5},{5,1},{9,13},{13,9},{2,6},{6,2},{1... | collective-permute-start | bytes 147464 | tf_op jit(solution)/shard_map/ppermute | solution.py:67
  4.5 6.4 %collective-permute-start.1 = (bf16[3,8,1024]{2,1,0:T(8,128)(2,1)S(1)}, bf16[3,8,1024]{2,1,0:T(8,128)(2,1)S(1)}, u32[]{:S(2)}, u32[]{:S(2)}) collective-permute-start(bf16[3,8,1024]{2,1,0:T(8,128)(2,1)S(1)} %pack.1.refs_0_), channel_id=1, source_target_pairs={{0,8},{4,12},{8,0},{12,4},{1,9},{5,13},{9,1},{13,5},{2,10},{6,14},... | collective-permute-start | bytes 147464 | tf_op jit(solution)/shard_map/ppermute | solution.py:67
  7.1 5.9 %collective-permute-start.2 = (bf16[3,8,1024]{2,1,0:T(8,128)(2,1)S(1)}, bf16[3,8,1024]{2,1,0:T(8,128)(2,1)S(1)}, u32[]{:S(2)}, u32[]{:S(2)}) collective-permute-start(bf16[3,8,1024]{2,1,0:T(8,128)(2,1)S(1)} %pack.1.refs_0_), channel_id=1, source_target_pairs={{0,12},{4,8},{8,4},{12,0},{1,13},{5,9},{9,5},{13,1},{2,14},{6,10},... | collective-permute-start | bytes 147464 | tf_op jit(solution)/shard_map/ppermute | solution.py:67
  13.6 6.3 %collective-permute-start.3 = (bf16[13,8,1024]{2,1,0:T(8,128)(2,1)S(1)}, bf16[13,8,1024]{2,1,0:T(8,128)(2,1)S(1)}, u32[]{:S(2)}, u32[]{:S(2)}) collective-permute-start(bf16[13,8,1024]{2,1,0:T(8,128)(2,1)S(1)} %relay.1.refs_3_.refs_4_), channel_id=1, source_target_pairs={{0,16},{16,0},{1,17},{17,1},{2,18},{18,2},{3,19},{19,3},{4,20},{20... | collective-permute-start | bytes 638984 | tf_op jit(solution)/shard_map/ppermute | solution.py:67
  22.5 3.1 %collective-permute-start.4 = (f32[3,48,768]{2,1,0:T(8,128)S(1)}, f32[3,48,768]{2,1,0:T(8,128)S(1)}, u32[]{:S(2)}, u32[]{:S(2)}) collective-permute-start(f32[3,48,768]{2,1,0:T(8,128)S(1)} %get-tuple-element.45), channel_id=1, source_target_pairs={{0,1},{1,0},{2,3},{3,2},{4,5},{5,4},{6,7},{7,6},{8,9},{9,8},{10,11... | collective-permute-start | bytes 1327112 | tf_op jit(solution)/shard_map/ppermute | solution.py:67
  25.0 10.0 %collective-permute-start.5 = (f32[3,48,768]{2,1,0:T(8,128)S(1)}, f32[3,48,768]{2,1,0:T(8,128)S(1)}, u32[]{:S(2)}, u32[]{:S(2)}) collective-permute-start(f32[3,48,768]{2,1,0:T(8,128)S(1)} %get-tuple-element.47), channel_id=1, source_target_pairs={{0,1},{1,0},{2,3},{3,2},{4,5},{5,4},{6,7},{7,6},{8,9},{9,8},{10,11... | collective-permute-start | bytes 1327112 | tf_op jit(solution)/shard_map/ppermute | solution.py:67
  27.9 7.5 %copy-start = (f32[6144]{0:T(1024)S(1)}, f32[6144]{0:T(1024)}, u32[]{:S(2)}) copy-start(f32[6144]{0:T(1024)} %param.12) | copy-start | bytes 73732
  27.9 7.4 %collective-permute-start.6 = (bf16[3,48,768]{2,1,0:T(8,128)(2,1)S(1)}, bf16[3,48,768]{2,1,0:T(8,128)(2,1)S(1)}, u32[]{:S(2)}, u32[]{:S(2)}) collective-permute-start(bf16[3,48,768]{2,1,0:T(8,128)(2,1)S(1)} %forward_2.1.refs_5_), channel_id=1, source_target_pairs={{0,2},{1,3},{2,0},{3,1},{4,6},{5,7},{6,4},{7,5},{8,10},{9,11},{10,... | collective-permute-start | bytes 663560 | tf_op jit(solution)/shard_map/ppermute | solution.py:67
  35.7 3.5 %collective-permute-start.8 = (bf16[112,768]{1,0:T(8,128)(2,1)S(1)}, bf16[112,768]{1,0:T(8,128)(2,1)S(1)}, u32[]{:S(2)}, u32[]{:S(2)}) collective-permute-start(bf16[112,768]{1,0:T(8,128)(2,1)S(1)} %get-tuple-element.50.message.refs_0_), channel_id=1, source_target_pairs={{0,1},{1,0},{2,3},{3,2},{4,5},{5,4},{6,7},{7,6},{8,9},{9,8},{10,11... | collective-permute-start | bytes 516104 | tf_op jit(solution)/shard_map/ppermute | solution.py:67
  35.7 6.8 %collective-permute-start.7 = (bf16[112,768]{1,0:T(8,128)(2,1)S(1)}, bf16[112,768]{1,0:T(8,128)(2,1)S(1)}, u32[]{:S(2)}, u32[]{:S(2)}) collective-permute-start(bf16[112,768]{1,0:T(8,128)(2,1)S(1)} %get-tuple-element.50.message.refs_0_), channel_id=1, source_target_pairs={{0,2},{1,3},{2,0},{3,1},{4,6},{5,7},{6,4},{7,5},{8,10},{9,11},{10,... | collective-permute-start | bytes 516104 | tf_op jit(solution)/shard_map/ppermute | solution.py:67
  42.5 1.9 %collective-permute-start.9 = (bf16[112,768]{1,0:T(8,128)(2,1)S(1)}, bf16[112,768]{1,0:T(8,128)(2,1)S(1)}, u32[]{:S(2)}, u32[]{:S(2)}) collective-permute-start(bf16[112,768]{1,0:T(8,128)(2,1)S(1)} %collective-permute-done.7.message.refs_2_), channel_id=1, source_target_pairs={{0,1},{1,0},{2,3},{3,2},{4,5},{5,4},{6,7},{7,6},{8,9},{9,8},{10,11... | collective-permute-start | bytes 516104 | tf_op jit(solution)/shard_map/ppermute | solution.py:67
  46.5 6.0 %collective-permute-start.10 = (bf16[4,8,2048]{2,1,0:T(8,128)(2,1)S(1)}, bf16[4,8,2048]{2,1,0:T(8,128)(2,1)S(1)}, u32[]{:S(2)}, u32[]{:S(2)}) collective-permute-start(bf16[4,8,2048]{2,1,0:T(8,128)(2,1)S(1)} %get-tuple-element.56), channel_id=1, source_target_pairs={{0,16},{16,0},{1,17},{17,1},{2,18},{18,2},{3,19},{19,3},{4,20},{20... | collective-permute-start | bytes 393224 | tf_op jit(solution)/shard_map/ppermute | solution.py:67
  53.1 4.4 %collective-permute-start.11 = (bf16[8,2048]{1,0:T(8,128)(2,1)S(1)}, bf16[8,2048]{1,0:T(8,128)(2,1)S(1)}, u32[]{:S(2)}, u32[]{:S(2)}) collective-permute-start(bf16[8,2048]{1,0:T(8,128)(2,1)S(1)} %get-tuple-element.60), channel_id=1, source_target_pairs={{0,4},{4,0},{8,12},{12,8},{1,5},{5,1},{9,13},{13,9},{2,6},{6,2},{1... | collective-permute-start | bytes 98312 | tf_op jit(solution)/shard_map/ppermute | solution.py:67
  53.1 5.1 %collective-permute-start.12 = (bf16[8,2048]{1,0:T(8,128)(2,1)S(1)}, bf16[8,2048]{1,0:T(8,128)(2,1)S(1)}, u32[]{:S(2)}, u32[]{:S(2)}) collective-permute-start(bf16[8,2048]{1,0:T(8,128)(2,1)S(1)} %get-tuple-element.61), channel_id=1, source_target_pairs={{0,8},{4,12},{8,0},{12,4},{1,9},{5,13},{9,1},{13,5},{2,10},{6,14},... | collective-permute-start | bytes 98312 | tf_op jit(solution)/shard_map/ppermute | solution.py:67
  55.5 5.7 %collective-permute-start.13 = (bf16[8,2048]{1,0:T(8,128)(2,1)S(1)}, bf16[8,2048]{1,0:T(8,128)(2,1)S(1)}, u32[]{:S(2)}, u32[]{:S(2)}) collective-permute-start(bf16[8,2048]{1,0:T(8,128)(2,1)S(1)} %get-tuple-element.62), channel_id=1, source_target_pairs={{0,12},{4,8},{8,4},{12,0},{1,13},{5,9},{9,5},{13,1},{2,14},{6,10},... | collective-permute-start | bytes 98312 | tf_op jit(solution)/shard_map/ppermute | solution.py:67

commit v5 on v4

--- a/solution.py
+++ b/solution.py
@@ -169,9 +169,11 @@
         put(DOWN, span, contract_rows(cotans[...], down[span, :]))
 
 
-def forward_kernel(tokens, cotans, gate, up, down, out):
+def forward_kernel(tokens, cotans, gate, up, down, *refs):
+    out = refs[-1]
+
     def put(kind, span, part):
-        out[kind, :, span] = part
+        out[kind, :, span] = part.astype(out.dtype)
 
     strip_parts(tokens, cotans, gate, up, down, put)
 
@@ -200,15 +202,18 @@
 
 
 def own_strip_kernel(groups, *refs):
-    sources, (tokens, cotans) = refs[:3], refs[3:5]
-    out, (gate, up, down), sem = refs[-5], refs[-4:-1], refs[-1]
-    pieces = [(kind, 0) for kind in WHOLE_STRIP]
-    copies = start_loads(pieces, groups, sources, (gate, up, down), sem)
-    copies[GATE].wait()
-    out[GATE] = jnp.dot(tokens[...], gate[...], preferred_element_type=jnp.float32)
-    copies[UP].wait()
-    out[UP] = jnp.dot(tokens[...], up[...], preferred_element_type=jnp.float32)
-    copies[DOWN].wait()
+    sources, (tokens, cotans, gate, up) = refs[:3], refs[3:7]
+    out, down, sem = refs[-3:]
+    copies = start_loads([(DOWN, 0)], groups, sources, [down], sem)
+    tile = 256
+
+    @pl.loop(0, gate.shape[1] // tile)
+    def _(i):
+        span = pl.ds(pl.multiple_of(i * tile, tile), tile)
+        out[GATE, :, span] = jnp.dot(tokens[...], gate[:, span], preferred_element_type=jnp.float32)
+        out[UP, :, span] = jnp.dot(tokens[...], up[:, span], preferred_element_type=jnp.float32)
+
+    copies[0].wait()
     out[DOWN] = contract_rows(cotans[...], down[...])
 
 
@@ -217,7 +222,7 @@
     message, grads, other_grads, stage = refs[-4:]
     _, tokens, width = own.shape
     narrow, group = lax.axis_index("narrow"), lax.axis_index("groups")
-    sums = [own[i] + arrived[i] + crossed[i].astype(jnp.float32) for i in range(3)]
+    sums = [own[i] + arrived[i].astype(jnp.float32) + crossed[i].astype(jnp.float32) for i in range(3)]
     start = pl.multiple_of((narrow * groups + group) * width, width)
     product, d_gate, d_up = local_grads(*sums, scale[:, pl.ds(start, width)])
     message[0:tokens, :] = d_gate
@@ -271,24 +276,24 @@
     others, other_grads = refs[:3], refs[3]
     own, own_tail, send = refs[4:7]
     half, features = own.shape
+    wide = send.shape[2]
     for start in range(0, features, TILE):
         span = slice(start, start + TILE)
         total = before[:, span] + backward_part(message, gate, up, start)
         own[:, span] = total[:half]
+        at = slice(start % wide, start % wide + TILE)
         for k in range(half // 8):
-            send[k, :, span] = total[half + 8 * k : half + 8 * k + 8].astype(jnp.bfloat16)
+            slab = start // wide * (half // 8) + k
+            send[slab, :, at] = total[half + 8 * k : half + 8 * k + 8].astype(jnp.bfloat16)
     squares = sum(ref[ref.shape[0] - 16 :, 0:128].astype(jnp.float32) for ref in (message,) + others)
     high, low = split_high(squares[0:8] + squares[8:16])
     own_tail[...] = jnp.zeros_like(own_tail)
     width = other_grads.shape[1]
     for i, rows in enumerate(split_high(other_grads[...])):
         own_tail[i * SEQS : (i + 1) * SEQS, 0:width] = rows
-    first = features - 8 * 128
-    for k in range(8):
-        span = slice(first + k * 128, first + (k + 1) * 128)
-        own_tail[0:1, span] = high[k : k + 1]
-        own_tail[1:2, span] = low[k : k + 1]
-    send[half // 8] = own_tail[...].astype(jnp.bfloat16)
+    own_tail[:, width : width + 128] = high
+    own_tail[:, width + 128 : width + 256] = low
+    send[send.shape[0] - 1] = own_tail[...].astype(jnp.bfloat16)
 
 
 def combine_kernel(share, own, own_tail, arrived, grads, *refs):
@@ -296,16 +301,22 @@
     half, features = own.shape
     width = grads.shape[1]
     group = lax.axis_index("groups")
-    slabs = half // 8
+    slabs, wide = half // 8, own_tail.shape[1]
     for k in range(slabs):
-        total[8 * k : 8 * k + 8, :] = own[8 * k : 8 * k + 8, :] + arrived[k].astype(jnp.float32)
-    tail = arrived[slabs].astype(jnp.float32)
+        for i in range(features // wide):
+            span = slice(i * wide, (i + 1) * wide)
+            total[8 * k : 8 * k + 8, span] = own[8 * k : 8 * k + 8, span] + arrived[i * slabs + k].astype(jnp.float32)
+    tail = arrived[arrived.shape[0] - 1].astype(jnp.float32)
     other = tail[0:SEQS, 0:width] + tail[SEQS : 2 * SEQS, 0:width]
     example_grads[:, pl.ds(pl.multiple_of(group * width, width), width)] = grads[...]
     example_grads[:, pl.ds(pl.multiple_of((1 - group) * width, width), width)] = other
-    first, lanes = features - 8 * 128, SEQS * 128
-    here = own_tail[0:1, first : first + lanes] + own_tail[1:2, first : first + lanes]
-    there = tail[0:1, first + lanes : first + 2 * lanes] + tail[1:2, first + lanes : first + 2 * lanes]
+    lanes = SEQS * 128
+
+    def squares(ref, first):
+        rows = ref[:, width : width + 128] + ref[:, width + 128 : width + 256]
+        return jnp.concatenate([rows[first + e : first + e + 1] for e in range(SEQS)], axis=1)
+
+    here, there = squares(own_tail[...], 0), squares(tail, SEQS)
     high, low = split_high(here + there)
     for i, target in enumerate((own_block,) + tuple(sends)):
         rows = total[i * share : (i + 1) * share, :]
@@ -385,47 +396,50 @@
         [pltpu.with_memory_space_constraint(array, pltpu.HBM) for array in (inputs, cotangent)],
         scratch=[pltpu.VMEM((4 * share, features // 2), f32)],
     )
-    arrived = {s: exchange(packed, "wide", s) for s in reversed(range(1, wide))}
+    arrived = [exchange(packed, "wide", s) for s in range(1, wide)]
     load("load_a", [(kind, 3) for kind in WHOLE_STRIP])
     relayed = call(
         functools.partial(relay_kernel, share),
         "relay",
         pltpu.VMEM((wide * slabs + 1, 8, features // 2), bf16),
-        [packed] + [arrived[s] for s in range(1, wide)] + [seq_ids] + hold(3, [GATE]),
+        [packed] + arrived + [seq_ids] + hold(3, [GATE]),
         {wide: pltpu.SMEM},
     )
     other_relayed = exchange(relayed, "groups", 1)
-    load("load_b", [(kind, 1) for kind in WHOLE_STRIP] + [(GATE, 2)], [relayed])
+    load("load_b", [(kind, 2) for kind in WHOLE_STRIP] + [(GATE, 1)], [relayed])
 
     part = pltpu.VMEM((3, tokens, width), f32)
+    near_shape = pltpu.VMEM((3, tokens, width), bf16)
     tokens_all, cotans_all, diagonal = call_loading(
         functools.partial(first_kernel, share),
         "forward_3",
-        [(UP, 2)],
+        [(UP, 1)],
         [pltpu.VMEM((tokens, features), bf16)] * 2 + [part],
-        [relayed, other_relayed] + hold(3) + hold(1, [GATE]),
+        [relayed, other_relayed] + hold(3) + hold(2, [GATE]),
         [pltpu.VMEM((tokens, features), f32)] * 2,
     )
     panel = [tokens_all, cotans_all]
     diagonal = exchange(diagonal, "narrow", 1)
-    (near,) = call_loading(forward_kernel, "forward_1", [(DOWN, 2)], [part], panel + hold(1))
-    near = exchange(near, "narrow", 1)
-    crossing = call(
+    (crossing,) = call_loading(
         forward_add_kernel,
         "forward_2",
-        pltpu.VMEM((3, tokens, width), bf16),
+        [(DOWN, 1)],
+        [pltpu.VMEM((3, tokens, width), bf16)],
         panel + hold(2) + [diagonal],
     )
     crossed = exchange(crossing, "narrow", 2)
-    own_part, *arrays = call(
+    (near,) = call_loading(
+        forward_kernel, "forward_1", [(GATE, 0), (UP, 0)], [near_shape], panel + hold(1) + [held(crossing)]
+    )
+    near = exchange(near, "narrow", 1)
+    own_part, kept[DOWN, 0] = call(
         functools.partial(own_strip_kernel, groups),
         "forward_0",
-        [part] + weight_shapes,
-        list(weights) + panel + [held(crossing)],
+        [part, weight_shapes[DOWN]],
+        list(weights) + panel + hold(0, [GATE, UP]),
         {i: pltpu.HBM for i in range(3)},
-        [pltpu.SemaphoreType.DMA((3,))],
-    )
-    kept.update({(kind, 0): array for kind, array in enumerate(arrays)})
+        [pltpu.SemaphoreType.DMA((1,))],
+    )
 
     resident = [array for s in range(strips) for array in hold(s, [GATE, UP])]
     message, grads, other_grads = call(
@@ -453,8 +467,8 @@
         "backward_3",
         [
             pltpu.VMEM((half, features), f32),
-            pltpu.VMEM((8, features), f32),
-            pltpu.VMEM((half // 8 + 1, 8, features), bf16),
+            pltpu.VMEM((8, features // 2), f32),
+            pltpu.VMEM((half // 4 + 1, 8, features // 2), bf16),
         ],
         [message_3] + hold(3, [GATE, UP]) + [sums, message, message_1, message_2, other_grads],
     )
@@ -467,7 +481,7 @@
         [own, own_tail, arrived, grads],
         scratch=[pltpu.VMEM((half + 8, features), f32)],
     )
-    arrived = [exchange(block, "wide", s + 1) for s, block in enumerate(sends)]
+    arrived = [exchange(sends[s - 1], "wide", s) for s in reversed(range(1, wide))]
     input_grad, norms = call(
         last_kernel,
         "last",
@@ -491,9 +505,9 @@
         and narrow == 4
         and power_of_two(wide)
         and hidden % (narrow * groups * 256) == 0
-        and features % TILE == 0
         and features >= 2048
-        and width <= features - 1024
+        and width <= features // 2 - 256
+        and features % (2 * TILE) == 0
         and share <= 6
         and share % 2 == 0
         and (share * wide) % 8 == 0

time: 62 us -> 59.8 us (0.965)
  Pallas kernels: 32.1 us -> 30.8 us
  starting transfers between devices: 16.6 us -> 15.9 us
    pallas_call x15, Pallas kernels: 32.1 us -> 30.8 us  [call(): pl.pallas_call(body, out_shape=outs, in_specs=[pl.BlockSpec(memory_space=...]
    ppermute x14, starting transfers between devices: 16.6 us -> 15.9 us  [exchange(): lax.ppermute(array, axis, [(i, i ^ step) for i in range(lax.axis_size(axi...]
  transfers between devices with their start and end apart: 14 -> 14, of which waited for: 6 -> 6; matrix products, arithmetic and copies ran while one was open for 0% -> 0% of each run, Pallas kernels for 40% -> 35%
where the time goes in v5:
time: 59.8 us; the launch traced here: 59.6 us
  Pallas kernels  30.8 us (52%)
  starting transfers between devices  15.9 us (27%)
  waiting for transfers between devices  12.1 us (20%)
  between operations  0.82 us (1%)
    pallas_call x15, Pallas kernels, call(): pl.pallas_call(body, out_shape=outs, in_specs=[pl.BlockSpec(memory_space=...  30.8 us
    ppermute x14, starting transfers between devices, exchange(): lax.ppermute(array, axis, [(i, i ^ step) for i in range(lax.axis_size(axi...  15.9 us
    ppermute x14, waiting for transfers between devices, exchange(): lax.ppermute(array, axis, [(i, i ^ step) for i in range(lax.axis_size(axi...  12.1 us
  transfers between devices with their start and end apart: 14, of which 6 were waited for; matrix products, arithmetic and copies ran while one was open for 0% of the time, Pallas kernels for 35%

profile of v5, /device:TPU:0, one launch (start us, length us, event | category | flops | bytes accessed | tf_op | source)
XLA Modules:
  0.0 59.6 jit_solution(4142580326759542155)
XLA Ops:
  0.6 0.8 %pack.1.refs_0_ = bf16[3,8,1024]{2,1,0:T(8,128)(2,1)S(1)} custom-call(bf16[6,2048]{1,0:T(8,128)(2,1)} %inputs.1, bf16[6,2048]{1,0:T(8,128)(2,1)} %cotangent.1), custom_call_target="tpu_custom_call" | custom-call | flops 1000 | bytes 1000 | tf_op jit(solution)/shard_map/pack/pallas_call | solution.py:80
  1.4 0.0 copy-start.1
  1.4 5.1 %collective-permute-start.2 = (bf16[3,8,1024]{2,1,0:T(8,128)(2,1)S(1)}, bf16[3,8,1024]{2,1,0:T(8,128)(2,1)S(1)}, u32[]{:S(2)}, u32[]{:S(2)}) collective-permute-start(bf16[3,8,1024]{2,1,0:T(8,128)(2,1)S(1)} %pack.1.refs_0_), channel_id=1, source_target_pairs={{0,12},{4,8},{8,4},{12,0},{1,13},{5,9},{9,5},{13,1},{2,14},{6,10},... | collective-permute-start | bytes 147464 | tf_op jit(solution)/shard_map/ppermute | solution.py:67
  6.6 0.0 collective-permute-start.1
  6.6 0.6 %collective-permute-start = (bf16[3,8,1024]{2,1,0:T(8,128)(2,1)S(1)}, bf16[3,8,1024]{2,1,0:T(8,128)(2,1)S(1)}, u32[]{:S(2)}, u32[]{:S(2)}) collective-permute-start(bf16[3,8,1024]{2,1,0:T(8,128)(2,1)S(1)} %pack.1.refs_0_), channel_id=1, source_target_pairs={{0,4},{4,0},{8,12},{12,8},{1,5},{5,1},{9,13},{13,9},{2,6},{6,2},{1... | collective-permute-start | bytes 147464 | tf_op jit(solution)/shard_map/ppermute | solution.py:67
  7.2 3.8 %load_a.1 = (bf16[2048,768]{1,0:T(8,128)(2,1)S(1)}, bf16[2048,768]{1,0:T(8,128)(2,1)S(1)}, bf16[768,2048]{1,0:T(8,128)(2,1)S(1)}) custom-call(bf16[2048,6144]{1,0:T(8,128)(2,1)} %refs_0_.11, bf16[2048,6144]{1,0:T(8,128)(2,1)} %refs_1_.11, bf16[6144,2048]{1,0:T(8,128)(2,1)} %refs_2_.11), custom_call_target="tpu_custom_call" | custom-call | flops 1000 | bytes 1000 | tf_op jit(solution)/shard_map/load_a/pallas_call | solution.py:80
  11.0 0.0 collective-permute-done.2.refs_3_
  11.0 0.5 collective-permute-done.1.refs_2_
  11.5 0.0 collective-permute-done.refs_1_
  11.5 0.0 copy-done.1
  11.5 0.6 relay.1.refs_3_.refs_4_
  12.1 1.6 %collective-permute-start.3 = (bf16[13,8,1024]{2,1,0:T(8,128)(2,1)S(1)}, bf16[13,8,1024]{2,1,0:T(8,128)(2,1)S(1)}, u32[]{:S(2)}, u32[]{:S(2)}) collective-permute-start(bf16[13,8,1024]{2,1,0:T(8,128)(2,1)S(1)} %relay.1.refs_3_.refs_4_), channel_id=1, source_target_pairs={{0,16},{16,0},{1,17},{17,1},{2,18},{18,2},{3,19},{19,3},{4,20},{20... | collective-permute-start | bytes 638984 | tf_op jit(solution)/shard_map/ppermute | solution.py:67
  13.7 4.8 %load_b.1 = (bf16[2048,768]{1,0:T(8,128)(2,1)S(1)}, bf16[2048,768]{1,0:T(8,128)(2,1)S(1)}, bf16[768,2048]{1,0:T(8,128)(2,1)S(1)}, bf16[2048,768]{1,0:T(8,128)(2,1)S(1)}) custom-call(bf16[2048,6144]{1,0:T(8,128)(2,1)} %refs_0_.11, bf16[2048,6144]{1,0:T(8,128)(2,1)} %refs_1_.11, bf16[6144,2048]{1,0:T(8,128)(2,1)} %refs_2_.11, ...), custom_call_target="tpu_custom_call" | custom-call | flops 1000 | bytes 1000 | tf_op jit(solution)/shard_map/load_b/pallas_call | solution.py:80
  18.5 0.0 collective-permute-done.3.refs_4_.refs_5_
  18.5 2.5 %forward_3.1 = (bf16[2048,768]{1,0:T(8,128)(2,1)S(1)}, bf16[48,2048]{1,0:T(8,128)(2,1)S(1)}, bf16[48,2048]{1,0:T(8,128)(2,1)S(1)}, f32[3,48,768]{2,1,0:T(8,128)S(1)}) custom-call(bf16[2048,6144]{1,0:T(8,128)(2,1)} %refs_0_.11, bf16[2048,6144]{1,0:T(8,128)(2,1)} %refs_1_.11, bf16[6144,2048]{1,0:T(8,128)(2,1)} %refs_2_.11, ...), custom_call_target="tpu_custom_call" | custom-call | flops 1000 | bytes 1000 | tf_op jit(solution)/shard_map/forward_3/pallas_call | solution.py:80
  21.1 0.1 collective-permute-start.4
  21.1 1.8 %collective-permute-done.4.refs_8_ = f32[3,48,768]{2,1,0:T(8,128)S(1)} collective-permute-done((f32[3,48,768]{2,1,0:T(8,128)S(1)}, f32[3,48,768]{2,1,0:T(8,128)S(1)}, u32[]{:S(2)}, u32[]{:S(2)}) %collective-permute-start.4) | collective-permute-done | bytes 442400 | tf_op jit(solution)/shard_map/ppermute | solution.py:67
  22.9 2.4 %forward_2.1 = (bf16[768,2048]{1,0:T(8,128)(2,1)S(1)}, bf16[3,48,768]{2,1,0:T(8,128)(2,1)S(1)}) custom-call(bf16[2048,6144]{1,0:T(8,128)(2,1)} %refs_0_.11, bf16[2048,6144]{1,0:T(8,128)(2,1)} %refs_1_.11, bf16[6144,2048]{1,0:T(8,128)(2,1)} %refs_2_.11, bf16[48,2048]{1,0:T(8,128)(2,1)S(1)} %get-tuple-element.39.refs_3_, ...), custom_call_target="tpu_custom_call" | custom-call | flops 1000 | bytes 1000 | tf_op jit(solution)/shard_map/forward_2/pallas_call | solution.py:80
  25.4 1.5 %collective-permute-start.6 = (bf16[3,48,768]{2,1,0:T(8,128)(2,1)S(1)}, bf16[3,48,768]{2,1,0:T(8,128)(2,1)S(1)}, u32[]{:S(2)}, u32[]{:S(2)}) collective-permute-start(bf16[3,48,768]{2,1,0:T(8,128)(2,1)S(1)} %get-tuple-element.47.refs_8_), channel_id=1, source_target_pairs={{0,2},{1,3},{2,0},{3,1},{4,6},{5,7},{6,4},{7,5},{8,10},{9,11},{10,... | collective-permute-start | bytes 663560 | tf_op jit(solution)/shard_map/ppermute | solution.py:67
  26.9 2.9 %forward_1.1 = (bf16[2048,768]{1,0:T(8,128)(2,1)S(1)}, bf16[2048,768]{1,0:T(8,128)(2,1)S(1)}, bf16[3,48,768]{2,1,0:T(8,128)(2,1)S(1)}) custom-call(bf16[2048,6144]{1,0:T(8,128)(2,1)} %refs_0_.11, bf16[2048,6144]{1,0:T(8,128)(2,1)} %refs_1_.11, bf16[6144,2048]{1,0:T(8,128)(2,1)} %refs_2_.11, bf16[48,2048]{1,0:T(8,128)(2,1)S(1)} %get-tuple-element.39.refs_3_, ...), custom_call_target="tpu_custom_call" | custom-call | flops 1000 | bytes 1000 | tf_op jit(solution)/shard_map/forward_1/pallas_call | solution.py:80
  29.8 0.1 collective-permute-start.5
  29.8 0.0 copy-start
  29.8 3.5 %forward_0.1 = (f32[3,48,768]{2,1,0:T(8,128)S(1)}, bf16[768,2048]{1,0:T(8,128)(2,1)}) custom-call(bf16[2048,6144]{1,0:T(8,128)(2,1)} %refs_0_.11, bf16[2048,6144]{1,0:T(8,128)(2,1)} %refs_1_.11, bf16[6144,2048]{1,0:T(8,128)(2,1)} %refs_2_.11, bf16[48,2048]{1,0:T(8,128)(2,1)S(1)} %get-tuple-element.39.refs_3_, ...), custom_call_target="tpu_custom_call" | custom-call | flops 1000 | bytes 1000 | tf_op jit(solution)/shard_map/forward_0/pallas_call | solution.py:80
  33.4 0.0 collective-permute-done.6.refs_2_
  33.4 0.0 collective-permute-done.5.refs_1_
  33.4 0.0 copy-done
  33.4 0.4 middle.1
  33.8 0.5 collective-permute-start.8
  34.3 0.6 collective-permute-start.7
  34.9 1.9 %backward_0.1.before = f32[48,2048]{1,0:T(8,128)S(1)} custom-call(bf16[112,768]{1,0:T(8,128)(2,1)S(1)} %get-tuple-element.52.message.refs_0_, bf16[2048,768]{1,0:T(8,128)(2,1)S(1)} %get-tuple-element.48.refs_5_.refs_6_.gate, bf16[2048,768]{1,0:T(8,128)(2,1)S(1)} %get-tuple-element.49.refs_6_.refs_7_.up), custom_call_target="tpu_custom_call" | custom-call | flops 1000 | bytes 1000 | tf_op jit(solution)/shard_map/backward_0/pallas_call | solution.py:80
  36.8 0.0 collective-permute-done.8.message.refs_1_
  36.8 1.9 %backward_1.1.before = f32[48,2048]{1,0:T(8,128)S(1)} custom-call(bf16[112,768]{1,0:T(8,128)(2,1)S(1)} %collective-permute-done.8.message.refs_1_, bf16[2048,768]{1,0:T(8,128)(2,1)S(1)} %get-tuple-element.41.refs_5_.refs_8_.gate, bf16[2048,768]{1,0:T(8,128)(2,1)S(1)} %get-tuple-element.42.refs_6_.refs_9_.up, f32[48,2048]{1,0:T(8,128)S(1)} %backward_0.1.before), custom_call_target="tpu_custom_call" | custom-call | flops 1000 | bytes 1000 | tf_op jit(solution)/shard_map/backward_1/pallas_call | solution.py:80
  38.7 1.9 %collective-permute-done.7.message.refs_2_ = bf16[112,768]{1,0:T(8,128)(2,1)S(1)} collective-permute-done((bf16[112,768]{1,0:T(8,128)(2,1)S(1)}, bf16[112,768]{1,0:T(8,128)(2,1)S(1)}, u32[]{:S(2)}, u32[]{:S(2)}) %collective-permute-start.7) | collective-permute-done | bytes 172064 | tf_op jit(solution)/shard_map/ppermute | solution.py:67
  40.6 0.0 collective-permute-start.9
  40.6 1.9 %backward_2.1.before = f32[48,2048]{1,0:T(8,128)S(1)} custom-call(bf16[112,768]{1,0:T(8,128)(2,1)S(1)} %collective-permute-done.7.message.refs_2_, bf16[2048,768]{1,0:T(8,128)(2,1)S(1)} %get-tuple-element.38.refs_8_.refs_5_.refs_10_.gate, bf16[2048,768]{1,0:T(8,128)(2,1)S(1)} %get-tuple-element.43.refs_6_.refs_11_.up, f32[48,2048]{1,0:T(8,128)S(1)} %backward_1.1.before), custom_call_target="tpu_custom_call" | custom-call | flops 1000 | bytes 1000 | tf_op jit(solution)/shard_map/backward_2/pallas_call | solution.py:80
  42.6 0.0 collective-permute-done.9.message
  42.6 2.0 %backward_3.1 = (f32[24,2048]{1,0:T(8,128)S(1)}, f32[8,1024]{1,0:T(8,128)S(1)}, bf16[7,8,1024]{2,1,0:T(8,128)(2,1)S(1)}) custom-call(bf16[112,768]{1,0:T(8,128)(2,1)S(1)} %collective-permute-done.9.message, bf16[2048,768]{1,0:T(8,128)(2,1)S(1)} %get-tuple-element.35.refs_5_.refs_12_.gate, bf16[2048,768]{1,0:T(8,128)(2,1)S(1)} %get-tuple-element.36.refs_6_.refs_13_.up, ...), custom_call_target="tpu_custom_call" | custom-call | flops 1000 | bytes 1000 | tf_op jit(solution)/shard_map/backward_3/pallas_call | solution.py:80
  44.6 1.4 %collective-permute-start.10 = (bf16[7,8,1024]{2,1,0:T(8,128)(2,1)S(1)}, bf16[7,8,1024]{2,1,0:T(8,128)(2,1)S(1)}, u32[]{:S(2)}, u32[]{:S(2)}) collective-permute-start(bf16[7,8,1024]{2,1,0:T(8,128)(2,1)S(1)} %get-tuple-element.58), channel_id=1, source_target_pairs={{0,16},{16,0},{1,17},{17,1},{2,18},{18,2},{3,19},{19,3},{4,20},{20... | collective-permute-start | bytes 344072 | tf_op jit(solution)/shard_map/ppermute | solution.py:67
  46.0 4.2 %collective-permute-done.10.arrived = bf16[7,8,1024]{2,1,0:T(8,128)(2,1)S(1)} collective-permute-done((bf16[7,8,1024]{2,1,0:T(8,128)(2,1)S(1)}, bf16[7,8,1024]{2,1,0:T(8,128)(2,1)S(1)}, u32[]{:S(2)}, u32[]{:S(2)}) %collective-permute-start.10) | collective-permute-done | bytes 114720 | tf_op jit(solution)/shard_map/ppermute | solution.py:67
  50.2 0.7 %combine.1 = (f32[4,1536]{1,0:T(4,128)}, f32[8,2048]{1,0:T(8,128)S(1)}, bf16[8,2048]{1,0:T(8,128)(2,1)S(1)}, bf16[8,2048]{1,0:T(8,128)(2,1)S(1)}, bf16[8,2048]{1,0:T(8,128)(2,1)S(1)}) custom-call(f32[24,2048]{1,0:T(8,128)S(1)} %get-tuple-element.56.own, f32[8,1024]{1,0:T(8,128)S(1)} %get-tuple-element.57.own_tail, ...), custom_call_target="tpu_custom_call" | custom-call | flops 1000 | bytes 1000 | tf_op jit(solution)/shard_map/combine/pallas_call | solution.py:80
  50.9 3.3 %collective-permute-start.11 = (bf16[8,2048]{1,0:T(8,128)(2,1)S(1)}, bf16[8,2048]{1,0:T(8,128)(2,1)S(1)}, u32[]{:S(2)}, u32[]{:S(2)}) collective-permute-start(bf16[8,2048]{1,0:T(8,128)(2,1)S(1)} %get-tuple-element.62), channel_id=1, source_target_pairs={{0,12},{4,8},{8,4},{12,0},{1,13},{5,9},{9,5},{13,1},{2,14},{6,10},... | collective-permute-start | bytes 98312 | tf_op jit(solution)/shard_map/ppermute | solution.py:67
  54.1 0.0 collective-permute-start.12
  54.1 1.1 %collective-permute-start.13 = (bf16[8,2048]{1,0:T(8,128)(2,1)S(1)}, bf16[8,2048]{1,0:T(8,128)(2,1)S(1)}, u32[]{:S(2)}, u32[]{:S(2)}) collective-permute-start(bf16[8,2048]{1,0:T(8,128)(2,1)S(1)} %get-tuple-element.64), channel_id=1, source_target_pairs={{0,4},{4,0},{8,12},{12,8},{1,5},{5,1},{9,13},{13,9},{2,6},{6,2},{1... | collective-permute-start | bytes 98312 | tf_op jit(solution)/shard_map/ppermute | solution.py:67
  55.2 1.4 %collective-permute-done.11.refs_1_ = bf16[8,2048]{1,0:T(8,128)(2,1)S(1)} collective-permute-done((bf16[8,2048]{1,0:T(8,128)(2,1)S(1)}, bf16[8,2048]{1,0:T(8,128)(2,1)S(1)}, u32[]{:S(2)}, u32[]{:S(2)}) %collective-permute-start.11) | collective-permute-done | bytes 32800 | tf_op jit(solution)/shard_map/ppermute | solution.py:67
  56.7 2.3 %collective-permute-done.12.refs_2_ = bf16[8,2048]{1,0:T(8,128)(2,1)S(1)} collective-permute-done((bf16[8,2048]{1,0:T(8,128)(2,1)S(1)}, bf16[8,2048]{1,0:T(8,128)(2,1)S(1)}, u32[]{:S(2)}, u32[]{:S(2)}) %collective-permute-start.12) | collective-permute-done | bytes 32800 | tf_op jit(solution)/shard_map/ppermute | solution.py:67
  58.9 0.0 collective-permute-done.13.refs_3_
  58.9 0.7 %last.1 = (bf16[6,2048]{1,0:T(8,128)(2,1)}, f32[4]{0:T(128)}) custom-call(f32[8,2048]{1,0:T(8,128)S(1)} %get-tuple-element.61.refs_0_, bf16[8,2048]{1,0:T(8,128)(2,1)S(1)} %collective-permute-done.11.refs_1_, bf16[8,2048]{1,0:T(8,128)(2,1)S(1)} %collective-permute-done.12.refs_2_, bf16[8,2048]{1,0:T(8,128)(2,1)S(1)} %collective-permute-done.13.refs_3_), custom_call_target="tpu_custom_call" | custom-call | flops 1000 | bytes 1000 | tf_op jit(solution)/shard_map/last/pallas_call | solution.py:80
Async XLA Ops:
  1.4 10.1 %copy-start.1 = (s32[24]{0:T(128)S(1)}, s32[24]{0:T(128)}, u32[]{:S(2)}) copy-start(s32[24]{0:T(128)} %refs_4_.1) | copy-start | bytes 292
  1.4 9.6 %collective-permute-start.2 = (bf16[3,8,1024]{2,1,0:T(8,128)(2,1)S(1)}, bf16[3,8,1024]{2,1,0:T(8,128)(2,1)S(1)}, u32[]{:S(2)}, u32[]{:S(2)}) collective-permute-start(bf16[3,8,1024]{2,1,0:T(8,128)(2,1)S(1)} %pack.1.refs_0_), channel_id=1, source_target_pairs={{0,12},{4,8},{8,4},{12,0},{1,13},{5,9},{9,5},{13,1},{2,14},{6,10},... | collective-permute-start | bytes 147464 | tf_op jit(solution)/shard_map/ppermute | solution.py:67
  6.6 5.0 %collective-permute-start.1 = (bf16[3,8,1024]{2,1,0:T(8,128)(2,1)S(1)}, bf16[3,8,1024]{2,1,0:T(8,128)(2,1)S(1)}, u32[]{:S(2)}, u32[]{:S(2)}) collective-permute-start(bf16[3,8,1024]{2,1,0:T(8,128)(2,1)S(1)} %pack.1.refs_0_), channel_id=1, source_target_pairs={{0,8},{4,12},{8,0},{12,4},{1,9},{5,13},{9,1},{13,5},{2,10},{6,14},... | collective-permute-start | bytes 147464 | tf_op jit(solution)/shard_map/ppermute | solution.py:67
  6.6 5.0 %collective-permute-start = (bf16[3,8,1024]{2,1,0:T(8,128)(2,1)S(1)}, bf16[3,8,1024]{2,1,0:T(8,128)(2,1)S(1)}, u32[]{:S(2)}, u32[]{:S(2)}) collective-permute-start(bf16[3,8,1024]{2,1,0:T(8,128)(2,1)S(1)} %pack.1.refs_0_), channel_id=1, source_target_pairs={{0,4},{4,0},{8,12},{12,8},{1,5},{5,1},{9,13},{13,9},{2,6},{6,2},{1... | collective-permute-start | bytes 147464 | tf_op jit(solution)/shard_map/ppermute | solution.py:67
  12.1 6.4 %collective-permute-start.3 = (bf16[13,8,1024]{2,1,0:T(8,128)(2,1)S(1)}, bf16[13,8,1024]{2,1,0:T(8,128)(2,1)S(1)}, u32[]{:S(2)}, u32[]{:S(2)}) collective-permute-start(bf16[13,8,1024]{2,1,0:T(8,128)(2,1)S(1)} %relay.1.refs_3_.refs_4_), channel_id=1, source_target_pairs={{0,16},{16,0},{1,17},{17,1},{2,18},{18,2},{3,19},{19,3},{4,20},{20... | collective-permute-start | bytes 638984 | tf_op jit(solution)/shard_map/ppermute | solution.py:67
  21.1 1.9 %collective-permute-start.4 = (f32[3,48,768]{2,1,0:T(8,128)S(1)}, f32[3,48,768]{2,1,0:T(8,128)S(1)}, u32[]{:S(2)}, u32[]{:S(2)}) collective-permute-start(f32[3,48,768]{2,1,0:T(8,128)S(1)} %get-tuple-element.45), channel_id=1, source_target_pairs={{0,1},{1,0},{2,3},{3,2},{4,5},{5,4},{6,7},{7,6},{8,9},{9,8},{10,11... | collective-permute-start | bytes 1327112 | tf_op jit(solution)/shard_map/ppermute | solution.py:67
  25.4 8.0 %collective-permute-start.6 = (bf16[3,48,768]{2,1,0:T(8,128)(2,1)S(1)}, bf16[3,48,768]{2,1,0:T(8,128)(2,1)S(1)}, u32[]{:S(2)}, u32[]{:S(2)}) collective-permute-start(bf16[3,48,768]{2,1,0:T(8,128)(2,1)S(1)} %get-tuple-element.47.refs_8_), channel_id=1, source_target_pairs={{0,2},{1,3},{2,0},{3,1},{4,6},{5,7},{6,4},{7,5},{8,10},{9,11},{10,... | collective-permute-start | bytes 663560 | tf_op jit(solution)/shard_map/ppermute | solution.py:67
  29.8 3.7 %collective-permute-start.5 = (bf16[3,48,768]{2,1,0:T(8,128)(2,1)S(1)}, bf16[3,48,768]{2,1,0:T(8,128)(2,1)S(1)}, u32[]{:S(2)}, u32[]{:S(2)}) collective-permute-start(bf16[3,48,768]{2,1,0:T(8,128)(2,1)S(1)} %get-tuple-element.51), channel_id=1, source_target_pairs={{0,1},{1,0},{2,3},{3,2},{4,5},{5,4},{6,7},{7,6},{8,9},{9,8},{10,11... | collective-permute-start | bytes 663560 | tf_op jit(solution)/shard_map/ppermute | solution.py:67
  29.8 3.6 %copy-start = (f32[6144]{0:T(1024)S(1)}, f32[6144]{0:T(1024)}, u32[]{:S(2)}) copy-start(f32[6144]{0:T(1024)} %param.12) | copy-start | bytes 73732
  33.8 3.0 %collective-permute-start.8 = (bf16[112,768]{1,0:T(8,128)(2,1)S(1)}, bf16[112,768]{1,0:T(8,128)(2,1)S(1)}, u32[]{:S(2)}, u32[]{:S(2)}) collective-permute-start(bf16[112,768]{1,0:T(8,128)(2,1)S(1)} %get-tuple-element.52.message.refs_0_), channel_id=1, source_target_pairs={{0,1},{1,0},{2,3},{3,2},{4,5},{5,4},{6,7},{7,6},{8,9},{9,8},{10,11... | collective-permute-start | bytes 516104 | tf_op jit(solution)/shard_map/ppermute | solution.py:67
  34.3 6.3 %collective-permute-start.7 = (bf16[112,768]{1,0:T(8,128)(2,1)S(1)}, bf16[112,768]{1,0:T(8,128)(2,1)S(1)}, u32[]{:S(2)}, u32[]{:S(2)}) collective-permute-start(bf16[112,768]{1,0:T(8,128)(2,1)S(1)} %get-tuple-element.52.message.refs_0_), channel_id=1, source_target_pairs={{0,2},{1,3},{2,0},{3,1},{4,6},{5,7},{6,4},{7,5},{8,10},{9,11},{10,... | collective-permute-start | bytes 516104 | tf_op jit(solution)/shard_map/ppermute | solution.py:67
  40.6 1.9 %collective-permute-start.9 = (bf16[112,768]{1,0:T(8,128)(2,1)S(1)}, bf16[112,768]{1,0:T(8,128)(2,1)S(1)}, u32[]{:S(2)}, u32[]{:S(2)}) collective-permute-start(bf16[112,768]{1,0:T(8,128)(2,1)S(1)} %collective-permute-done.7.message.refs_2_), channel_id=1, source_target_pairs={{0,1},{1,0},{2,3},{3,2},{4,5},{5,4},{6,7},{7,6},{8,9},{9,8},{10,11... | collective-permute-start | bytes 516104 | tf_op jit(solution)/shard_map/ppermute | solution.py:67
  44.6 5.6 %collective-permute-start.10 = (bf16[7,8,1024]{2,1,0:T(8,128)(2,1)S(1)}, bf16[7,8,1024]{2,1,0:T(8,128)(2,1)S(1)}, u32[]{:S(2)}, u32[]{:S(2)}) collective-permute-start(bf16[7,8,1024]{2,1,0:T(8,128)(2,1)S(1)} %get-tuple-element.58), channel_id=1, source_target_pairs={{0,16},{16,0},{1,17},{17,1},{2,18},{18,2},{3,19},{19,3},{4,20},{20... | collective-permute-start | bytes 344072 | tf_op jit(solution)/shard_map/ppermute | solution.py:67
  50.9 5.8 %collective-permute-start.11 = (bf16[8,2048]{1,0:T(8,128)(2,1)S(1)}, bf16[8,2048]{1,0:T(8,128)(2,1)S(1)}, u32[]{:S(2)}, u32[]{:S(2)}) collective-permute-start(bf16[8,2048]{1,0:T(8,128)(2,1)S(1)} %get-tuple-element.62), channel_id=1, source_target_pairs={{0,12},{4,8},{8,4},{12,0},{1,13},{5,9},{9,5},{13,1},{2,14},{6,10},... | collective-permute-start | bytes 98312 | tf_op jit(solution)/shard_map/ppermute | solution.py:67
  54.1 4.8 %collective-permute-start.12 = (bf16[8,2048]{1,0:T(8,128)(2,1)S(1)}, bf16[8,2048]{1,0:T(8,128)(2,1)S(1)}, u32[]{:S(2)}, u32[]{:S(2)}) collective-permute-start(bf16[8,2048]{1,0:T(8,128)(2,1)S(1)} %get-tuple-element.63), channel_id=1, source_target_pairs={{0,8},{4,12},{8,0},{12,4},{1,9},{5,13},{9,1},{13,5},{2,10},{6,14},... | collective-permute-start | bytes 98312 | tf_op jit(solution)/shard_map/ppermute | solution.py:67
  54.1 4.8 %collective-permute-start.13 = (bf16[8,2048]{1,0:T(8,128)(2,1)S(1)}, bf16[8,2048]{1,0:T(8,128)(2,1)S(1)}, u32[]{:S(2)}, u32[]{:S(2)}) collective-permute-start(bf16[8,2048]{1,0:T(8,128)(2,1)S(1)} %get-tuple-element.64), channel_id=1, source_target_pairs={{0,4},{4,0},{8,12},{12,8},{1,5},{5,1},{9,13},{13,9},{2,6},{6,2},{1... | collective-permute-start | bytes 98312 | tf_op jit(solution)/shard_map/ppermute | solution.py:67

commit v6 on v0

--- a/solution.py
+++ b/solution.py
@@ -1,9 +1,14 @@
+from types import SimpleNamespace
+
 import jax
 import jax.numpy as jnp
 from jax import lax
+from jax.experimental import pallas as pl
+from jax.experimental.pallas import tpu as pltpu
 from jax.sharding import PartitionSpec as P
 
 SEQS = 4
+KERNEL_VMEM = 6 << 20
 
 
 def contract_rows(left, right):
@@ -16,7 +21,7 @@
     sigmoid_gate = jax.nn.sigmoid(gate_pre)
     activation = gate_pre * sigmoid_gate
     hidden = activation * up_pre
-    scaled = scale_part[None, :] * mid_grad
+    scaled = scale_part * mid_grad
     d_up = (scaled * activation).astype(jnp.bfloat16)
     d_gate = (scaled * up_pre * sigmoid_gate * (1.0 + gate_pre * (1.0 - sigmoid_gate))).astype(
         jnp.bfloat16
@@ -24,7 +29,7 @@
     return (hidden * mid_grad, d_gate, d_up)
 
 
-def local(inputs, cotangent, gate_weight, up_weight, down_weight, ia3_scale, seq_ids):
+def whole_block(inputs, cotangent, gate_weight, up_weight, down_weight, ia3_scale, seq_ids):
     panel_inputs = lax.all_gather(inputs, "wide", axis=0, tiled=True)
     panel_cotangent = lax.all_gather(cotangent, "wide", axis=0, tiled=True)
     gate_part = jnp.dot(panel_inputs, gate_weight, preferred_element_type=jnp.float32)
@@ -41,7 +46,7 @@
         lax.psum_scatter(mid_part, "narrow", scatter_dimension=1, tiled=True),
     )
     scale_part = lax.dynamic_slice_in_dim(ia3_scale, position * quarter, quarter, 0)
-    product, d_gate, d_up = local_grads(gate_pre, up_pre, mid_grad, scale_part)
+    product, d_gate, d_up = local_grads(gate_pre, up_pre, mid_grad, scale_part[None, :])
     example_grads = jnp.dot(onehot_full, product, precision=lax.Precision.HIGHEST)
     whole_gate, whole_up = (
         lax.all_gather(d_gate, "narrow", axis=1, tiled=True),
@@ -56,6 +61,527 @@
         tiled=True,
     ).astype(jnp.bfloat16)
     return (example_grads, grad_norms, input_grad)
+
+
+def exchange(array, axis, step):
+    return lax.ppermute(array, axis, [(i, i ^ step) for i in range(lax.axis_size(axis))])
+
+
+def held(array):
+    return pltpu.with_memory_space_constraint(array, pltpu.VMEM)
+
+
+def in_hbm(array):
+    return pltpu.with_memory_space_constraint(array, pltpu.HBM)
+
+
+def call(body, name, outs, ins, scratch=None, in_spaces=None, out_spaces=None):
+    scratch, in_spaces, out_spaces = scratch or {}, in_spaces or {}, out_spaces or {}
+    names = list(ins) + list(outs) + list(scratch)
+
+    def kernel(*refs):
+        body(SimpleNamespace(**dict(zip(names, refs))))
+
+    arrays = pl.pallas_call(
+        kernel,
+        out_shape=list(outs.values()),
+        in_specs=[pl.BlockSpec(memory_space=in_spaces.get(key, pltpu.VMEM)) for key in ins],
+        out_specs=[pl.BlockSpec(memory_space=out_spaces.get(key, pltpu.VMEM)) for key in outs],
+        scratch_shapes=list(scratch.values()),
+        compiler_params=pltpu.CompilerParams(vmem_limit_bytes=KERNEL_VMEM),
+        cost_estimate=pl.CostEstimate(flops=1000, bytes_accessed=1000, transcendentals=0),
+        name=name,
+    )(*ins.values())
+    return dict(zip(outs, arrays))
+
+
+GATE, UP, DOWN = "gate", "up", "down"
+KINDS = (GATE, UP, DOWN)
+CHUNKS = 4
+TILE = 512
+
+
+def piece(kind, strip):
+    return f"{kind}_{strip}"
+
+
+def start_loads(r, pieces, groups):
+    waits = {}
+    for i, (kind, strip) in enumerate(pieces):
+        target, source = getattr(r, piece(kind, strip)), getattr(r, kind)
+        rows, columns = target.shape
+        owner = (lax.axis_index("narrow") ^ strip) * groups + lax.axis_index("groups")
+        copies = []
+        for c in range(CHUNKS):
+            size = rows // CHUNKS
+            if kind == DOWN:
+                part = source.at[pl.ds(pl.multiple_of(owner * rows + c * size, size), size), :]
+            else:
+                part = source.at[c * size : (c + 1) * size, pl.ds(pl.multiple_of(owner * columns, columns), columns)]
+            copies.append(pltpu.make_async_copy(part, target.at[c * size : (c + 1) * size, :], r.sem.at[i, c]))
+        waits[kind, strip] = copies
+    for copies in waits.values():
+        for copy in copies:
+            copy.start()
+
+    def wait(*which):
+        for key in which or list(waits):
+            for copy in waits.pop(key):
+                copy.wait()
+
+    return wait
+
+
+def product(r, kind, strip, span):
+    weight = getattr(r, piece(kind, strip))
+    if kind == DOWN:
+        return contract_rows(r.cotans[...], weight[span, :])
+    return jnp.dot(r.tokens[...], weight[:, span], preferred_element_type=jnp.float32)
+
+
+def by_tiles(width, body):
+    tile = 256
+
+    @pl.loop(0, width // tile)
+    def _(i):
+        body(pl.ds(pl.multiple_of(i * tile, tile), tile))
+
+
+def split_high(values):
+    high = values.astype(jnp.bfloat16).astype(jnp.float32)
+    return high, values - high
+
+
+def shared(inputs, cotangent, gate_weight, up_weight, down_weight, ia3_scale, seq_ids):
+    groups, wide, strips = lax.axis_size("groups"), lax.axis_size("wide"), lax.axis_size("narrow")
+    share, features = inputs.shape
+    width = gate_weight.shape[1] // (strips * groups)
+    half = share * wide
+    tokens = half * groups
+    f32, bf16 = jnp.float32, jnp.bfloat16
+    slabs, side = 4 * share // 8, features // 2
+    sources = {GATE: in_hbm(gate_weight), UP: in_hbm(up_weight), DOWN: in_hbm(down_weight)}
+    weight_shape = {
+        GATE: pltpu.VMEM((features, width), bf16),
+        UP: pltpu.VMEM((features, width), bf16),
+        DOWN: pltpu.VMEM((width, features), bf16),
+    }
+    kept = {}
+
+    def hold(*pieces):
+        return {piece(*key): held(kept[key]) for key in pieces}
+
+    def loading(body, name, pieces, outs, ins, scratch=None):
+        def whole(r):
+            wait = start_loads(r, pieces, groups)
+            body(r, wait)
+
+        made = call(
+            whole,
+            name,
+            {**{piece(*key): weight_shape[key[0]] for key in pieces}, **outs},
+            {**sources, **ins},
+            {**(scratch or {}), "sem": pltpu.SemaphoreType.DMA((len(pieces), CHUNKS))},
+            {kind: pltpu.HBM for kind in KINDS},
+        )
+        kept.update({key: made[piece(*key)] for key in pieces})
+        return made
+
+    def pack(r):
+        for i, ref in enumerate((r.inputs, r.cotangent)):
+            rows = ref[...].astype(f32)
+            for j in range(2):
+                at = (2 * i + j) * share
+                r.stage[at : at + share, :] = rows[:, j * side : (j + 1) * side]
+        for k in range(slabs):
+            slab = r.stage[8 * k : 8 * k + 8, :].astype(bf16)
+            r.packed[k] = slab
+            r.marked[k] = slab
+        row = lax.broadcasted_iota(jnp.int32, (8, 128), 0)
+        position = lax.axis_index("wide")
+        keys = []
+        for k in range(half // 8):
+            key = jnp.zeros((8, 128), jnp.int32)
+            for i in range(8):
+                block, j = divmod(8 * k + i, share)
+                key = jnp.where(row == i, r.ids[(position ^ block) * share + j], key)
+            keys.append(key.astype(f32))
+        keys.append(jnp.zeros((8, side - 128 * len(keys)), f32))
+        r.marked[slabs] = jnp.concatenate(keys, axis=1).astype(bf16)
+
+    made = call(
+        pack,
+        "pack",
+        {"packed": pltpu.VMEM((slabs, 8, side), bf16), "marked": pltpu.VMEM((slabs + 1, 8, side), bf16)},
+        {"inputs": in_hbm(inputs), "cotangent": in_hbm(cotangent), "ids": in_hbm(seq_ids)},
+        {"stage": pltpu.VMEM((4 * share, side), f32)},
+        {"ids": pltpu.SMEM},
+    )
+    marked = made["marked"]
+    blocks = [marked] + [exchange(made["packed"], "wide", s) for s in range(1, wide)]
+    others = [exchange(marked, "groups", 1)]
+
+    def only_wait(r, wait):
+        wait()
+
+    def load_a(r, wait):
+        r.mark[...] = jnp.zeros_like(r.mark)
+        wait()
+
+    mark = loading(load_a, "load_a", [(kind, 3) for kind in KINDS], {"mark": pltpu.VMEM((8, 128), f32)}, {})["mark"]
+    for s in reversed(range(1, wide)):
+        blocks[s], mark = lax.optimization_barrier((blocks[s], mark))
+        others.insert(1, exchange(blocks[s], "groups", 1))
+    loading(only_wait, "load_b", [(DOWN, 2), (GATE, 2)], {}, {"after": mark})
+
+    def forward_3_rest(r, wait):
+        for i in range(groups * wide):
+            packed = getattr(r, f"block_{i}")[0:slabs].astype(f32).reshape(4 * share, side)
+            for j, target in enumerate((r.rows, r.rows, r.cots, r.cots)):
+                span = slice((j % 2) * side, (j % 2 + 1) * side)
+                target[i * share : (i + 1) * share, span] = packed[j * share : (j + 1) * share]
+        r.tokens[...] = r.rows[...].astype(bf16)
+        r.cotans[...] = r.cots[...].astype(bf16)
+
+        def step(span):
+            for i, kind in enumerate((GATE, UP)):
+                r.part[i, :, span] = product(r, kind, 3, span)
+
+        by_tiles(width, step)
+        wait()
+
+    panel_shape = pltpu.VMEM((tokens, features), bf16)
+    made = loading(
+        forward_3_rest,
+        "forward_3_rest",
+        [(UP, 2)],
+        {"tokens": panel_shape, "cotans": panel_shape, "part": pltpu.VMEM((2, tokens, width), f32)},
+        {
+            **{f"block_{i}": block for i, block in enumerate(blocks + others)},
+            **hold((GATE, 3), (UP, 3), (DOWN, 2)),
+        },
+        {"rows": pltpu.VMEM((tokens, features), f32), "cots": pltpu.VMEM((tokens, features), f32)},
+    )
+    tokens_in, cotans_in = {"tokens": made["tokens"]}, {"cotans": made["cotans"]}
+    far_rest = exchange(made["part"], "narrow", 1)
+
+    def forward_3_down(r, wait):
+        def step(span):
+            r.part[:, span] = product(r, DOWN, 3, span)
+
+        by_tiles(width, step)
+        wait()
+
+    made = loading(
+        forward_3_down,
+        "forward_3_down",
+        [(DOWN, 1)],
+        {"part": pltpu.VMEM((tokens, width), f32)},
+        {**cotans_in, **hold((DOWN, 3)), "after": held(made["part"])},
+    )
+    far_down = exchange(made["part"], "narrow", 1)
+
+    def forward_2_rest(r, wait):
+        def step(span):
+            for i, kind in enumerate((GATE, UP)):
+                r.part[i, :, span] = (product(r, kind, 2, span) + r.arrived[i, :, span]).astype(bf16)
+
+        by_tiles(width, step)
+        wait()
+
+    made = loading(
+        forward_2_rest,
+        "forward_2_rest",
+        [(GATE, 1)],
+        {"part": pltpu.VMEM((2, tokens, width), bf16)},
+        {**tokens_in, **hold((GATE, 2), (UP, 2)), "arrived": far_rest, "after": held(made["part"])},
+    )
+
+    def forward_2_down(r):
+        r.part[0:2] = r.rest[...]
+
+        def step(span):
+            r.part[2, :, span] = (product(r, DOWN, 2, span) + r.arrived[:, span]).astype(bf16)
+
+        by_tiles(width, step)
+
+    made = call(
+        forward_2_down,
+        "forward_2_down",
+        {"part": pltpu.VMEM((3, tokens, width), bf16)},
+        {**cotans_in, **hold((DOWN, 2)), "arrived": far_down, "rest": held(made["part"])},
+    )
+    crossed = exchange(made["part"], "narrow", 2)
+
+    def forward_1(r, wait):
+        def step(span):
+            r.part[0, :, span] = product(r, GATE, 1, span).astype(bf16)
+            r.part[2, :, span] = product(r, DOWN, 1, span).astype(bf16)
+
+        by_tiles(width, step)
+        wait((UP, 1))
+        r.part[1] = product(r, UP, 1, slice(None)).astype(bf16)
+        wait()
+
+    made = loading(
+        forward_1,
+        "forward_1",
+        [(UP, 1), (GATE, 0)],
+        {"part": pltpu.VMEM((3, tokens, width), bf16)},
+        {**tokens_in, **cotans_in, **hold((GATE, 1), (DOWN, 1)), "after": held(made["part"])},
+    )
+    near = exchange(made["part"], "narrow", 1)
+
+    def forward_0(r, wait):
+        def step(span):
+            r.part[0, :, span] = product(r, GATE, 0, span)
+
+        by_tiles(width, step)
+        wait((UP, 0))
+        r.part[1] = product(r, UP, 0, slice(None))
+        wait((DOWN, 0))
+        r.part[2] = product(r, DOWN, 0, slice(None))
+
+    made = loading(
+        forward_0,
+        "forward_0",
+        [(UP, 0), (DOWN, 0)],
+        {"part": pltpu.VMEM((3, tokens, width), f32)},
+        {**tokens_in, **cotans_in, **hold((GATE, 0))},
+    )
+    own_part = made["part"]
+
+    def middle(r):
+        narrow, group = lax.axis_index("narrow"), lax.axis_index("groups")
+        sums = [r.own[i] + r.near[i].astype(f32) + r.crossed[i].astype(f32) for i in range(3)]
+        start = pl.multiple_of((narrow * groups + group) * width, width)
+        contribution, d_gate, d_up = local_grads(*sums, r.scale[:, pl.ds(start, width)])
+        r.message[0:tokens, :] = d_gate
+        r.message[tokens : 2 * tokens, :] = d_up
+        r.message_gate[0:tokens, :] = d_gate
+        r.message_up[...] = d_up
+        for i, (source, target) in enumerate(((r.marked, r.grads), (r.other_marked, r.other_grads))):
+            marks = source[slabs].astype(f32)
+            seq = jnp.concatenate(
+                [
+                    jnp.concatenate([marks[:, k * 128 : (k + 1) * 128]] * (width // 128), axis=1)
+                    for k in range(half // 8)
+                ],
+                axis=0,
+            )
+            part = contribution[i * half : (i + 1) * half]
+            for e in range(SEQS):
+                total = jnp.sum(jnp.where(seq == float(e), part, 0.0), axis=0, keepdims=True)
+                target[e : e + 1, :] = total
+                r.stage[i * SEQS + e : i * SEQS + e + 1, :] = total
+        every = r.stage[...]
+        squares = jnp.broadcast_to(jnp.sum(every * every, axis=1, keepdims=True), every.shape)
+        tail = jnp.concatenate(split_high(squares), axis=0).astype(bf16)
+        r.message[2 * tokens :, :] = tail
+        r.message_gate[tokens:, :] = tail
+
+    resident = [(kind, s) for s in range(strips) for kind in (GATE, UP)]
+    made = call(
+        middle,
+        "middle",
+        {
+            "message": pltpu.VMEM((2 * tokens + 16, width), bf16),
+            "message_gate": pltpu.VMEM((tokens + 16, width), bf16),
+            "message_up": pltpu.VMEM((tokens, width), bf16),
+            "grads": pltpu.VMEM((SEQS, width), f32),
+            "other_grads": pltpu.VMEM((SEQS, width), f32),
+        },
+        {
+            "own": own_part,
+            "near": near,
+            "crossed": crossed,
+            "scale": ia3_scale[None, :],
+            "marked": marked,
+            "other_marked": others[0],
+            **hold(*resident),
+        },
+        {"stage": pltpu.VMEM((groups * SEQS, width), f32)},
+    )
+    message, grads, other_grads = made["message"], made["grads"], made["other_grads"]
+
+    def term(r, strip, kind, grads_in, start):
+        weight = getattr(r, piece(kind, strip))
+        return contract_rows(grads_in, weight[start : start + TILE, :])
+
+    total_shape = {"total": pltpu.VMEM((tokens, features), f32)}
+
+    def both_terms(strip, before):
+        def body(r):
+            for start in range(0, features, TILE):
+                span = slice(start, start + TILE)
+                value = term(r, strip, GATE, r.message[0:tokens, :], start)
+                value = value + term(r, strip, UP, r.message[tokens : 2 * tokens, :], start)
+                r.total[:, span] = r.before[:, span] + value if before else value
+
+        return body
+
+    def one_term(strip, kind):
+        def body(r):
+            for start in range(0, features, TILE):
+                span = slice(start, start + TILE)
+                r.total[:, span] = r.before[:, span] + term(r, strip, kind, r.message[0:tokens, :], start)
+
+        return body
+
+    across_gate = exchange(made["message_gate"], "narrow", 2)
+    across_up = exchange(made["message_up"], "narrow", 2)
+    beside = exchange(message, "narrow", 1)
+    sums = call(both_terms(0, False), "backward_0", total_shape, {"message": message, **hold(*resident[0:2])})
+    sums = call(
+        both_terms(1, True),
+        "backward_1",
+        total_shape,
+        {"message": beside, "before": sums["total"], **hold(*resident[2:4])},
+    )
+    across_gate, before = lax.optimization_barrier((across_gate, sums["total"]))
+    far_gate = exchange(across_gate, "narrow", 1)
+    sums = call(
+        one_term(2, GATE), "backward_2_gate", total_shape, {"message": across_gate, "before": before, **hold((GATE, 2))}
+    )
+    across_up, before = lax.optimization_barrier((across_up, sums["total"]))
+    far_up = exchange(across_up, "narrow", 1)
+    sums = call(
+        one_term(2, UP), "backward_2_up", total_shape, {"message": across_up, "before": before, **hold((UP, 2))}
+    )
+    sums = call(
+        one_term(3, GATE),
+        "backward_3_gate",
+        total_shape,
+        {"message": far_gate, "before": sums["total"], **hold((GATE, 3))},
+    )
+
+    def backward_last(r):
+        for start in range(0, features, TILE):
+            span, at = slice(start, start + TILE), slice(start % side, start % side + TILE)
+            total = r.before[:, span] + term(r, 3, UP, r.message[...], start)
+            r.own[:, span] = total[:half]
+            for k in range(half // 8):
+                r.send[start // side * (half // 8) + k, :, at] = total[half + 8 * k : half + 8 * k + 8].astype(bf16)
+        tails = (r.message_0, r.message_1, r.message_2, r.message_3)
+        squares = sum(ref[ref.shape[0] - 16 :, 0:128].astype(f32) for ref in tails)
+        high, low = split_high(squares[0:8] + squares[8:16])
+        r.own_tail[...] = jnp.zeros_like(r.own_tail)
+        for i, rows in enumerate(split_high(r.other_grads[...])):
+            r.own_tail[i * SEQS : (i + 1) * SEQS, 0:width] = rows
+        r.own_tail[:, width : width + 128] = high
+        r.own_tail[:, width + 128 : width + 256] = low
+        r.send[r.send.shape[0] - 1] = r.own_tail[...].astype(bf16)
+
+    made = call(
+        backward_last,
+        "backward_3_up",
+        {
+            "own": pltpu.VMEM((half, features), f32),
+            "own_tail": pltpu.VMEM((8, side), f32),
+            "send": pltpu.VMEM((half // 4 + 1, 8, side), bf16),
+        },
+        {
+            "message": far_up,
+            "before": sums["total"],
+            "message_0": message,
+            "message_1": beside,
+            "message_2": across_gate,
+            "message_3": far_gate,
+            "other_grads": other_grads,
+            **hold((UP, 3)),
+        },
+    )
+
+    def combine(r):
+        group = lax.axis_index("groups")
+        count = half // 8
+        for k in range(count):
+            for i in range(features // side):
+                span = slice(i * side, (i + 1) * side)
+                part = r.own[8 * k : 8 * k + 8, span] + r.arrived[i * count + k].astype(f32)
+                r.total[8 * k : 8 * k + 8, span] = part
+        tail = r.arrived[r.arrived.shape[0] - 1].astype(f32)
+        other = tail[0:SEQS, 0:width] + tail[SEQS : 2 * SEQS, 0:width]
+        r.example_grads[:, pl.ds(pl.multiple_of(group * width, width), width)] = r.grads[...]
+        r.example_grads[:, pl.ds(pl.multiple_of((1 - group) * width, width), width)] = other
+        lanes = SEQS * 128
+
+        def squares(values, first):
+            rows = values[:, width : width + 128] + values[:, width + 128 : width + 256]
+            return jnp.concatenate([rows[first + e : first + e + 1] for e in range(SEQS)], axis=1)
+
+        high, low = split_high(squares(r.own_tail[...], 0) + squares(tail, SEQS))
+        r.block_0[...] = jnp.zeros_like(r.block_0)
+        r.block_0[6:7, 0:lanes] = high
+        r.block_0[7:8, 0:lanes] = low
+        for i in range(1, wide):
+            r.block_0[0:share, :] = r.total[i * share : (i + 1) * share, :]
+            getattr(r, f"block_{i}")[...] = r.block_0[...].astype(bf16)
+        r.block_0[0:share, :] = r.total[0:share, :]
+
+    made = call(
+        combine,
+        "combine",
+        {
+            "example_grads": jax.ShapeDtypeStruct((SEQS, groups * width), f32),
+            "block_0": pltpu.VMEM((8, features), f32),
+            **{f"block_{i}": pltpu.VMEM((8, features), bf16) for i in range(1, wide)},
+        },
+        {
+            "own": made["own"],
+            "own_tail": made["own_tail"],
+            "arrived": exchange(made["send"], "groups", 1),
+            "grads": grads,
+        },
+        {"total": pltpu.VMEM((half, features), f32)},
+    )
+
+    def last(r):
+        total = r.block_0[...]
+        for i in range(1, wide):
+            total = total + getattr(r, f"block_{i}")[...].astype(f32)
+        r.input_grad[...] = total[0:share].astype(bf16)
+        roots = jnp.sqrt(total[6:7, 0 : SEQS * 128] + total[7:8, 0 : SEQS * 128])
+        for e in range(SEQS):
+            r.norms[e] = jnp.max(roots[:, e * 128 : (e + 1) * 128])
+
+    ends = call(
+        last,
+        "last",
+        {"input_grad": jax.ShapeDtypeStruct((share, features), bf16), "norms": jax.ShapeDtypeStruct((SEQS,), f32)},
+        {
+            "block_0": made["block_0"],
+            **{f"block_{i}": exchange(made[f"block_{i}"], "wide", i) for i in reversed(range(1, wide))},
+        },
+        out_spaces={"norms": pltpu.SMEM},
+    )
+    return (made["example_grads"], ends["norms"], ends["input_grad"])
+
+
+def power_of_two(number):
+    return number & (number - 1) == 0
+
+
+def local(inputs, cotangent, gate_weight, up_weight, down_weight, ia3_scale, seq_ids):
+    groups, wide, narrow = lax.axis_size("groups"), lax.axis_size("wide"), lax.axis_size("narrow")
+    share, (features, hidden) = inputs.shape[0], gate_weight.shape
+    width = hidden // (narrow * groups)
+    fits = (
+        groups == 2
+        and narrow == 4
+        and power_of_two(wide)
+        and hidden % (narrow * groups * 256) == 0
+        and features >= 2048
+        and width <= features // 2 - 256
+        and features % (2 * TILE) == 0
+        and share <= 6
+        and share % 2 == 0
+        and (share * wide) % 8 == 0
+        and share * wide <= 64
+        and 3 * features * hidden // groups * 2 <= 40 << 20
+    )
+    plan = shared if fits else whole_block
+    return plan(inputs, cotangent, gate_weight, up_weight, down_weight, ia3_scale, seq_ids)
 
 
 def solution(mesh):

time: 200 us -> 62.4 us (0.31)
  blocking collectives: 85.6 us -> 0 us
  matrix products: 58.1 us -> 0 us
  Pallas kernels: 0 us -> 31.6 us
  waiting for transfers between devices: 35.3 us -> 9.11 us
  starting transfers between devices: 2.1 us -> 20.5 us
  between operations: 14.5 us -> 0.92 us
  local copies, waits for them, and re-layouts: 2.78 us -> 0.01 us
    dot_general x6 -> x0, matrix products: 58.1 us -> none  [the longest x3 35.4 us: contract_rows(): lax.dot_general(left, right, (((1,), (1,)), ((), ())), preferred_element_...]
    all_gather x4 -> x0, blocking collectives: 41 us -> none  [the longest x1 15.3 us: local(): panel_cotangent = lax.all_gather(cotangent, 'wide', axis=0, tiled=True)]
    reduce_scatter x3 -> x0, waiting for transfers between devices: 35.2 us -> none  [the longest x1 24.6 us: local(): lax.psum_scatter(gate_part, 'narrow', scatter_dimension=1, tiled=True)]
    pallas_call x0 -> x18, Pallas kernels: none -> 31.6 us  [call(): pl.pallas_call(kernel, out_shape=list(outs.values()), in_specs=[pl.BlockS...]
    psum x1 -> x0, blocking collectives: 29.5 us -> none  [local(): lax.psum(jnp.sum(example_grads * example_grads, axis=1), ('wide', 'narrow'))]
    ppermute x0 -> x20, starting transfers between devices: none -> 20.5 us  [exchange(): lax.ppermute(array, axis, [(i, i ^ step) for i in range(lax.axis_size(axi...]
    unnamed x1 -> x0, blocking collectives: 15.1 us -> none
    ppermute x0 -> x20, waiting for transfers between devices: none -> 9.11 us  [exchange(): lax.ppermute(array, axis, [(i, i ^ step) for i in range(lax.axis_size(axi...]
  transfers between devices with their start and end apart: 4 -> 20, of which waited for: 2 -> 4; matrix products, arithmetic and copies ran while one was open for 12% -> 0% of each run, Pallas kernels for 0% -> 40%
where the time goes in v6:
time: 62.4 us; the launch traced here: 62.2 us
  Pallas kernels  31.6 us (51%)
  starting transfers between devices  20.5 us (33%)
  waiting for transfers between devices  9.11 us (15%)
  between operations  0.92 us (1%)
    pallas_call x18, Pallas kernels, call(): pl.pallas_call(kernel, out_shape=list(outs.values()), in_specs=[pl.BlockS...  31.6 us
    ppermute x20, starting transfers between devices, exchange(): lax.ppermute(array, axis, [(i, i ^ step) for i in range(lax.axis_size(axi...  20.5 us
    ppermute x20, waiting for transfers between devices, exchange(): lax.ppermute(array, axis, [(i, i ^ step) for i in range(lax.axis_size(axi...  9.11 us
  transfers between devices with their start and end apart: 20, of which 4 were waited for; matrix products, arithmetic and copies ran while one was open for 0% of the time, Pallas kernels for 40%

profile of v6, /device:TPU:0, one launch (start us, length us, event | category | flops | bytes accessed | tf_op | source)
XLA Modules:
  0.0 62.2 jit_solution(928678750990580081)
XLA Ops:
  0.6 0.8 %pack.1 = (bf16[3,8,1024]{2,1,0:T(8,128)(2,1)S(1)}, bf16[4,8,1024]{2,1,0:T(8,128)(2,1)S(1)}) custom-call(bf16[6,2048]{1,0:T(8,128)(2,1)} %refs_0_.8, bf16[6,2048]{1,0:T(8,128)(2,1)} %refs_1_.8, s32[24]{0:T(128)} %refs_2_.8), custom_call_target="tpu_custom_call" | custom-call | flops 1000 | bytes 1000 | tf_op jit(solution)/shard_map/pack/pallas_call | solution.py:85
  1.5 5.1 %collective-permute-start.2 = (bf16[3,8,1024]{2,1,0:T(8,128)(2,1)S(1)}, bf16[3,8,1024]{2,1,0:T(8,128)(2,1)S(1)}, u32[]{:S(2)}, u32[]{:S(2)}) collective-permute-start(bf16[3,8,1024]{2,1,0:T(8,128)(2,1)S(1)} %get-tuple-element.50), channel_id=1, source_target_pairs={{0,12},{4,8},{8,4},{12,0},{1,13},{5,9},{9,5},{13,1},{2,14},{6,10},... | collective-permute-start | bytes 147464 | tf_op jit(solution)/shard_map/ppermute | solution.py:67
  6.6 0.6 %collective-permute-start = (bf16[3,8,1024]{2,1,0:T(8,128)(2,1)S(1)}, bf16[3,8,1024]{2,1,0:T(8,128)(2,1)S(1)}, u32[]{:S(2)}, u32[]{:S(2)}) collective-permute-start(bf16[3,8,1024]{2,1,0:T(8,128)(2,1)S(1)} %get-tuple-element.50), channel_id=1, source_target_pairs={{0,4},{4,0},{8,12},{12,8},{1,5},{5,1},{9,13},{13,9},{2,6},{6,2},{1... | collective-permute-start | bytes 147464 | tf_op jit(solution)/shard_map/ppermute | solution.py:67
  7.2 1.7 %collective-permute-start.3 = (bf16[4,8,1024]{2,1,0:T(8,128)(2,1)S(1)}, bf16[4,8,1024]{2,1,0:T(8,128)(2,1)S(1)}, u32[]{:S(2)}, u32[]{:S(2)}) collective-permute-start(bf16[4,8,1024]{2,1,0:T(8,128)(2,1)S(1)} %get-tuple-element.49.refs_3_.refs_4_), channel_id=1, source_target_pairs={{0,16},{16,0},{1,17},{17,1},{2,18},{18,2},{3,19},{19,3},{4,20},{20... | collective-permute-start | bytes 196616 | tf_op jit(solution)/shard_map/ppermute | solution.py:67
  8.9 3.9 %load_a.1 = (bf16[2048,768]{1,0:T(8,128)(2,1)S(1)}, bf16[2048,768]{1,0:T(8,128)(2,1)S(1)}, bf16[768,2048]{1,0:T(8,128)(2,1)S(1)}, f32[8,128]{1,0:T(8,128)S(1)}) custom-call(bf16[2048,6144]{1,0:T(8,128)(2,1)} %refs_0_.15, bf16[2048,6144]{1,0:T(8,128)(2,1)} %refs_1_.15, bf16[6144,2048]{1,0:T(8,128)(2,1)} %refs_2_.15), custom_call_target="tpu_custom_call" | custom-call | flops 1000 | bytes 1000 | tf_op jit(solution)/shard_map/load_a/pallas_call | solution.py:85
  12.8 0.0 collective-permute-done.1.refs_5_
  12.8 0.0 collective-permute-done.refs_4_
  12.8 0.4 collective-permute-start.4
  13.2 1.7 %collective-permute-start.5 = (bf16[3,8,1024]{2,1,0:T(8,128)(2,1)S(1)}, bf16[3,8,1024]{2,1,0:T(8,128)(2,1)S(1)}, u32[]{:S(2)}, u32[]{:S(2)}) collective-permute-start(bf16[3,8,1024]{2,1,0:T(8,128)(2,1)S(1)} %collective-permute-done.1.refs_5_), channel_id=1, source_target_pairs={{0,16},{16,0},{1,17},{17,1},{2,18},{18,2},{3,19},{19,3},{4,20},{20... | collective-permute-start | bytes 147464 | tf_op jit(solution)/shard_map/ppermute | solution.py:67
  14.9 0.4 collective-permute-start.6
  15.3 2.9 %load_b.1 = (bf16[768,2048]{1,0:T(8,128)(2,1)S(1)}, bf16[2048,768]{1,0:T(8,128)(2,1)S(1)}) custom-call(bf16[2048,6144]{1,0:T(8,128)(2,1)} %refs_0_.15, bf16[2048,6144]{1,0:T(8,128)(2,1)} %refs_1_.15, bf16[6144,2048]{1,0:T(8,128)(2,1)} %refs_2_.15, f32[8,128]{1,0:T(8,128)S(1)} %get-tuple-element.59.refs_3_), custom_call_target="tpu_custom_call" | custom-call | flops 1000 | bytes 1000 | tf_op jit(solution)/shard_map/load_b/pallas_call | solution.py:85
  18.1 0.0 collective-permute-done.4.refs_8_
  18.2 0.0 collective-permute-done.5.refs_9_
  18.2 0.8 %collective-permute-done.6.refs_10_ = bf16[3,8,1024]{2,1,0:T(8,128)(2,1)S(1)} collective-permute-done((bf16[3,8,1024]{2,1,0:T(8,128)(2,1)S(1)}, bf16[3,8,1024]{2,1,0:T(8,128)(2,1)S(1)}, u32[]{:S(2)}, u32[]{:S(2)}) %collective-permute-start.6) | collective-permute-done | bytes 49184 | tf_op jit(solution)/shard_map/ppermute | solution.py:67
  19.0 1.9 %forward_3_rest.1 = (bf16[2048,768]{1,0:T(8,128)(2,1)S(1)}, bf16[48,2048]{1,0:T(8,128)(2,1)S(1)}, bf16[48,2048]{1,0:T(8,128)(2,1)S(1)}, f32[2,48,768]{2,1,0:T(8,128)S(1)}) custom-call(bf16[2048,6144]{1,0:T(8,128)(2,1)} %refs_0_.15, bf16[2048,6144]{1,0:T(8,128)(2,1)} %refs_1_.15, bf16[6144,2048]{1,0:T(8,128)(2,1)} %refs_2_.15, ...), custom_call_target="tpu_custom_call" | custom-call | flops 1000 | bytes 1000 | tf_op jit(solution)/shard_map/forward_3_rest/pallas_call | solution.py:85
  20.9 0.1 collective-permute-start.7
  21.0 1.9 %forward_3_down.1 = (bf16[768,2048]{1,0:T(8,128)(2,1)S(1)}, f32[48,768]{1,0:T(8,128)S(1)}) custom-call(bf16[2048,6144]{1,0:T(8,128)(2,1)} %refs_0_.15, bf16[2048,6144]{1,0:T(8,128)(2,1)} %refs_1_.15, bf16[6144,2048]{1,0:T(8,128)(2,1)} %refs_2_.15, bf16[48,2048]{1,0:T(8,128)(2,1)S(1)} %get-tuple-element.62.refs_3_.refs_0_.refs_4_, ...), custom_call_target="tpu_custom_call" | custom-call | flops 1000 | bytes 1000 | tf_op jit(solution)/shard_map/forward_3_down/pallas_call | solution.py:85
  22.9 0.5 collective-permute-start.8
  23.4 0.0 collective-permute-done.7.refs_6_
  23.4 1.9 %forward_2_rest.1 = (bf16[2048,768]{1,0:T(8,128)(2,1)S(1)}, bf16[2,48,768]{2,1,0:T(8,128)(2,1)S(1)}) custom-call(bf16[2048,6144]{1,0:T(8,128)(2,1)} %refs_0_.15, bf16[2048,6144]{1,0:T(8,128)(2,1)} %refs_1_.15, bf16[6144,2048]{1,0:T(8,128)(2,1)} %refs_2_.15, bf16[48,2048]{1,0:T(8,128)(2,1)S(1)} %get-tuple-element.61.refs_3_, ...), custom_call_target="tpu_custom_call" | custom-call | flops 1000 | bytes 1000 | tf_op jit(solution)/shard_map/forward_2_rest/pallas_call | solution.py:85
  25.3 0.0 collective-permute-done.8.refs_2_
  25.3 1.3 %forward_2_down.1.refs_7_ = bf16[3,48,768]{2,1,0:T(8,128)(2,1)S(1)} custom-call(bf16[48,2048]{1,0:T(8,128)(2,1)S(1)} %get-tuple-element.62.refs_3_.refs_0_.refs_4_, bf16[768,2048]{1,0:T(8,128)(2,1)S(1)} %get-tuple-element.60.refs_13_.refs_1_, f32[48,768]{1,0:T(8,128)S(1)} %collective-permute-done.8.refs_2_, bf16[2,48,768]{2,1,0:T(8,128)(2,1)S(1)} %get-tuple-element.70.refs_3_), custom_call_target="tpu_custom_call" | custom-call | flops 1000 | bytes 1000 | tf_op jit(solution)/shard_map/forward_2_down/pallas_call | solution.py:85
  26.7 1.5 %collective-permute-start.10 = (bf16[3,48,768]{2,1,0:T(8,128)(2,1)S(1)}, bf16[3,48,768]{2,1,0:T(8,128)(2,1)S(1)}, u32[]{:S(2)}, u32[]{:S(2)}) collective-permute-start(bf16[3,48,768]{2,1,0:T(8,128)(2,1)S(1)} %forward_2_down.1.refs_7_), channel_id=1, source_target_pairs={{0,2},{1,3},{2,0},{3,1},{4,6},{5,7},{6,4},{7,5},{8,10},{9,11},{10,... | collective-permute-start | bytes 663560 | tf_op jit(solution)/shard_map/ppermute | solution.py:67
  28.2 2.9 %forward_1.1 = (bf16[2048,768]{1,0:T(8,128)(2,1)S(1)}, bf16[2048,768]{1,0:T(8,128)(2,1)S(1)}, bf16[3,48,768]{2,1,0:T(8,128)(2,1)S(1)}) custom-call(bf16[2048,6144]{1,0:T(8,128)(2,1)} %refs_0_.15, bf16[2048,6144]{1,0:T(8,128)(2,1)} %refs_1_.15, bf16[6144,2048]{1,0:T(8,128)(2,1)} %refs_2_.15, bf16[48,2048]{1,0:T(8,128)(2,1)S(1)} %get-tuple-element.61.refs_3_, ...), custom_call_target="tpu_custom_call" | custom-call | flops 1000 | bytes 1000 | tf_op jit(solution)/shard_map/forward_1/pallas_call | solution.py:85
  31.1 0.1 collective-permute-start.9
  31.1 0.0 copy-start
  31.2 4.5 %forward_0.1 = (bf16[2048,768]{1,0:T(8,128)(2,1)S(1)}, bf16[768,2048]{1,0:T(8,128)(2,1)}, f32[3,48,768]{2,1,0:T(8,128)S(1)}) custom-call(bf16[2048,6144]{1,0:T(8,128)(2,1)} %refs_0_.15, bf16[2048,6144]{1,0:T(8,128)(2,1)} %refs_1_.15, bf16[6144,2048]{1,0:T(8,128)(2,1)} %refs_2_.15, bf16[48,2048]{1,0:T(8,128)(2,1)S(1)} %get-tuple-element.61.refs_3_, ...), custom_call_target="tpu_custom_call" | custom-call | flops 1000 | bytes 1000 | tf_op jit(solution)/shard_map/forward_0/pallas_call | solution.py:85
  35.7 0.4 middle.1
  36.1 0.5 collective-permute-start.13
  36.6 0.6 collective-permute-start.12
  37.1 1.5 %collective-permute-start.11 = (bf16[48,768]{1,0:T(8,128)(2,1)S(1)}, bf16[48,768]{1,0:T(8,128)(2,1)S(1)}, u32[]{:S(2)}, u32[]{:S(2)}) collective-permute-start(bf16[48,768]{1,0:T(8,128)(2,1)S(1)} %get-tuple-element.76), channel_id=1, source_target_pairs={{0,2},{1,3},{2,0},{3,1},{4,6},{5,7},{6,4},{7,5},{8,10},{9,11},{10,... | collective-permute-start | bytes 221192 | tf_op jit(solution)/shard_map/ppermute | solution.py:67
  38.6 1.9 %backward_0.1.refs_1_ = f32[48,2048]{1,0:T(8,128)S(1)} custom-call(bf16[112,768]{1,0:T(8,128)(2,1)S(1)} %get-tuple-element.78.refs_0_.refs_2_, bf16[2048,768]{1,0:T(8,128)(2,1)S(1)} %get-tuple-element.71.refs_5_.refs_6_.refs_1_, bf16[2048,768]{1,0:T(8,128)(2,1)S(1)} %get-tuple-element.74.refs_7_.refs_2_), custom_call_target="tpu_custom_call" | custom-call | flops 1000 | bytes 1000 | tf_op jit(solution)/shard_map/backward_0/pallas_call | solution.py:85
  40.5 0.0 collective-permute-done.13.refs_0_.refs_3_
  40.5 1.9 %backward_1.1.refs_1_ = f32[48,2048]{1,0:T(8,128)S(1)} custom-call(bf16[112,768]{1,0:T(8,128)(2,1)S(1)} %collective-permute-done.13.refs_0_.refs_3_, f32[48,2048]{1,0:T(8,128)S(1)} %backward_0.1.refs_1_, bf16[2048,768]{1,0:T(8,128)(2,1)S(1)} %get-tuple-element.68.refs_5_.refs_8_.refs_2_, bf16[2048,768]{1,0:T(8,128)(2,1)S(1)} %get-tuple-element.75.refs_9_.refs_3_), custom_call_target="tpu_custom_call" | custom-call | flops 1000 | bytes 1000 | tf_op jit(solution)/shard_map/backward_1/pallas_call | solution.py:85
  42.5 0.1 collective-permute-start.15
  42.6 1.0 %backward_2_gate.1.refs_1_ = f32[48,2048]{1,0:T(8,128)S(1)} custom-call(bf16[64,768]{1,0:T(8,128)(2,1)S(1)} %collective-permute-done.12.refs_0_.refs_4_, f32[48,2048]{1,0:T(8,128)S(1)} %backward_1.1.refs_1_, bf16[2048,768]{1,0:T(8,128)(2,1)S(1)} %get-tuple-element.63.refs_4_.refs_10_.refs_2_), custom_call_target="tpu_custom_call" | custom-call | flops 1000 | bytes 1000 | tf_op jit(solution)/shard_map/backward_2_gate/pallas_call | solution.py:85
  43.6 0.6 collective-permute-start.14
  44.2 1.0 %backward_2_up.1.refs_1_ = f32[48,2048]{1,0:T(8,128)S(1)} custom-call(bf16[48,768]{1,0:T(8,128)(2,1)S(1)} %collective-permute-done.11.refs_0_, f32[48,2048]{1,0:T(8,128)S(1)} %backward_2_gate.1.refs_1_, bf16[2048,768]{1,0:T(8,128)(2,1)S(1)} %get-tuple-element.64.refs_5_.refs_11_.refs_2_), custom_call_target="tpu_custom_call" | custom-call | flops 1000 | bytes 1000 | tf_op jit(solution)/shard_map/backward_2_up/pallas_call | solution.py:85
  45.2 1.0 %backward_3_gate.1.refs_1_ = f32[48,2048]{1,0:T(8,128)S(1)} custom-call(bf16[64,768]{1,0:T(8,128)(2,1)S(1)} %collective-permute-done.15.refs_0_.refs_5_, f32[48,2048]{1,0:T(8,128)S(1)} %backward_2_up.1.refs_1_, bf16[2048,768]{1,0:T(8,128)(2,1)S(1)} %get-tuple-element.57.refs_11_.refs_12_.refs_2_), custom_call_target="tpu_custom_call" | custom-call | flops 1000 | bytes 1000 | tf_op jit(solution)/shard_map/backward_3_gate/pallas_call | solution.py:85
  46.3 1.0 %backward_3_up.1 = (f32[24,2048]{1,0:T(8,128)S(1)}, f32[8,1024]{1,0:T(8,128)S(1)}, bf16[7,8,1024]{2,1,0:T(8,128)(2,1)S(1)}) custom-call(bf16[48,768]{1,0:T(8,128)(2,1)S(1)} %collective-permute-done.14.refs_0_, f32[48,2048]{1,0:T(8,128)S(1)} %backward_3_gate.1.refs_1_, bf16[112,768]{1,0:T(8,128)(2,1)S(1)} %get-tuple-element.78.refs_0_.refs_2_, ...), custom_call_target="tpu_custom_call" | custom-call | flops 1000 | bytes 1000 | tf_op jit(solution)/shard_map/backward_3_up/pallas_call | solution.py:85
  47.3 0.9 %collective-permute-start.16 = (bf16[7,8,1024]{2,1,0:T(8,128)(2,1)S(1)}, bf16[7,8,1024]{2,1,0:T(8,128)(2,1)S(1)}, u32[]{:S(2)}, u32[]{:S(2)}) collective-permute-start(bf16[7,8,1024]{2,1,0:T(8,128)(2,1)S(1)} %get-tuple-element.86), channel_id=1, source_target_pairs={{0,16},{16,0},{1,17},{17,1},{2,18},{18,2},{3,19},{19,3},{4,20},{20... | collective-permute-start | bytes 344072 | tf_op jit(solution)/shard_map/ppermute | solution.py:67
  48.3 4.2 %collective-permute-done.16.refs_2_ = bf16[7,8,1024]{2,1,0:T(8,128)(2,1)S(1)} collective-permute-done((bf16[7,8,1024]{2,1,0:T(8,128)(2,1)S(1)}, bf16[7,8,1024]{2,1,0:T(8,128)(2,1)S(1)}, u32[]{:S(2)}, u32[]{:S(2)}) %collective-permute-start.16) | collective-permute-done | bytes 114720 | tf_op jit(solution)/shard_map/ppermute | solution.py:67
  52.5 0.6 %combine.1 = (f32[4,1536]{1,0:T(4,128)}, f32[8,2048]{1,0:T(8,128)S(1)}, bf16[8,2048]{1,0:T(8,128)(2,1)S(1)}, bf16[8,2048]{1,0:T(8,128)(2,1)S(1)}, bf16[8,2048]{1,0:T(8,128)(2,1)S(1)}) custom-call(f32[24,2048]{1,0:T(8,128)S(1)} %get-tuple-element.84.refs_0_, f32[8,1024]{1,0:T(8,128)S(1)} %get-tuple-element.85.refs_1_, ...), custom_call_target="tpu_custom_call" | custom-call | flops 1000 | bytes 1000 | tf_op jit(solution)/shard_map/combine/pallas_call | solution.py:85
  53.1 3.6 %collective-permute-start.17 = (bf16[8,2048]{1,0:T(8,128)(2,1)S(1)}, bf16[8,2048]{1,0:T(8,128)(2,1)S(1)}, u32[]{:S(2)}, u32[]{:S(2)}) collective-permute-start(bf16[8,2048]{1,0:T(8,128)(2,1)S(1)} %get-tuple-element.90), channel_id=1, source_target_pairs={{0,12},{4,8},{8,4},{12,0},{1,13},{5,9},{9,5},{13,1},{2,14},{6,10},... | collective-permute-start | bytes 98312 | tf_op jit(solution)/shard_map/ppermute | solution.py:67
  56.7 0.8 %collective-permute-start.19 = (bf16[8,2048]{1,0:T(8,128)(2,1)S(1)}, bf16[8,2048]{1,0:T(8,128)(2,1)S(1)}, u32[]{:S(2)}, u32[]{:S(2)}) collective-permute-start(bf16[8,2048]{1,0:T(8,128)(2,1)S(1)} %get-tuple-element.92), channel_id=1, source_target_pairs={{0,4},{4,0},{8,12},{12,8},{1,5},{5,1},{9,13},{13,9},{2,6},{6,2},{1... | collective-permute-start | bytes 98312 | tf_op jit(solution)/shard_map/ppermute | solution.py:67
  57.5 1.4 %collective-permute-done.17.refs_1_ = bf16[8,2048]{1,0:T(8,128)(2,1)S(1)} collective-permute-done((bf16[8,2048]{1,0:T(8,128)(2,1)S(1)}, bf16[8,2048]{1,0:T(8,128)(2,1)S(1)}, u32[]{:S(2)}, u32[]{:S(2)}) %collective-permute-start.17) | collective-permute-done | bytes 32800 | tf_op jit(solution)/shard_map/ppermute | solution.py:67
  58.9 2.6 %collective-permute-done.18.refs_2_ = bf16[8,2048]{1,0:T(8,128)(2,1)S(1)} collective-permute-done((bf16[8,2048]{1,0:T(8,128)(2,1)S(1)}, bf16[8,2048]{1,0:T(8,128)(2,1)S(1)}, u32[]{:S(2)}, u32[]{:S(2)}) %collective-permute-start.18) | collective-permute-done | bytes 32800 | tf_op jit(solution)/shard_map/ppermute | solution.py:67
  61.5 0.7 %last.1 = (bf16[6,2048]{1,0:T(8,128)(2,1)}, f32[4]{0:T(128)}) custom-call(f32[8,2048]{1,0:T(8,128)S(1)} %get-tuple-element.89.refs_0_, bf16[8,2048]{1,0:T(8,128)(2,1)S(1)} %collective-permute-done.17.refs_1_, bf16[8,2048]{1,0:T(8,128)(2,1)S(1)} %collective-permute-done.18.refs_2_, bf16[8,2048]{1,0:T(8,128)(2,1)S(1)} %collective-permute-done.19.refs_3_), custom_call_target="tpu_custom_call" | custom-call | flops 1000 | bytes 1000 | tf_op jit(solution)/shard_map/last/pallas_call | solution.py:85
  (12 shorter events, 0.0 us)
Async XLA Ops:
  1.5 11.3 %collective-permute-start.2 = (bf16[3,8,1024]{2,1,0:T(8,128)(2,1)S(1)}, bf16[3,8,1024]{2,1,0:T(8,128)(2,1)S(1)}, u32[]{:S(2)}, u32[]{:S(2)}) collective-permute-start(bf16[3,8,1024]{2,1,0:T(8,128)(2,1)S(1)} %get-tuple-element.50), channel_id=1, source_target_pairs={{0,12},{4,8},{8,4},{12,0},{1,13},{5,9},{9,5},{13,1},{2,14},{6,10},... | collective-permute-start | bytes 147464 | tf_op jit(solution)/shard_map/ppermute | solution.py:67
  6.6 6.2 %collective-permute-start.1 = (bf16[3,8,1024]{2,1,0:T(8,128)(2,1)S(1)}, bf16[3,8,1024]{2,1,0:T(8,128)(2,1)S(1)}, u32[]{:S(2)}, u32[]{:S(2)}) collective-permute-start(bf16[3,8,1024]{2,1,0:T(8,128)(2,1)S(1)} %get-tuple-element.50), channel_id=1, source_target_pairs={{0,8},{4,12},{8,0},{12,4},{1,9},{5,13},{9,1},{13,5},{2,10},{6,14},... | collective-permute-start | bytes 147464 | tf_op jit(solution)/shard_map/ppermute | solution.py:67
  6.6 6.2 %collective-permute-start = (bf16[3,8,1024]{2,1,0:T(8,128)(2,1)S(1)}, bf16[3,8,1024]{2,1,0:T(8,128)(2,1)S(1)}, u32[]{:S(2)}, u32[]{:S(2)}) collective-permute-start(bf16[3,8,1024]{2,1,0:T(8,128)(2,1)S(1)} %get-tuple-element.50), channel_id=1, source_target_pairs={{0,4},{4,0},{8,12},{12,8},{1,5},{5,1},{9,13},{13,9},{2,6},{6,2},{1... | collective-permute-start | bytes 147464 | tf_op jit(solution)/shard_map/ppermute | solution.py:67
  7.2 10.9 %collective-permute-start.3 = (bf16[4,8,1024]{2,1,0:T(8,128)(2,1)S(1)}, bf16[4,8,1024]{2,1,0:T(8,128)(2,1)S(1)}, u32[]{:S(2)}, u32[]{:S(2)}) collective-permute-start(bf16[4,8,1024]{2,1,0:T(8,128)(2,1)S(1)} %get-tuple-element.49.refs_3_.refs_4_), channel_id=1, source_target_pairs={{0,16},{16,0},{1,17},{17,1},{2,18},{18,2},{3,19},{19,3},{4,20},{20... | collective-permute-start | bytes 196616 | tf_op jit(solution)/shard_map/ppermute | solution.py:67
  12.8 5.3 %collective-permute-start.4 = (bf16[3,8,1024]{2,1,0:T(8,128)(2,1)S(1)}, bf16[3,8,1024]{2,1,0:T(8,128)(2,1)S(1)}, u32[]{:S(2)}, u32[]{:S(2)}) collective-permute-start(bf16[3,8,1024]{2,1,0:T(8,128)(2,1)S(1)} %collective-permute-done.refs_4_), channel_id=1, source_target_pairs={{0,16},{16,0},{1,17},{17,1},{2,18},{18,2},{3,19},{19,3},{4,20},{20... | collective-permute-start | bytes 147464 | tf_op jit(solution)/shard_map/ppermute | solution.py:67
  13.2 4.9 %collective-permute-start.5 = (bf16[3,8,1024]{2,1,0:T(8,128)(2,1)S(1)}, bf16[3,8,1024]{2,1,0:T(8,128)(2,1)S(1)}, u32[]{:S(2)}, u32[]{:S(2)}) collective-permute-start(bf16[3,8,1024]{2,1,0:T(8,128)(2,1)S(1)} %collective-permute-done.1.refs_5_), channel_id=1, source_target_pairs={{0,16},{16,0},{1,17},{17,1},{2,18},{18,2},{3,19},{19,3},{4,20},{20... | collective-permute-start | bytes 147464 | tf_op jit(solution)/shard_map/ppermute | solution.py:67
  14.9 4.1 %collective-permute-start.6 = (bf16[3,8,1024]{2,1,0:T(8,128)(2,1)S(1)}, bf16[3,8,1024]{2,1,0:T(8,128)(2,1)S(1)}, u32[]{:S(2)}, u32[]{:S(2)}) collective-permute-start(bf16[3,8,1024]{2,1,0:T(8,128)(2,1)S(1)} %collective-permute-done.2.refs_6_), channel_id=1, source_target_pairs={{0,16},{16,0},{1,17},{17,1},{2,18},{18,2},{3,19},{19,3},{4,20},{20... | collective-permute-start | bytes 147464 | tf_op jit(solution)/shard_map/ppermute | solution.py:67
  20.9 2.5 %collective-permute-start.7 = (f32[2,48,768]{2,1,0:T(8,128)S(1)}, f32[2,48,768]{2,1,0:T(8,128)S(1)}, u32[]{:S(2)}, u32[]{:S(2)}) collective-permute-start(f32[2,48,768]{2,1,0:T(8,128)S(1)} %get-tuple-element.65.refs_5_), channel_id=1, source_target_pairs={{0,1},{1,0},{2,3},{3,2},{4,5},{5,4},{6,7},{7,6},{8,9},{9,8},{10,11... | collective-permute-start | bytes 884744 | tf_op jit(solution)/shard_map/ppermute | solution.py:67
  22.9 2.4 %collective-permute-start.8 = (f32[48,768]{1,0:T(8,128)S(1)}, f32[48,768]{1,0:T(8,128)S(1)}, u32[]{:S(2)}, u32[]{:S(2)}) collective-permute-start(f32[48,768]{1,0:T(8,128)S(1)} %get-tuple-element.67.refs_7_), channel_id=1, source_target_pairs={{0,1},{1,0},{2,3},{3,2},{4,5},{5,4},{6,7},{7,6},{8,9},{9,8},{10,11... | collective-permute-start | bytes 442376 | tf_op jit(solution)/shard_map/ppermute | solution.py:67
  26.7 9.0 %collective-permute-start.10 = (bf16[3,48,768]{2,1,0:T(8,128)(2,1)S(1)}, bf16[3,48,768]{2,1,0:T(8,128)(2,1)S(1)}, u32[]{:S(2)}, u32[]{:S(2)}) collective-permute-start(bf16[3,48,768]{2,1,0:T(8,128)(2,1)S(1)} %forward_2_down.1.refs_7_), channel_id=1, source_target_pairs={{0,2},{1,3},{2,0},{3,1},{4,6},{5,7},{6,4},{7,5},{8,10},{9,11},{10,... | collective-permute-start | bytes 663560 | tf_op jit(solution)/shard_map/ppermute | solution.py:67
  31.1 4.6 %collective-permute-start.9 = (bf16[3,48,768]{2,1,0:T(8,128)(2,1)S(1)}, bf16[3,48,768]{2,1,0:T(8,128)(2,1)S(1)}, u32[]{:S(2)}, u32[]{:S(2)}) collective-permute-start(bf16[3,48,768]{2,1,0:T(8,128)(2,1)S(1)} %get-tuple-element.73), channel_id=1, source_target_pairs={{0,1},{1,0},{2,3},{3,2},{4,5},{5,4},{6,7},{7,6},{8,9},{9,8},{10,11... | collective-permute-start | bytes 663560 | tf_op jit(solution)/shard_map/ppermute | solution.py:67
  31.1 4.6 %copy-start = (f32[6144]{0:T(1024)S(1)}, f32[6144]{0:T(1024)}, u32[]{:S(2)}) copy-start(f32[6144]{0:T(1024)} %param.12) | copy-start | bytes 73732
  36.1 4.5 %collective-permute-start.13 = (bf16[112,768]{1,0:T(8,128)(2,1)S(1)}, bf16[112,768]{1,0:T(8,128)(2,1)S(1)}, u32[]{:S(2)}, u32[]{:S(2)}) collective-permute-start(bf16[112,768]{1,0:T(8,128)(2,1)S(1)} %get-tuple-element.78.refs_0_.refs_2_), channel_id=1, source_target_pairs={{0,1},{1,0},{2,3},{3,2},{4,5},{5,4},{6,7},{7,6},{8,9},{9,8},{10,11... | collective-permute-start | bytes 516104 | tf_op jit(solution)/shard_map/ppermute | solution.py:67
  36.6 5.9 %collective-permute-start.12 = (bf16[64,768]{1,0:T(8,128)(2,1)S(1)}, bf16[64,768]{1,0:T(8,128)(2,1)S(1)}, u32[]{:S(2)}, u32[]{:S(2)}) collective-permute-start(bf16[64,768]{1,0:T(8,128)(2,1)S(1)} %get-tuple-element.77), channel_id=1, source_target_pairs={{0,2},{1,3},{2,0},{3,1},{4,6},{5,7},{6,4},{7,5},{8,10},{9,11},{10,... | collective-permute-start | bytes 294920 | tf_op jit(solution)/shard_map/ppermute | solution.py:67
  37.1 6.5 %collective-permute-start.11 = (bf16[48,768]{1,0:T(8,128)(2,1)S(1)}, bf16[48,768]{1,0:T(8,128)(2,1)S(1)}, u32[]{:S(2)}, u32[]{:S(2)}) collective-permute-start(bf16[48,768]{1,0:T(8,128)(2,1)S(1)} %get-tuple-element.76), channel_id=1, source_target_pairs={{0,2},{1,3},{2,0},{3,1},{4,6},{5,7},{6,4},{7,5},{8,10},{9,11},{10,... | collective-permute-start | bytes 221192 | tf_op jit(solution)/shard_map/ppermute | solution.py:67
  42.5 2.7 %collective-permute-start.15 = (bf16[64,768]{1,0:T(8,128)(2,1)S(1)}, bf16[64,768]{1,0:T(8,128)(2,1)S(1)}, u32[]{:S(2)}, u32[]{:S(2)}) collective-permute-start(bf16[64,768]{1,0:T(8,128)(2,1)S(1)} %collective-permute-done.12.refs_0_.refs_4_), channel_id=1, source_target_pairs={{0,1},{1,0},{2,3},{3,2},{4,5},{5,4},{6,7},{7,6},{8,9},{9,8},{10,11... | collective-permute-start | bytes 294920 | tf_op jit(solution)/shard_map/ppermute | solution.py:67
  43.6 2.6 %collective-permute-start.14 = (bf16[48,768]{1,0:T(8,128)(2,1)S(1)}, bf16[48,768]{1,0:T(8,128)(2,1)S(1)}, u32[]{:S(2)}, u32[]{:S(2)}) collective-permute-start(bf16[48,768]{1,0:T(8,128)(2,1)S(1)} %collective-permute-done.11.refs_0_), channel_id=1, source_target_pairs={{0,1},{1,0},{2,3},{3,2},{4,5},{5,4},{6,7},{7,6},{8,9},{9,8},{10,11... | collective-permute-start | bytes 221192 | tf_op jit(solution)/shard_map/ppermute | solution.py:67
  47.3 5.1 %collective-permute-start.16 = (bf16[7,8,1024]{2,1,0:T(8,128)(2,1)S(1)}, bf16[7,8,1024]{2,1,0:T(8,128)(2,1)S(1)}, u32[]{:S(2)}, u32[]{:S(2)}) collective-permute-start(bf16[7,8,1024]{2,1,0:T(8,128)(2,1)S(1)} %get-tuple-element.86), channel_id=1, source_target_pairs={{0,16},{16,0},{1,17},{17,1},{2,18},{18,2},{3,19},{19,3},{4,20},{20... | collective-permute-start | bytes 344072 | tf_op jit(solution)/shard_map/ppermute | solution.py:67
  53.1 5.8 %collective-permute-start.17 = (bf16[8,2048]{1,0:T(8,128)(2,1)S(1)}, bf16[8,2048]{1,0:T(8,128)(2,1)S(1)}, u32[]{:S(2)}, u32[]{:S(2)}) collective-permute-start(bf16[8,2048]{1,0:T(8,128)(2,1)S(1)} %get-tuple-element.90), channel_id=1, source_target_pairs={{0,12},{4,8},{8,4},{12,0},{1,13},{5,9},{9,5},{13,1},{2,14},{6,10},... | collective-permute-start | bytes 98312 | tf_op jit(solution)/shard_map/ppermute | solution.py:67
  56.7 4.8 %collective-permute-start.18 = (bf16[8,2048]{1,0:T(8,128)(2,1)S(1)}, bf16[8,2048]{1,0:T(8,128)(2,1)S(1)}, u32[]{:S(2)}, u32[]{:S(2)}) collective-permute-start(bf16[8,2048]{1,0:T(8,128)(2,1)S(1)} %get-tuple-element.91), channel_id=1, source_target_pairs={{0,8},{4,12},{8,0},{12,4},{1,9},{5,13},{9,1},{13,5},{2,10},{6,14},... | collective-permute-start | bytes 98312 | tf_op jit(solution)/shard_map/ppermute | solution.py:67
  56.7 4.8 %collective-permute-start.19 = (bf16[8,2048]{1,0:T(8,128)(2,1)S(1)}, bf16[8,2048]{1,0:T(8,128)(2,1)S(1)}, u32[]{:S(2)}, u32[]{:S(2)}) collective-permute-start(bf16[8,2048]{1,0:T(8,128)(2,1)S(1)} %get-tuple-element.92), channel_id=1, source_target_pairs={{0,4},{4,0},{8,12},{12,8},{1,5},{5,1},{9,13},{13,9},{2,6},{6,2},{1... | collective-permute-start | bytes 98312 | tf_op jit(solution)/shard_map/ppermute | solution.py:67

commit v7 on v5

--- a/solution.py
+++ b/solution.py
@@ -120,6 +120,7 @@
 
 GATE, UP, DOWN = range(3)
 WHOLE_STRIP = (GATE, UP, DOWN)
+CHUNKS = 4
 
 
 def start_loads(pieces, groups, sources, targets, sem):
@@ -131,7 +132,10 @@
         start = pl.multiple_of((owner * groups + lax.axis_index("groups")) * width, width)
         source = sources[kind]
         source = source.at[pl.ds(start, width), :] if kind == DOWN else source.at[:, pl.ds(start, width)]
-        copies.append(pltpu.make_async_copy(source, target, sem.at[i]))
+        size = target.shape[0] // CHUNKS
+        for c in range(CHUNKS):
+            span = slice(c * size, (c + 1) * size)
+            copies.append(pltpu.make_async_copy(source.at[span, :], target.at[span, :], sem.at[i, c]))
     for copy in copies:
         copy.start()
     return copies
@@ -213,13 +217,14 @@
         out[GATE, :, span] = jnp.dot(tokens[...], gate[:, span], preferred_element_type=jnp.float32)
         out[UP, :, span] = jnp.dot(tokens[...], up[:, span], preferred_element_type=jnp.float32)
 
-    copies[0].wait()
+    for copy in copies:
+        copy.wait()
     out[DOWN] = contract_rows(cotans[...], down[...])
 
 
 def middle_kernel(groups, *refs):
     own, arrived, crossed, scale, relayed, other_relayed = refs[:6]
-    message, grads, other_grads, stage = refs[-4:]
+    message, near_gate, near_up, grads, other_grads, stage = refs[-6:]
     _, tokens, width = own.shape
     narrow, group = lax.axis_index("narrow"), lax.axis_index("groups")
     sums = [own[i] + arrived[i].astype(jnp.float32) + crossed[i].astype(jnp.float32) for i in range(3)]
@@ -227,6 +232,8 @@
     product, d_gate, d_up = local_grads(*sums, scale[:, pl.ds(start, width)])
     message[0:tokens, :] = d_gate
     message[tokens : 2 * tokens, :] = d_up
+    near_gate[0:tokens, :] = d_gate
+    near_up[...] = d_up
     half = tokens // groups
     for side, (source, target) in enumerate(((relayed, grads), (other_relayed, other_grads))):
         marks = source[source.shape[0] - 1].astype(jnp.float32)
@@ -244,27 +251,41 @@
             stage[side * SEQS + e : side * SEQS + e + 1, :] = total
     every = stage[...]
     squares = jnp.broadcast_to(jnp.sum(every * every, axis=1, keepdims=True), every.shape)
-    high = squares.astype(jnp.bfloat16).astype(jnp.float32)
-    message[2 * tokens :, :] = jnp.concatenate([high, squares - high], axis=0).astype(jnp.bfloat16)
+    tail = jnp.concatenate(split_high(squares), axis=0).astype(jnp.bfloat16)
+    message[2 * tokens :, :] = tail
+    near_gate[tokens:, :] = tail
 
 
 TILE = 512
 
 
-def backward_part(message, gate, up, start):
+def backward_part(grads, gate, up, start):
+    d_gate, d_up = grads
+    gate_term = contract_rows(gate[start : start + TILE, :], d_gate)
+    return gate_term + contract_rows(up[start : start + TILE, :], d_up)
+
+
+def halves(message):
     tokens = (message.shape[0] - 16) // 2
-    gate_term = contract_rows(message[0:tokens, :], gate[start : start + TILE, :])
-    return gate_term + contract_rows(message[tokens : 2 * tokens, :], up[start : start + TILE, :])
+    return message[0:tokens, :], message[tokens : 2 * tokens, :]
 
 
 def backward_first_kernel(message, gate, up, total):
-    for start in range(0, total.shape[1], TILE):
-        total[:, start : start + TILE] = backward_part(message, gate, up, start)
+    for start in range(0, total.shape[0], TILE):
+        total[start : start + TILE, :] = backward_part(halves(message), gate, up, start)
+
+
+def backward_near_kernel(d_gate, d_up, gate, up, before, total):
+    tokens = d_up.shape[0]
+    for start in range(0, total.shape[0], TILE):
+        part = backward_part((d_gate[0:tokens, :], d_up[...]), gate, up, start)
+        total[start : start + TILE, :] = before[start : start + TILE, :] + part
 
 
 def backward_next_kernel(message, gate, up, before, total):
-    for start in range(0, total.shape[1], TILE):
-        total[:, start : start + TILE] = before[:, start : start + TILE] + backward_part(message, gate, up, start)
+    for start in range(0, total.shape[0], TILE):
+        part = backward_part(halves(message), gate, up, start)
+        total[start : start + TILE, :] = before[start : start + TILE, :] + part
 
 
 def split_high(values):
@@ -279,7 +300,7 @@
     wide = send.shape[2]
     for start in range(0, features, TILE):
         span = slice(start, start + TILE)
-        total = before[:, span] + backward_part(message, gate, up, start)
+        total = (before[span, :] + backward_part(halves(message), gate, up, start)).T
         own[:, span] = total[:half]
         at = slice(start % wide, start % wide + TILE)
         for k in range(half // 8):
@@ -370,7 +391,7 @@
             [weight_shapes[kind] for kind, _ in pieces],
             args,
             {i: pltpu.HBM if i < 3 else pl.ANY for i in range(len(args))},
-            [pltpu.SemaphoreType.DMA((len(pieces),))],
+            [pltpu.SemaphoreType.DMA((len(pieces), CHUNKS))],
         )
         kept.update(zip(pieces, arrays))
 
@@ -381,7 +402,7 @@
             [weight_shapes[kind] for kind, _ in pieces] + outs,
             list(weights) + args,
             {i: pltpu.HBM for i in range(3)},
-            list(scratch) + [pltpu.SemaphoreType.DMA((len(pieces),))],
+            list(scratch) + [pltpu.SemaphoreType.DMA((len(pieces), CHUNKS))],
         )
         kept.update(zip(pieces, made))
         return made[len(pieces) :]
@@ -438,15 +459,17 @@
         [part, weight_shapes[DOWN]],
         list(weights) + panel + hold(0, [GATE, UP]),
         {i: pltpu.HBM for i in range(3)},
-        [pltpu.SemaphoreType.DMA((1,))],
+        [pltpu.SemaphoreType.DMA((1, CHUNKS))],
     )
 
     resident = [array for s in range(strips) for array in hold(s, [GATE, UP])]
-    message, grads, other_grads = call(
+    message, near_gate, near_up, grads, other_grads = call(
         functools.partial(middle_kernel, groups),
         "middle",
         [
             pltpu.VMEM((2 * tokens + 16, width), bf16),
+            pltpu.VMEM((tokens + 16, width), bf16),
+            pltpu.VMEM((tokens, width), bf16),
             pltpu.VMEM((SEQS, width), f32),
             pltpu.VMEM((SEQS, width), f32),
         ],
@@ -454,11 +477,11 @@
         scratch=[pltpu.VMEM((groups * SEQS, width), f32)],
     )
 
-    total = pltpu.VMEM((tokens, features), f32)
-    message_1 = exchange(message, "narrow", 1)
+    total = pltpu.VMEM((features, tokens), f32)
+    near_gate, near_up = exchange(near_gate, "narrow", 1), exchange(near_up, "narrow", 1)
     message_2 = exchange(message, "narrow", 2)
     sums = call(backward_first_kernel, "backward_0", total, [message] + hold(0, [GATE, UP]))
-    sums = call(backward_next_kernel, "backward_1", total, [message_1] + hold(1, [GATE, UP]) + [sums])
+    sums = call(backward_near_kernel, "backward_1", total, [near_gate, near_up] + hold(1, [GATE, UP]) + [sums])
     message_2, sums = lax.optimization_barrier((message_2, sums))
     message_3 = exchange(message_2, "narrow", 1)
     sums = call(backward_next_kernel, "backward_2", total, [message_2] + hold(2, [GATE, UP]) + [sums])
@@ -470,7 +493,7 @@
             pltpu.VMEM((8, features // 2), f32),
             pltpu.VMEM((half // 4 + 1, 8, features // 2), bf16),
         ],
-        [message_3] + hold(3, [GATE, UP]) + [sums, message, message_1, message_2, other_grads],
+        [message_3] + hold(3, [GATE, UP]) + [sums, message, near_gate, message_2, other_grads],
     )
     arrived = exchange(send, "groups", 1)
     example_grads, own_block, *sends = call(

time: 59.8 us -> 59.6 us (level)
    ppermute x14 -> x15, starting transfers between devices: 15.9 us -> 16.1 us  [exchange(): lax.ppermute(array, axis, [(i, i ^ step) for i in range(lax.axis_size(axi...]
    ppermute x14 -> x15, waiting for transfers between devices: 12.1 us -> 12.1 us  [exchange(): lax.ppermute(array, axis, [(i, i ^ step) for i in range(lax.axis_size(axi...]
  transfers between devices with their start and end apart: 14 -> 15, of which waited for: 6 -> 6; matrix products, arithmetic and copies ran while one was open for 0% -> 0% of each run, Pallas kernels for 35% -> 34%
where the time goes in v7:
time: 59.6 us; the launch traced here: 59.4 us
  Pallas kernels  30.4 us (51%)
  starting transfers between devices  16.1 us (27%)
  waiting for transfers between devices  12.1 us (20%)
  between operations  0.81 us (1%)
    pallas_call x15, Pallas kernels, call(): pl.pallas_call(body, out_shape=outs, in_specs=[pl.BlockSpec(memory_space=...  30.4 us
    ppermute x15, starting transfers between devices, exchange(): lax.ppermute(array, axis, [(i, i ^ step) for i in range(lax.axis_size(axi...  16.1 us
    ppermute x15, waiting for transfers between devices, exchange(): lax.ppermute(array, axis, [(i, i ^ step) for i in range(lax.axis_size(axi...  12.1 us
  transfers between devices with their start and end apart: 15, of which 6 were waited for; matrix products, arithmetic and copies ran while one was open for 0% of the time, Pallas kernels for 34%

profile of v7, /device:TPU:0, one launch (start us, length us, event | category | flops | bytes accessed | tf_op | source)
XLA Modules:
  0.0 59.4 jit_solution(16595986104620388326)
XLA Ops:
  0.6 0.8 %pack.1.refs_0_ = bf16[3,8,1024]{2,1,0:T(8,128)(2,1)S(1)} custom-call(bf16[6,2048]{1,0:T(8,128)(2,1)} %inputs.1, bf16[6,2048]{1,0:T(8,128)(2,1)} %cotangent.1), custom_call_target="tpu_custom_call" | custom-call | flops 1000 | bytes 1000 | tf_op jit(solution)/shard_map/pack/pallas_call | solution.py:80
  1.4 0.0 copy-start.1
  1.4 5.1 %collective-permute-start.2 = (bf16[3,8,1024]{2,1,0:T(8,128)(2,1)S(1)}, bf16[3,8,1024]{2,1,0:T(8,128)(2,1)S(1)}, u32[]{:S(2)}, u32[]{:S(2)}) collective-permute-start(bf16[3,8,1024]{2,1,0:T(8,128)(2,1)S(1)} %pack.1.refs_0_), channel_id=1, source_target_pairs={{0,12},{4,8},{8,4},{12,0},{1,13},{5,9},{9,5},{13,1},{2,14},{6,10},... | collective-permute-start | bytes 147464 | tf_op jit(solution)/shard_map/ppermute | solution.py:67
  6.6 0.0 collective-permute-start.1
  6.6 0.6 %collective-permute-start = (bf16[3,8,1024]{2,1,0:T(8,128)(2,1)S(1)}, bf16[3,8,1024]{2,1,0:T(8,128)(2,1)S(1)}, u32[]{:S(2)}, u32[]{:S(2)}) collective-permute-start(bf16[3,8,1024]{2,1,0:T(8,128)(2,1)S(1)} %pack.1.refs_0_), channel_id=1, source_target_pairs={{0,4},{4,0},{8,12},{12,8},{1,5},{5,1},{9,13},{13,9},{2,6},{6,2},{1... | collective-permute-start | bytes 147464 | tf_op jit(solution)/shard_map/ppermute | solution.py:67
  7.2 3.9 %load_a.1 = (bf16[2048,768]{1,0:T(8,128)(2,1)S(1)}, bf16[2048,768]{1,0:T(8,128)(2,1)S(1)}, bf16[768,2048]{1,0:T(8,128)(2,1)S(1)}) custom-call(bf16[2048,6144]{1,0:T(8,128)(2,1)} %refs_0_.11, bf16[2048,6144]{1,0:T(8,128)(2,1)} %refs_1_.11, bf16[6144,2048]{1,0:T(8,128)(2,1)} %refs_2_.11), custom_call_target="tpu_custom_call" | custom-call | flops 1000 | bytes 1000 | tf_op jit(solution)/shard_map/load_a/pallas_call | solution.py:80
  11.1 0.0 collective-permute-done.2.refs_3_
  11.1 0.5 collective-permute-done.1.refs_2_
  11.5 0.0 collective-permute-done.refs_1_
  11.5 0.0 copy-done.1
  11.5 0.6 relay.1.refs_3_.refs_4_
  12.1 1.6 %collective-permute-start.3 = (bf16[13,8,1024]{2,1,0:T(8,128)(2,1)S(1)}, bf16[13,8,1024]{2,1,0:T(8,128)(2,1)S(1)}, u32[]{:S(2)}, u32[]{:S(2)}) collective-permute-start(bf16[13,8,1024]{2,1,0:T(8,128)(2,1)S(1)} %relay.1.refs_3_.refs_4_), channel_id=1, source_target_pairs={{0,16},{16,0},{1,17},{17,1},{2,18},{18,2},{3,19},{19,3},{4,20},{20... | collective-permute-start | bytes 638984 | tf_op jit(solution)/shard_map/ppermute | solution.py:67
  13.7 4.9 %load_b.1 = (bf16[2048,768]{1,0:T(8,128)(2,1)S(1)}, bf16[2048,768]{1,0:T(8,128)(2,1)S(1)}, bf16[768,2048]{1,0:T(8,128)(2,1)S(1)}, bf16[2048,768]{1,0:T(8,128)(2,1)S(1)}) custom-call(bf16[2048,6144]{1,0:T(8,128)(2,1)} %refs_0_.11, bf16[2048,6144]{1,0:T(8,128)(2,1)} %refs_1_.11, bf16[6144,2048]{1,0:T(8,128)(2,1)} %refs_2_.11, ...), custom_call_target="tpu_custom_call" | custom-call | flops 1000 | bytes 1000 | tf_op jit(solution)/shard_map/load_b/pallas_call | solution.py:80
  18.6 0.0 collective-permute-done.3.refs_4_.refs_5_
  18.6 2.6 %forward_3.1 = (bf16[2048,768]{1,0:T(8,128)(2,1)S(1)}, bf16[48,2048]{1,0:T(8,128)(2,1)S(1)}, bf16[48,2048]{1,0:T(8,128)(2,1)S(1)}, f32[3,48,768]{2,1,0:T(8,128)S(1)}) custom-call(bf16[2048,6144]{1,0:T(8,128)(2,1)} %refs_0_.11, bf16[2048,6144]{1,0:T(8,128)(2,1)} %refs_1_.11, bf16[6144,2048]{1,0:T(8,128)(2,1)} %refs_2_.11, ...), custom_call_target="tpu_custom_call" | custom-call | flops 1000 | bytes 1000 | tf_op jit(solution)/shard_map/forward_3/pallas_call | solution.py:80
  21.2 0.1 collective-permute-start.4
  21.3 1.8 %collective-permute-done.4.refs_8_ = f32[3,48,768]{2,1,0:T(8,128)S(1)} collective-permute-done((f32[3,48,768]{2,1,0:T(8,128)S(1)}, f32[3,48,768]{2,1,0:T(8,128)S(1)}, u32[]{:S(2)}, u32[]{:S(2)}) %collective-permute-start.4) | collective-permute-done | bytes 442400 | tf_op jit(solution)/shard_map/ppermute | solution.py:67
  23.1 2.4 %forward_2.1 = (bf16[768,2048]{1,0:T(8,128)(2,1)S(1)}, bf16[3,48,768]{2,1,0:T(8,128)(2,1)S(1)}) custom-call(bf16[2048,6144]{1,0:T(8,128)(2,1)} %refs_0_.11, bf16[2048,6144]{1,0:T(8,128)(2,1)} %refs_1_.11, bf16[6144,2048]{1,0:T(8,128)(2,1)} %refs_2_.11, bf16[48,2048]{1,0:T(8,128)(2,1)S(1)} %get-tuple-element.41.refs_3_, ...), custom_call_target="tpu_custom_call" | custom-call | flops 1000 | bytes 1000 | tf_op jit(solution)/shard_map/forward_2/pallas_call | solution.py:80
  25.5 1.5 %collective-permute-start.6 = (bf16[3,48,768]{2,1,0:T(8,128)(2,1)S(1)}, bf16[3,48,768]{2,1,0:T(8,128)(2,1)S(1)}, u32[]{:S(2)}, u32[]{:S(2)}) collective-permute-start(bf16[3,48,768]{2,1,0:T(8,128)(2,1)S(1)} %get-tuple-element.49.refs_8_), channel_id=1, source_target_pairs={{0,2},{1,3},{2,0},{3,1},{4,6},{5,7},{6,4},{7,5},{8,10},{9,11},{10,... | collective-permute-start | bytes 663560 | tf_op jit(solution)/shard_map/ppermute | solution.py:67
  27.0 2.9 %forward_1.1 = (bf16[2048,768]{1,0:T(8,128)(2,1)S(1)}, bf16[2048,768]{1,0:T(8,128)(2,1)S(1)}, bf16[3,48,768]{2,1,0:T(8,128)(2,1)S(1)}) custom-call(bf16[2048,6144]{1,0:T(8,128)(2,1)} %refs_0_.11, bf16[2048,6144]{1,0:T(8,128)(2,1)} %refs_1_.11, bf16[6144,2048]{1,0:T(8,128)(2,1)} %refs_2_.11, bf16[48,2048]{1,0:T(8,128)(2,1)S(1)} %get-tuple-element.41.refs_3_, ...), custom_call_target="tpu_custom_call" | custom-call | flops 1000 | bytes 1000 | tf_op jit(solution)/shard_map/forward_1/pallas_call | solution.py:80
  29.9 0.1 collective-permute-start.5
  30.0 0.0 copy-start
  30.0 3.5 %forward_0.1 = (f32[3,48,768]{2,1,0:T(8,128)S(1)}, bf16[768,2048]{1,0:T(8,128)(2,1)}) custom-call(bf16[2048,6144]{1,0:T(8,128)(2,1)} %refs_0_.11, bf16[2048,6144]{1,0:T(8,128)(2,1)} %refs_1_.11, bf16[6144,2048]{1,0:T(8,128)(2,1)} %refs_2_.11, bf16[48,2048]{1,0:T(8,128)(2,1)S(1)} %get-tuple-element.41.refs_3_, ...), custom_call_target="tpu_custom_call" | custom-call | flops 1000 | bytes 1000 | tf_op jit(solution)/shard_map/forward_0/pallas_call | solution.py:80
  33.6 0.0 collective-permute-done.6.refs_2_
  33.6 0.0 collective-permute-done.5.refs_1_
  33.6 0.4 middle.1
  34.0 0.9 %collective-permute-start.7 = (bf16[112,768]{1,0:T(8,128)(2,1)S(1)}, bf16[112,768]{1,0:T(8,128)(2,1)S(1)}, u32[]{:S(2)}, u32[]{:S(2)}) collective-permute-start(bf16[112,768]{1,0:T(8,128)(2,1)S(1)} %get-tuple-element.54.message.refs_0_), channel_id=1, source_target_pairs={{0,2},{1,3},{2,0},{3,1},{4,6},{5,7},{6,4},{7,5},{8,10},{9,11},{10,... | collective-permute-start | bytes 516104 | tf_op jit(solution)/shard_map/ppermute | solution.py:67
  34.9 0.0 collective-permute-start.8
  34.9 0.5 collective-permute-start.9
  35.4 1.7 %backward_0.1.before = f32[2048,48]{1,0:T(8,128)S(1)} custom-call(bf16[112,768]{1,0:T(8,128)(2,1)S(1)} %get-tuple-element.54.message.refs_0_, bf16[2048,768]{1,0:T(8,128)(2,1)S(1)} %get-tuple-element.50.refs_5_.refs_6_.gate, bf16[2048,768]{1,0:T(8,128)(2,1)S(1)} %get-tuple-element.51.refs_6_.refs_7_.up), custom_call_target="tpu_custom_call" | custom-call | flops 1000 | bytes 1000 | tf_op jit(solution)/shard_map/backward_0/pallas_call | solution.py:80
  37.2 0.0 collective-permute-done.9.d_up
  37.2 0.0 collective-permute-done.8.d_gate.refs_1_
  37.2 1.8 %backward_1.1.before = f32[2048,48]{1,0:T(8,128)S(1)} custom-call(bf16[64,768]{1,0:T(8,128)(2,1)S(1)} %collective-permute-done.8.d_gate.refs_1_, bf16[48,768]{1,0:T(8,128)(2,1)S(1)} %collective-permute-done.9.d_up, bf16[2048,768]{1,0:T(8,128)(2,1)S(1)} %get-tuple-element.43.refs_5_.refs_8_.gate, bf16[2048,768]{1,0:T(8,128)(2,1)S(1)} %get-tuple-element.44.refs_6_.refs_9_.up, ...), custom_call_target="tpu_custom_call" | custom-call | flops 1000 | bytes 1000 | tf_op jit(solution)/shard_map/backward_1/pallas_call | solution.py:80
  39.0 1.8 %collective-permute-done.7.message.refs_2_ = bf16[112,768]{1,0:T(8,128)(2,1)S(1)} collective-permute-done((bf16[112,768]{1,0:T(8,128)(2,1)S(1)}, bf16[112,768]{1,0:T(8,128)(2,1)S(1)}, u32[]{:S(2)}, u32[]{:S(2)}) %collective-permute-start.7) | collective-permute-done | bytes 172064 | tf_op jit(solution)/shard_map/ppermute | solution.py:67
  40.7 0.0 collective-permute-start.10
  40.7 1.8 %backward_2.1.before = f32[2048,48]{1,0:T(8,128)S(1)} custom-call(bf16[112,768]{1,0:T(8,128)(2,1)S(1)} %collective-permute-done.7.message.refs_2_, bf16[2048,768]{1,0:T(8,128)(2,1)S(1)} %get-tuple-element.40.refs_8_.refs_5_.refs_10_.gate, bf16[2048,768]{1,0:T(8,128)(2,1)S(1)} %get-tuple-element.45.refs_6_.refs_11_.up, f32[2048,48]{1,0:T(8,128)S(1)} %backward_1.1.before), custom_call_target="tpu_custom_call" | custom-call | flops 1000 | bytes 1000 | tf_op jit(solution)/shard_map/backward_2/pallas_call | solution.py:80
  42.5 0.0 collective-permute-done.10.message
  42.5 1.8 %backward_3.1 = (f32[24,2048]{1,0:T(8,128)S(1)}, f32[8,1024]{1,0:T(8,128)S(1)}, bf16[7,8,1024]{2,1,0:T(8,128)(2,1)S(1)}) custom-call(bf16[112,768]{1,0:T(8,128)(2,1)S(1)} %collective-permute-done.10.message, bf16[2048,768]{1,0:T(8,128)(2,1)S(1)} %get-tuple-element.37.refs_5_.refs_12_.gate, bf16[2048,768]{1,0:T(8,128)(2,1)S(1)} %get-tuple-element.38.refs_6_.refs_13_.up, ...), custom_call_target="tpu_custom_call" | custom-call | flops 1000 | bytes 1000 | tf_op jit(solution)/shard_map/backward_3/pallas_call | solution.py:80
  44.3 1.3 %collective-permute-start.11 = (bf16[7,8,1024]{2,1,0:T(8,128)(2,1)S(1)}, bf16[7,8,1024]{2,1,0:T(8,128)(2,1)S(1)}, u32[]{:S(2)}, u32[]{:S(2)}) collective-permute-start(bf16[7,8,1024]{2,1,0:T(8,128)(2,1)S(1)} %get-tuple-element.62), channel_id=1, source_target_pairs={{0,16},{16,0},{1,17},{17,1},{2,18},{18,2},{3,19},{19,3},{4,20},{20... | collective-permute-start | bytes 344072 | tf_op jit(solution)/shard_map/ppermute | solution.py:67
  45.6 4.3 %collective-permute-done.11.arrived = bf16[7,8,1024]{2,1,0:T(8,128)(2,1)S(1)} collective-permute-done((bf16[7,8,1024]{2,1,0:T(8,128)(2,1)S(1)}, bf16[7,8,1024]{2,1,0:T(8,128)(2,1)S(1)}, u32[]{:S(2)}, u32[]{:S(2)}) %collective-permute-start.11) | collective-permute-done | bytes 114720 | tf_op jit(solution)/shard_map/ppermute | solution.py:67
  50.0 0.7 %combine.1 = (f32[4,1536]{1,0:T(4,128)}, f32[8,2048]{1,0:T(8,128)S(1)}, bf16[8,2048]{1,0:T(8,128)(2,1)S(1)}, bf16[8,2048]{1,0:T(8,128)(2,1)S(1)}, bf16[8,2048]{1,0:T(8,128)(2,1)S(1)}) custom-call(f32[24,2048]{1,0:T(8,128)S(1)} %get-tuple-element.60.own, f32[8,1024]{1,0:T(8,128)S(1)} %get-tuple-element.61.own_tail, ...), custom_call_target="tpu_custom_call" | custom-call | flops 1000 | bytes 1000 | tf_op jit(solution)/shard_map/combine/pallas_call | solution.py:80
  50.6 3.3 %collective-permute-start.12 = (bf16[8,2048]{1,0:T(8,128)(2,1)S(1)}, bf16[8,2048]{1,0:T(8,128)(2,1)S(1)}, u32[]{:S(2)}, u32[]{:S(2)}) collective-permute-start(bf16[8,2048]{1,0:T(8,128)(2,1)S(1)} %get-tuple-element.66), channel_id=1, source_target_pairs={{0,12},{4,8},{8,4},{12,0},{1,13},{5,9},{9,5},{13,1},{2,14},{6,10},... | collective-permute-start | bytes 98312 | tf_op jit(solution)/shard_map/ppermute | solution.py:67
  54.0 0.0 collective-permute-start.13
  54.0 1.0 %collective-permute-start.14 = (bf16[8,2048]{1,0:T(8,128)(2,1)S(1)}, bf16[8,2048]{1,0:T(8,128)(2,1)S(1)}, u32[]{:S(2)}, u32[]{:S(2)}) collective-permute-start(bf16[8,2048]{1,0:T(8,128)(2,1)S(1)} %get-tuple-element.68), channel_id=1, source_target_pairs={{0,4},{4,0},{8,12},{12,8},{1,5},{5,1},{9,13},{13,9},{2,6},{6,2},{1... | collective-permute-start | bytes 98312 | tf_op jit(solution)/shard_map/ppermute | solution.py:67
  55.0 1.4 %collective-permute-done.12.refs_1_ = bf16[8,2048]{1,0:T(8,128)(2,1)S(1)} collective-permute-done((bf16[8,2048]{1,0:T(8,128)(2,1)S(1)}, bf16[8,2048]{1,0:T(8,128)(2,1)S(1)}, u32[]{:S(2)}, u32[]{:S(2)}) %collective-permute-start.12) | collective-permute-done | bytes 32800 | tf_op jit(solution)/shard_map/ppermute | solution.py:67
  56.4 2.4 %collective-permute-done.13.refs_2_ = bf16[8,2048]{1,0:T(8,128)(2,1)S(1)} collective-permute-done((bf16[8,2048]{1,0:T(8,128)(2,1)S(1)}, bf16[8,2048]{1,0:T(8,128)(2,1)S(1)}, u32[]{:S(2)}, u32[]{:S(2)}) %collective-permute-start.13) | collective-permute-done | bytes 32800 | tf_op jit(solution)/shard_map/ppermute | solution.py:67
  58.8 0.0 collective-permute-done.14.refs_3_
  58.8 0.7 %last.1 = (bf16[6,2048]{1,0:T(8,128)(2,1)}, f32[4]{0:T(128)}) custom-call(f32[8,2048]{1,0:T(8,128)S(1)} %get-tuple-element.65.refs_0_, bf16[8,2048]{1,0:T(8,128)(2,1)S(1)} %collective-permute-done.12.refs_1_, bf16[8,2048]{1,0:T(8,128)(2,1)S(1)} %collective-permute-done.13.refs_2_, bf16[8,2048]{1,0:T(8,128)(2,1)S(1)} %collective-permute-done.14.refs_3_), custom_call_target="tpu_custom_call" | custom-call | flops 1000 | bytes 1000 | tf_op jit(solution)/shard_map/last/pallas_call | solution.py:80
  (1 shorter events, 0.0 us)
Async XLA Ops:
  1.4 10.1 %copy-start.1 = (s32[24]{0:T(128)S(1)}, s32[24]{0:T(128)}, u32[]{:S(2)}) copy-start(s32[24]{0:T(128)} %refs_4_.1) | copy-start | bytes 292
  1.4 9.6 %collective-permute-start.2 = (bf16[3,8,1024]{2,1,0:T(8,128)(2,1)S(1)}, bf16[3,8,1024]{2,1,0:T(8,128)(2,1)S(1)}, u32[]{:S(2)}, u32[]{:S(2)}) collective-permute-start(bf16[3,8,1024]{2,1,0:T(8,128)(2,1)S(1)} %pack.1.refs_0_), channel_id=1, source_target_pairs={{0,12},{4,8},{8,4},{12,0},{1,13},{5,9},{9,5},{13,1},{2,14},{6,10},... | collective-permute-start | bytes 147464 | tf_op jit(solution)/shard_map/ppermute | solution.py:67
  6.6 5.0 %collective-permute-start.1 = (bf16[3,8,1024]{2,1,0:T(8,128)(2,1)S(1)}, bf16[3,8,1024]{2,1,0:T(8,128)(2,1)S(1)}, u32[]{:S(2)}, u32[]{:S(2)}) collective-permute-start(bf16[3,8,1024]{2,1,0:T(8,128)(2,1)S(1)} %pack.1.refs_0_), channel_id=1, source_target_pairs={{0,8},{4,12},{8,0},{12,4},{1,9},{5,13},{9,1},{13,5},{2,10},{6,14},... | collective-permute-start | bytes 147464 | tf_op jit(solution)/shard_map/ppermute | solution.py:67
  6.6 5.0 %collective-permute-start = (bf16[3,8,1024]{2,1,0:T(8,128)(2,1)S(1)}, bf16[3,8,1024]{2,1,0:T(8,128)(2,1)S(1)}, u32[]{:S(2)}, u32[]{:S(2)}) collective-permute-start(bf16[3,8,1024]{2,1,0:T(8,128)(2,1)S(1)} %pack.1.refs_0_), channel_id=1, source_target_pairs={{0,4},{4,0},{8,12},{12,8},{1,5},{5,1},{9,13},{13,9},{2,6},{6,2},{1... | collective-permute-start | bytes 147464 | tf_op jit(solution)/shard_map/ppermute | solution.py:67
  12.1 6.5 %collective-permute-start.3 = (bf16[13,8,1024]{2,1,0:T(8,128)(2,1)S(1)}, bf16[13,8,1024]{2,1,0:T(8,128)(2,1)S(1)}, u32[]{:S(2)}, u32[]{:S(2)}) collective-permute-start(bf16[13,8,1024]{2,1,0:T(8,128)(2,1)S(1)} %relay.1.refs_3_.refs_4_), channel_id=1, source_target_pairs={{0,16},{16,0},{1,17},{17,1},{2,18},{18,2},{3,19},{19,3},{4,20},{20... | collective-permute-start | bytes 638984 | tf_op jit(solution)/shard_map/ppermute | solution.py:67
  21.2 1.9 %collective-permute-start.4 = (f32[3,48,768]{2,1,0:T(8,128)S(1)}, f32[3,48,768]{2,1,0:T(8,128)S(1)}, u32[]{:S(2)}, u32[]{:S(2)}) collective-permute-start(f32[3,48,768]{2,1,0:T(8,128)S(1)} %get-tuple-element.47), channel_id=1, source_target_pairs={{0,1},{1,0},{2,3},{3,2},{4,5},{5,4},{6,7},{7,6},{8,9},{9,8},{10,11... | collective-permute-start | bytes 1327112 | tf_op jit(solution)/shard_map/ppermute | solution.py:67
  25.5 8.0 %collective-permute-start.6 = (bf16[3,48,768]{2,1,0:T(8,128)(2,1)S(1)}, bf16[3,48,768]{2,1,0:T(8,128)(2,1)S(1)}, u32[]{:S(2)}, u32[]{:S(2)}) collective-permute-start(bf16[3,48,768]{2,1,0:T(8,128)(2,1)S(1)} %get-tuple-element.49.refs_8_), channel_id=1, source_target_pairs={{0,2},{1,3},{2,0},{3,1},{4,6},{5,7},{6,4},{7,5},{8,10},{9,11},{10,... | collective-permute-start | bytes 663560 | tf_op jit(solution)/shard_map/ppermute | solution.py:67
  29.9 3.6 %collective-permute-start.5 = (bf16[3,48,768]{2,1,0:T(8,128)(2,1)S(1)}, bf16[3,48,768]{2,1,0:T(8,128)(2,1)S(1)}, u32[]{:S(2)}, u32[]{:S(2)}) collective-permute-start(bf16[3,48,768]{2,1,0:T(8,128)(2,1)S(1)} %get-tuple-element.53), channel_id=1, source_target_pairs={{0,1},{1,0},{2,3},{3,2},{4,5},{5,4},{6,7},{7,6},{8,9},{9,8},{10,11... | collective-permute-start | bytes 663560 | tf_op jit(solution)/shard_map/ppermute | solution.py:67
  30.0 3.6 %copy-start = (f32[6144]{0:T(1024)S(1)}, f32[6144]{0:T(1024)}, u32[]{:S(2)}) copy-start(f32[6144]{0:T(1024)} %param.12) | copy-start | bytes 73732
  34.0 6.8 %collective-permute-start.7 = (bf16[112,768]{1,0:T(8,128)(2,1)S(1)}, bf16[112,768]{1,0:T(8,128)(2,1)S(1)}, u32[]{:S(2)}, u32[]{:S(2)}) collective-permute-start(bf16[112,768]{1,0:T(8,128)(2,1)S(1)} %get-tuple-element.54.message.refs_0_), channel_id=1, source_target_pairs={{0,2},{1,3},{2,0},{3,1},{4,6},{5,7},{6,4},{7,5},{8,10},{9,11},{10,... | collective-permute-start | bytes 516104 | tf_op jit(solution)/shard_map/ppermute | solution.py:67
  34.9 2.3 %collective-permute-start.8 = (bf16[64,768]{1,0:T(8,128)(2,1)S(1)}, bf16[64,768]{1,0:T(8,128)(2,1)S(1)}, u32[]{:S(2)}, u32[]{:S(2)}) collective-permute-start(bf16[64,768]{1,0:T(8,128)(2,1)S(1)} %get-tuple-element.55), channel_id=1, source_target_pairs={{0,1},{1,0},{2,3},{3,2},{4,5},{5,4},{6,7},{7,6},{8,9},{9,8},{10,11... | collective-permute-start | bytes 294920 | tf_op jit(solution)/shard_map/ppermute | solution.py:67
  34.9 2.3 %collective-permute-start.9 = (bf16[48,768]{1,0:T(8,128)(2,1)S(1)}, bf16[48,768]{1,0:T(8,128)(2,1)S(1)}, u32[]{:S(2)}, u32[]{:S(2)}) collective-permute-start(bf16[48,768]{1,0:T(8,128)(2,1)S(1)} %get-tuple-element.56), channel_id=1, source_target_pairs={{0,1},{1,0},{2,3},{3,2},{4,5},{5,4},{6,7},{7,6},{8,9},{9,8},{10,11... | collective-permute-start | bytes 221192 | tf_op jit(solution)/shard_map/ppermute | solution.py:67
  40.7 1.8 %collective-permute-start.10 = (bf16[112,768]{1,0:T(8,128)(2,1)S(1)}, bf16[112,768]{1,0:T(8,128)(2,1)S(1)}, u32[]{:S(2)}, u32[]{:S(2)}) collective-permute-start(bf16[112,768]{1,0:T(8,128)(2,1)S(1)} %collective-permute-done.7.message.refs_2_), channel_id=1, source_target_pairs={{0,1},{1,0},{2,3},{3,2},{4,5},{5,4},{6,7},{7,6},{8,9},{9,8},{10,11... | collective-permute-start | bytes 516104 | tf_op jit(solution)/shard_map/ppermute | solution.py:67
  44.3 5.6 %collective-permute-start.11 = (bf16[7,8,1024]{2,1,0:T(8,128)(2,1)S(1)}, bf16[7,8,1024]{2,1,0:T(8,128)(2,1)S(1)}, u32[]{:S(2)}, u32[]{:S(2)}) collective-permute-start(bf16[7,8,1024]{2,1,0:T(8,128)(2,1)S(1)} %get-tuple-element.62), channel_id=1, source_target_pairs={{0,16},{16,0},{1,17},{17,1},{2,18},{18,2},{3,19},{19,3},{4,20},{20... | collective-permute-start | bytes 344072 | tf_op jit(solution)/shard_map/ppermute | solution.py:67
  50.6 5.7 %collective-permute-start.12 = (bf16[8,2048]{1,0:T(8,128)(2,1)S(1)}, bf16[8,2048]{1,0:T(8,128)(2,1)S(1)}, u32[]{:S(2)}, u32[]{:S(2)}) collective-permute-start(bf16[8,2048]{1,0:T(8,128)(2,1)S(1)} %get-tuple-element.66), channel_id=1, source_target_pairs={{0,12},{4,8},{8,4},{12,0},{1,13},{5,9},{9,5},{13,1},{2,14},{6,10},... | collective-permute-start | bytes 98312 | tf_op jit(solution)/shard_map/ppermute | solution.py:67
  54.0 4.8 %collective-permute-start.13 = (bf16[8,2048]{1,0:T(8,128)(2,1)S(1)}, bf16[8,2048]{1,0:T(8,128)(2,1)S(1)}, u32[]{:S(2)}, u32[]{:S(2)}) collective-permute-start(bf16[8,2048]{1,0:T(8,128)(2,1)S(1)} %get-tuple-element.67), channel_id=1, source_target_pairs={{0,8},{4,12},{8,0},{12,4},{1,9},{5,13},{9,1},{13,5},{2,10},{6,14},... | collective-permute-start | bytes 98312 | tf_op jit(solution)/shard_map/ppermute | solution.py:67
  54.0 4.8 %collective-permute-start.14 = (bf16[8,2048]{1,0:T(8,128)(2,1)S(1)}, bf16[8,2048]{1,0:T(8,128)(2,1)S(1)}, u32[]{:S(2)}, u32[]{:S(2)}) collective-permute-start(bf16[8,2048]{1,0:T(8,128)(2,1)S(1)} %get-tuple-element.68), channel_id=1, source_target_pairs={{0,4},{4,0},{8,12},{12,8},{1,5},{5,1},{9,13},{13,9},{2,6},{6,2},{1... | collective-permute-start | bytes 98312 | tf_op jit(solution)/shard_map/ppermute | solution.py:67

commit v8 on v7

--- a/solution.py
+++ b/solution.py
@@ -182,11 +182,8 @@
     strip_parts(tokens, cotans, gate, up, down, put)
 
 
-def forward_add_kernel(tokens, cotans, gate, up, down, arrived, out):
-    def put(kind, span, part):
-        out[kind, :, span] = (part + arrived[kind, :, span]).astype(out.dtype)
-
-    strip_parts(tokens, cotans, gate, up, down, put)
+def join_kernel(own, arrived, out):
+    out[...] = (own[...] + arrived[...]).astype(out.dtype)
 
 
 def first_kernel(share, relayed, other, gate, up, down, *refs):
@@ -206,20 +203,20 @@
 
 
 def own_strip_kernel(groups, *refs):
-    sources, (tokens, cotans, gate, up) = refs[:3], refs[3:7]
-    out, down, sem = refs[-3:]
-    copies = start_loads([(DOWN, 0)], groups, sources, [down], sem)
+    sources, (tokens, cotans, up, down) = refs[:3], refs[3:7]
+    out, gate, sem = refs[-3:]
+    copies = start_loads([(GATE, 0)], groups, sources, [gate], sem)
     tile = 256
 
-    @pl.loop(0, gate.shape[1] // tile)
+    @pl.loop(0, up.shape[1] // tile)
     def _(i):
         span = pl.ds(pl.multiple_of(i * tile, tile), tile)
-        out[GATE, :, span] = jnp.dot(tokens[...], gate[:, span], preferred_element_type=jnp.float32)
         out[UP, :, span] = jnp.dot(tokens[...], up[:, span], preferred_element_type=jnp.float32)
+        out[DOWN, :, span] = contract_rows(cotans[...], down[span, :])
 
     for copy in copies:
         copy.wait()
-    out[DOWN] = contract_rows(cotans[...], down[...])
+    out[GATE] = jnp.dot(tokens[...], gate[...], preferred_element_type=jnp.float32)
 
 
 def middle_kernel(groups, *refs):
@@ -293,75 +290,74 @@
     return high, values - high
 
 
-def backward_last_kernel(message, gate, up, before, *refs):
-    others, other_grads = refs[:3], refs[3]
-    own, own_tail, send = refs[4:7]
-    half, features = own.shape
-    wide = send.shape[2]
+def backward_last_kernel(share, message, gate, up, before, *refs):
+    others, (own, own_squares), sends, (total, stage) = refs[:3], refs[3:5], refs[5:-2], refs[-2:]
+    tokens, features = total.shape
+    side = features // 2
     for start in range(0, features, TILE):
-        span = slice(start, start + TILE)
-        total = (before[span, :] + backward_part(halves(message), gate, up, start)).T
-        own[:, span] = total[:half]
-        at = slice(start % wide, start % wide + TILE)
-        for k in range(half // 8):
-            slab = start // wide * (half // 8) + k
-            send[slab, :, at] = total[half + 8 * k : half + 8 * k + 8].astype(jnp.bfloat16)
+        part = before[start : start + TILE, :] + backward_part(halves(message), gate, up, start)
+        total[:, start : start + TILE] = part.T
     squares = sum(ref[ref.shape[0] - 16 :, 0:128].astype(jnp.float32) for ref in (message,) + others)
-    high, low = split_high(squares[0:8] + squares[8:16])
-    own_tail[...] = jnp.zeros_like(own_tail)
+    squares = squares[0:8] + squares[8:16]
+    own_squares[...] = squares
+    tails = split_high(squares)
+    wide = len(sends) + 1
+    for i, target in enumerate((own,) + tuple(sends)):
+        rows = own if i == 0 else stage
+        for group in range(2):
+            at = (group * wide + i) * share
+            for j in range(2):
+                to = (2 * group + j) * share
+                rows[to : to + share, :] = total[at : at + share, j * side : (j + 1) * side]
+        if i > 0:
+            for k in range(target.shape[0]):
+                target[k, :, 0:side] = stage[8 * k : 8 * k + 8, :].astype(jnp.bfloat16)
+                tail = tails[k] if k < 2 else jnp.zeros_like(squares)
+                target[k, :, side:] = tail.astype(jnp.bfloat16)
+
+
+def combine_kernel(share, own, own_squares, other_grads, *refs):
+    arrived, (kept_rows, kept_squares, send, total, stage) = refs[:-5], refs[-5:]
+    slabs, side = arrived[0].shape[0], own.shape[1]
+    squares = own_squares[...]
+    for k in range(slabs):
+        rows = own[8 * k : 8 * k + 8, :]
+        for ref in arrived:
+            values = ref[k].astype(jnp.float32)
+            rows = rows + values[:, 0:side]
+            if k < 2:
+                squares = squares + values[:, side:]
+        total[8 * k : 8 * k + 8, :] = rows
+    kept_squares[...] = squares
+    count = 2 * share
+    kept_rows[0:count, :] = total[0:count, :]
+    stage[...] = jnp.zeros_like(stage)
+    stage[0:count, :] = total[count : 2 * count, :]
     width = other_grads.shape[1]
     for i, rows in enumerate(split_high(other_grads[...])):
-        own_tail[i * SEQS : (i + 1) * SEQS, 0:width] = rows
-    own_tail[:, width : width + 128] = high
-    own_tail[:, width + 128 : width + 256] = low
-    send[send.shape[0] - 1] = own_tail[...].astype(jnp.bfloat16)
-
-
-def combine_kernel(share, own, own_tail, arrived, grads, *refs):
-    example_grads, own_block, sends, total = refs[0], refs[1], refs[2:-1], refs[-1]
-    half, features = own.shape
-    width = grads.shape[1]
+        stage[16 + i * SEQS : 16 + (i + 1) * SEQS, 0:width] = rows
+    for i, rows in enumerate(split_high(squares)):
+        stage[16:24, width + i * 128 : width + (i + 1) * 128] = rows
+    for k in range(3):
+        send[k] = stage[8 * k : 8 * k + 8, :].astype(jnp.bfloat16)
+
+
+def last_kernel(share, own, own_squares, arrived, grads, input_grad, example_grads, norms, stage):
+    side, width = own.shape[1], grads.shape[1]
     group = lax.axis_index("groups")
-    slabs, wide = half // 8, own_tail.shape[1]
-    for k in range(slabs):
-        for i in range(features // wide):
-            span = slice(i * wide, (i + 1) * wide)
-            total[8 * k : 8 * k + 8, span] = own[8 * k : 8 * k + 8, span] + arrived[i * slabs + k].astype(jnp.float32)
-    tail = arrived[arrived.shape[0] - 1].astype(jnp.float32)
+    for k in range(2):
+        stage[8 * k : 8 * k + 8, :] = own[8 * k : 8 * k + 8, :] + arrived[k].astype(jnp.float32)
+    for j in range(2):
+        rows = stage[j * share : (j + 1) * share, :]
+        input_grad[:, j * side : (j + 1) * side] = rows.astype(jnp.bfloat16)
+    tail = arrived[2].astype(jnp.float32)
     other = tail[0:SEQS, 0:width] + tail[SEQS : 2 * SEQS, 0:width]
     example_grads[:, pl.ds(pl.multiple_of(group * width, width), width)] = grads[...]
     example_grads[:, pl.ds(pl.multiple_of((1 - group) * width, width), width)] = other
-    lanes = SEQS * 128
-
-    def squares(ref, first):
-        rows = ref[:, width : width + 128] + ref[:, width + 128 : width + 256]
-        return jnp.concatenate([rows[first + e : first + e + 1] for e in range(SEQS)], axis=1)
-
-    here, there = squares(own_tail[...], 0), squares(tail, SEQS)
-    high, low = split_high(here + there)
-    for i, target in enumerate((own_block,) + tuple(sends)):
-        rows = total[i * share : (i + 1) * share, :]
-        if i == 0:
-            target[...] = jnp.zeros_like(target)
-            target[0:share, :] = rows
-            target[6:7, 0:lanes] = high
-            target[7:8, 0:lanes] = low
-        else:
-            total[half : half + share, :] = rows
-            if i == 1:
-                total[half + 6 : half + 8, :] = jnp.zeros((2, features), jnp.float32)
-                total[half + 6 : half + 7, 0:lanes] = high
-                total[half + 7 : half + 8, 0:lanes] = low
-            target[...] = total[half : half + 8, :].astype(jnp.bfloat16)
-
-
-def last_kernel(*refs):
-    own, arrived, (input_grad, norms) = refs[0], refs[1:-2], refs[-2:]
-    total = own[...] + sum(ref[...].astype(jnp.float32) for ref in arrived)
-    input_grad[...] = total[0 : input_grad.shape[0]].astype(jnp.bfloat16)
-    roots = jnp.sqrt(total[6:7, 0 : SEQS * 128] + total[7:8, 0 : SEQS * 128])
+    squares = tail[:, width : width + 128] + tail[:, width + 128 : width + 256]
+    roots = jnp.sqrt(own_squares[0:SEQS, :] + squares[SEQS : 2 * SEQS])
     for e in range(SEQS):
-        norms[e] = jnp.max(roots[:, e * 128 : (e + 1) * 128])
+        norms[e] = jnp.max(roots[e : e + 1])
 
 
 def shared(inputs, cotangent, gate_weight, up_weight, down_weight, ia3_scale, seq_ids):
@@ -441,23 +437,18 @@
     )
     panel = [tokens_all, cotans_all]
     diagonal = exchange(diagonal, "narrow", 1)
-    (crossing,) = call_loading(
-        forward_add_kernel,
-        "forward_2",
-        [(DOWN, 1)],
-        [pltpu.VMEM((3, tokens, width), bf16)],
-        panel + hold(2) + [diagonal],
-    )
+    (second,) = call_loading(forward_kernel, "forward_2", [(DOWN, 1)], [part], panel + hold(2))
+    crossing = call(join_kernel, "join", near_shape, [held(second), diagonal])
     crossed = exchange(crossing, "narrow", 2)
     (near,) = call_loading(
-        forward_kernel, "forward_1", [(GATE, 0), (UP, 0)], [near_shape], panel + hold(1) + [held(crossing)]
+        forward_kernel, "forward_1", [(UP, 0), (DOWN, 0)], [near_shape], panel + hold(1) + [held(crossing)]
     )
     near = exchange(near, "narrow", 1)
-    own_part, kept[DOWN, 0] = call(
+    own_part, kept[GATE, 0] = call(
         functools.partial(own_strip_kernel, groups),
         "forward_0",
-        [part, weight_shapes[DOWN]],
-        list(weights) + panel + hold(0, [GATE, UP]),
+        [part, weight_shapes[GATE]],
+        list(weights) + panel + hold(0, [UP, DOWN]),
         {i: pltpu.HBM for i in range(3)},
         [pltpu.SemaphoreType.DMA((1, CHUNKS))],
     )
@@ -485,32 +476,34 @@
     message_2, sums = lax.optimization_barrier((message_2, sums))
     message_3 = exchange(message_2, "narrow", 1)
     sums = call(backward_next_kernel, "backward_2", total, [message_2] + hold(2, [GATE, UP]) + [sums])
-    own, own_tail, send = call(
-        backward_last_kernel,
+    side = features // 2
+    block = pltpu.VMEM((slabs, 8, side + 128), bf16)
+    own, own_squares, *sends = call(
+        functools.partial(backward_last_kernel, share),
         "backward_3",
-        [
-            pltpu.VMEM((half, features), f32),
-            pltpu.VMEM((8, features // 2), f32),
-            pltpu.VMEM((half // 4 + 1, 8, features // 2), bf16),
-        ],
-        [message_3] + hold(3, [GATE, UP]) + [sums, message, near_gate, message_2, other_grads],
-    )
-    arrived = exchange(send, "groups", 1)
-    example_grads, own_block, *sends = call(
+        [pltpu.VMEM((4 * share, side), f32), pltpu.VMEM((8, 128), f32)] + [block] * (wide - 1),
+        [message_3] + hold(3, [GATE, UP]) + [sums, message, near_gate, message_2],
+        scratch=[pltpu.VMEM((tokens, features), f32), pltpu.VMEM((4 * share, side), f32)],
+    )
+    arrived = [exchange(sends[s - 1], "wide", s) for s in reversed(range(1, wide))]
+    own, own_squares, send = call(
         functools.partial(combine_kernel, share),
         "combine",
-        [jax.ShapeDtypeStruct((SEQS, groups * width), f32), pltpu.VMEM((8, features), f32)]
-        + [pltpu.VMEM((8, features), bf16)] * (wide - 1),
-        [own, own_tail, arrived, grads],
-        scratch=[pltpu.VMEM((half + 8, features), f32)],
-    )
-    arrived = [exchange(sends[s - 1], "wide", s) for s in reversed(range(1, wide))]
-    input_grad, norms = call(
-        last_kernel,
+        [pltpu.VMEM((16, side), f32), pltpu.VMEM((8, 128), f32), pltpu.VMEM((3, 8, side), bf16)],
+        [own, own_squares, other_grads] + arrived,
+        scratch=[pltpu.VMEM((4 * share, side), f32), pltpu.VMEM((24, side), f32)],
+    )
+    input_grad, example_grads, norms = call(
+        functools.partial(last_kernel, share),
         "last",
-        [jax.ShapeDtypeStruct((share, features), bf16), jax.ShapeDtypeStruct((SEQS,), f32)],
-        [own_block] + arrived,
-        out_spaces={1: pltpu.SMEM},
+        [
+            jax.ShapeDtypeStruct((share, features), bf16),
+            jax.ShapeDtypeStruct((SEQS, groups * width), f32),
+            jax.ShapeDtypeStruct((SEQS,), f32),
+        ],
+        [own, own_squares, exchange(send, "groups", 1), grads],
+        scratch=[pltpu.VMEM((16, side), f32)],
+        out_spaces={2: pltpu.SMEM},
     )
     return (example_grads, norms, input_grad)
 
@@ -531,8 +524,7 @@
         and features >= 2048
         and width <= features // 2 - 256
         and features % (2 * TILE) == 0
-        and share <= 6
-        and share % 2 == 0
+        and share in (4, 6)
         and (share * wide) % 8 == 0
         and share * wide <= 64
         and 3 * features * hidden // groups * 2 <= 40 << 20

time: 59.6 us -> 55.6 us (0.933)
  waiting for transfers between devices: 12.1 us -> 8.75 us
  Pallas kernels: 30.4 us -> 28.9 us
  starting transfers between devices: 16.1 us -> 16.9 us
    ppermute x15, waiting for transfers between devices: 12.1 us -> 8.75 us  [exchange(): lax.ppermute(array, axis, [(i, i ^ step) for i in range(lax.axis_size(axi...]
    pallas_call x15 -> x16, Pallas kernels: 30.4 us -> 28.9 us  [call(): pl.pallas_call(body, out_shape=outs, in_specs=[pl.BlockSpec(memory_space=...]
    ppermute x15, starting transfers between devices: 16.1 us -> 16.9 us  [exchange(): lax.ppermute(array, axis, [(i, i ^ step) for i in range(lax.axis_size(axi...]
  transfers between devices with their start and end apart: 15 -> 15, of which waited for: 6 -> 7; matrix products, arithmetic and copies ran while one was open for 0% -> 0% of each run, Pallas kernels for 34% -> 40%
where the time goes in v8:
time: 55.6 us; the launch traced here: 55.4 us
  Pallas kernels  28.9 us (52%)
  starting transfers between devices  16.9 us (30%)
  waiting for transfers between devices  8.75 us (16%)
  between operations  0.79 us (1%)
    pallas_call x16, Pallas kernels, call(): pl.pallas_call(body, out_shape=outs, in_specs=[pl.BlockSpec(memory_space=...  28.9 us
    ppermute x15, starting transfers between devices, exchange(): lax.ppermute(array, axis, [(i, i ^ step) for i in range(lax.axis_size(axi...  16.9 us
    ppermute x15, waiting for transfers between devices, exchange(): lax.ppermute(array, axis, [(i, i ^ step) for i in range(lax.axis_size(axi...  8.75 us
  transfers between devices with their start and end apart: 15, of which 7 were waited for; matrix products, arithmetic and copies ran while one was open for 0% of the time, Pallas kernels for 40%

profile of v8, /device:TPU:0, one launch (start us, length us, event | category | flops | bytes accessed | tf_op | source)
XLA Modules:
  0.0 55.4 jit_solution(13063512420999620821)
XLA Ops:
  0.6 0.8 %pack.1.refs_0_ = bf16[3,8,1024]{2,1,0:T(8,128)(2,1)S(1)} custom-call(bf16[6,2048]{1,0:T(8,128)(2,1)} %inputs.1, bf16[6,2048]{1,0:T(8,128)(2,1)} %cotangent.1), custom_call_target="tpu_custom_call" | custom-call | flops 1000 | bytes 1000 | tf_op jit(solution)/shard_map/pack/pallas_call | solution.py:80
  1.4 0.0 copy-start.1
  1.4 5.1 %collective-permute-start.2 = (bf16[3,8,1024]{2,1,0:T(8,128)(2,1)S(1)}, bf16[3,8,1024]{2,1,0:T(8,128)(2,1)S(1)}, u32[]{:S(2)}, u32[]{:S(2)}) collective-permute-start(bf16[3,8,1024]{2,1,0:T(8,128)(2,1)S(1)} %pack.1.refs_0_), channel_id=1, source_target_pairs={{0,12},{4,8},{8,4},{12,0},{1,13},{5,9},{9,5},{13,1},{2,14},{6,10},... | collective-permute-start | bytes 147464 | tf_op jit(solution)/shard_map/ppermute | solution.py:67
  6.6 0.0 collective-permute-start.1
  6.6 0.6 %collective-permute-start = (bf16[3,8,1024]{2,1,0:T(8,128)(2,1)S(1)}, bf16[3,8,1024]{2,1,0:T(8,128)(2,1)S(1)}, u32[]{:S(2)}, u32[]{:S(2)}) collective-permute-start(bf16[3,8,1024]{2,1,0:T(8,128)(2,1)S(1)} %pack.1.refs_0_), channel_id=1, source_target_pairs={{0,4},{4,0},{8,12},{12,8},{1,5},{5,1},{9,13},{13,9},{2,6},{6,2},{1... | collective-permute-start | bytes 147464 | tf_op jit(solution)/shard_map/ppermute | solution.py:67
  7.2 3.9 %load_a.1 = (bf16[2048,768]{1,0:T(8,128)(2,1)S(1)}, bf16[2048,768]{1,0:T(8,128)(2,1)S(1)}, bf16[768,2048]{1,0:T(8,128)(2,1)S(1)}) custom-call(bf16[2048,6144]{1,0:T(8,128)(2,1)} %refs_0_.11, bf16[2048,6144]{1,0:T(8,128)(2,1)} %refs_1_.11, bf16[6144,2048]{1,0:T(8,128)(2,1)} %refs_2_.11), custom_call_target="tpu_custom_call" | custom-call | flops 1000 | bytes 1000 | tf_op jit(solution)/shard_map/load_a/pallas_call | solution.py:80
  11.1 0.0 collective-permute-done.2.refs_3_
  11.1 0.5 collective-permute-done.1.refs_2_
  11.5 0.0 collective-permute-done.refs_1_
  11.5 0.0 copy-done.1
  11.5 0.6 %relay.1.refs_3_.refs_4_ = bf16[13,8,1024]{2,1,0:T(8,128)(2,1)S(1)} custom-call(bf16[3,8,1024]{2,1,0:T(8,128)(2,1)S(1)} %pack.1.refs_0_, bf16[3,8,1024]{2,1,0:T(8,128)(2,1)S(1)} %collective-permute-done.refs_1_, bf16[3,8,1024]{2,1,0:T(8,128)(2,1)S(1)} %collective-permute-done.1.refs_2_, bf16[3,8,1024]{2,1,0:T(8,128)(2,1)S(1)} %collective-permute-done.2.refs_3_, ...), custom_call_target="tpu_custom_call" | custom-call | flops 1000 | bytes 1000 | tf_op jit(solution)/shard_map/relay/pallas_call | solution.py:80
  12.1 1.6 %collective-permute-start.3 = (bf16[13,8,1024]{2,1,0:T(8,128)(2,1)S(1)}, bf16[13,8,1024]{2,1,0:T(8,128)(2,1)S(1)}, u32[]{:S(2)}, u32[]{:S(2)}) collective-permute-start(bf16[13,8,1024]{2,1,0:T(8,128)(2,1)S(1)} %relay.1.refs_3_.refs_4_), channel_id=1, source_target_pairs={{0,16},{16,0},{1,17},{17,1},{2,18},{18,2},{3,19},{19,3},{4,20},{20... | collective-permute-start | bytes 638984 | tf_op jit(solution)/shard_map/ppermute | solution.py:67
  13.7 4.9 %load_b.1 = (bf16[2048,768]{1,0:T(8,128)(2,1)S(1)}, bf16[2048,768]{1,0:T(8,128)(2,1)S(1)}, bf16[768,2048]{1,0:T(8,128)(2,1)S(1)}, bf16[2048,768]{1,0:T(8,128)(2,1)S(1)}) custom-call(bf16[2048,6144]{1,0:T(8,128)(2,1)} %refs_0_.11, bf16[2048,6144]{1,0:T(8,128)(2,1)} %refs_1_.11, bf16[6144,2048]{1,0:T(8,128)(2,1)} %refs_2_.11, ...), custom_call_target="tpu_custom_call" | custom-call | flops 1000 | bytes 1000 | tf_op jit(solution)/shard_map/load_b/pallas_call | solution.py:80
  18.6 0.0 collective-permute-done.3.refs_4_.refs_5_
  18.6 2.6 %forward_3.1 = (bf16[2048,768]{1,0:T(8,128)(2,1)S(1)}, bf16[48,2048]{1,0:T(8,128)(2,1)S(1)}, bf16[48,2048]{1,0:T(8,128)(2,1)S(1)}, f32[3,48,768]{2,1,0:T(8,128)S(1)}) custom-call(bf16[2048,6144]{1,0:T(8,128)(2,1)} %refs_0_.11, bf16[2048,6144]{1,0:T(8,128)(2,1)} %refs_1_.11, bf16[6144,2048]{1,0:T(8,128)(2,1)} %refs_2_.11, ...), custom_call_target="tpu_custom_call" | custom-call | flops 1000 | bytes 1000 | tf_op jit(solution)/shard_map/forward_3/pallas_call | solution.py:80
  21.2 0.1 collective-permute-start.4
  21.3 2.5 %forward_2.1 = (bf16[768,2048]{1,0:T(8,128)(2,1)S(1)}, f32[3,48,768]{2,1,0:T(8,128)S(1)}) custom-call(bf16[2048,6144]{1,0:T(8,128)(2,1)} %refs_0_.11, bf16[2048,6144]{1,0:T(8,128)(2,1)} %refs_1_.11, bf16[6144,2048]{1,0:T(8,128)(2,1)} %refs_2_.11, bf16[48,2048]{1,0:T(8,128)(2,1)S(1)} %get-tuple-element.43.refs_3_, ...), custom_call_target="tpu_custom_call" | custom-call | flops 1000 | bytes 1000 | tf_op jit(solution)/shard_map/forward_2/pallas_call | solution.py:80
  23.8 0.0 collective-permute-done.4.arrived
  23.8 1.5 %collective-permute-start.6 = (bf16[3,48,768]{2,1,0:T(8,128)(2,1)S(1)}, bf16[3,48,768]{2,1,0:T(8,128)(2,1)S(1)}, u32[]{:S(2)}, u32[]{:S(2)}) collective-permute-start(bf16[3,48,768]{2,1,0:T(8,128)(2,1)S(1)} %join.1.refs_8_), channel_id=1, source_target_pairs={{0,2},{1,3},{2,0},{3,1},{4,6},{5,7},{6,4},{7,5},{8,10},{9,11},{10,... | collective-permute-start | bytes 663560 | tf_op jit(solution)/shard_map/ppermute | solution.py:67
  25.3 2.9 %forward_1.1 = (bf16[2048,768]{1,0:T(8,128)(2,1)S(1)}, bf16[768,2048]{1,0:T(8,128)(2,1)S(1)}, bf16[3,48,768]{2,1,0:T(8,128)(2,1)S(1)}) custom-call(bf16[2048,6144]{1,0:T(8,128)(2,1)} %refs_0_.11, bf16[2048,6144]{1,0:T(8,128)(2,1)} %refs_1_.11, bf16[6144,2048]{1,0:T(8,128)(2,1)} %refs_2_.11, bf16[48,2048]{1,0:T(8,128)(2,1)S(1)} %get-tuple-element.43.refs_3_, ...), custom_call_target="tpu_custom_call" | custom-call | flops 1000 | bytes 1000 | tf_op jit(solution)/shard_map/forward_1/pallas_call | solution.py:80
  28.2 0.3 collective-permute-start.5
  28.5 0.0 copy-start
  28.5 2.5 %forward_0.1 = (f32[3,48,768]{2,1,0:T(8,128)S(1)}, bf16[2048,768]{1,0:T(8,128)(2,1)S(1)}) custom-call(bf16[2048,6144]{1,0:T(8,128)(2,1)} %refs_0_.11, bf16[2048,6144]{1,0:T(8,128)(2,1)} %refs_1_.11, bf16[6144,2048]{1,0:T(8,128)(2,1)} %refs_2_.11, bf16[48,2048]{1,0:T(8,128)(2,1)S(1)} %get-tuple-element.43.refs_3_, ...), custom_call_target="tpu_custom_call" | custom-call | flops 1000 | bytes 1000 | tf_op jit(solution)/shard_map/forward_0/pallas_call | solution.py:80
  31.0 0.7 %collective-permute-done.6.refs_2_ = bf16[3,48,768]{2,1,0:T(8,128)(2,1)S(1)} collective-permute-done((bf16[3,48,768]{2,1,0:T(8,128)(2,1)S(1)}, bf16[3,48,768]{2,1,0:T(8,128)(2,1)S(1)}, u32[]{:S(2)}, u32[]{:S(2)}) %collective-permute-start.6) | collective-permute-done | bytes 221216 | tf_op jit(solution)/shard_map/ppermute | solution.py:67
  31.7 0.0 collective-permute-done.5.refs_1_
  31.7 0.0 copy-done
  31.7 0.4 middle.1
  32.1 1.5 %collective-permute-start.7 = (bf16[112,768]{1,0:T(8,128)(2,1)S(1)}, bf16[112,768]{1,0:T(8,128)(2,1)S(1)}, u32[]{:S(2)}, u32[]{:S(2)}) collective-permute-start(bf16[112,768]{1,0:T(8,128)(2,1)S(1)} %get-tuple-element.57.message.refs_0_), channel_id=1, source_target_pairs={{0,2},{1,3},{2,0},{3,1},{4,6},{5,7},{6,4},{7,5},{8,10},{9,11},{10,... | collective-permute-start | bytes 516104 | tf_op jit(solution)/shard_map/ppermute | solution.py:67
  33.5 0.0 collective-permute-start.8
  33.5 0.5 collective-permute-start.9
  34.0 1.7 %backward_0.1.before = f32[2048,48]{1,0:T(8,128)S(1)} custom-call(bf16[112,768]{1,0:T(8,128)(2,1)S(1)} %get-tuple-element.57.message.refs_0_, bf16[2048,768]{1,0:T(8,128)(2,1)S(1)} %get-tuple-element.56.refs_6_.gate, bf16[2048,768]{1,0:T(8,128)(2,1)S(1)} %get-tuple-element.52.refs_5_.refs_7_.up), custom_call_target="tpu_custom_call" | custom-call | flops 1000 | bytes 1000 | tf_op jit(solution)/shard_map/backward_0/pallas_call | solution.py:80
  35.8 0.0 collective-permute-done.9.d_up
  35.8 0.0 collective-permute-done.8.d_gate.refs_1_
  35.8 1.8 %backward_1.1.before = f32[2048,48]{1,0:T(8,128)S(1)} custom-call(bf16[64,768]{1,0:T(8,128)(2,1)S(1)} %collective-permute-done.8.d_gate.refs_1_, bf16[48,768]{1,0:T(8,128)(2,1)S(1)} %collective-permute-done.9.d_up, bf16[2048,768]{1,0:T(8,128)(2,1)S(1)} %get-tuple-element.45.refs_5_.refs_8_.gate, bf16[2048,768]{1,0:T(8,128)(2,1)S(1)} %get-tuple-element.46.refs_6_.refs_9_.up, ...), custom_call_target="tpu_custom_call" | custom-call | flops 1000 | bytes 1000 | tf_op jit(solution)/shard_map/backward_1/pallas_call | solution.py:80
  37.6 0.5 collective-permute-done.7.message.refs_2_
  38.0 0.0 collective-permute-start.10
  38.0 1.8 %backward_2.1.before = f32[2048,48]{1,0:T(8,128)S(1)} custom-call(bf16[112,768]{1,0:T(8,128)(2,1)S(1)} %collective-permute-done.7.message.refs_2_, bf16[2048,768]{1,0:T(8,128)(2,1)S(1)} %get-tuple-element.42.refs_8_.refs_5_.refs_10_.gate, bf16[2048,768]{1,0:T(8,128)(2,1)S(1)} %get-tuple-element.47.refs_6_.refs_11_.up, f32[2048,48]{1,0:T(8,128)S(1)} %backward_1.1.before), custom_call_target="tpu_custom_call" | custom-call | flops 1000 | bytes 1000 | tf_op jit(solution)/shard_map/backward_2/pallas_call | solution.py:80
  39.8 0.0 collective-permute-done.10.message
  39.8 1.9 %backward_3.1 = (f32[24,1024]{1,0:T(8,128)S(1)}, f32[8,128]{1,0:T(8,128)S(1)}, bf16[3,8,1152]{2,1,0:T(8,128)(2,1)S(1)}, bf16[3,8,1152]{2,1,0:T(8,128)(2,1)S(1)}, bf16[3,8,1152]{2,1,0:T(8,128)(2,1)S(1)}) custom-call(bf16[112,768]{1,0:T(8,128)(2,1)S(1)} %collective-permute-done.10.message, bf16[2048,768]{1,0:T(8,128)(2,1)S(1)} %get-tuple-element.39.refs_5_.refs_12_.gate, ...), custom_call_target="tpu_custom_call" | custom-call | flops 1000 | bytes 1000 | tf_op jit(solution)/shard_map/backward_3/pallas_call | solution.py:80
  41.7 3.4 %collective-permute-start.11 = (bf16[3,8,1152]{2,1,0:T(8,128)(2,1)S(1)}, bf16[3,8,1152]{2,1,0:T(8,128)(2,1)S(1)}, u32[]{:S(2)}, u32[]{:S(2)}) collective-permute-start(bf16[3,8,1152]{2,1,0:T(8,128)(2,1)S(1)} %get-tuple-element.65), channel_id=1, source_target_pairs={{0,12},{4,8},{8,4},{12,0},{1,13},{5,9},{9,5},{13,1},{2,14},{6,10},... | collective-permute-start | bytes 165896 | tf_op jit(solution)/shard_map/ppermute | solution.py:67
  45.2 0.0 collective-permute-start.12
  45.2 1.0 %collective-permute-start.13 = (bf16[3,8,1152]{2,1,0:T(8,128)(2,1)S(1)}, bf16[3,8,1152]{2,1,0:T(8,128)(2,1)S(1)}, u32[]{:S(2)}, u32[]{:S(2)}) collective-permute-start(bf16[3,8,1152]{2,1,0:T(8,128)(2,1)S(1)} %get-tuple-element.67), channel_id=1, source_target_pairs={{0,4},{4,0},{8,12},{12,8},{1,5},{5,1},{9,13},{13,9},{2,6},{6,2},{1... | collective-permute-start | bytes 165896 | tf_op jit(solution)/shard_map/ppermute | solution.py:67
  46.2 2.0 %collective-permute-done.11.refs_0_ = bf16[3,8,1152]{2,1,0:T(8,128)(2,1)S(1)} collective-permute-done((bf16[3,8,1152]{2,1,0:T(8,128)(2,1)S(1)}, bf16[3,8,1152]{2,1,0:T(8,128)(2,1)S(1)}, u32[]{:S(2)}, u32[]{:S(2)}) %collective-permute-start.11) | collective-permute-done | bytes 55328 | tf_op jit(solution)/shard_map/ppermute | solution.py:67
  48.2 2.1 %collective-permute-done.12.refs_1_ = bf16[3,8,1152]{2,1,0:T(8,128)(2,1)S(1)} collective-permute-done((bf16[3,8,1152]{2,1,0:T(8,128)(2,1)S(1)}, bf16[3,8,1152]{2,1,0:T(8,128)(2,1)S(1)}, u32[]{:S(2)}, u32[]{:S(2)}) %collective-permute-start.12) | collective-permute-done | bytes 55328 | tf_op jit(solution)/shard_map/ppermute | solution.py:67
  50.4 0.1 collective-permute-done.13.refs_2_
  50.5 1.3 %collective-permute-start.14 = (bf16[3,8,1024]{2,1,0:T(8,128)(2,1)S(1)}, bf16[3,8,1024]{2,1,0:T(8,128)(2,1)S(1)}, u32[]{:S(2)}, u32[]{:S(2)}) collective-permute-start(bf16[3,8,1024]{2,1,0:T(8,128)(2,1)S(1)} %get-tuple-element.70), channel_id=1, source_target_pairs={{0,16},{16,0},{1,17},{17,1},{2,18},{18,2},{3,19},{19,3},{4,20},{20... | collective-permute-start | bytes 147464 | tf_op jit(solution)/shard_map/ppermute | solution.py:67
  51.8 2.9 %collective-permute-done.14.arrived = bf16[3,8,1024]{2,1,0:T(8,128)(2,1)S(1)} collective-permute-done((bf16[3,8,1024]{2,1,0:T(8,128)(2,1)S(1)}, bf16[3,8,1024]{2,1,0:T(8,128)(2,1)S(1)}, u32[]{:S(2)}, u32[]{:S(2)}) %collective-permute-start.14) | collective-permute-done | bytes 49184 | tf_op jit(solution)/shard_map/ppermute | solution.py:67
  54.7 0.7 %last.1 = (bf16[6,2048]{1,0:T(8,128)(2,1)}, f32[4,1536]{1,0:T(4,128)}, f32[4]{0:T(128)}) custom-call(f32[16,1024]{1,0:T(8,128)S(1)} %get-tuple-element.68.own, f32[8,128]{1,0:T(8,128)S(1)} %get-tuple-element.69.own_squares, bf16[3,8,1024]{2,1,0:T(8,128)(2,1)S(1)} %collective-permute-done.14.arrived, f32[4,768]{1,0:T(4,128)S(1)} %get-tuple-element.71.grads), custom_call_target="tpu_custom_call" | custom-call | flops 1000 | bytes 1000 | tf_op jit(solution)/shard_map/last/pallas_call | solution.py:80
  (2 shorter events, 0.1 us)
Async XLA Ops:
  1.4 10.1 %copy-start.1 = (s32[24]{0:T(128)S(1)}, s32[24]{0:T(128)}, u32[]{:S(2)}) copy-start(s32[24]{0:T(128)} %refs_4_.1) | copy-start | bytes 292
  1.4 9.6 %collective-permute-start.2 = (bf16[3,8,1024]{2,1,0:T(8,128)(2,1)S(1)}, bf16[3,8,1024]{2,1,0:T(8,128)(2,1)S(1)}, u32[]{:S(2)}, u32[]{:S(2)}) collective-permute-start(bf16[3,8,1024]{2,1,0:T(8,128)(2,1)S(1)} %pack.1.refs_0_), channel_id=1, source_target_pairs={{0,12},{4,8},{8,4},{12,0},{1,13},{5,9},{9,5},{13,1},{2,14},{6,10},... | collective-permute-start | bytes 147464 | tf_op jit(solution)/shard_map/ppermute | solution.py:67
  6.6 5.0 %collective-permute-start.1 = (bf16[3,8,1024]{2,1,0:T(8,128)(2,1)S(1)}, bf16[3,8,1024]{2,1,0:T(8,128)(2,1)S(1)}, u32[]{:S(2)}, u32[]{:S(2)}) collective-permute-start(bf16[3,8,1024]{2,1,0:T(8,128)(2,1)S(1)} %pack.1.refs_0_), channel_id=1, source_target_pairs={{0,8},{4,12},{8,0},{12,4},{1,9},{5,13},{9,1},{13,5},{2,10},{6,14},... | collective-permute-start | bytes 147464 | tf_op jit(solution)/shard_map/ppermute | solution.py:67
  6.6 5.0 %collective-permute-start = (bf16[3,8,1024]{2,1,0:T(8,128)(2,1)S(1)}, bf16[3,8,1024]{2,1,0:T(8,128)(2,1)S(1)}, u32[]{:S(2)}, u32[]{:S(2)}) collective-permute-start(bf16[3,8,1024]{2,1,0:T(8,128)(2,1)S(1)} %pack.1.refs_0_), channel_id=1, source_target_pairs={{0,4},{4,0},{8,12},{12,8},{1,5},{5,1},{9,13},{13,9},{2,6},{6,2},{1... | collective-permute-start | bytes 147464 | tf_op jit(solution)/shard_map/ppermute | solution.py:67
  12.1 6.5 %collective-permute-start.3 = (bf16[13,8,1024]{2,1,0:T(8,128)(2,1)S(1)}, bf16[13,8,1024]{2,1,0:T(8,128)(2,1)S(1)}, u32[]{:S(2)}, u32[]{:S(2)}) collective-permute-start(bf16[13,8,1024]{2,1,0:T(8,128)(2,1)S(1)} %relay.1.refs_3_.refs_4_), channel_id=1, source_target_pairs={{0,16},{16,0},{1,17},{17,1},{2,18},{18,2},{3,19},{19,3},{4,20},{20... | collective-permute-start | bytes 638984 | tf_op jit(solution)/shard_map/ppermute | solution.py:67
  21.2 2.5 %collective-permute-start.4 = (f32[3,48,768]{2,1,0:T(8,128)S(1)}, f32[3,48,768]{2,1,0:T(8,128)S(1)}, u32[]{:S(2)}, u32[]{:S(2)}) collective-permute-start(f32[3,48,768]{2,1,0:T(8,128)S(1)} %get-tuple-element.51), channel_id=1, source_target_pairs={{0,1},{1,0},{2,3},{3,2},{4,5},{5,4},{6,7},{7,6},{8,9},{9,8},{10,11... | collective-permute-start | bytes 1327112 | tf_op jit(solution)/shard_map/ppermute | solution.py:67
  23.8 7.9 %collective-permute-start.6 = (bf16[3,48,768]{2,1,0:T(8,128)(2,1)S(1)}, bf16[3,48,768]{2,1,0:T(8,128)(2,1)S(1)}, u32[]{:S(2)}, u32[]{:S(2)}) collective-permute-start(bf16[3,48,768]{2,1,0:T(8,128)(2,1)S(1)} %join.1.refs_8_), channel_id=1, source_target_pairs={{0,2},{1,3},{2,0},{3,1},{4,6},{5,7},{6,4},{7,5},{8,10},{9,11},{10,... | collective-permute-start | bytes 663560 | tf_op jit(solution)/shard_map/ppermute | solution.py:67
  28.2 3.5 %collective-permute-start.5 = (bf16[3,48,768]{2,1,0:T(8,128)(2,1)S(1)}, bf16[3,48,768]{2,1,0:T(8,128)(2,1)S(1)}, u32[]{:S(2)}, u32[]{:S(2)}) collective-permute-start(bf16[3,48,768]{2,1,0:T(8,128)(2,1)S(1)} %get-tuple-element.55), channel_id=1, source_target_pairs={{0,1},{1,0},{2,3},{3,2},{4,5},{5,4},{6,7},{7,6},{8,9},{9,8},{10,11... | collective-permute-start | bytes 663560 | tf_op jit(solution)/shard_map/ppermute | solution.py:67
  28.5 3.2 %copy-start = (f32[6144]{0:T(1024)S(1)}, f32[6144]{0:T(1024)}, u32[]{:S(2)}) copy-start(f32[6144]{0:T(1024)} %param.12) | copy-start | bytes 73732
  32.1 6.0 %collective-permute-start.7 = (bf16[112,768]{1,0:T(8,128)(2,1)S(1)}, bf16[112,768]{1,0:T(8,128)(2,1)S(1)}, u32[]{:S(2)}, u32[]{:S(2)}) collective-permute-start(bf16[112,768]{1,0:T(8,128)(2,1)S(1)} %get-tuple-element.57.message.refs_0_), channel_id=1, source_target_pairs={{0,2},{1,3},{2,0},{3,1},{4,6},{5,7},{6,4},{7,5},{8,10},{9,11},{10,... | collective-permute-start | bytes 516104 | tf_op jit(solution)/shard_map/ppermute | solution.py:67
  33.5 2.3 %collective-permute-start.8 = (bf16[64,768]{1,0:T(8,128)(2,1)S(1)}, bf16[64,768]{1,0:T(8,128)(2,1)S(1)}, u32[]{:S(2)}, u32[]{:S(2)}) collective-permute-start(bf16[64,768]{1,0:T(8,128)(2,1)S(1)} %get-tuple-element.58), channel_id=1, source_target_pairs={{0,1},{1,0},{2,3},{3,2},{4,5},{5,4},{6,7},{7,6},{8,9},{9,8},{10,11... | collective-permute-start | bytes 294920 | tf_op jit(solution)/shard_map/ppermute | solution.py:67
  33.5 2.3 %collective-permute-start.9 = (bf16[48,768]{1,0:T(8,128)(2,1)S(1)}, bf16[48,768]{1,0:T(8,128)(2,1)S(1)}, u32[]{:S(2)}, u32[]{:S(2)}) collective-permute-start(bf16[48,768]{1,0:T(8,128)(2,1)S(1)} %get-tuple-element.59), channel_id=1, source_target_pairs={{0,1},{1,0},{2,3},{3,2},{4,5},{5,4},{6,7},{7,6},{8,9},{9,8},{10,11... | collective-permute-start | bytes 221192 | tf_op jit(solution)/shard_map/ppermute | solution.py:67
  38.0 1.8 %collective-permute-start.10 = (bf16[112,768]{1,0:T(8,128)(2,1)S(1)}, bf16[112,768]{1,0:T(8,128)(2,1)S(1)}, u32[]{:S(2)}, u32[]{:S(2)}) collective-permute-start(bf16[112,768]{1,0:T(8,128)(2,1)S(1)} %collective-permute-done.7.message.refs_2_), channel_id=1, source_target_pairs={{0,1},{1,0},{2,3},{3,2},{4,5},{5,4},{6,7},{7,6},{8,9},{9,8},{10,11... | collective-permute-start | bytes 516104 | tf_op jit(solution)/shard_map/ppermute | solution.py:67
  41.7 6.5 %collective-permute-start.11 = (bf16[3,8,1152]{2,1,0:T(8,128)(2,1)S(1)}, bf16[3,8,1152]{2,1,0:T(8,128)(2,1)S(1)}, u32[]{:S(2)}, u32[]{:S(2)}) collective-permute-start(bf16[3,8,1152]{2,1,0:T(8,128)(2,1)S(1)} %get-tuple-element.65), channel_id=1, source_target_pairs={{0,12},{4,8},{8,4},{12,0},{1,13},{5,9},{9,5},{13,1},{2,14},{6,10},... | collective-permute-start | bytes 165896 | tf_op jit(solution)/shard_map/ppermute | solution.py:67
  45.2 5.2 %collective-permute-start.12 = (bf16[3,8,1152]{2,1,0:T(8,128)(2,1)S(1)}, bf16[3,8,1152]{2,1,0:T(8,128)(2,1)S(1)}, u32[]{:S(2)}, u32[]{:S(2)}) collective-permute-start(bf16[3,8,1152]{2,1,0:T(8,128)(2,1)S(1)} %get-tuple-element.66), channel_id=1, source_target_pairs={{0,8},{4,12},{8,0},{12,4},{1,9},{5,13},{9,1},{13,5},{2,10},{6,14},... | collective-permute-start | bytes 165896 | tf_op jit(solution)/shard_map/ppermute | solution.py:67
  45.2 5.3 %collective-permute-start.13 = (bf16[3,8,1152]{2,1,0:T(8,128)(2,1)S(1)}, bf16[3,8,1152]{2,1,0:T(8,128)(2,1)S(1)}, u32[]{:S(2)}, u32[]{:S(2)}) collective-permute-start(bf16[3,8,1152]{2,1,0:T(8,128)(2,1)S(1)} %get-tuple-element.67), channel_id=1, source_target_pairs={{0,4},{4,0},{8,12},{12,8},{1,5},{5,1},{9,13},{13,9},{2,6},{6,2},{1... | collective-permute-start | bytes 165896 | tf_op jit(solution)/shard_map/ppermute | solution.py:67
  50.5 4.2 %collective-permute-start.14 = (bf16[3,8,1024]{2,1,0:T(8,128)(2,1)S(1)}, bf16[3,8,1024]{2,1,0:T(8,128)(2,1)S(1)}, u32[]{:S(2)}, u32[]{:S(2)}) collective-permute-start(bf16[3,8,1024]{2,1,0:T(8,128)(2,1)S(1)} %get-tuple-element.70), channel_id=1, source_target_pairs={{0,16},{16,0},{1,17},{17,1},{2,18},{18,2},{3,19},{19,3},{4,20},{20... | collective-permute-start | bytes 147464 | tf_op jit(solution)/shard_map/ppermute | solution.py:67

commit v9 on v8

--- a/solution.py
+++ b/solution.py
@@ -1,4 +1,5 @@
 import functools
+import math
 
 import jax
 import jax.numpy as jnp
@@ -64,7 +65,9 @@
 
 
 def exchange(array, axis, step):
-    return lax.ppermute(array, axis, [(i, i ^ step) for i in range(lax.axis_size(axis))])
+    axes = axis if isinstance(axis, tuple) else (axis,)
+    size = math.prod(lax.axis_size(name) for name in axes)
+    return lax.ppermute(array, axes, [(i, i ^ step) for i in range(size)])
 
 
 def held(array):
@@ -100,24 +103,29 @@
         out[k] = stage[8 * k : 8 * k + 8, :].astype(jnp.bfloat16)
 
 
-def relay_kernel(share, *refs):
-    blocks, ids, out = refs[:-3], refs[-3], refs[-1]
-    slabs = blocks[0].shape[0]
+def keys_kernel(share, ids, marks):
     position = lax.axis_index("wide")
-    for i, block in enumerate(blocks):
-        out[i * slabs : (i + 1) * slabs] = block[...]
     row = lax.broadcasted_iota(jnp.int32, (8, 128), 0)
     keys = []
-    for k in range(len(blocks) * share // 8):
+    for k in range(WIDE * share // 8):
         key = jnp.zeros((8, 128), jnp.int32)
         for r in range(8):
             block, j = divmod(8 * k + r, share)
             key = jnp.where(row == r, ids[(position ^ block) * share + j], key)
         keys.append(key.astype(jnp.float32))
-    keys.append(jnp.zeros((8, out.shape[2] - 128 * len(keys)), jnp.float32))
-    out[len(blocks) * slabs] = jnp.concatenate(keys, axis=1).astype(jnp.bfloat16)
-
-
+    keys.append(jnp.zeros((8, marks.shape[1] - 128 * len(keys)), jnp.float32))
+    marks[...] = jnp.concatenate(keys, axis=1).astype(jnp.bfloat16)
+
+
+def relay_kernel(own, far, marks, pair, marked):
+    slabs = own.shape[0]
+    for target in (pair, marked):
+        target[0:slabs] = own[...]
+        target[slabs : 2 * slabs] = far[...]
+    marked[2 * slabs] = marks[...]
+
+
+WIDE, NEXT, FAR = 4, 1, 3
 GATE, UP, DOWN = range(3)
 WHOLE_STRIP = (GATE, UP, DOWN)
 CHUNKS = 4
@@ -186,17 +194,20 @@
     out[...] = (own[...] + arrived[...]).astype(out.dtype)
 
 
-def first_kernel(share, relayed, other, gate, up, down, *refs):
+def first_kernel(share, marked, beside, other, diagonal, gate, up, down, *refs):
     tokens, cotans, part, rows, cots = refs[-5:]
     slabs, half = 4 * share // 8, rows.shape[1] // 2
-    count = (relayed.shape[0] - 1) // slabs
-    for side, source in enumerate((relayed, other)):
-        for i in range(count):
+    for source, places in (
+        (marked, (0, FAR)),
+        (beside, (NEXT, FAR ^ NEXT)),
+        (other, (WIDE, WIDE + FAR)),
+        (diagonal, (WIDE + NEXT, WIDE + (FAR ^ NEXT))),
+    ):
+        for i, place in enumerate(places):
             packed = source[i * slabs : (i + 1) * slabs].astype(jnp.float32).reshape(4 * share, half)
-            at = (side * count + i) * share
             for j, target in enumerate((rows, rows, cots, cots)):
                 span = slice((j % 2) * half, (j % 2 + 1) * half)
-                target[at : at + share, span] = packed[j * share : (j + 1) * share]
+                target[place * share : (place + 1) * share, span] = packed[j * share : (j + 1) * share]
     tokens[...] = rows[...].astype(jnp.bfloat16)
     cotans[...] = cots[...].astype(jnp.bfloat16)
     forward_kernel(tokens, cotans, gate, up, down, part)
@@ -291,7 +302,7 @@
 
 
 def backward_last_kernel(share, message, gate, up, before, *refs):
-    others, (own, own_squares), sends, (total, stage) = refs[:3], refs[3:5], refs[5:-2], refs[-2:]
+    others, other_grads, (own, own_squares), sends, (total, stage) = refs[:3], refs[3], refs[4:6], refs[6:9], refs[9:]
     tokens, features = total.shape
     side = features // 2
     for start in range(0, features, TILE):
@@ -301,48 +312,61 @@
     squares = squares[0:8] + squares[8:16]
     own_squares[...] = squares
     tails = split_high(squares)
-    wide = len(sends) + 1
-    for i, target in enumerate((own,) + tuple(sends)):
-        rows = own if i == 0 else stage
-        for group in range(2):
-            at = (group * wide + i) * share
+    slabs = 4 * share // 8
+    for target, group, nearby in zip((own,) + tuple(sends), (0, 0, 1, 1), (0, NEXT, 0, NEXT)):
+        rows = own if target is own else stage
+        for i, place in enumerate((nearby, nearby ^ FAR)):
+            at = (group * WIDE + place) * share
             for j in range(2):
-                to = (2 * group + j) * share
+                to = (2 * i + j) * share
                 rows[to : to + share, :] = total[at : at + share, j * side : (j + 1) * side]
-        if i > 0:
-            for k in range(target.shape[0]):
+        if target is not own:
+            for k in range(slabs):
                 target[k, :, 0:side] = stage[8 * k : 8 * k + 8, :].astype(jnp.bfloat16)
-                tail = tails[k] if k < 2 else jnp.zeros_like(squares)
-                target[k, :, side:] = tail.astype(jnp.bfloat16)
-
-
-def combine_kernel(share, own, own_squares, other_grads, *refs):
-    arrived, (kept_rows, kept_squares, send, total, stage) = refs[:-5], refs[-5:]
-    slabs, side = arrived[0].shape[0], own.shape[1]
-    squares = own_squares[...]
+                if target.shape[2] > side:
+                    tail = tails[k] if k < 2 else jnp.zeros_like(squares)
+                    target[k, :, side:] = tail.astype(jnp.bfloat16)
+    width = other_grads.shape[1]
+    stage[0:8, :] = jnp.zeros((8, side), jnp.float32)
+    for i, rows in enumerate(split_high(other_grads[...])):
+        stage[i * SEQS : (i + 1) * SEQS, 0:width] = rows
+    for i, rows in enumerate(tails):
+        stage[0:8, width + i * 128 : width + (i + 1) * 128] = rows
+    sends[1][slabs] = stage[0:8, :].astype(jnp.bfloat16)
+
+
+def combine_kernel(share, own, own_squares, beside, across, diagonal, *refs):
+    kept_rows, other_grads, send, total, stage = refs
+    slabs, side = beside.shape[0], own.shape[1]
+    width = other_grads.shape[1]
     for k in range(slabs):
-        rows = own[8 * k : 8 * k + 8, :]
-        for ref in arrived:
-            values = ref[k].astype(jnp.float32)
-            rows = rows + values[:, 0:side]
-            if k < 2:
-                squares = squares + values[:, side:]
+        rows = own[8 * k : 8 * k + 8, :] + across[k].astype(jnp.float32)
+        for ref in (beside, diagonal):
+            rows = rows + ref[k, :, 0:side].astype(jnp.float32)
         total[8 * k : 8 * k + 8, :] = rows
-    kept_squares[...] = squares
+    tail = across[slabs].astype(jnp.float32)
+    other_grads[...] = tail[0:SEQS, 0:width] + tail[SEQS : 2 * SEQS, 0:width]
+    same, turned = own_squares[...], tail[:, width : width + 128] + tail[:, width + 128 : width + 256]
+    for k in range(2):
+        same = same + beside[k, :, side:].astype(jnp.float32)
+        turned = turned + diagonal[k, :, side:].astype(jnp.float32)
+    squares = same[0:SEQS] + turned[SEQS : 2 * SEQS]
     count = 2 * share
+    kept_rows[...] = jnp.zeros_like(kept_rows)
+    stage[...] = jnp.zeros_like(stage)
     kept_rows[0:count, :] = total[0:count, :]
-    stage[...] = jnp.zeros_like(stage)
     stage[0:count, :] = total[count : 2 * count, :]
-    width = other_grads.shape[1]
-    for i, rows in enumerate(split_high(other_grads[...])):
-        stage[16 + i * SEQS : 16 + (i + 1) * SEQS, 0:width] = rows
-    for i, rows in enumerate(split_high(squares)):
-        stage[16:24, width + i * 128 : width + (i + 1) * 128] = rows
-    for k in range(3):
+    high, low = split_high(squares)
+    for e in range(SEQS):
+        span = slice(e * 128, (e + 1) * 128)
+        for ref in (kept_rows, stage):
+            ref[count : count + 1, span] = high[e : e + 1]
+            ref[count + 1 : count + 2, span] = low[e : e + 1]
+    for k in range(2):
         send[k] = stage[8 * k : 8 * k + 8, :].astype(jnp.bfloat16)
 
 
-def last_kernel(share, own, own_squares, arrived, grads, input_grad, example_grads, norms, stage):
+def last_kernel(share, own, arrived, grads, other_grads, input_grad, example_grads, norms, stage):
     side, width = own.shape[1], grads.shape[1]
     group = lax.axis_index("groups")
     for k in range(2):
@@ -350,14 +374,13 @@
     for j in range(2):
         rows = stage[j * share : (j + 1) * share, :]
         input_grad[:, j * side : (j + 1) * side] = rows.astype(jnp.bfloat16)
-    tail = arrived[2].astype(jnp.float32)
-    other = tail[0:SEQS, 0:width] + tail[SEQS : 2 * SEQS, 0:width]
     example_grads[:, pl.ds(pl.multiple_of(group * width, width), width)] = grads[...]
-    example_grads[:, pl.ds(pl.multiple_of((1 - group) * width, width), width)] = other
-    squares = tail[:, width : width + 128] + tail[:, width + 128 : width + 256]
-    roots = jnp.sqrt(own_squares[0:SEQS, :] + squares[SEQS : 2 * SEQS])
+    example_grads[:, pl.ds(pl.multiple_of((1 - group) * width, width), width)] = other_grads[...]
+    count = 2 * share
+    squares = stage[count : count + 1, 0 : SEQS * 128] + stage[count + 1 : count + 2, 0 : SEQS * 128]
+    roots = jnp.sqrt(squares)
     for e in range(SEQS):
-        norms[e] = jnp.max(roots[e : e + 1])
+        norms[e] = jnp.max(roots[:, e * 128 : (e + 1) * 128])
 
 
 def shared(inputs, cotangent, gate_weight, up_weight, down_weight, ia3_scale, seq_ids):
@@ -367,7 +390,7 @@
     half = share * wide
     tokens = half * groups
     f32, bf16 = jnp.float32, jnp.bfloat16
-    slabs = 4 * share // 8
+    slabs, side = 4 * share // 8, features // 2
     weights = tuple(
         pltpu.with_memory_space_constraint(weight, pltpu.HBM)
         for weight in (gate_weight, up_weight, down_weight)
@@ -391,13 +414,13 @@
         )
         kept.update(zip(pieces, arrays))
 
-    def call_loading(body, name, pieces, outs, args, scratch=()):
+    def call_loading(body, name, pieces, outs, args, scratch=(), spaces=None):
         made = call(
             loading(body, pieces, groups, (len(outs), len(outs) + len(scratch))),
             name,
             [weight_shapes[kind] for kind, _ in pieces] + outs,
             list(weights) + args,
-            {i: pltpu.HBM for i in range(3)},
+            {**{i: pltpu.HBM for i in range(3)}, **(spaces or {})},
             list(scratch) + [pltpu.SemaphoreType.DMA((len(pieces), CHUNKS))],
         )
         kept.update(zip(pieces, made))
@@ -413,31 +436,39 @@
         [pltpu.with_memory_space_constraint(array, pltpu.HBM) for array in (inputs, cotangent)],
         scratch=[pltpu.VMEM((4 * share, features // 2), f32)],
     )
-    arrived = [exchange(packed, "wide", s) for s in range(1, wide)]
-    load("load_a", [(kind, 3) for kind in WHOLE_STRIP])
-    relayed = call(
-        functools.partial(relay_kernel, share),
+    far = exchange(packed, "wide", FAR)
+    (marks,) = call_loading(
+        functools.partial(keys_kernel, share),
+        "load_a",
+        [(kind, 3) for kind in WHOLE_STRIP],
+        [pltpu.VMEM((8, side), bf16)],
+        [pltpu.with_memory_space_constraint(seq_ids, pltpu.HBM)],
+        spaces={3: pltpu.SMEM},
+    )
+    pair, marked = call(
+        relay_kernel,
         "relay",
-        pltpu.VMEM((wide * slabs + 1, 8, features // 2), bf16),
-        [packed] + arrived + [seq_ids] + hold(3, [GATE]),
-        {wide: pltpu.SMEM},
-    )
-    other_relayed = exchange(relayed, "groups", 1)
-    load("load_b", [(kind, 2) for kind in WHOLE_STRIP] + [(GATE, 1)], [relayed])
+        [pltpu.VMEM((2 * slabs, 8, side), bf16), pltpu.VMEM((2 * slabs + 1, 8, side), bf16)],
+        [packed, far, marks],
+    )
+    diagonal = exchange(pair, ("groups", "wide"), WIDE + NEXT)
+    other_marked = exchange(marked, "groups", 1)
+    beside = exchange(pair, "wide", NEXT)
+    load("load_b", [(kind, 2) for kind in WHOLE_STRIP], [pair])
 
     part = pltpu.VMEM((3, tokens, width), f32)
     near_shape = pltpu.VMEM((3, tokens, width), bf16)
     tokens_all, cotans_all, diagonal = call_loading(
         functools.partial(first_kernel, share),
         "forward_3",
-        [(UP, 1)],
+        [(GATE, 1), (DOWN, 1)],
         [pltpu.VMEM((tokens, features), bf16)] * 2 + [part],
-        [relayed, other_relayed] + hold(3) + hold(2, [GATE]),
+        [marked, beside, other_marked, diagonal] + hold(3) + hold(2, [GATE]),
         [pltpu.VMEM((tokens, features), f32)] * 2,
     )
     panel = [tokens_all, cotans_all]
     diagonal = exchange(diagonal, "narrow", 1)
-    (second,) = call_loading(forward_kernel, "forward_2", [(DOWN, 1)], [part], panel + hold(2))
+    (second,) = call_loading(forward_kernel, "forward_2", [(UP, 1)], [part], panel + hold(2))
     crossing = call(join_kernel, "join", near_shape, [held(second), diagonal])
     crossed = exchange(crossing, "narrow", 2)
     (near,) = call_loading(
@@ -464,7 +495,7 @@
             pltpu.VMEM((SEQS, width), f32),
             pltpu.VMEM((SEQS, width), f32),
         ],
-        [own_part, near, crossed, ia3_scale[None, :], relayed, other_relayed] + resident,
+        [own_part, near, crossed, ia3_scale[None, :], marked, other_marked] + resident,
         scratch=[pltpu.VMEM((groups * SEQS, width), f32)],
     )
 
@@ -476,22 +507,29 @@
     message_2, sums = lax.optimization_barrier((message_2, sums))
     message_3 = exchange(message_2, "narrow", 1)
     sums = call(backward_next_kernel, "backward_2", total, [message_2] + hold(2, [GATE, UP]) + [sums])
-    side = features // 2
     block = pltpu.VMEM((slabs, 8, side + 128), bf16)
     own, own_squares, *sends = call(
         functools.partial(backward_last_kernel, share),
         "backward_3",
-        [pltpu.VMEM((4 * share, side), f32), pltpu.VMEM((8, 128), f32)] + [block] * (wide - 1),
-        [message_3] + hold(3, [GATE, UP]) + [sums, message, near_gate, message_2],
+        [
+            pltpu.VMEM((4 * share, side), f32),
+            pltpu.VMEM((8, 128), f32),
+            block,
+            pltpu.VMEM((slabs + 1, 8, side), bf16),
+            block,
+        ],
+        [message_3] + hold(3, [GATE, UP]) + [sums, message, near_gate, message_2, other_grads],
         scratch=[pltpu.VMEM((tokens, features), f32), pltpu.VMEM((4 * share, side), f32)],
     )
-    arrived = [exchange(sends[s - 1], "wide", s) for s in reversed(range(1, wide))]
-    own, own_squares, send = call(
+    diagonal = exchange(sends[2], ("groups", "wide"), WIDE + NEXT)
+    across = exchange(sends[1], "groups", 1)
+    beside = exchange(sends[0], "wide", NEXT)
+    own, other_grads, send = call(
         functools.partial(combine_kernel, share),
         "combine",
-        [pltpu.VMEM((16, side), f32), pltpu.VMEM((8, 128), f32), pltpu.VMEM((3, 8, side), bf16)],
-        [own, own_squares, other_grads] + arrived,
-        scratch=[pltpu.VMEM((4 * share, side), f32), pltpu.VMEM((24, side), f32)],
+        [pltpu.VMEM((16, side), f32), pltpu.VMEM((SEQS, width), f32), pltpu.VMEM((2, 8, side), bf16)],
+        [own, own_squares, beside, across, diagonal],
+        scratch=[pltpu.VMEM((4 * share, side), f32), pltpu.VMEM((16, side), f32)],
     )
     input_grad, example_grads, norms = call(
         functools.partial(last_kernel, share),
@@ -501,15 +539,11 @@
             jax.ShapeDtypeStruct((SEQS, groups * width), f32),
             jax.ShapeDtypeStruct((SEQS,), f32),
         ],
-        [own, own_squares, exchange(send, "groups", 1), grads],
+        [own, exchange(send, "wide", FAR), grads, other_grads],
         scratch=[pltpu.VMEM((16, side), f32)],
         out_spaces={2: pltpu.SMEM},
     )
     return (example_grads, norms, input_grad)
-
-
-def power_of_two(number):
-    return number & (number - 1) == 0
 
 
 def local(inputs, cotangent, gate_weight, up_weight, down_weight, ia3_scale, seq_ids):
@@ -519,7 +553,7 @@
     fits = (
         groups == 2
         and narrow == 4
-        and power_of_two(wide)
+        and wide == WIDE
         and hidden % (narrow * groups * 256) == 0
         and features >= 2048
         and width <= features // 2 - 256

time: 55.6 us -> 56.2 us (1.011)
  waiting for transfers between devices: 8.75 us -> 9.41 us
  starting transfers between devices: 16.9 us -> 17.5 us
  Pallas kernels: 28.9 us -> 28.3 us
    ppermute x15, waiting for transfers between devices: 8.75 us -> 9.41 us  [exchange(): return lax.ppermute(array, axes, [(i, i ^ step) for i in range(size)])]
    pallas_call x16, Pallas kernels: 28.9 us -> 28.3 us  [call(): pl.pallas_call(body, out_shape=outs, in_specs=[pl.BlockSpec(memory_space=...]
  transfers between devices with their start and end apart: 15 -> 15, of which waited for: 7 -> 7; matrix products, arithmetic and copies ran while one was open for 0% -> 0% of each run, Pallas kernels for 40% -> 39%
where the time goes in v9:
time: 56.2 us; the launch traced here: 55.9 us
  Pallas kernels  28.3 us (50%)
  starting transfers between devices  17.5 us (31%)
  waiting for transfers between devices  9.41 us (17%)
  between operations  0.78 us (1%)
    pallas_call x16, Pallas kernels, call(): pl.pallas_call(body, out_shape=outs, in_specs=[pl.BlockSpec(memory_space=...  28.3 us
    ppermute x15, starting transfers between devices, exchange(): return lax.ppermute(array, axes, [(i, i ^ step) for i in range(size)])  17.5 us
    ppermute x15, waiting for transfers between devices, exchange(): return lax.ppermute(array, axes, [(i, i ^ step) for i in range(size)])  9.41 us
  transfers between devices with their start and end apart: 15, of which 7 were waited for; matrix products, arithmetic and copies ran while one was open for 0% of the time, Pallas kernels for 39%

profile of v9, /device:TPU:0, one launch (start us, length us, event | category | flops | bytes accessed | tf_op | source)
XLA Modules:
  0.0 55.9 jit_solution(17612387973703463512)
XLA Ops:
  0.6 0.8 %pack.1.own = bf16[3,8,1024]{2,1,0:T(8,128)(2,1)S(1)} custom-call(bf16[6,2048]{1,0:T(8,128)(2,1)} %inputs.1, bf16[6,2048]{1,0:T(8,128)(2,1)} %cotangent.1), custom_call_target="tpu_custom_call" | custom-call | flops 1000 | bytes 1000 | tf_op jit(solution)/shard_map/pack/pallas_call | solution.py:83
  1.4 5.1 %collective-permute-start = (bf16[3,8,1024]{2,1,0:T(8,128)(2,1)S(1)}, bf16[3,8,1024]{2,1,0:T(8,128)(2,1)S(1)}, u32[]{:S(2)}, u32[]{:S(2)}) collective-permute-start(bf16[3,8,1024]{2,1,0:T(8,128)(2,1)S(1)} %pack.1.own), channel_id=1, source_target_pairs={{0,12},{4,8},{8,4},{12,0},{1,13},{5,9},{9,5},{13,1},{2,14},{6,10},... | collective-permute-start | bytes 147464 | tf_op jit(solution)/shard_map/ppermute | solution.py:70
  6.5 4.5 %load_a.1 = (bf16[2048,768]{1,0:T(8,128)(2,1)S(1)}, bf16[2048,768]{1,0:T(8,128)(2,1)S(1)}, bf16[768,2048]{1,0:T(8,128)(2,1)S(1)}, bf16[8,1024]{1,0:T(8,128)(2,1)S(1)}) custom-call(bf16[2048,6144]{1,0:T(8,128)(2,1)} %refs_0_.11, bf16[2048,6144]{1,0:T(8,128)(2,1)} %refs_1_.11, bf16[6144,2048]{1,0:T(8,128)(2,1)} %refs_2_.11, s32[24]{0:T(128)} %refs_3_.1), custom_call_target="tpu_custom_call" | custom-call | flops 1000 | bytes 1000 | tf_op jit(solution)/shard_map/load_a/pallas_call | solution.py:83
  11.1 0.0 collective-permute-done.far
  11.1 1.6 %collective-permute-start.2 = (bf16[7,8,1024]{2,1,0:T(8,128)(2,1)S(1)}, bf16[7,8,1024]{2,1,0:T(8,128)(2,1)S(1)}, u32[]{:S(2)}, u32[]{:S(2)}) collective-permute-start(bf16[7,8,1024]{2,1,0:T(8,128)(2,1)S(1)} %get-tuple-element.43.refs_3_.refs_4_), channel_id=1, source_target_pairs={{0,16},{16,0},{1,17},{17,1},{2,18},{18,2},{3,19},{19,3},{4,20},{20... | collective-permute-start | bytes 344072 | tf_op jit(solution)/shard_map/ppermute | solution.py:70
  12.7 0.0 collective-permute-start.3
  12.7 2.0 %collective-permute-start.1 = (bf16[6,8,1024]{2,1,0:T(8,128)(2,1)S(1)}, bf16[6,8,1024]{2,1,0:T(8,128)(2,1)S(1)}, u32[]{:S(2)}, u32[]{:S(2)}) collective-permute-start(bf16[6,8,1024]{2,1,0:T(8,128)(2,1)S(1)} %get-tuple-element.44.refs_3_), channel_id=1, source_target_pairs={{0,4},{4,0},{8,12},{12,8},{1,5},{5,1},{9,13},{13,9},{2,6},{6,2},{1... | collective-permute-start | bytes 294920 | tf_op jit(solution)/shard_map/ppermute | solution.py:70
  14.7 3.8 %load_b.1 = (bf16[2048,768]{1,0:T(8,128)(2,1)S(1)}, bf16[2048,768]{1,0:T(8,128)(2,1)S(1)}, bf16[768,2048]{1,0:T(8,128)(2,1)S(1)}) custom-call(bf16[2048,6144]{1,0:T(8,128)(2,1)} %refs_0_.11, bf16[2048,6144]{1,0:T(8,128)(2,1)} %refs_1_.11, bf16[6144,2048]{1,0:T(8,128)(2,1)} %refs_2_.11, bf16[6,8,1024]{2,1,0:T(8,128)(2,1)S(1)} %get-tuple-element.44.refs_3_), custom_call_target="tpu_custom_call" | custom-call | flops 1000 | bytes 1000 | tf_op jit(solution)/shard_map/load_b/pallas_call | solution.py:83
  18.5 0.1 collective-permute-done.3.refs_6_
  18.6 0.1 collective-permute-done.1.refs_4_
  18.7 0.0 collective-permute-done.2.refs_5_
  18.7 2.9 %forward_3.1 = (bf16[2048,768]{1,0:T(8,128)(2,1)S(1)}, bf16[768,2048]{1,0:T(8,128)(2,1)S(1)}, bf16[48,2048]{1,0:T(8,128)(2,1)S(1)}, bf16[48,2048]{1,0:T(8,128)(2,1)S(1)}, f32[3,48,768]{2,1,0:T(8,128)S(1)}) custom-call(bf16[2048,6144]{1,0:T(8,128)(2,1)} %refs_0_.11, bf16[2048,6144]{1,0:T(8,128)(2,1)} %refs_1_.11, bf16[6144,2048]{1,0:T(8,128)(2,1)} %refs_2_.11, ...), custom_call_target="tpu_custom_call" | custom-call | flops 1000 | bytes 1000 | tf_op jit(solution)/shard_map/forward_3/pallas_call | solution.py:83
  21.6 0.1 collective-permute-start.4
  21.7 2.5 %forward_2.1 = (bf16[2048,768]{1,0:T(8,128)(2,1)S(1)}, f32[3,48,768]{2,1,0:T(8,128)S(1)}) custom-call(bf16[2048,6144]{1,0:T(8,128)(2,1)} %refs_0_.11, bf16[2048,6144]{1,0:T(8,128)(2,1)} %refs_1_.11, bf16[6144,2048]{1,0:T(8,128)(2,1)} %refs_2_.11, bf16[48,2048]{1,0:T(8,128)(2,1)S(1)} %get-tuple-element.49.refs_3_, ...), custom_call_target="tpu_custom_call" | custom-call | flops 1000 | bytes 1000 | tf_op jit(solution)/shard_map/forward_2/pallas_call | solution.py:83
  24.2 0.0 collective-permute-done.4.arrived
  24.3 1.5 %collective-permute-start.6 = (bf16[3,48,768]{2,1,0:T(8,128)(2,1)S(1)}, bf16[3,48,768]{2,1,0:T(8,128)(2,1)S(1)}, u32[]{:S(2)}, u32[]{:S(2)}) collective-permute-start(bf16[3,48,768]{2,1,0:T(8,128)(2,1)S(1)} %join.1.refs_8_), channel_id=1, source_target_pairs={{0,2},{1,3},{2,0},{3,1},{4,6},{5,7},{6,4},{7,5},{8,10},{9,11},{10,... | collective-permute-start | bytes 663560 | tf_op jit(solution)/shard_map/ppermute | solution.py:70
  25.8 2.9 %forward_1.1 = (bf16[2048,768]{1,0:T(8,128)(2,1)S(1)}, bf16[768,2048]{1,0:T(8,128)(2,1)S(1)}, bf16[3,48,768]{2,1,0:T(8,128)(2,1)S(1)}) custom-call(bf16[2048,6144]{1,0:T(8,128)(2,1)} %refs_0_.11, bf16[2048,6144]{1,0:T(8,128)(2,1)} %refs_1_.11, bf16[6144,2048]{1,0:T(8,128)(2,1)} %refs_2_.11, bf16[48,2048]{1,0:T(8,128)(2,1)S(1)} %get-tuple-element.49.refs_3_, ...), custom_call_target="tpu_custom_call" | custom-call | flops 1000 | bytes 1000 | tf_op jit(solution)/shard_map/forward_1/pallas_call | solution.py:83
  28.7 0.3 collective-permute-start.5
  29.0 0.0 copy-start
  29.0 2.6 %forward_0.1 = (f32[3,48,768]{2,1,0:T(8,128)S(1)}, bf16[2048,768]{1,0:T(8,128)(2,1)S(1)}) custom-call(bf16[2048,6144]{1,0:T(8,128)(2,1)} %refs_0_.11, bf16[2048,6144]{1,0:T(8,128)(2,1)} %refs_1_.11, bf16[6144,2048]{1,0:T(8,128)(2,1)} %refs_2_.11, bf16[48,2048]{1,0:T(8,128)(2,1)S(1)} %get-tuple-element.49.refs_3_, ...), custom_call_target="tpu_custom_call" | custom-call | flops 1000 | bytes 1000 | tf_op jit(solution)/shard_map/forward_0/pallas_call | solution.py:83
  31.5 0.6 %collective-permute-done.6.refs_2_ = bf16[3,48,768]{2,1,0:T(8,128)(2,1)S(1)} collective-permute-done((bf16[3,48,768]{2,1,0:T(8,128)(2,1)S(1)}, bf16[3,48,768]{2,1,0:T(8,128)(2,1)S(1)}, u32[]{:S(2)}, u32[]{:S(2)}) %collective-permute-start.6) | collective-permute-done | bytes 221216 | tf_op jit(solution)/shard_map/ppermute | solution.py:70
  32.1 0.0 collective-permute-done.5.refs_1_
  32.1 0.0 copy-done
  32.1 0.4 middle.1
  32.5 1.5 %collective-permute-start.7 = (bf16[112,768]{1,0:T(8,128)(2,1)S(1)}, bf16[112,768]{1,0:T(8,128)(2,1)S(1)}, u32[]{:S(2)}, u32[]{:S(2)}) collective-permute-start(bf16[112,768]{1,0:T(8,128)(2,1)S(1)} %get-tuple-element.63.message.refs_0_), channel_id=1, source_target_pairs={{0,2},{1,3},{2,0},{3,1},{4,6},{5,7},{6,4},{7,5},{8,10},{9,11},{10,... | collective-permute-start | bytes 516104 | tf_op jit(solution)/shard_map/ppermute | solution.py:70
  34.0 0.0 collective-permute-start.8
  34.0 0.5 collective-permute-start.9
  34.5 1.8 %backward_0.1.before = f32[2048,48]{1,0:T(8,128)S(1)} custom-call(bf16[112,768]{1,0:T(8,128)(2,1)S(1)} %get-tuple-element.63.message.refs_0_, bf16[2048,768]{1,0:T(8,128)(2,1)S(1)} %get-tuple-element.62.refs_6_.gate, bf16[2048,768]{1,0:T(8,128)(2,1)S(1)} %get-tuple-element.58.refs_5_.refs_7_.up), custom_call_target="tpu_custom_call" | custom-call | flops 1000 | bytes 1000 | tf_op jit(solution)/shard_map/backward_0/pallas_call | solution.py:83
  36.3 0.0 collective-permute-done.9.d_up
  36.3 0.0 collective-permute-done.8.d_gate.refs_1_
  36.3 1.8 %backward_1.1.before = f32[2048,48]{1,0:T(8,128)S(1)} custom-call(bf16[64,768]{1,0:T(8,128)(2,1)S(1)} %collective-permute-done.8.d_gate.refs_1_, bf16[48,768]{1,0:T(8,128)(2,1)S(1)} %collective-permute-done.9.d_up, bf16[2048,768]{1,0:T(8,128)(2,1)S(1)} %get-tuple-element.51.refs_5_.refs_8_.gate, bf16[2048,768]{1,0:T(8,128)(2,1)S(1)} %get-tuple-element.54.refs_6_.refs_9_.up, ...), custom_call_target="tpu_custom_call" | custom-call | flops 1000 | bytes 1000 | tf_op jit(solution)/shard_map/backward_1/pallas_call | solution.py:83
  38.1 0.4 collective-permute-done.7.message.refs_2_
  38.5 0.0 collective-permute-start.10
  38.5 1.8 %backward_2.1.before = f32[2048,48]{1,0:T(8,128)S(1)} custom-call(bf16[112,768]{1,0:T(8,128)(2,1)S(1)} %collective-permute-done.7.message.refs_2_, bf16[2048,768]{1,0:T(8,128)(2,1)S(1)} %get-tuple-element.48.refs_10_.refs_5_.gate, bf16[2048,768]{1,0:T(8,128)(2,1)S(1)} %get-tuple-element.52.refs_6_.refs_11_.up, f32[2048,48]{1,0:T(8,128)S(1)} %backward_1.1.before), custom_call_target="tpu_custom_call" | custom-call | flops 1000 | bytes 1000 | tf_op jit(solution)/shard_map/backward_2/pallas_call | solution.py:83
  40.3 0.0 collective-permute-done.10.message
  40.3 1.9 %backward_3.1 = (f32[24,1024]{1,0:T(8,128)S(1)}, f32[8,128]{1,0:T(8,128)S(1)}, bf16[3,8,1152]{2,1,0:T(8,128)(2,1)S(1)}, bf16[4,8,1024]{2,1,0:T(8,128)(2,1)S(1)}, bf16[3,8,1152]{2,1,0:T(8,128)(2,1)S(1)}) custom-call(bf16[112,768]{1,0:T(8,128)(2,1)S(1)} %collective-permute-done.10.message, bf16[2048,768]{1,0:T(8,128)(2,1)S(1)} %get-tuple-element.45.refs_7_.refs_12_.gate, ...), custom_call_target="tpu_custom_call" | custom-call | flops 1000 | bytes 1000 | tf_op jit(solution)/shard_map/backward_3/pallas_call | solution.py:83
  42.2 1.6 %collective-permute-start.12 = (bf16[4,8,1024]{2,1,0:T(8,128)(2,1)S(1)}, bf16[4,8,1024]{2,1,0:T(8,128)(2,1)S(1)}, u32[]{:S(2)}, u32[]{:S(2)}) collective-permute-start(bf16[4,8,1024]{2,1,0:T(8,128)(2,1)S(1)} %get-tuple-element.72), channel_id=1, source_target_pairs={{0,16},{16,0},{1,17},{17,1},{2,18},{18,2},{3,19},{19,3},{4,20},{20... | collective-permute-start | bytes 196616 | tf_op jit(solution)/shard_map/ppermute | solution.py:70
  43.8 0.6 %collective-permute-start.11 = (bf16[3,8,1152]{2,1,0:T(8,128)(2,1)S(1)}, bf16[3,8,1152]{2,1,0:T(8,128)(2,1)S(1)}, u32[]{:S(2)}, u32[]{:S(2)}) collective-permute-start(bf16[3,8,1152]{2,1,0:T(8,128)(2,1)S(1)} %get-tuple-element.71), channel_id=1, source_target_pairs={{0,4},{4,0},{8,12},{12,8},{1,5},{5,1},{9,13},{13,9},{2,6},{6,2},{1... | collective-permute-start | bytes 165896 | tf_op jit(solution)/shard_map/ppermute | solution.py:70
  44.4 1.4 %collective-permute-start.13 = (bf16[3,8,1152]{2,1,0:T(8,128)(2,1)S(1)}, bf16[3,8,1152]{2,1,0:T(8,128)(2,1)S(1)}, u32[]{:S(2)}, u32[]{:S(2)}) collective-permute-start(bf16[3,8,1152]{2,1,0:T(8,128)(2,1)S(1)} %get-tuple-element.73), channel_id=1, source_target_pairs={{0,20},{4,16},{8,28},{12,24},{16,4},{20,0},{24,12},{28,8},{1,21},{... | collective-permute-start | bytes 165896 | tf_op jit(solution)/shard_map/ppermute | solution.py:70
  45.8 2.6 %collective-permute-done.11.beside = bf16[3,8,1152]{2,1,0:T(8,128)(2,1)S(1)} collective-permute-done((bf16[3,8,1152]{2,1,0:T(8,128)(2,1)S(1)}, bf16[3,8,1152]{2,1,0:T(8,128)(2,1)S(1)}, u32[]{:S(2)}, u32[]{:S(2)}) %collective-permute-start.11) | collective-permute-done | bytes 55328 | tf_op jit(solution)/shard_map/ppermute | solution.py:70
  48.4 1.0 %collective-permute-done.13.diagonal = bf16[3,8,1152]{2,1,0:T(8,128)(2,1)S(1)} collective-permute-done((bf16[3,8,1152]{2,1,0:T(8,128)(2,1)S(1)}, bf16[3,8,1152]{2,1,0:T(8,128)(2,1)S(1)}, u32[]{:S(2)}, u32[]{:S(2)}) %collective-permute-start.13) | collective-permute-done | bytes 55328 | tf_op jit(solution)/shard_map/ppermute | solution.py:70
  49.5 0.0 collective-permute-done.12.across
  49.5 1.4 %collective-permute-start.14 = (bf16[2,8,1024]{2,1,0:T(8,128)(2,1)S(1)}, bf16[2,8,1024]{2,1,0:T(8,128)(2,1)S(1)}, u32[]{:S(2)}, u32[]{:S(2)}) collective-permute-start(bf16[2,8,1024]{2,1,0:T(8,128)(2,1)S(1)} %get-tuple-element.75), channel_id=1, source_target_pairs={{0,12},{4,8},{8,4},{12,0},{1,13},{5,9},{9,5},{13,1},{2,14},{6,10},... | collective-permute-start | bytes 98312 | tf_op jit(solution)/shard_map/ppermute | solution.py:70
  50.9 4.4 %collective-permute-done.14.arrived = bf16[2,8,1024]{2,1,0:T(8,128)(2,1)S(1)} collective-permute-done((bf16[2,8,1024]{2,1,0:T(8,128)(2,1)S(1)}, bf16[2,8,1024]{2,1,0:T(8,128)(2,1)S(1)}, u32[]{:S(2)}, u32[]{:S(2)}) %collective-permute-start.14) | collective-permute-done | bytes 32800 | tf_op jit(solution)/shard_map/ppermute | solution.py:70
  55.3 0.7 %last.1 = (bf16[6,2048]{1,0:T(8,128)(2,1)}, f32[4,1536]{1,0:T(4,128)}, f32[4]{0:T(128)}) custom-call(f32[16,1024]{1,0:T(8,128)S(1)} %get-tuple-element.74.own, bf16[2,8,1024]{2,1,0:T(8,128)(2,1)S(1)} %collective-permute-done.14.arrived, f32[4,768]{1,0:T(4,128)S(1)} %get-tuple-element.76.grads, f32[4,768]{1,0:T(4,128)S(1)} %get-tuple-element.77.other_grads), custom_call_target="tpu_custom_call" | custom-call | flops 1000 | bytes 1000 | tf_op jit(solution)/shard_map/last/pallas_call | solution.py:83
  (3 shorter events, 0.1 us)
Async XLA Ops:
  1.4 9.7 %collective-permute-start = (bf16[3,8,1024]{2,1,0:T(8,128)(2,1)S(1)}, bf16[3,8,1024]{2,1,0:T(8,128)(2,1)S(1)}, u32[]{:S(2)}, u32[]{:S(2)}) collective-permute-start(bf16[3,8,1024]{2,1,0:T(8,128)(2,1)S(1)} %pack.1.own), channel_id=1, source_target_pairs={{0,12},{4,8},{8,4},{12,0},{1,13},{5,9},{9,5},{13,1},{2,14},{6,10},... | collective-permute-start | bytes 147464 | tf_op jit(solution)/shard_map/ppermute | solution.py:70
  11.1 7.6 %collective-permute-start.2 = (bf16[7,8,1024]{2,1,0:T(8,128)(2,1)S(1)}, bf16[7,8,1024]{2,1,0:T(8,128)(2,1)S(1)}, u32[]{:S(2)}, u32[]{:S(2)}) collective-permute-start(bf16[7,8,1024]{2,1,0:T(8,128)(2,1)S(1)} %get-tuple-element.43.refs_3_.refs_4_), channel_id=1, source_target_pairs={{0,16},{16,0},{1,17},{17,1},{2,18},{18,2},{3,19},{19,3},{4,20},{20... | collective-permute-start | bytes 344072 | tf_op jit(solution)/shard_map/ppermute | solution.py:70
  12.7 5.9 %collective-permute-start.3 = (bf16[6,8,1024]{2,1,0:T(8,128)(2,1)S(1)}, bf16[6,8,1024]{2,1,0:T(8,128)(2,1)S(1)}, u32[]{:S(2)}, u32[]{:S(2)}) collective-permute-start(bf16[6,8,1024]{2,1,0:T(8,128)(2,1)S(1)} %get-tuple-element.44.refs_3_), channel_id=1, source_target_pairs={{0,20},{4,16},{8,28},{12,24},{16,4},{20,0},{24,12},{28,8},{1,21},{... | collective-permute-start | bytes 294920 | tf_op jit(solution)/shard_map/ppermute | solution.py:70
  12.7 6.0 %collective-permute-start.1 = (bf16[6,8,1024]{2,1,0:T(8,128)(2,1)S(1)}, bf16[6,8,1024]{2,1,0:T(8,128)(2,1)S(1)}, u32[]{:S(2)}, u32[]{:S(2)}) collective-permute-start(bf16[6,8,1024]{2,1,0:T(8,128)(2,1)S(1)} %get-tuple-element.44.refs_3_), channel_id=1, source_target_pairs={{0,4},{4,0},{8,12},{12,8},{1,5},{5,1},{9,13},{13,9},{2,6},{6,2},{1... | collective-permute-start | bytes 294920 | tf_op jit(solution)/shard_map/ppermute | solution.py:70
  21.6 2.5 %collective-permute-start.4 = (f32[3,48,768]{2,1,0:T(8,128)S(1)}, f32[3,48,768]{2,1,0:T(8,128)S(1)}, u32[]{:S(2)}, u32[]{:S(2)}) collective-permute-start(f32[3,48,768]{2,1,0:T(8,128)S(1)} %get-tuple-element.57), channel_id=1, source_target_pairs={{0,1},{1,0},{2,3},{3,2},{4,5},{5,4},{6,7},{7,6},{8,9},{9,8},{10,11... | collective-permute-start | bytes 1327112 | tf_op jit(solution)/shard_map/ppermute | solution.py:70
  24.3 7.9 %collective-permute-start.6 = (bf16[3,48,768]{2,1,0:T(8,128)(2,1)S(1)}, bf16[3,48,768]{2,1,0:T(8,128)(2,1)S(1)}, u32[]{:S(2)}, u32[]{:S(2)}) collective-permute-start(bf16[3,48,768]{2,1,0:T(8,128)(2,1)S(1)} %join.1.refs_8_), channel_id=1, source_target_pairs={{0,2},{1,3},{2,0},{3,1},{4,6},{5,7},{6,4},{7,5},{8,10},{9,11},{10,... | collective-permute-start | bytes 663560 | tf_op jit(solution)/shard_map/ppermute | solution.py:70
  28.7 3.5 %collective-permute-start.5 = (bf16[3,48,768]{2,1,0:T(8,128)(2,1)S(1)}, bf16[3,48,768]{2,1,0:T(8,128)(2,1)S(1)}, u32[]{:S(2)}, u32[]{:S(2)}) collective-permute-start(bf16[3,48,768]{2,1,0:T(8,128)(2,1)S(1)} %get-tuple-element.61), channel_id=1, source_target_pairs={{0,1},{1,0},{2,3},{3,2},{4,5},{5,4},{6,7},{7,6},{8,9},{9,8},{10,11... | collective-permute-start | bytes 663560 | tf_op jit(solution)/shard_map/ppermute | solution.py:70
  29.0 3.2 %copy-start = (f32[6144]{0:T(1024)S(1)}, f32[6144]{0:T(1024)}, u32[]{:S(2)}) copy-start(f32[6144]{0:T(1024)} %param.12) | copy-start | bytes 73732
  32.5 6.0 %collective-permute-start.7 = (bf16[112,768]{1,0:T(8,128)(2,1)S(1)}, bf16[112,768]{1,0:T(8,128)(2,1)S(1)}, u32[]{:S(2)}, u32[]{:S(2)}) collective-permute-start(bf16[112,768]{1,0:T(8,128)(2,1)S(1)} %get-tuple-element.63.message.refs_0_), channel_id=1, source_target_pairs={{0,2},{1,3},{2,0},{3,1},{4,6},{5,7},{6,4},{7,5},{8,10},{9,11},{10,... | collective-permute-start | bytes 516104 | tf_op jit(solution)/shard_map/ppermute | solution.py:70
  34.0 2.3 %collective-permute-start.8 = (bf16[64,768]{1,0:T(8,128)(2,1)S(1)}, bf16[64,768]{1,0:T(8,128)(2,1)S(1)}, u32[]{:S(2)}, u32[]{:S(2)}) collective-permute-start(bf16[64,768]{1,0:T(8,128)(2,1)S(1)} %get-tuple-element.64), channel_id=1, source_target_pairs={{0,1},{1,0},{2,3},{3,2},{4,5},{5,4},{6,7},{7,6},{8,9},{9,8},{10,11... | collective-permute-start | bytes 294920 | tf_op jit(solution)/shard_map/ppermute | solution.py:70
  34.0 2.3 %collective-permute-start.9 = (bf16[48,768]{1,0:T(8,128)(2,1)S(1)}, bf16[48,768]{1,0:T(8,128)(2,1)S(1)}, u32[]{:S(2)}, u32[]{:S(2)}) collective-permute-start(bf16[48,768]{1,0:T(8,128)(2,1)S(1)} %get-tuple-element.65), channel_id=1, source_target_pairs={{0,1},{1,0},{2,3},{3,2},{4,5},{5,4},{6,7},{7,6},{8,9},{9,8},{10,11... | collective-permute-start | bytes 221192 | tf_op jit(solution)/shard_map/ppermute | solution.py:70
  38.5 1.8 %collective-permute-start.10 = (bf16[112,768]{1,0:T(8,128)(2,1)S(1)}, bf16[112,768]{1,0:T(8,128)(2,1)S(1)}, u32[]{:S(2)}, u32[]{:S(2)}) collective-permute-start(bf16[112,768]{1,0:T(8,128)(2,1)S(1)} %collective-permute-done.7.message.refs_2_), channel_id=1, source_target_pairs={{0,1},{1,0},{2,3},{3,2},{4,5},{5,4},{6,7},{7,6},{8,9},{9,8},{10,11... | collective-permute-start | bytes 516104 | tf_op jit(solution)/shard_map/ppermute | solution.py:70
  42.2 7.2 %collective-permute-start.12 = (bf16[4,8,1024]{2,1,0:T(8,128)(2,1)S(1)}, bf16[4,8,1024]{2,1,0:T(8,128)(2,1)S(1)}, u32[]{:S(2)}, u32[]{:S(2)}) collective-permute-start(bf16[4,8,1024]{2,1,0:T(8,128)(2,1)S(1)} %get-tuple-element.72), channel_id=1, source_target_pairs={{0,16},{16,0},{1,17},{17,1},{2,18},{18,2},{3,19},{19,3},{4,20},{20... | collective-permute-start | bytes 196616 | tf_op jit(solution)/shard_map/ppermute | solution.py:70
  43.8 4.6 %collective-permute-start.11 = (bf16[3,8,1152]{2,1,0:T(8,128)(2,1)S(1)}, bf16[3,8,1152]{2,1,0:T(8,128)(2,1)S(1)}, u32[]{:S(2)}, u32[]{:S(2)}) collective-permute-start(bf16[3,8,1152]{2,1,0:T(8,128)(2,1)S(1)} %get-tuple-element.71), channel_id=1, source_target_pairs={{0,4},{4,0},{8,12},{12,8},{1,5},{5,1},{9,13},{13,9},{2,6},{6,2},{1... | collective-permute-start | bytes 165896 | tf_op jit(solution)/shard_map/ppermute | solution.py:70
  44.4 5.1 %collective-permute-start.13 = (bf16[3,8,1152]{2,1,0:T(8,128)(2,1)S(1)}, bf16[3,8,1152]{2,1,0:T(8,128)(2,1)S(1)}, u32[]{:S(2)}, u32[]{:S(2)}) collective-permute-start(bf16[3,8,1152]{2,1,0:T(8,128)(2,1)S(1)} %get-tuple-element.73), channel_id=1, source_target_pairs={{0,20},{4,16},{8,28},{12,24},{16,4},{20,0},{24,12},{28,8},{1,21},{... | collective-permute-start | bytes 165896 | tf_op jit(solution)/shard_map/ppermute | solution.py:70
  49.5 5.8 %collective-permute-start.14 = (bf16[2,8,1024]{2,1,0:T(8,128)(2,1)S(1)}, bf16[2,8,1024]{2,1,0:T(8,128)(2,1)S(1)}, u32[]{:S(2)}, u32[]{:S(2)}) collective-permute-start(bf16[2,8,1024]{2,1,0:T(8,128)(2,1)S(1)} %get-tuple-element.75), channel_id=1, source_target_pairs={{0,12},{4,8},{8,4},{12,0},{1,13},{5,9},{9,5},{13,1},{2,14},{6,10},... | collective-permute-start | bytes 98312 | tf_op jit(solution)/shard_map/ppermute | solution.py:70

commit v10 on v9

--- a/solution.py
+++ b/solution.py
@@ -163,7 +163,11 @@
         at = len(rest) - outs[1] - 1 - count
         targets, sem = rest[at : at + count], rest[at + count + outs[1]]
         copies = start_loads(pieces, groups, sources, targets, sem)
-        body(*rest[:at], *rest[at + count : at + count + outs[1]])
+
+        @pl.when(lax.axis_index("narrow") >= 0)
+        def _():
+            body(*rest[:at], *rest[at + count : at + count + outs[1]])
+
         for copy in copies:
             copy.wait()
 
@@ -335,7 +339,7 @@
     sends[1][slabs] = stage[0:8, :].astype(jnp.bfloat16)
 
 
-def combine_kernel(share, own, own_squares, beside, across, diagonal, *refs):
+def combine_kernel(share, own, own_squares, diagonal, across, beside, *refs):
     kept_rows, other_grads, send, total, stage = refs
     slabs, side = beside.shape[0], own.shape[1]
     width = other_grads.shape[1]
@@ -521,14 +525,14 @@
         [message_3] + hold(3, [GATE, UP]) + [sums, message, near_gate, message_2, other_grads],
         scratch=[pltpu.VMEM((tokens, features), f32), pltpu.VMEM((4 * share, side), f32)],
     )
-    diagonal = exchange(sends[2], ("groups", "wide"), WIDE + NEXT)
     across = exchange(sends[1], "groups", 1)
     beside = exchange(sends[0], "wide", NEXT)
+    diagonal = exchange(sends[2], ("groups", "wide"), WIDE + NEXT)
     own, other_grads, send = call(
         functools.partial(combine_kernel, share),
         "combine",
         [pltpu.VMEM((16, side), f32), pltpu.VMEM((SEQS, width), f32), pltpu.VMEM((2, 8, side), bf16)],
-        [own, own_squares, beside, across, diagonal],
+        [own, own_squares, diagonal, across, beside],
         scratch=[pltpu.VMEM((4 * share, side), f32), pltpu.VMEM((16, side), f32)],
     )
     input_grad, example_grads, norms = call(

time: 56.2 us -> 56 us (level)
  transfers between devices with their start and end apart: 15 -> 15, of which waited for: 7 -> 6; matrix products, arithmetic and copies ran while one was open for 0% -> 0% of each run, Pallas kernels for 39% -> 39%
where the time goes in v10:
time: 56 us; the launch traced here: 55.8 us
  Pallas kernels  28.2 us (50%)
  starting transfers between devices  17.3 us (31%)
  waiting for transfers between devices  9.43 us (17%)
  between operations  0.78 us (1%)
    pallas_call x16, Pallas kernels, call(): pl.pallas_call(body, out_shape=outs, in_specs=[pl.BlockSpec(memory_space=...  28.2 us
    ppermute x15, starting transfers between devices, exchange(): return lax.ppermute(array, axes, [(i, i ^ step) for i in range(size)])  17.3 us
    ppermute x15, waiting for transfers between devices, exchange(): return lax.ppermute(array, axes, [(i, i ^ step) for i in range(size)])  9.43 us
  transfers between devices with their start and end apart: 15, of which 6 were waited for; matrix products, arithmetic and copies ran while one was open for 0% of the time, Pallas kernels for 39%

profile of v10, /device:TPU:0, one launch (start us, length us, event | category | flops | bytes accessed | tf_op | source)
XLA Modules:
  0.0 55.8 jit_solution(15031833813851394717)
XLA Ops:
  0.6 0.8 %pack.1.own = bf16[3,8,1024]{2,1,0:T(8,128)(2,1)S(1)} custom-call(bf16[6,2048]{1,0:T(8,128)(2,1)} %inputs.1, bf16[6,2048]{1,0:T(8,128)(2,1)} %cotangent.1), custom_call_target="tpu_custom_call" | custom-call | flops 1000 | bytes 1000 | tf_op jit(solution)/shard_map/pack/pallas_call | solution.py:83
  1.4 5.1 %collective-permute-start = (bf16[3,8,1024]{2,1,0:T(8,128)(2,1)S(1)}, bf16[3,8,1024]{2,1,0:T(8,128)(2,1)S(1)}, u32[]{:S(2)}, u32[]{:S(2)}) collective-permute-start(bf16[3,8,1024]{2,1,0:T(8,128)(2,1)S(1)} %pack.1.own), channel_id=1, source_target_pairs={{0,12},{4,8},{8,4},{12,0},{1,13},{5,9},{9,5},{13,1},{2,14},{6,10},... | collective-permute-start | bytes 147464 | tf_op jit(solution)/shard_map/ppermute | solution.py:70
  6.5 4.5 %load_a.1 = (bf16[2048,768]{1,0:T(8,128)(2,1)S(1)}, bf16[2048,768]{1,0:T(8,128)(2,1)S(1)}, bf16[768,2048]{1,0:T(8,128)(2,1)S(1)}, bf16[8,1024]{1,0:T(8,128)(2,1)S(1)}) custom-call(bf16[2048,6144]{1,0:T(8,128)(2,1)} %refs_0_.11, bf16[2048,6144]{1,0:T(8,128)(2,1)} %refs_1_.11, bf16[6144,2048]{1,0:T(8,128)(2,1)} %refs_2_.11, s32[24]{0:T(128)} %refs_3_.1), custom_call_target="tpu_custom_call" | custom-call | flops 1000 | bytes 1000 | tf_op jit(solution)/shard_map/load_a/pallas_call | solution.py:83
  11.1 0.0 collective-permute-done.far
  11.1 1.6 %collective-permute-start.2 = (bf16[7,8,1024]{2,1,0:T(8,128)(2,1)S(1)}, bf16[7,8,1024]{2,1,0:T(8,128)(2,1)S(1)}, u32[]{:S(2)}, u32[]{:S(2)}) collective-permute-start(bf16[7,8,1024]{2,1,0:T(8,128)(2,1)S(1)} %get-tuple-element.43.refs_3_.refs_4_), channel_id=1, source_target_pairs={{0,16},{16,0},{1,17},{17,1},{2,18},{18,2},{3,19},{19,3},{4,20},{20... | collective-permute-start | bytes 344072 | tf_op jit(solution)/shard_map/ppermute | solution.py:70
  12.7 0.0 collective-permute-start.3
  12.7 2.0 %collective-permute-start.1 = (bf16[6,8,1024]{2,1,0:T(8,128)(2,1)S(1)}, bf16[6,8,1024]{2,1,0:T(8,128)(2,1)S(1)}, u32[]{:S(2)}, u32[]{:S(2)}) collective-permute-start(bf16[6,8,1024]{2,1,0:T(8,128)(2,1)S(1)} %get-tuple-element.44.refs_3_), channel_id=1, source_target_pairs={{0,4},{4,0},{8,12},{12,8},{1,5},{5,1},{9,13},{13,9},{2,6},{6,2},{1... | collective-permute-start | bytes 294920 | tf_op jit(solution)/shard_map/ppermute | solution.py:70
  14.7 3.8 %load_b.1 = (bf16[2048,768]{1,0:T(8,128)(2,1)S(1)}, bf16[2048,768]{1,0:T(8,128)(2,1)S(1)}, bf16[768,2048]{1,0:T(8,128)(2,1)S(1)}) custom-call(bf16[2048,6144]{1,0:T(8,128)(2,1)} %refs_0_.11, bf16[2048,6144]{1,0:T(8,128)(2,1)} %refs_1_.11, bf16[6144,2048]{1,0:T(8,128)(2,1)} %refs_2_.11, bf16[6,8,1024]{2,1,0:T(8,128)(2,1)S(1)} %get-tuple-element.44.refs_3_), custom_call_target="tpu_custom_call" | custom-call | flops 1000 | bytes 1000 | tf_op jit(solution)/shard_map/load_b/pallas_call | solution.py:83
  18.5 0.1 collective-permute-done.3.refs_6_
  18.6 0.1 collective-permute-done.1.refs_4_
  18.7 0.0 collective-permute-done.2.refs_5_
  18.7 2.9 %forward_3.1 = (bf16[2048,768]{1,0:T(8,128)(2,1)S(1)}, bf16[768,2048]{1,0:T(8,128)(2,1)S(1)}, bf16[48,2048]{1,0:T(8,128)(2,1)S(1)}, bf16[48,2048]{1,0:T(8,128)(2,1)S(1)}, f32[3,48,768]{2,1,0:T(8,128)S(1)}) custom-call(bf16[2048,6144]{1,0:T(8,128)(2,1)} %refs_0_.11, bf16[2048,6144]{1,0:T(8,128)(2,1)} %refs_1_.11, bf16[6144,2048]{1,0:T(8,128)(2,1)} %refs_2_.11, ...), custom_call_target="tpu_custom_call" | custom-call | flops 1000 | bytes 1000 | tf_op jit(solution)/shard_map/forward_3/pallas_call | solution.py:83
  21.6 0.1 collective-permute-start.4
  21.7 2.5 %forward_2.1 = (bf16[2048,768]{1,0:T(8,128)(2,1)S(1)}, f32[3,48,768]{2,1,0:T(8,128)S(1)}) custom-call(bf16[2048,6144]{1,0:T(8,128)(2,1)} %refs_0_.11, bf16[2048,6144]{1,0:T(8,128)(2,1)} %refs_1_.11, bf16[6144,2048]{1,0:T(8,128)(2,1)} %refs_2_.11, bf16[48,2048]{1,0:T(8,128)(2,1)S(1)} %get-tuple-element.49.refs_3_, ...), custom_call_target="tpu_custom_call" | custom-call | flops 1000 | bytes 1000 | tf_op jit(solution)/shard_map/forward_2/pallas_call | solution.py:83
  24.2 0.0 collective-permute-done.4.arrived
  24.2 1.6 %collective-permute-start.6 = (bf16[3,48,768]{2,1,0:T(8,128)(2,1)S(1)}, bf16[3,48,768]{2,1,0:T(8,128)(2,1)S(1)}, u32[]{:S(2)}, u32[]{:S(2)}) collective-permute-start(bf16[3,48,768]{2,1,0:T(8,128)(2,1)S(1)} %join.1.refs_8_), channel_id=1, source_target_pairs={{0,2},{1,3},{2,0},{3,1},{4,6},{5,7},{6,4},{7,5},{8,10},{9,11},{10,... | collective-permute-start | bytes 663560 | tf_op jit(solution)/shard_map/ppermute | solution.py:70
  25.8 2.9 %forward_1.1 = (bf16[2048,768]{1,0:T(8,128)(2,1)S(1)}, bf16[768,2048]{1,0:T(8,128)(2,1)S(1)}, bf16[3,48,768]{2,1,0:T(8,128)(2,1)S(1)}) custom-call(bf16[2048,6144]{1,0:T(8,128)(2,1)} %refs_0_.11, bf16[2048,6144]{1,0:T(8,128)(2,1)} %refs_1_.11, bf16[6144,2048]{1,0:T(8,128)(2,1)} %refs_2_.11, bf16[48,2048]{1,0:T(8,128)(2,1)S(1)} %get-tuple-element.49.refs_3_, ...), custom_call_target="tpu_custom_call" | custom-call | flops 1000 | bytes 1000 | tf_op jit(solution)/shard_map/forward_1/pallas_call | solution.py:83
  28.7 0.3 collective-permute-start.5
  28.9 0.0 copy-start
  28.9 2.5 %forward_0.1 = (f32[3,48,768]{2,1,0:T(8,128)S(1)}, bf16[2048,768]{1,0:T(8,128)(2,1)S(1)}) custom-call(bf16[2048,6144]{1,0:T(8,128)(2,1)} %refs_0_.11, bf16[2048,6144]{1,0:T(8,128)(2,1)} %refs_1_.11, bf16[6144,2048]{1,0:T(8,128)(2,1)} %refs_2_.11, bf16[48,2048]{1,0:T(8,128)(2,1)S(1)} %get-tuple-element.49.refs_3_, ...), custom_call_target="tpu_custom_call" | custom-call | flops 1000 | bytes 1000 | tf_op jit(solution)/shard_map/forward_0/pallas_call | solution.py:83
  31.5 0.6 %collective-permute-done.6.refs_2_ = bf16[3,48,768]{2,1,0:T(8,128)(2,1)S(1)} collective-permute-done((bf16[3,48,768]{2,1,0:T(8,128)(2,1)S(1)}, bf16[3,48,768]{2,1,0:T(8,128)(2,1)S(1)}, u32[]{:S(2)}, u32[]{:S(2)}) %collective-permute-start.6) | collective-permute-done | bytes 221216 | tf_op jit(solution)/shard_map/ppermute | solution.py:70
  32.1 0.0 collective-permute-done.5.refs_1_
  32.1 0.0 copy-done
  32.1 0.4 middle.1
  32.5 1.5 %collective-permute-start.7 = (bf16[112,768]{1,0:T(8,128)(2,1)S(1)}, bf16[112,768]{1,0:T(8,128)(2,1)S(1)}, u32[]{:S(2)}, u32[]{:S(2)}) collective-permute-start(bf16[112,768]{1,0:T(8,128)(2,1)S(1)} %get-tuple-element.63.message.refs_0_), channel_id=1, source_target_pairs={{0,2},{1,3},{2,0},{3,1},{4,6},{5,7},{6,4},{7,5},{8,10},{9,11},{10,... | collective-permute-start | bytes 516104 | tf_op jit(solution)/shard_map/ppermute | solution.py:70
  34.0 0.0 collective-permute-start.8
  34.0 0.5 collective-permute-start.9
  34.5 1.7 %backward_0.1.before = f32[2048,48]{1,0:T(8,128)S(1)} custom-call(bf16[112,768]{1,0:T(8,128)(2,1)S(1)} %get-tuple-element.63.message.refs_0_, bf16[2048,768]{1,0:T(8,128)(2,1)S(1)} %get-tuple-element.62.refs_6_.gate, bf16[2048,768]{1,0:T(8,128)(2,1)S(1)} %get-tuple-element.58.refs_5_.refs_7_.up), custom_call_target="tpu_custom_call" | custom-call | flops 1000 | bytes 1000 | tf_op jit(solution)/shard_map/backward_0/pallas_call | solution.py:83
  36.2 0.0 collective-permute-done.9.d_up
  36.2 0.0 collective-permute-done.8.d_gate.refs_1_
  36.2 1.8 %backward_1.1.before = f32[2048,48]{1,0:T(8,128)S(1)} custom-call(bf16[64,768]{1,0:T(8,128)(2,1)S(1)} %collective-permute-done.8.d_gate.refs_1_, bf16[48,768]{1,0:T(8,128)(2,1)S(1)} %collective-permute-done.9.d_up, bf16[2048,768]{1,0:T(8,128)(2,1)S(1)} %get-tuple-element.51.refs_5_.refs_8_.gate, bf16[2048,768]{1,0:T(8,128)(2,1)S(1)} %get-tuple-element.54.refs_6_.refs_9_.up, ...), custom_call_target="tpu_custom_call" | custom-call | flops 1000 | bytes 1000 | tf_op jit(solution)/shard_map/backward_1/pallas_call | solution.py:83
  38.0 0.4 collective-permute-done.7.message.refs_2_
  38.5 0.0 collective-permute-start.10
  38.5 1.8 %backward_2.1.before = f32[2048,48]{1,0:T(8,128)S(1)} custom-call(bf16[112,768]{1,0:T(8,128)(2,1)S(1)} %collective-permute-done.7.message.refs_2_, bf16[2048,768]{1,0:T(8,128)(2,1)S(1)} %get-tuple-element.48.refs_10_.refs_5_.gate, bf16[2048,768]{1,0:T(8,128)(2,1)S(1)} %get-tuple-element.52.refs_6_.refs_11_.up, f32[2048,48]{1,0:T(8,128)S(1)} %backward_1.1.before), custom_call_target="tpu_custom_call" | custom-call | flops 1000 | bytes 1000 | tf_op jit(solution)/shard_map/backward_2/pallas_call | solution.py:83
  40.3 0.0 collective-permute-done.10.message
  40.3 1.9 %backward_3.1 = (f32[24,1024]{1,0:T(8,128)S(1)}, f32[8,128]{1,0:T(8,128)S(1)}, bf16[3,8,1152]{2,1,0:T(8,128)(2,1)S(1)}, bf16[4,8,1024]{2,1,0:T(8,128)(2,1)S(1)}, bf16[3,8,1152]{2,1,0:T(8,128)(2,1)S(1)}) custom-call(bf16[112,768]{1,0:T(8,128)(2,1)S(1)} %collective-permute-done.10.message, bf16[2048,768]{1,0:T(8,128)(2,1)S(1)} %get-tuple-element.45.refs_7_.refs_12_.gate, ...), custom_call_target="tpu_custom_call" | custom-call | flops 1000 | bytes 1000 | tf_op jit(solution)/shard_map/backward_3/pallas_call | solution.py:83
  42.2 1.6 %collective-permute-start.12 = (bf16[4,8,1024]{2,1,0:T(8,128)(2,1)S(1)}, bf16[4,8,1024]{2,1,0:T(8,128)(2,1)S(1)}, u32[]{:S(2)}, u32[]{:S(2)}) collective-permute-start(bf16[4,8,1024]{2,1,0:T(8,128)(2,1)S(1)} %get-tuple-element.72), channel_id=1, source_target_pairs={{0,16},{16,0},{1,17},{17,1},{2,18},{18,2},{3,19},{19,3},{4,20},{20... | collective-permute-start | bytes 196616 | tf_op jit(solution)/shard_map/ppermute | solution.py:70
  43.8 0.6 %collective-permute-start.11 = (bf16[3,8,1152]{2,1,0:T(8,128)(2,1)S(1)}, bf16[3,8,1152]{2,1,0:T(8,128)(2,1)S(1)}, u32[]{:S(2)}, u32[]{:S(2)}) collective-permute-start(bf16[3,8,1152]{2,1,0:T(8,128)(2,1)S(1)} %get-tuple-element.71), channel_id=1, source_target_pairs={{0,20},{4,16},{8,28},{12,24},{16,4},{20,0},{24,12},{28,8},{1,21},{... | collective-permute-start | bytes 165896 | tf_op jit(solution)/shard_map/ppermute | solution.py:70
  44.4 1.4 %collective-permute-start.13 = (bf16[3,8,1152]{2,1,0:T(8,128)(2,1)S(1)}, bf16[3,8,1152]{2,1,0:T(8,128)(2,1)S(1)}, u32[]{:S(2)}, u32[]{:S(2)}) collective-permute-start(bf16[3,8,1152]{2,1,0:T(8,128)(2,1)S(1)} %get-tuple-element.73), channel_id=1, source_target_pairs={{0,4},{4,0},{8,12},{12,8},{1,5},{5,1},{9,13},{13,9},{2,6},{6,2},{1... | collective-permute-start | bytes 165896 | tf_op jit(solution)/shard_map/ppermute | solution.py:70
  45.8 3.5 %collective-permute-done.11.diagonal = bf16[3,8,1152]{2,1,0:T(8,128)(2,1)S(1)} collective-permute-done((bf16[3,8,1152]{2,1,0:T(8,128)(2,1)S(1)}, bf16[3,8,1152]{2,1,0:T(8,128)(2,1)S(1)}, u32[]{:S(2)}, u32[]{:S(2)}) %collective-permute-start.11) | collective-permute-done | bytes 55328 | tf_op jit(solution)/shard_map/ppermute | solution.py:70
  49.3 0.0 collective-permute-done.13.beside
  49.3 0.0 collective-permute-done.12.across
  49.3 1.2 %collective-permute-start.14 = (bf16[2,8,1024]{2,1,0:T(8,128)(2,1)S(1)}, bf16[2,8,1024]{2,1,0:T(8,128)(2,1)S(1)}, u32[]{:S(2)}, u32[]{:S(2)}) collective-permute-start(bf16[2,8,1024]{2,1,0:T(8,128)(2,1)S(1)} %get-tuple-element.75), channel_id=1, source_target_pairs={{0,12},{4,8},{8,4},{12,0},{1,13},{5,9},{9,5},{13,1},{2,14},{6,10},... | collective-permute-start | bytes 98312 | tf_op jit(solution)/shard_map/ppermute | solution.py:70
  50.6 4.6 %collective-permute-done.14.arrived = bf16[2,8,1024]{2,1,0:T(8,128)(2,1)S(1)} collective-permute-done((bf16[2,8,1024]{2,1,0:T(8,128)(2,1)S(1)}, bf16[2,8,1024]{2,1,0:T(8,128)(2,1)S(1)}, u32[]{:S(2)}, u32[]{:S(2)}) %collective-permute-start.14) | collective-permute-done | bytes 32800 | tf_op jit(solution)/shard_map/ppermute | solution.py:70
  55.1 0.7 %last.1 = (bf16[6,2048]{1,0:T(8,128)(2,1)}, f32[4,1536]{1,0:T(4,128)}, f32[4]{0:T(128)}) custom-call(f32[16,1024]{1,0:T(8,128)S(1)} %get-tuple-element.74.own, bf16[2,8,1024]{2,1,0:T(8,128)(2,1)S(1)} %collective-permute-done.14.arrived, f32[4,768]{1,0:T(4,128)S(1)} %get-tuple-element.76.grads, f32[4,768]{1,0:T(4,128)S(1)} %get-tuple-element.77.other_grads), custom_call_target="tpu_custom_call" | custom-call | flops 1000 | bytes 1000 | tf_op jit(solution)/shard_map/last/pallas_call | solution.py:83
  (3 shorter events, 0.1 us)
Async XLA Ops:
  1.4 9.7 %collective-permute-start = (bf16[3,8,1024]{2,1,0:T(8,128)(2,1)S(1)}, bf16[3,8,1024]{2,1,0:T(8,128)(2,1)S(1)}, u32[]{:S(2)}, u32[]{:S(2)}) collective-permute-start(bf16[3,8,1024]{2,1,0:T(8,128)(2,1)S(1)} %pack.1.own), channel_id=1, source_target_pairs={{0,12},{4,8},{8,4},{12,0},{1,13},{5,9},{9,5},{13,1},{2,14},{6,10},... | collective-permute-start | bytes 147464 | tf_op jit(solution)/shard_map/ppermute | solution.py:70
  11.1 7.6 %collective-permute-start.2 = (bf16[7,8,1024]{2,1,0:T(8,128)(2,1)S(1)}, bf16[7,8,1024]{2,1,0:T(8,128)(2,1)S(1)}, u32[]{:S(2)}, u32[]{:S(2)}) collective-permute-start(bf16[7,8,1024]{2,1,0:T(8,128)(2,1)S(1)} %get-tuple-element.43.refs_3_.refs_4_), channel_id=1, source_target_pairs={{0,16},{16,0},{1,17},{17,1},{2,18},{18,2},{3,19},{19,3},{4,20},{20... | collective-permute-start | bytes 344072 | tf_op jit(solution)/shard_map/ppermute | solution.py:70
  12.7 5.9 %collective-permute-start.3 = (bf16[6,8,1024]{2,1,0:T(8,128)(2,1)S(1)}, bf16[6,8,1024]{2,1,0:T(8,128)(2,1)S(1)}, u32[]{:S(2)}, u32[]{:S(2)}) collective-permute-start(bf16[6,8,1024]{2,1,0:T(8,128)(2,1)S(1)} %get-tuple-element.44.refs_3_), channel_id=1, source_target_pairs={{0,20},{4,16},{8,28},{12,24},{16,4},{20,0},{24,12},{28,8},{1,21},{... | collective-permute-start | bytes 294920 | tf_op jit(solution)/shard_map/ppermute | solution.py:70
  12.7 6.0 %collective-permute-start.1 = (bf16[6,8,1024]{2,1,0:T(8,128)(2,1)S(1)}, bf16[6,8,1024]{2,1,0:T(8,128)(2,1)S(1)}, u32[]{:S(2)}, u32[]{:S(2)}) collective-permute-start(bf16[6,8,1024]{2,1,0:T(8,128)(2,1)S(1)} %get-tuple-element.44.refs_3_), channel_id=1, source_target_pairs={{0,4},{4,0},{8,12},{12,8},{1,5},{5,1},{9,13},{13,9},{2,6},{6,2},{1... | collective-permute-start | bytes 294920 | tf_op jit(solution)/shard_map/ppermute | solution.py:70
  21.6 2.5 %collective-permute-start.4 = (f32[3,48,768]{2,1,0:T(8,128)S(1)}, f32[3,48,768]{2,1,0:T(8,128)S(1)}, u32[]{:S(2)}, u32[]{:S(2)}) collective-permute-start(f32[3,48,768]{2,1,0:T(8,128)S(1)} %get-tuple-element.57), channel_id=1, source_target_pairs={{0,1},{1,0},{2,3},{3,2},{4,5},{5,4},{6,7},{7,6},{8,9},{9,8},{10,11... | collective-permute-start | bytes 1327112 | tf_op jit(solution)/shard_map/ppermute | solution.py:70
  24.2 7.9 %collective-permute-start.6 = (bf16[3,48,768]{2,1,0:T(8,128)(2,1)S(1)}, bf16[3,48,768]{2,1,0:T(8,128)(2,1)S(1)}, u32[]{:S(2)}, u32[]{:S(2)}) collective-permute-start(bf16[3,48,768]{2,1,0:T(8,128)(2,1)S(1)} %join.1.refs_8_), channel_id=1, source_target_pairs={{0,2},{1,3},{2,0},{3,1},{4,6},{5,7},{6,4},{7,5},{8,10},{9,11},{10,... | collective-permute-start | bytes 663560 | tf_op jit(solution)/shard_map/ppermute | solution.py:70
  28.7 3.5 %collective-permute-start.5 = (bf16[3,48,768]{2,1,0:T(8,128)(2,1)S(1)}, bf16[3,48,768]{2,1,0:T(8,128)(2,1)S(1)}, u32[]{:S(2)}, u32[]{:S(2)}) collective-permute-start(bf16[3,48,768]{2,1,0:T(8,128)(2,1)S(1)} %get-tuple-element.61), channel_id=1, source_target_pairs={{0,1},{1,0},{2,3},{3,2},{4,5},{5,4},{6,7},{7,6},{8,9},{9,8},{10,11... | collective-permute-start | bytes 663560 | tf_op jit(solution)/shard_map/ppermute | solution.py:70
  28.9 3.2 %copy-start = (f32[6144]{0:T(1024)S(1)}, f32[6144]{0:T(1024)}, u32[]{:S(2)}) copy-start(f32[6144]{0:T(1024)} %param.12) | copy-start | bytes 73732
  32.5 6.0 %collective-permute-start.7 = (bf16[112,768]{1,0:T(8,128)(2,1)S(1)}, bf16[112,768]{1,0:T(8,128)(2,1)S(1)}, u32[]{:S(2)}, u32[]{:S(2)}) collective-permute-start(bf16[112,768]{1,0:T(8,128)(2,1)S(1)} %get-tuple-element.63.message.refs_0_), channel_id=1, source_target_pairs={{0,2},{1,3},{2,0},{3,1},{4,6},{5,7},{6,4},{7,5},{8,10},{9,11},{10,... | collective-permute-start | bytes 516104 | tf_op jit(solution)/shard_map/ppermute | solution.py:70
  34.0 2.3 %collective-permute-start.8 = (bf16[64,768]{1,0:T(8,128)(2,1)S(1)}, bf16[64,768]{1,0:T(8,128)(2,1)S(1)}, u32[]{:S(2)}, u32[]{:S(2)}) collective-permute-start(bf16[64,768]{1,0:T(8,128)(2,1)S(1)} %get-tuple-element.64), channel_id=1, source_target_pairs={{0,1},{1,0},{2,3},{3,2},{4,5},{5,4},{6,7},{7,6},{8,9},{9,8},{10,11... | collective-permute-start | bytes 294920 | tf_op jit(solution)/shard_map/ppermute | solution.py:70
  34.0 2.3 %collective-permute-start.9 = (bf16[48,768]{1,0:T(8,128)(2,1)S(1)}, bf16[48,768]{1,0:T(8,128)(2,1)S(1)}, u32[]{:S(2)}, u32[]{:S(2)}) collective-permute-start(bf16[48,768]{1,0:T(8,128)(2,1)S(1)} %get-tuple-element.65), channel_id=1, source_target_pairs={{0,1},{1,0},{2,3},{3,2},{4,5},{5,4},{6,7},{7,6},{8,9},{9,8},{10,11... | collective-permute-start | bytes 221192 | tf_op jit(solution)/shard_map/ppermute | solution.py:70
  38.5 1.8 %collective-permute-start.10 = (bf16[112,768]{1,0:T(8,128)(2,1)S(1)}, bf16[112,768]{1,0:T(8,128)(2,1)S(1)}, u32[]{:S(2)}, u32[]{:S(2)}) collective-permute-start(bf16[112,768]{1,0:T(8,128)(2,1)S(1)} %collective-permute-done.7.message.refs_2_), channel_id=1, source_target_pairs={{0,1},{1,0},{2,3},{3,2},{4,5},{5,4},{6,7},{7,6},{8,9},{9,8},{10,11... | collective-permute-start | bytes 516104 | tf_op jit(solution)/shard_map/ppermute | solution.py:70
  42.2 7.1 %collective-permute-start.12 = (bf16[4,8,1024]{2,1,0:T(8,128)(2,1)S(1)}, bf16[4,8,1024]{2,1,0:T(8,128)(2,1)S(1)}, u32[]{:S(2)}, u32[]{:S(2)}) collective-permute-start(bf16[4,8,1024]{2,1,0:T(8,128)(2,1)S(1)} %get-tuple-element.72), channel_id=1, source_target_pairs={{0,16},{16,0},{1,17},{17,1},{2,18},{18,2},{3,19},{19,3},{4,20},{20... | collective-permute-start | bytes 196616 | tf_op jit(solution)/shard_map/ppermute | solution.py:70
  43.8 5.5 %collective-permute-start.11 = (bf16[3,8,1152]{2,1,0:T(8,128)(2,1)S(1)}, bf16[3,8,1152]{2,1,0:T(8,128)(2,1)S(1)}, u32[]{:S(2)}, u32[]{:S(2)}) collective-permute-start(bf16[3,8,1152]{2,1,0:T(8,128)(2,1)S(1)} %get-tuple-element.71), channel_id=1, source_target_pairs={{0,20},{4,16},{8,28},{12,24},{16,4},{20,0},{24,12},{28,8},{1,21},{... | collective-permute-start | bytes 165896 | tf_op jit(solution)/shard_map/ppermute | solution.py:70
  44.4 4.9 %collective-permute-start.13 = (bf16[3,8,1152]{2,1,0:T(8,128)(2,1)S(1)}, bf16[3,8,1152]{2,1,0:T(8,128)(2,1)S(1)}, u32[]{:S(2)}, u32[]{:S(2)}) collective-permute-start(bf16[3,8,1152]{2,1,0:T(8,128)(2,1)S(1)} %get-tuple-element.73), channel_id=1, source_target_pairs={{0,4},{4,0},{8,12},{12,8},{1,5},{5,1},{9,13},{13,9},{2,6},{6,2},{1... | collective-permute-start | bytes 165896 | tf_op jit(solution)/shard_map/ppermute | solution.py:70
  49.3 5.8 %collective-permute-start.14 = (bf16[2,8,1024]{2,1,0:T(8,128)(2,1)S(1)}, bf16[2,8,1024]{2,1,0:T(8,128)(2,1)S(1)}, u32[]{:S(2)}, u32[]{:S(2)}) collective-permute-start(bf16[2,8,1024]{2,1,0:T(8,128)(2,1)S(1)} %get-tuple-element.75), channel_id=1, source_target_pairs={{0,12},{4,8},{8,4},{12,0},{1,13},{5,9},{9,5},{13,1},{2,14},{6,10},... | collective-permute-start | bytes 98312 | tf_op jit(solution)/shard_map/ppermute | solution.py:70

commit v11 on v8

--- a/solution.py
+++ b/solution.py
@@ -1,4 +1,5 @@
 import functools
+import math
 
 import jax
 import jax.numpy as jnp
@@ -64,7 +65,9 @@
 
 
 def exchange(array, axis, step):
-    return lax.ppermute(array, axis, [(i, i ^ step) for i in range(lax.axis_size(axis))])
+    axes = axis if isinstance(axis, tuple) else (axis,)
+    size = math.prod(lax.axis_size(name) for name in axes)
+    return lax.ppermute(array, axes, [(i, i ^ step) for i in range(size)])
 
 
 def held(array):
@@ -100,24 +103,35 @@
         out[k] = stage[8 * k : 8 * k + 8, :].astype(jnp.bfloat16)
 
 
-def relay_kernel(share, *refs):
-    blocks, ids, out = refs[:-3], refs[-3], refs[-1]
-    slabs = blocks[0].shape[0]
-    position = lax.axis_index("wide")
-    for i, block in enumerate(blocks):
-        out[i * slabs : (i + 1) * slabs] = block[...]
-    row = lax.broadcasted_iota(jnp.int32, (8, 128), 0)
+def fetch_ids(ids_in, marks, ids, sem):
+    return pltpu.make_async_copy(ids_in, ids, sem.at[0])
+
+
+def keys_kernel(share, ids_in, marks, ids, sem):
+    fetch_ids(ids_in, marks, ids, sem).wait()
+    position, count = lax.axis_index("wide"), ids.shape[1]
+    shape = (8, count)
+    token, row = (lax.broadcasted_iota(jnp.int32, shape, axis) for axis in (1, 0))
     keys = []
-    for k in range(len(blocks) * share // 8):
-        key = jnp.zeros((8, 128), jnp.int32)
-        for r in range(8):
-            block, j = divmod(8 * k + r, share)
-            key = jnp.where(row == r, ids[(position ^ block) * share + j], key)
-        keys.append(key.astype(jnp.float32))
-    keys.append(jnp.zeros((8, out.shape[2] - 128 * len(keys)), jnp.float32))
-    out[len(blocks) * slabs] = jnp.concatenate(keys, axis=1).astype(jnp.bfloat16)
-
-
+    for base in range(0, WIDE * share, 8):
+        at = row + base
+        block = sum((at >= share * i).astype(jnp.int32) for i in range(1, WIDE))
+        own = token == (position ^ block) * share + (at - block * share)
+        key = jnp.sum(jnp.where(own, ids[...].astype(jnp.float32), 0.0), axis=1, keepdims=True)
+        keys.append(jnp.broadcast_to(key, (8, 128)))
+    keys.append(jnp.zeros((8, marks.shape[1] - 128 * len(keys)), jnp.float32))
+    marks[...] = jnp.concatenate(keys, axis=1).astype(jnp.bfloat16)
+
+
+def relay_kernel(own, far, marks, pair, marked):
+    slabs = own.shape[0]
+    for target in (pair, marked):
+        target[0:slabs] = own[...]
+        target[slabs : 2 * slabs] = far[...]
+    marked[2 * slabs] = marks[...]
+
+
+WIDE, NEXT, FAR = 4, 1, 3
 GATE, UP, DOWN = range(3)
 WHOLE_STRIP = (GATE, UP, DOWN)
 CHUNKS = 4
@@ -147,15 +161,22 @@
         copy.wait()
 
 
-def loading(body, pieces, groups, outs):
+def loading(body, pieces, groups, outs, own_copy=None):
     count = len(pieces)
 
     def kernel(*refs):
         sources, rest = refs[:3], refs[3:]
         at = len(rest) - outs[1] - 1 - count
         targets, sem = rest[at : at + count], rest[at + count + outs[1]]
+        own = rest[:at] + rest[at + count : at + count + outs[1]]
+        if own_copy is not None:
+            own_copy(*own).start()
         copies = start_loads(pieces, groups, sources, targets, sem)
-        body(*rest[:at], *rest[at + count : at + count + outs[1]])
+
+        @pl.when(lax.axis_index("narrow") >= 0)
+        def _():
+            body(*own)
+
         for copy in copies:
             copy.wait()
 
@@ -186,17 +207,20 @@
     out[...] = (own[...] + arrived[...]).astype(out.dtype)
 
 
-def first_kernel(share, relayed, other, gate, up, down, *refs):
+def first_kernel(share, marked, beside, other, diagonal, gate, up, down, *refs):
     tokens, cotans, part, rows, cots = refs[-5:]
     slabs, half = 4 * share // 8, rows.shape[1] // 2
-    count = (relayed.shape[0] - 1) // slabs
-    for side, source in enumerate((relayed, other)):
-        for i in range(count):
+    for source, places in (
+        (marked, (0, FAR)),
+        (beside, (NEXT, FAR ^ NEXT)),
+        (other, (WIDE, WIDE + FAR)),
+        (diagonal, (WIDE + NEXT, WIDE + (FAR ^ NEXT))),
+    ):
+        for i, place in enumerate(places):
             packed = source[i * slabs : (i + 1) * slabs].astype(jnp.float32).reshape(4 * share, half)
-            at = (side * count + i) * share
             for j, target in enumerate((rows, rows, cots, cots)):
                 span = slice((j % 2) * half, (j % 2 + 1) * half)
-                target[at : at + share, span] = packed[j * share : (j + 1) * share]
+                target[place * share : (place + 1) * share, span] = packed[j * share : (j + 1) * share]
     tokens[...] = rows[...].astype(jnp.bfloat16)
     cotans[...] = cots[...].astype(jnp.bfloat16)
     forward_kernel(tokens, cotans, gate, up, down, part)
@@ -367,7 +391,7 @@
     half = share * wide
     tokens = half * groups
     f32, bf16 = jnp.float32, jnp.bfloat16
-    slabs = 4 * share // 8
+    slabs, side = 4 * share // 8, features // 2
     weights = tuple(
         pltpu.with_memory_space_constraint(weight, pltpu.HBM)
         for weight in (gate_weight, up_weight, down_weight)
@@ -391,13 +415,13 @@
         )
         kept.update(zip(pieces, arrays))
 
-    def call_loading(body, name, pieces, outs, args, scratch=()):
+    def call_loading(body, name, pieces, outs, args, scratch=(), spaces=None, own_copy=None):
         made = call(
-            loading(body, pieces, groups, (len(outs), len(outs) + len(scratch))),
+            loading(body, pieces, groups, (len(outs), len(outs) + len(scratch)), own_copy),
             name,
             [weight_shapes[kind] for kind, _ in pieces] + outs,
             list(weights) + args,
-            {i: pltpu.HBM for i in range(3)},
+            {**{i: pltpu.HBM for i in range(3)}, **(spaces or {})},
             list(scratch) + [pltpu.SemaphoreType.DMA((len(pieces), CHUNKS))],
         )
         kept.update(zip(pieces, made))
@@ -413,31 +437,41 @@
         [pltpu.with_memory_space_constraint(array, pltpu.HBM) for array in (inputs, cotangent)],
         scratch=[pltpu.VMEM((4 * share, features // 2), f32)],
     )
-    arrived = [exchange(packed, "wide", s) for s in range(1, wide)]
-    load("load_a", [(kind, 3) for kind in WHOLE_STRIP])
-    relayed = call(
-        functools.partial(relay_kernel, share),
+    far = exchange(packed, "wide", FAR)
+    (marks,) = call_loading(
+        functools.partial(keys_kernel, share),
+        "load_a",
+        [(kind, 3) for kind in WHOLE_STRIP],
+        [pltpu.VMEM((8, side), bf16)],
+        [pltpu.with_memory_space_constraint(seq_ids[None, :], pltpu.HBM)],
+        [pltpu.VMEM((1, half), jnp.int32), pltpu.SemaphoreType.DMA((1,))],
+        {3: pltpu.HBM},
+        fetch_ids,
+    )
+    pair, marked = call(
+        relay_kernel,
         "relay",
-        pltpu.VMEM((wide * slabs + 1, 8, features // 2), bf16),
-        [packed] + arrived + [seq_ids] + hold(3, [GATE]),
-        {wide: pltpu.SMEM},
-    )
-    other_relayed = exchange(relayed, "groups", 1)
-    load("load_b", [(kind, 2) for kind in WHOLE_STRIP] + [(GATE, 1)], [relayed])
+        [pltpu.VMEM((2 * slabs, 8, side), bf16), pltpu.VMEM((2 * slabs + 1, 8, side), bf16)],
+        [packed, far, marks],
+    )
+    diagonal = exchange(pair, ("groups", "wide"), WIDE + NEXT)
+    other_marked = exchange(marked, "groups", 1)
+    beside = exchange(pair, "wide", NEXT)
+    load("load_b", [(kind, 2) for kind in WHOLE_STRIP], [pair])
 
     part = pltpu.VMEM((3, tokens, width), f32)
     near_shape = pltpu.VMEM((3, tokens, width), bf16)
     tokens_all, cotans_all, diagonal = call_loading(
         functools.partial(first_kernel, share),
         "forward_3",
-        [(UP, 1)],
+        [(GATE, 1), (DOWN, 1)],
         [pltpu.VMEM((tokens, features), bf16)] * 2 + [part],
-        [relayed, other_relayed] + hold(3) + hold(2, [GATE]),
+        [marked, beside, other_marked, diagonal] + hold(3) + hold(2, [GATE]),
         [pltpu.VMEM((tokens, features), f32)] * 2,
     )
     panel = [tokens_all, cotans_all]
     diagonal = exchange(diagonal, "narrow", 1)
-    (second,) = call_loading(forward_kernel, "forward_2", [(DOWN, 1)], [part], panel + hold(2))
+    (second,) = call_loading(forward_kernel, "forward_2", [(UP, 1)], [part], panel + hold(2))
     crossing = call(join_kernel, "join", near_shape, [held(second), diagonal])
     crossed = exchange(crossing, "narrow", 2)
     (near,) = call_loading(
@@ -464,7 +498,7 @@
             pltpu.VMEM((SEQS, width), f32),
             pltpu.VMEM((SEQS, width), f32),
         ],
-        [own_part, near, crossed, ia3_scale[None, :], relayed, other_relayed] + resident,
+        [own_part, near, crossed, ia3_scale[None, :], marked, other_marked] + resident,
         scratch=[pltpu.VMEM((groups * SEQS, width), f32)],
     )
 
@@ -476,7 +510,6 @@
     message_2, sums = lax.optimization_barrier((message_2, sums))
     message_3 = exchange(message_2, "narrow", 1)
     sums = call(backward_next_kernel, "backward_2", total, [message_2] + hold(2, [GATE, UP]) + [sums])
-    side = features // 2
     block = pltpu.VMEM((slabs, 8, side + 128), bf16)
     own, own_squares, *sends = call(
         functools.partial(backward_last_kernel, share),
@@ -508,10 +541,6 @@
     return (example_grads, norms, input_grad)
 
 
-def power_of_two(number):
-    return number & (number - 1) == 0
-
-
 def local(inputs, cotangent, gate_weight, up_weight, down_weight, ia3_scale, seq_ids):
     groups, wide, narrow = lax.axis_size("groups"), lax.axis_size("wide"), lax.axis_size("narrow")
     share, (features, hidden) = inputs.shape[0], gate_weight.shape
@@ -519,7 +548,7 @@
     fits = (
         groups == 2
         and narrow == 4
-        and power_of_two(wide)
+        and wide == WIDE
         and hidden % (narrow * groups * 256) == 0
         and features >= 2048
         and width <= features // 2 - 256

time: 55.6 us -> 55.1 us (level)
  starting transfers between devices: 16.9 us -> 18.6 us
  Pallas kernels: 28.9 us -> 27.6 us
  waiting for transfers between devices: 8.75 us -> 7.96 us
    ppermute x15, starting transfers between devices: 16.9 us -> 18.6 us  [exchange(): return lax.ppermute(array, axes, [(i, i ^ step) for i in range(size)])]
    pallas_call x16, Pallas kernels: 28.9 us -> 27.6 us  [call(): pl.pallas_call(body, out_shape=outs, in_specs=[pl.BlockSpec(memory_space=...]
    ppermute x15, waiting for transfers between devices: 8.75 us -> 7.96 us  [exchange(): return lax.ppermute(array, axes, [(i, i ^ step) for i in range(size)])]
  transfers between devices with their start and end apart: 15 -> 15, of which waited for: 7 -> 7; matrix products, arithmetic and copies ran while one was open for 0% -> 0% of each run, Pallas kernels for 40% -> 38%
where the time goes in v11:
time: 55.1 us; the launch traced here: 54.9 us
  Pallas kernels  27.6 us (50%)
  starting transfers between devices  18.6 us (34%)
  waiting for transfers between devices  7.96 us (14%)
  between operations  0.78 us (1%)
    pallas_call x16, Pallas kernels, call(): pl.pallas_call(body, out_shape=outs, in_specs=[pl.BlockSpec(memory_space=...  27.6 us
    ppermute x15, starting transfers between devices, exchange(): return lax.ppermute(array, axes, [(i, i ^ step) for i in range(size)])  18.6 us
    ppermute x15, waiting for transfers between devices, exchange(): return lax.ppermute(array, axes, [(i, i ^ step) for i in range(size)])  7.96 us
  transfers between devices with their start and end apart: 15, of which 7 were waited for; matrix products, arithmetic and copies ran while one was open for 0% of the time, Pallas kernels for 38%

profile of v11, /device:TPU:0, one launch (start us, length us, event | category | flops | bytes accessed | tf_op | source)
XLA Modules:
  0.0 54.9 jit_solution(8193941489394386863)
XLA Ops:
  0.6 0.8 %pack.1.own = bf16[3,8,1024]{2,1,0:T(8,128)(2,1)S(1)} custom-call(bf16[6,2048]{1,0:T(8,128)(2,1)} %inputs.1, bf16[6,2048]{1,0:T(8,128)(2,1)} %cotangent.1), custom_call_target="tpu_custom_call" | custom-call | flops 1000 | bytes 1000 | tf_op jit(solution)/shard_map/pack/pallas_call | solution.py:83
  1.4 5.1 %collective-permute-start = (bf16[3,8,1024]{2,1,0:T(8,128)(2,1)S(1)}, bf16[3,8,1024]{2,1,0:T(8,128)(2,1)S(1)}, u32[]{:S(2)}, u32[]{:S(2)}) collective-permute-start(bf16[3,8,1024]{2,1,0:T(8,128)(2,1)S(1)} %pack.1.own), channel_id=1, source_target_pairs={{0,12},{4,8},{8,4},{12,0},{1,13},{5,9},{9,5},{13,1},{2,14},{6,10},... | collective-permute-start | bytes 147464 | tf_op jit(solution)/shard_map/ppermute | solution.py:70
  6.5 3.9 %load_a.1 = (bf16[2048,768]{1,0:T(8,128)(2,1)S(1)}, bf16[2048,768]{1,0:T(8,128)(2,1)S(1)}, bf16[768,2048]{1,0:T(8,128)(2,1)S(1)}, bf16[8,1024]{1,0:T(8,128)(2,1)S(1)}) custom-call(bf16[2048,6144]{1,0:T(8,128)(2,1)} %refs_0_.11, bf16[2048,6144]{1,0:T(8,128)(2,1)} %refs_1_.11, bf16[6144,2048]{1,0:T(8,128)(2,1)} %refs_2_.11, s32[1,24]{1,0:T(1,128)} %bitcast.3), custom_call_target="tpu_custom_call" | custom-call | flops 1000 | bytes 1000 | tf_op jit(solution)/shard_map/load_a/pallas_call | solution.py:83
  10.4 0.0 collective-permute-done.far
  10.5 1.6 %collective-permute-start.2 = (bf16[7,8,1024]{2,1,0:T(8,128)(2,1)S(1)}, bf16[7,8,1024]{2,1,0:T(8,128)(2,1)S(1)}, u32[]{:S(2)}, u32[]{:S(2)}) collective-permute-start(bf16[7,8,1024]{2,1,0:T(8,128)(2,1)S(1)} %get-tuple-element.43.refs_3_.refs_4_), channel_id=1, source_target_pairs={{0,16},{16,0},{1,17},{17,1},{2,18},{18,2},{3,19},{19,3},{4,20},{20... | collective-permute-start | bytes 344072 | tf_op jit(solution)/shard_map/ppermute | solution.py:70
  12.0 0.0 collective-permute-start.3
  12.0 2.0 %collective-permute-start.1 = (bf16[6,8,1024]{2,1,0:T(8,128)(2,1)S(1)}, bf16[6,8,1024]{2,1,0:T(8,128)(2,1)S(1)}, u32[]{:S(2)}, u32[]{:S(2)}) collective-permute-start(bf16[6,8,1024]{2,1,0:T(8,128)(2,1)S(1)} %get-tuple-element.44.refs_3_), channel_id=1, source_target_pairs={{0,4},{4,0},{8,12},{12,8},{1,5},{5,1},{9,13},{13,9},{2,6},{6,2},{1... | collective-permute-start | bytes 294920 | tf_op jit(solution)/shard_map/ppermute | solution.py:70
  14.0 3.8 %load_b.1 = (bf16[2048,768]{1,0:T(8,128)(2,1)S(1)}, bf16[2048,768]{1,0:T(8,128)(2,1)S(1)}, bf16[768,2048]{1,0:T(8,128)(2,1)S(1)}) custom-call(bf16[2048,6144]{1,0:T(8,128)(2,1)} %refs_0_.11, bf16[2048,6144]{1,0:T(8,128)(2,1)} %refs_1_.11, bf16[6144,2048]{1,0:T(8,128)(2,1)} %refs_2_.11, bf16[6,8,1024]{2,1,0:T(8,128)(2,1)S(1)} %get-tuple-element.44.refs_3_), custom_call_target="tpu_custom_call" | custom-call | flops 1000 | bytes 1000 | tf_op jit(solution)/shard_map/load_b/pallas_call | solution.py:83
  17.8 0.1 collective-permute-done.3.refs_6_
  18.0 0.1 collective-permute-done.1.refs_4_
  18.1 0.0 collective-permute-done.2.refs_5_
  18.1 2.9 %forward_3.1 = (bf16[2048,768]{1,0:T(8,128)(2,1)S(1)}, bf16[768,2048]{1,0:T(8,128)(2,1)S(1)}, bf16[48,2048]{1,0:T(8,128)(2,1)S(1)}, bf16[48,2048]{1,0:T(8,128)(2,1)S(1)}, f32[3,48,768]{2,1,0:T(8,128)S(1)}) custom-call(bf16[2048,6144]{1,0:T(8,128)(2,1)} %refs_0_.11, bf16[2048,6144]{1,0:T(8,128)(2,1)} %refs_1_.11, bf16[6144,2048]{1,0:T(8,128)(2,1)} %refs_2_.11, ...), custom_call_target="tpu_custom_call" | custom-call | flops 1000 | bytes 1000 | tf_op jit(solution)/shard_map/forward_3/pallas_call | solution.py:83
  21.0 0.1 collective-permute-start.4
  21.0 2.5 %forward_2.1 = (bf16[2048,768]{1,0:T(8,128)(2,1)S(1)}, f32[3,48,768]{2,1,0:T(8,128)S(1)}) custom-call(bf16[2048,6144]{1,0:T(8,128)(2,1)} %refs_0_.11, bf16[2048,6144]{1,0:T(8,128)(2,1)} %refs_1_.11, bf16[6144,2048]{1,0:T(8,128)(2,1)} %refs_2_.11, bf16[48,2048]{1,0:T(8,128)(2,1)S(1)} %get-tuple-element.49.refs_3_, ...), custom_call_target="tpu_custom_call" | custom-call | flops 1000 | bytes 1000 | tf_op jit(solution)/shard_map/forward_2/pallas_call | solution.py:83
  23.5 0.0 collective-permute-done.4.arrived
  23.6 1.6 %collective-permute-start.6 = (bf16[3,48,768]{2,1,0:T(8,128)(2,1)S(1)}, bf16[3,48,768]{2,1,0:T(8,128)(2,1)S(1)}, u32[]{:S(2)}, u32[]{:S(2)}) collective-permute-start(bf16[3,48,768]{2,1,0:T(8,128)(2,1)S(1)} %join.1.refs_8_), channel_id=1, source_target_pairs={{0,2},{1,3},{2,0},{3,1},{4,6},{5,7},{6,4},{7,5},{8,10},{9,11},{10,... | collective-permute-start | bytes 663560 | tf_op jit(solution)/shard_map/ppermute | solution.py:70
  25.1 2.9 %forward_1.1 = (bf16[2048,768]{1,0:T(8,128)(2,1)S(1)}, bf16[768,2048]{1,0:T(8,128)(2,1)S(1)}, bf16[3,48,768]{2,1,0:T(8,128)(2,1)S(1)}) custom-call(bf16[2048,6144]{1,0:T(8,128)(2,1)} %refs_0_.11, bf16[2048,6144]{1,0:T(8,128)(2,1)} %refs_1_.11, bf16[6144,2048]{1,0:T(8,128)(2,1)} %refs_2_.11, bf16[48,2048]{1,0:T(8,128)(2,1)S(1)} %get-tuple-element.49.refs_3_, ...), custom_call_target="tpu_custom_call" | custom-call | flops 1000 | bytes 1000 | tf_op jit(solution)/shard_map/forward_1/pallas_call | solution.py:83
  28.0 0.3 collective-permute-start.5
  28.3 0.0 copy-start
  28.3 2.5 %forward_0.1 = (f32[3,48,768]{2,1,0:T(8,128)S(1)}, bf16[2048,768]{1,0:T(8,128)(2,1)S(1)}) custom-call(bf16[2048,6144]{1,0:T(8,128)(2,1)} %refs_0_.11, bf16[2048,6144]{1,0:T(8,128)(2,1)} %refs_1_.11, bf16[6144,2048]{1,0:T(8,128)(2,1)} %refs_2_.11, bf16[48,2048]{1,0:T(8,128)(2,1)S(1)} %get-tuple-element.49.refs_3_, ...), custom_call_target="tpu_custom_call" | custom-call | flops 1000 | bytes 1000 | tf_op jit(solution)/shard_map/forward_0/pallas_call | solution.py:83
  30.8 0.6 %collective-permute-done.6.refs_2_ = bf16[3,48,768]{2,1,0:T(8,128)(2,1)S(1)} collective-permute-done((bf16[3,48,768]{2,1,0:T(8,128)(2,1)S(1)}, bf16[3,48,768]{2,1,0:T(8,128)(2,1)S(1)}, u32[]{:S(2)}, u32[]{:S(2)}) %collective-permute-start.6) | collective-permute-done | bytes 221216 | tf_op jit(solution)/shard_map/ppermute | solution.py:70
  31.4 0.0 collective-permute-done.5.refs_1_
  31.5 0.0 copy-done
  31.5 0.4 middle.1
  31.8 1.5 %collective-permute-start.7 = (bf16[112,768]{1,0:T(8,128)(2,1)S(1)}, bf16[112,768]{1,0:T(8,128)(2,1)S(1)}, u32[]{:S(2)}, u32[]{:S(2)}) collective-permute-start(bf16[112,768]{1,0:T(8,128)(2,1)S(1)} %get-tuple-element.63.message.refs_0_), channel_id=1, source_target_pairs={{0,2},{1,3},{2,0},{3,1},{4,6},{5,7},{6,4},{7,5},{8,10},{9,11},{10,... | collective-permute-start | bytes 516104 | tf_op jit(solution)/shard_map/ppermute | solution.py:70
  33.3 0.0 collective-permute-start.8
  33.3 0.5 collective-permute-start.9
  33.8 1.7 %backward_0.1.before = f32[2048,48]{1,0:T(8,128)S(1)} custom-call(bf16[112,768]{1,0:T(8,128)(2,1)S(1)} %get-tuple-element.63.message.refs_0_, bf16[2048,768]{1,0:T(8,128)(2,1)S(1)} %get-tuple-element.62.refs_6_.gate, bf16[2048,768]{1,0:T(8,128)(2,1)S(1)} %get-tuple-element.58.refs_5_.refs_7_.up), custom_call_target="tpu_custom_call" | custom-call | flops 1000 | bytes 1000 | tf_op jit(solution)/shard_map/backward_0/pallas_call | solution.py:83
  35.6 0.0 collective-permute-done.9.d_up
  35.6 0.0 collective-permute-done.8.d_gate.refs_1_
  35.6 1.8 %backward_1.1.before = f32[2048,48]{1,0:T(8,128)S(1)} custom-call(bf16[64,768]{1,0:T(8,128)(2,1)S(1)} %collective-permute-done.8.d_gate.refs_1_, bf16[48,768]{1,0:T(8,128)(2,1)S(1)} %collective-permute-done.9.d_up, bf16[2048,768]{1,0:T(8,128)(2,1)S(1)} %get-tuple-element.51.refs_5_.refs_8_.gate, bf16[2048,768]{1,0:T(8,128)(2,1)S(1)} %get-tuple-element.54.refs_6_.refs_9_.up, ...), custom_call_target="tpu_custom_call" | custom-call | flops 1000 | bytes 1000 | tf_op jit(solution)/shard_map/backward_1/pallas_call | solution.py:83
  37.4 0.4 collective-permute-done.7.message.refs_2_
  37.8 0.0 collective-permute-start.10
  37.8 1.8 %backward_2.1.before = f32[2048,48]{1,0:T(8,128)S(1)} custom-call(bf16[112,768]{1,0:T(8,128)(2,1)S(1)} %collective-permute-done.7.message.refs_2_, bf16[2048,768]{1,0:T(8,128)(2,1)S(1)} %get-tuple-element.48.refs_10_.refs_5_.gate, bf16[2048,768]{1,0:T(8,128)(2,1)S(1)} %get-tuple-element.52.refs_6_.refs_11_.up, f32[2048,48]{1,0:T(8,128)S(1)} %backward_1.1.before), custom_call_target="tpu_custom_call" | custom-call | flops 1000 | bytes 1000 | tf_op jit(solution)/shard_map/backward_2/pallas_call | solution.py:83
  39.6 0.0 collective-permute-done.10.message
  39.6 1.9 %backward_3.1 = (f32[24,1024]{1,0:T(8,128)S(1)}, f32[8,128]{1,0:T(8,128)S(1)}, bf16[3,8,1152]{2,1,0:T(8,128)(2,1)S(1)}, bf16[3,8,1152]{2,1,0:T(8,128)(2,1)S(1)}, bf16[3,8,1152]{2,1,0:T(8,128)(2,1)S(1)}) custom-call(bf16[112,768]{1,0:T(8,128)(2,1)S(1)} %collective-permute-done.10.message, bf16[2048,768]{1,0:T(8,128)(2,1)S(1)} %get-tuple-element.45.refs_7_.refs_12_.gate, ...), custom_call_target="tpu_custom_call" | custom-call | flops 1000 | bytes 1000 | tf_op jit(solution)/shard_map/backward_3/pallas_call | solution.py:83
  41.5 1.9 %collective-permute-start.11 = (bf16[3,8,1152]{2,1,0:T(8,128)(2,1)S(1)}, bf16[3,8,1152]{2,1,0:T(8,128)(2,1)S(1)}, u32[]{:S(2)}, u32[]{:S(2)}) collective-permute-start(bf16[3,8,1152]{2,1,0:T(8,128)(2,1)S(1)} %get-tuple-element.71), channel_id=1, source_target_pairs={{0,12},{4,8},{8,4},{12,0},{1,13},{5,9},{9,5},{13,1},{2,14},{6,10},... | collective-permute-start | bytes 165896 | tf_op jit(solution)/shard_map/ppermute | solution.py:70
  43.4 0.3 collective-permute-start.12
  43.7 2.3 %collective-permute-start.13 = (bf16[3,8,1152]{2,1,0:T(8,128)(2,1)S(1)}, bf16[3,8,1152]{2,1,0:T(8,128)(2,1)S(1)}, u32[]{:S(2)}, u32[]{:S(2)}) collective-permute-start(bf16[3,8,1152]{2,1,0:T(8,128)(2,1)S(1)} %get-tuple-element.73), channel_id=1, source_target_pairs={{0,4},{4,0},{8,12},{12,8},{1,5},{5,1},{9,13},{13,9},{2,6},{6,2},{1... | collective-permute-start | bytes 165896 | tf_op jit(solution)/shard_map/ppermute | solution.py:70
  46.0 2.2 %collective-permute-done.11.refs_0_ = bf16[3,8,1152]{2,1,0:T(8,128)(2,1)S(1)} collective-permute-done((bf16[3,8,1152]{2,1,0:T(8,128)(2,1)S(1)}, bf16[3,8,1152]{2,1,0:T(8,128)(2,1)S(1)}, u32[]{:S(2)}, u32[]{:S(2)}) %collective-permute-start.11) | collective-permute-done | bytes 55328 | tf_op jit(solution)/shard_map/ppermute | solution.py:70
  48.2 1.9 %collective-permute-done.12.refs_1_ = bf16[3,8,1152]{2,1,0:T(8,128)(2,1)S(1)} collective-permute-done((bf16[3,8,1152]{2,1,0:T(8,128)(2,1)S(1)}, bf16[3,8,1152]{2,1,0:T(8,128)(2,1)S(1)}, u32[]{:S(2)}, u32[]{:S(2)}) %collective-permute-start.12) | collective-permute-done | bytes 55328 | tf_op jit(solution)/shard_map/ppermute | solution.py:70
  50.1 0.0 collective-permute-done.13.refs_2_
  50.1 1.6 %collective-permute-start.14 = (bf16[3,8,1024]{2,1,0:T(8,128)(2,1)S(1)}, bf16[3,8,1024]{2,1,0:T(8,128)(2,1)S(1)}, u32[]{:S(2)}, u32[]{:S(2)}) collective-permute-start(bf16[3,8,1024]{2,1,0:T(8,128)(2,1)S(1)} %get-tuple-element.76), channel_id=1, source_target_pairs={{0,16},{16,0},{1,17},{17,1},{2,18},{18,2},{3,19},{19,3},{4,20},{20... | collective-permute-start | bytes 147464 | tf_op jit(solution)/shard_map/ppermute | solution.py:70
  51.7 2.6 %collective-permute-done.14.arrived = bf16[3,8,1024]{2,1,0:T(8,128)(2,1)S(1)} collective-permute-done((bf16[3,8,1024]{2,1,0:T(8,128)(2,1)S(1)}, bf16[3,8,1024]{2,1,0:T(8,128)(2,1)S(1)}, u32[]{:S(2)}, u32[]{:S(2)}) %collective-permute-start.14) | collective-permute-done | bytes 49184 | tf_op jit(solution)/shard_map/ppermute | solution.py:70
  54.3 0.7 %last.1 = (bf16[6,2048]{1,0:T(8,128)(2,1)}, f32[4,1536]{1,0:T(4,128)}, f32[4]{0:T(128)}) custom-call(f32[16,1024]{1,0:T(8,128)S(1)} %get-tuple-element.74.own, f32[8,128]{1,0:T(8,128)S(1)} %get-tuple-element.75.own_squares, bf16[3,8,1024]{2,1,0:T(8,128)(2,1)S(1)} %collective-permute-done.14.arrived, f32[4,768]{1,0:T(4,128)S(1)} %get-tuple-element.77.grads), custom_call_target="tpu_custom_call" | custom-call | flops 1000 | bytes 1000 | tf_op jit(solution)/shard_map/last/pallas_call | solution.py:83
  (3 shorter events, 0.1 us)
Async XLA Ops:
  1.4 9.0 %collective-permute-start = (bf16[3,8,1024]{2,1,0:T(8,128)(2,1)S(1)}, bf16[3,8,1024]{2,1,0:T(8,128)(2,1)S(1)}, u32[]{:S(2)}, u32[]{:S(2)}) collective-permute-start(bf16[3,8,1024]{2,1,0:T(8,128)(2,1)S(1)} %pack.1.own), channel_id=1, source_target_pairs={{0,12},{4,8},{8,4},{12,0},{1,13},{5,9},{9,5},{13,1},{2,14},{6,10},... | collective-permute-start | bytes 147464 | tf_op jit(solution)/shard_map/ppermute | solution.py:70
  10.5 7.6 %collective-permute-start.2 = (bf16[7,8,1024]{2,1,0:T(8,128)(2,1)S(1)}, bf16[7,8,1024]{2,1,0:T(8,128)(2,1)S(1)}, u32[]{:S(2)}, u32[]{:S(2)}) collective-permute-start(bf16[7,8,1024]{2,1,0:T(8,128)(2,1)S(1)} %get-tuple-element.43.refs_3_.refs_4_), channel_id=1, source_target_pairs={{0,16},{16,0},{1,17},{17,1},{2,18},{18,2},{3,19},{19,3},{4,20},{20... | collective-permute-start | bytes 344072 | tf_op jit(solution)/shard_map/ppermute | solution.py:70
  12.0 5.9 %collective-permute-start.3 = (bf16[6,8,1024]{2,1,0:T(8,128)(2,1)S(1)}, bf16[6,8,1024]{2,1,0:T(8,128)(2,1)S(1)}, u32[]{:S(2)}, u32[]{:S(2)}) collective-permute-start(bf16[6,8,1024]{2,1,0:T(8,128)(2,1)S(1)} %get-tuple-element.44.refs_3_), channel_id=1, source_target_pairs={{0,20},{4,16},{8,28},{12,24},{16,4},{20,0},{24,12},{28,8},{1,21},{... | collective-permute-start | bytes 294920 | tf_op jit(solution)/shard_map/ppermute | solution.py:70
  12.0 6.0 %collective-permute-start.1 = (bf16[6,8,1024]{2,1,0:T(8,128)(2,1)S(1)}, bf16[6,8,1024]{2,1,0:T(8,128)(2,1)S(1)}, u32[]{:S(2)}, u32[]{:S(2)}) collective-permute-start(bf16[6,8,1024]{2,1,0:T(8,128)(2,1)S(1)} %get-tuple-element.44.refs_3_), channel_id=1, source_target_pairs={{0,4},{4,0},{8,12},{12,8},{1,5},{5,1},{9,13},{13,9},{2,6},{6,2},{1... | collective-permute-start | bytes 294920 | tf_op jit(solution)/shard_map/ppermute | solution.py:70
  21.0 2.5 %collective-permute-start.4 = (f32[3,48,768]{2,1,0:T(8,128)S(1)}, f32[3,48,768]{2,1,0:T(8,128)S(1)}, u32[]{:S(2)}, u32[]{:S(2)}) collective-permute-start(f32[3,48,768]{2,1,0:T(8,128)S(1)} %get-tuple-element.57), channel_id=1, source_target_pairs={{0,1},{1,0},{2,3},{3,2},{4,5},{5,4},{6,7},{7,6},{8,9},{9,8},{10,11... | collective-permute-start | bytes 1327112 | tf_op jit(solution)/shard_map/ppermute | solution.py:70
  23.6 7.9 %collective-permute-start.6 = (bf16[3,48,768]{2,1,0:T(8,128)(2,1)S(1)}, bf16[3,48,768]{2,1,0:T(8,128)(2,1)S(1)}, u32[]{:S(2)}, u32[]{:S(2)}) collective-permute-start(bf16[3,48,768]{2,1,0:T(8,128)(2,1)S(1)} %join.1.refs_8_), channel_id=1, source_target_pairs={{0,2},{1,3},{2,0},{3,1},{4,6},{5,7},{6,4},{7,5},{8,10},{9,11},{10,... | collective-permute-start | bytes 663560 | tf_op jit(solution)/shard_map/ppermute | solution.py:70
  28.0 3.4 %collective-permute-start.5 = (bf16[3,48,768]{2,1,0:T(8,128)(2,1)S(1)}, bf16[3,48,768]{2,1,0:T(8,128)(2,1)S(1)}, u32[]{:S(2)}, u32[]{:S(2)}) collective-permute-start(bf16[3,48,768]{2,1,0:T(8,128)(2,1)S(1)} %get-tuple-element.61), channel_id=1, source_target_pairs={{0,1},{1,0},{2,3},{3,2},{4,5},{5,4},{6,7},{7,6},{8,9},{9,8},{10,11... | collective-permute-start | bytes 663560 | tf_op jit(solution)/shard_map/ppermute | solution.py:70
  28.3 3.2 %copy-start = (f32[6144]{0:T(1024)S(1)}, f32[6144]{0:T(1024)}, u32[]{:S(2)}) copy-start(f32[6144]{0:T(1024)} %param.12) | copy-start | bytes 73732
  31.8 6.0 %collective-permute-start.7 = (bf16[112,768]{1,0:T(8,128)(2,1)S(1)}, bf16[112,768]{1,0:T(8,128)(2,1)S(1)}, u32[]{:S(2)}, u32[]{:S(2)}) collective-permute-start(bf16[112,768]{1,0:T(8,128)(2,1)S(1)} %get-tuple-element.63.message.refs_0_), channel_id=1, source_target_pairs={{0,2},{1,3},{2,0},{3,1},{4,6},{5,7},{6,4},{7,5},{8,10},{9,11},{10,... | collective-permute-start | bytes 516104 | tf_op jit(solution)/shard_map/ppermute | solution.py:70
  33.3 2.3 %collective-permute-start.8 = (bf16[64,768]{1,0:T(8,128)(2,1)S(1)}, bf16[64,768]{1,0:T(8,128)(2,1)S(1)}, u32[]{:S(2)}, u32[]{:S(2)}) collective-permute-start(bf16[64,768]{1,0:T(8,128)(2,1)S(1)} %get-tuple-element.64), channel_id=1, source_target_pairs={{0,1},{1,0},{2,3},{3,2},{4,5},{5,4},{6,7},{7,6},{8,9},{9,8},{10,11... | collective-permute-start | bytes 294920 | tf_op jit(solution)/shard_map/ppermute | solution.py:70
  33.3 2.3 %collective-permute-start.9 = (bf16[48,768]{1,0:T(8,128)(2,1)S(1)}, bf16[48,768]{1,0:T(8,128)(2,1)S(1)}, u32[]{:S(2)}, u32[]{:S(2)}) collective-permute-start(bf16[48,768]{1,0:T(8,128)(2,1)S(1)} %get-tuple-element.65), channel_id=1, source_target_pairs={{0,1},{1,0},{2,3},{3,2},{4,5},{5,4},{6,7},{7,6},{8,9},{9,8},{10,11... | collective-permute-start | bytes 221192 | tf_op jit(solution)/shard_map/ppermute | solution.py:70
  37.8 1.8 %collective-permute-start.10 = (bf16[112,768]{1,0:T(8,128)(2,1)S(1)}, bf16[112,768]{1,0:T(8,128)(2,1)S(1)}, u32[]{:S(2)}, u32[]{:S(2)}) collective-permute-start(bf16[112,768]{1,0:T(8,128)(2,1)S(1)} %collective-permute-done.7.message.refs_2_), channel_id=1, source_target_pairs={{0,1},{1,0},{2,3},{3,2},{4,5},{5,4},{6,7},{7,6},{8,9},{9,8},{10,11... | collective-permute-start | bytes 516104 | tf_op jit(solution)/shard_map/ppermute | solution.py:70
  41.5 6.6 %collective-permute-start.11 = (bf16[3,8,1152]{2,1,0:T(8,128)(2,1)S(1)}, bf16[3,8,1152]{2,1,0:T(8,128)(2,1)S(1)}, u32[]{:S(2)}, u32[]{:S(2)}) collective-permute-start(bf16[3,8,1152]{2,1,0:T(8,128)(2,1)S(1)} %get-tuple-element.71), channel_id=1, source_target_pairs={{0,12},{4,8},{8,4},{12,0},{1,13},{5,9},{9,5},{13,1},{2,14},{6,10},... | collective-permute-start | bytes 165896 | tf_op jit(solution)/shard_map/ppermute | solution.py:70
  43.4 6.7 %collective-permute-start.12 = (bf16[3,8,1152]{2,1,0:T(8,128)(2,1)S(1)}, bf16[3,8,1152]{2,1,0:T(8,128)(2,1)S(1)}, u32[]{:S(2)}, u32[]{:S(2)}) collective-permute-start(bf16[3,8,1152]{2,1,0:T(8,128)(2,1)S(1)} %get-tuple-element.72), channel_id=1, source_target_pairs={{0,8},{4,12},{8,0},{12,4},{1,9},{5,13},{9,1},{13,5},{2,10},{6,14},... | collective-permute-start | bytes 165896 | tf_op jit(solution)/shard_map/ppermute | solution.py:70
  43.7 6.4 %collective-permute-start.13 = (bf16[3,8,1152]{2,1,0:T(8,128)(2,1)S(1)}, bf16[3,8,1152]{2,1,0:T(8,128)(2,1)S(1)}, u32[]{:S(2)}, u32[]{:S(2)}) collective-permute-start(bf16[3,8,1152]{2,1,0:T(8,128)(2,1)S(1)} %get-tuple-element.73), channel_id=1, source_target_pairs={{0,4},{4,0},{8,12},{12,8},{1,5},{5,1},{9,13},{13,9},{2,6},{6,2},{1... | collective-permute-start | bytes 165896 | tf_op jit(solution)/shard_map/ppermute | solution.py:70
  50.1 4.2 %collective-permute-start.14 = (bf16[3,8,1024]{2,1,0:T(8,128)(2,1)S(1)}, bf16[3,8,1024]{2,1,0:T(8,128)(2,1)S(1)}, u32[]{:S(2)}, u32[]{:S(2)}) collective-permute-start(bf16[3,8,1024]{2,1,0:T(8,128)(2,1)S(1)} %get-tuple-element.76), channel_id=1, source_target_pairs={{0,16},{16,0},{1,17},{17,1},{2,18},{18,2},{3,19},{19,3},{4,20},{20... | collective-permute-start | bytes 147464 | tf_op jit(solution)/shard_map/ppermute | solution.py:70

commit v12 on v11

--- a/solution.py
+++ b/solution.py
@@ -131,7 +131,7 @@
     marked[2 * slabs] = marks[...]
 
 
-WIDE, NEXT, FAR = 4, 1, 3
+WIDE, NEXT, FAR = 4, 1, 2
 GATE, UP, DOWN = range(3)
 WHOLE_STRIP = (GATE, UP, DOWN)
 CHUNKS = 4
@@ -185,10 +185,8 @@
 
 def strip_parts(tokens, cotans, gate, up, down, put):
     tile = 256
-
-    @pl.loop(0, gate.shape[1] // tile)
-    def _(i):
-        span = pl.ds(pl.multiple_of(i * tile, tile), tile)
+    for start in range(0, gate.shape[1], tile):
+        span = slice(start, start + tile)
         put(GATE, span, jnp.dot(tokens[...], gate[:, span], preferred_element_type=jnp.float32))
         put(UP, span, jnp.dot(tokens[...], up[:, span], preferred_element_type=jnp.float32))
         put(DOWN, span, contract_rows(cotans[...], down[span, :]))
@@ -230,13 +228,11 @@
     sources, (tokens, cotans, up, down) = refs[:3], refs[3:7]
     out, gate, sem = refs[-3:]
     copies = start_loads([(GATE, 0)], groups, sources, [gate], sem)
-    tile = 256
-
-    @pl.loop(0, up.shape[1] // tile)
-    def _(i):
-        span = pl.ds(pl.multiple_of(i * tile, tile), tile)
-        out[UP, :, span] = jnp.dot(tokens[...], up[:, span], preferred_element_type=jnp.float32)
-        out[DOWN, :, span] = contract_rows(cotans[...], down[span, :])
+
+    @pl.when(lax.axis_index("narrow") >= 0)
+    def _():
+        out[UP] = jnp.dot(tokens[...], up[...], preferred_element_type=jnp.float32)
+        out[DOWN] = contract_rows(cotans[...], down[...])
 
     for copy in copies:
         copy.wait()
@@ -340,8 +336,8 @@
                 target[k, :, side:] = tail.astype(jnp.bfloat16)
 
 
-def combine_kernel(share, own, own_squares, other_grads, *refs):
-    arrived, (kept_rows, kept_squares, send, total, stage) = refs[:-5], refs[-5:]
+def combine_kernel(share, own, own_squares, *refs):
+    arrived, (kept_rows, send, total, stage) = refs[:-4], refs[-4:]
     slabs, side = arrived[0].shape[0], own.shape[1]
     squares = own_squares[...]
     for k in range(slabs):
@@ -352,21 +348,20 @@
             if k < 2:
                 squares = squares + values[:, side:]
         total[8 * k : 8 * k + 8, :] = rows
-    kept_squares[...] = squares
     count = 2 * share
-    kept_rows[0:count, :] = total[0:count, :]
-    stage[...] = jnp.zeros_like(stage)
-    stage[0:count, :] = total[count : 2 * count, :]
-    width = other_grads.shape[1]
-    for i, rows in enumerate(split_high(other_grads[...])):
-        stage[16 + i * SEQS : 16 + (i + 1) * SEQS, 0:width] = rows
-    for i, rows in enumerate(split_high(squares)):
-        stage[16:24, width + i * 128 : width + (i + 1) * 128] = rows
-    for k in range(3):
+    tails = split_high(squares)
+    for group, target in enumerate((kept_rows, stage)):
+        target[...] = jnp.zeros_like(target)
+        target[0:count, :] = total[group * count : (group + 1) * count, :]
+        for i, rows in enumerate(tails):
+            for e in range(SEQS):
+                row = rows[group * SEQS + e : group * SEQS + e + 1]
+                target[count + i : count + i + 1, e * 128 : (e + 1) * 128] = row
+    for k in range(2):
         send[k] = stage[8 * k : 8 * k + 8, :].astype(jnp.bfloat16)
 
 
-def last_kernel(share, own, own_squares, arrived, grads, input_grad, example_grads, norms, stage):
+def last_kernel(share, own, arrived, grads, other_grads, input_grad, example_grads, norms, stage):
     side, width = own.shape[1], grads.shape[1]
     group = lax.axis_index("groups")
     for k in range(2):
@@ -374,14 +369,12 @@
     for j in range(2):
         rows = stage[j * share : (j + 1) * share, :]
         input_grad[:, j * side : (j + 1) * side] = rows.astype(jnp.bfloat16)
-    tail = arrived[2].astype(jnp.float32)
-    other = tail[0:SEQS, 0:width] + tail[SEQS : 2 * SEQS, 0:width]
     example_grads[:, pl.ds(pl.multiple_of(group * width, width), width)] = grads[...]
-    example_grads[:, pl.ds(pl.multiple_of((1 - group) * width, width), width)] = other
-    squares = tail[:, width : width + 128] + tail[:, width + 128 : width + 256]
-    roots = jnp.sqrt(own_squares[0:SEQS, :] + squares[SEQS : 2 * SEQS])
+    example_grads[:, pl.ds(pl.multiple_of((1 - group) * width, width), width)] = other_grads[...]
+    count = 2 * share
+    roots = jnp.sqrt(stage[count : count + 1, 0 : SEQS * 128] + stage[count + 1 : count + 2, 0 : SEQS * 128])
     for e in range(SEQS):
-        norms[e] = jnp.max(roots[e : e + 1])
+        norms[e] = jnp.max(roots[:, e * 128 : (e + 1) * 128])
 
 
 def shared(inputs, cotangent, gate_weight, up_weight, down_weight, ia3_scale, seq_ids):
@@ -519,12 +512,13 @@
         scratch=[pltpu.VMEM((tokens, features), f32), pltpu.VMEM((4 * share, side), f32)],
     )
     arrived = [exchange(sends[s - 1], "wide", s) for s in reversed(range(1, wide))]
-    own, own_squares, send = call(
+    other_grads, own_squares = lax.optimization_barrier((other_grads, own_squares))
+    own, send = call(
         functools.partial(combine_kernel, share),
         "combine",
-        [pltpu.VMEM((16, side), f32), pltpu.VMEM((8, 128), f32), pltpu.VMEM((3, 8, side), bf16)],
-        [own, own_squares, other_grads] + arrived,
-        scratch=[pltpu.VMEM((4 * share, side), f32), pltpu.VMEM((24, side), f32)],
+        [pltpu.VMEM((16, side), f32), pltpu.VMEM((2, 8, side), bf16)],
+        [own, own_squares] + arrived,
+        scratch=[pltpu.VMEM((4 * share, side), f32), pltpu.VMEM((16, side), f32)],
     )
     input_grad, example_grads, norms = call(
         functools.partial(last_kernel, share),
@@ -534,7 +528,7 @@
             jax.ShapeDtypeStruct((SEQS, groups * width), f32),
             jax.ShapeDtypeStruct((SEQS,), f32),
         ],
-        [own, own_squares, exchange(send, "groups", 1), grads],
+        [own, exchange(send, "groups", 1), grads, exchange(other_grads, "groups", 1)],
         scratch=[pltpu.VMEM((16, side), f32)],
         out_spaces={2: pltpu.SMEM},
     )

time: 55.1 us -> 55.4 us (level)
  waiting for transfers between devices: 7.96 us -> 8.96 us
    ppermute x15 -> x16, waiting for transfers between devices: 7.96 us -> 8.96 us  [exchange(): return lax.ppermute(array, axes, [(i, i ^ step) for i in range(size)])]
    ppermute x15 -> x16, starting transfers between devices: 18.6 us -> 18.1 us  [exchange(): return lax.ppermute(array, axes, [(i, i ^ step) for i in range(size)])]
  transfers between devices with their start and end apart: 15 -> 16, of which waited for: 7 -> 7; matrix products, arithmetic and copies ran while one was open for 0% -> 0% of each run, Pallas kernels for 38% -> 37%
where the time goes in v12:
time: 55.4 us; the launch traced here: 55.2 us
  Pallas kernels  27.2 us (49%)
  starting transfers between devices  18.1 us (33%)
  waiting for transfers between devices  8.96 us (16%)
  between operations  0.94 us (2%)
    pallas_call x16, Pallas kernels, call(): pl.pallas_call(body, out_shape=outs, in_specs=[pl.BlockSpec(memory_space=...  27.2 us
    ppermute x16, starting transfers between devices, exchange(): return lax.ppermute(array, axes, [(i, i ^ step) for i in range(size)])  18.1 us
    ppermute x16, waiting for transfers between devices, exchange(): return lax.ppermute(array, axes, [(i, i ^ step) for i in range(size)])  8.96 us
  transfers between devices with their start and end apart: 16, of which 7 were waited for; matrix products, arithmetic and copies ran while one was open for 0% of the time, Pallas kernels for 37%

profile of v12, /device:TPU:0, one launch (start us, length us, event | category | flops | bytes accessed | tf_op | source)
XLA Modules:
  0.0 55.2 jit_solution(13022698884415426204)
XLA Ops:
  0.6 0.8 %pack.1.own = bf16[3,8,1024]{2,1,0:T(8,128)(2,1)S(1)} custom-call(bf16[6,2048]{1,0:T(8,128)(2,1)} %inputs.1, bf16[6,2048]{1,0:T(8,128)(2,1)} %cotangent.1), custom_call_target="tpu_custom_call" | custom-call | flops 1000 | bytes 1000 | tf_op jit(solution)/shard_map/pack/pallas_call | solution.py:83
  1.4 4.1 %collective-permute-start = (bf16[3,8,1024]{2,1,0:T(8,128)(2,1)S(1)}, bf16[3,8,1024]{2,1,0:T(8,128)(2,1)S(1)}, u32[]{:S(2)}, u32[]{:S(2)}) collective-permute-start(bf16[3,8,1024]{2,1,0:T(8,128)(2,1)S(1)} %pack.1.own), channel_id=1, source_target_pairs={{0,8},{4,12},{8,0},{12,4},{1,9},{5,13},{9,1},{13,5},{2,10},{6,14},... | collective-permute-start | bytes 147464 | tf_op jit(solution)/shard_map/ppermute | solution.py:70
  5.5 3.9 %load_a.1 = (bf16[2048,768]{1,0:T(8,128)(2,1)S(1)}, bf16[2048,768]{1,0:T(8,128)(2,1)S(1)}, bf16[768,2048]{1,0:T(8,128)(2,1)S(1)}, bf16[8,1024]{1,0:T(8,128)(2,1)S(1)}) custom-call(bf16[2048,6144]{1,0:T(8,128)(2,1)} %refs_0_.11, bf16[2048,6144]{1,0:T(8,128)(2,1)} %refs_1_.11, bf16[6144,2048]{1,0:T(8,128)(2,1)} %refs_2_.11, s32[1,24]{1,0:T(1,128)} %bitcast.3), custom_call_target="tpu_custom_call" | custom-call | flops 1000 | bytes 1000 | tf_op jit(solution)/shard_map/load_a/pallas_call | solution.py:83
  9.4 0.0 collective-permute-done.far
  9.4 1.6 %collective-permute-start.2 = (bf16[7,8,1024]{2,1,0:T(8,128)(2,1)S(1)}, bf16[7,8,1024]{2,1,0:T(8,128)(2,1)S(1)}, u32[]{:S(2)}, u32[]{:S(2)}) collective-permute-start(bf16[7,8,1024]{2,1,0:T(8,128)(2,1)S(1)} %get-tuple-element.44.refs_3_.refs_4_), channel_id=1, source_target_pairs={{0,16},{16,0},{1,17},{17,1},{2,18},{18,2},{3,19},{19,3},{4,20},{20... | collective-permute-start | bytes 344072 | tf_op jit(solution)/shard_map/ppermute | solution.py:70
  11.0 1.5 %collective-permute-start.3 = (bf16[6,8,1024]{2,1,0:T(8,128)(2,1)S(1)}, bf16[6,8,1024]{2,1,0:T(8,128)(2,1)S(1)}, u32[]{:S(2)}, u32[]{:S(2)}) collective-permute-start(bf16[6,8,1024]{2,1,0:T(8,128)(2,1)S(1)} %get-tuple-element.45.refs_3_), channel_id=1, source_target_pairs={{0,20},{4,16},{8,28},{12,24},{16,4},{20,0},{24,12},{28,8},{1,21},{... | collective-permute-start | bytes 294920 | tf_op jit(solution)/shard_map/ppermute | solution.py:70
  12.6 0.4 collective-permute-start.1
  13.0 3.8 %load_b.1 = (bf16[2048,768]{1,0:T(8,128)(2,1)S(1)}, bf16[2048,768]{1,0:T(8,128)(2,1)S(1)}, bf16[768,2048]{1,0:T(8,128)(2,1)S(1)}) custom-call(bf16[2048,6144]{1,0:T(8,128)(2,1)} %refs_0_.11, bf16[2048,6144]{1,0:T(8,128)(2,1)} %refs_1_.11, bf16[6144,2048]{1,0:T(8,128)(2,1)} %refs_2_.11, bf16[6,8,1024]{2,1,0:T(8,128)(2,1)S(1)} %get-tuple-element.45.refs_3_), custom_call_target="tpu_custom_call" | custom-call | flops 1000 | bytes 1000 | tf_op jit(solution)/shard_map/load_b/pallas_call | solution.py:83
  16.8 0.3 collective-permute-done.3.refs_6_
  17.2 0.1 collective-permute-done.1.refs_4_
  17.3 0.0 collective-permute-done.2.refs_5_
  17.3 2.9 %forward_3.1 = (bf16[2048,768]{1,0:T(8,128)(2,1)S(1)}, bf16[768,2048]{1,0:T(8,128)(2,1)S(1)}, bf16[48,2048]{1,0:T(8,128)(2,1)S(1)}, bf16[48,2048]{1,0:T(8,128)(2,1)S(1)}, f32[3,48,768]{2,1,0:T(8,128)S(1)}) custom-call(bf16[2048,6144]{1,0:T(8,128)(2,1)} %refs_0_.11, bf16[2048,6144]{1,0:T(8,128)(2,1)} %refs_1_.11, bf16[6144,2048]{1,0:T(8,128)(2,1)} %refs_2_.11, ...), custom_call_target="tpu_custom_call" | custom-call | flops 1000 | bytes 1000 | tf_op jit(solution)/shard_map/forward_3/pallas_call | solution.py:83
  20.1 0.1 collective-permute-start.4
  20.2 2.0 %forward_2.1 = (bf16[2048,768]{1,0:T(8,128)(2,1)S(1)}, f32[3,48,768]{2,1,0:T(8,128)S(1)}) custom-call(bf16[2048,6144]{1,0:T(8,128)(2,1)} %refs_0_.11, bf16[2048,6144]{1,0:T(8,128)(2,1)} %refs_1_.11, bf16[6144,2048]{1,0:T(8,128)(2,1)} %refs_2_.11, bf16[48,2048]{1,0:T(8,128)(2,1)S(1)} %get-tuple-element.50.refs_3_, ...), custom_call_target="tpu_custom_call" | custom-call | flops 1000 | bytes 1000 | tf_op jit(solution)/shard_map/forward_2/pallas_call | solution.py:83
  22.3 0.0 collective-permute-done.4.arrived
  22.3 1.6 %collective-permute-start.6 = (bf16[3,48,768]{2,1,0:T(8,128)(2,1)S(1)}, bf16[3,48,768]{2,1,0:T(8,128)(2,1)S(1)}, u32[]{:S(2)}, u32[]{:S(2)}) collective-permute-start(bf16[3,48,768]{2,1,0:T(8,128)(2,1)S(1)} %join.1.refs_8_), channel_id=1, source_target_pairs={{0,2},{1,3},{2,0},{3,1},{4,6},{5,7},{6,4},{7,5},{8,10},{9,11},{10,... | collective-permute-start | bytes 663560 | tf_op jit(solution)/shard_map/ppermute | solution.py:70
  23.9 2.9 %forward_1.1 = (bf16[2048,768]{1,0:T(8,128)(2,1)S(1)}, bf16[768,2048]{1,0:T(8,128)(2,1)S(1)}, bf16[3,48,768]{2,1,0:T(8,128)(2,1)S(1)}) custom-call(bf16[2048,6144]{1,0:T(8,128)(2,1)} %refs_0_.11, bf16[2048,6144]{1,0:T(8,128)(2,1)} %refs_1_.11, bf16[6144,2048]{1,0:T(8,128)(2,1)} %refs_2_.11, bf16[48,2048]{1,0:T(8,128)(2,1)S(1)} %get-tuple-element.50.refs_3_, ...), custom_call_target="tpu_custom_call" | custom-call | flops 1000 | bytes 1000 | tf_op jit(solution)/shard_map/forward_1/pallas_call | solution.py:83
  26.8 0.3 collective-permute-start.5
  27.1 0.0 copy-start
  27.1 2.6 %forward_0.1 = (f32[3,48,768]{2,1,0:T(8,128)S(1)}, bf16[2048,768]{1,0:T(8,128)(2,1)S(1)}) custom-call(bf16[2048,6144]{1,0:T(8,128)(2,1)} %refs_0_.11, bf16[2048,6144]{1,0:T(8,128)(2,1)} %refs_1_.11, bf16[6144,2048]{1,0:T(8,128)(2,1)} %refs_2_.11, bf16[48,2048]{1,0:T(8,128)(2,1)S(1)} %get-tuple-element.50.refs_3_, ...), custom_call_target="tpu_custom_call" | custom-call | flops 1000 | bytes 1000 | tf_op jit(solution)/shard_map/forward_0/pallas_call | solution.py:83
  29.6 0.6 %collective-permute-done.6.refs_2_ = bf16[3,48,768]{2,1,0:T(8,128)(2,1)S(1)} collective-permute-done((bf16[3,48,768]{2,1,0:T(8,128)(2,1)S(1)}, bf16[3,48,768]{2,1,0:T(8,128)(2,1)S(1)}, u32[]{:S(2)}, u32[]{:S(2)}) %collective-permute-start.6) | collective-permute-done | bytes 221216 | tf_op jit(solution)/shard_map/ppermute | solution.py:70
  30.2 0.0 collective-permute-done.5.refs_1_
  30.2 0.0 copy-done
  30.2 0.4 middle.1
  30.6 1.5 %collective-permute-start.7 = (bf16[112,768]{1,0:T(8,128)(2,1)S(1)}, bf16[112,768]{1,0:T(8,128)(2,1)S(1)}, u32[]{:S(2)}, u32[]{:S(2)}) collective-permute-start(bf16[112,768]{1,0:T(8,128)(2,1)S(1)} %get-tuple-element.64.message.refs_0_), channel_id=1, source_target_pairs={{0,2},{1,3},{2,0},{3,1},{4,6},{5,7},{6,4},{7,5},{8,10},{9,11},{10,... | collective-permute-start | bytes 516104 | tf_op jit(solution)/shard_map/ppermute | solution.py:70
  32.1 0.0 collective-permute-start.8
  32.1 0.5 collective-permute-start.9
  32.6 1.7 %backward_0.1.before = f32[2048,48]{1,0:T(8,128)S(1)} custom-call(bf16[112,768]{1,0:T(8,128)(2,1)S(1)} %get-tuple-element.64.message.refs_0_, bf16[2048,768]{1,0:T(8,128)(2,1)S(1)} %get-tuple-element.63.refs_6_.gate, bf16[2048,768]{1,0:T(8,128)(2,1)S(1)} %get-tuple-element.59.refs_5_.refs_7_.up), custom_call_target="tpu_custom_call" | custom-call | flops 1000 | bytes 1000 | tf_op jit(solution)/shard_map/backward_0/pallas_call | solution.py:83
  34.3 0.0 collective-permute-done.9.d_up
  34.4 0.0 collective-permute-done.8.d_gate.refs_1_
  34.4 1.8 %backward_1.1.before = f32[2048,48]{1,0:T(8,128)S(1)} custom-call(bf16[64,768]{1,0:T(8,128)(2,1)S(1)} %collective-permute-done.8.d_gate.refs_1_, bf16[48,768]{1,0:T(8,128)(2,1)S(1)} %collective-permute-done.9.d_up, bf16[2048,768]{1,0:T(8,128)(2,1)S(1)} %get-tuple-element.52.refs_5_.refs_8_.gate, bf16[2048,768]{1,0:T(8,128)(2,1)S(1)} %get-tuple-element.55.refs_6_.refs_9_.up, ...), custom_call_target="tpu_custom_call" | custom-call | flops 1000 | bytes 1000 | tf_op jit(solution)/shard_map/backward_1/pallas_call | solution.py:83
  36.1 0.4 collective-permute-done.7.message.refs_2_
  36.6 0.0 collective-permute-start.10
  36.6 1.8 %backward_2.1.before = f32[2048,48]{1,0:T(8,128)S(1)} custom-call(bf16[112,768]{1,0:T(8,128)(2,1)S(1)} %collective-permute-done.7.message.refs_2_, bf16[2048,768]{1,0:T(8,128)(2,1)S(1)} %get-tuple-element.49.refs_10_.refs_5_.gate, bf16[2048,768]{1,0:T(8,128)(2,1)S(1)} %get-tuple-element.53.refs_6_.refs_11_.up, f32[2048,48]{1,0:T(8,128)S(1)} %backward_1.1.before), custom_call_target="tpu_custom_call" | custom-call | flops 1000 | bytes 1000 | tf_op jit(solution)/shard_map/backward_2/pallas_call | solution.py:83
  38.4 0.0 collective-permute-done.10.message
  38.4 1.9 %backward_3.1 = (f32[24,1024]{1,0:T(8,128)S(1)}, f32[8,128]{1,0:T(8,128)S(1)}, bf16[3,8,1152]{2,1,0:T(8,128)(2,1)S(1)}, bf16[3,8,1152]{2,1,0:T(8,128)(2,1)S(1)}, bf16[3,8,1152]{2,1,0:T(8,128)(2,1)S(1)}) custom-call(bf16[112,768]{1,0:T(8,128)(2,1)S(1)} %collective-permute-done.10.message, bf16[2048,768]{1,0:T(8,128)(2,1)S(1)} %get-tuple-element.46.refs_7_.refs_12_.gate, ...), custom_call_target="tpu_custom_call" | custom-call | flops 1000 | bytes 1000 | tf_op jit(solution)/shard_map/backward_3/pallas_call | solution.py:83
  40.3 2.2 %collective-permute-start.11 = (bf16[3,8,1152]{2,1,0:T(8,128)(2,1)S(1)}, bf16[3,8,1152]{2,1,0:T(8,128)(2,1)S(1)}, u32[]{:S(2)}, u32[]{:S(2)}) collective-permute-start(bf16[3,8,1152]{2,1,0:T(8,128)(2,1)S(1)} %get-tuple-element.73), channel_id=1, source_target_pairs={{0,12},{4,8},{8,4},{12,0},{1,13},{5,9},{9,5},{13,1},{2,14},{6,10},... | collective-permute-start | bytes 165896 | tf_op jit(solution)/shard_map/ppermute | solution.py:70
  42.5 0.7 %collective-permute-start.12 = (bf16[3,8,1152]{2,1,0:T(8,128)(2,1)S(1)}, bf16[3,8,1152]{2,1,0:T(8,128)(2,1)S(1)}, u32[]{:S(2)}, u32[]{:S(2)}) collective-permute-start(bf16[3,8,1152]{2,1,0:T(8,128)(2,1)S(1)} %get-tuple-element.74), channel_id=1, source_target_pairs={{0,8},{4,12},{8,0},{12,4},{1,9},{5,13},{9,1},{13,5},{2,10},{6,14},... | collective-permute-start | bytes 165896 | tf_op jit(solution)/shard_map/ppermute | solution.py:70
  43.2 1.5 %collective-permute-start.13 = (bf16[3,8,1152]{2,1,0:T(8,128)(2,1)S(1)}, bf16[3,8,1152]{2,1,0:T(8,128)(2,1)S(1)}, u32[]{:S(2)}, u32[]{:S(2)}) collective-permute-start(bf16[3,8,1152]{2,1,0:T(8,128)(2,1)S(1)} %get-tuple-element.75), channel_id=1, source_target_pairs={{0,4},{4,0},{8,12},{12,8},{1,5},{5,1},{9,13},{13,9},{2,6},{6,2},{1... | collective-permute-start | bytes 165896 | tf_op jit(solution)/shard_map/ppermute | solution.py:70
  44.8 2.2 %collective-permute-done.11.refs_0_ = bf16[3,8,1152]{2,1,0:T(8,128)(2,1)S(1)} collective-permute-done((bf16[3,8,1152]{2,1,0:T(8,128)(2,1)S(1)}, bf16[3,8,1152]{2,1,0:T(8,128)(2,1)S(1)}, u32[]{:S(2)}, u32[]{:S(2)}) %collective-permute-start.11) | collective-permute-done | bytes 55328 | tf_op jit(solution)/shard_map/ppermute | solution.py:70
  47.0 2.1 %collective-permute-done.12.refs_1_ = bf16[3,8,1152]{2,1,0:T(8,128)(2,1)S(1)} collective-permute-done((bf16[3,8,1152]{2,1,0:T(8,128)(2,1)S(1)}, bf16[3,8,1152]{2,1,0:T(8,128)(2,1)S(1)}, u32[]{:S(2)}, u32[]{:S(2)}) %collective-permute-start.12) | collective-permute-done | bytes 55328 | tf_op jit(solution)/shard_map/ppermute | solution.py:70
  49.0 0.0 collective-permute-done.13.refs_2_
  49.1 1.6 %collective-permute-start.14 = (bf16[2,8,1024]{2,1,0:T(8,128)(2,1)S(1)}, bf16[2,8,1024]{2,1,0:T(8,128)(2,1)S(1)}, u32[]{:S(2)}, u32[]{:S(2)}) collective-permute-start(bf16[2,8,1024]{2,1,0:T(8,128)(2,1)S(1)} %get-tuple-element.77), channel_id=1, source_target_pairs={{0,16},{16,0},{1,17},{17,1},{2,18},{18,2},{3,19},{19,3},{4,20},{20... | collective-permute-start | bytes 98312 | tf_op jit(solution)/shard_map/ppermute | solution.py:70
  50.7 0.5 collective-permute-start.15
  51.2 3.2 %collective-permute-done.15.other_grads = f32[4,768]{1,0:T(4,128)S(1)} collective-permute-done((f32[4,768]{1,0:T(4,128)S(1)}, f32[4,768]{1,0:T(4,128)S(1)}, u32[]{:S(2)}, u32[]{:S(2)}) %collective-permute-start.15) | collective-permute-done | bytes 12320 | tf_op jit(solution)/shard_map/ppermute | solution.py:70
  54.4 0.0 collective-permute-done.14.arrived
  54.4 0.7 %last.1 = (bf16[6,2048]{1,0:T(8,128)(2,1)}, f32[4,1536]{1,0:T(4,128)}, f32[4]{0:T(128)}) custom-call(f32[16,1024]{1,0:T(8,128)S(1)} %get-tuple-element.76.own, bf16[2,8,1024]{2,1,0:T(8,128)(2,1)S(1)} %collective-permute-done.14.arrived, f32[4,768]{1,0:T(4,128)S(1)} %get-tuple-element.78.grads, f32[4,768]{1,0:T(4,128)S(1)} %collective-permute-done.15.other_grads), custom_call_target="tpu_custom_call" | custom-call | flops 1000 | bytes 1000 | tf_op jit(solution)/shard_map/last/pallas_call | solution.py:83
  (3 shorter events, 0.1 us)
Async XLA Ops:
  1.4 8.0 %collective-permute-start = (bf16[3,8,1024]{2,1,0:T(8,128)(2,1)S(1)}, bf16[3,8,1024]{2,1,0:T(8,128)(2,1)S(1)}, u32[]{:S(2)}, u32[]{:S(2)}) collective-permute-start(bf16[3,8,1024]{2,1,0:T(8,128)(2,1)S(1)} %pack.1.own), channel_id=1, source_target_pairs={{0,8},{4,12},{8,0},{12,4},{1,9},{5,13},{9,1},{13,5},{2,10},{6,14},... | collective-permute-start | bytes 147464 | tf_op jit(solution)/shard_map/ppermute | solution.py:70
  9.4 7.8 %collective-permute-start.2 = (bf16[7,8,1024]{2,1,0:T(8,128)(2,1)S(1)}, bf16[7,8,1024]{2,1,0:T(8,128)(2,1)S(1)}, u32[]{:S(2)}, u32[]{:S(2)}) collective-permute-start(bf16[7,8,1024]{2,1,0:T(8,128)(2,1)S(1)} %get-tuple-element.44.refs_3_.refs_4_), channel_id=1, source_target_pairs={{0,16},{16,0},{1,17},{17,1},{2,18},{18,2},{3,19},{19,3},{4,20},{20... | collective-permute-start | bytes 344072 | tf_op jit(solution)/shard_map/ppermute | solution.py:70
  11.0 6.1 %collective-permute-start.3 = (bf16[6,8,1024]{2,1,0:T(8,128)(2,1)S(1)}, bf16[6,8,1024]{2,1,0:T(8,128)(2,1)S(1)}, u32[]{:S(2)}, u32[]{:S(2)}) collective-permute-start(bf16[6,8,1024]{2,1,0:T(8,128)(2,1)S(1)} %get-tuple-element.45.refs_3_), channel_id=1, source_target_pairs={{0,20},{4,16},{8,28},{12,24},{16,4},{20,0},{24,12},{28,8},{1,21},{... | collective-permute-start | bytes 294920 | tf_op jit(solution)/shard_map/ppermute | solution.py:70
  12.6 4.7 %collective-permute-start.1 = (bf16[6,8,1024]{2,1,0:T(8,128)(2,1)S(1)}, bf16[6,8,1024]{2,1,0:T(8,128)(2,1)S(1)}, u32[]{:S(2)}, u32[]{:S(2)}) collective-permute-start(bf16[6,8,1024]{2,1,0:T(8,128)(2,1)S(1)} %get-tuple-element.45.refs_3_), channel_id=1, source_target_pairs={{0,4},{4,0},{8,12},{12,8},{1,5},{5,1},{9,13},{13,9},{2,6},{6,2},{1... | collective-permute-start | bytes 294920 | tf_op jit(solution)/shard_map/ppermute | solution.py:70
  20.1 2.1 %collective-permute-start.4 = (f32[3,48,768]{2,1,0:T(8,128)S(1)}, f32[3,48,768]{2,1,0:T(8,128)S(1)}, u32[]{:S(2)}, u32[]{:S(2)}) collective-permute-start(f32[3,48,768]{2,1,0:T(8,128)S(1)} %get-tuple-element.58), channel_id=1, source_target_pairs={{0,1},{1,0},{2,3},{3,2},{4,5},{5,4},{6,7},{7,6},{8,9},{9,8},{10,11... | collective-permute-start | bytes 1327112 | tf_op jit(solution)/shard_map/ppermute | solution.py:70
  22.3 7.9 %collective-permute-start.6 = (bf16[3,48,768]{2,1,0:T(8,128)(2,1)S(1)}, bf16[3,48,768]{2,1,0:T(8,128)(2,1)S(1)}, u32[]{:S(2)}, u32[]{:S(2)}) collective-permute-start(bf16[3,48,768]{2,1,0:T(8,128)(2,1)S(1)} %join.1.refs_8_), channel_id=1, source_target_pairs={{0,2},{1,3},{2,0},{3,1},{4,6},{5,7},{6,4},{7,5},{8,10},{9,11},{10,... | collective-permute-start | bytes 663560 | tf_op jit(solution)/shard_map/ppermute | solution.py:70
  26.8 3.4 %collective-permute-start.5 = (bf16[3,48,768]{2,1,0:T(8,128)(2,1)S(1)}, bf16[3,48,768]{2,1,0:T(8,128)(2,1)S(1)}, u32[]{:S(2)}, u32[]{:S(2)}) collective-permute-start(bf16[3,48,768]{2,1,0:T(8,128)(2,1)S(1)} %get-tuple-element.62), channel_id=1, source_target_pairs={{0,1},{1,0},{2,3},{3,2},{4,5},{5,4},{6,7},{7,6},{8,9},{9,8},{10,11... | collective-permute-start | bytes 663560 | tf_op jit(solution)/shard_map/ppermute | solution.py:70
  27.1 3.2 %copy-start = (f32[6144]{0:T(1024)S(1)}, f32[6144]{0:T(1024)}, u32[]{:S(2)}) copy-start(f32[6144]{0:T(1024)} %param.12) | copy-start | bytes 73732
  30.6 6.0 %collective-permute-start.7 = (bf16[112,768]{1,0:T(8,128)(2,1)S(1)}, bf16[112,768]{1,0:T(8,128)(2,1)S(1)}, u32[]{:S(2)}, u32[]{:S(2)}) collective-permute-start(bf16[112,768]{1,0:T(8,128)(2,1)S(1)} %get-tuple-element.64.message.refs_0_), channel_id=1, source_target_pairs={{0,2},{1,3},{2,0},{3,1},{4,6},{5,7},{6,4},{7,5},{8,10},{9,11},{10,... | collective-permute-start | bytes 516104 | tf_op jit(solution)/shard_map/ppermute | solution.py:70
  32.1 2.3 %collective-permute-start.8 = (bf16[64,768]{1,0:T(8,128)(2,1)S(1)}, bf16[64,768]{1,0:T(8,128)(2,1)S(1)}, u32[]{:S(2)}, u32[]{:S(2)}) collective-permute-start(bf16[64,768]{1,0:T(8,128)(2,1)S(1)} %get-tuple-element.65), channel_id=1, source_target_pairs={{0,1},{1,0},{2,3},{3,2},{4,5},{5,4},{6,7},{7,6},{8,9},{9,8},{10,11... | collective-permute-start | bytes 294920 | tf_op jit(solution)/shard_map/ppermute | solution.py:70
  32.1 2.3 %collective-permute-start.9 = (bf16[48,768]{1,0:T(8,128)(2,1)S(1)}, bf16[48,768]{1,0:T(8,128)(2,1)S(1)}, u32[]{:S(2)}, u32[]{:S(2)}) collective-permute-start(bf16[48,768]{1,0:T(8,128)(2,1)S(1)} %get-tuple-element.66), channel_id=1, source_target_pairs={{0,1},{1,0},{2,3},{3,2},{4,5},{5,4},{6,7},{7,6},{8,9},{9,8},{10,11... | collective-permute-start | bytes 221192 | tf_op jit(solution)/shard_map/ppermute | solution.py:70
  36.6 1.8 %collective-permute-start.10 = (bf16[112,768]{1,0:T(8,128)(2,1)S(1)}, bf16[112,768]{1,0:T(8,128)(2,1)S(1)}, u32[]{:S(2)}, u32[]{:S(2)}) collective-permute-start(bf16[112,768]{1,0:T(8,128)(2,1)S(1)} %collective-permute-done.7.message.refs_2_), channel_id=1, source_target_pairs={{0,1},{1,0},{2,3},{3,2},{4,5},{5,4},{6,7},{7,6},{8,9},{9,8},{10,11... | collective-permute-start | bytes 516104 | tf_op jit(solution)/shard_map/ppermute | solution.py:70
  40.3 6.6 %collective-permute-start.11 = (bf16[3,8,1152]{2,1,0:T(8,128)(2,1)S(1)}, bf16[3,8,1152]{2,1,0:T(8,128)(2,1)S(1)}, u32[]{:S(2)}, u32[]{:S(2)}) collective-permute-start(bf16[3,8,1152]{2,1,0:T(8,128)(2,1)S(1)} %get-tuple-element.73), channel_id=1, source_target_pairs={{0,12},{4,8},{8,4},{12,0},{1,13},{5,9},{9,5},{13,1},{2,14},{6,10},... | collective-permute-start | bytes 165896 | tf_op jit(solution)/shard_map/ppermute | solution.py:70
  42.5 6.5 %collective-permute-start.12 = (bf16[3,8,1152]{2,1,0:T(8,128)(2,1)S(1)}, bf16[3,8,1152]{2,1,0:T(8,128)(2,1)S(1)}, u32[]{:S(2)}, u32[]{:S(2)}) collective-permute-start(bf16[3,8,1152]{2,1,0:T(8,128)(2,1)S(1)} %get-tuple-element.74), channel_id=1, source_target_pairs={{0,8},{4,12},{8,0},{12,4},{1,9},{5,13},{9,1},{13,5},{2,10},{6,14},... | collective-permute-start | bytes 165896 | tf_op jit(solution)/shard_map/ppermute | solution.py:70
  43.2 5.8 %collective-permute-start.13 = (bf16[3,8,1152]{2,1,0:T(8,128)(2,1)S(1)}, bf16[3,8,1152]{2,1,0:T(8,128)(2,1)S(1)}, u32[]{:S(2)}, u32[]{:S(2)}) collective-permute-start(bf16[3,8,1152]{2,1,0:T(8,128)(2,1)S(1)} %get-tuple-element.75), channel_id=1, source_target_pairs={{0,4},{4,0},{8,12},{12,8},{1,5},{5,1},{9,13},{13,9},{2,6},{6,2},{1... | collective-permute-start | bytes 165896 | tf_op jit(solution)/shard_map/ppermute | solution.py:70
  49.1 5.3 %collective-permute-start.14 = (bf16[2,8,1024]{2,1,0:T(8,128)(2,1)S(1)}, bf16[2,8,1024]{2,1,0:T(8,128)(2,1)S(1)}, u32[]{:S(2)}, u32[]{:S(2)}) collective-permute-start(bf16[2,8,1024]{2,1,0:T(8,128)(2,1)S(1)} %get-tuple-element.77), channel_id=1, source_target_pairs={{0,16},{16,0},{1,17},{17,1},{2,18},{18,2},{3,19},{19,3},{4,20},{20... | collective-permute-start | bytes 98312 | tf_op jit(solution)/shard_map/ppermute | solution.py:70
  50.7 3.7 %collective-permute-start.15 = (f32[4,768]{1,0:T(4,128)S(1)}, f32[4,768]{1,0:T(4,128)S(1)}, u32[]{:S(2)}, u32[]{:S(2)}) collective-permute-start(f32[4,768]{1,0:T(4,128)S(1)} %get-tuple-element.79), channel_id=1, source_target_pairs={{0,16},{16,0},{1,17},{17,1},{2,18},{18,2},{3,19},{19,3},{4,20},{20... | collective-permute-start | bytes 36872 | tf_op jit(solution)/shard_map/ppermute | solution.py:70

commit v13 on v11

--- a/solution.py
+++ b/solution.py
@@ -131,7 +131,7 @@
     marked[2 * slabs] = marks[...]
 
 
-WIDE, NEXT, FAR = 4, 1, 3
+WIDE, NEXT, FAR = 4, 1, 2
 GATE, UP, DOWN = range(3)
 WHOLE_STRIP = (GATE, UP, DOWN)
 CHUNKS = 4
@@ -185,10 +185,8 @@
 
 def strip_parts(tokens, cotans, gate, up, down, put):
     tile = 256
-
-    @pl.loop(0, gate.shape[1] // tile)
-    def _(i):
-        span = pl.ds(pl.multiple_of(i * tile, tile), tile)
+    for start in range(0, gate.shape[1], tile):
+        span = slice(start, start + tile)
         put(GATE, span, jnp.dot(tokens[...], gate[:, span], preferred_element_type=jnp.float32))
         put(UP, span, jnp.dot(tokens[...], up[:, span], preferred_element_type=jnp.float32))
         put(DOWN, span, contract_rows(cotans[...], down[span, :]))
@@ -230,13 +228,11 @@
     sources, (tokens, cotans, up, down) = refs[:3], refs[3:7]
     out, gate, sem = refs[-3:]
     copies = start_loads([(GATE, 0)], groups, sources, [gate], sem)
-    tile = 256
-
-    @pl.loop(0, up.shape[1] // tile)
-    def _(i):
-        span = pl.ds(pl.multiple_of(i * tile, tile), tile)
-        out[UP, :, span] = jnp.dot(tokens[...], up[:, span], preferred_element_type=jnp.float32)
-        out[DOWN, :, span] = contract_rows(cotans[...], down[span, :])
+
+    @pl.when(lax.axis_index("narrow") >= 0)
+    def _():
+        out[UP] = jnp.dot(tokens[...], up[...], preferred_element_type=jnp.float32)
+        out[DOWN] = contract_rows(cotans[...], down[...])
 
     for copy in copies:
         copy.wait()
@@ -441,7 +437,7 @@
     (marks,) = call_loading(
         functools.partial(keys_kernel, share),
         "load_a",
-        [(kind, 3) for kind in WHOLE_STRIP],
+        [(kind, 3) for kind in WHOLE_STRIP] + [(GATE, 2)],
         [pltpu.VMEM((8, side), bf16)],
         [pltpu.with_memory_space_constraint(seq_ids[None, :], pltpu.HBM)],
         [pltpu.VMEM((1, half), jnp.int32), pltpu.SemaphoreType.DMA((1,))],
@@ -457,7 +453,7 @@
     diagonal = exchange(pair, ("groups", "wide"), WIDE + NEXT)
     other_marked = exchange(marked, "groups", 1)
     beside = exchange(pair, "wide", NEXT)
-    load("load_b", [(kind, 2) for kind in WHOLE_STRIP], [pair])
+    load("load_b", [(UP, 2), (DOWN, 2)], [pair])
 
     part = pltpu.VMEM((3, tokens, width), f32)
     near_shape = pltpu.VMEM((3, tokens, width), bf16)
@@ -466,7 +462,7 @@
         "forward_3",
         [(GATE, 1), (DOWN, 1)],
         [pltpu.VMEM((tokens, features), bf16)] * 2 + [part],
-        [marked, beside, other_marked, diagonal] + hold(3) + hold(2, [GATE]),
+        [marked, beside, other_marked, diagonal] + hold(3) + hold(2, [UP]),
         [pltpu.VMEM((tokens, features), f32)] * 2,
     )
     panel = [tokens_all, cotans_all]

time: 55.1 us -> 55.2 us (level)
  waiting for transfers between devices: 7.96 us -> 9.18 us
  starting transfers between devices: 18.6 us -> 17.6 us
    ppermute x15, waiting for transfers between devices: 7.96 us -> 9.18 us  [exchange(): return lax.ppermute(array, axes, [(i, i ^ step) for i in range(size)])]
    ppermute x15, starting transfers between devices: 18.6 us -> 17.6 us  [exchange(): return lax.ppermute(array, axes, [(i, i ^ step) for i in range(size)])]
  transfers between devices with their start and end apart: 15 -> 15, of which waited for: 7 -> 7; matrix products, arithmetic and copies ran while one was open for 0% -> 0% of each run, Pallas kernels for 38% -> 37%
where the time goes in v13:
time: 55.2 us; the launch traced here: 55 us
  Pallas kernels  27.3 us (49%)
  starting transfers between devices  17.6 us (32%)
  waiting for transfers between devices  9.18 us (17%)
  between operations  0.94 us (2%)
    pallas_call x16, Pallas kernels, call(): pl.pallas_call(body, out_shape=outs, in_specs=[pl.BlockSpec(memory_space=...  27.3 us
    ppermute x15, starting transfers between devices, exchange(): return lax.ppermute(array, axes, [(i, i ^ step) for i in range(size)])  17.6 us
    ppermute x15, waiting for transfers between devices, exchange(): return lax.ppermute(array, axes, [(i, i ^ step) for i in range(size)])  9.18 us
  transfers between devices with their start and end apart: 15, of which 7 were waited for; matrix products, arithmetic and copies ran while one was open for 0% of the time, Pallas kernels for 37%

profile of v13, /device:TPU:0, one launch (start us, length us, event | category | flops | bytes accessed | tf_op | source)
XLA Modules:
  0.0 55.0 jit_solution(11224457160067152405)
XLA Ops:
  0.6 0.8 %pack.1.own = bf16[3,8,1024]{2,1,0:T(8,128)(2,1)S(1)} custom-call(bf16[6,2048]{1,0:T(8,128)(2,1)} %inputs.1, bf16[6,2048]{1,0:T(8,128)(2,1)} %cotangent.1), custom_call_target="tpu_custom_call" | custom-call | flops 1000 | bytes 1000 | tf_op jit(solution)/shard_map/pack/pallas_call | solution.py:83
  1.4 4.1 %collective-permute-start = (bf16[3,8,1024]{2,1,0:T(8,128)(2,1)S(1)}, bf16[3,8,1024]{2,1,0:T(8,128)(2,1)S(1)}, u32[]{:S(2)}, u32[]{:S(2)}) collective-permute-start(bf16[3,8,1024]{2,1,0:T(8,128)(2,1)S(1)} %pack.1.own), channel_id=1, source_target_pairs={{0,8},{4,12},{8,0},{12,4},{1,9},{5,13},{9,1},{13,5},{2,10},{6,14},... | collective-permute-start | bytes 147464 | tf_op jit(solution)/shard_map/ppermute | solution.py:70
  5.5 4.9 %load_a.1 = (bf16[2048,768]{1,0:T(8,128)(2,1)S(1)}, bf16[2048,768]{1,0:T(8,128)(2,1)S(1)}, bf16[768,2048]{1,0:T(8,128)(2,1)S(1)}, bf16[2048,768]{1,0:T(8,128)(2,1)S(1)}, bf16[8,1024]{1,0:T(8,128)(2,1)S(1)}) custom-call(bf16[2048,6144]{1,0:T(8,128)(2,1)} %refs_0_.11, bf16[2048,6144]{1,0:T(8,128)(2,1)} %refs_1_.11, bf16[6144,2048]{1,0:T(8,128)(2,1)} %refs_2_.11, ...), custom_call_target="tpu_custom_call" | custom-call | flops 1000 | bytes 1000 | tf_op jit(solution)/shard_map/load_a/pallas_call | solution.py:83
  10.4 0.0 collective-permute-done.far
  10.5 1.6 %collective-permute-start.2 = (bf16[7,8,1024]{2,1,0:T(8,128)(2,1)S(1)}, bf16[7,8,1024]{2,1,0:T(8,128)(2,1)S(1)}, u32[]{:S(2)}, u32[]{:S(2)}) collective-permute-start(bf16[7,8,1024]{2,1,0:T(8,128)(2,1)S(1)} %get-tuple-element.43.refs_3_.refs_4_), channel_id=1, source_target_pairs={{0,16},{16,0},{1,17},{17,1},{2,18},{18,2},{3,19},{19,3},{4,20},{20... | collective-permute-start | bytes 344072 | tf_op jit(solution)/shard_map/ppermute | solution.py:70
  12.0 1.5 %collective-permute-start.3 = (bf16[6,8,1024]{2,1,0:T(8,128)(2,1)S(1)}, bf16[6,8,1024]{2,1,0:T(8,128)(2,1)S(1)}, u32[]{:S(2)}, u32[]{:S(2)}) collective-permute-start(bf16[6,8,1024]{2,1,0:T(8,128)(2,1)S(1)} %get-tuple-element.44.refs_3_), channel_id=1, source_target_pairs={{0,20},{4,16},{8,28},{12,24},{16,4},{20,0},{24,12},{28,8},{1,21},{... | collective-permute-start | bytes 294920 | tf_op jit(solution)/shard_map/ppermute | solution.py:70
  13.6 0.4 collective-permute-start.1
  14.0 2.9 %load_b.1 = (bf16[2048,768]{1,0:T(8,128)(2,1)S(1)}, bf16[768,2048]{1,0:T(8,128)(2,1)S(1)}) custom-call(bf16[2048,6144]{1,0:T(8,128)(2,1)} %refs_0_.11, bf16[2048,6144]{1,0:T(8,128)(2,1)} %refs_1_.11, bf16[6144,2048]{1,0:T(8,128)(2,1)} %refs_2_.11, bf16[6,8,1024]{2,1,0:T(8,128)(2,1)S(1)} %get-tuple-element.44.refs_3_), custom_call_target="tpu_custom_call" | custom-call | flops 1000 | bytes 1000 | tf_op jit(solution)/shard_map/load_b/pallas_call | solution.py:83
  16.9 1.2 %collective-permute-done.3.refs_6_ = bf16[6,8,1024]{2,1,0:T(8,128)(2,1)S(1)} collective-permute-done((bf16[6,8,1024]{2,1,0:T(8,128)(2,1)S(1)}, bf16[6,8,1024]{2,1,0:T(8,128)(2,1)S(1)}, u32[]{:S(2)}, u32[]{:S(2)}) %collective-permute-start.3) | collective-permute-done | bytes 98336 | tf_op jit(solution)/shard_map/ppermute | solution.py:70
  18.1 0.1 collective-permute-done.1.refs_4_
  18.2 0.0 collective-permute-done.2.refs_5_
  18.2 2.9 %forward_3.1 = (bf16[2048,768]{1,0:T(8,128)(2,1)S(1)}, bf16[768,2048]{1,0:T(8,128)(2,1)S(1)}, bf16[48,2048]{1,0:T(8,128)(2,1)S(1)}, bf16[48,2048]{1,0:T(8,128)(2,1)S(1)}, f32[3,48,768]{2,1,0:T(8,128)S(1)}) custom-call(bf16[2048,6144]{1,0:T(8,128)(2,1)} %refs_0_.11, bf16[2048,6144]{1,0:T(8,128)(2,1)} %refs_1_.11, bf16[6144,2048]{1,0:T(8,128)(2,1)} %refs_2_.11, ...), custom_call_target="tpu_custom_call" | custom-call | flops 1000 | bytes 1000 | tf_op jit(solution)/shard_map/forward_3/pallas_call | solution.py:83
  21.1 0.1 collective-permute-start.4
  21.2 2.0 %forward_2.1 = (bf16[2048,768]{1,0:T(8,128)(2,1)S(1)}, f32[3,48,768]{2,1,0:T(8,128)S(1)}) custom-call(bf16[2048,6144]{1,0:T(8,128)(2,1)} %refs_0_.11, bf16[2048,6144]{1,0:T(8,128)(2,1)} %refs_1_.11, bf16[6144,2048]{1,0:T(8,128)(2,1)} %refs_2_.11, bf16[48,2048]{1,0:T(8,128)(2,1)S(1)} %get-tuple-element.49.refs_3_, ...), custom_call_target="tpu_custom_call" | custom-call | flops 1000 | bytes 1000 | tf_op jit(solution)/shard_map/forward_2/pallas_call | solution.py:83
  23.2 0.0 collective-permute-done.4.arrived
  23.3 1.6 %collective-permute-start.6 = (bf16[3,48,768]{2,1,0:T(8,128)(2,1)S(1)}, bf16[3,48,768]{2,1,0:T(8,128)(2,1)S(1)}, u32[]{:S(2)}, u32[]{:S(2)}) collective-permute-start(bf16[3,48,768]{2,1,0:T(8,128)(2,1)S(1)} %join.1.refs_8_), channel_id=1, source_target_pairs={{0,2},{1,3},{2,0},{3,1},{4,6},{5,7},{6,4},{7,5},{8,10},{9,11},{10,... | collective-permute-start | bytes 663560 | tf_op jit(solution)/shard_map/ppermute | solution.py:70
  24.8 2.9 %forward_1.1 = (bf16[2048,768]{1,0:T(8,128)(2,1)S(1)}, bf16[768,2048]{1,0:T(8,128)(2,1)S(1)}, bf16[3,48,768]{2,1,0:T(8,128)(2,1)S(1)}) custom-call(bf16[2048,6144]{1,0:T(8,128)(2,1)} %refs_0_.11, bf16[2048,6144]{1,0:T(8,128)(2,1)} %refs_1_.11, bf16[6144,2048]{1,0:T(8,128)(2,1)} %refs_2_.11, bf16[48,2048]{1,0:T(8,128)(2,1)S(1)} %get-tuple-element.49.refs_3_, ...), custom_call_target="tpu_custom_call" | custom-call | flops 1000 | bytes 1000 | tf_op jit(solution)/shard_map/forward_1/pallas_call | solution.py:83
  27.7 0.3 collective-permute-start.5
  28.0 0.0 copy-start
  28.0 2.6 %forward_0.1 = (f32[3,48,768]{2,1,0:T(8,128)S(1)}, bf16[2048,768]{1,0:T(8,128)(2,1)S(1)}) custom-call(bf16[2048,6144]{1,0:T(8,128)(2,1)} %refs_0_.11, bf16[2048,6144]{1,0:T(8,128)(2,1)} %refs_1_.11, bf16[6144,2048]{1,0:T(8,128)(2,1)} %refs_2_.11, bf16[48,2048]{1,0:T(8,128)(2,1)S(1)} %get-tuple-element.49.refs_3_, ...), custom_call_target="tpu_custom_call" | custom-call | flops 1000 | bytes 1000 | tf_op jit(solution)/shard_map/forward_0/pallas_call | solution.py:83
  30.6 0.6 %collective-permute-done.6.refs_2_ = bf16[3,48,768]{2,1,0:T(8,128)(2,1)S(1)} collective-permute-done((bf16[3,48,768]{2,1,0:T(8,128)(2,1)S(1)}, bf16[3,48,768]{2,1,0:T(8,128)(2,1)S(1)}, u32[]{:S(2)}, u32[]{:S(2)}) %collective-permute-start.6) | collective-permute-done | bytes 221216 | tf_op jit(solution)/shard_map/ppermute | solution.py:70
  31.2 0.0 collective-permute-done.5.refs_1_
  31.2 0.0 copy-done
  31.2 0.4 middle.1
  31.5 1.5 %collective-permute-start.7 = (bf16[112,768]{1,0:T(8,128)(2,1)S(1)}, bf16[112,768]{1,0:T(8,128)(2,1)S(1)}, u32[]{:S(2)}, u32[]{:S(2)}) collective-permute-start(bf16[112,768]{1,0:T(8,128)(2,1)S(1)} %get-tuple-element.63.message.refs_0_), channel_id=1, source_target_pairs={{0,2},{1,3},{2,0},{3,1},{4,6},{5,7},{6,4},{7,5},{8,10},{9,11},{10,... | collective-permute-start | bytes 516104 | tf_op jit(solution)/shard_map/ppermute | solution.py:70
  33.0 0.0 collective-permute-start.8
  33.0 0.5 collective-permute-start.9
  33.5 1.7 %backward_0.1.before = f32[2048,48]{1,0:T(8,128)S(1)} custom-call(bf16[112,768]{1,0:T(8,128)(2,1)S(1)} %get-tuple-element.63.message.refs_0_, bf16[2048,768]{1,0:T(8,128)(2,1)S(1)} %get-tuple-element.62.refs_6_.gate, bf16[2048,768]{1,0:T(8,128)(2,1)S(1)} %get-tuple-element.58.refs_5_.refs_7_.up), custom_call_target="tpu_custom_call" | custom-call | flops 1000 | bytes 1000 | tf_op jit(solution)/shard_map/backward_0/pallas_call | solution.py:83
  35.3 0.0 collective-permute-done.9.d_up
  35.3 0.0 collective-permute-done.8.d_gate.refs_1_
  35.3 1.8 %backward_1.1.before = f32[2048,48]{1,0:T(8,128)S(1)} custom-call(bf16[64,768]{1,0:T(8,128)(2,1)S(1)} %collective-permute-done.8.d_gate.refs_1_, bf16[48,768]{1,0:T(8,128)(2,1)S(1)} %collective-permute-done.9.d_up, bf16[2048,768]{1,0:T(8,128)(2,1)S(1)} %get-tuple-element.51.refs_5_.refs_8_.gate, bf16[2048,768]{1,0:T(8,128)(2,1)S(1)} %get-tuple-element.54.refs_6_.refs_9_.up, ...), custom_call_target="tpu_custom_call" | custom-call | flops 1000 | bytes 1000 | tf_op jit(solution)/shard_map/backward_1/pallas_call | solution.py:83
  37.1 0.4 collective-permute-done.7.message.refs_2_
  37.5 0.0 collective-permute-start.10
  37.5 1.8 %backward_2.1.before = f32[2048,48]{1,0:T(8,128)S(1)} custom-call(bf16[112,768]{1,0:T(8,128)(2,1)S(1)} %collective-permute-done.7.message.refs_2_, bf16[2048,768]{1,0:T(8,128)(2,1)S(1)} %get-tuple-element.52.refs_5_.refs_10_.gate, bf16[2048,768]{1,0:T(8,128)(2,1)S(1)} %get-tuple-element.48.refs_10_.refs_6_.refs_11_.up, f32[2048,48]{1,0:T(8,128)S(1)} %backward_1.1.before), custom_call_target="tpu_custom_call" | custom-call | flops 1000 | bytes 1000 | tf_op jit(solution)/shard_map/backward_2/pallas_call | solution.py:83
  39.3 0.0 collective-permute-done.10.message
  39.3 1.9 %backward_3.1 = (f32[24,1024]{1,0:T(8,128)S(1)}, f32[8,128]{1,0:T(8,128)S(1)}, bf16[3,8,1152]{2,1,0:T(8,128)(2,1)S(1)}, bf16[3,8,1152]{2,1,0:T(8,128)(2,1)S(1)}, bf16[3,8,1152]{2,1,0:T(8,128)(2,1)S(1)}) custom-call(bf16[112,768]{1,0:T(8,128)(2,1)S(1)} %collective-permute-done.10.message, bf16[2048,768]{1,0:T(8,128)(2,1)S(1)} %get-tuple-element.45.refs_7_.refs_12_.gate, ...), custom_call_target="tpu_custom_call" | custom-call | flops 1000 | bytes 1000 | tf_op jit(solution)/shard_map/backward_3/pallas_call | solution.py:83
  41.3 1.2 %collective-permute-start.11 = (bf16[3,8,1152]{2,1,0:T(8,128)(2,1)S(1)}, bf16[3,8,1152]{2,1,0:T(8,128)(2,1)S(1)}, u32[]{:S(2)}, u32[]{:S(2)}) collective-permute-start(bf16[3,8,1152]{2,1,0:T(8,128)(2,1)S(1)} %get-tuple-element.71), channel_id=1, source_target_pairs={{0,12},{4,8},{8,4},{12,0},{1,13},{5,9},{9,5},{13,1},{2,14},{6,10},... | collective-permute-start | bytes 165896 | tf_op jit(solution)/shard_map/ppermute | solution.py:70
  42.5 1.7 %collective-permute-start.12 = (bf16[3,8,1152]{2,1,0:T(8,128)(2,1)S(1)}, bf16[3,8,1152]{2,1,0:T(8,128)(2,1)S(1)}, u32[]{:S(2)}, u32[]{:S(2)}) collective-permute-start(bf16[3,8,1152]{2,1,0:T(8,128)(2,1)S(1)} %get-tuple-element.72), channel_id=1, source_target_pairs={{0,8},{4,12},{8,0},{12,4},{1,9},{5,13},{9,1},{13,5},{2,10},{6,14},... | collective-permute-start | bytes 165896 | tf_op jit(solution)/shard_map/ppermute | solution.py:70
  44.2 1.5 %collective-permute-start.13 = (bf16[3,8,1152]{2,1,0:T(8,128)(2,1)S(1)}, bf16[3,8,1152]{2,1,0:T(8,128)(2,1)S(1)}, u32[]{:S(2)}, u32[]{:S(2)}) collective-permute-start(bf16[3,8,1152]{2,1,0:T(8,128)(2,1)S(1)} %get-tuple-element.73), channel_id=1, source_target_pairs={{0,4},{4,0},{8,12},{12,8},{1,5},{5,1},{9,13},{13,9},{2,6},{6,2},{1... | collective-permute-start | bytes 165896 | tf_op jit(solution)/shard_map/ppermute | solution.py:70
  45.7 2.2 %collective-permute-done.11.refs_0_ = bf16[3,8,1152]{2,1,0:T(8,128)(2,1)S(1)} collective-permute-done((bf16[3,8,1152]{2,1,0:T(8,128)(2,1)S(1)}, bf16[3,8,1152]{2,1,0:T(8,128)(2,1)S(1)}, u32[]{:S(2)}, u32[]{:S(2)}) %collective-permute-start.11) | collective-permute-done | bytes 55328 | tf_op jit(solution)/shard_map/ppermute | solution.py:70
  47.9 2.1 %collective-permute-done.12.refs_1_ = bf16[3,8,1152]{2,1,0:T(8,128)(2,1)S(1)} collective-permute-done((bf16[3,8,1152]{2,1,0:T(8,128)(2,1)S(1)}, bf16[3,8,1152]{2,1,0:T(8,128)(2,1)S(1)}, u32[]{:S(2)}, u32[]{:S(2)}) %collective-permute-start.12) | collective-permute-done | bytes 55328 | tf_op jit(solution)/shard_map/ppermute | solution.py:70
  50.0 0.0 collective-permute-done.13.refs_2_
  50.0 1.6 %collective-permute-start.14 = (bf16[3,8,1024]{2,1,0:T(8,128)(2,1)S(1)}, bf16[3,8,1024]{2,1,0:T(8,128)(2,1)S(1)}, u32[]{:S(2)}, u32[]{:S(2)}) collective-permute-start(bf16[3,8,1024]{2,1,0:T(8,128)(2,1)S(1)} %get-tuple-element.76), channel_id=1, source_target_pairs={{0,16},{16,0},{1,17},{17,1},{2,18},{18,2},{3,19},{19,3},{4,20},{20... | collective-permute-start | bytes 147464 | tf_op jit(solution)/shard_map/ppermute | solution.py:70
  51.6 2.6 %collective-permute-done.14.arrived = bf16[3,8,1024]{2,1,0:T(8,128)(2,1)S(1)} collective-permute-done((bf16[3,8,1024]{2,1,0:T(8,128)(2,1)S(1)}, bf16[3,8,1024]{2,1,0:T(8,128)(2,1)S(1)}, u32[]{:S(2)}, u32[]{:S(2)}) %collective-permute-start.14) | collective-permute-done | bytes 49184 | tf_op jit(solution)/shard_map/ppermute | solution.py:70
  54.2 0.7 %last.1 = (bf16[6,2048]{1,0:T(8,128)(2,1)}, f32[4,1536]{1,0:T(4,128)}, f32[4]{0:T(128)}) custom-call(f32[16,1024]{1,0:T(8,128)S(1)} %get-tuple-element.74.own, f32[8,128]{1,0:T(8,128)S(1)} %get-tuple-element.75.own_squares, bf16[3,8,1024]{2,1,0:T(8,128)(2,1)S(1)} %collective-permute-done.14.arrived, f32[4,768]{1,0:T(4,128)S(1)} %get-tuple-element.77.grads), custom_call_target="tpu_custom_call" | custom-call | flops 1000 | bytes 1000 | tf_op jit(solution)/shard_map/last/pallas_call | solution.py:83
  (3 shorter events, 0.1 us)
Async XLA Ops:
  1.4 9.0 %collective-permute-start = (bf16[3,8,1024]{2,1,0:T(8,128)(2,1)S(1)}, bf16[3,8,1024]{2,1,0:T(8,128)(2,1)S(1)}, u32[]{:S(2)}, u32[]{:S(2)}) collective-permute-start(bf16[3,8,1024]{2,1,0:T(8,128)(2,1)S(1)} %pack.1.own), channel_id=1, source_target_pairs={{0,8},{4,12},{8,0},{12,4},{1,9},{5,13},{9,1},{13,5},{2,10},{6,14},... | collective-permute-start | bytes 147464 | tf_op jit(solution)/shard_map/ppermute | solution.py:70
  10.5 7.7 %collective-permute-start.2 = (bf16[7,8,1024]{2,1,0:T(8,128)(2,1)S(1)}, bf16[7,8,1024]{2,1,0:T(8,128)(2,1)S(1)}, u32[]{:S(2)}, u32[]{:S(2)}) collective-permute-start(bf16[7,8,1024]{2,1,0:T(8,128)(2,1)S(1)} %get-tuple-element.43.refs_3_.refs_4_), channel_id=1, source_target_pairs={{0,16},{16,0},{1,17},{17,1},{2,18},{18,2},{3,19},{19,3},{4,20},{20... | collective-permute-start | bytes 344072 | tf_op jit(solution)/shard_map/ppermute | solution.py:70
  12.0 6.1 %collective-permute-start.3 = (bf16[6,8,1024]{2,1,0:T(8,128)(2,1)S(1)}, bf16[6,8,1024]{2,1,0:T(8,128)(2,1)S(1)}, u32[]{:S(2)}, u32[]{:S(2)}) collective-permute-start(bf16[6,8,1024]{2,1,0:T(8,128)(2,1)S(1)} %get-tuple-element.44.refs_3_), channel_id=1, source_target_pairs={{0,20},{4,16},{8,28},{12,24},{16,4},{20,0},{24,12},{28,8},{1,21},{... | collective-permute-start | bytes 294920 | tf_op jit(solution)/shard_map/ppermute | solution.py:70
  13.6 4.6 %collective-permute-start.1 = (bf16[6,8,1024]{2,1,0:T(8,128)(2,1)S(1)}, bf16[6,8,1024]{2,1,0:T(8,128)(2,1)S(1)}, u32[]{:S(2)}, u32[]{:S(2)}) collective-permute-start(bf16[6,8,1024]{2,1,0:T(8,128)(2,1)S(1)} %get-tuple-element.44.refs_3_), channel_id=1, source_target_pairs={{0,4},{4,0},{8,12},{12,8},{1,5},{5,1},{9,13},{13,9},{2,6},{6,2},{1... | collective-permute-start | bytes 294920 | tf_op jit(solution)/shard_map/ppermute | solution.py:70
  21.1 2.1 %collective-permute-start.4 = (f32[3,48,768]{2,1,0:T(8,128)S(1)}, f32[3,48,768]{2,1,0:T(8,128)S(1)}, u32[]{:S(2)}, u32[]{:S(2)}) collective-permute-start(f32[3,48,768]{2,1,0:T(8,128)S(1)} %get-tuple-element.57), channel_id=1, source_target_pairs={{0,1},{1,0},{2,3},{3,2},{4,5},{5,4},{6,7},{7,6},{8,9},{9,8},{10,11... | collective-permute-start | bytes 1327112 | tf_op jit(solution)/shard_map/ppermute | solution.py:70
  23.3 7.9 %collective-permute-start.6 = (bf16[3,48,768]{2,1,0:T(8,128)(2,1)S(1)}, bf16[3,48,768]{2,1,0:T(8,128)(2,1)S(1)}, u32[]{:S(2)}, u32[]{:S(2)}) collective-permute-start(bf16[3,48,768]{2,1,0:T(8,128)(2,1)S(1)} %join.1.refs_8_), channel_id=1, source_target_pairs={{0,2},{1,3},{2,0},{3,1},{4,6},{5,7},{6,4},{7,5},{8,10},{9,11},{10,... | collective-permute-start | bytes 663560 | tf_op jit(solution)/shard_map/ppermute | solution.py:70
  27.7 3.4 %collective-permute-start.5 = (bf16[3,48,768]{2,1,0:T(8,128)(2,1)S(1)}, bf16[3,48,768]{2,1,0:T(8,128)(2,1)S(1)}, u32[]{:S(2)}, u32[]{:S(2)}) collective-permute-start(bf16[3,48,768]{2,1,0:T(8,128)(2,1)S(1)} %get-tuple-element.61), channel_id=1, source_target_pairs={{0,1},{1,0},{2,3},{3,2},{4,5},{5,4},{6,7},{7,6},{8,9},{9,8},{10,11... | collective-permute-start | bytes 663560 | tf_op jit(solution)/shard_map/ppermute | solution.py:70
  28.0 3.2 %copy-start = (f32[6144]{0:T(1024)S(1)}, f32[6144]{0:T(1024)}, u32[]{:S(2)}) copy-start(f32[6144]{0:T(1024)} %param.12) | copy-start | bytes 73732
  31.5 6.0 %collective-permute-start.7 = (bf16[112,768]{1,0:T(8,128)(2,1)S(1)}, bf16[112,768]{1,0:T(8,128)(2,1)S(1)}, u32[]{:S(2)}, u32[]{:S(2)}) collective-permute-start(bf16[112,768]{1,0:T(8,128)(2,1)S(1)} %get-tuple-element.63.message.refs_0_), channel_id=1, source_target_pairs={{0,2},{1,3},{2,0},{3,1},{4,6},{5,7},{6,4},{7,5},{8,10},{9,11},{10,... | collective-permute-start | bytes 516104 | tf_op jit(solution)/shard_map/ppermute | solution.py:70
  33.0 2.3 %collective-permute-start.8 = (bf16[64,768]{1,0:T(8,128)(2,1)S(1)}, bf16[64,768]{1,0:T(8,128)(2,1)S(1)}, u32[]{:S(2)}, u32[]{:S(2)}) collective-permute-start(bf16[64,768]{1,0:T(8,128)(2,1)S(1)} %get-tuple-element.64), channel_id=1, source_target_pairs={{0,1},{1,0},{2,3},{3,2},{4,5},{5,4},{6,7},{7,6},{8,9},{9,8},{10,11... | collective-permute-start | bytes 294920 | tf_op jit(solution)/shard_map/ppermute | solution.py:70
  33.0 2.3 %collective-permute-start.9 = (bf16[48,768]{1,0:T(8,128)(2,1)S(1)}, bf16[48,768]{1,0:T(8,128)(2,1)S(1)}, u32[]{:S(2)}, u32[]{:S(2)}) collective-permute-start(bf16[48,768]{1,0:T(8,128)(2,1)S(1)} %get-tuple-element.65), channel_id=1, source_target_pairs={{0,1},{1,0},{2,3},{3,2},{4,5},{5,4},{6,7},{7,6},{8,9},{9,8},{10,11... | collective-permute-start | bytes 221192 | tf_op jit(solution)/shard_map/ppermute | solution.py:70
  37.5 1.8 %collective-permute-start.10 = (bf16[112,768]{1,0:T(8,128)(2,1)S(1)}, bf16[112,768]{1,0:T(8,128)(2,1)S(1)}, u32[]{:S(2)}, u32[]{:S(2)}) collective-permute-start(bf16[112,768]{1,0:T(8,128)(2,1)S(1)} %collective-permute-done.7.message.refs_2_), channel_id=1, source_target_pairs={{0,1},{1,0},{2,3},{3,2},{4,5},{5,4},{6,7},{7,6},{8,9},{9,8},{10,11... | collective-permute-start | bytes 516104 | tf_op jit(solution)/shard_map/ppermute | solution.py:70
  41.3 6.6 %collective-permute-start.11 = (bf16[3,8,1152]{2,1,0:T(8,128)(2,1)S(1)}, bf16[3,8,1152]{2,1,0:T(8,128)(2,1)S(1)}, u32[]{:S(2)}, u32[]{:S(2)}) collective-permute-start(bf16[3,8,1152]{2,1,0:T(8,128)(2,1)S(1)} %get-tuple-element.71), channel_id=1, source_target_pairs={{0,12},{4,8},{8,4},{12,0},{1,13},{5,9},{9,5},{13,1},{2,14},{6,10},... | collective-permute-start | bytes 165896 | tf_op jit(solution)/shard_map/ppermute | solution.py:70
  42.5 7.5 %collective-permute-start.12 = (bf16[3,8,1152]{2,1,0:T(8,128)(2,1)S(1)}, bf16[3,8,1152]{2,1,0:T(8,128)(2,1)S(1)}, u32[]{:S(2)}, u32[]{:S(2)}) collective-permute-start(bf16[3,8,1152]{2,1,0:T(8,128)(2,1)S(1)} %get-tuple-element.72), channel_id=1, source_target_pairs={{0,8},{4,12},{8,0},{12,4},{1,9},{5,13},{9,1},{13,5},{2,10},{6,14},... | collective-permute-start | bytes 165896 | tf_op jit(solution)/shard_map/ppermute | solution.py:70
  44.2 5.8 %collective-permute-start.13 = (bf16[3,8,1152]{2,1,0:T(8,128)(2,1)S(1)}, bf16[3,8,1152]{2,1,0:T(8,128)(2,1)S(1)}, u32[]{:S(2)}, u32[]{:S(2)}) collective-permute-start(bf16[3,8,1152]{2,1,0:T(8,128)(2,1)S(1)} %get-tuple-element.73), channel_id=1, source_target_pairs={{0,4},{4,0},{8,12},{12,8},{1,5},{5,1},{9,13},{13,9},{2,6},{6,2},{1... | collective-permute-start | bytes 165896 | tf_op jit(solution)/shard_map/ppermute | solution.py:70
  50.0 4.2 %collective-permute-start.14 = (bf16[3,8,1024]{2,1,0:T(8,128)(2,1)S(1)}, bf16[3,8,1024]{2,1,0:T(8,128)(2,1)S(1)}, u32[]{:S(2)}, u32[]{:S(2)}) collective-permute-start(bf16[3,8,1024]{2,1,0:T(8,128)(2,1)S(1)} %get-tuple-element.76), channel_id=1, source_target_pairs={{0,16},{16,0},{1,17},{17,1},{2,18},{18,2},{3,19},{19,3},{4,20},{20... | collective-permute-start | bytes 147464 | tf_op jit(solution)/shard_map/ppermute | solution.py:70

commit v14 on v10

--- a/solution.py
+++ b/solution.py
@@ -103,16 +103,22 @@
         out[k] = stage[8 * k : 8 * k + 8, :].astype(jnp.bfloat16)
 
 
-def keys_kernel(share, ids, marks):
-    position = lax.axis_index("wide")
-    row = lax.broadcasted_iota(jnp.int32, (8, 128), 0)
+def fetch_ids(ids_in, marks, ids, sem):
+    return pltpu.make_async_copy(ids_in, ids, sem.at[0])
+
+
+def keys_kernel(share, ids_in, marks, ids, sem):
+    fetch_ids(ids_in, marks, ids, sem).wait()
+    position, count = lax.axis_index("wide"), ids.shape[1]
+    shape = (8, count)
+    token, row = (lax.broadcasted_iota(jnp.int32, shape, axis) for axis in (1, 0))
     keys = []
-    for k in range(WIDE * share // 8):
-        key = jnp.zeros((8, 128), jnp.int32)
-        for r in range(8):
-            block, j = divmod(8 * k + r, share)
-            key = jnp.where(row == r, ids[(position ^ block) * share + j], key)
-        keys.append(key.astype(jnp.float32))
+    for base in range(0, WIDE * share, 8):
+        at = row + base
+        block = sum((at >= share * i).astype(jnp.int32) for i in range(1, WIDE))
+        own = token == (position ^ block) * share + (at - block * share)
+        key = jnp.sum(jnp.where(own, ids[...].astype(jnp.float32), 0.0), axis=1, keepdims=True)
+        keys.append(jnp.broadcast_to(key, (8, 128)))
     keys.append(jnp.zeros((8, marks.shape[1] - 128 * len(keys)), jnp.float32))
     marks[...] = jnp.concatenate(keys, axis=1).astype(jnp.bfloat16)
 
@@ -125,7 +131,7 @@
     marked[2 * slabs] = marks[...]
 
 
-WIDE, NEXT, FAR = 4, 1, 3
+WIDE, NEXT, FAR = 4, 1, 2
 GATE, UP, DOWN = range(3)
 WHOLE_STRIP = (GATE, UP, DOWN)
 CHUNKS = 4
@@ -155,18 +161,21 @@
         copy.wait()
 
 
-def loading(body, pieces, groups, outs):
+def loading(body, pieces, groups, outs, own_copy=None):
     count = len(pieces)
 
     def kernel(*refs):
         sources, rest = refs[:3], refs[3:]
         at = len(rest) - outs[1] - 1 - count
         targets, sem = rest[at : at + count], rest[at + count + outs[1]]
+        own = rest[:at] + rest[at + count : at + count + outs[1]]
+        if own_copy is not None:
+            own_copy(*own).start()
         copies = start_loads(pieces, groups, sources, targets, sem)
 
         @pl.when(lax.axis_index("narrow") >= 0)
         def _():
-            body(*rest[:at], *rest[at + count : at + count + outs[1]])
+            body(*own)
 
         for copy in copies:
             copy.wait()
@@ -176,10 +185,8 @@
 
 def strip_parts(tokens, cotans, gate, up, down, put):
     tile = 256
-
-    @pl.loop(0, gate.shape[1] // tile)
-    def _(i):
-        span = pl.ds(pl.multiple_of(i * tile, tile), tile)
+    for start in range(0, gate.shape[1], tile):
+        span = slice(start, start + tile)
         put(GATE, span, jnp.dot(tokens[...], gate[:, span], preferred_element_type=jnp.float32))
         put(UP, span, jnp.dot(tokens[...], up[:, span], preferred_element_type=jnp.float32))
         put(DOWN, span, contract_rows(cotans[...], down[span, :]))
@@ -221,13 +228,11 @@
     sources, (tokens, cotans, up, down) = refs[:3], refs[3:7]
     out, gate, sem = refs[-3:]
     copies = start_loads([(GATE, 0)], groups, sources, [gate], sem)
-    tile = 256
-
-    @pl.loop(0, up.shape[1] // tile)
-    def _(i):
-        span = pl.ds(pl.multiple_of(i * tile, tile), tile)
-        out[UP, :, span] = jnp.dot(tokens[...], up[:, span], preferred_element_type=jnp.float32)
-        out[DOWN, :, span] = contract_rows(cotans[...], down[span, :])
+
+    @pl.when(lax.axis_index("narrow") >= 0)
+    def _():
+        out[UP] = jnp.dot(tokens[...], up[...], preferred_element_type=jnp.float32)
+        out[DOWN] = contract_rows(cotans[...], down[...])
 
     for copy in copies:
         copy.wait()
@@ -418,9 +423,9 @@
         )
         kept.update(zip(pieces, arrays))
 
-    def call_loading(body, name, pieces, outs, args, scratch=(), spaces=None):
+    def call_loading(body, name, pieces, outs, args, scratch=(), spaces=None, own_copy=None):
         made = call(
-            loading(body, pieces, groups, (len(outs), len(outs) + len(scratch))),
+            loading(body, pieces, groups, (len(outs), len(outs) + len(scratch)), own_copy),
             name,
             [weight_shapes[kind] for kind, _ in pieces] + outs,
             list(weights) + args,
@@ -446,8 +451,10 @@
         "load_a",
         [(kind, 3) for kind in WHOLE_STRIP],
         [pltpu.VMEM((8, side), bf16)],
-        [pltpu.with_memory_space_constraint(seq_ids, pltpu.HBM)],
-        spaces={3: pltpu.SMEM},
+        [pltpu.with_memory_space_constraint(seq_ids[None, :], pltpu.HBM)],
+        [pltpu.VMEM((1, half), jnp.int32), pltpu.SemaphoreType.DMA((1,))],
+        {3: pltpu.HBM},
+        fetch_ids,
     )
     pair, marked = call(
         relay_kernel,

time: 56 us -> 53.3 us (0.952)
  Pallas kernels: 28.2 us -> 27.2 us
  waiting for transfers between devices: 9.43 us -> 8.53 us
  starting transfers between devices: 17.3 us -> 16.5 us
    pallas_call x16, Pallas kernels: 28.2 us -> 27.2 us  [call(): pl.pallas_call(body, out_shape=outs, in_specs=[pl.BlockSpec(memory_space=...]
    ppermute x15, waiting for transfers between devices: 9.43 us -> 8.53 us  [exchange(): return lax.ppermute(array, axes, [(i, i ^ step) for i in range(size)])]
    ppermute x15, starting transfers between devices: 17.3 us -> 16.5 us  [exchange(): return lax.ppermute(array, axes, [(i, i ^ step) for i in range(size)])]
  transfers between devices with their start and end apart: 15 -> 15, of which waited for: 6 -> 7; matrix products, arithmetic and copies ran while one was open for 0% -> 0% of each run, Pallas kernels for 39% -> 39%
where the time goes in v14:
time: 53.3 us; the launch traced here: 53.1 us
  Pallas kernels  27.2 us (51%)
  starting transfers between devices  16.5 us (31%)
  waiting for transfers between devices  8.53 us (16%)
  between operations  0.94 us (2%)
    pallas_call x16, Pallas kernels, call(): pl.pallas_call(body, out_shape=outs, in_specs=[pl.BlockSpec(memory_space=...  27.2 us
    ppermute x15, starting transfers between devices, exchange(): return lax.ppermute(array, axes, [(i, i ^ step) for i in range(size)])  16.5 us
    ppermute x15, waiting for transfers between devices, exchange(): return lax.ppermute(array, axes, [(i, i ^ step) for i in range(size)])  8.53 us
  transfers between devices with their start and end apart: 15, of which 7 were waited for; matrix products, arithmetic and copies ran while one was open for 0% of the time, Pallas kernels for 39%

profile of v14, /device:TPU:0, one launch (start us, length us, event | category | flops | bytes accessed | tf_op | source)
XLA Modules:
  0.0 53.1 jit_solution(4647139155971655899)
XLA Ops:
  0.6 0.8 %pack.1.own = bf16[3,8,1024]{2,1,0:T(8,128)(2,1)S(1)} custom-call(bf16[6,2048]{1,0:T(8,128)(2,1)} %inputs.1, bf16[6,2048]{1,0:T(8,128)(2,1)} %cotangent.1), custom_call_target="tpu_custom_call" | custom-call | flops 1000 | bytes 1000 | tf_op jit(solution)/shard_map/pack/pallas_call | solution.py:83
  1.4 4.1 %collective-permute-start = (bf16[3,8,1024]{2,1,0:T(8,128)(2,1)S(1)}, bf16[3,8,1024]{2,1,0:T(8,128)(2,1)S(1)}, u32[]{:S(2)}, u32[]{:S(2)}) collective-permute-start(bf16[3,8,1024]{2,1,0:T(8,128)(2,1)S(1)} %pack.1.own), channel_id=1, source_target_pairs={{0,8},{4,12},{8,0},{12,4},{1,9},{5,13},{9,1},{13,5},{2,10},{6,14},... | collective-permute-start | bytes 147464 | tf_op jit(solution)/shard_map/ppermute | solution.py:70
  5.5 3.9 %load_a.1 = (bf16[2048,768]{1,0:T(8,128)(2,1)S(1)}, bf16[2048,768]{1,0:T(8,128)(2,1)S(1)}, bf16[768,2048]{1,0:T(8,128)(2,1)S(1)}, bf16[8,1024]{1,0:T(8,128)(2,1)S(1)}) custom-call(bf16[2048,6144]{1,0:T(8,128)(2,1)} %refs_0_.11, bf16[2048,6144]{1,0:T(8,128)(2,1)} %refs_1_.11, bf16[6144,2048]{1,0:T(8,128)(2,1)} %refs_2_.11, s32[1,24]{1,0:T(1,128)} %bitcast.3), custom_call_target="tpu_custom_call" | custom-call | flops 1000 | bytes 1000 | tf_op jit(solution)/shard_map/load_a/pallas_call | solution.py:83
  9.4 0.0 collective-permute-done.far
  9.4 1.6 %collective-permute-start.2 = (bf16[7,8,1024]{2,1,0:T(8,128)(2,1)S(1)}, bf16[7,8,1024]{2,1,0:T(8,128)(2,1)S(1)}, u32[]{:S(2)}, u32[]{:S(2)}) collective-permute-start(bf16[7,8,1024]{2,1,0:T(8,128)(2,1)S(1)} %get-tuple-element.43.refs_3_.refs_4_), channel_id=1, source_target_pairs={{0,16},{16,0},{1,17},{17,1},{2,18},{18,2},{3,19},{19,3},{4,20},{20... | collective-permute-start | bytes 344072 | tf_op jit(solution)/shard_map/ppermute | solution.py:70
  11.0 1.5 %collective-permute-start.3 = (bf16[6,8,1024]{2,1,0:T(8,128)(2,1)S(1)}, bf16[6,8,1024]{2,1,0:T(8,128)(2,1)S(1)}, u32[]{:S(2)}, u32[]{:S(2)}) collective-permute-start(bf16[6,8,1024]{2,1,0:T(8,128)(2,1)S(1)} %get-tuple-element.44.refs_3_), channel_id=1, source_target_pairs={{0,20},{4,16},{8,28},{12,24},{16,4},{20,0},{24,12},{28,8},{1,21},{... | collective-permute-start | bytes 294920 | tf_op jit(solution)/shard_map/ppermute | solution.py:70
  12.6 0.4 collective-permute-start.1
  13.0 3.8 %load_b.1 = (bf16[2048,768]{1,0:T(8,128)(2,1)S(1)}, bf16[2048,768]{1,0:T(8,128)(2,1)S(1)}, bf16[768,2048]{1,0:T(8,128)(2,1)S(1)}) custom-call(bf16[2048,6144]{1,0:T(8,128)(2,1)} %refs_0_.11, bf16[2048,6144]{1,0:T(8,128)(2,1)} %refs_1_.11, bf16[6144,2048]{1,0:T(8,128)(2,1)} %refs_2_.11, bf16[6,8,1024]{2,1,0:T(8,128)(2,1)S(1)} %get-tuple-element.44.refs_3_), custom_call_target="tpu_custom_call" | custom-call | flops 1000 | bytes 1000 | tf_op jit(solution)/shard_map/load_b/pallas_call | solution.py:83
  16.8 0.3 collective-permute-done.3.refs_6_
  17.2 0.1 collective-permute-done.1.refs_4_
  17.3 0.0 collective-permute-done.2.refs_5_
  17.3 2.9 %forward_3.1 = (bf16[2048,768]{1,0:T(8,128)(2,1)S(1)}, bf16[768,2048]{1,0:T(8,128)(2,1)S(1)}, bf16[48,2048]{1,0:T(8,128)(2,1)S(1)}, bf16[48,2048]{1,0:T(8,128)(2,1)S(1)}, f32[3,48,768]{2,1,0:T(8,128)S(1)}) custom-call(bf16[2048,6144]{1,0:T(8,128)(2,1)} %refs_0_.11, bf16[2048,6144]{1,0:T(8,128)(2,1)} %refs_1_.11, bf16[6144,2048]{1,0:T(8,128)(2,1)} %refs_2_.11, ...), custom_call_target="tpu_custom_call" | custom-call | flops 1000 | bytes 1000 | tf_op jit(solution)/shard_map/forward_3/pallas_call | solution.py:83
  20.1 0.1 collective-permute-start.4
  20.2 2.0 %forward_2.1 = (bf16[2048,768]{1,0:T(8,128)(2,1)S(1)}, f32[3,48,768]{2,1,0:T(8,128)S(1)}) custom-call(bf16[2048,6144]{1,0:T(8,128)(2,1)} %refs_0_.11, bf16[2048,6144]{1,0:T(8,128)(2,1)} %refs_1_.11, bf16[6144,2048]{1,0:T(8,128)(2,1)} %refs_2_.11, bf16[48,2048]{1,0:T(8,128)(2,1)S(1)} %get-tuple-element.49.refs_3_, ...), custom_call_target="tpu_custom_call" | custom-call | flops 1000 | bytes 1000 | tf_op jit(solution)/shard_map/forward_2/pallas_call | solution.py:83
  22.3 0.0 collective-permute-done.4.arrived
  22.3 1.6 %collective-permute-start.6 = (bf16[3,48,768]{2,1,0:T(8,128)(2,1)S(1)}, bf16[3,48,768]{2,1,0:T(8,128)(2,1)S(1)}, u32[]{:S(2)}, u32[]{:S(2)}) collective-permute-start(bf16[3,48,768]{2,1,0:T(8,128)(2,1)S(1)} %join.1.refs_8_), channel_id=1, source_target_pairs={{0,2},{1,3},{2,0},{3,1},{4,6},{5,7},{6,4},{7,5},{8,10},{9,11},{10,... | collective-permute-start | bytes 663560 | tf_op jit(solution)/shard_map/ppermute | solution.py:70
  23.9 2.9 %forward_1.1 = (bf16[2048,768]{1,0:T(8,128)(2,1)S(1)}, bf16[768,2048]{1,0:T(8,128)(2,1)S(1)}, bf16[3,48,768]{2,1,0:T(8,128)(2,1)S(1)}) custom-call(bf16[2048,6144]{1,0:T(8,128)(2,1)} %refs_0_.11, bf16[2048,6144]{1,0:T(8,128)(2,1)} %refs_1_.11, bf16[6144,2048]{1,0:T(8,128)(2,1)} %refs_2_.11, bf16[48,2048]{1,0:T(8,128)(2,1)S(1)} %get-tuple-element.49.refs_3_, ...), custom_call_target="tpu_custom_call" | custom-call | flops 1000 | bytes 1000 | tf_op jit(solution)/shard_map/forward_1/pallas_call | solution.py:83
  26.8 0.3 collective-permute-start.5
  27.1 0.0 copy-start
  27.1 2.6 %forward_0.1 = (f32[3,48,768]{2,1,0:T(8,128)S(1)}, bf16[2048,768]{1,0:T(8,128)(2,1)S(1)}) custom-call(bf16[2048,6144]{1,0:T(8,128)(2,1)} %refs_0_.11, bf16[2048,6144]{1,0:T(8,128)(2,1)} %refs_1_.11, bf16[6144,2048]{1,0:T(8,128)(2,1)} %refs_2_.11, bf16[48,2048]{1,0:T(8,128)(2,1)S(1)} %get-tuple-element.49.refs_3_, ...), custom_call_target="tpu_custom_call" | custom-call | flops 1000 | bytes 1000 | tf_op jit(solution)/shard_map/forward_0/pallas_call | solution.py:83
  29.6 0.6 %collective-permute-done.6.refs_2_ = bf16[3,48,768]{2,1,0:T(8,128)(2,1)S(1)} collective-permute-done((bf16[3,48,768]{2,1,0:T(8,128)(2,1)S(1)}, bf16[3,48,768]{2,1,0:T(8,128)(2,1)S(1)}, u32[]{:S(2)}, u32[]{:S(2)}) %collective-permute-start.6) | collective-permute-done | bytes 221216 | tf_op jit(solution)/shard_map/ppermute | solution.py:70
  30.2 0.0 collective-permute-done.5.refs_1_
  30.2 0.0 copy-done
  30.2 0.4 middle.1
  30.6 1.5 %collective-permute-start.7 = (bf16[112,768]{1,0:T(8,128)(2,1)S(1)}, bf16[112,768]{1,0:T(8,128)(2,1)S(1)}, u32[]{:S(2)}, u32[]{:S(2)}) collective-permute-start(bf16[112,768]{1,0:T(8,128)(2,1)S(1)} %get-tuple-element.63.message.refs_0_), channel_id=1, source_target_pairs={{0,2},{1,3},{2,0},{3,1},{4,6},{5,7},{6,4},{7,5},{8,10},{9,11},{10,... | collective-permute-start | bytes 516104 | tf_op jit(solution)/shard_map/ppermute | solution.py:70
  32.1 0.0 collective-permute-start.8
  32.1 0.5 collective-permute-start.9
  32.6 1.7 %backward_0.1.before = f32[2048,48]{1,0:T(8,128)S(1)} custom-call(bf16[112,768]{1,0:T(8,128)(2,1)S(1)} %get-tuple-element.63.message.refs_0_, bf16[2048,768]{1,0:T(8,128)(2,1)S(1)} %get-tuple-element.62.refs_6_.gate, bf16[2048,768]{1,0:T(8,128)(2,1)S(1)} %get-tuple-element.58.refs_5_.refs_7_.up), custom_call_target="tpu_custom_call" | custom-call | flops 1000 | bytes 1000 | tf_op jit(solution)/shard_map/backward_0/pallas_call | solution.py:83
  34.3 0.0 collective-permute-done.9.d_up
  34.4 0.0 collective-permute-done.8.d_gate.refs_1_
  34.4 1.8 %backward_1.1.before = f32[2048,48]{1,0:T(8,128)S(1)} custom-call(bf16[64,768]{1,0:T(8,128)(2,1)S(1)} %collective-permute-done.8.d_gate.refs_1_, bf16[48,768]{1,0:T(8,128)(2,1)S(1)} %collective-permute-done.9.d_up, bf16[2048,768]{1,0:T(8,128)(2,1)S(1)} %get-tuple-element.51.refs_5_.refs_8_.gate, bf16[2048,768]{1,0:T(8,128)(2,1)S(1)} %get-tuple-element.54.refs_6_.refs_9_.up, ...), custom_call_target="tpu_custom_call" | custom-call | flops 1000 | bytes 1000 | tf_op jit(solution)/shard_map/backward_1/pallas_call | solution.py:83
  36.1 0.4 collective-permute-done.7.message.refs_2_
  36.6 0.0 collective-permute-start.10
  36.6 1.8 %backward_2.1.before = f32[2048,48]{1,0:T(8,128)S(1)} custom-call(bf16[112,768]{1,0:T(8,128)(2,1)S(1)} %collective-permute-done.7.message.refs_2_, bf16[2048,768]{1,0:T(8,128)(2,1)S(1)} %get-tuple-element.48.refs_10_.refs_5_.gate, bf16[2048,768]{1,0:T(8,128)(2,1)S(1)} %get-tuple-element.52.refs_6_.refs_11_.up, f32[2048,48]{1,0:T(8,128)S(1)} %backward_1.1.before), custom_call_target="tpu_custom_call" | custom-call | flops 1000 | bytes 1000 | tf_op jit(solution)/shard_map/backward_2/pallas_call | solution.py:83
  38.4 0.0 collective-permute-done.10.message
  38.4 1.9 %backward_3.1 = (f32[24,1024]{1,0:T(8,128)S(1)}, f32[8,128]{1,0:T(8,128)S(1)}, bf16[3,8,1152]{2,1,0:T(8,128)(2,1)S(1)}, bf16[4,8,1024]{2,1,0:T(8,128)(2,1)S(1)}, bf16[3,8,1152]{2,1,0:T(8,128)(2,1)S(1)}) custom-call(bf16[112,768]{1,0:T(8,128)(2,1)S(1)} %collective-permute-done.10.message, bf16[2048,768]{1,0:T(8,128)(2,1)S(1)} %get-tuple-element.45.refs_7_.refs_12_.gate, ...), custom_call_target="tpu_custom_call" | custom-call | flops 1000 | bytes 1000 | tf_op jit(solution)/shard_map/backward_3/pallas_call | solution.py:83
  40.3 1.6 %collective-permute-start.12 = (bf16[4,8,1024]{2,1,0:T(8,128)(2,1)S(1)}, bf16[4,8,1024]{2,1,0:T(8,128)(2,1)S(1)}, u32[]{:S(2)}, u32[]{:S(2)}) collective-permute-start(bf16[4,8,1024]{2,1,0:T(8,128)(2,1)S(1)} %get-tuple-element.72), channel_id=1, source_target_pairs={{0,16},{16,0},{1,17},{17,1},{2,18},{18,2},{3,19},{19,3},{4,20},{20... | collective-permute-start | bytes 196616 | tf_op jit(solution)/shard_map/ppermute | solution.py:70
  41.9 1.3 %collective-permute-start.11 = (bf16[3,8,1152]{2,1,0:T(8,128)(2,1)S(1)}, bf16[3,8,1152]{2,1,0:T(8,128)(2,1)S(1)}, u32[]{:S(2)}, u32[]{:S(2)}) collective-permute-start(bf16[3,8,1152]{2,1,0:T(8,128)(2,1)S(1)} %get-tuple-element.71), channel_id=1, source_target_pairs={{0,20},{4,16},{8,28},{12,24},{16,4},{20,0},{24,12},{28,8},{1,21},{... | collective-permute-start | bytes 165896 | tf_op jit(solution)/shard_map/ppermute | solution.py:70
  43.2 0.6 %collective-permute-start.13 = (bf16[3,8,1152]{2,1,0:T(8,128)(2,1)S(1)}, bf16[3,8,1152]{2,1,0:T(8,128)(2,1)S(1)}, u32[]{:S(2)}, u32[]{:S(2)}) collective-permute-start(bf16[3,8,1152]{2,1,0:T(8,128)(2,1)S(1)} %get-tuple-element.73), channel_id=1, source_target_pairs={{0,4},{4,0},{8,12},{12,8},{1,5},{5,1},{9,13},{13,9},{2,6},{6,2},{1... | collective-permute-start | bytes 165896 | tf_op jit(solution)/shard_map/ppermute | solution.py:70
  43.9 3.4 %collective-permute-done.11.diagonal = bf16[3,8,1152]{2,1,0:T(8,128)(2,1)S(1)} collective-permute-done((bf16[3,8,1152]{2,1,0:T(8,128)(2,1)S(1)}, bf16[3,8,1152]{2,1,0:T(8,128)(2,1)S(1)}, u32[]{:S(2)}, u32[]{:S(2)}) %collective-permute-start.11) | collective-permute-done | bytes 55328 | tf_op jit(solution)/shard_map/ppermute | solution.py:70
  47.3 0.1 collective-permute-done.13.beside
  47.4 0.0 collective-permute-done.12.across
  47.4 1.4 %collective-permute-start.14 = (bf16[2,8,1024]{2,1,0:T(8,128)(2,1)S(1)}, bf16[2,8,1024]{2,1,0:T(8,128)(2,1)S(1)}, u32[]{:S(2)}, u32[]{:S(2)}) collective-permute-start(bf16[2,8,1024]{2,1,0:T(8,128)(2,1)S(1)} %get-tuple-element.75), channel_id=1, source_target_pairs={{0,8},{4,12},{8,0},{12,4},{1,9},{5,13},{9,1},{13,5},{2,10},{6,14},... | collective-permute-start | bytes 98312 | tf_op jit(solution)/shard_map/ppermute | solution.py:70
  48.8 3.5 %collective-permute-done.14.arrived = bf16[2,8,1024]{2,1,0:T(8,128)(2,1)S(1)} collective-permute-done((bf16[2,8,1024]{2,1,0:T(8,128)(2,1)S(1)}, bf16[2,8,1024]{2,1,0:T(8,128)(2,1)S(1)}, u32[]{:S(2)}, u32[]{:S(2)}) %collective-permute-start.14) | collective-permute-done | bytes 32800 | tf_op jit(solution)/shard_map/ppermute | solution.py:70
  52.3 0.7 %last.1 = (bf16[6,2048]{1,0:T(8,128)(2,1)}, f32[4,1536]{1,0:T(4,128)}, f32[4]{0:T(128)}) custom-call(f32[16,1024]{1,0:T(8,128)S(1)} %get-tuple-element.74.own, bf16[2,8,1024]{2,1,0:T(8,128)(2,1)S(1)} %collective-permute-done.14.arrived, f32[4,768]{1,0:T(4,128)S(1)} %get-tuple-element.76.grads, f32[4,768]{1,0:T(4,128)S(1)} %get-tuple-element.77.other_grads), custom_call_target="tpu_custom_call" | custom-call | flops 1000 | bytes 1000 | tf_op jit(solution)/shard_map/last/pallas_call | solution.py:83
  (3 shorter events, 0.1 us)
Async XLA Ops:
  1.4 8.0 %collective-permute-start = (bf16[3,8,1024]{2,1,0:T(8,128)(2,1)S(1)}, bf16[3,8,1024]{2,1,0:T(8,128)(2,1)S(1)}, u32[]{:S(2)}, u32[]{:S(2)}) collective-permute-start(bf16[3,8,1024]{2,1,0:T(8,128)(2,1)S(1)} %pack.1.own), channel_id=1, source_target_pairs={{0,8},{4,12},{8,0},{12,4},{1,9},{5,13},{9,1},{13,5},{2,10},{6,14},... | collective-permute-start | bytes 147464 | tf_op jit(solution)/shard_map/ppermute | solution.py:70
  9.4 7.8 %collective-permute-start.2 = (bf16[7,8,1024]{2,1,0:T(8,128)(2,1)S(1)}, bf16[7,8,1024]{2,1,0:T(8,128)(2,1)S(1)}, u32[]{:S(2)}, u32[]{:S(2)}) collective-permute-start(bf16[7,8,1024]{2,1,0:T(8,128)(2,1)S(1)} %get-tuple-element.43.refs_3_.refs_4_), channel_id=1, source_target_pairs={{0,16},{16,0},{1,17},{17,1},{2,18},{18,2},{3,19},{19,3},{4,20},{20... | collective-permute-start | bytes 344072 | tf_op jit(solution)/shard_map/ppermute | solution.py:70
  11.0 6.1 %collective-permute-start.3 = (bf16[6,8,1024]{2,1,0:T(8,128)(2,1)S(1)}, bf16[6,8,1024]{2,1,0:T(8,128)(2,1)S(1)}, u32[]{:S(2)}, u32[]{:S(2)}) collective-permute-start(bf16[6,8,1024]{2,1,0:T(8,128)(2,1)S(1)} %get-tuple-element.44.refs_3_), channel_id=1, source_target_pairs={{0,20},{4,16},{8,28},{12,24},{16,4},{20,0},{24,12},{28,8},{1,21},{... | collective-permute-start | bytes 294920 | tf_op jit(solution)/shard_map/ppermute | solution.py:70
  12.6 4.7 %collective-permute-start.1 = (bf16[6,8,1024]{2,1,0:T(8,128)(2,1)S(1)}, bf16[6,8,1024]{2,1,0:T(8,128)(2,1)S(1)}, u32[]{:S(2)}, u32[]{:S(2)}) collective-permute-start(bf16[6,8,1024]{2,1,0:T(8,128)(2,1)S(1)} %get-tuple-element.44.refs_3_), channel_id=1, source_target_pairs={{0,4},{4,0},{8,12},{12,8},{1,5},{5,1},{9,13},{13,9},{2,6},{6,2},{1... | collective-permute-start | bytes 294920 | tf_op jit(solution)/shard_map/ppermute | solution.py:70
  20.1 2.1 %collective-permute-start.4 = (f32[3,48,768]{2,1,0:T(8,128)S(1)}, f32[3,48,768]{2,1,0:T(8,128)S(1)}, u32[]{:S(2)}, u32[]{:S(2)}) collective-permute-start(f32[3,48,768]{2,1,0:T(8,128)S(1)} %get-tuple-element.57), channel_id=1, source_target_pairs={{0,1},{1,0},{2,3},{3,2},{4,5},{5,4},{6,7},{7,6},{8,9},{9,8},{10,11... | collective-permute-start | bytes 1327112 | tf_op jit(solution)/shard_map/ppermute | solution.py:70
  22.3 7.9 %collective-permute-start.6 = (bf16[3,48,768]{2,1,0:T(8,128)(2,1)S(1)}, bf16[3,48,768]{2,1,0:T(8,128)(2,1)S(1)}, u32[]{:S(2)}, u32[]{:S(2)}) collective-permute-start(bf16[3,48,768]{2,1,0:T(8,128)(2,1)S(1)} %join.1.refs_8_), channel_id=1, source_target_pairs={{0,2},{1,3},{2,0},{3,1},{4,6},{5,7},{6,4},{7,5},{8,10},{9,11},{10,... | collective-permute-start | bytes 663560 | tf_op jit(solution)/shard_map/ppermute | solution.py:70
  26.8 3.4 %collective-permute-start.5 = (bf16[3,48,768]{2,1,0:T(8,128)(2,1)S(1)}, bf16[3,48,768]{2,1,0:T(8,128)(2,1)S(1)}, u32[]{:S(2)}, u32[]{:S(2)}) collective-permute-start(bf16[3,48,768]{2,1,0:T(8,128)(2,1)S(1)} %get-tuple-element.61), channel_id=1, source_target_pairs={{0,1},{1,0},{2,3},{3,2},{4,5},{5,4},{6,7},{7,6},{8,9},{9,8},{10,11... | collective-permute-start | bytes 663560 | tf_op jit(solution)/shard_map/ppermute | solution.py:70
  27.1 3.2 %copy-start = (f32[6144]{0:T(1024)S(1)}, f32[6144]{0:T(1024)}, u32[]{:S(2)}) copy-start(f32[6144]{0:T(1024)} %param.12) | copy-start | bytes 73732
  30.6 6.0 %collective-permute-start.7 = (bf16[112,768]{1,0:T(8,128)(2,1)S(1)}, bf16[112,768]{1,0:T(8,128)(2,1)S(1)}, u32[]{:S(2)}, u32[]{:S(2)}) collective-permute-start(bf16[112,768]{1,0:T(8,128)(2,1)S(1)} %get-tuple-element.63.message.refs_0_), channel_id=1, source_target_pairs={{0,2},{1,3},{2,0},{3,1},{4,6},{5,7},{6,4},{7,5},{8,10},{9,11},{10,... | collective-permute-start | bytes 516104 | tf_op jit(solution)/shard_map/ppermute | solution.py:70
  32.1 2.3 %collective-permute-start.8 = (bf16[64,768]{1,0:T(8,128)(2,1)S(1)}, bf16[64,768]{1,0:T(8,128)(2,1)S(1)}, u32[]{:S(2)}, u32[]{:S(2)}) collective-permute-start(bf16[64,768]{1,0:T(8,128)(2,1)S(1)} %get-tuple-element.64), channel_id=1, source_target_pairs={{0,1},{1,0},{2,3},{3,2},{4,5},{5,4},{6,7},{7,6},{8,9},{9,8},{10,11... | collective-permute-start | bytes 294920 | tf_op jit(solution)/shard_map/ppermute | solution.py:70
  32.1 2.3 %collective-permute-start.9 = (bf16[48,768]{1,0:T(8,128)(2,1)S(1)}, bf16[48,768]{1,0:T(8,128)(2,1)S(1)}, u32[]{:S(2)}, u32[]{:S(2)}) collective-permute-start(bf16[48,768]{1,0:T(8,128)(2,1)S(1)} %get-tuple-element.65), channel_id=1, source_target_pairs={{0,1},{1,0},{2,3},{3,2},{4,5},{5,4},{6,7},{7,6},{8,9},{9,8},{10,11... | collective-permute-start | bytes 221192 | tf_op jit(solution)/shard_map/ppermute | solution.py:70
  36.6 1.8 %collective-permute-start.10 = (bf16[112,768]{1,0:T(8,128)(2,1)S(1)}, bf16[112,768]{1,0:T(8,128)(2,1)S(1)}, u32[]{:S(2)}, u32[]{:S(2)}) collective-permute-start(bf16[112,768]{1,0:T(8,128)(2,1)S(1)} %collective-permute-done.7.message.refs_2_), channel_id=1, source_target_pairs={{0,1},{1,0},{2,3},{3,2},{4,5},{5,4},{6,7},{7,6},{8,9},{9,8},{10,11... | collective-permute-start | bytes 516104 | tf_op jit(solution)/shard_map/ppermute | solution.py:70
  40.3 7.1 %collective-permute-start.12 = (bf16[4,8,1024]{2,1,0:T(8,128)(2,1)S(1)}, bf16[4,8,1024]{2,1,0:T(8,128)(2,1)S(1)}, u32[]{:S(2)}, u32[]{:S(2)}) collective-permute-start(bf16[4,8,1024]{2,1,0:T(8,128)(2,1)S(1)} %get-tuple-element.72), channel_id=1, source_target_pairs={{0,16},{16,0},{1,17},{17,1},{2,18},{18,2},{3,19},{19,3},{4,20},{20... | collective-permute-start | bytes 196616 | tf_op jit(solution)/shard_map/ppermute | solution.py:70
  41.9 5.4 %collective-permute-start.11 = (bf16[3,8,1152]{2,1,0:T(8,128)(2,1)S(1)}, bf16[3,8,1152]{2,1,0:T(8,128)(2,1)S(1)}, u32[]{:S(2)}, u32[]{:S(2)}) collective-permute-start(bf16[3,8,1152]{2,1,0:T(8,128)(2,1)S(1)} %get-tuple-element.71), channel_id=1, source_target_pairs={{0,20},{4,16},{8,28},{12,24},{16,4},{20,0},{24,12},{28,8},{1,21},{... | collective-permute-start | bytes 165896 | tf_op jit(solution)/shard_map/ppermute | solution.py:70
  43.2 4.2 %collective-permute-start.13 = (bf16[3,8,1152]{2,1,0:T(8,128)(2,1)S(1)}, bf16[3,8,1152]{2,1,0:T(8,128)(2,1)S(1)}, u32[]{:S(2)}, u32[]{:S(2)}) collective-permute-start(bf16[3,8,1152]{2,1,0:T(8,128)(2,1)S(1)} %get-tuple-element.73), channel_id=1, source_target_pairs={{0,4},{4,0},{8,12},{12,8},{1,5},{5,1},{9,13},{13,9},{2,6},{6,2},{1... | collective-permute-start | bytes 165896 | tf_op jit(solution)/shard_map/ppermute | solution.py:70
  47.4 4.9 %collective-permute-start.14 = (bf16[2,8,1024]{2,1,0:T(8,128)(2,1)S(1)}, bf16[2,8,1024]{2,1,0:T(8,128)(2,1)S(1)}, u32[]{:S(2)}, u32[]{:S(2)}) collective-permute-start(bf16[2,8,1024]{2,1,0:T(8,128)(2,1)S(1)} %get-tuple-element.75), channel_id=1, source_target_pairs={{0,8},{4,12},{8,0},{12,4},{1,9},{5,13},{9,1},{13,5},{2,10},{6,14},... | collective-permute-start | bytes 98312 | tf_op jit(solution)/shard_map/ppermute | solution.py:70

commit v15 on v14

--- a/solution.py
+++ b/solution.py
@@ -68,6 +68,17 @@
     axes = axis if isinstance(axis, tuple) else (axis,)
     size = math.prod(lax.axis_size(name) for name in axes)
     return lax.ppermute(array, axes, [(i, i ^ step) for i in range(size)])
+
+
+def exchange_by_core(array, even, odd):
+    axes = ("groups", "wide", "narrow")
+    narrow = lax.axis_size("narrow")
+    size = math.prod(lax.axis_size(name) for name in axes)
+    return lax.ppermute(array, axes, [(i, i ^ ((odd if i % 2 else even) * narrow)) for i in range(size)])
+
+
+def on_odd_core():
+    return lax.axis_index("narrow") % 2 == 1
 
 
 def held(array):
@@ -205,17 +216,22 @@
     out[...] = (own[...] + arrived[...]).astype(out.dtype)
 
 
-def first_kernel(share, marked, beside, other, diagonal, gate, up, down, *refs):
+def first_kernel(share, marked, one, two, diagonal, gate, up, down, *refs):
     tokens, cotans, part, rows, cots = refs[-5:]
     slabs, half = 4 * share // 8, rows.shape[1] // 2
+    odd = on_odd_core()
+
+    def slabs_of(ref, i):
+        return ref[i * slabs : (i + 1) * slabs].astype(jnp.float32).reshape(4 * share, half)
+
     for source, places in (
-        (marked, (0, FAR)),
-        (beside, (NEXT, FAR ^ NEXT)),
-        (other, (WIDE, WIDE + FAR)),
-        (diagonal, (WIDE + NEXT, WIDE + (FAR ^ NEXT))),
+        (lambda i: slabs_of(marked, i), (0, FAR)),
+        (lambda i: jnp.where(odd, slabs_of(one, i), slabs_of(two, i)), (NEXT, FAR ^ NEXT)),
+        (lambda i: jnp.where(odd, slabs_of(two, i), slabs_of(one, i)), (WIDE, WIDE + FAR)),
+        (lambda i: slabs_of(diagonal, i), (WIDE + NEXT, WIDE + (FAR ^ NEXT))),
     ):
         for i, place in enumerate(places):
-            packed = source[i * slabs : (i + 1) * slabs].astype(jnp.float32).reshape(4 * share, half)
+            packed = source(i)
             for j, target in enumerate((rows, rows, cots, cots)):
                 span = slice((j % 2) * half, (j % 2 + 1) * half)
                 target[place * share : (place + 1) * share, span] = packed[j * share : (j + 1) * share]
@@ -240,7 +256,7 @@
 
 
 def middle_kernel(groups, *refs):
-    own, arrived, crossed, scale, relayed, other_relayed = refs[:6]
+    own, arrived, crossed, scale, marked, one, two = refs[:7]
     message, near_gate, near_up, grads, other_grads, stage = refs[-6:]
     _, tokens, width = own.shape
     narrow, group = lax.axis_index("narrow"), lax.axis_index("groups")
@@ -252,8 +268,9 @@
     near_gate[0:tokens, :] = d_gate
     near_up[...] = d_up
     half = tokens // groups
-    for side, (source, target) in enumerate(((relayed, grads), (other_relayed, other_grads))):
-        marks = source[source.shape[0] - 1].astype(jnp.float32)
+    own_marks, marks_one, marks_two = (ref[ref.shape[0] - 1].astype(jnp.float32) for ref in (marked, one, two))
+    other_marks = jnp.where(on_odd_core(), marks_two, marks_one)
+    for side, (marks, target) in enumerate(((own_marks, grads), (other_marks, other_grads))):
         seq = jnp.concatenate(
             [
                 jnp.concatenate([marks[:, k * 128 : (k + 1) * 128]] * (width // 128), axis=1)
@@ -311,7 +328,8 @@
 
 
 def backward_last_kernel(share, message, gate, up, before, *refs):
-    others, other_grads, (own, own_squares), sends, (total, stage) = refs[:3], refs[3], refs[4:6], refs[6:9], refs[9:]
+    others, other_grads, (own, own_squares), sends = refs[:3], refs[3], refs[4:6], refs[6:9]
+    total, stage, other_stage = refs[9:]
     tokens, features = total.shape
     side = features // 2
     for start in range(0, features, TILE):
@@ -322,42 +340,52 @@
     own_squares[...] = squares
     tails = split_high(squares)
     slabs = 4 * share // 8
-    for target, group, nearby in zip((own,) + tuple(sends), (0, 0, 1, 1), (0, NEXT, 0, NEXT)):
-        rows = own if target is own else stage
+
+    def pack_rows(rows, group, nearby):
         for i, place in enumerate((nearby, nearby ^ FAR)):
             at = (group * WIDE + place) * share
             for j in range(2):
                 to = (2 * i + j) * share
                 rows[to : to + share, :] = total[at : at + share, j * side : (j + 1) * side]
-        if target is not own:
-            for k in range(slabs):
-                target[k, :, 0:side] = stage[8 * k : 8 * k + 8, :].astype(jnp.bfloat16)
-                if target.shape[2] > side:
-                    tail = tails[k] if k < 2 else jnp.zeros_like(squares)
-                    target[k, :, side:] = tail.astype(jnp.bfloat16)
+
+    one, two, diagonal = sends
+    pack_rows(own, 0, 0)
+    pack_rows(stage, 1, NEXT)
+    for k in range(slabs):
+        diagonal[k, :, 0:side] = stage[8 * k : 8 * k + 8, :].astype(jnp.bfloat16)
+        tail = tails[k] if k < 2 else jnp.zeros_like(squares)
+        diagonal[k, :, side:] = tail.astype(jnp.bfloat16)
+    odd = on_odd_core()
+    pack_rows(stage, 1, 0)
+    pack_rows(other_stage, 0, NEXT)
+    for k in range(slabs):
+        across, beside = stage[8 * k : 8 * k + 8, :], other_stage[8 * k : 8 * k + 8, :]
+        one[k] = jnp.where(odd, beside, across).astype(jnp.bfloat16)
+        two[k] = jnp.where(odd, across, beside).astype(jnp.bfloat16)
     width = other_grads.shape[1]
     stage[0:8, :] = jnp.zeros((8, side), jnp.float32)
     for i, rows in enumerate(split_high(other_grads[...])):
         stage[i * SEQS : (i + 1) * SEQS, 0:width] = rows
     for i, rows in enumerate(tails):
         stage[0:8, width + i * 128 : width + (i + 1) * 128] = rows
-    sends[1][slabs] = stage[0:8, :].astype(jnp.bfloat16)
-
-
-def combine_kernel(share, own, own_squares, diagonal, across, beside, *refs):
+    for target in (one, two):
+        target[slabs] = stage[0:8, :].astype(jnp.bfloat16)
+
+
+def combine_kernel(share, own, own_squares, diagonal, one, two, *refs):
     kept_rows, other_grads, send, total, stage = refs
-    slabs, side = beside.shape[0], own.shape[1]
+    slabs, side = diagonal.shape[0], own.shape[1]
     width = other_grads.shape[1]
     for k in range(slabs):
-        rows = own[8 * k : 8 * k + 8, :] + across[k].astype(jnp.float32)
-        for ref in (beside, diagonal):
-            rows = rows + ref[k, :, 0:side].astype(jnp.float32)
-        total[8 * k : 8 * k + 8, :] = rows
-    tail = across[slabs].astype(jnp.float32)
-    other_grads[...] = tail[0:SEQS, 0:width] + tail[SEQS : 2 * SEQS, 0:width]
-    same, turned = own_squares[...], tail[:, width : width + 128] + tail[:, width + 128 : width + 256]
+        rows = own[8 * k : 8 * k + 8, :] + diagonal[k, :, 0:side].astype(jnp.float32)
+        total[8 * k : 8 * k + 8, :] = rows + one[k].astype(jnp.float32) + two[k].astype(jnp.float32)
+    odd = on_odd_core()
+    tail_one, tail_two = one[slabs].astype(jnp.float32), two[slabs].astype(jnp.float32)
+    across, beside = jnp.where(odd, tail_two, tail_one), jnp.where(odd, tail_one, tail_two)
+    other_grads[...] = across[0:SEQS, 0:width] + across[SEQS : 2 * SEQS, 0:width]
+    same, turned = (tail[:, width : width + 128] + tail[:, width + 128 : width + 256] for tail in (beside, across))
+    same = same + own_squares[...]
     for k in range(2):
-        same = same + beside[k, :, side:].astype(jnp.float32)
         turned = turned + diagonal[k, :, side:].astype(jnp.float32)
     squares = same[0:SEQS] + turned[SEQS : 2 * SEQS]
     count = 2 * share
@@ -463,8 +491,8 @@
         [packed, far, marks],
     )
     diagonal = exchange(pair, ("groups", "wide"), WIDE + NEXT)
-    other_marked = exchange(marked, "groups", 1)
-    beside = exchange(pair, "wide", NEXT)
+    one = exchange_by_core(marked, WIDE, NEXT)
+    two = exchange_by_core(marked, NEXT, WIDE)
     load("load_b", [(kind, 2) for kind in WHOLE_STRIP], [pair])
 
     part = pltpu.VMEM((3, tokens, width), f32)
@@ -474,7 +502,7 @@
         "forward_3",
         [(GATE, 1), (DOWN, 1)],
         [pltpu.VMEM((tokens, features), bf16)] * 2 + [part],
-        [marked, beside, other_marked, diagonal] + hold(3) + hold(2, [GATE]),
+        [marked, one, two, diagonal] + hold(3) + hold(2, [GATE]),
         [pltpu.VMEM((tokens, features), f32)] * 2,
     )
     panel = [tokens_all, cotans_all]
@@ -506,7 +534,7 @@
             pltpu.VMEM((SEQS, width), f32),
             pltpu.VMEM((SEQS, width), f32),
         ],
-        [own_part, near, crossed, ia3_scale[None, :], marked, other_marked] + resident,
+        [own_part, near, crossed, ia3_scale[None, :], marked, one, two] + resident,
         scratch=[pltpu.VMEM((groups * SEQS, width), f32)],
     )
 
@@ -518,28 +546,27 @@
     message_2, sums = lax.optimization_barrier((message_2, sums))
     message_3 = exchange(message_2, "narrow", 1)
     sums = call(backward_next_kernel, "backward_2", total, [message_2] + hold(2, [GATE, UP]) + [sums])
-    block = pltpu.VMEM((slabs, 8, side + 128), bf16)
     own, own_squares, *sends = call(
         functools.partial(backward_last_kernel, share),
         "backward_3",
         [
             pltpu.VMEM((4 * share, side), f32),
             pltpu.VMEM((8, 128), f32),
-            block,
             pltpu.VMEM((slabs + 1, 8, side), bf16),
-            block,
+            pltpu.VMEM((slabs + 1, 8, side), bf16),
+            pltpu.VMEM((slabs, 8, side + 128), bf16),
         ],
         [message_3] + hold(3, [GATE, UP]) + [sums, message, near_gate, message_2, other_grads],
-        scratch=[pltpu.VMEM((tokens, features), f32), pltpu.VMEM((4 * share, side), f32)],
-    )
-    across = exchange(sends[1], "groups", 1)
-    beside = exchange(sends[0], "wide", NEXT)
+        scratch=[pltpu.VMEM((tokens, features), f32)] + [pltpu.VMEM((4 * share, side), f32)] * 2,
+    )
+    one = exchange_by_core(sends[0], WIDE, NEXT)
+    two = exchange_by_core(sends[1], NEXT, WIDE)
     diagonal = exchange(sends[2], ("groups", "wide"), WIDE + NEXT)
     own, other_grads, send = call(
         functools.partial(combine_kernel, share),
         "combine",
         [pltpu.VMEM((16, side), f32), pltpu.VMEM((SEQS, width), f32), pltpu.VMEM((2, 8, side), bf16)],
-        [own, own_squares, diagonal, across, beside],
+        [own, own_squares, diagonal, one, two],
         scratch=[pltpu.VMEM((4 * share, side), f32), pltpu.VMEM((16, side), f32)],
     )
     input_grad, example_grads, norms = call(

time: 53.3 us -> 54.6 us (1.024)
  waiting for transfers between devices: 8.53 us -> 10 us
    ppermute x15 -> x11, starting transfers between devices: 16.5 us -> 10.7 us  [exchange(): return lax.ppermute(array, axes, [(i, i ^ step) for i in range(size)])]
    ppermute x0 -> x4, starting transfers between devices: none -> 5.54 us  [exchange_by_core(): lax.ppermute(array, axes, [(i, i ^ (odd if i % 2 else even) * narrow) for...]
    ppermute x15 -> x11, waiting for transfers between devices: 8.53 us -> 10 us  [exchange(): return lax.ppermute(array, axes, [(i, i ^ step) for i in range(size)])]
  transfers between devices with their start and end apart: 15 -> 15, of which waited for: 7 -> 5; matrix products, arithmetic and copies ran while one was open for 0% -> 0% of each run, Pallas kernels for 39% -> 38%
where the time goes in v15:
time: 54.6 us; the launch traced here: 54.4 us
  Pallas kernels  27.2 us (50%)
  starting transfers between devices  16.3 us (30%)
  waiting for transfers between devices  10 us (18%)
  between operations  0.94 us (2%)
    pallas_call x16, Pallas kernels, call(): pl.pallas_call(body, out_shape=outs, in_specs=[pl.BlockSpec(memory_space=...  27.2 us
    ppermute x11, starting transfers between devices, exchange(): return lax.ppermute(array, axes, [(i, i ^ step) for i in range(size)])  10.7 us
    ppermute x11, waiting for transfers between devices, exchange(): return lax.ppermute(array, axes, [(i, i ^ step) for i in range(size)])  10 us
    ppermute x4, starting transfers between devices, exchange_by_core(): lax.ppermute(array, axes, [(i, i ^ (odd if i % 2 else even) * narrow) for...  5.54 us
  transfers between devices with their start and end apart: 15, of which 5 were waited for; matrix products, arithmetic and copies ran while one was open for 0% of the time, Pallas kernels for 38%

profile of v15, /device:TPU:0, one launch (start us, length us, event | category | flops | bytes accessed | tf_op | source)
XLA Modules:
  0.0 54.4 jit_solution(959940328865601114)
XLA Ops:
  0.6 0.8 %pack.1.own = bf16[3,8,1024]{2,1,0:T(8,128)(2,1)S(1)} custom-call(bf16[6,2048]{1,0:T(8,128)(2,1)} %inputs.1, bf16[6,2048]{1,0:T(8,128)(2,1)} %cotangent.1), custom_call_target="tpu_custom_call" | custom-call | flops 1000 | bytes 1000 | tf_op jit(solution)/shard_map/pack/pallas_call | solution.py:94
  1.4 4.1 %collective-permute-start = (bf16[3,8,1024]{2,1,0:T(8,128)(2,1)S(1)}, bf16[3,8,1024]{2,1,0:T(8,128)(2,1)S(1)}, u32[]{:S(2)}, u32[]{:S(2)}) collective-permute-start(bf16[3,8,1024]{2,1,0:T(8,128)(2,1)S(1)} %pack.1.own), channel_id=1, source_target_pairs={{0,8},{4,12},{8,0},{12,4},{1,9},{5,13},{9,1},{13,5},{2,10},{6,14},... | collective-permute-start | bytes 147464 | tf_op jit(solution)/shard_map/ppermute | solution.py:70
  5.5 3.9 %load_a.1 = (bf16[2048,768]{1,0:T(8,128)(2,1)S(1)}, bf16[2048,768]{1,0:T(8,128)(2,1)S(1)}, bf16[768,2048]{1,0:T(8,128)(2,1)S(1)}, bf16[8,1024]{1,0:T(8,128)(2,1)S(1)}) custom-call(bf16[2048,6144]{1,0:T(8,128)(2,1)} %refs_0_.11, bf16[2048,6144]{1,0:T(8,128)(2,1)} %refs_1_.11, bf16[6144,2048]{1,0:T(8,128)(2,1)} %refs_2_.11, s32[1,24]{1,0:T(1,128)} %bitcast.3), custom_call_target="tpu_custom_call" | custom-call | flops 1000 | bytes 1000 | tf_op jit(solution)/shard_map/load_a/pallas_call | solution.py:94
  9.4 0.0 collective-permute-done.far
  9.4 1.6 %collective-permute-start.2 = (bf16[7,8,1024]{2,1,0:T(8,128)(2,1)S(1)}, bf16[7,8,1024]{2,1,0:T(8,128)(2,1)S(1)}, u32[]{:S(2)}, u32[]{:S(2)}) collective-permute-start(bf16[7,8,1024]{2,1,0:T(8,128)(2,1)S(1)} %get-tuple-element.43.refs_3_.refs_4_), channel_id=1, source_target_pairs={{0,4},{1,17},{2,6},{3,19},{4,0},{5,21},{6,2},{7,23},{8,12},{9,25},... | collective-permute-start | bytes 344072 | tf_op jit(solution)/shard_map/ppermute | solution.py:77
  11.1 1.5 %collective-permute-start.1 = (bf16[7,8,1024]{2,1,0:T(8,128)(2,1)S(1)}, bf16[7,8,1024]{2,1,0:T(8,128)(2,1)S(1)}, u32[]{:S(2)}, u32[]{:S(2)}) collective-permute-start(bf16[7,8,1024]{2,1,0:T(8,128)(2,1)S(1)} %get-tuple-element.43.refs_3_.refs_4_), channel_id=1, source_target_pairs={{0,16},{1,5},{2,18},{3,7},{4,20},{5,1},{6,22},{7,3},{8,24},{9,13},... | collective-permute-start | bytes 344072 | tf_op jit(solution)/shard_map/ppermute | solution.py:77
  12.6 0.4 collective-permute-start.3
  13.0 3.8 %load_b.1 = (bf16[2048,768]{1,0:T(8,128)(2,1)S(1)}, bf16[2048,768]{1,0:T(8,128)(2,1)S(1)}, bf16[768,2048]{1,0:T(8,128)(2,1)S(1)}) custom-call(bf16[2048,6144]{1,0:T(8,128)(2,1)} %refs_0_.11, bf16[2048,6144]{1,0:T(8,128)(2,1)} %refs_1_.11, bf16[6144,2048]{1,0:T(8,128)(2,1)} %refs_2_.11, bf16[6,8,1024]{2,1,0:T(8,128)(2,1)S(1)} %get-tuple-element.44.refs_3_), custom_call_target="tpu_custom_call" | custom-call | flops 1000 | bytes 1000 | tf_op jit(solution)/shard_map/load_b/pallas_call | solution.py:94
  16.8 1.3 %collective-permute-done.3.refs_6_ = bf16[6,8,1024]{2,1,0:T(8,128)(2,1)S(1)} collective-permute-done((bf16[6,8,1024]{2,1,0:T(8,128)(2,1)S(1)}, bf16[6,8,1024]{2,1,0:T(8,128)(2,1)S(1)}, u32[]{:S(2)}, u32[]{:S(2)}) %collective-permute-start.3) | collective-permute-done | bytes 98336 | tf_op jit(solution)/shard_map/ppermute | solution.py:70
  18.1 0.0 collective-permute-done.2.refs_5_.refs_6_
  18.1 0.0 collective-permute-done.1.refs_4_.refs_5_
  18.1 2.9 %forward_3.1 = (bf16[2048,768]{1,0:T(8,128)(2,1)S(1)}, bf16[768,2048]{1,0:T(8,128)(2,1)S(1)}, bf16[48,2048]{1,0:T(8,128)(2,1)S(1)}, bf16[48,2048]{1,0:T(8,128)(2,1)S(1)}, f32[3,48,768]{2,1,0:T(8,128)S(1)}) custom-call(bf16[2048,6144]{1,0:T(8,128)(2,1)} %refs_0_.11, bf16[2048,6144]{1,0:T(8,128)(2,1)} %refs_1_.11, bf16[6144,2048]{1,0:T(8,128)(2,1)} %refs_2_.11, ...), custom_call_target="tpu_custom_call" | custom-call | flops 1000 | bytes 1000 | tf_op jit(solution)/shard_map/forward_3/pallas_call | solution.py:94
  21.0 0.1 collective-permute-start.4
  21.1 2.0 %forward_2.1 = (bf16[2048,768]{1,0:T(8,128)(2,1)S(1)}, f32[3,48,768]{2,1,0:T(8,128)S(1)}) custom-call(bf16[2048,6144]{1,0:T(8,128)(2,1)} %refs_0_.11, bf16[2048,6144]{1,0:T(8,128)(2,1)} %refs_1_.11, bf16[6144,2048]{1,0:T(8,128)(2,1)} %refs_2_.11, bf16[48,2048]{1,0:T(8,128)(2,1)S(1)} %get-tuple-element.49.refs_3_, ...), custom_call_target="tpu_custom_call" | custom-call | flops 1000 | bytes 1000 | tf_op jit(solution)/shard_map/forward_2/pallas_call | solution.py:94
  23.1 0.0 collective-permute-done.4.arrived
  23.2 1.6 %collective-permute-start.6 = (bf16[3,48,768]{2,1,0:T(8,128)(2,1)S(1)}, bf16[3,48,768]{2,1,0:T(8,128)(2,1)S(1)}, u32[]{:S(2)}, u32[]{:S(2)}) collective-permute-start(bf16[3,48,768]{2,1,0:T(8,128)(2,1)S(1)} %join.1.refs_8_), channel_id=1, source_target_pairs={{0,2},{1,3},{2,0},{3,1},{4,6},{5,7},{6,4},{7,5},{8,10},{9,11},{10,... | collective-permute-start | bytes 663560 | tf_op jit(solution)/shard_map/ppermute | solution.py:70
  24.8 2.9 %forward_1.1 = (bf16[2048,768]{1,0:T(8,128)(2,1)S(1)}, bf16[768,2048]{1,0:T(8,128)(2,1)S(1)}, bf16[3,48,768]{2,1,0:T(8,128)(2,1)S(1)}) custom-call(bf16[2048,6144]{1,0:T(8,128)(2,1)} %refs_0_.11, bf16[2048,6144]{1,0:T(8,128)(2,1)} %refs_1_.11, bf16[6144,2048]{1,0:T(8,128)(2,1)} %refs_2_.11, bf16[48,2048]{1,0:T(8,128)(2,1)S(1)} %get-tuple-element.49.refs_3_, ...), custom_call_target="tpu_custom_call" | custom-call | flops 1000 | bytes 1000 | tf_op jit(solution)/shard_map/forward_1/pallas_call | solution.py:94
  27.7 0.3 collective-permute-start.5
  28.0 0.0 copy-start
  28.0 2.6 %forward_0.1 = (f32[3,48,768]{2,1,0:T(8,128)S(1)}, bf16[2048,768]{1,0:T(8,128)(2,1)S(1)}) custom-call(bf16[2048,6144]{1,0:T(8,128)(2,1)} %refs_0_.11, bf16[2048,6144]{1,0:T(8,128)(2,1)} %refs_1_.11, bf16[6144,2048]{1,0:T(8,128)(2,1)} %refs_2_.11, bf16[48,2048]{1,0:T(8,128)(2,1)S(1)} %get-tuple-element.49.refs_3_, ...), custom_call_target="tpu_custom_call" | custom-call | flops 1000 | bytes 1000 | tf_op jit(solution)/shard_map/forward_0/pallas_call | solution.py:94
  30.5 0.6 %collective-permute-done.6.refs_2_ = bf16[3,48,768]{2,1,0:T(8,128)(2,1)S(1)} collective-permute-done((bf16[3,48,768]{2,1,0:T(8,128)(2,1)S(1)}, bf16[3,48,768]{2,1,0:T(8,128)(2,1)S(1)}, u32[]{:S(2)}, u32[]{:S(2)}) %collective-permute-start.6) | collective-permute-done | bytes 221216 | tf_op jit(solution)/shard_map/ppermute | solution.py:70
  31.1 0.0 collective-permute-done.5.refs_1_
  31.1 0.0 copy-done
  31.1 0.4 middle.1
  31.5 1.5 %collective-permute-start.7 = (bf16[112,768]{1,0:T(8,128)(2,1)S(1)}, bf16[112,768]{1,0:T(8,128)(2,1)S(1)}, u32[]{:S(2)}, u32[]{:S(2)}) collective-permute-start(bf16[112,768]{1,0:T(8,128)(2,1)S(1)} %get-tuple-element.63.message.refs_0_), channel_id=1, source_target_pairs={{0,2},{1,3},{2,0},{3,1},{4,6},{5,7},{6,4},{7,5},{8,10},{9,11},{10,... | collective-permute-start | bytes 516104 | tf_op jit(solution)/shard_map/ppermute | solution.py:70
  33.0 0.0 collective-permute-start.8
  33.0 0.5 collective-permute-start.9
  33.5 1.7 %backward_0.1.before = f32[2048,48]{1,0:T(8,128)S(1)} custom-call(bf16[112,768]{1,0:T(8,128)(2,1)S(1)} %get-tuple-element.63.message.refs_0_, bf16[2048,768]{1,0:T(8,128)(2,1)S(1)} %get-tuple-element.62.refs_7_.gate, bf16[2048,768]{1,0:T(8,128)(2,1)S(1)} %get-tuple-element.58.refs_5_.refs_8_.up), custom_call_target="tpu_custom_call" | custom-call | flops 1000 | bytes 1000 | tf_op jit(solution)/shard_map/backward_0/pallas_call | solution.py:94
  35.3 0.0 collective-permute-done.9.d_up
  35.3 0.0 collective-permute-done.8.d_gate.refs_1_
  35.3 1.8 %backward_1.1.before = f32[2048,48]{1,0:T(8,128)S(1)} custom-call(bf16[64,768]{1,0:T(8,128)(2,1)S(1)} %collective-permute-done.8.d_gate.refs_1_, bf16[48,768]{1,0:T(8,128)(2,1)S(1)} %collective-permute-done.9.d_up, bf16[2048,768]{1,0:T(8,128)(2,1)S(1)} %get-tuple-element.51.refs_5_.refs_9_.gate, bf16[2048,768]{1,0:T(8,128)(2,1)S(1)} %get-tuple-element.54.refs_6_.refs_10_.up, ...), custom_call_target="tpu_custom_call" | custom-call | flops 1000 | bytes 1000 | tf_op jit(solution)/shard_map/backward_1/pallas_call | solution.py:94
  37.1 0.5 collective-permute-done.7.message.refs_2_
  37.5 0.0 collective-permute-start.10
  37.5 1.8 %backward_2.1.before = f32[2048,48]{1,0:T(8,128)S(1)} custom-call(bf16[112,768]{1,0:T(8,128)(2,1)S(1)} %collective-permute-done.7.message.refs_2_, bf16[2048,768]{1,0:T(8,128)(2,1)S(1)} %get-tuple-element.48.refs_10_.refs_5_.refs_11_.gate, bf16[2048,768]{1,0:T(8,128)(2,1)S(1)} %get-tuple-element.52.refs_6_.refs_12_.up, f32[2048,48]{1,0:T(8,128)S(1)} %backward_1.1.before), custom_call_target="tpu_custom_call" | custom-call | flops 1000 | bytes 1000 | tf_op jit(solution)/shard_map/backward_2/pallas_call | solution.py:94
  39.3 0.0 collective-permute-done.10.message
  39.3 1.9 %backward_3.1 = (f32[24,1024]{1,0:T(8,128)S(1)}, f32[8,128]{1,0:T(8,128)S(1)}, bf16[4,8,1024]{2,1,0:T(8,128)(2,1)S(1)}, bf16[4,8,1024]{2,1,0:T(8,128)(2,1)S(1)}, bf16[3,8,1152]{2,1,0:T(8,128)(2,1)S(1)}) custom-call(bf16[112,768]{1,0:T(8,128)(2,1)S(1)} %collective-permute-done.10.message, bf16[2048,768]{1,0:T(8,128)(2,1)S(1)} %get-tuple-element.45.refs_7_.refs_13_.gate, ...), custom_call_target="tpu_custom_call" | custom-call | flops 1000 | bytes 1000 | tf_op jit(solution)/shard_map/backward_3/pallas_call | solution.py:94
  41.2 1.4 %collective-permute-start.12 = (bf16[4,8,1024]{2,1,0:T(8,128)(2,1)S(1)}, bf16[4,8,1024]{2,1,0:T(8,128)(2,1)S(1)}, u32[]{:S(2)}, u32[]{:S(2)}) collective-permute-start(bf16[4,8,1024]{2,1,0:T(8,128)(2,1)S(1)} %get-tuple-element.72), channel_id=1, source_target_pairs={{0,16},{1,5},{2,18},{3,7},{4,20},{5,1},{6,22},{7,3},{8,24},{9,13},... | collective-permute-start | bytes 196616 | tf_op jit(solution)/shard_map/ppermute | solution.py:77
  42.7 0.9 %collective-permute-start.13 = (bf16[4,8,1024]{2,1,0:T(8,128)(2,1)S(1)}, bf16[4,8,1024]{2,1,0:T(8,128)(2,1)S(1)}, u32[]{:S(2)}, u32[]{:S(2)}) collective-permute-start(bf16[4,8,1024]{2,1,0:T(8,128)(2,1)S(1)} %get-tuple-element.73), channel_id=1, source_target_pairs={{0,4},{1,17},{2,6},{3,19},{4,0},{5,21},{6,2},{7,23},{8,12},{9,25},... | collective-permute-start | bytes 196616 | tf_op jit(solution)/shard_map/ppermute | solution.py:77
  43.6 1.2 %collective-permute-start.11 = (bf16[3,8,1152]{2,1,0:T(8,128)(2,1)S(1)}, bf16[3,8,1152]{2,1,0:T(8,128)(2,1)S(1)}, u32[]{:S(2)}, u32[]{:S(2)}) collective-permute-start(bf16[3,8,1152]{2,1,0:T(8,128)(2,1)S(1)} %get-tuple-element.71), channel_id=1, source_target_pairs={{0,20},{4,16},{8,28},{12,24},{16,4},{20,0},{24,12},{28,8},{1,21},{... | collective-permute-start | bytes 165896 | tf_op jit(solution)/shard_map/ppermute | solution.py:70
  44.8 3.9 %collective-permute-done.11.diagonal = bf16[3,8,1152]{2,1,0:T(8,128)(2,1)S(1)} collective-permute-done((bf16[3,8,1152]{2,1,0:T(8,128)(2,1)S(1)}, bf16[3,8,1152]{2,1,0:T(8,128)(2,1)S(1)}, u32[]{:S(2)}, u32[]{:S(2)}) %collective-permute-start.11) | collective-permute-done | bytes 55328 | tf_op jit(solution)/shard_map/ppermute | solution.py:70
  48.7 0.0 collective-permute-done.12.one
  48.7 0.0 collective-permute-done.13.two
  48.7 0.1 combine.1
  48.7 1.1 %collective-permute-start.14 = (bf16[2,8,1024]{2,1,0:T(8,128)(2,1)S(1)}, bf16[2,8,1024]{2,1,0:T(8,128)(2,1)S(1)}, u32[]{:S(2)}, u32[]{:S(2)}) collective-permute-start(bf16[2,8,1024]{2,1,0:T(8,128)(2,1)S(1)} %get-tuple-element.75), channel_id=1, source_target_pairs={{0,8},{4,12},{8,0},{12,4},{1,9},{5,13},{9,1},{13,5},{2,10},{6,14},... | collective-permute-start | bytes 98312 | tf_op jit(solution)/shard_map/ppermute | solution.py:70
  49.8 3.8 %collective-permute-done.14.arrived = bf16[2,8,1024]{2,1,0:T(8,128)(2,1)S(1)} collective-permute-done((bf16[2,8,1024]{2,1,0:T(8,128)(2,1)S(1)}, bf16[2,8,1024]{2,1,0:T(8,128)(2,1)S(1)}, u32[]{:S(2)}, u32[]{:S(2)}) %collective-permute-start.14) | collective-permute-done | bytes 32800 | tf_op jit(solution)/shard_map/ppermute | solution.py:70
  53.6 0.7 %last.1 = (bf16[6,2048]{1,0:T(8,128)(2,1)}, f32[4,1536]{1,0:T(4,128)}, f32[4]{0:T(128)}) custom-call(f32[16,1024]{1,0:T(8,128)S(1)} %get-tuple-element.74.own, bf16[2,8,1024]{2,1,0:T(8,128)(2,1)S(1)} %collective-permute-done.14.arrived, f32[4,768]{1,0:T(4,128)S(1)} %get-tuple-element.76.grads, f32[4,768]{1,0:T(4,128)S(1)} %get-tuple-element.77.other_grads), custom_call_target="tpu_custom_call" | custom-call | flops 1000 | bytes 1000 | tf_op jit(solution)/shard_map/last/pallas_call | solution.py:94
  (2 shorter events, 0.1 us)
Async XLA Ops:
  1.4 8.0 %collective-permute-start = (bf16[3,8,1024]{2,1,0:T(8,128)(2,1)S(1)}, bf16[3,8,1024]{2,1,0:T(8,128)(2,1)S(1)}, u32[]{:S(2)}, u32[]{:S(2)}) collective-permute-start(bf16[3,8,1024]{2,1,0:T(8,128)(2,1)S(1)} %pack.1.own), channel_id=1, source_target_pairs={{0,8},{4,12},{8,0},{12,4},{1,9},{5,13},{9,1},{13,5},{2,10},{6,14},... | collective-permute-start | bytes 147464 | tf_op jit(solution)/shard_map/ppermute | solution.py:70
  9.4 8.7 %collective-permute-start.2 = (bf16[7,8,1024]{2,1,0:T(8,128)(2,1)S(1)}, bf16[7,8,1024]{2,1,0:T(8,128)(2,1)S(1)}, u32[]{:S(2)}, u32[]{:S(2)}) collective-permute-start(bf16[7,8,1024]{2,1,0:T(8,128)(2,1)S(1)} %get-tuple-element.43.refs_3_.refs_4_), channel_id=1, source_target_pairs={{0,4},{1,17},{2,6},{3,19},{4,0},{5,21},{6,2},{7,23},{8,12},{9,25},... | collective-permute-start | bytes 344072 | tf_op jit(solution)/shard_map/ppermute | solution.py:77
  11.1 7.0 %collective-permute-start.1 = (bf16[7,8,1024]{2,1,0:T(8,128)(2,1)S(1)}, bf16[7,8,1024]{2,1,0:T(8,128)(2,1)S(1)}, u32[]{:S(2)}, u32[]{:S(2)}) collective-permute-start(bf16[7,8,1024]{2,1,0:T(8,128)(2,1)S(1)} %get-tuple-element.43.refs_3_.refs_4_), channel_id=1, source_target_pairs={{0,16},{1,5},{2,18},{3,7},{4,20},{5,1},{6,22},{7,3},{8,24},{9,13},... | collective-permute-start | bytes 344072 | tf_op jit(solution)/shard_map/ppermute | solution.py:77
  12.6 5.5 %collective-permute-start.3 = (bf16[6,8,1024]{2,1,0:T(8,128)(2,1)S(1)}, bf16[6,8,1024]{2,1,0:T(8,128)(2,1)S(1)}, u32[]{:S(2)}, u32[]{:S(2)}) collective-permute-start(bf16[6,8,1024]{2,1,0:T(8,128)(2,1)S(1)} %get-tuple-element.44.refs_3_), channel_id=1, source_target_pairs={{0,20},{4,16},{8,28},{12,24},{16,4},{20,0},{24,12},{28,8},{1,21},{... | collective-permute-start | bytes 294920 | tf_op jit(solution)/shard_map/ppermute | solution.py:70
  21.0 2.1 %collective-permute-start.4 = (f32[3,48,768]{2,1,0:T(8,128)S(1)}, f32[3,48,768]{2,1,0:T(8,128)S(1)}, u32[]{:S(2)}, u32[]{:S(2)}) collective-permute-start(f32[3,48,768]{2,1,0:T(8,128)S(1)} %get-tuple-element.57), channel_id=1, source_target_pairs={{0,1},{1,0},{2,3},{3,2},{4,5},{5,4},{6,7},{7,6},{8,9},{9,8},{10,11... | collective-permute-start | bytes 1327112 | tf_op jit(solution)/shard_map/ppermute | solution.py:70
  23.2 7.9 %collective-permute-start.6 = (bf16[3,48,768]{2,1,0:T(8,128)(2,1)S(1)}, bf16[3,48,768]{2,1,0:T(8,128)(2,1)S(1)}, u32[]{:S(2)}, u32[]{:S(2)}) collective-permute-start(bf16[3,48,768]{2,1,0:T(8,128)(2,1)S(1)} %join.1.refs_8_), channel_id=1, source_target_pairs={{0,2},{1,3},{2,0},{3,1},{4,6},{5,7},{6,4},{7,5},{8,10},{9,11},{10,... | collective-permute-start | bytes 663560 | tf_op jit(solution)/shard_map/ppermute | solution.py:70
  27.7 3.4 %collective-permute-start.5 = (bf16[3,48,768]{2,1,0:T(8,128)(2,1)S(1)}, bf16[3,48,768]{2,1,0:T(8,128)(2,1)S(1)}, u32[]{:S(2)}, u32[]{:S(2)}) collective-permute-start(bf16[3,48,768]{2,1,0:T(8,128)(2,1)S(1)} %get-tuple-element.61), channel_id=1, source_target_pairs={{0,1},{1,0},{2,3},{3,2},{4,5},{5,4},{6,7},{7,6},{8,9},{9,8},{10,11... | collective-permute-start | bytes 663560 | tf_op jit(solution)/shard_map/ppermute | solution.py:70
  28.0 3.1 %copy-start = (f32[6144]{0:T(1024)S(1)}, f32[6144]{0:T(1024)}, u32[]{:S(2)}) copy-start(f32[6144]{0:T(1024)} %param.12) | copy-start | bytes 73732
  31.5 6.1 %collective-permute-start.7 = (bf16[112,768]{1,0:T(8,128)(2,1)S(1)}, bf16[112,768]{1,0:T(8,128)(2,1)S(1)}, u32[]{:S(2)}, u32[]{:S(2)}) collective-permute-start(bf16[112,768]{1,0:T(8,128)(2,1)S(1)} %get-tuple-element.63.message.refs_0_), channel_id=1, source_target_pairs={{0,2},{1,3},{2,0},{3,1},{4,6},{5,7},{6,4},{7,5},{8,10},{9,11},{10,... | collective-permute-start | bytes 516104 | tf_op jit(solution)/shard_map/ppermute | solution.py:70
  33.0 2.3 %collective-permute-start.8 = (bf16[64,768]{1,0:T(8,128)(2,1)S(1)}, bf16[64,768]{1,0:T(8,128)(2,1)S(1)}, u32[]{:S(2)}, u32[]{:S(2)}) collective-permute-start(bf16[64,768]{1,0:T(8,128)(2,1)S(1)} %get-tuple-element.64), channel_id=1, source_target_pairs={{0,1},{1,0},{2,3},{3,2},{4,5},{5,4},{6,7},{7,6},{8,9},{9,8},{10,11... | collective-permute-start | bytes 294920 | tf_op jit(solution)/shard_map/ppermute | solution.py:70
  33.0 2.3 %collective-permute-start.9 = (bf16[48,768]{1,0:T(8,128)(2,1)S(1)}, bf16[48,768]{1,0:T(8,128)(2,1)S(1)}, u32[]{:S(2)}, u32[]{:S(2)}) collective-permute-start(bf16[48,768]{1,0:T(8,128)(2,1)S(1)} %get-tuple-element.65), channel_id=1, source_target_pairs={{0,1},{1,0},{2,3},{3,2},{4,5},{5,4},{6,7},{7,6},{8,9},{9,8},{10,11... | collective-permute-start | bytes 221192 | tf_op jit(solution)/shard_map/ppermute | solution.py:70
  37.5 1.8 %collective-permute-start.10 = (bf16[112,768]{1,0:T(8,128)(2,1)S(1)}, bf16[112,768]{1,0:T(8,128)(2,1)S(1)}, u32[]{:S(2)}, u32[]{:S(2)}) collective-permute-start(bf16[112,768]{1,0:T(8,128)(2,1)S(1)} %collective-permute-done.7.message.refs_2_), channel_id=1, source_target_pairs={{0,1},{1,0},{2,3},{3,2},{4,5},{5,4},{6,7},{7,6},{8,9},{9,8},{10,11... | collective-permute-start | bytes 516104 | tf_op jit(solution)/shard_map/ppermute | solution.py:70
  41.2 7.4 %collective-permute-start.12 = (bf16[4,8,1024]{2,1,0:T(8,128)(2,1)S(1)}, bf16[4,8,1024]{2,1,0:T(8,128)(2,1)S(1)}, u32[]{:S(2)}, u32[]{:S(2)}) collective-permute-start(bf16[4,8,1024]{2,1,0:T(8,128)(2,1)S(1)} %get-tuple-element.72), channel_id=1, source_target_pairs={{0,16},{1,5},{2,18},{3,7},{4,20},{5,1},{6,22},{7,3},{8,24},{9,13},... | collective-permute-start | bytes 196616 | tf_op jit(solution)/shard_map/ppermute | solution.py:77
  42.7 6.0 %collective-permute-start.13 = (bf16[4,8,1024]{2,1,0:T(8,128)(2,1)S(1)}, bf16[4,8,1024]{2,1,0:T(8,128)(2,1)S(1)}, u32[]{:S(2)}, u32[]{:S(2)}) collective-permute-start(bf16[4,8,1024]{2,1,0:T(8,128)(2,1)S(1)} %get-tuple-element.73), channel_id=1, source_target_pairs={{0,4},{1,17},{2,6},{3,19},{4,0},{5,21},{6,2},{7,23},{8,12},{9,25},... | collective-permute-start | bytes 196616 | tf_op jit(solution)/shard_map/ppermute | solution.py:77
  43.6 5.1 %collective-permute-start.11 = (bf16[3,8,1152]{2,1,0:T(8,128)(2,1)S(1)}, bf16[3,8,1152]{2,1,0:T(8,128)(2,1)S(1)}, u32[]{:S(2)}, u32[]{:S(2)}) collective-permute-start(bf16[3,8,1152]{2,1,0:T(8,128)(2,1)S(1)} %get-tuple-element.71), channel_id=1, source_target_pairs={{0,20},{4,16},{8,28},{12,24},{16,4},{20,0},{24,12},{28,8},{1,21},{... | collective-permute-start | bytes 165896 | tf_op jit(solution)/shard_map/ppermute | solution.py:70
  48.7 4.9 %collective-permute-start.14 = (bf16[2,8,1024]{2,1,0:T(8,128)(2,1)S(1)}, bf16[2,8,1024]{2,1,0:T(8,128)(2,1)S(1)}, u32[]{:S(2)}, u32[]{:S(2)}) collective-permute-start(bf16[2,8,1024]{2,1,0:T(8,128)(2,1)S(1)} %get-tuple-element.75), channel_id=1, source_target_pairs={{0,8},{4,12},{8,0},{12,4},{1,9},{5,13},{9,1},{13,5},{2,10},{6,14},... | collective-permute-start | bytes 98312 | tf_op jit(solution)/shard_map/ppermute | solution.py:70

commit v16 on v14

--- a/solution.py
+++ b/solution.py
@@ -146,8 +146,9 @@
         start = pl.multiple_of((owner * groups + lax.axis_index("groups")) * width, width)
         source = sources[kind]
         source = source.at[pl.ds(start, width), :] if kind == DOWN else source.at[:, pl.ds(start, width)]
-        size = target.shape[0] // CHUNKS
-        for c in range(CHUNKS):
+        chunks = CHUNKS if len(pieces) == 1 else 1
+        size = target.shape[0] // chunks
+        for c in range(chunks):
             span = slice(c * size, (c + 1) * size)
             copies.append(pltpu.make_async_copy(source.at[span, :], target.at[span, :], sem.at[i, c]))
     for copy in copies:
@@ -239,9 +240,27 @@
     out[GATE] = jnp.dot(tokens[...], gate[...], preferred_element_type=jnp.float32)
 
 
+def to_tiles(values, tiles, first):
+    rows, columns = values.shape
+    values = values.astype(jnp.float32)
+    for i in range(rows // 8):
+        for j in range(columns // 128):
+            tile = values[8 * i : 8 * i + 8, 128 * j : 128 * j + 128]
+            tiles[first + i * (columns // 128) + j] = tile.astype(tiles.dtype)
+
+
+def from_tiles(tiles, first, rows, columns):
+    across = columns // 128
+    parts = [
+        jnp.concatenate([tiles[first + i * across + j].astype(jnp.float32) for j in range(across)], axis=1)
+        for i in range(rows // 8)
+    ]
+    return jnp.concatenate(parts, axis=0).astype(tiles.dtype)
+
+
 def middle_kernel(groups, *refs):
     own, arrived, crossed, scale, relayed, other_relayed = refs[:6]
-    message, near_gate, near_up, grads, other_grads, stage = refs[-6:]
+    message, tiles, near_gate, near_up, grads, other_grads, stage = refs[-7:]
     _, tokens, width = own.shape
     narrow, group = lax.axis_index("narrow"), lax.axis_index("groups")
     sums = [own[i] + arrived[i].astype(jnp.float32) + crossed[i].astype(jnp.float32) for i in range(3)]
@@ -251,6 +270,9 @@
     message[tokens : 2 * tokens, :] = d_up
     near_gate[0:tokens, :] = d_gate
     near_up[...] = d_up
+    count = tokens // 8 * (width // 128)
+    to_tiles(d_gate, tiles, 0)
+    to_tiles(d_up, tiles, count)
     half = tokens // groups
     for side, (source, target) in enumerate(((relayed, grads), (other_relayed, other_grads))):
         marks = source[source.shape[0] - 1].astype(jnp.float32)
@@ -270,6 +292,8 @@
     squares = jnp.broadcast_to(jnp.sum(every * every, axis=1, keepdims=True), every.shape)
     tail = jnp.concatenate(split_high(squares), axis=0).astype(jnp.bfloat16)
     message[2 * tokens :, :] = tail
+    for i, rows in enumerate(split_high(squares)):
+        tiles[2 * count + i] = rows[:, 0:128].astype(jnp.bfloat16)
     near_gate[tokens:, :] = tail
 
 
@@ -285,6 +309,20 @@
 def halves(message):
     tokens = (message.shape[0] - 16) // 2
     return message[0:tokens, :], message[tokens : 2 * tokens, :]
+
+
+def halves_of_tiles(tiles, width):
+    count = (tiles.shape[0] - 2) // 2
+    rows = count // (width // 128) * 8
+    return from_tiles(tiles, 0, rows, width), from_tiles(tiles, count, rows, width)
+
+
+def squares_of(message):
+    if len(message.shape) == 3:
+        tiles = message.shape[0]
+        return message[tiles - 2].astype(jnp.float32) + message[tiles - 1].astype(jnp.float32)
+    rows = message[message.shape[0] - 16 :, 0:128].astype(jnp.float32)
+    return rows[0:8] + rows[8:16]
 
 
 def backward_first_kernel(message, gate, up, total):
@@ -299,9 +337,10 @@
         total[start : start + TILE, :] = before[start : start + TILE, :] + part
 
 
-def backward_next_kernel(message, gate, up, before, total):
+def backward_next_kernel(tiles, gate, up, before, total):
+    grads = halves_of_tiles(tiles, gate.shape[1])
     for start in range(0, total.shape[0], TILE):
-        part = backward_part(halves(message), gate, up, start)
+        part = backward_part(grads, gate, up, start)
         total[start : start + TILE, :] = before[start : start + TILE, :] + part
 
 
@@ -310,15 +349,15 @@
     return high, values - high
 
 
-def backward_last_kernel(share, message, gate, up, before, *refs):
+def backward_last_kernel(share, tiles, gate, up, before, *refs):
     others, other_grads, (own, own_squares), sends, (total, stage) = refs[:3], refs[3], refs[4:6], refs[6:9], refs[9:]
     tokens, features = total.shape
     side = features // 2
+    grads = halves_of_tiles(tiles, gate.shape[1])
     for start in range(0, features, TILE):
-        part = before[start : start + TILE, :] + backward_part(halves(message), gate, up, start)
+        part = before[start : start + TILE, :] + backward_part(grads, gate, up, start)
         total[:, start : start + TILE] = part.T
-    squares = sum(ref[ref.shape[0] - 16 :, 0:128].astype(jnp.float32) for ref in (message,) + others)
-    squares = squares[0:8] + squares[8:16]
+    squares = sum(squares_of(ref) for ref in (tiles,) + others)
     own_squares[...] = squares
     tails = split_high(squares)
     slabs = 4 * share // 8
@@ -496,11 +535,12 @@
     )
 
     resident = [array for s in range(strips) for array in hold(s, [GATE, UP])]
-    message, near_gate, near_up, grads, other_grads = call(
+    message, tiles, near_gate, near_up, grads, other_grads = call(
         functools.partial(middle_kernel, groups),
         "middle",
         [
             pltpu.VMEM((2 * tokens + 16, width), bf16),
+            pltpu.VMEM((2 * (tokens // 8) * (width // 128) + 2, 8, 128), bf16),
             pltpu.VMEM((tokens + 16, width), bf16),
             pltpu.VMEM((tokens, width), bf16),
             pltpu.VMEM((SEQS, width), f32),
@@ -512,7 +552,7 @@
 
     total = pltpu.VMEM((features, tokens), f32)
     near_gate, near_up = exchange(near_gate, "narrow", 1), exchange(near_up, "narrow", 1)
-    message_2 = exchange(message, "narrow", 2)
+    message_2 = exchange(tiles, "narrow", 2)
     sums = call(backward_first_kernel, "backward_0", total, [message] + hold(0, [GATE, UP]))
     sums = call(backward_near_kernel, "backward_1", total, [near_gate, near_up] + hold(1, [GATE, UP]) + [sums])
     message_2, sums = lax.optimization_barrier((message_2, sums))

time: 53.3 us -> 53.2 us (level)
  transfers between devices with their start and end apart: 15 -> 15, of which waited for: 7 -> 6; matrix products, arithmetic and copies ran while one was open for 0% -> 0% of each run, Pallas kernels for 39% -> 39%
where the time goes in v16:
time: 53.2 us; the launch traced here: 53 us
  Pallas kernels  27.5 us (52%)
  starting transfers between devices  16.5 us (31%)
  waiting for transfers between devices  8.04 us (15%)
  between operations  0.94 us (2%)
    pallas_call x16, Pallas kernels, call(): pl.pallas_call(body, out_shape=outs, in_specs=[pl.BlockSpec(memory_space=...  27.5 us
    ppermute x15, starting transfers between devices, exchange(): return lax.ppermute(array, axes, [(i, i ^ step) for i in range(size)])  16.5 us
    ppermute x15, waiting for transfers between devices, exchange(): return lax.ppermute(array, axes, [(i, i ^ step) for i in range(size)])  8.04 us
  transfers between devices with their start and end apart: 15, of which 6 were waited for; matrix products, arithmetic and copies ran while one was open for 0% of the time, Pallas kernels for 39%

profile of v16, /device:TPU:0, one launch (start us, length us, event | category | flops | bytes accessed | tf_op | source)
XLA Modules:
  0.0 53.0 jit_solution(1545752719878840500)
XLA Ops:
  0.6 0.8 %pack.1.own = bf16[3,8,1024]{2,1,0:T(8,128)(2,1)S(1)} custom-call(bf16[6,2048]{1,0:T(8,128)(2,1)} %inputs.1, bf16[6,2048]{1,0:T(8,128)(2,1)} %cotangent.1), custom_call_target="tpu_custom_call" | custom-call | flops 1000 | bytes 1000 | tf_op jit(solution)/shard_map/pack/pallas_call | solution.py:83
  1.4 4.1 %collective-permute-start = (bf16[3,8,1024]{2,1,0:T(8,128)(2,1)S(1)}, bf16[3,8,1024]{2,1,0:T(8,128)(2,1)S(1)}, u32[]{:S(2)}, u32[]{:S(2)}) collective-permute-start(bf16[3,8,1024]{2,1,0:T(8,128)(2,1)S(1)} %pack.1.own), channel_id=1, source_target_pairs={{0,8},{4,12},{8,0},{12,4},{1,9},{5,13},{9,1},{13,5},{2,10},{6,14},... | collective-permute-start | bytes 147464 | tf_op jit(solution)/shard_map/ppermute | solution.py:70
  5.5 3.9 %load_a.1 = (bf16[2048,768]{1,0:T(8,128)(2,1)S(1)}, bf16[2048,768]{1,0:T(8,128)(2,1)S(1)}, bf16[768,2048]{1,0:T(8,128)(2,1)S(1)}, bf16[8,1024]{1,0:T(8,128)(2,1)S(1)}) custom-call(bf16[2048,6144]{1,0:T(8,128)(2,1)} %refs_0_.11, bf16[2048,6144]{1,0:T(8,128)(2,1)} %refs_1_.11, bf16[6144,2048]{1,0:T(8,128)(2,1)} %refs_2_.11, s32[1,24]{1,0:T(1,128)} %bitcast.3), custom_call_target="tpu_custom_call" | custom-call | flops 1000 | bytes 1000 | tf_op jit(solution)/shard_map/load_a/pallas_call | solution.py:83
  9.5 0.0 collective-permute-done.far
  9.5 1.6 %collective-permute-start.2 = (bf16[7,8,1024]{2,1,0:T(8,128)(2,1)S(1)}, bf16[7,8,1024]{2,1,0:T(8,128)(2,1)S(1)}, u32[]{:S(2)}, u32[]{:S(2)}) collective-permute-start(bf16[7,8,1024]{2,1,0:T(8,128)(2,1)S(1)} %get-tuple-element.44.refs_3_.refs_4_), channel_id=1, source_target_pairs={{0,16},{16,0},{1,17},{17,1},{2,18},{18,2},{3,19},{19,3},{4,20},{20... | collective-permute-start | bytes 344072 | tf_op jit(solution)/shard_map/ppermute | solution.py:70
  11.1 1.5 %collective-permute-start.3 = (bf16[6,8,1024]{2,1,0:T(8,128)(2,1)S(1)}, bf16[6,8,1024]{2,1,0:T(8,128)(2,1)S(1)}, u32[]{:S(2)}, u32[]{:S(2)}) collective-permute-start(bf16[6,8,1024]{2,1,0:T(8,128)(2,1)S(1)} %get-tuple-element.45.refs_3_), channel_id=1, source_target_pairs={{0,20},{4,16},{8,28},{12,24},{16,4},{20,0},{24,12},{28,8},{1,21},{... | collective-permute-start | bytes 294920 | tf_op jit(solution)/shard_map/ppermute | solution.py:70
  12.6 0.4 collective-permute-start.1
  13.0 3.9 %load_b.1 = (bf16[2048,768]{1,0:T(8,128)(2,1)S(1)}, bf16[2048,768]{1,0:T(8,128)(2,1)S(1)}, bf16[768,2048]{1,0:T(8,128)(2,1)S(1)}) custom-call(bf16[2048,6144]{1,0:T(8,128)(2,1)} %refs_0_.11, bf16[2048,6144]{1,0:T(8,128)(2,1)} %refs_1_.11, bf16[6144,2048]{1,0:T(8,128)(2,1)} %refs_2_.11, bf16[6,8,1024]{2,1,0:T(8,128)(2,1)S(1)} %get-tuple-element.45.refs_3_), custom_call_target="tpu_custom_call" | custom-call | flops 1000 | bytes 1000 | tf_op jit(solution)/shard_map/load_b/pallas_call | solution.py:83
  16.9 0.3 collective-permute-done.3.refs_6_
  17.2 0.1 collective-permute-done.1.refs_4_
  17.3 0.0 collective-permute-done.2.refs_5_
  17.3 2.9 %forward_3.1 = (bf16[2048,768]{1,0:T(8,128)(2,1)S(1)}, bf16[768,2048]{1,0:T(8,128)(2,1)S(1)}, bf16[48,2048]{1,0:T(8,128)(2,1)S(1)}, bf16[48,2048]{1,0:T(8,128)(2,1)S(1)}, f32[3,48,768]{2,1,0:T(8,128)S(1)}) custom-call(bf16[2048,6144]{1,0:T(8,128)(2,1)} %refs_0_.11, bf16[2048,6144]{1,0:T(8,128)(2,1)} %refs_1_.11, bf16[6144,2048]{1,0:T(8,128)(2,1)} %refs_2_.11, ...), custom_call_target="tpu_custom_call" | custom-call | flops 1000 | bytes 1000 | tf_op jit(solution)/shard_map/forward_3/pallas_call | solution.py:83
  20.3 0.1 collective-permute-start.4
  20.4 2.1 %forward_2.1 = (bf16[2048,768]{1,0:T(8,128)(2,1)S(1)}, f32[3,48,768]{2,1,0:T(8,128)S(1)}) custom-call(bf16[2048,6144]{1,0:T(8,128)(2,1)} %refs_0_.11, bf16[2048,6144]{1,0:T(8,128)(2,1)} %refs_1_.11, bf16[6144,2048]{1,0:T(8,128)(2,1)} %refs_2_.11, bf16[48,2048]{1,0:T(8,128)(2,1)S(1)} %get-tuple-element.50.refs_3_, ...), custom_call_target="tpu_custom_call" | custom-call | flops 1000 | bytes 1000 | tf_op jit(solution)/shard_map/forward_2/pallas_call | solution.py:83
  22.4 0.0 collective-permute-done.4.arrived
  22.5 1.6 %collective-permute-start.6 = (bf16[3,48,768]{2,1,0:T(8,128)(2,1)S(1)}, bf16[3,48,768]{2,1,0:T(8,128)(2,1)S(1)}, u32[]{:S(2)}, u32[]{:S(2)}) collective-permute-start(bf16[3,48,768]{2,1,0:T(8,128)(2,1)S(1)} %join.1.refs_8_), channel_id=1, source_target_pairs={{0,2},{1,3},{2,0},{3,1},{4,6},{5,7},{6,4},{7,5},{8,10},{9,11},{10,... | collective-permute-start | bytes 663560 | tf_op jit(solution)/shard_map/ppermute | solution.py:70
  24.1 2.9 %forward_1.1 = (bf16[2048,768]{1,0:T(8,128)(2,1)S(1)}, bf16[768,2048]{1,0:T(8,128)(2,1)S(1)}, bf16[3,48,768]{2,1,0:T(8,128)(2,1)S(1)}) custom-call(bf16[2048,6144]{1,0:T(8,128)(2,1)} %refs_0_.11, bf16[2048,6144]{1,0:T(8,128)(2,1)} %refs_1_.11, bf16[6144,2048]{1,0:T(8,128)(2,1)} %refs_2_.11, bf16[48,2048]{1,0:T(8,128)(2,1)S(1)} %get-tuple-element.50.refs_3_, ...), custom_call_target="tpu_custom_call" | custom-call | flops 1000 | bytes 1000 | tf_op jit(solution)/shard_map/forward_1/pallas_call | solution.py:83
  27.0 0.3 collective-permute-start.5
  27.3 0.0 copy-start
  27.3 2.5 %forward_0.1 = (f32[3,48,768]{2,1,0:T(8,128)S(1)}, bf16[2048,768]{1,0:T(8,128)(2,1)S(1)}) custom-call(bf16[2048,6144]{1,0:T(8,128)(2,1)} %refs_0_.11, bf16[2048,6144]{1,0:T(8,128)(2,1)} %refs_1_.11, bf16[6144,2048]{1,0:T(8,128)(2,1)} %refs_2_.11, bf16[48,2048]{1,0:T(8,128)(2,1)S(1)} %get-tuple-element.50.refs_3_, ...), custom_call_target="tpu_custom_call" | custom-call | flops 1000 | bytes 1000 | tf_op jit(solution)/shard_map/forward_0/pallas_call | solution.py:83
  29.8 0.6 %collective-permute-done.6.refs_2_ = bf16[3,48,768]{2,1,0:T(8,128)(2,1)S(1)} collective-permute-done((bf16[3,48,768]{2,1,0:T(8,128)(2,1)S(1)}, bf16[3,48,768]{2,1,0:T(8,128)(2,1)S(1)}, u32[]{:S(2)}, u32[]{:S(2)}) %collective-permute-start.6) | collective-permute-done | bytes 221216 | tf_op jit(solution)/shard_map/ppermute | solution.py:70
  30.4 0.0 collective-permute-done.5.refs_1_
  30.4 0.0 copy-done
  30.4 0.4 middle.1
  30.8 1.5 %collective-permute-start.7 = (bf16[74,8,128]{2,1,0:T(8,128)(2,1)S(1)}, bf16[74,8,128]{2,1,0:T(8,128)(2,1)S(1)}, u32[]{:S(2)}, u32[]{:S(2)}) collective-permute-start(bf16[74,8,128]{2,1,0:T(8,128)(2,1)S(1)} %get-tuple-element.64), channel_id=1, source_target_pairs={{0,2},{1,3},{2,0},{3,1},{4,6},{5,7},{6,4},{7,5},{8,10},{9,11},{10,... | collective-permute-start | bytes 454664 | tf_op jit(solution)/shard_map/ppermute | solution.py:70
  32.3 0.0 collective-permute-start.8
  32.3 0.5 collective-permute-start.9
  32.8 1.7 %backward_0.1.before = f32[2048,48]{1,0:T(8,128)S(1)} custom-call(bf16[112,768]{1,0:T(8,128)(2,1)S(1)} %get-tuple-element.67.message.refs_0_, bf16[2048,768]{1,0:T(8,128)(2,1)S(1)} %get-tuple-element.63.refs_6_.gate, bf16[2048,768]{1,0:T(8,128)(2,1)S(1)} %get-tuple-element.59.refs_5_.refs_7_.up), custom_call_target="tpu_custom_call" | custom-call | flops 1000 | bytes 1000 | tf_op jit(solution)/shard_map/backward_0/pallas_call | solution.py:83
  34.5 0.0 collective-permute-done.9.d_up
  34.5 0.0 collective-permute-done.8.d_gate.refs_1_
  34.5 1.8 %backward_1.1.before = f32[2048,48]{1,0:T(8,128)S(1)} custom-call(bf16[64,768]{1,0:T(8,128)(2,1)S(1)} %collective-permute-done.8.d_gate.refs_1_, bf16[48,768]{1,0:T(8,128)(2,1)S(1)} %collective-permute-done.9.d_up, bf16[2048,768]{1,0:T(8,128)(2,1)S(1)} %get-tuple-element.52.refs_5_.refs_8_.gate, bf16[2048,768]{1,0:T(8,128)(2,1)S(1)} %get-tuple-element.55.refs_6_.refs_9_.up, ...), custom_call_target="tpu_custom_call" | custom-call | flops 1000 | bytes 1000 | tf_op jit(solution)/shard_map/backward_1/pallas_call | solution.py:83
  36.4 0.0 collective-permute-done.7.tiles.refs_2_
  36.4 0.1 collective-permute-start.10
  36.5 1.8 %backward_2.1.before = f32[2048,48]{1,0:T(8,128)S(1)} custom-call(bf16[74,8,128]{2,1,0:T(8,128)(2,1)S(1)} %collective-permute-done.7.tiles.refs_2_, bf16[2048,768]{1,0:T(8,128)(2,1)S(1)} %get-tuple-element.49.refs_10_.refs_5_.gate, bf16[2048,768]{1,0:T(8,128)(2,1)S(1)} %get-tuple-element.53.refs_6_.refs_11_.up, f32[2048,48]{1,0:T(8,128)S(1)} %backward_1.1.before), custom_call_target="tpu_custom_call" | custom-call | flops 1000 | bytes 1000 | tf_op jit(solution)/shard_map/backward_2/pallas_call | solution.py:83
  38.2 0.0 collective-permute-done.10.tiles
  38.3 1.9 %backward_3.1 = (f32[24,1024]{1,0:T(8,128)S(1)}, f32[8,128]{1,0:T(8,128)S(1)}, bf16[3,8,1152]{2,1,0:T(8,128)(2,1)S(1)}, bf16[4,8,1024]{2,1,0:T(8,128)(2,1)S(1)}, bf16[3,8,1152]{2,1,0:T(8,128)(2,1)S(1)}) custom-call(bf16[74,8,128]{2,1,0:T(8,128)(2,1)S(1)} %collective-permute-done.10.tiles, bf16[2048,768]{1,0:T(8,128)(2,1)S(1)} %get-tuple-element.46.refs_7_.refs_12_.gate, ...), custom_call_target="tpu_custom_call" | custom-call | flops 1000 | bytes 1000 | tf_op jit(solution)/shard_map/backward_3/pallas_call | solution.py:83
  40.2 1.6 %collective-permute-start.12 = (bf16[4,8,1024]{2,1,0:T(8,128)(2,1)S(1)}, bf16[4,8,1024]{2,1,0:T(8,128)(2,1)S(1)}, u32[]{:S(2)}, u32[]{:S(2)}) collective-permute-start(bf16[4,8,1024]{2,1,0:T(8,128)(2,1)S(1)} %get-tuple-element.74), channel_id=1, source_target_pairs={{0,16},{16,0},{1,17},{17,1},{2,18},{18,2},{3,19},{19,3},{4,20},{20... | collective-permute-start | bytes 196616 | tf_op jit(solution)/shard_map/ppermute | solution.py:70
  41.8 1.3 %collective-permute-start.11 = (bf16[3,8,1152]{2,1,0:T(8,128)(2,1)S(1)}, bf16[3,8,1152]{2,1,0:T(8,128)(2,1)S(1)}, u32[]{:S(2)}, u32[]{:S(2)}) collective-permute-start(bf16[3,8,1152]{2,1,0:T(8,128)(2,1)S(1)} %get-tuple-element.73), channel_id=1, source_target_pairs={{0,20},{4,16},{8,28},{12,24},{16,4},{20,0},{24,12},{28,8},{1,21},{... | collective-permute-start | bytes 165896 | tf_op jit(solution)/shard_map/ppermute | solution.py:70
  43.1 0.6 %collective-permute-start.13 = (bf16[3,8,1152]{2,1,0:T(8,128)(2,1)S(1)}, bf16[3,8,1152]{2,1,0:T(8,128)(2,1)S(1)}, u32[]{:S(2)}, u32[]{:S(2)}) collective-permute-start(bf16[3,8,1152]{2,1,0:T(8,128)(2,1)S(1)} %get-tuple-element.75), channel_id=1, source_target_pairs={{0,4},{4,0},{8,12},{12,8},{1,5},{5,1},{9,13},{13,9},{2,6},{6,2},{1... | collective-permute-start | bytes 165896 | tf_op jit(solution)/shard_map/ppermute | solution.py:70
  43.7 3.4 %collective-permute-done.11.diagonal = bf16[3,8,1152]{2,1,0:T(8,128)(2,1)S(1)} collective-permute-done((bf16[3,8,1152]{2,1,0:T(8,128)(2,1)S(1)}, bf16[3,8,1152]{2,1,0:T(8,128)(2,1)S(1)}, u32[]{:S(2)}, u32[]{:S(2)}) %collective-permute-start.11) | collective-permute-done | bytes 55328 | tf_op jit(solution)/shard_map/ppermute | solution.py:70
  47.2 0.1 collective-permute-done.13.beside
  47.3 0.0 collective-permute-done.12.across
  47.3 0.1 combine.1
  47.3 1.4 %collective-permute-start.14 = (bf16[2,8,1024]{2,1,0:T(8,128)(2,1)S(1)}, bf16[2,8,1024]{2,1,0:T(8,128)(2,1)S(1)}, u32[]{:S(2)}, u32[]{:S(2)}) collective-permute-start(bf16[2,8,1024]{2,1,0:T(8,128)(2,1)S(1)} %get-tuple-element.77), channel_id=1, source_target_pairs={{0,8},{4,12},{8,0},{12,4},{1,9},{5,13},{9,1},{13,5},{2,10},{6,14},... | collective-permute-start | bytes 98312 | tf_op jit(solution)/shard_map/ppermute | solution.py:70
  48.7 3.5 %collective-permute-done.14.arrived = bf16[2,8,1024]{2,1,0:T(8,128)(2,1)S(1)} collective-permute-done((bf16[2,8,1024]{2,1,0:T(8,128)(2,1)S(1)}, bf16[2,8,1024]{2,1,0:T(8,128)(2,1)S(1)}, u32[]{:S(2)}, u32[]{:S(2)}) %collective-permute-start.14) | collective-permute-done | bytes 32800 | tf_op jit(solution)/shard_map/ppermute | solution.py:70
  52.2 0.7 %last.1 = (bf16[6,2048]{1,0:T(8,128)(2,1)}, f32[4,1536]{1,0:T(4,128)}, f32[4]{0:T(128)}) custom-call(f32[16,1024]{1,0:T(8,128)S(1)} %get-tuple-element.76.own, bf16[2,8,1024]{2,1,0:T(8,128)(2,1)S(1)} %collective-permute-done.14.arrived, f32[4,768]{1,0:T(4,128)S(1)} %get-tuple-element.78.grads, f32[4,768]{1,0:T(4,128)S(1)} %get-tuple-element.79.other_grads), custom_call_target="tpu_custom_call" | custom-call | flops 1000 | bytes 1000 | tf_op jit(solution)/shard_map/last/pallas_call | solution.py:83
  (2 shorter events, 0.1 us)
Async XLA Ops:
  1.4 8.0 %collective-permute-start = (bf16[3,8,1024]{2,1,0:T(8,128)(2,1)S(1)}, bf16[3,8,1024]{2,1,0:T(8,128)(2,1)S(1)}, u32[]{:S(2)}, u32[]{:S(2)}) collective-permute-start(bf16[3,8,1024]{2,1,0:T(8,128)(2,1)S(1)} %pack.1.own), channel_id=1, source_target_pairs={{0,8},{4,12},{8,0},{12,4},{1,9},{5,13},{9,1},{13,5},{2,10},{6,14},... | collective-permute-start | bytes 147464 | tf_op jit(solution)/shard_map/ppermute | solution.py:70
  9.5 7.9 %collective-permute-start.2 = (bf16[7,8,1024]{2,1,0:T(8,128)(2,1)S(1)}, bf16[7,8,1024]{2,1,0:T(8,128)(2,1)S(1)}, u32[]{:S(2)}, u32[]{:S(2)}) collective-permute-start(bf16[7,8,1024]{2,1,0:T(8,128)(2,1)S(1)} %get-tuple-element.44.refs_3_.refs_4_), channel_id=1, source_target_pairs={{0,16},{16,0},{1,17},{17,1},{2,18},{18,2},{3,19},{19,3},{4,20},{20... | collective-permute-start | bytes 344072 | tf_op jit(solution)/shard_map/ppermute | solution.py:70
  11.1 6.2 %collective-permute-start.3 = (bf16[6,8,1024]{2,1,0:T(8,128)(2,1)S(1)}, bf16[6,8,1024]{2,1,0:T(8,128)(2,1)S(1)}, u32[]{:S(2)}, u32[]{:S(2)}) collective-permute-start(bf16[6,8,1024]{2,1,0:T(8,128)(2,1)S(1)} %get-tuple-element.45.refs_3_), channel_id=1, source_target_pairs={{0,20},{4,16},{8,28},{12,24},{16,4},{20,0},{24,12},{28,8},{1,21},{... | collective-permute-start | bytes 294920 | tf_op jit(solution)/shard_map/ppermute | solution.py:70
  12.6 4.7 %collective-permute-start.1 = (bf16[6,8,1024]{2,1,0:T(8,128)(2,1)S(1)}, bf16[6,8,1024]{2,1,0:T(8,128)(2,1)S(1)}, u32[]{:S(2)}, u32[]{:S(2)}) collective-permute-start(bf16[6,8,1024]{2,1,0:T(8,128)(2,1)S(1)} %get-tuple-element.45.refs_3_), channel_id=1, source_target_pairs={{0,4},{4,0},{8,12},{12,8},{1,5},{5,1},{9,13},{13,9},{2,6},{6,2},{1... | collective-permute-start | bytes 294920 | tf_op jit(solution)/shard_map/ppermute | solution.py:70
  20.3 2.2 %collective-permute-start.4 = (f32[3,48,768]{2,1,0:T(8,128)S(1)}, f32[3,48,768]{2,1,0:T(8,128)S(1)}, u32[]{:S(2)}, u32[]{:S(2)}) collective-permute-start(f32[3,48,768]{2,1,0:T(8,128)S(1)} %get-tuple-element.58), channel_id=1, source_target_pairs={{0,1},{1,0},{2,3},{3,2},{4,5},{5,4},{6,7},{7,6},{8,9},{9,8},{10,11... | collective-permute-start | bytes 1327112 | tf_op jit(solution)/shard_map/ppermute | solution.py:70
  22.5 7.9 %collective-permute-start.6 = (bf16[3,48,768]{2,1,0:T(8,128)(2,1)S(1)}, bf16[3,48,768]{2,1,0:T(8,128)(2,1)S(1)}, u32[]{:S(2)}, u32[]{:S(2)}) collective-permute-start(bf16[3,48,768]{2,1,0:T(8,128)(2,1)S(1)} %join.1.refs_8_), channel_id=1, source_target_pairs={{0,2},{1,3},{2,0},{3,1},{4,6},{5,7},{6,4},{7,5},{8,10},{9,11},{10,... | collective-permute-start | bytes 663560 | tf_op jit(solution)/shard_map/ppermute | solution.py:70
  27.0 3.4 %collective-permute-start.5 = (bf16[3,48,768]{2,1,0:T(8,128)(2,1)S(1)}, bf16[3,48,768]{2,1,0:T(8,128)(2,1)S(1)}, u32[]{:S(2)}, u32[]{:S(2)}) collective-permute-start(bf16[3,48,768]{2,1,0:T(8,128)(2,1)S(1)} %get-tuple-element.62), channel_id=1, source_target_pairs={{0,1},{1,0},{2,3},{3,2},{4,5},{5,4},{6,7},{7,6},{8,9},{9,8},{10,11... | collective-permute-start | bytes 663560 | tf_op jit(solution)/shard_map/ppermute | solution.py:70
  27.3 3.1 %copy-start = (f32[6144]{0:T(1024)S(1)}, f32[6144]{0:T(1024)}, u32[]{:S(2)}) copy-start(f32[6144]{0:T(1024)} %param.12) | copy-start | bytes 73732
  30.8 5.6 %collective-permute-start.7 = (bf16[74,8,128]{2,1,0:T(8,128)(2,1)S(1)}, bf16[74,8,128]{2,1,0:T(8,128)(2,1)S(1)}, u32[]{:S(2)}, u32[]{:S(2)}) collective-permute-start(bf16[74,8,128]{2,1,0:T(8,128)(2,1)S(1)} %get-tuple-element.64), channel_id=1, source_target_pairs={{0,2},{1,3},{2,0},{3,1},{4,6},{5,7},{6,4},{7,5},{8,10},{9,11},{10,... | collective-permute-start | bytes 454664 | tf_op jit(solution)/shard_map/ppermute | solution.py:70
  32.3 2.3 %collective-permute-start.8 = (bf16[64,768]{1,0:T(8,128)(2,1)S(1)}, bf16[64,768]{1,0:T(8,128)(2,1)S(1)}, u32[]{:S(2)}, u32[]{:S(2)}) collective-permute-start(bf16[64,768]{1,0:T(8,128)(2,1)S(1)} %get-tuple-element.65), channel_id=1, source_target_pairs={{0,1},{1,0},{2,3},{3,2},{4,5},{5,4},{6,7},{7,6},{8,9},{9,8},{10,11... | collective-permute-start | bytes 294920 | tf_op jit(solution)/shard_map/ppermute | solution.py:70
  32.3 2.3 %collective-permute-start.9 = (bf16[48,768]{1,0:T(8,128)(2,1)S(1)}, bf16[48,768]{1,0:T(8,128)(2,1)S(1)}, u32[]{:S(2)}, u32[]{:S(2)}) collective-permute-start(bf16[48,768]{1,0:T(8,128)(2,1)S(1)} %get-tuple-element.66), channel_id=1, source_target_pairs={{0,1},{1,0},{2,3},{3,2},{4,5},{5,4},{6,7},{7,6},{8,9},{9,8},{10,11... | collective-permute-start | bytes 221192 | tf_op jit(solution)/shard_map/ppermute | solution.py:70
  36.4 1.8 %collective-permute-start.10 = (bf16[74,8,128]{2,1,0:T(8,128)(2,1)S(1)}, bf16[74,8,128]{2,1,0:T(8,128)(2,1)S(1)}, u32[]{:S(2)}, u32[]{:S(2)}) collective-permute-start(bf16[74,8,128]{2,1,0:T(8,128)(2,1)S(1)} %collective-permute-done.7.tiles.refs_2_), channel_id=1, source_target_pairs={{0,1},{1,0},{2,3},{3,2},{4,5},{5,4},{6,7},{7,6},{8,9},{9,8},{10,11... | collective-permute-start | bytes 454664 | tf_op jit(solution)/shard_map/ppermute | solution.py:70
  40.2 7.1 %collective-permute-start.12 = (bf16[4,8,1024]{2,1,0:T(8,128)(2,1)S(1)}, bf16[4,8,1024]{2,1,0:T(8,128)(2,1)S(1)}, u32[]{:S(2)}, u32[]{:S(2)}) collective-permute-start(bf16[4,8,1024]{2,1,0:T(8,128)(2,1)S(1)} %get-tuple-element.74), channel_id=1, source_target_pairs={{0,16},{16,0},{1,17},{17,1},{2,18},{18,2},{3,19},{19,3},{4,20},{20... | collective-permute-start | bytes 196616 | tf_op jit(solution)/shard_map/ppermute | solution.py:70
  41.8 5.4 %collective-permute-start.11 = (bf16[3,8,1152]{2,1,0:T(8,128)(2,1)S(1)}, bf16[3,8,1152]{2,1,0:T(8,128)(2,1)S(1)}, u32[]{:S(2)}, u32[]{:S(2)}) collective-permute-start(bf16[3,8,1152]{2,1,0:T(8,128)(2,1)S(1)} %get-tuple-element.73), channel_id=1, source_target_pairs={{0,20},{4,16},{8,28},{12,24},{16,4},{20,0},{24,12},{28,8},{1,21},{... | collective-permute-start | bytes 165896 | tf_op jit(solution)/shard_map/ppermute | solution.py:70
  43.1 4.2 %collective-permute-start.13 = (bf16[3,8,1152]{2,1,0:T(8,128)(2,1)S(1)}, bf16[3,8,1152]{2,1,0:T(8,128)(2,1)S(1)}, u32[]{:S(2)}, u32[]{:S(2)}) collective-permute-start(bf16[3,8,1152]{2,1,0:T(8,128)(2,1)S(1)} %get-tuple-element.75), channel_id=1, source_target_pairs={{0,4},{4,0},{8,12},{12,8},{1,5},{5,1},{9,13},{13,9},{2,6},{6,2},{1... | collective-permute-start | bytes 165896 | tf_op jit(solution)/shard_map/ppermute | solution.py:70
  47.3 4.9 %collective-permute-start.14 = (bf16[2,8,1024]{2,1,0:T(8,128)(2,1)S(1)}, bf16[2,8,1024]{2,1,0:T(8,128)(2,1)S(1)}, u32[]{:S(2)}, u32[]{:S(2)}) collective-permute-start(bf16[2,8,1024]{2,1,0:T(8,128)(2,1)S(1)} %get-tuple-element.77), channel_id=1, source_target_pairs={{0,8},{4,12},{8,0},{12,4},{1,9},{5,13},{9,1},{13,5},{2,10},{6,14},... | collective-permute-start | bytes 98312 | tf_op jit(solution)/shard_map/ppermute | solution.py:70

commit v17 on v16

--- a/solution.py
+++ b/solution.py
@@ -134,7 +134,7 @@
 WIDE, NEXT, FAR = 4, 1, 2
 GATE, UP, DOWN = range(3)
 WHOLE_STRIP = (GATE, UP, DOWN)
-CHUNKS = 4
+CHUNKS = 8
 
 
 def start_loads(pieces, groups, sources, targets, sem):
@@ -146,9 +146,8 @@
         start = pl.multiple_of((owner * groups + lax.axis_index("groups")) * width, width)
         source = sources[kind]
         source = source.at[pl.ds(start, width), :] if kind == DOWN else source.at[:, pl.ds(start, width)]
-        chunks = CHUNKS if len(pieces) == 1 else 1
-        size = target.shape[0] // chunks
-        for c in range(chunks):
+        size = target.shape[0] // CHUNKS
+        for c in range(CHUNKS):
             span = slice(c * size, (c + 1) * size)
             copies.append(pltpu.make_async_copy(source.at[span, :], target.at[span, :], sem.at[i, c]))
     for copy in copies:
@@ -371,7 +370,7 @@
         if target is not own:
             for k in range(slabs):
                 target[k, :, 0:side] = stage[8 * k : 8 * k + 8, :].astype(jnp.bfloat16)
-                if target.shape[2] > side:
+                if target is sends[0]:
                     tail = tails[k] if k < 2 else jnp.zeros_like(squares)
                     target[k, :, side:] = tail.astype(jnp.bfloat16)
     width = other_grads.shape[1]
@@ -380,7 +379,8 @@
         stage[i * SEQS : (i + 1) * SEQS, 0:width] = rows
     for i, rows in enumerate(tails):
         stage[0:8, width + i * 128 : width + (i + 1) * 128] = rows
-    sends[1][slabs] = stage[0:8, :].astype(jnp.bfloat16)
+    for target in sends[1:]:
+        target[slabs] = stage[0:8, :].astype(jnp.bfloat16)
 
 
 def combine_kernel(share, own, own_squares, diagonal, across, beside, *refs):
@@ -394,10 +394,11 @@
         total[8 * k : 8 * k + 8, :] = rows
     tail = across[slabs].astype(jnp.float32)
     other_grads[...] = tail[0:SEQS, 0:width] + tail[SEQS : 2 * SEQS, 0:width]
-    same, turned = own_squares[...], tail[:, width : width + 128] + tail[:, width + 128 : width + 256]
+    same, turned = own_squares[...], jnp.zeros(own_squares.shape, jnp.float32)
     for k in range(2):
         same = same + beside[k, :, side:].astype(jnp.float32)
-        turned = turned + diagonal[k, :, side:].astype(jnp.float32)
+        for rows in (tail, diagonal[slabs].astype(jnp.float32)):
+            turned = turned + rows[:, width + k * 128 : width + (k + 1) * 128]
     squares = same[0:SEQS] + turned[SEQS : 2 * SEQS]
     count = 2 * share
     kept_rows[...] = jnp.zeros_like(kept_rows)
@@ -501,7 +502,7 @@
         [pltpu.VMEM((2 * slabs, 8, side), bf16), pltpu.VMEM((2 * slabs + 1, 8, side), bf16)],
         [packed, far, marks],
     )
-    diagonal = exchange(pair, ("groups", "wide"), WIDE + NEXT)
+    diagonal = exchange(marked, ("groups", "wide"), WIDE + NEXT)
     other_marked = exchange(marked, "groups", 1)
     beside = exchange(pair, "wide", NEXT)
     load("load_b", [(kind, 2) for kind in WHOLE_STRIP], [pair])
@@ -567,7 +568,7 @@
             pltpu.VMEM((8, 128), f32),
             block,
             pltpu.VMEM((slabs + 1, 8, side), bf16),
-            block,
+            pltpu.VMEM((slabs + 1, 8, side), bf16),
         ],
         [message_3] + hold(3, [GATE, UP]) + [sums, message, near_gate, message_2, other_grads],
         scratch=[pltpu.VMEM((tokens, features), f32), pltpu.VMEM((4 * share, side), f32)],

time: 53.2 us -> 53.6 us (level)
  waiting for transfers between devices: 8.04 us -> 8.64 us
    ppermute x15, waiting for transfers between devices: 8.04 us -> 8.64 us  [exchange(): return lax.ppermute(array, axes, [(i, i ^ step) for i in range(size)])]
  transfers between devices with their start and end apart: 15 -> 15, of which waited for: 6 -> 5; matrix products, arithmetic and copies ran while one was open for 0% -> 0% of each run, Pallas kernels for 39% -> 39%
where the time goes in v17:
time: 53.6 us; the launch traced here: 53.4 us
  Pallas kernels  27.6 us (51%)
  starting transfers between devices  16.2 us (30%)
  waiting for transfers between devices  8.64 us (16%)
  between operations  0.95 us (2%)
    pallas_call x16, Pallas kernels, call(): pl.pallas_call(body, out_shape=outs, in_specs=[pl.BlockSpec(memory_space=...  27.6 us
    ppermute x15, starting transfers between devices, exchange(): return lax.ppermute(array, axes, [(i, i ^ step) for i in range(size)])  16.2 us
    ppermute x15, waiting for transfers between devices, exchange(): return lax.ppermute(array, axes, [(i, i ^ step) for i in range(size)])  8.64 us
  transfers between devices with their start and end apart: 15, of which 5 were waited for; matrix products, arithmetic and copies ran while one was open for 0% of the time, Pallas kernels for 39%

profile of v17, /device:TPU:0, one launch (start us, length us, event | category | flops | bytes accessed | tf_op | source)
XLA Modules:
  0.0 53.4 jit_solution(2536268695990935759)
XLA Ops:
  0.6 0.8 %pack.1.own = bf16[3,8,1024]{2,1,0:T(8,128)(2,1)S(1)} custom-call(bf16[6,2048]{1,0:T(8,128)(2,1)} %inputs.1, bf16[6,2048]{1,0:T(8,128)(2,1)} %cotangent.1), custom_call_target="tpu_custom_call" | custom-call | flops 1000 | bytes 1000 | tf_op jit(solution)/shard_map/pack/pallas_call | solution.py:83
  1.4 4.1 %collective-permute-start = (bf16[3,8,1024]{2,1,0:T(8,128)(2,1)S(1)}, bf16[3,8,1024]{2,1,0:T(8,128)(2,1)S(1)}, u32[]{:S(2)}, u32[]{:S(2)}) collective-permute-start(bf16[3,8,1024]{2,1,0:T(8,128)(2,1)S(1)} %pack.1.own), channel_id=1, source_target_pairs={{0,8},{4,12},{8,0},{12,4},{1,9},{5,13},{9,1},{13,5},{2,10},{6,14},... | collective-permute-start | bytes 147464 | tf_op jit(solution)/shard_map/ppermute | solution.py:70
  5.5 4.0 %load_a.1 = (bf16[2048,768]{1,0:T(8,128)(2,1)S(1)}, bf16[2048,768]{1,0:T(8,128)(2,1)S(1)}, bf16[768,2048]{1,0:T(8,128)(2,1)S(1)}, bf16[8,1024]{1,0:T(8,128)(2,1)S(1)}) custom-call(bf16[2048,6144]{1,0:T(8,128)(2,1)} %refs_0_.11, bf16[2048,6144]{1,0:T(8,128)(2,1)} %refs_1_.11, bf16[6144,2048]{1,0:T(8,128)(2,1)} %refs_2_.11, s32[1,24]{1,0:T(1,128)} %bitcast.3), custom_call_target="tpu_custom_call" | custom-call | flops 1000 | bytes 1000 | tf_op jit(solution)/shard_map/load_a/pallas_call | solution.py:83
  9.5 0.0 collective-permute-done.far
  9.6 2.6 %collective-permute-start.3 = (bf16[7,8,1024]{2,1,0:T(8,128)(2,1)S(1)}, bf16[7,8,1024]{2,1,0:T(8,128)(2,1)S(1)}, u32[]{:S(2)}, u32[]{:S(2)}) collective-permute-start(bf16[7,8,1024]{2,1,0:T(8,128)(2,1)S(1)} %get-tuple-element.44.refs_3_.refs_4_), channel_id=1, source_target_pairs={{0,20},{4,16},{8,28},{12,24},{16,4},{20,0},{24,12},{28,8},{1,21},{... | collective-permute-start | bytes 344072 | tf_op jit(solution)/shard_map/ppermute | solution.py:70
  12.2 0.5 collective-permute-start.2
  12.7 0.4 collective-permute-start.1
  13.1 3.9 %load_b.1 = (bf16[2048,768]{1,0:T(8,128)(2,1)S(1)}, bf16[2048,768]{1,0:T(8,128)(2,1)S(1)}, bf16[768,2048]{1,0:T(8,128)(2,1)S(1)}) custom-call(bf16[2048,6144]{1,0:T(8,128)(2,1)} %refs_0_.11, bf16[2048,6144]{1,0:T(8,128)(2,1)} %refs_1_.11, bf16[6144,2048]{1,0:T(8,128)(2,1)} %refs_2_.11, bf16[6,8,1024]{2,1,0:T(8,128)(2,1)S(1)} %get-tuple-element.45.refs_3_), custom_call_target="tpu_custom_call" | custom-call | flops 1000 | bytes 1000 | tf_op jit(solution)/shard_map/load_b/pallas_call | solution.py:83
  17.0 0.4 collective-permute-done.1.refs_4_
  17.5 0.0 collective-permute-done.3.refs_6_
  17.5 0.2 collective-permute-done.2.refs_5_
  17.6 2.9 %forward_3.1 = (bf16[2048,768]{1,0:T(8,128)(2,1)S(1)}, bf16[768,2048]{1,0:T(8,128)(2,1)S(1)}, bf16[48,2048]{1,0:T(8,128)(2,1)S(1)}, bf16[48,2048]{1,0:T(8,128)(2,1)S(1)}, f32[3,48,768]{2,1,0:T(8,128)S(1)}) custom-call(bf16[2048,6144]{1,0:T(8,128)(2,1)} %refs_0_.11, bf16[2048,6144]{1,0:T(8,128)(2,1)} %refs_1_.11, bf16[6144,2048]{1,0:T(8,128)(2,1)} %refs_2_.11, ...), custom_call_target="tpu_custom_call" | custom-call | flops 1000 | bytes 1000 | tf_op jit(solution)/shard_map/forward_3/pallas_call | solution.py:83
  20.6 0.1 collective-permute-start.4
  20.6 2.1 %forward_2.1 = (bf16[2048,768]{1,0:T(8,128)(2,1)S(1)}, f32[3,48,768]{2,1,0:T(8,128)S(1)}) custom-call(bf16[2048,6144]{1,0:T(8,128)(2,1)} %refs_0_.11, bf16[2048,6144]{1,0:T(8,128)(2,1)} %refs_1_.11, bf16[6144,2048]{1,0:T(8,128)(2,1)} %refs_2_.11, bf16[48,2048]{1,0:T(8,128)(2,1)S(1)} %get-tuple-element.50.refs_3_, ...), custom_call_target="tpu_custom_call" | custom-call | flops 1000 | bytes 1000 | tf_op jit(solution)/shard_map/forward_2/pallas_call | solution.py:83
  22.8 0.0 collective-permute-done.4.arrived
  22.8 1.6 %collective-permute-start.6 = (bf16[3,48,768]{2,1,0:T(8,128)(2,1)S(1)}, bf16[3,48,768]{2,1,0:T(8,128)(2,1)S(1)}, u32[]{:S(2)}, u32[]{:S(2)}) collective-permute-start(bf16[3,48,768]{2,1,0:T(8,128)(2,1)S(1)} %join.1.refs_8_), channel_id=1, source_target_pairs={{0,2},{1,3},{2,0},{3,1},{4,6},{5,7},{6,4},{7,5},{8,10},{9,11},{10,... | collective-permute-start | bytes 663560 | tf_op jit(solution)/shard_map/ppermute | solution.py:70
  24.4 2.9 %forward_1.1 = (bf16[2048,768]{1,0:T(8,128)(2,1)S(1)}, bf16[768,2048]{1,0:T(8,128)(2,1)S(1)}, bf16[3,48,768]{2,1,0:T(8,128)(2,1)S(1)}) custom-call(bf16[2048,6144]{1,0:T(8,128)(2,1)} %refs_0_.11, bf16[2048,6144]{1,0:T(8,128)(2,1)} %refs_1_.11, bf16[6144,2048]{1,0:T(8,128)(2,1)} %refs_2_.11, bf16[48,2048]{1,0:T(8,128)(2,1)S(1)} %get-tuple-element.50.refs_3_, ...), custom_call_target="tpu_custom_call" | custom-call | flops 1000 | bytes 1000 | tf_op jit(solution)/shard_map/forward_1/pallas_call | solution.py:83
  27.4 0.3 collective-permute-start.5
  27.6 0.0 copy-start
  27.6 2.6 %forward_0.1 = (f32[3,48,768]{2,1,0:T(8,128)S(1)}, bf16[2048,768]{1,0:T(8,128)(2,1)S(1)}) custom-call(bf16[2048,6144]{1,0:T(8,128)(2,1)} %refs_0_.11, bf16[2048,6144]{1,0:T(8,128)(2,1)} %refs_1_.11, bf16[6144,2048]{1,0:T(8,128)(2,1)} %refs_2_.11, bf16[48,2048]{1,0:T(8,128)(2,1)S(1)} %get-tuple-element.50.refs_3_, ...), custom_call_target="tpu_custom_call" | custom-call | flops 1000 | bytes 1000 | tf_op jit(solution)/shard_map/forward_0/pallas_call | solution.py:83
  30.2 0.5 collective-permute-done.6.refs_2_
  30.7 0.0 collective-permute-done.5.refs_1_
  30.7 0.0 copy-done
  30.7 0.4 middle.1
  31.1 1.5 %collective-permute-start.7 = (bf16[74,8,128]{2,1,0:T(8,128)(2,1)S(1)}, bf16[74,8,128]{2,1,0:T(8,128)(2,1)S(1)}, u32[]{:S(2)}, u32[]{:S(2)}) collective-permute-start(bf16[74,8,128]{2,1,0:T(8,128)(2,1)S(1)} %get-tuple-element.64), channel_id=1, source_target_pairs={{0,2},{1,3},{2,0},{3,1},{4,6},{5,7},{6,4},{7,5},{8,10},{9,11},{10,... | collective-permute-start | bytes 454664 | tf_op jit(solution)/shard_map/ppermute | solution.py:70
  32.6 0.0 collective-permute-start.8
  32.6 0.5 collective-permute-start.9
  33.1 1.7 %backward_0.1.before = f32[2048,48]{1,0:T(8,128)S(1)} custom-call(bf16[112,768]{1,0:T(8,128)(2,1)S(1)} %get-tuple-element.67.message.refs_0_, bf16[2048,768]{1,0:T(8,128)(2,1)S(1)} %get-tuple-element.63.refs_6_.gate, bf16[2048,768]{1,0:T(8,128)(2,1)S(1)} %get-tuple-element.59.refs_5_.refs_7_.up), custom_call_target="tpu_custom_call" | custom-call | flops 1000 | bytes 1000 | tf_op jit(solution)/shard_map/backward_0/pallas_call | solution.py:83
  34.9 0.0 collective-permute-done.9.d_up
  34.9 0.0 collective-permute-done.8.d_gate.refs_1_
  34.9 1.8 %backward_1.1.before = f32[2048,48]{1,0:T(8,128)S(1)} custom-call(bf16[64,768]{1,0:T(8,128)(2,1)S(1)} %collective-permute-done.8.d_gate.refs_1_, bf16[48,768]{1,0:T(8,128)(2,1)S(1)} %collective-permute-done.9.d_up, bf16[2048,768]{1,0:T(8,128)(2,1)S(1)} %get-tuple-element.52.refs_5_.refs_8_.gate, bf16[2048,768]{1,0:T(8,128)(2,1)S(1)} %get-tuple-element.55.refs_6_.refs_9_.up, ...), custom_call_target="tpu_custom_call" | custom-call | flops 1000 | bytes 1000 | tf_op jit(solution)/shard_map/backward_1/pallas_call | solution.py:83
  36.7 0.0 collective-permute-done.7.tiles.refs_2_
  36.8 0.0 collective-permute-start.10
  36.8 1.8 %backward_2.1.before = f32[2048,48]{1,0:T(8,128)S(1)} custom-call(bf16[74,8,128]{2,1,0:T(8,128)(2,1)S(1)} %collective-permute-done.7.tiles.refs_2_, bf16[2048,768]{1,0:T(8,128)(2,1)S(1)} %get-tuple-element.49.refs_10_.refs_5_.gate, bf16[2048,768]{1,0:T(8,128)(2,1)S(1)} %get-tuple-element.53.refs_6_.refs_11_.up, f32[2048,48]{1,0:T(8,128)S(1)} %backward_1.1.before), custom_call_target="tpu_custom_call" | custom-call | flops 1000 | bytes 1000 | tf_op jit(solution)/shard_map/backward_2/pallas_call | solution.py:83
  38.6 0.0 collective-permute-done.10.tiles
  38.6 1.9 %backward_3.1 = (f32[24,1024]{1,0:T(8,128)S(1)}, f32[8,128]{1,0:T(8,128)S(1)}, bf16[3,8,1152]{2,1,0:T(8,128)(2,1)S(1)}, bf16[4,8,1024]{2,1,0:T(8,128)(2,1)S(1)}, bf16[4,8,1024]{2,1,0:T(8,128)(2,1)S(1)}) custom-call(bf16[74,8,128]{2,1,0:T(8,128)(2,1)S(1)} %collective-permute-done.10.tiles, bf16[2048,768]{1,0:T(8,128)(2,1)S(1)} %get-tuple-element.46.refs_7_.refs_12_.gate, ...), custom_call_target="tpu_custom_call" | custom-call | flops 1000 | bytes 1000 | tf_op jit(solution)/shard_map/backward_3/pallas_call | solution.py:83
  40.5 2.1 %collective-permute-start.11 = (bf16[4,8,1024]{2,1,0:T(8,128)(2,1)S(1)}, bf16[4,8,1024]{2,1,0:T(8,128)(2,1)S(1)}, u32[]{:S(2)}, u32[]{:S(2)}) collective-permute-start(bf16[4,8,1024]{2,1,0:T(8,128)(2,1)S(1)} %get-tuple-element.73), channel_id=1, source_target_pairs={{0,20},{4,16},{8,28},{12,24},{16,4},{20,0},{24,12},{28,8},{1,21},{... | collective-permute-start | bytes 196616 | tf_op jit(solution)/shard_map/ppermute | solution.py:70
  42.6 0.9 %collective-permute-start.12 = (bf16[4,8,1024]{2,1,0:T(8,128)(2,1)S(1)}, bf16[4,8,1024]{2,1,0:T(8,128)(2,1)S(1)}, u32[]{:S(2)}, u32[]{:S(2)}) collective-permute-start(bf16[4,8,1024]{2,1,0:T(8,128)(2,1)S(1)} %get-tuple-element.74), channel_id=1, source_target_pairs={{0,16},{16,0},{1,17},{17,1},{2,18},{18,2},{3,19},{19,3},{4,20},{20... | collective-permute-start | bytes 196616 | tf_op jit(solution)/shard_map/ppermute | solution.py:70
  43.5 0.6 %collective-permute-start.13 = (bf16[3,8,1152]{2,1,0:T(8,128)(2,1)S(1)}, bf16[3,8,1152]{2,1,0:T(8,128)(2,1)S(1)}, u32[]{:S(2)}, u32[]{:S(2)}) collective-permute-start(bf16[3,8,1152]{2,1,0:T(8,128)(2,1)S(1)} %get-tuple-element.75), channel_id=1, source_target_pairs={{0,4},{4,0},{8,12},{12,8},{1,5},{5,1},{9,13},{13,9},{2,6},{6,2},{1... | collective-permute-start | bytes 165896 | tf_op jit(solution)/shard_map/ppermute | solution.py:70
  44.1 3.6 %collective-permute-done.13.beside = bf16[3,8,1152]{2,1,0:T(8,128)(2,1)S(1)} collective-permute-done((bf16[3,8,1152]{2,1,0:T(8,128)(2,1)S(1)}, bf16[3,8,1152]{2,1,0:T(8,128)(2,1)S(1)}, u32[]{:S(2)}, u32[]{:S(2)}) %collective-permute-start.13) | collective-permute-done | bytes 55328 | tf_op jit(solution)/shard_map/ppermute | solution.py:70
  47.7 0.0 collective-permute-done.11.diagonal
  47.7 0.0 collective-permute-done.12.across
  47.7 0.1 combine.1
  47.7 1.0 %collective-permute-start.14 = (bf16[2,8,1024]{2,1,0:T(8,128)(2,1)S(1)}, bf16[2,8,1024]{2,1,0:T(8,128)(2,1)S(1)}, u32[]{:S(2)}, u32[]{:S(2)}) collective-permute-start(bf16[2,8,1024]{2,1,0:T(8,128)(2,1)S(1)} %get-tuple-element.77), channel_id=1, source_target_pairs={{0,8},{4,12},{8,0},{12,4},{1,9},{5,13},{9,1},{13,5},{2,10},{6,14},... | collective-permute-start | bytes 98312 | tf_op jit(solution)/shard_map/ppermute | solution.py:70
  48.7 3.9 %collective-permute-done.14.arrived = bf16[2,8,1024]{2,1,0:T(8,128)(2,1)S(1)} collective-permute-done((bf16[2,8,1024]{2,1,0:T(8,128)(2,1)S(1)}, bf16[2,8,1024]{2,1,0:T(8,128)(2,1)S(1)}, u32[]{:S(2)}, u32[]{:S(2)}) %collective-permute-start.14) | collective-permute-done | bytes 32800 | tf_op jit(solution)/shard_map/ppermute | solution.py:70
  52.6 0.7 %last.1 = (bf16[6,2048]{1,0:T(8,128)(2,1)}, f32[4,1536]{1,0:T(4,128)}, f32[4]{0:T(128)}) custom-call(f32[16,1024]{1,0:T(8,128)S(1)} %get-tuple-element.76.own, bf16[2,8,1024]{2,1,0:T(8,128)(2,1)S(1)} %collective-permute-done.14.arrived, f32[4,768]{1,0:T(4,128)S(1)} %get-tuple-element.78.grads, f32[4,768]{1,0:T(4,128)S(1)} %get-tuple-element.79.other_grads), custom_call_target="tpu_custom_call" | custom-call | flops 1000 | bytes 1000 | tf_op jit(solution)/shard_map/last/pallas_call | solution.py:83
  (2 shorter events, 0.1 us)
Async XLA Ops:
  1.4 8.1 %collective-permute-start = (bf16[3,8,1024]{2,1,0:T(8,128)(2,1)S(1)}, bf16[3,8,1024]{2,1,0:T(8,128)(2,1)S(1)}, u32[]{:S(2)}, u32[]{:S(2)}) collective-permute-start(bf16[3,8,1024]{2,1,0:T(8,128)(2,1)S(1)} %pack.1.own), channel_id=1, source_target_pairs={{0,8},{4,12},{8,0},{12,4},{1,9},{5,13},{9,1},{13,5},{2,10},{6,14},... | collective-permute-start | bytes 147464 | tf_op jit(solution)/shard_map/ppermute | solution.py:70
  9.6 7.9 %collective-permute-start.3 = (bf16[7,8,1024]{2,1,0:T(8,128)(2,1)S(1)}, bf16[7,8,1024]{2,1,0:T(8,128)(2,1)S(1)}, u32[]{:S(2)}, u32[]{:S(2)}) collective-permute-start(bf16[7,8,1024]{2,1,0:T(8,128)(2,1)S(1)} %get-tuple-element.44.refs_3_.refs_4_), channel_id=1, source_target_pairs={{0,20},{4,16},{8,28},{12,24},{16,4},{20,0},{24,12},{28,8},{1,21},{... | collective-permute-start | bytes 344072 | tf_op jit(solution)/shard_map/ppermute | solution.py:70
  12.2 5.5 %collective-permute-start.2 = (bf16[7,8,1024]{2,1,0:T(8,128)(2,1)S(1)}, bf16[7,8,1024]{2,1,0:T(8,128)(2,1)S(1)}, u32[]{:S(2)}, u32[]{:S(2)}) collective-permute-start(bf16[7,8,1024]{2,1,0:T(8,128)(2,1)S(1)} %get-tuple-element.44.refs_3_.refs_4_), channel_id=1, source_target_pairs={{0,16},{16,0},{1,17},{17,1},{2,18},{18,2},{3,19},{19,3},{4,20},{20... | collective-permute-start | bytes 344072 | tf_op jit(solution)/shard_map/ppermute | solution.py:70
  12.7 4.8 %collective-permute-start.1 = (bf16[6,8,1024]{2,1,0:T(8,128)(2,1)S(1)}, bf16[6,8,1024]{2,1,0:T(8,128)(2,1)S(1)}, u32[]{:S(2)}, u32[]{:S(2)}) collective-permute-start(bf16[6,8,1024]{2,1,0:T(8,128)(2,1)S(1)} %get-tuple-element.45.refs_3_), channel_id=1, source_target_pairs={{0,4},{4,0},{8,12},{12,8},{1,5},{5,1},{9,13},{13,9},{2,6},{6,2},{1... | collective-permute-start | bytes 294920 | tf_op jit(solution)/shard_map/ppermute | solution.py:70
  20.6 2.2 %collective-permute-start.4 = (f32[3,48,768]{2,1,0:T(8,128)S(1)}, f32[3,48,768]{2,1,0:T(8,128)S(1)}, u32[]{:S(2)}, u32[]{:S(2)}) collective-permute-start(f32[3,48,768]{2,1,0:T(8,128)S(1)} %get-tuple-element.58), channel_id=1, source_target_pairs={{0,1},{1,0},{2,3},{3,2},{4,5},{5,4},{6,7},{7,6},{8,9},{9,8},{10,11... | collective-permute-start | bytes 1327112 | tf_op jit(solution)/shard_map/ppermute | solution.py:70
  22.8 7.9 %collective-permute-start.6 = (bf16[3,48,768]{2,1,0:T(8,128)(2,1)S(1)}, bf16[3,48,768]{2,1,0:T(8,128)(2,1)S(1)}, u32[]{:S(2)}, u32[]{:S(2)}) collective-permute-start(bf16[3,48,768]{2,1,0:T(8,128)(2,1)S(1)} %join.1.refs_8_), channel_id=1, source_target_pairs={{0,2},{1,3},{2,0},{3,1},{4,6},{5,7},{6,4},{7,5},{8,10},{9,11},{10,... | collective-permute-start | bytes 663560 | tf_op jit(solution)/shard_map/ppermute | solution.py:70
  27.4 3.4 %collective-permute-start.5 = (bf16[3,48,768]{2,1,0:T(8,128)(2,1)S(1)}, bf16[3,48,768]{2,1,0:T(8,128)(2,1)S(1)}, u32[]{:S(2)}, u32[]{:S(2)}) collective-permute-start(bf16[3,48,768]{2,1,0:T(8,128)(2,1)S(1)} %get-tuple-element.62), channel_id=1, source_target_pairs={{0,1},{1,0},{2,3},{3,2},{4,5},{5,4},{6,7},{7,6},{8,9},{9,8},{10,11... | collective-permute-start | bytes 663560 | tf_op jit(solution)/shard_map/ppermute | solution.py:70
  27.6 3.1 %copy-start = (f32[6144]{0:T(1024)S(1)}, f32[6144]{0:T(1024)}, u32[]{:S(2)}) copy-start(f32[6144]{0:T(1024)} %param.12) | copy-start | bytes 73732
  31.1 5.7 %collective-permute-start.7 = (bf16[74,8,128]{2,1,0:T(8,128)(2,1)S(1)}, bf16[74,8,128]{2,1,0:T(8,128)(2,1)S(1)}, u32[]{:S(2)}, u32[]{:S(2)}) collective-permute-start(bf16[74,8,128]{2,1,0:T(8,128)(2,1)S(1)} %get-tuple-element.64), channel_id=1, source_target_pairs={{0,2},{1,3},{2,0},{3,1},{4,6},{5,7},{6,4},{7,5},{8,10},{9,11},{10,... | collective-permute-start | bytes 454664 | tf_op jit(solution)/shard_map/ppermute | solution.py:70
  32.6 2.3 %collective-permute-start.8 = (bf16[64,768]{1,0:T(8,128)(2,1)S(1)}, bf16[64,768]{1,0:T(8,128)(2,1)S(1)}, u32[]{:S(2)}, u32[]{:S(2)}) collective-permute-start(bf16[64,768]{1,0:T(8,128)(2,1)S(1)} %get-tuple-element.65), channel_id=1, source_target_pairs={{0,1},{1,0},{2,3},{3,2},{4,5},{5,4},{6,7},{7,6},{8,9},{9,8},{10,11... | collective-permute-start | bytes 294920 | tf_op jit(solution)/shard_map/ppermute | solution.py:70
  32.6 2.3 %collective-permute-start.9 = (bf16[48,768]{1,0:T(8,128)(2,1)S(1)}, bf16[48,768]{1,0:T(8,128)(2,1)S(1)}, u32[]{:S(2)}, u32[]{:S(2)}) collective-permute-start(bf16[48,768]{1,0:T(8,128)(2,1)S(1)} %get-tuple-element.66), channel_id=1, source_target_pairs={{0,1},{1,0},{2,3},{3,2},{4,5},{5,4},{6,7},{7,6},{8,9},{9,8},{10,11... | collective-permute-start | bytes 221192 | tf_op jit(solution)/shard_map/ppermute | solution.py:70
  36.8 1.8 %collective-permute-start.10 = (bf16[74,8,128]{2,1,0:T(8,128)(2,1)S(1)}, bf16[74,8,128]{2,1,0:T(8,128)(2,1)S(1)}, u32[]{:S(2)}, u32[]{:S(2)}) collective-permute-start(bf16[74,8,128]{2,1,0:T(8,128)(2,1)S(1)} %collective-permute-done.7.tiles.refs_2_), channel_id=1, source_target_pairs={{0,1},{1,0},{2,3},{3,2},{4,5},{5,4},{6,7},{7,6},{8,9},{9,8},{10,11... | collective-permute-start | bytes 454664 | tf_op jit(solution)/shard_map/ppermute | solution.py:70
  40.5 7.1 %collective-permute-start.11 = (bf16[4,8,1024]{2,1,0:T(8,128)(2,1)S(1)}, bf16[4,8,1024]{2,1,0:T(8,128)(2,1)S(1)}, u32[]{:S(2)}, u32[]{:S(2)}) collective-permute-start(bf16[4,8,1024]{2,1,0:T(8,128)(2,1)S(1)} %get-tuple-element.73), channel_id=1, source_target_pairs={{0,20},{4,16},{8,28},{12,24},{16,4},{20,0},{24,12},{28,8},{1,21},{... | collective-permute-start | bytes 196616 | tf_op jit(solution)/shard_map/ppermute | solution.py:70
  42.6 5.0 %collective-permute-start.12 = (bf16[4,8,1024]{2,1,0:T(8,128)(2,1)S(1)}, bf16[4,8,1024]{2,1,0:T(8,128)(2,1)S(1)}, u32[]{:S(2)}, u32[]{:S(2)}) collective-permute-start(bf16[4,8,1024]{2,1,0:T(8,128)(2,1)S(1)} %get-tuple-element.74), channel_id=1, source_target_pairs={{0,16},{16,0},{1,17},{17,1},{2,18},{18,2},{3,19},{19,3},{4,20},{20... | collective-permute-start | bytes 196616 | tf_op jit(solution)/shard_map/ppermute | solution.py:70
  43.5 4.2 %collective-permute-start.13 = (bf16[3,8,1152]{2,1,0:T(8,128)(2,1)S(1)}, bf16[3,8,1152]{2,1,0:T(8,128)(2,1)S(1)}, u32[]{:S(2)}, u32[]{:S(2)}) collective-permute-start(bf16[3,8,1152]{2,1,0:T(8,128)(2,1)S(1)} %get-tuple-element.75), channel_id=1, source_target_pairs={{0,4},{4,0},{8,12},{12,8},{1,5},{5,1},{9,13},{13,9},{2,6},{6,2},{1... | collective-permute-start | bytes 165896 | tf_op jit(solution)/shard_map/ppermute | solution.py:70
  47.7 4.9 %collective-permute-start.14 = (bf16[2,8,1024]{2,1,0:T(8,128)(2,1)S(1)}, bf16[2,8,1024]{2,1,0:T(8,128)(2,1)S(1)}, u32[]{:S(2)}, u32[]{:S(2)}) collective-permute-start(bf16[2,8,1024]{2,1,0:T(8,128)(2,1)S(1)} %get-tuple-element.77), channel_id=1, source_target_pairs={{0,8},{4,12},{8,0},{12,4},{1,9},{5,13},{9,1},{13,5},{2,10},{6,14},... | collective-permute-start | bytes 98312 | tf_op jit(solution)/shard_map/ppermute | solution.py:70

commit v18 on v16

--- a/solution.py
+++ b/solution.py
@@ -146,9 +146,8 @@
         start = pl.multiple_of((owner * groups + lax.axis_index("groups")) * width, width)
         source = sources[kind]
         source = source.at[pl.ds(start, width), :] if kind == DOWN else source.at[:, pl.ds(start, width)]
-        chunks = CHUNKS if len(pieces) == 1 else 1
-        size = target.shape[0] // chunks
-        for c in range(chunks):
+        size = target.shape[0] // CHUNKS
+        for c in range(CHUNKS):
             span = slice(c * size, (c + 1) * size)
             copies.append(pltpu.make_async_copy(source.at[span, :], target.at[span, :], sem.at[i, c]))
     for copy in copies:
@@ -260,7 +259,7 @@
 
 def middle_kernel(groups, *refs):
     own, arrived, crossed, scale, relayed, other_relayed = refs[:6]
-    message, tiles, near_gate, near_up, grads, other_grads, stage = refs[-7:]
+    message, tiles, near_tiles, grads, other_grads, stage = refs[-6:]
     _, tokens, width = own.shape
     narrow, group = lax.axis_index("narrow"), lax.axis_index("groups")
     sums = [own[i] + arrived[i].astype(jnp.float32) + crossed[i].astype(jnp.float32) for i in range(3)]
@@ -268,11 +267,10 @@
     product, d_gate, d_up = local_grads(*sums, scale[:, pl.ds(start, width)])
     message[0:tokens, :] = d_gate
     message[tokens : 2 * tokens, :] = d_up
-    near_gate[0:tokens, :] = d_gate
-    near_up[...] = d_up
     count = tokens // 8 * (width // 128)
-    to_tiles(d_gate, tiles, 0)
-    to_tiles(d_up, tiles, count)
+    for target in (tiles, near_tiles):
+        to_tiles(d_gate, target, 0)
+        to_tiles(d_up, target, count)
     half = tokens // groups
     for side, (source, target) in enumerate(((relayed, grads), (other_relayed, other_grads))):
         marks = source[source.shape[0] - 1].astype(jnp.float32)
@@ -293,8 +291,9 @@
     tail = jnp.concatenate(split_high(squares), axis=0).astype(jnp.bfloat16)
     message[2 * tokens :, :] = tail
     for i, rows in enumerate(split_high(squares)):
-        tiles[2 * count + i] = rows[:, 0:128].astype(jnp.bfloat16)
-    near_gate[tokens:, :] = tail
+        for target in (tiles, near_tiles):
+            target[2 * count + i] = rows[:, 0:128].astype(jnp.bfloat16)
+    tiles[2 * count + 2] = jnp.zeros((8, 128), jnp.bfloat16)
 
 
 TILE = 512
@@ -319,8 +318,8 @@
 
 def squares_of(message):
     if len(message.shape) == 3:
-        tiles = message.shape[0]
-        return message[tiles - 2].astype(jnp.float32) + message[tiles - 1].astype(jnp.float32)
+        first = (message.shape[0] - 2) // 2 * 2
+        return message[first].astype(jnp.float32) + message[first + 1].astype(jnp.float32)
     rows = message[message.shape[0] - 16 :, 0:128].astype(jnp.float32)
     return rows[0:8] + rows[8:16]
 
@@ -328,13 +327,6 @@
 def backward_first_kernel(message, gate, up, total):
     for start in range(0, total.shape[0], TILE):
         total[start : start + TILE, :] = backward_part(halves(message), gate, up, start)
-
-
-def backward_near_kernel(d_gate, d_up, gate, up, before, total):
-    tokens = d_up.shape[0]
-    for start in range(0, total.shape[0], TILE):
-        part = backward_part((d_gate[0:tokens, :], d_up[...]), gate, up, start)
-        total[start : start + TILE, :] = before[start : start + TILE, :] + part
 
 
 def backward_next_kernel(tiles, gate, up, before, total):
@@ -535,14 +527,13 @@
     )
 
     resident = [array for s in range(strips) for array in hold(s, [GATE, UP])]
-    message, tiles, near_gate, near_up, grads, other_grads = call(
+    message, tiles, near_tiles, grads, other_grads = call(
         functools.partial(middle_kernel, groups),
         "middle",
         [
             pltpu.VMEM((2 * tokens + 16, width), bf16),
+            pltpu.VMEM((2 * (tokens // 8) * (width // 128) + 3, 8, 128), bf16),
             pltpu.VMEM((2 * (tokens // 8) * (width // 128) + 2, 8, 128), bf16),
-            pltpu.VMEM((tokens + 16, width), bf16),
-            pltpu.VMEM((tokens, width), bf16),
             pltpu.VMEM((SEQS, width), f32),
             pltpu.VMEM((SEQS, width), f32),
         ],
@@ -551,10 +542,10 @@
     )
 
     total = pltpu.VMEM((features, tokens), f32)
-    near_gate, near_up = exchange(near_gate, "narrow", 1), exchange(near_up, "narrow", 1)
+    message_1 = exchange(near_tiles, "narrow", 1)
     message_2 = exchange(tiles, "narrow", 2)
     sums = call(backward_first_kernel, "backward_0", total, [message] + hold(0, [GATE, UP]))
-    sums = call(backward_near_kernel, "backward_1", total, [near_gate, near_up] + hold(1, [GATE, UP]) + [sums])
+    sums = call(backward_next_kernel, "backward_1", total, [message_1] + hold(1, [GATE, UP]) + [sums])
     message_2, sums = lax.optimization_barrier((message_2, sums))
     message_3 = exchange(message_2, "narrow", 1)
     sums = call(backward_next_kernel, "backward_2", total, [message_2] + hold(2, [GATE, UP]) + [sums])
@@ -569,7 +560,7 @@
             pltpu.VMEM((slabs + 1, 8, side), bf16),
             block,
         ],
-        [message_3] + hold(3, [GATE, UP]) + [sums, message, near_gate, message_2, other_grads],
+        [message_3] + hold(3, [GATE, UP]) + [sums, message, message_1, message_2, other_grads],
         scratch=[pltpu.VMEM((tokens, features), f32), pltpu.VMEM((4 * share, side), f32)],
     )
     across = exchange(sends[1], "groups", 1)

time: 53.2 us -> 53 us (level)
  waiting for transfers between devices: 8.04 us -> 8.59 us
    ppermute x15 -> x14, waiting for transfers between devices: 8.04 us -> 8.59 us  [exchange(): return lax.ppermute(array, axes, [(i, i ^ step) for i in range(size)])]
    ppermute x15 -> x14, starting transfers between devices: 16.5 us -> 16 us  [exchange(): return lax.ppermute(array, axes, [(i, i ^ step) for i in range(size)])]
  transfers between devices with their start and end apart: 15 -> 14, of which waited for: 6 -> 7; matrix products, arithmetic and copies ran while one was open for 0% -> 0% of each run, Pallas kernels for 39% -> 39%
where the time goes in v18:
time: 53 us; the launch traced here: 52.8 us
  Pallas kernels  27.2 us (51%)
  starting transfers between devices  16 us (30%)
  waiting for transfers between devices  8.59 us (16%)
  between operations  0.93 us (2%)
    pallas_call x16, Pallas kernels, call(): pl.pallas_call(body, out_shape=outs, in_specs=[pl.BlockSpec(memory_space=...  27.2 us
    ppermute x14, starting transfers between devices, exchange(): return lax.ppermute(array, axes, [(i, i ^ step) for i in range(size)])  16 us
    ppermute x14, waiting for transfers between devices, exchange(): return lax.ppermute(array, axes, [(i, i ^ step) for i in range(size)])  8.59 us
  transfers between devices with their start and end apart: 14, of which 7 were waited for; matrix products, arithmetic and copies ran while one was open for 0% of the time, Pallas kernels for 39%

profile of v18, /device:TPU:0, one launch (start us, length us, event | category | flops | bytes accessed | tf_op | source)
XLA Modules:
  0.0 52.8 jit_solution(1750410263291136634)
XLA Ops:
  0.6 0.8 %pack.1.own = bf16[3,8,1024]{2,1,0:T(8,128)(2,1)S(1)} custom-call(bf16[6,2048]{1,0:T(8,128)(2,1)} %inputs.1, bf16[6,2048]{1,0:T(8,128)(2,1)} %cotangent.1), custom_call_target="tpu_custom_call" | custom-call | flops 1000 | bytes 1000 | tf_op jit(solution)/shard_map/pack/pallas_call | solution.py:83
  1.4 4.1 %collective-permute-start = (bf16[3,8,1024]{2,1,0:T(8,128)(2,1)S(1)}, bf16[3,8,1024]{2,1,0:T(8,128)(2,1)S(1)}, u32[]{:S(2)}, u32[]{:S(2)}) collective-permute-start(bf16[3,8,1024]{2,1,0:T(8,128)(2,1)S(1)} %pack.1.own), channel_id=1, source_target_pairs={{0,8},{4,12},{8,0},{12,4},{1,9},{5,13},{9,1},{13,5},{2,10},{6,14},... | collective-permute-start | bytes 147464 | tf_op jit(solution)/shard_map/ppermute | solution.py:70
  5.5 3.9 %load_a.1 = (bf16[2048,768]{1,0:T(8,128)(2,1)S(1)}, bf16[2048,768]{1,0:T(8,128)(2,1)S(1)}, bf16[768,2048]{1,0:T(8,128)(2,1)S(1)}, bf16[8,1024]{1,0:T(8,128)(2,1)S(1)}) custom-call(bf16[2048,6144]{1,0:T(8,128)(2,1)} %refs_0_.11, bf16[2048,6144]{1,0:T(8,128)(2,1)} %refs_1_.11, bf16[6144,2048]{1,0:T(8,128)(2,1)} %refs_2_.11, s32[1,24]{1,0:T(1,128)} %bitcast.3), custom_call_target="tpu_custom_call" | custom-call | flops 1000 | bytes 1000 | tf_op jit(solution)/shard_map/load_a/pallas_call | solution.py:83
  9.4 0.0 collective-permute-done.far
  9.4 1.6 %collective-permute-start.2 = (bf16[7,8,1024]{2,1,0:T(8,128)(2,1)S(1)}, bf16[7,8,1024]{2,1,0:T(8,128)(2,1)S(1)}, u32[]{:S(2)}, u32[]{:S(2)}) collective-permute-start(bf16[7,8,1024]{2,1,0:T(8,128)(2,1)S(1)} %get-tuple-element.43.refs_3_.refs_4_), channel_id=1, source_target_pairs={{0,16},{16,0},{1,17},{17,1},{2,18},{18,2},{3,19},{19,3},{4,20},{20... | collective-permute-start | bytes 344072 | tf_op jit(solution)/shard_map/ppermute | solution.py:70
  11.0 1.5 %collective-permute-start.3 = (bf16[6,8,1024]{2,1,0:T(8,128)(2,1)S(1)}, bf16[6,8,1024]{2,1,0:T(8,128)(2,1)S(1)}, u32[]{:S(2)}, u32[]{:S(2)}) collective-permute-start(bf16[6,8,1024]{2,1,0:T(8,128)(2,1)S(1)} %get-tuple-element.44.refs_3_), channel_id=1, source_target_pairs={{0,20},{4,16},{8,28},{12,24},{16,4},{20,0},{24,12},{28,8},{1,21},{... | collective-permute-start | bytes 294920 | tf_op jit(solution)/shard_map/ppermute | solution.py:70
  12.6 0.4 collective-permute-start.1
  13.0 3.8 %load_b.1 = (bf16[2048,768]{1,0:T(8,128)(2,1)S(1)}, bf16[2048,768]{1,0:T(8,128)(2,1)S(1)}, bf16[768,2048]{1,0:T(8,128)(2,1)S(1)}) custom-call(bf16[2048,6144]{1,0:T(8,128)(2,1)} %refs_0_.11, bf16[2048,6144]{1,0:T(8,128)(2,1)} %refs_1_.11, bf16[6144,2048]{1,0:T(8,128)(2,1)} %refs_2_.11, bf16[6,8,1024]{2,1,0:T(8,128)(2,1)S(1)} %get-tuple-element.44.refs_3_), custom_call_target="tpu_custom_call" | custom-call | flops 1000 | bytes 1000 | tf_op jit(solution)/shard_map/load_b/pallas_call | solution.py:83
  16.8 0.3 collective-permute-done.3.refs_6_
  17.2 0.1 collective-permute-done.1.refs_4_
  17.3 0.0 collective-permute-done.2.refs_5_
  17.3 2.9 %forward_3.1 = (bf16[2048,768]{1,0:T(8,128)(2,1)S(1)}, bf16[768,2048]{1,0:T(8,128)(2,1)S(1)}, bf16[48,2048]{1,0:T(8,128)(2,1)S(1)}, bf16[48,2048]{1,0:T(8,128)(2,1)S(1)}, f32[3,48,768]{2,1,0:T(8,128)S(1)}) custom-call(bf16[2048,6144]{1,0:T(8,128)(2,1)} %refs_0_.11, bf16[2048,6144]{1,0:T(8,128)(2,1)} %refs_1_.11, bf16[6144,2048]{1,0:T(8,128)(2,1)} %refs_2_.11, ...), custom_call_target="tpu_custom_call" | custom-call | flops 1000 | bytes 1000 | tf_op jit(solution)/shard_map/forward_3/pallas_call | solution.py:83
  20.1 0.1 collective-permute-start.4
  20.2 2.1 %forward_2.1 = (bf16[2048,768]{1,0:T(8,128)(2,1)S(1)}, f32[3,48,768]{2,1,0:T(8,128)S(1)}) custom-call(bf16[2048,6144]{1,0:T(8,128)(2,1)} %refs_0_.11, bf16[2048,6144]{1,0:T(8,128)(2,1)} %refs_1_.11, bf16[6144,2048]{1,0:T(8,128)(2,1)} %refs_2_.11, bf16[48,2048]{1,0:T(8,128)(2,1)S(1)} %get-tuple-element.49.refs_3_, ...), custom_call_target="tpu_custom_call" | custom-call | flops 1000 | bytes 1000 | tf_op jit(solution)/shard_map/forward_2/pallas_call | solution.py:83
  22.3 0.0 collective-permute-done.4.arrived
  22.4 1.6 %collective-permute-start.6 = (bf16[3,48,768]{2,1,0:T(8,128)(2,1)S(1)}, bf16[3,48,768]{2,1,0:T(8,128)(2,1)S(1)}, u32[]{:S(2)}, u32[]{:S(2)}) collective-permute-start(bf16[3,48,768]{2,1,0:T(8,128)(2,1)S(1)} %join.1.refs_8_), channel_id=1, source_target_pairs={{0,2},{1,3},{2,0},{3,1},{4,6},{5,7},{6,4},{7,5},{8,10},{9,11},{10,... | collective-permute-start | bytes 663560 | tf_op jit(solution)/shard_map/ppermute | solution.py:70
  23.9 2.9 %forward_1.1 = (bf16[2048,768]{1,0:T(8,128)(2,1)S(1)}, bf16[768,2048]{1,0:T(8,128)(2,1)S(1)}, bf16[3,48,768]{2,1,0:T(8,128)(2,1)S(1)}) custom-call(bf16[2048,6144]{1,0:T(8,128)(2,1)} %refs_0_.11, bf16[2048,6144]{1,0:T(8,128)(2,1)} %refs_1_.11, bf16[6144,2048]{1,0:T(8,128)(2,1)} %refs_2_.11, bf16[48,2048]{1,0:T(8,128)(2,1)S(1)} %get-tuple-element.49.refs_3_, ...), custom_call_target="tpu_custom_call" | custom-call | flops 1000 | bytes 1000 | tf_op jit(solution)/shard_map/forward_1/pallas_call | solution.py:83
  26.8 0.3 collective-permute-start.5
  27.1 0.0 copy-start
  27.1 2.5 %forward_0.1 = (f32[3,48,768]{2,1,0:T(8,128)S(1)}, bf16[2048,768]{1,0:T(8,128)(2,1)S(1)}) custom-call(bf16[2048,6144]{1,0:T(8,128)(2,1)} %refs_0_.11, bf16[2048,6144]{1,0:T(8,128)(2,1)} %refs_1_.11, bf16[6144,2048]{1,0:T(8,128)(2,1)} %refs_2_.11, bf16[48,2048]{1,0:T(8,128)(2,1)S(1)} %get-tuple-element.49.refs_3_, ...), custom_call_target="tpu_custom_call" | custom-call | flops 1000 | bytes 1000 | tf_op jit(solution)/shard_map/forward_0/pallas_call | solution.py:83
  29.6 0.6 %collective-permute-done.6.refs_2_ = bf16[3,48,768]{2,1,0:T(8,128)(2,1)S(1)} collective-permute-done((bf16[3,48,768]{2,1,0:T(8,128)(2,1)S(1)}, bf16[3,48,768]{2,1,0:T(8,128)(2,1)S(1)}, u32[]{:S(2)}, u32[]{:S(2)}) %collective-permute-start.6) | collective-permute-done | bytes 221216 | tf_op jit(solution)/shard_map/ppermute | solution.py:70
  30.2 0.0 collective-permute-done.5.refs_1_
  30.3 0.0 copy-done
  30.3 0.4 middle.1
  30.6 1.5 %collective-permute-start.7 = (bf16[75,8,128]{2,1,0:T(8,128)(2,1)S(1)}, bf16[75,8,128]{2,1,0:T(8,128)(2,1)S(1)}, u32[]{:S(2)}, u32[]{:S(2)}) collective-permute-start(bf16[75,8,128]{2,1,0:T(8,128)(2,1)S(1)} %get-tuple-element.63), channel_id=1, source_target_pairs={{0,2},{1,3},{2,0},{3,1},{4,6},{5,7},{6,4},{7,5},{8,10},{9,11},{10,... | collective-permute-start | bytes 460808 | tf_op jit(solution)/shard_map/ppermute | solution.py:70
  32.1 0.0 collective-permute-start.8
  32.1 1.7 %backward_0.1.before = f32[2048,48]{1,0:T(8,128)S(1)} custom-call(bf16[112,768]{1,0:T(8,128)(2,1)S(1)} %get-tuple-element.65.message.refs_0_, bf16[2048,768]{1,0:T(8,128)(2,1)S(1)} %get-tuple-element.62.refs_6_.gate, bf16[2048,768]{1,0:T(8,128)(2,1)S(1)} %get-tuple-element.58.refs_5_.refs_7_.up), custom_call_target="tpu_custom_call" | custom-call | flops 1000 | bytes 1000 | tf_op jit(solution)/shard_map/backward_0/pallas_call | solution.py:83
  33.9 0.0 collective-permute-done.8.tiles.refs_1_
  33.9 1.8 %backward_1.1.before = f32[2048,48]{1,0:T(8,128)S(1)} custom-call(bf16[74,8,128]{2,1,0:T(8,128)(2,1)S(1)} %collective-permute-done.8.tiles.refs_1_, bf16[2048,768]{1,0:T(8,128)(2,1)S(1)} %get-tuple-element.51.refs_5_.refs_8_.gate, bf16[2048,768]{1,0:T(8,128)(2,1)S(1)} %get-tuple-element.54.refs_6_.refs_9_.up, f32[2048,48]{1,0:T(8,128)S(1)} %backward_0.1.before), custom_call_target="tpu_custom_call" | custom-call | flops 1000 | bytes 1000 | tf_op jit(solution)/shard_map/backward_1/pallas_call | solution.py:83
  35.7 0.6 %collective-permute-done.7.tiles.refs_2_ = bf16[75,8,128]{2,1,0:T(8,128)(2,1)S(1)} collective-permute-done((bf16[75,8,128]{2,1,0:T(8,128)(2,1)S(1)}, bf16[75,8,128]{2,1,0:T(8,128)(2,1)S(1)}, u32[]{:S(2)}, u32[]{:S(2)}) %collective-permute-start.7) | collective-permute-done | bytes 153632 | tf_op jit(solution)/shard_map/ppermute | solution.py:70
  36.2 0.0 collective-permute-start.9
  36.3 1.8 %backward_2.1.before = f32[2048,48]{1,0:T(8,128)S(1)} custom-call(bf16[75,8,128]{2,1,0:T(8,128)(2,1)S(1)} %collective-permute-done.7.tiles.refs_2_, bf16[2048,768]{1,0:T(8,128)(2,1)S(1)} %get-tuple-element.48.refs_10_.refs_5_.gate, bf16[2048,768]{1,0:T(8,128)(2,1)S(1)} %get-tuple-element.52.refs_6_.refs_11_.up, f32[2048,48]{1,0:T(8,128)S(1)} %backward_1.1.before), custom_call_target="tpu_custom_call" | custom-call | flops 1000 | bytes 1000 | tf_op jit(solution)/shard_map/backward_2/pallas_call | solution.py:83
  38.1 0.0 collective-permute-done.9.tiles
  38.1 1.9 %backward_3.1 = (f32[24,1024]{1,0:T(8,128)S(1)}, f32[8,128]{1,0:T(8,128)S(1)}, bf16[3,8,1152]{2,1,0:T(8,128)(2,1)S(1)}, bf16[4,8,1024]{2,1,0:T(8,128)(2,1)S(1)}, bf16[3,8,1152]{2,1,0:T(8,128)(2,1)S(1)}) custom-call(bf16[75,8,128]{2,1,0:T(8,128)(2,1)S(1)} %collective-permute-done.9.tiles, bf16[2048,768]{1,0:T(8,128)(2,1)S(1)} %get-tuple-element.45.refs_7_.refs_12_.gate, ...), custom_call_target="tpu_custom_call" | custom-call | flops 1000 | bytes 1000 | tf_op jit(solution)/shard_map/backward_3/pallas_call | solution.py:83
  40.0 1.6 %collective-permute-start.11 = (bf16[4,8,1024]{2,1,0:T(8,128)(2,1)S(1)}, bf16[4,8,1024]{2,1,0:T(8,128)(2,1)S(1)}, u32[]{:S(2)}, u32[]{:S(2)}) collective-permute-start(bf16[4,8,1024]{2,1,0:T(8,128)(2,1)S(1)} %get-tuple-element.72), channel_id=1, source_target_pairs={{0,16},{16,0},{1,17},{17,1},{2,18},{18,2},{3,19},{19,3},{4,20},{20... | collective-permute-start | bytes 196616 | tf_op jit(solution)/shard_map/ppermute | solution.py:70
  41.6 1.3 %collective-permute-start.10 = (bf16[3,8,1152]{2,1,0:T(8,128)(2,1)S(1)}, bf16[3,8,1152]{2,1,0:T(8,128)(2,1)S(1)}, u32[]{:S(2)}, u32[]{:S(2)}) collective-permute-start(bf16[3,8,1152]{2,1,0:T(8,128)(2,1)S(1)} %get-tuple-element.71), channel_id=1, source_target_pairs={{0,20},{4,16},{8,28},{12,24},{16,4},{20,0},{24,12},{28,8},{1,21},{... | collective-permute-start | bytes 165896 | tf_op jit(solution)/shard_map/ppermute | solution.py:70
  42.9 0.7 %collective-permute-start.12 = (bf16[3,8,1152]{2,1,0:T(8,128)(2,1)S(1)}, bf16[3,8,1152]{2,1,0:T(8,128)(2,1)S(1)}, u32[]{:S(2)}, u32[]{:S(2)}) collective-permute-start(bf16[3,8,1152]{2,1,0:T(8,128)(2,1)S(1)} %get-tuple-element.73), channel_id=1, source_target_pairs={{0,4},{4,0},{8,12},{12,8},{1,5},{5,1},{9,13},{13,9},{2,6},{6,2},{1... | collective-permute-start | bytes 165896 | tf_op jit(solution)/shard_map/ppermute | solution.py:70
  43.5 3.3 %collective-permute-done.10.diagonal = bf16[3,8,1152]{2,1,0:T(8,128)(2,1)S(1)} collective-permute-done((bf16[3,8,1152]{2,1,0:T(8,128)(2,1)S(1)}, bf16[3,8,1152]{2,1,0:T(8,128)(2,1)S(1)}, u32[]{:S(2)}, u32[]{:S(2)}) %collective-permute-start.10) | collective-permute-done | bytes 55328 | tf_op jit(solution)/shard_map/ppermute | solution.py:70
  46.9 0.2 collective-permute-done.12.beside
  47.0 0.0 collective-permute-done.11.across
  47.1 1.4 %collective-permute-start.13 = (bf16[2,8,1024]{2,1,0:T(8,128)(2,1)S(1)}, bf16[2,8,1024]{2,1,0:T(8,128)(2,1)S(1)}, u32[]{:S(2)}, u32[]{:S(2)}) collective-permute-start(bf16[2,8,1024]{2,1,0:T(8,128)(2,1)S(1)} %get-tuple-element.75), channel_id=1, source_target_pairs={{0,8},{4,12},{8,0},{12,4},{1,9},{5,13},{9,1},{13,5},{2,10},{6,14},... | collective-permute-start | bytes 98312 | tf_op jit(solution)/shard_map/ppermute | solution.py:70
  48.5 3.5 %collective-permute-done.13.arrived = bf16[2,8,1024]{2,1,0:T(8,128)(2,1)S(1)} collective-permute-done((bf16[2,8,1024]{2,1,0:T(8,128)(2,1)S(1)}, bf16[2,8,1024]{2,1,0:T(8,128)(2,1)S(1)}, u32[]{:S(2)}, u32[]{:S(2)}) %collective-permute-start.13) | collective-permute-done | bytes 32800 | tf_op jit(solution)/shard_map/ppermute | solution.py:70
  52.0 0.7 %last.1 = (bf16[6,2048]{1,0:T(8,128)(2,1)}, f32[4,1536]{1,0:T(4,128)}, f32[4]{0:T(128)}) custom-call(f32[16,1024]{1,0:T(8,128)S(1)} %get-tuple-element.74.own, bf16[2,8,1024]{2,1,0:T(8,128)(2,1)S(1)} %collective-permute-done.13.arrived, f32[4,768]{1,0:T(4,128)S(1)} %get-tuple-element.76.grads, f32[4,768]{1,0:T(4,128)S(1)} %get-tuple-element.77.other_grads), custom_call_target="tpu_custom_call" | custom-call | flops 1000 | bytes 1000 | tf_op jit(solution)/shard_map/last/pallas_call | solution.py:83
  (3 shorter events, 0.1 us)
Async XLA Ops:
  1.4 8.0 %collective-permute-start = (bf16[3,8,1024]{2,1,0:T(8,128)(2,1)S(1)}, bf16[3,8,1024]{2,1,0:T(8,128)(2,1)S(1)}, u32[]{:S(2)}, u32[]{:S(2)}) collective-permute-start(bf16[3,8,1024]{2,1,0:T(8,128)(2,1)S(1)} %pack.1.own), channel_id=1, source_target_pairs={{0,8},{4,12},{8,0},{12,4},{1,9},{5,13},{9,1},{13,5},{2,10},{6,14},... | collective-permute-start | bytes 147464 | tf_op jit(solution)/shard_map/ppermute | solution.py:70
  9.4 7.8 %collective-permute-start.2 = (bf16[7,8,1024]{2,1,0:T(8,128)(2,1)S(1)}, bf16[7,8,1024]{2,1,0:T(8,128)(2,1)S(1)}, u32[]{:S(2)}, u32[]{:S(2)}) collective-permute-start(bf16[7,8,1024]{2,1,0:T(8,128)(2,1)S(1)} %get-tuple-element.43.refs_3_.refs_4_), channel_id=1, source_target_pairs={{0,16},{16,0},{1,17},{17,1},{2,18},{18,2},{3,19},{19,3},{4,20},{20... | collective-permute-start | bytes 344072 | tf_op jit(solution)/shard_map/ppermute | solution.py:70
  11.0 6.1 %collective-permute-start.3 = (bf16[6,8,1024]{2,1,0:T(8,128)(2,1)S(1)}, bf16[6,8,1024]{2,1,0:T(8,128)(2,1)S(1)}, u32[]{:S(2)}, u32[]{:S(2)}) collective-permute-start(bf16[6,8,1024]{2,1,0:T(8,128)(2,1)S(1)} %get-tuple-element.44.refs_3_), channel_id=1, source_target_pairs={{0,20},{4,16},{8,28},{12,24},{16,4},{20,0},{24,12},{28,8},{1,21},{... | collective-permute-start | bytes 294920 | tf_op jit(solution)/shard_map/ppermute | solution.py:70
  12.6 4.7 %collective-permute-start.1 = (bf16[6,8,1024]{2,1,0:T(8,128)(2,1)S(1)}, bf16[6,8,1024]{2,1,0:T(8,128)(2,1)S(1)}, u32[]{:S(2)}, u32[]{:S(2)}) collective-permute-start(bf16[6,8,1024]{2,1,0:T(8,128)(2,1)S(1)} %get-tuple-element.44.refs_3_), channel_id=1, source_target_pairs={{0,4},{4,0},{8,12},{12,8},{1,5},{5,1},{9,13},{13,9},{2,6},{6,2},{1... | collective-permute-start | bytes 294920 | tf_op jit(solution)/shard_map/ppermute | solution.py:70
  20.1 2.2 %collective-permute-start.4 = (f32[3,48,768]{2,1,0:T(8,128)S(1)}, f32[3,48,768]{2,1,0:T(8,128)S(1)}, u32[]{:S(2)}, u32[]{:S(2)}) collective-permute-start(f32[3,48,768]{2,1,0:T(8,128)S(1)} %get-tuple-element.57), channel_id=1, source_target_pairs={{0,1},{1,0},{2,3},{3,2},{4,5},{5,4},{6,7},{7,6},{8,9},{9,8},{10,11... | collective-permute-start | bytes 1327112 | tf_op jit(solution)/shard_map/ppermute | solution.py:70
  22.4 7.9 %collective-permute-start.6 = (bf16[3,48,768]{2,1,0:T(8,128)(2,1)S(1)}, bf16[3,48,768]{2,1,0:T(8,128)(2,1)S(1)}, u32[]{:S(2)}, u32[]{:S(2)}) collective-permute-start(bf16[3,48,768]{2,1,0:T(8,128)(2,1)S(1)} %join.1.refs_8_), channel_id=1, source_target_pairs={{0,2},{1,3},{2,0},{3,1},{4,6},{5,7},{6,4},{7,5},{8,10},{9,11},{10,... | collective-permute-start | bytes 663560 | tf_op jit(solution)/shard_map/ppermute | solution.py:70
  26.8 3.4 %collective-permute-start.5 = (bf16[3,48,768]{2,1,0:T(8,128)(2,1)S(1)}, bf16[3,48,768]{2,1,0:T(8,128)(2,1)S(1)}, u32[]{:S(2)}, u32[]{:S(2)}) collective-permute-start(bf16[3,48,768]{2,1,0:T(8,128)(2,1)S(1)} %get-tuple-element.61), channel_id=1, source_target_pairs={{0,1},{1,0},{2,3},{3,2},{4,5},{5,4},{6,7},{7,6},{8,9},{9,8},{10,11... | collective-permute-start | bytes 663560 | tf_op jit(solution)/shard_map/ppermute | solution.py:70
  27.1 3.2 %copy-start = (f32[6144]{0:T(1024)S(1)}, f32[6144]{0:T(1024)}, u32[]{:S(2)}) copy-start(f32[6144]{0:T(1024)} %param.12) | copy-start | bytes 73732
  30.6 5.6 %collective-permute-start.7 = (bf16[75,8,128]{2,1,0:T(8,128)(2,1)S(1)}, bf16[75,8,128]{2,1,0:T(8,128)(2,1)S(1)}, u32[]{:S(2)}, u32[]{:S(2)}) collective-permute-start(bf16[75,8,128]{2,1,0:T(8,128)(2,1)S(1)} %get-tuple-element.63), channel_id=1, source_target_pairs={{0,2},{1,3},{2,0},{3,1},{4,6},{5,7},{6,4},{7,5},{8,10},{9,11},{10,... | collective-permute-start | bytes 460808 | tf_op jit(solution)/shard_map/ppermute | solution.py:70
  32.1 1.8 %collective-permute-start.8 = (bf16[74,8,128]{2,1,0:T(8,128)(2,1)S(1)}, bf16[74,8,128]{2,1,0:T(8,128)(2,1)S(1)}, u32[]{:S(2)}, u32[]{:S(2)}) collective-permute-start(bf16[74,8,128]{2,1,0:T(8,128)(2,1)S(1)} %get-tuple-element.64), channel_id=1, source_target_pairs={{0,1},{1,0},{2,3},{3,2},{4,5},{5,4},{6,7},{7,6},{8,9},{9,8},{10,11... | collective-permute-start | bytes 454664 | tf_op jit(solution)/shard_map/ppermute | solution.py:70
  36.2 1.8 %collective-permute-start.9 = (bf16[75,8,128]{2,1,0:T(8,128)(2,1)S(1)}, bf16[75,8,128]{2,1,0:T(8,128)(2,1)S(1)}, u32[]{:S(2)}, u32[]{:S(2)}) collective-permute-start(bf16[75,8,128]{2,1,0:T(8,128)(2,1)S(1)} %collective-permute-done.7.tiles.refs_2_), channel_id=1, source_target_pairs={{0,1},{1,0},{2,3},{3,2},{4,5},{5,4},{6,7},{7,6},{8,9},{9,8},{10,11... | collective-permute-start | bytes 460808 | tf_op jit(solution)/shard_map/ppermute | solution.py:70
  40.0 7.1 %collective-permute-start.11 = (bf16[4,8,1024]{2,1,0:T(8,128)(2,1)S(1)}, bf16[4,8,1024]{2,1,0:T(8,128)(2,1)S(1)}, u32[]{:S(2)}, u32[]{:S(2)}) collective-permute-start(bf16[4,8,1024]{2,1,0:T(8,128)(2,1)S(1)} %get-tuple-element.72), channel_id=1, source_target_pairs={{0,16},{16,0},{1,17},{17,1},{2,18},{18,2},{3,19},{19,3},{4,20},{20... | collective-permute-start | bytes 196616 | tf_op jit(solution)/shard_map/ppermute | solution.py:70
  41.6 5.3 %collective-permute-start.10 = (bf16[3,8,1152]{2,1,0:T(8,128)(2,1)S(1)}, bf16[3,8,1152]{2,1,0:T(8,128)(2,1)S(1)}, u32[]{:S(2)}, u32[]{:S(2)}) collective-permute-start(bf16[3,8,1152]{2,1,0:T(8,128)(2,1)S(1)} %get-tuple-element.71), channel_id=1, source_target_pairs={{0,20},{4,16},{8,28},{12,24},{16,4},{20,0},{24,12},{28,8},{1,21},{... | collective-permute-start | bytes 165896 | tf_op jit(solution)/shard_map/ppermute | solution.py:70
  42.9 4.2 %collective-permute-start.12 = (bf16[3,8,1152]{2,1,0:T(8,128)(2,1)S(1)}, bf16[3,8,1152]{2,1,0:T(8,128)(2,1)S(1)}, u32[]{:S(2)}, u32[]{:S(2)}) collective-permute-start(bf16[3,8,1152]{2,1,0:T(8,128)(2,1)S(1)} %get-tuple-element.73), channel_id=1, source_target_pairs={{0,4},{4,0},{8,12},{12,8},{1,5},{5,1},{9,13},{13,9},{2,6},{6,2},{1... | collective-permute-start | bytes 165896 | tf_op jit(solution)/shard_map/ppermute | solution.py:70
  47.1 4.9 %collective-permute-start.13 = (bf16[2,8,1024]{2,1,0:T(8,128)(2,1)S(1)}, bf16[2,8,1024]{2,1,0:T(8,128)(2,1)S(1)}, u32[]{:S(2)}, u32[]{:S(2)}) collective-permute-start(bf16[2,8,1024]{2,1,0:T(8,128)(2,1)S(1)} %get-tuple-element.75), channel_id=1, source_target_pairs={{0,8},{4,12},{8,0},{12,4},{1,9},{5,13},{9,1},{13,5},{2,10},{6,14},... | collective-permute-start | bytes 98312 | tf_op jit(solution)/shard_map/ppermute | solution.py:70

commit v19 on v18

--- a/solution.py
+++ b/solution.py
@@ -124,11 +124,15 @@
 
 
 def relay_kernel(own, far, marks, pair, marked):
-    slabs = own.shape[0]
-    for target in (pair, marked):
-        target[0:slabs] = own[...]
-        target[slabs : 2 * slabs] = far[...]
-    marked[2 * slabs] = marks[...]
+    slabs, across = own.shape[0], own.shape[2] // 128
+    pair[0:slabs] = own[...]
+    pair[slabs : 2 * slabs] = far[...]
+    for k in range(2 * slabs):
+        rows = (own if k < slabs else far)[k % slabs]
+        for j in range(across):
+            marked[k * across + j] = rows[:, j * 128 : (j + 1) * 128]
+    for k in range(marked.shape[0] - 2 * slabs * across):
+        marked[2 * slabs * across + k] = marks[:, k * 128 : (k + 1) * 128]
 
 
 WIDE, NEXT, FAR = 4, 1, 2
@@ -205,17 +209,20 @@
     out[...] = (own[...] + arrived[...]).astype(out.dtype)
 
 
-def first_kernel(share, marked, beside, other, diagonal, gate, up, down, *refs):
+def first_kernel(share, pair, beside, other, diagonal, gate, up, down, *refs):
     tokens, cotans, part, rows, cots = refs[-5:]
     slabs, half = 4 * share // 8, rows.shape[1] // 2
     for source, places in (
-        (marked, (0, FAR)),
+        (pair, (0, FAR)),
         (beside, (NEXT, FAR ^ NEXT)),
         (other, (WIDE, WIDE + FAR)),
         (diagonal, (WIDE + NEXT, WIDE + (FAR ^ NEXT))),
     ):
         for i, place in enumerate(places):
-            packed = source[i * slabs : (i + 1) * slabs].astype(jnp.float32).reshape(4 * share, half)
+            if source is other:
+                packed = from_tiles(source, i * slabs * (half // 128), 4 * share, half)
+            else:
+                packed = source[i * slabs : (i + 1) * slabs].astype(jnp.float32).reshape(4 * share, half)
             for j, target in enumerate((rows, rows, cots, cots)):
                 span = slice((j % 2) * half, (j % 2 + 1) * half)
                 target[place * share : (place + 1) * share, span] = packed[j * share : (j + 1) * share]
@@ -254,7 +261,7 @@
         jnp.concatenate([tiles[first + i * across + j].astype(jnp.float32) for j in range(across)], axis=1)
         for i in range(rows // 8)
     ]
-    return jnp.concatenate(parts, axis=0).astype(tiles.dtype)
+    return jnp.concatenate(parts, axis=0)
 
 
 def middle_kernel(groups, *refs):
@@ -272,8 +279,10 @@
         to_tiles(d_gate, target, 0)
         to_tiles(d_up, target, count)
     half = tokens // groups
-    for side, (source, target) in enumerate(((relayed, grads), (other_relayed, other_grads))):
-        marks = source[source.shape[0] - 1].astype(jnp.float32)
+    first = other_relayed.shape[0] - half // 8
+    own_marks = relayed[...].astype(jnp.float32)
+    other_marks = jnp.concatenate([other_relayed[first + k].astype(jnp.float32) for k in range(half // 8)], axis=1)
+    for side, (marks, target) in enumerate(((own_marks, grads), (other_marks, other_grads))):
         seq = jnp.concatenate(
             [
                 jnp.concatenate([marks[:, k * 128 : (k + 1) * 128]] * (width // 128), axis=1)
@@ -313,7 +322,7 @@
 def halves_of_tiles(tiles, width):
     count = (tiles.shape[0] - 2) // 2
     rows = count // (width // 128) * 8
-    return from_tiles(tiles, 0, rows, width), from_tiles(tiles, count, rows, width)
+    return tuple(from_tiles(tiles, first, rows, width).astype(tiles.dtype) for first in (0, count))
 
 
 def squares_of(message):
@@ -490,7 +499,7 @@
     pair, marked = call(
         relay_kernel,
         "relay",
-        [pltpu.VMEM((2 * slabs, 8, side), bf16), pltpu.VMEM((2 * slabs + 1, 8, side), bf16)],
+        [pltpu.VMEM((2 * slabs, 8, side), bf16), pltpu.VMEM((2 * slabs * (side // 128) + half // 8, 8, 128), bf16)],
         [packed, far, marks],
     )
     diagonal = exchange(pair, ("groups", "wide"), WIDE + NEXT)
@@ -505,7 +514,7 @@
         "forward_3",
         [(GATE, 1), (DOWN, 1)],
         [pltpu.VMEM((tokens, features), bf16)] * 2 + [part],
-        [marked, beside, other_marked, diagonal] + hold(3) + hold(2, [GATE]),
+        [pair, beside, other_marked, diagonal] + hold(3) + hold(2, [GATE]),
         [pltpu.VMEM((tokens, features), f32)] * 2,
     )
     panel = [tokens_all, cotans_all]
@@ -537,7 +546,7 @@
             pltpu.VMEM((SEQS, width), f32),
             pltpu.VMEM((SEQS, width), f32),
         ],
-        [own_part, near, crossed, ia3_scale[None, :], marked, other_marked] + resident,
+        [own_part, near, crossed, ia3_scale[None, :], marks, other_marked] + resident,
         scratch=[pltpu.VMEM((groups * SEQS, width), f32)],
     )
 

time: 53 us -> 53 us (level)
  no operation moved by 1% of the time
where the time goes in v19:
time: 53 us; the launch traced here: 52.8 us
  Pallas kernels  27.3 us (52%)
  starting transfers between devices  16.1 us (30%)
  waiting for transfers between devices  8.43 us (16%)
  between operations  0.93 us (2%)
    pallas_call x16, Pallas kernels, call(): pl.pallas_call(body, out_shape=outs, in_specs=[pl.BlockSpec(memory_space=...  27.3 us
    ppermute x14, starting transfers between devices, exchange(): return lax.ppermute(array, axes, [(i, i ^ step) for i in range(size)])  16.1 us
    ppermute x14, waiting for transfers between devices, exchange(): return lax.ppermute(array, axes, [(i, i ^ step) for i in range(size)])  8.43 us
  transfers between devices with their start and end apart: 14, of which 7 were waited for; matrix products, arithmetic and copies ran while one was open for 0% of the time, Pallas kernels for 39%

profile of v19, /device:TPU:0, one launch (start us, length us, event | category | flops | bytes accessed | tf_op | source)
XLA Modules:
  0.0 52.8 jit_solution(12916875539710577048)
XLA Ops:
  0.6 0.8 %pack.1.own = bf16[3,8,1024]{2,1,0:T(8,128)(2,1)S(1)} custom-call(bf16[6,2048]{1,0:T(8,128)(2,1)} %inputs.1, bf16[6,2048]{1,0:T(8,128)(2,1)} %cotangent.1), custom_call_target="tpu_custom_call" | custom-call | flops 1000 | bytes 1000 | tf_op jit(solution)/shard_map/pack/pallas_call | solution.py:83
  1.4 4.1 %collective-permute-start = (bf16[3,8,1024]{2,1,0:T(8,128)(2,1)S(1)}, bf16[3,8,1024]{2,1,0:T(8,128)(2,1)S(1)}, u32[]{:S(2)}, u32[]{:S(2)}) collective-permute-start(bf16[3,8,1024]{2,1,0:T(8,128)(2,1)S(1)} %pack.1.own), channel_id=1, source_target_pairs={{0,8},{4,12},{8,0},{12,4},{1,9},{5,13},{9,1},{13,5},{2,10},{6,14},... | collective-permute-start | bytes 147464 | tf_op jit(solution)/shard_map/ppermute | solution.py:70
  5.5 3.9 %load_a.1 = (bf16[2048,768]{1,0:T(8,128)(2,1)S(1)}, bf16[2048,768]{1,0:T(8,128)(2,1)S(1)}, bf16[768,2048]{1,0:T(8,128)(2,1)S(1)}, bf16[8,1024]{1,0:T(8,128)(2,1)S(1)}) custom-call(bf16[2048,6144]{1,0:T(8,128)(2,1)} %refs_0_.11, bf16[2048,6144]{1,0:T(8,128)(2,1)} %refs_1_.11, bf16[6144,2048]{1,0:T(8,128)(2,1)} %refs_2_.11, s32[1,24]{1,0:T(1,128)} %bitcast.3), custom_call_target="tpu_custom_call" | custom-call | flops 1000 | bytes 1000 | tf_op jit(solution)/shard_map/load_a/pallas_call | solution.py:83
  9.4 0.0 collective-permute-done.far
  9.5 1.6 %collective-permute-start.2 = (bf16[51,8,128]{2,1,0:T(8,128)(2,1)S(1)}, bf16[51,8,128]{2,1,0:T(8,128)(2,1)S(1)}, u32[]{:S(2)}, u32[]{:S(2)}) collective-permute-start(bf16[51,8,128]{2,1,0:T(8,128)(2,1)S(1)} %get-tuple-element.44), channel_id=1, source_target_pairs={{0,16},{16,0},{1,17},{17,1},{2,18},{18,2},{3,19},{19,3},{4,20},{20... | collective-permute-start | bytes 313352 | tf_op jit(solution)/shard_map/ppermute | solution.py:70
  11.0 1.5 %collective-permute-start.3 = (bf16[6,8,1024]{2,1,0:T(8,128)(2,1)S(1)}, bf16[6,8,1024]{2,1,0:T(8,128)(2,1)S(1)}, u32[]{:S(2)}, u32[]{:S(2)}) collective-permute-start(bf16[6,8,1024]{2,1,0:T(8,128)(2,1)S(1)} %get-tuple-element.43.refs_3_), channel_id=1, source_target_pairs={{0,20},{4,16},{8,28},{12,24},{16,4},{20,0},{24,12},{28,8},{1,21},{... | collective-permute-start | bytes 294920 | tf_op jit(solution)/shard_map/ppermute | solution.py:70
  12.6 0.4 collective-permute-start.1
  13.0 3.8 %load_b.1 = (bf16[2048,768]{1,0:T(8,128)(2,1)S(1)}, bf16[2048,768]{1,0:T(8,128)(2,1)S(1)}, bf16[768,2048]{1,0:T(8,128)(2,1)S(1)}) custom-call(bf16[2048,6144]{1,0:T(8,128)(2,1)} %refs_0_.11, bf16[2048,6144]{1,0:T(8,128)(2,1)} %refs_1_.11, bf16[6144,2048]{1,0:T(8,128)(2,1)} %refs_2_.11, bf16[6,8,1024]{2,1,0:T(8,128)(2,1)S(1)} %get-tuple-element.43.refs_3_), custom_call_target="tpu_custom_call" | custom-call | flops 1000 | bytes 1000 | tf_op jit(solution)/shard_map/load_b/pallas_call | solution.py:83
  16.8 0.3 collective-permute-done.3.refs_6_
  17.2 0.1 collective-permute-done.1.refs_4_
  17.3 0.0 collective-permute-done.2.refs_5_
  17.3 2.9 %forward_3.1 = (bf16[2048,768]{1,0:T(8,128)(2,1)S(1)}, bf16[768,2048]{1,0:T(8,128)(2,1)S(1)}, bf16[48,2048]{1,0:T(8,128)(2,1)S(1)}, bf16[48,2048]{1,0:T(8,128)(2,1)S(1)}, f32[3,48,768]{2,1,0:T(8,128)S(1)}) custom-call(bf16[2048,6144]{1,0:T(8,128)(2,1)} %refs_0_.11, bf16[2048,6144]{1,0:T(8,128)(2,1)} %refs_1_.11, bf16[6144,2048]{1,0:T(8,128)(2,1)} %refs_2_.11, ...), custom_call_target="tpu_custom_call" | custom-call | flops 1000 | bytes 1000 | tf_op jit(solution)/shard_map/forward_3/pallas_call | solution.py:83
  20.2 0.1 collective-permute-start.4
  20.2 2.1 %forward_2.1 = (bf16[2048,768]{1,0:T(8,128)(2,1)S(1)}, f32[3,48,768]{2,1,0:T(8,128)S(1)}) custom-call(bf16[2048,6144]{1,0:T(8,128)(2,1)} %refs_0_.11, bf16[2048,6144]{1,0:T(8,128)(2,1)} %refs_1_.11, bf16[6144,2048]{1,0:T(8,128)(2,1)} %refs_2_.11, bf16[48,2048]{1,0:T(8,128)(2,1)S(1)} %get-tuple-element.49.refs_3_, ...), custom_call_target="tpu_custom_call" | custom-call | flops 1000 | bytes 1000 | tf_op jit(solution)/shard_map/forward_2/pallas_call | solution.py:83
  22.3 0.0 collective-permute-done.4.arrived
  22.3 0.1 join.1.refs_8_
  22.4 1.6 %collective-permute-start.6 = (bf16[3,48,768]{2,1,0:T(8,128)(2,1)S(1)}, bf16[3,48,768]{2,1,0:T(8,128)(2,1)S(1)}, u32[]{:S(2)}, u32[]{:S(2)}) collective-permute-start(bf16[3,48,768]{2,1,0:T(8,128)(2,1)S(1)} %join.1.refs_8_), channel_id=1, source_target_pairs={{0,2},{1,3},{2,0},{3,1},{4,6},{5,7},{6,4},{7,5},{8,10},{9,11},{10,... | collective-permute-start | bytes 663560 | tf_op jit(solution)/shard_map/ppermute | solution.py:70
  24.0 2.9 %forward_1.1 = (bf16[2048,768]{1,0:T(8,128)(2,1)S(1)}, bf16[768,2048]{1,0:T(8,128)(2,1)S(1)}, bf16[3,48,768]{2,1,0:T(8,128)(2,1)S(1)}) custom-call(bf16[2048,6144]{1,0:T(8,128)(2,1)} %refs_0_.11, bf16[2048,6144]{1,0:T(8,128)(2,1)} %refs_1_.11, bf16[6144,2048]{1,0:T(8,128)(2,1)} %refs_2_.11, bf16[48,2048]{1,0:T(8,128)(2,1)S(1)} %get-tuple-element.49.refs_3_, ...), custom_call_target="tpu_custom_call" | custom-call | flops 1000 | bytes 1000 | tf_op jit(solution)/shard_map/forward_1/pallas_call | solution.py:83
  26.8 0.3 collective-permute-start.5
  27.1 0.0 copy-start
  27.1 2.6 %forward_0.1 = (f32[3,48,768]{2,1,0:T(8,128)S(1)}, bf16[2048,768]{1,0:T(8,128)(2,1)S(1)}) custom-call(bf16[2048,6144]{1,0:T(8,128)(2,1)} %refs_0_.11, bf16[2048,6144]{1,0:T(8,128)(2,1)} %refs_1_.11, bf16[6144,2048]{1,0:T(8,128)(2,1)} %refs_2_.11, bf16[48,2048]{1,0:T(8,128)(2,1)S(1)} %get-tuple-element.49.refs_3_, ...), custom_call_target="tpu_custom_call" | custom-call | flops 1000 | bytes 1000 | tf_op jit(solution)/shard_map/forward_0/pallas_call | solution.py:83
  29.7 0.6 %collective-permute-done.6.refs_2_ = bf16[3,48,768]{2,1,0:T(8,128)(2,1)S(1)} collective-permute-done((bf16[3,48,768]{2,1,0:T(8,128)(2,1)S(1)}, bf16[3,48,768]{2,1,0:T(8,128)(2,1)S(1)}, u32[]{:S(2)}, u32[]{:S(2)}) %collective-permute-start.6) | collective-permute-done | bytes 221216 | tf_op jit(solution)/shard_map/ppermute | solution.py:70
  30.3 0.0 collective-permute-done.5.refs_1_
  30.3 0.0 copy-done
  30.3 0.4 middle.1
  30.7 1.5 %collective-permute-start.7 = (bf16[75,8,128]{2,1,0:T(8,128)(2,1)S(1)}, bf16[75,8,128]{2,1,0:T(8,128)(2,1)S(1)}, u32[]{:S(2)}, u32[]{:S(2)}) collective-permute-start(bf16[75,8,128]{2,1,0:T(8,128)(2,1)S(1)} %get-tuple-element.63), channel_id=1, source_target_pairs={{0,2},{1,3},{2,0},{3,1},{4,6},{5,7},{6,4},{7,5},{8,10},{9,11},{10,... | collective-permute-start | bytes 460808 | tf_op jit(solution)/shard_map/ppermute | solution.py:70
  32.2 0.0 collective-permute-start.8
  32.2 1.8 %backward_0.1.before = f32[2048,48]{1,0:T(8,128)S(1)} custom-call(bf16[112,768]{1,0:T(8,128)(2,1)S(1)} %get-tuple-element.65.message.refs_0_, bf16[2048,768]{1,0:T(8,128)(2,1)S(1)} %get-tuple-element.62.refs_6_.gate, bf16[2048,768]{1,0:T(8,128)(2,1)S(1)} %get-tuple-element.58.refs_5_.refs_7_.up), custom_call_target="tpu_custom_call" | custom-call | flops 1000 | bytes 1000 | tf_op jit(solution)/shard_map/backward_0/pallas_call | solution.py:83
  33.9 0.0 collective-permute-done.8.tiles.refs_1_
  33.9 1.8 %backward_1.1.before = f32[2048,48]{1,0:T(8,128)S(1)} custom-call(bf16[74,8,128]{2,1,0:T(8,128)(2,1)S(1)} %collective-permute-done.8.tiles.refs_1_, bf16[2048,768]{1,0:T(8,128)(2,1)S(1)} %get-tuple-element.51.refs_5_.refs_8_.gate, bf16[2048,768]{1,0:T(8,128)(2,1)S(1)} %get-tuple-element.54.refs_6_.refs_9_.up, f32[2048,48]{1,0:T(8,128)S(1)} %backward_0.1.before), custom_call_target="tpu_custom_call" | custom-call | flops 1000 | bytes 1000 | tf_op jit(solution)/shard_map/backward_1/pallas_call | solution.py:83
  35.8 0.5 collective-permute-done.7.tiles.refs_2_
  36.3 0.1 collective-permute-start.9
  36.3 1.8 %backward_2.1.before = f32[2048,48]{1,0:T(8,128)S(1)} custom-call(bf16[75,8,128]{2,1,0:T(8,128)(2,1)S(1)} %collective-permute-done.7.tiles.refs_2_, bf16[2048,768]{1,0:T(8,128)(2,1)S(1)} %get-tuple-element.48.refs_10_.refs_5_.gate, bf16[2048,768]{1,0:T(8,128)(2,1)S(1)} %get-tuple-element.52.refs_6_.refs_11_.up, f32[2048,48]{1,0:T(8,128)S(1)} %backward_1.1.before), custom_call_target="tpu_custom_call" | custom-call | flops 1000 | bytes 1000 | tf_op jit(solution)/shard_map/backward_2/pallas_call | solution.py:83
  38.1 0.0 collective-permute-done.9.tiles
  38.1 1.9 %backward_3.1 = (f32[24,1024]{1,0:T(8,128)S(1)}, f32[8,128]{1,0:T(8,128)S(1)}, bf16[3,8,1152]{2,1,0:T(8,128)(2,1)S(1)}, bf16[4,8,1024]{2,1,0:T(8,128)(2,1)S(1)}, bf16[3,8,1152]{2,1,0:T(8,128)(2,1)S(1)}) custom-call(bf16[75,8,128]{2,1,0:T(8,128)(2,1)S(1)} %collective-permute-done.9.tiles, bf16[2048,768]{1,0:T(8,128)(2,1)S(1)} %get-tuple-element.45.refs_7_.refs_12_.gate, ...), custom_call_target="tpu_custom_call" | custom-call | flops 1000 | bytes 1000 | tf_op jit(solution)/shard_map/backward_3/pallas_call | solution.py:83
  40.0 1.6 %collective-permute-start.11 = (bf16[4,8,1024]{2,1,0:T(8,128)(2,1)S(1)}, bf16[4,8,1024]{2,1,0:T(8,128)(2,1)S(1)}, u32[]{:S(2)}, u32[]{:S(2)}) collective-permute-start(bf16[4,8,1024]{2,1,0:T(8,128)(2,1)S(1)} %get-tuple-element.72), channel_id=1, source_target_pairs={{0,16},{16,0},{1,17},{17,1},{2,18},{18,2},{3,19},{19,3},{4,20},{20... | collective-permute-start | bytes 196616 | tf_op jit(solution)/shard_map/ppermute | solution.py:70
  41.6 1.3 %collective-permute-start.10 = (bf16[3,8,1152]{2,1,0:T(8,128)(2,1)S(1)}, bf16[3,8,1152]{2,1,0:T(8,128)(2,1)S(1)}, u32[]{:S(2)}, u32[]{:S(2)}) collective-permute-start(bf16[3,8,1152]{2,1,0:T(8,128)(2,1)S(1)} %get-tuple-element.71), channel_id=1, source_target_pairs={{0,20},{4,16},{8,28},{12,24},{16,4},{20,0},{24,12},{28,8},{1,21},{... | collective-permute-start | bytes 165896 | tf_op jit(solution)/shard_map/ppermute | solution.py:70
  42.9 0.7 %collective-permute-start.12 = (bf16[3,8,1152]{2,1,0:T(8,128)(2,1)S(1)}, bf16[3,8,1152]{2,1,0:T(8,128)(2,1)S(1)}, u32[]{:S(2)}, u32[]{:S(2)}) collective-permute-start(bf16[3,8,1152]{2,1,0:T(8,128)(2,1)S(1)} %get-tuple-element.73), channel_id=1, source_target_pairs={{0,4},{4,0},{8,12},{12,8},{1,5},{5,1},{9,13},{13,9},{2,6},{6,2},{1... | collective-permute-start | bytes 165896 | tf_op jit(solution)/shard_map/ppermute | solution.py:70
  43.6 3.4 %collective-permute-done.10.diagonal = bf16[3,8,1152]{2,1,0:T(8,128)(2,1)S(1)} collective-permute-done((bf16[3,8,1152]{2,1,0:T(8,128)(2,1)S(1)}, bf16[3,8,1152]{2,1,0:T(8,128)(2,1)S(1)}, u32[]{:S(2)}, u32[]{:S(2)}) %collective-permute-start.10) | collective-permute-done | bytes 55328 | tf_op jit(solution)/shard_map/ppermute | solution.py:70
  47.0 0.1 collective-permute-done.12.beside
  47.1 0.0 collective-permute-done.11.across
  47.1 1.5 %collective-permute-start.13 = (bf16[2,8,1024]{2,1,0:T(8,128)(2,1)S(1)}, bf16[2,8,1024]{2,1,0:T(8,128)(2,1)S(1)}, u32[]{:S(2)}, u32[]{:S(2)}) collective-permute-start(bf16[2,8,1024]{2,1,0:T(8,128)(2,1)S(1)} %get-tuple-element.75), channel_id=1, source_target_pairs={{0,8},{4,12},{8,0},{12,4},{1,9},{5,13},{9,1},{13,5},{2,10},{6,14},... | collective-permute-start | bytes 98312 | tf_op jit(solution)/shard_map/ppermute | solution.py:70
  48.6 3.4 %collective-permute-done.13.arrived = bf16[2,8,1024]{2,1,0:T(8,128)(2,1)S(1)} collective-permute-done((bf16[2,8,1024]{2,1,0:T(8,128)(2,1)S(1)}, bf16[2,8,1024]{2,1,0:T(8,128)(2,1)S(1)}, u32[]{:S(2)}, u32[]{:S(2)}) %collective-permute-start.13) | collective-permute-done | bytes 32800 | tf_op jit(solution)/shard_map/ppermute | solution.py:70
  52.0 0.7 %last.1 = (bf16[6,2048]{1,0:T(8,128)(2,1)}, f32[4,1536]{1,0:T(4,128)}, f32[4]{0:T(128)}) custom-call(f32[16,1024]{1,0:T(8,128)S(1)} %get-tuple-element.74.own, bf16[2,8,1024]{2,1,0:T(8,128)(2,1)S(1)} %collective-permute-done.13.arrived, f32[4,768]{1,0:T(4,128)S(1)} %get-tuple-element.76.grads, f32[4,768]{1,0:T(4,128)S(1)} %get-tuple-element.77.other_grads), custom_call_target="tpu_custom_call" | custom-call | flops 1000 | bytes 1000 | tf_op jit(solution)/shard_map/last/pallas_call | solution.py:83
  (2 shorter events, 0.1 us)
Async XLA Ops:
  1.4 8.0 %collective-permute-start = (bf16[3,8,1024]{2,1,0:T(8,128)(2,1)S(1)}, bf16[3,8,1024]{2,1,0:T(8,128)(2,1)S(1)}, u32[]{:S(2)}, u32[]{:S(2)}) collective-permute-start(bf16[3,8,1024]{2,1,0:T(8,128)(2,1)S(1)} %pack.1.own), channel_id=1, source_target_pairs={{0,8},{4,12},{8,0},{12,4},{1,9},{5,13},{9,1},{13,5},{2,10},{6,14},... | collective-permute-start | bytes 147464 | tf_op jit(solution)/shard_map/ppermute | solution.py:70
  9.5 7.8 %collective-permute-start.2 = (bf16[51,8,128]{2,1,0:T(8,128)(2,1)S(1)}, bf16[51,8,128]{2,1,0:T(8,128)(2,1)S(1)}, u32[]{:S(2)}, u32[]{:S(2)}) collective-permute-start(bf16[51,8,128]{2,1,0:T(8,128)(2,1)S(1)} %get-tuple-element.44), channel_id=1, source_target_pairs={{0,16},{16,0},{1,17},{17,1},{2,18},{18,2},{3,19},{19,3},{4,20},{20... | collective-permute-start | bytes 313352 | tf_op jit(solution)/shard_map/ppermute | solution.py:70
  11.0 6.1 %collective-permute-start.3 = (bf16[6,8,1024]{2,1,0:T(8,128)(2,1)S(1)}, bf16[6,8,1024]{2,1,0:T(8,128)(2,1)S(1)}, u32[]{:S(2)}, u32[]{:S(2)}) collective-permute-start(bf16[6,8,1024]{2,1,0:T(8,128)(2,1)S(1)} %get-tuple-element.43.refs_3_), channel_id=1, source_target_pairs={{0,20},{4,16},{8,28},{12,24},{16,4},{20,0},{24,12},{28,8},{1,21},{... | collective-permute-start | bytes 294920 | tf_op jit(solution)/shard_map/ppermute | solution.py:70
  12.6 4.7 %collective-permute-start.1 = (bf16[6,8,1024]{2,1,0:T(8,128)(2,1)S(1)}, bf16[6,8,1024]{2,1,0:T(8,128)(2,1)S(1)}, u32[]{:S(2)}, u32[]{:S(2)}) collective-permute-start(bf16[6,8,1024]{2,1,0:T(8,128)(2,1)S(1)} %get-tuple-element.43.refs_3_), channel_id=1, source_target_pairs={{0,4},{4,0},{8,12},{12,8},{1,5},{5,1},{9,13},{13,9},{2,6},{6,2},{1... | collective-permute-start | bytes 294920 | tf_op jit(solution)/shard_map/ppermute | solution.py:70
  20.2 2.2 %collective-permute-start.4 = (f32[3,48,768]{2,1,0:T(8,128)S(1)}, f32[3,48,768]{2,1,0:T(8,128)S(1)}, u32[]{:S(2)}, u32[]{:S(2)}) collective-permute-start(f32[3,48,768]{2,1,0:T(8,128)S(1)} %get-tuple-element.57), channel_id=1, source_target_pairs={{0,1},{1,0},{2,3},{3,2},{4,5},{5,4},{6,7},{7,6},{8,9},{9,8},{10,11... | collective-permute-start | bytes 1327112 | tf_op jit(solution)/shard_map/ppermute | solution.py:70
  22.4 7.9 %collective-permute-start.6 = (bf16[3,48,768]{2,1,0:T(8,128)(2,1)S(1)}, bf16[3,48,768]{2,1,0:T(8,128)(2,1)S(1)}, u32[]{:S(2)}, u32[]{:S(2)}) collective-permute-start(bf16[3,48,768]{2,1,0:T(8,128)(2,1)S(1)} %join.1.refs_8_), channel_id=1, source_target_pairs={{0,2},{1,3},{2,0},{3,1},{4,6},{5,7},{6,4},{7,5},{8,10},{9,11},{10,... | collective-permute-start | bytes 663560 | tf_op jit(solution)/shard_map/ppermute | solution.py:70
  26.8 3.4 %collective-permute-start.5 = (bf16[3,48,768]{2,1,0:T(8,128)(2,1)S(1)}, bf16[3,48,768]{2,1,0:T(8,128)(2,1)S(1)}, u32[]{:S(2)}, u32[]{:S(2)}) collective-permute-start(bf16[3,48,768]{2,1,0:T(8,128)(2,1)S(1)} %get-tuple-element.61), channel_id=1, source_target_pairs={{0,1},{1,0},{2,3},{3,2},{4,5},{5,4},{6,7},{7,6},{8,9},{9,8},{10,11... | collective-permute-start | bytes 663560 | tf_op jit(solution)/shard_map/ppermute | solution.py:70
  27.1 3.2 %copy-start = (f32[6144]{0:T(1024)S(1)}, f32[6144]{0:T(1024)}, u32[]{:S(2)}) copy-start(f32[6144]{0:T(1024)} %param.12) | copy-start | bytes 73732
  30.7 5.6 %collective-permute-start.7 = (bf16[75,8,128]{2,1,0:T(8,128)(2,1)S(1)}, bf16[75,8,128]{2,1,0:T(8,128)(2,1)S(1)}, u32[]{:S(2)}, u32[]{:S(2)}) collective-permute-start(bf16[75,8,128]{2,1,0:T(8,128)(2,1)S(1)} %get-tuple-element.63), channel_id=1, source_target_pairs={{0,2},{1,3},{2,0},{3,1},{4,6},{5,7},{6,4},{7,5},{8,10},{9,11},{10,... | collective-permute-start | bytes 460808 | tf_op jit(solution)/shard_map/ppermute | solution.py:70
  32.2 1.8 %collective-permute-start.8 = (bf16[74,8,128]{2,1,0:T(8,128)(2,1)S(1)}, bf16[74,8,128]{2,1,0:T(8,128)(2,1)S(1)}, u32[]{:S(2)}, u32[]{:S(2)}) collective-permute-start(bf16[74,8,128]{2,1,0:T(8,128)(2,1)S(1)} %get-tuple-element.64), channel_id=1, source_target_pairs={{0,1},{1,0},{2,3},{3,2},{4,5},{5,4},{6,7},{7,6},{8,9},{9,8},{10,11... | collective-permute-start | bytes 454664 | tf_op jit(solution)/shard_map/ppermute | solution.py:70
  36.3 1.9 %collective-permute-start.9 = (bf16[75,8,128]{2,1,0:T(8,128)(2,1)S(1)}, bf16[75,8,128]{2,1,0:T(8,128)(2,1)S(1)}, u32[]{:S(2)}, u32[]{:S(2)}) collective-permute-start(bf16[75,8,128]{2,1,0:T(8,128)(2,1)S(1)} %collective-permute-done.7.tiles.refs_2_), channel_id=1, source_target_pairs={{0,1},{1,0},{2,3},{3,2},{4,5},{5,4},{6,7},{7,6},{8,9},{9,8},{10,11... | collective-permute-start | bytes 460808 | tf_op jit(solution)/shard_map/ppermute | solution.py:70
  40.0 7.0 %collective-permute-start.11 = (bf16[4,8,1024]{2,1,0:T(8,128)(2,1)S(1)}, bf16[4,8,1024]{2,1,0:T(8,128)(2,1)S(1)}, u32[]{:S(2)}, u32[]{:S(2)}) collective-permute-start(bf16[4,8,1024]{2,1,0:T(8,128)(2,1)S(1)} %get-tuple-element.72), channel_id=1, source_target_pairs={{0,16},{16,0},{1,17},{17,1},{2,18},{18,2},{3,19},{19,3},{4,20},{20... | collective-permute-start | bytes 196616 | tf_op jit(solution)/shard_map/ppermute | solution.py:70
  41.6 5.3 %collective-permute-start.10 = (bf16[3,8,1152]{2,1,0:T(8,128)(2,1)S(1)}, bf16[3,8,1152]{2,1,0:T(8,128)(2,1)S(1)}, u32[]{:S(2)}, u32[]{:S(2)}) collective-permute-start(bf16[3,8,1152]{2,1,0:T(8,128)(2,1)S(1)} %get-tuple-element.71), channel_id=1, source_target_pairs={{0,20},{4,16},{8,28},{12,24},{16,4},{20,0},{24,12},{28,8},{1,21},{... | collective-permute-start | bytes 165896 | tf_op jit(solution)/shard_map/ppermute | solution.py:70
  42.9 4.2 %collective-permute-start.12 = (bf16[3,8,1152]{2,1,0:T(8,128)(2,1)S(1)}, bf16[3,8,1152]{2,1,0:T(8,128)(2,1)S(1)}, u32[]{:S(2)}, u32[]{:S(2)}) collective-permute-start(bf16[3,8,1152]{2,1,0:T(8,128)(2,1)S(1)} %get-tuple-element.73), channel_id=1, source_target_pairs={{0,4},{4,0},{8,12},{12,8},{1,5},{5,1},{9,13},{13,9},{2,6},{6,2},{1... | collective-permute-start | bytes 165896 | tf_op jit(solution)/shard_map/ppermute | solution.py:70
  47.1 4.9 %collective-permute-start.13 = (bf16[2,8,1024]{2,1,0:T(8,128)(2,1)S(1)}, bf16[2,8,1024]{2,1,0:T(8,128)(2,1)S(1)}, u32[]{:S(2)}, u32[]{:S(2)}) collective-permute-start(bf16[2,8,1024]{2,1,0:T(8,128)(2,1)S(1)} %get-tuple-element.75), channel_id=1, source_target_pairs={{0,8},{4,12},{8,0},{12,4},{1,9},{5,13},{9,1},{13,5},{2,10},{6,14},... | collective-permute-start | bytes 98312 | tf_op jit(solution)/shard_map/ppermute | solution.py:70

commit v20 on v18

--- a/solution.py
+++ b/solution.py
@@ -134,7 +134,7 @@
 WIDE, NEXT, FAR = 4, 1, 2
 GATE, UP, DOWN = range(3)
 WHOLE_STRIP = (GATE, UP, DOWN)
-CHUNKS = 4
+CHUNKS = 2
 
 
 def start_loads(pieces, groups, sources, targets, sem):

time: 53 us -> 53 us (level)
  no operation moved by 1% of the time
where the time goes in v20:
time: 53 us; the launch traced here: 52.8 us
  Pallas kernels  27.2 us (51%)
  starting transfers between devices  16 us (30%)
  waiting for transfers between devices  8.64 us (16%)
  between operations  0.93 us (2%)
    pallas_call x16, Pallas kernels, call(): pl.pallas_call(body, out_shape=outs, in_specs=[pl.BlockSpec(memory_space=...  27.2 us
    ppermute x14, starting transfers between devices, exchange(): return lax.ppermute(array, axes, [(i, i ^ step) for i in range(size)])  16 us
    ppermute x14, waiting for transfers between devices, exchange(): return lax.ppermute(array, axes, [(i, i ^ step) for i in range(size)])  8.64 us
  transfers between devices with their start and end apart: 14, of which 7 were waited for; matrix products, arithmetic and copies ran while one was open for 0% of the time, Pallas kernels for 39%

profile of v20, /device:TPU:0, one launch (start us, length us, event | category | flops | bytes accessed | tf_op | source)
XLA Modules:
  0.0 52.8 jit_solution(14289355349499822083)
XLA Ops:
  0.6 0.8 %pack.1.own = bf16[3,8,1024]{2,1,0:T(8,128)(2,1)S(1)} custom-call(bf16[6,2048]{1,0:T(8,128)(2,1)} %inputs.1, bf16[6,2048]{1,0:T(8,128)(2,1)} %cotangent.1), custom_call_target="tpu_custom_call" | custom-call | flops 1000 | bytes 1000 | tf_op jit(solution)/shard_map/pack/pallas_call | solution.py:83
  1.4 4.1 %collective-permute-start = (bf16[3,8,1024]{2,1,0:T(8,128)(2,1)S(1)}, bf16[3,8,1024]{2,1,0:T(8,128)(2,1)S(1)}, u32[]{:S(2)}, u32[]{:S(2)}) collective-permute-start(bf16[3,8,1024]{2,1,0:T(8,128)(2,1)S(1)} %pack.1.own), channel_id=1, source_target_pairs={{0,8},{4,12},{8,0},{12,4},{1,9},{5,13},{9,1},{13,5},{2,10},{6,14},... | collective-permute-start | bytes 147464 | tf_op jit(solution)/shard_map/ppermute | solution.py:70
  5.5 3.8 %load_a.1 = (bf16[2048,768]{1,0:T(8,128)(2,1)S(1)}, bf16[2048,768]{1,0:T(8,128)(2,1)S(1)}, bf16[768,2048]{1,0:T(8,128)(2,1)S(1)}, bf16[8,1024]{1,0:T(8,128)(2,1)S(1)}) custom-call(bf16[2048,6144]{1,0:T(8,128)(2,1)} %refs_0_.11, bf16[2048,6144]{1,0:T(8,128)(2,1)} %refs_1_.11, bf16[6144,2048]{1,0:T(8,128)(2,1)} %refs_2_.11, s32[1,24]{1,0:T(1,128)} %bitcast.3), custom_call_target="tpu_custom_call" | custom-call | flops 1000 | bytes 1000 | tf_op jit(solution)/shard_map/load_a/pallas_call | solution.py:83
  9.4 0.0 collective-permute-done.far
  9.4 1.6 %collective-permute-start.2 = (bf16[7,8,1024]{2,1,0:T(8,128)(2,1)S(1)}, bf16[7,8,1024]{2,1,0:T(8,128)(2,1)S(1)}, u32[]{:S(2)}, u32[]{:S(2)}) collective-permute-start(bf16[7,8,1024]{2,1,0:T(8,128)(2,1)S(1)} %get-tuple-element.43.refs_3_.refs_4_), channel_id=1, source_target_pairs={{0,16},{16,0},{1,17},{17,1},{2,18},{18,2},{3,19},{19,3},{4,20},{20... | collective-permute-start | bytes 344072 | tf_op jit(solution)/shard_map/ppermute | solution.py:70
  11.0 1.5 %collective-permute-start.3 = (bf16[6,8,1024]{2,1,0:T(8,128)(2,1)S(1)}, bf16[6,8,1024]{2,1,0:T(8,128)(2,1)S(1)}, u32[]{:S(2)}, u32[]{:S(2)}) collective-permute-start(bf16[6,8,1024]{2,1,0:T(8,128)(2,1)S(1)} %get-tuple-element.44.refs_3_), channel_id=1, source_target_pairs={{0,20},{4,16},{8,28},{12,24},{16,4},{20,0},{24,12},{28,8},{1,21},{... | collective-permute-start | bytes 294920 | tf_op jit(solution)/shard_map/ppermute | solution.py:70
  12.5 0.4 collective-permute-start.1
  13.0 3.8 %load_b.1 = (bf16[2048,768]{1,0:T(8,128)(2,1)S(1)}, bf16[2048,768]{1,0:T(8,128)(2,1)S(1)}, bf16[768,2048]{1,0:T(8,128)(2,1)S(1)}) custom-call(bf16[2048,6144]{1,0:T(8,128)(2,1)} %refs_0_.11, bf16[2048,6144]{1,0:T(8,128)(2,1)} %refs_1_.11, bf16[6144,2048]{1,0:T(8,128)(2,1)} %refs_2_.11, bf16[6,8,1024]{2,1,0:T(8,128)(2,1)S(1)} %get-tuple-element.44.refs_3_), custom_call_target="tpu_custom_call" | custom-call | flops 1000 | bytes 1000 | tf_op jit(solution)/shard_map/load_b/pallas_call | solution.py:83
  16.8 0.4 collective-permute-done.3.refs_6_
  17.2 0.1 collective-permute-done.1.refs_4_
  17.3 0.0 collective-permute-done.2.refs_5_
  17.3 2.9 %forward_3.1 = (bf16[2048,768]{1,0:T(8,128)(2,1)S(1)}, bf16[768,2048]{1,0:T(8,128)(2,1)S(1)}, bf16[48,2048]{1,0:T(8,128)(2,1)S(1)}, bf16[48,2048]{1,0:T(8,128)(2,1)S(1)}, f32[3,48,768]{2,1,0:T(8,128)S(1)}) custom-call(bf16[2048,6144]{1,0:T(8,128)(2,1)} %refs_0_.11, bf16[2048,6144]{1,0:T(8,128)(2,1)} %refs_1_.11, bf16[6144,2048]{1,0:T(8,128)(2,1)} %refs_2_.11, ...), custom_call_target="tpu_custom_call" | custom-call | flops 1000 | bytes 1000 | tf_op jit(solution)/shard_map/forward_3/pallas_call | solution.py:83
  20.2 0.1 collective-permute-start.4
  20.2 2.0 %forward_2.1 = (bf16[2048,768]{1,0:T(8,128)(2,1)S(1)}, f32[3,48,768]{2,1,0:T(8,128)S(1)}) custom-call(bf16[2048,6144]{1,0:T(8,128)(2,1)} %refs_0_.11, bf16[2048,6144]{1,0:T(8,128)(2,1)} %refs_1_.11, bf16[6144,2048]{1,0:T(8,128)(2,1)} %refs_2_.11, bf16[48,2048]{1,0:T(8,128)(2,1)S(1)} %get-tuple-element.49.refs_3_, ...), custom_call_target="tpu_custom_call" | custom-call | flops 1000 | bytes 1000 | tf_op jit(solution)/shard_map/forward_2/pallas_call | solution.py:83
  22.3 0.0 collective-permute-done.4.arrived
  22.4 1.6 %collective-permute-start.6 = (bf16[3,48,768]{2,1,0:T(8,128)(2,1)S(1)}, bf16[3,48,768]{2,1,0:T(8,128)(2,1)S(1)}, u32[]{:S(2)}, u32[]{:S(2)}) collective-permute-start(bf16[3,48,768]{2,1,0:T(8,128)(2,1)S(1)} %join.1.refs_8_), channel_id=1, source_target_pairs={{0,2},{1,3},{2,0},{3,1},{4,6},{5,7},{6,4},{7,5},{8,10},{9,11},{10,... | collective-permute-start | bytes 663560 | tf_op jit(solution)/shard_map/ppermute | solution.py:70
  23.9 2.9 %forward_1.1 = (bf16[2048,768]{1,0:T(8,128)(2,1)S(1)}, bf16[768,2048]{1,0:T(8,128)(2,1)S(1)}, bf16[3,48,768]{2,1,0:T(8,128)(2,1)S(1)}) custom-call(bf16[2048,6144]{1,0:T(8,128)(2,1)} %refs_0_.11, bf16[2048,6144]{1,0:T(8,128)(2,1)} %refs_1_.11, bf16[6144,2048]{1,0:T(8,128)(2,1)} %refs_2_.11, bf16[48,2048]{1,0:T(8,128)(2,1)S(1)} %get-tuple-element.49.refs_3_, ...), custom_call_target="tpu_custom_call" | custom-call | flops 1000 | bytes 1000 | tf_op jit(solution)/shard_map/forward_1/pallas_call | solution.py:83
  26.8 0.3 collective-permute-start.5
  27.1 0.0 copy-start
  27.1 2.6 %forward_0.1 = (f32[3,48,768]{2,1,0:T(8,128)S(1)}, bf16[2048,768]{1,0:T(8,128)(2,1)S(1)}) custom-call(bf16[2048,6144]{1,0:T(8,128)(2,1)} %refs_0_.11, bf16[2048,6144]{1,0:T(8,128)(2,1)} %refs_1_.11, bf16[6144,2048]{1,0:T(8,128)(2,1)} %refs_2_.11, bf16[48,2048]{1,0:T(8,128)(2,1)S(1)} %get-tuple-element.49.refs_3_, ...), custom_call_target="tpu_custom_call" | custom-call | flops 1000 | bytes 1000 | tf_op jit(solution)/shard_map/forward_0/pallas_call | solution.py:83
  29.7 0.6 %collective-permute-done.6.refs_2_ = bf16[3,48,768]{2,1,0:T(8,128)(2,1)S(1)} collective-permute-done((bf16[3,48,768]{2,1,0:T(8,128)(2,1)S(1)}, bf16[3,48,768]{2,1,0:T(8,128)(2,1)S(1)}, u32[]{:S(2)}, u32[]{:S(2)}) %collective-permute-start.6) | collective-permute-done | bytes 221216 | tf_op jit(solution)/shard_map/ppermute | solution.py:70
  30.2 0.0 collective-permute-done.5.refs_1_
  30.2 0.0 copy-done
  30.2 0.4 middle.1
  30.6 1.5 %collective-permute-start.7 = (bf16[75,8,128]{2,1,0:T(8,128)(2,1)S(1)}, bf16[75,8,128]{2,1,0:T(8,128)(2,1)S(1)}, u32[]{:S(2)}, u32[]{:S(2)}) collective-permute-start(bf16[75,8,128]{2,1,0:T(8,128)(2,1)S(1)} %get-tuple-element.63), channel_id=1, source_target_pairs={{0,2},{1,3},{2,0},{3,1},{4,6},{5,7},{6,4},{7,5},{8,10},{9,11},{10,... | collective-permute-start | bytes 460808 | tf_op jit(solution)/shard_map/ppermute | solution.py:70
  32.1 0.0 collective-permute-start.8
  32.1 1.7 %backward_0.1.before = f32[2048,48]{1,0:T(8,128)S(1)} custom-call(bf16[112,768]{1,0:T(8,128)(2,1)S(1)} %get-tuple-element.65.message.refs_0_, bf16[2048,768]{1,0:T(8,128)(2,1)S(1)} %get-tuple-element.62.refs_6_.gate, bf16[2048,768]{1,0:T(8,128)(2,1)S(1)} %get-tuple-element.58.refs_5_.refs_7_.up), custom_call_target="tpu_custom_call" | custom-call | flops 1000 | bytes 1000 | tf_op jit(solution)/shard_map/backward_0/pallas_call | solution.py:83
  33.9 0.0 collective-permute-done.8.tiles.refs_1_
  33.9 1.8 %backward_1.1.before = f32[2048,48]{1,0:T(8,128)S(1)} custom-call(bf16[74,8,128]{2,1,0:T(8,128)(2,1)S(1)} %collective-permute-done.8.tiles.refs_1_, bf16[2048,768]{1,0:T(8,128)(2,1)S(1)} %get-tuple-element.51.refs_5_.refs_8_.gate, bf16[2048,768]{1,0:T(8,128)(2,1)S(1)} %get-tuple-element.54.refs_6_.refs_9_.up, f32[2048,48]{1,0:T(8,128)S(1)} %backward_0.1.before), custom_call_target="tpu_custom_call" | custom-call | flops 1000 | bytes 1000 | tf_op jit(solution)/shard_map/backward_1/pallas_call | solution.py:83
  35.7 0.6 %collective-permute-done.7.tiles.refs_2_ = bf16[75,8,128]{2,1,0:T(8,128)(2,1)S(1)} collective-permute-done((bf16[75,8,128]{2,1,0:T(8,128)(2,1)S(1)}, bf16[75,8,128]{2,1,0:T(8,128)(2,1)S(1)}, u32[]{:S(2)}, u32[]{:S(2)}) %collective-permute-start.7) | collective-permute-done | bytes 153632 | tf_op jit(solution)/shard_map/ppermute | solution.py:70
  36.3 0.0 collective-permute-start.9
  36.3 1.8 %backward_2.1.before = f32[2048,48]{1,0:T(8,128)S(1)} custom-call(bf16[75,8,128]{2,1,0:T(8,128)(2,1)S(1)} %collective-permute-done.7.tiles.refs_2_, bf16[2048,768]{1,0:T(8,128)(2,1)S(1)} %get-tuple-element.48.refs_10_.refs_5_.gate, bf16[2048,768]{1,0:T(8,128)(2,1)S(1)} %get-tuple-element.52.refs_6_.refs_11_.up, f32[2048,48]{1,0:T(8,128)S(1)} %backward_1.1.before), custom_call_target="tpu_custom_call" | custom-call | flops 1000 | bytes 1000 | tf_op jit(solution)/shard_map/backward_2/pallas_call | solution.py:83
  38.1 0.0 collective-permute-done.9.tiles
  38.1 1.9 %backward_3.1 = (f32[24,1024]{1,0:T(8,128)S(1)}, f32[8,128]{1,0:T(8,128)S(1)}, bf16[3,8,1152]{2,1,0:T(8,128)(2,1)S(1)}, bf16[4,8,1024]{2,1,0:T(8,128)(2,1)S(1)}, bf16[3,8,1152]{2,1,0:T(8,128)(2,1)S(1)}) custom-call(bf16[75,8,128]{2,1,0:T(8,128)(2,1)S(1)} %collective-permute-done.9.tiles, bf16[2048,768]{1,0:T(8,128)(2,1)S(1)} %get-tuple-element.45.refs_7_.refs_12_.gate, ...), custom_call_target="tpu_custom_call" | custom-call | flops 1000 | bytes 1000 | tf_op jit(solution)/shard_map/backward_3/pallas_call | solution.py:83
  40.0 1.6 %collective-permute-start.11 = (bf16[4,8,1024]{2,1,0:T(8,128)(2,1)S(1)}, bf16[4,8,1024]{2,1,0:T(8,128)(2,1)S(1)}, u32[]{:S(2)}, u32[]{:S(2)}) collective-permute-start(bf16[4,8,1024]{2,1,0:T(8,128)(2,1)S(1)} %get-tuple-element.72), channel_id=1, source_target_pairs={{0,16},{16,0},{1,17},{17,1},{2,18},{18,2},{3,19},{19,3},{4,20},{20... | collective-permute-start | bytes 196616 | tf_op jit(solution)/shard_map/ppermute | solution.py:70
  41.6 1.3 %collective-permute-start.10 = (bf16[3,8,1152]{2,1,0:T(8,128)(2,1)S(1)}, bf16[3,8,1152]{2,1,0:T(8,128)(2,1)S(1)}, u32[]{:S(2)}, u32[]{:S(2)}) collective-permute-start(bf16[3,8,1152]{2,1,0:T(8,128)(2,1)S(1)} %get-tuple-element.71), channel_id=1, source_target_pairs={{0,20},{4,16},{8,28},{12,24},{16,4},{20,0},{24,12},{28,8},{1,21},{... | collective-permute-start | bytes 165896 | tf_op jit(solution)/shard_map/ppermute | solution.py:70
  42.9 0.7 %collective-permute-start.12 = (bf16[3,8,1152]{2,1,0:T(8,128)(2,1)S(1)}, bf16[3,8,1152]{2,1,0:T(8,128)(2,1)S(1)}, u32[]{:S(2)}, u32[]{:S(2)}) collective-permute-start(bf16[3,8,1152]{2,1,0:T(8,128)(2,1)S(1)} %get-tuple-element.73), channel_id=1, source_target_pairs={{0,4},{4,0},{8,12},{12,8},{1,5},{5,1},{9,13},{13,9},{2,6},{6,2},{1... | collective-permute-start | bytes 165896 | tf_op jit(solution)/shard_map/ppermute | solution.py:70
  43.5 3.4 %collective-permute-done.10.diagonal = bf16[3,8,1152]{2,1,0:T(8,128)(2,1)S(1)} collective-permute-done((bf16[3,8,1152]{2,1,0:T(8,128)(2,1)S(1)}, bf16[3,8,1152]{2,1,0:T(8,128)(2,1)S(1)}, u32[]{:S(2)}, u32[]{:S(2)}) %collective-permute-start.10) | collective-permute-done | bytes 55328 | tf_op jit(solution)/shard_map/ppermute | solution.py:70
  47.0 0.1 collective-permute-done.12.beside
  47.0 0.0 collective-permute-done.11.across
  47.1 1.4 %collective-permute-start.13 = (bf16[2,8,1024]{2,1,0:T(8,128)(2,1)S(1)}, bf16[2,8,1024]{2,1,0:T(8,128)(2,1)S(1)}, u32[]{:S(2)}, u32[]{:S(2)}) collective-permute-start(bf16[2,8,1024]{2,1,0:T(8,128)(2,1)S(1)} %get-tuple-element.75), channel_id=1, source_target_pairs={{0,8},{4,12},{8,0},{12,4},{1,9},{5,13},{9,1},{13,5},{2,10},{6,14},... | collective-permute-start | bytes 98312 | tf_op jit(solution)/shard_map/ppermute | solution.py:70
  48.5 3.5 %collective-permute-done.13.arrived = bf16[2,8,1024]{2,1,0:T(8,128)(2,1)S(1)} collective-permute-done((bf16[2,8,1024]{2,1,0:T(8,128)(2,1)S(1)}, bf16[2,8,1024]{2,1,0:T(8,128)(2,1)S(1)}, u32[]{:S(2)}, u32[]{:S(2)}) %collective-permute-start.13) | collective-permute-done | bytes 32800 | tf_op jit(solution)/shard_map/ppermute | solution.py:70
  52.0 0.7 %last.1 = (bf16[6,2048]{1,0:T(8,128)(2,1)}, f32[4,1536]{1,0:T(4,128)}, f32[4]{0:T(128)}) custom-call(f32[16,1024]{1,0:T(8,128)S(1)} %get-tuple-element.74.own, bf16[2,8,1024]{2,1,0:T(8,128)(2,1)S(1)} %collective-permute-done.13.arrived, f32[4,768]{1,0:T(4,128)S(1)} %get-tuple-element.76.grads, f32[4,768]{1,0:T(4,128)S(1)} %get-tuple-element.77.other_grads), custom_call_target="tpu_custom_call" | custom-call | flops 1000 | bytes 1000 | tf_op jit(solution)/shard_map/last/pallas_call | solution.py:83
  (3 shorter events, 0.1 us)
Async XLA Ops:
  1.4 8.0 %collective-permute-start = (bf16[3,8,1024]{2,1,0:T(8,128)(2,1)S(1)}, bf16[3,8,1024]{2,1,0:T(8,128)(2,1)S(1)}, u32[]{:S(2)}, u32[]{:S(2)}) collective-permute-start(bf16[3,8,1024]{2,1,0:T(8,128)(2,1)S(1)} %pack.1.own), channel_id=1, source_target_pairs={{0,8},{4,12},{8,0},{12,4},{1,9},{5,13},{9,1},{13,5},{2,10},{6,14},... | collective-permute-start | bytes 147464 | tf_op jit(solution)/shard_map/ppermute | solution.py:70
  9.4 7.9 %collective-permute-start.2 = (bf16[7,8,1024]{2,1,0:T(8,128)(2,1)S(1)}, bf16[7,8,1024]{2,1,0:T(8,128)(2,1)S(1)}, u32[]{:S(2)}, u32[]{:S(2)}) collective-permute-start(bf16[7,8,1024]{2,1,0:T(8,128)(2,1)S(1)} %get-tuple-element.43.refs_3_.refs_4_), channel_id=1, source_target_pairs={{0,16},{16,0},{1,17},{17,1},{2,18},{18,2},{3,19},{19,3},{4,20},{20... | collective-permute-start | bytes 344072 | tf_op jit(solution)/shard_map/ppermute | solution.py:70
  11.0 6.2 %collective-permute-start.3 = (bf16[6,8,1024]{2,1,0:T(8,128)(2,1)S(1)}, bf16[6,8,1024]{2,1,0:T(8,128)(2,1)S(1)}, u32[]{:S(2)}, u32[]{:S(2)}) collective-permute-start(bf16[6,8,1024]{2,1,0:T(8,128)(2,1)S(1)} %get-tuple-element.44.refs_3_), channel_id=1, source_target_pairs={{0,20},{4,16},{8,28},{12,24},{16,4},{20,0},{24,12},{28,8},{1,21},{... | collective-permute-start | bytes 294920 | tf_op jit(solution)/shard_map/ppermute | solution.py:70
  12.5 4.7 %collective-permute-start.1 = (bf16[6,8,1024]{2,1,0:T(8,128)(2,1)S(1)}, bf16[6,8,1024]{2,1,0:T(8,128)(2,1)S(1)}, u32[]{:S(2)}, u32[]{:S(2)}) collective-permute-start(bf16[6,8,1024]{2,1,0:T(8,128)(2,1)S(1)} %get-tuple-element.44.refs_3_), channel_id=1, source_target_pairs={{0,4},{4,0},{8,12},{12,8},{1,5},{5,1},{9,13},{13,9},{2,6},{6,2},{1... | collective-permute-start | bytes 294920 | tf_op jit(solution)/shard_map/ppermute | solution.py:70
  20.2 2.1 %collective-permute-start.4 = (f32[3,48,768]{2,1,0:T(8,128)S(1)}, f32[3,48,768]{2,1,0:T(8,128)S(1)}, u32[]{:S(2)}, u32[]{:S(2)}) collective-permute-start(f32[3,48,768]{2,1,0:T(8,128)S(1)} %get-tuple-element.57), channel_id=1, source_target_pairs={{0,1},{1,0},{2,3},{3,2},{4,5},{5,4},{6,7},{7,6},{8,9},{9,8},{10,11... | collective-permute-start | bytes 1327112 | tf_op jit(solution)/shard_map/ppermute | solution.py:70
  22.4 7.9 %collective-permute-start.6 = (bf16[3,48,768]{2,1,0:T(8,128)(2,1)S(1)}, bf16[3,48,768]{2,1,0:T(8,128)(2,1)S(1)}, u32[]{:S(2)}, u32[]{:S(2)}) collective-permute-start(bf16[3,48,768]{2,1,0:T(8,128)(2,1)S(1)} %join.1.refs_8_), channel_id=1, source_target_pairs={{0,2},{1,3},{2,0},{3,1},{4,6},{5,7},{6,4},{7,5},{8,10},{9,11},{10,... | collective-permute-start | bytes 663560 | tf_op jit(solution)/shard_map/ppermute | solution.py:70
  26.8 3.4 %collective-permute-start.5 = (bf16[3,48,768]{2,1,0:T(8,128)(2,1)S(1)}, bf16[3,48,768]{2,1,0:T(8,128)(2,1)S(1)}, u32[]{:S(2)}, u32[]{:S(2)}) collective-permute-start(bf16[3,48,768]{2,1,0:T(8,128)(2,1)S(1)} %get-tuple-element.61), channel_id=1, source_target_pairs={{0,1},{1,0},{2,3},{3,2},{4,5},{5,4},{6,7},{7,6},{8,9},{9,8},{10,11... | collective-permute-start | bytes 663560 | tf_op jit(solution)/shard_map/ppermute | solution.py:70
  27.1 3.2 %copy-start = (f32[6144]{0:T(1024)S(1)}, f32[6144]{0:T(1024)}, u32[]{:S(2)}) copy-start(f32[6144]{0:T(1024)} %param.12) | copy-start | bytes 73732
  30.6 5.6 %collective-permute-start.7 = (bf16[75,8,128]{2,1,0:T(8,128)(2,1)S(1)}, bf16[75,8,128]{2,1,0:T(8,128)(2,1)S(1)}, u32[]{:S(2)}, u32[]{:S(2)}) collective-permute-start(bf16[75,8,128]{2,1,0:T(8,128)(2,1)S(1)} %get-tuple-element.63), channel_id=1, source_target_pairs={{0,2},{1,3},{2,0},{3,1},{4,6},{5,7},{6,4},{7,5},{8,10},{9,11},{10,... | collective-permute-start | bytes 460808 | tf_op jit(solution)/shard_map/ppermute | solution.py:70
  32.1 1.8 %collective-permute-start.8 = (bf16[74,8,128]{2,1,0:T(8,128)(2,1)S(1)}, bf16[74,8,128]{2,1,0:T(8,128)(2,1)S(1)}, u32[]{:S(2)}, u32[]{:S(2)}) collective-permute-start(bf16[74,8,128]{2,1,0:T(8,128)(2,1)S(1)} %get-tuple-element.64), channel_id=1, source_target_pairs={{0,1},{1,0},{2,3},{3,2},{4,5},{5,4},{6,7},{7,6},{8,9},{9,8},{10,11... | collective-permute-start | bytes 454664 | tf_op jit(solution)/shard_map/ppermute | solution.py:70
  36.3 1.8 %collective-permute-start.9 = (bf16[75,8,128]{2,1,0:T(8,128)(2,1)S(1)}, bf16[75,8,128]{2,1,0:T(8,128)(2,1)S(1)}, u32[]{:S(2)}, u32[]{:S(2)}) collective-permute-start(bf16[75,8,128]{2,1,0:T(8,128)(2,1)S(1)} %collective-permute-done.7.tiles.refs_2_), channel_id=1, source_target_pairs={{0,1},{1,0},{2,3},{3,2},{4,5},{5,4},{6,7},{7,6},{8,9},{9,8},{10,11... | collective-permute-start | bytes 460808 | tf_op jit(solution)/shard_map/ppermute | solution.py:70
  40.0 7.1 %collective-permute-start.11 = (bf16[4,8,1024]{2,1,0:T(8,128)(2,1)S(1)}, bf16[4,8,1024]{2,1,0:T(8,128)(2,1)S(1)}, u32[]{:S(2)}, u32[]{:S(2)}) collective-permute-start(bf16[4,8,1024]{2,1,0:T(8,128)(2,1)S(1)} %get-tuple-element.72), channel_id=1, source_target_pairs={{0,16},{16,0},{1,17},{17,1},{2,18},{18,2},{3,19},{19,3},{4,20},{20... | collective-permute-start | bytes 196616 | tf_op jit(solution)/shard_map/ppermute | solution.py:70
  41.6 5.4 %collective-permute-start.10 = (bf16[3,8,1152]{2,1,0:T(8,128)(2,1)S(1)}, bf16[3,8,1152]{2,1,0:T(8,128)(2,1)S(1)}, u32[]{:S(2)}, u32[]{:S(2)}) collective-permute-start(bf16[3,8,1152]{2,1,0:T(8,128)(2,1)S(1)} %get-tuple-element.71), channel_id=1, source_target_pairs={{0,20},{4,16},{8,28},{12,24},{16,4},{20,0},{24,12},{28,8},{1,21},{... | collective-permute-start | bytes 165896 | tf_op jit(solution)/shard_map/ppermute | solution.py:70
  42.9 4.2 %collective-permute-start.12 = (bf16[3,8,1152]{2,1,0:T(8,128)(2,1)S(1)}, bf16[3,8,1152]{2,1,0:T(8,128)(2,1)S(1)}, u32[]{:S(2)}, u32[]{:S(2)}) collective-permute-start(bf16[3,8,1152]{2,1,0:T(8,128)(2,1)S(1)} %get-tuple-element.73), channel_id=1, source_target_pairs={{0,4},{4,0},{8,12},{12,8},{1,5},{5,1},{9,13},{13,9},{2,6},{6,2},{1... | collective-permute-start | bytes 165896 | tf_op jit(solution)/shard_map/ppermute | solution.py:70
  47.1 4.9 %collective-permute-start.13 = (bf16[2,8,1024]{2,1,0:T(8,128)(2,1)S(1)}, bf16[2,8,1024]{2,1,0:T(8,128)(2,1)S(1)}, u32[]{:S(2)}, u32[]{:S(2)}) collective-permute-start(bf16[2,8,1024]{2,1,0:T(8,128)(2,1)S(1)} %get-tuple-element.75), channel_id=1, source_target_pairs={{0,8},{4,12},{8,0},{12,4},{1,9},{5,13},{9,1},{13,5},{2,10},{6,14},... | collective-permute-start | bytes 98312 | tf_op jit(solution)/shard_map/ppermute | solution.py:70
